TPU v7x, 32 devices: a whole 2x2x4 slice. The times are simulated.
32 devices in a mesh: dp: 2 (over y), seq: 4 (over z), tensor: 4 (over x, core).
Axes of the slice: x: 2, y: 2, z: 4, core: 2. Of those that a mesh axis runs over, the one named last changes fastest.
Arguments:
- tokens: bfloat16 [4, 2048, 1536], P('dp', 'seq'), may hold values from -6 to 6
- lengths: int32 [4, 8], P('dp'), may hold values from 1 to 1024, 2048 in all within a row
- cotangent: bfloat16 [4, 2048, 1536], P('dp', 'seq'), may hold values from -6 to 6
- q_weight: bfloat16 [1536, 1536], P(None, 'tensor'), may hold values from -0.15625 to 0.15625
- q_bias: bfloat16 [1536], P('tensor'), may hold values from -3 to 3
- k_weight: bfloat16 [1536, 256], replicated, may hold values from -0.15625 to 0.15625
- k_bias: bfloat16 [256], replicated, may hold values from -3 to 3
- v_weight: bfloat16 [1536, 256], replicated, may hold values from -0.15625 to 0.15625
- v_bias: bfloat16 [256], replicated, may hold values from -3 to 3
- o_weight: bfloat16 [1536, 1536], P(None, 'tensor'), may hold values from -0.625 to 0.625
- attn_gain: bfloat16 [1536], replicated, may hold values from 0.099609375 to 1.8984375
- ffn_gain: bfloat16 [1536], replicated, may hold values from 0.099609375 to 1.8984375
- gate_weight: bfloat16 [1536, 8960], P(None, 'tensor'), may hold values from -0.15625 to 0.15625
- up_weight: bfloat16 [1536, 8960], P(None, 'tensor'), may hold values from -0.15625 to 0.15625
- down_weight: bfloat16 [1536, 8960], P(None, 'tensor'), may hold values from -0.0625 to 0.0625
Outputs:
- layer_out: bfloat16 [4, 2048, 1536], P('dp', 'seq')
- token_grad: float32 [4, 2048, 1536], P('dp', 'seq')
- q_weight_grad: float32 [1536, 1536], P(('dp', 'seq'), 'tensor')
- q_bias_grad: float32 [1536], replicated
- k_weight_grad: float32 [1536, 256], P(('dp', 'seq', 'tensor'))
- k_bias_grad: float32 [256], replicated
- v_weight_grad: float32 [1536, 256], P(('dp', 'seq', 'tensor'))
- v_bias_grad: float32 [256], replicated
- o_weight_grad: float32 [1536, 1536], P(('dp', 'seq'), 'tensor')
- attn_gain_grad: float32 [1536], P(('dp', 'seq'))
- ffn_gain_grad: float32 [1536], P(('dp', 'seq'))
- gate_weight_grad: float32 [1536, 8960], P(('dp', 'seq'), 'tensor')
- up_weight_grad: float32 [1536, 8960], P(('dp', 'seq'), 'tensor')
- down_weight_grad: float32 [1536, 8960], P(('dp', 'seq'), 'tensor')
Inputs may be any that keep to these rules, and one draw needn't show every extreme that they name: Each row's entries are its document lengths in order followed by its padding tail; they sum to 2048, and every row's length list contains an entry equal to 1024, its largest.
All inputs are finite; a program needn't handle non-finite values.
Results may differ from a plain program's by a relative error of at most 0.025.
Values may be sent and summed in bfloat16 or wider, within the bound.
No kernel may reach another device: no remote copies, remote signals or barrier semaphores. Data moves between devices by JAX's collectives and lax.ppermute only.
A program may use at most 256 MiB of HBM per device.

v0:
```python
import math

import jax
import jax.numpy as jnp
from jax import lax
from jax.sharding import PartitionSpec as P

KVH = 2
HD = 128


EPS = 1e-06
ROPE_BASE = 10000.0
NEG_FILL = -1e30


def from_partner(block, axis, stride):
    count = lax.axis_size(axis)
    route = []
    for low in range(count):
        high = low | 1 << stride
        if high != low and high < count:
            route += [(low, high), (high, low)]
    return lax.ppermute(block, axis, route)


def to_bf(value):
    return value.astype(jnp.bfloat16)


def doc_tables(lengths, span):
    ends = jnp.cumsum(lengths, axis=1)
    starts = ends - lengths
    places = jnp.arange(span, dtype=jnp.int32)
    segment = jnp.sum((places[None, :, None] >= ends[:, None, :]).astype(jnp.int32), axis=2)
    slot_ids = jnp.arange(lengths.shape[1], dtype=jnp.int32)
    member = segment[:, :, None] == slot_ids[None, None, :]
    first = jnp.sum(
        jnp.where(member, starts[:, None, :], jnp.zeros_like(starts[:, None, :])), axis=2
    )
    position = places[None, :] - first
    valid = (segment < lengths.shape[1] - 1).astype(jnp.float32)
    return (segment, position, valid)


def rope_tables(position):
    half = HD // 2
    freqs = ROPE_BASE ** (-(jnp.arange(half, dtype=jnp.float32) * 2.0) / HD)
    angles = position.astype(jnp.float32)[..., None] * freqs
    cosine = jnp.cos(angles)
    sine = jnp.sin(angles)
    return (jnp.concatenate([cosine, cosine], -1), jnp.concatenate([sine, sine], -1))


def rotate(value, cosine, sine):
    half = value.shape[-1] // 2
    turned = jnp.concatenate([-value[..., half:], value[..., :half]], axis=-1)
    return value * cosine + turned * sine


def unrotate(grad, cosine, sine):
    half = grad.shape[-1] // 2
    scaled = grad * sine
    back = jnp.concatenate([scaled[..., half:], -scaled[..., :half]], axis=-1)
    return grad * cosine + back


def matmul(left, right):
    return jnp.dot(left, right, preferred_element_type=jnp.float32)


def matmul_nt(left, right):
    return lax.dot_general(
        left, right, (((1,), (1,)), ((), ())), preferred_element_type=jnp.float32
    )


def matmul_tn(left, right):
    return lax.dot_general(
        left, right, (((0,), (0,)), ((), ())), preferred_element_type=jnp.float32
    )


def masked_scores(q_row, k_row, seg_query, seg_key, place_query, place_key, scale):
    raw = jnp.einsum("qhd,kd->hqk", q_row, k_row, preferred_element_type=jnp.float32) * scale
    allowed = (seg_query[:, None] == seg_key[None, :]) & (
        place_query[:, None] >= place_key[None, :]
    )
    return jnp.where(allowed[None], raw, NEG_FILL)


def norm_back(grad_out, normed, factor, gain):
    weighted = grad_out * gain
    inner = jnp.mean(weighted * normed, axis=-1, keepdims=True)
    return (factor * (weighted - normed * inner), jnp.sum(grad_out * normed, axis=0))


def body(
    tokens,
    lengths,
    cotangent,
    q_weight,
    q_bias,
    k_weight,
    k_bias,
    v_weight,
    v_bias,
    o_weight,
    attn_gain,
    ffn_gain,
    gate_weight,
    up_weight,
    down_weight,
):
    row_count, local, width = tokens.shape
    total = row_count * local
    full_len = local * lax.axis_size("seq")
    heads_dev = q_weight.shape[1] // HD
    group = lax.axis_size("tensor") // KVH
    kv_head = lax.axis_index("tensor") // group
    offset = lax.axis_index("seq") * local
    scale = 1.0 / math.sqrt(HD)
    seg_all, pos_all, valid_all = doc_tables(lengths, full_len)
    seg_local = lax.dynamic_slice_in_dim(seg_all, offset, local, 1)
    pos_local = lax.dynamic_slice_in_dim(pos_all, offset, local, 1)
    valid_local = lax.dynamic_slice_in_dim(valid_all, offset, local, 1)
    place_query = offset + jnp.arange(local, dtype=jnp.int32)
    place_key = jnp.arange(full_len, dtype=jnp.int32)
    cosine, sine = rope_tables(pos_local.reshape(total))
    gain_one = attn_gain.astype(jnp.float32)
    gain_two = ffn_gain.astype(jnp.float32)
    wk_head = lax.dynamic_slice_in_dim(k_weight, kv_head * HD, HD, 1)
    wv_head = lax.dynamic_slice_in_dim(v_weight, kv_head * HD, HD, 1)
    bk_head = lax.dynamic_slice_in_dim(k_bias, kv_head * HD, HD, 0).astype(jnp.float32)
    bv_head = lax.dynamic_slice_in_dim(v_bias, kv_head * HD, HD, 0).astype(jnp.float32)
    inputs = tokens.astype(jnp.float32).reshape(total, width)
    factor_one = lax.rsqrt(jnp.mean(inputs * inputs, axis=-1, keepdims=True) + EPS)
    normed_one = inputs * factor_one
    h_one = to_bf(normed_one * gain_one)
    q_lin = matmul(h_one, q_weight) + q_bias.astype(jnp.float32)
    k_lin = matmul(h_one, wk_head) + bk_head
    v_lin = matmul(h_one, wv_head) + bv_head
    q_rot = to_bf(rotate(q_lin.reshape(total, heads_dev, HD), cosine[:, None, :], sine[:, None, :]))
    k_rot = to_bf(rotate(k_lin, cosine, sine)).reshape(row_count, local, HD)
    v_val = to_bf(v_lin).reshape(row_count, local, HD)
    k_rows, v_rows = (
        lax.all_gather(k_rot, "seq", axis=1, tiled=True),
        lax.all_gather(v_val, "seq", axis=1, tiled=True),
    )
    q_rows = q_rot.reshape(row_count, local, heads_dev, HD)

    def attend(item):
        q_row, k_row, v_row, seg_query, seg_key = item
        scores = masked_scores(q_row, k_row, seg_query, seg_key, place_query, place_key, scale)
        top = jnp.max(scores, axis=-1, keepdims=True)
        expo = jnp.exp(scores - top)
        summed = jnp.sum(expo, axis=-1, keepdims=True)
        probs = to_bf(expo / summed)
        mixed = jnp.einsum("hqk,kd->qhd", probs, v_row, preferred_element_type=jnp.float32)
        return (to_bf(mixed), top[..., 0] + jnp.log(summed[..., 0]))

    mixed_rows, log_totals = lax.map(attend, (q_rows, k_rows, v_rows, seg_local, seg_all))
    mixed_flat = mixed_rows.reshape(total, heads_dev * HD)
    branch = lax.psum(matmul_nt(mixed_flat, o_weight).astype(jnp.bfloat16), "tensor").astype(
        jnp.float32
    )
    middle = inputs + branch
    factor_two = lax.rsqrt(jnp.mean(middle * middle, axis=-1, keepdims=True) + EPS)
    normed_two = middle * factor_two
    h_two = to_bf(normed_two * gain_two)
    gate_lin = matmul(h_two, gate_weight)
    up_lin = matmul(h_two, up_weight)
    sigma = jax.nn.sigmoid(gate_lin)
    swish = gate_lin * sigma
    hidden = to_bf(swish * up_lin)
    ffn_part = lax.psum(matmul_nt(hidden, down_weight).astype(jnp.bfloat16), "tensor").astype(
        jnp.float32
    )
    result = middle + ffn_part
    layer_out = to_bf(result).reshape(row_count, local, width)
    grad_out = cotangent.astype(jnp.float32).reshape(total, width) * valid_local.reshape(total, 1)
    grad_ffn = to_bf(grad_out)
    down_term = matmul_tn(grad_ffn, hidden)
    grad_hidden = matmul(grad_ffn, down_weight)
    grad_gate = to_bf(grad_hidden * up_lin * sigma * (1.0 + gate_lin * (1.0 - sigma)))
    grad_up = to_bf(grad_hidden * swish)
    gate_term = matmul_tn(h_two, grad_gate)
    up_term = matmul_tn(h_two, grad_up)
    grad_h_two = lax.psum(
        (matmul_nt(grad_gate, gate_weight) + matmul_nt(grad_up, up_weight)).astype(jnp.bfloat16),
        "tensor",
    ).astype(jnp.float32)
    back_two, ffn_gain_term = norm_back(grad_h_two, normed_two, factor_two, gain_two)
    grad_middle = grad_out + back_two
    grad_branch = to_bf(grad_middle)
    out_term = matmul_tn(grad_branch, mixed_flat)
    grad_mixed = to_bf(matmul(grad_branch, o_weight)).reshape(row_count, local, heads_dev, HD)
    k_back, v_back = (k_rows, v_rows)

    def attend_back(item):
        q_row, k_row, v_row, grad_row, log_row, seg_query, seg_key = item
        scores = masked_scores(q_row, k_row, seg_query, seg_key, place_query, place_key, scale)
        probs = jnp.exp(scores - log_row[..., None])
        grad_v = jnp.einsum(
            "hqk,qhd->kd", to_bf(probs), grad_row, preferred_element_type=jnp.float32
        )
        grad_probs = jnp.einsum("qhd,kd->hqk", grad_row, v_row, preferred_element_type=jnp.float32)
        inner = jnp.sum(probs * grad_probs, axis=-1, keepdims=True)
        grad_scores = to_bf(probs * (grad_probs - inner))
        grad_q = (
            jnp.einsum("hqk,kd->qhd", grad_scores, k_row, preferred_element_type=jnp.float32)
            * scale
        )
        grad_k = (
            jnp.einsum("hqk,qhd->kd", grad_scores, q_row, preferred_element_type=jnp.float32)
            * scale
        )
        return (grad_q, grad_k, grad_v)

    grad_q_rows, grad_k_rows, grad_v_rows = lax.map(
        attend_back, (q_rows, k_back, v_back, grad_mixed, log_totals, seg_local, seg_all)
    )
    key_own, value_own = (
        lax.psum_scatter(
            grad_k_rows.astype(jnp.bfloat16), "seq", scatter_dimension=1, tiled=True
        ).astype(jnp.float32),
        lax.psum_scatter(
            grad_v_rows.astype(jnp.bfloat16), "seq", scatter_dimension=1, tiled=True
        ).astype(jnp.float32),
    )
    key_mate, value_mate = (
        from_partner(key_own.astype(jnp.bfloat16), "tensor", 0).astype(key_own.dtype),
        from_partner(value_own.astype(jnp.bfloat16), "tensor", 0).astype(value_own.dtype),
    )
    grad_k = to_bf(unrotate((key_own + key_mate).reshape(total, HD), cosine, sine))
    grad_vv = to_bf((value_own + value_mate).reshape(total, HD))
    grad_q = to_bf(
        unrotate(
            grad_q_rows.reshape(total, heads_dev, HD), cosine[:, None, :], sine[:, None, :]
        ).reshape(total, heads_dev * HD)
    )
    q_term = matmul_tn(h_one, grad_q)
    share = 1.0 / group
    head_pick = (jnp.arange(KVH, dtype=jnp.int32) == kv_head).astype(jnp.float32)
    rank_pick = (
        jnp.arange(lax.axis_size("tensor"), dtype=jnp.int32) == lax.axis_index("tensor")
    ).astype(jnp.float32)
    k_term = (head_pick[None, :, None] * (matmul_tn(h_one, grad_k) * share)[:, None, :]).reshape(
        width, KVH * HD
    )
    v_term = (head_pick[None, :, None] * (matmul_tn(h_one, grad_vv) * share)[:, None, :]).reshape(
        width, KVH * HD
    )
    q_bias_term = (
        rank_pick[:, None] * jnp.sum(grad_q.astype(jnp.float32), axis=0)[None, :]
    ).reshape(-1)
    k_bias_term = (
        head_pick[:, None] * (jnp.sum(grad_k.astype(jnp.float32), axis=0) * share)[None, :]
    ).reshape(-1)
    v_bias_term = (
        head_pick[:, None] * (jnp.sum(grad_vv.astype(jnp.float32), axis=0) * share)[None, :]
    ).reshape(-1)
    pair_part = (matmul_nt(grad_k, wk_head) + matmul_nt(grad_vv, wv_head)) * share
    grad_h_one = lax.psum(
        (matmul_nt(grad_q, q_weight) + pair_part).astype(jnp.bfloat16), "tensor"
    ).astype(jnp.float32)
    back_one, attn_gain_term = norm_back(grad_h_one, normed_one, factor_one, gain_one)
    token_grad = (grad_middle + back_one).reshape(row_count, local, width)
    q_grad, o_grad, gate_grad, up_grad, down_grad, attn_gain_grad, ffn_gain_grad = (
        lax.psum_scatter(
            q_term.astype(jnp.bfloat16), ("dp", "seq"), scatter_dimension=0, tiled=True
        ).astype(jnp.float32),
        lax.psum_scatter(
            out_term.astype(jnp.bfloat16), ("dp", "seq"), scatter_dimension=0, tiled=True
        ).astype(jnp.float32),
        lax.psum_scatter(
            gate_term.astype(jnp.bfloat16), ("dp", "seq"), scatter_dimension=0, tiled=True
        ).astype(jnp.float32),
        lax.psum_scatter(
            up_term.astype(jnp.bfloat16), ("dp", "seq"), scatter_dimension=0, tiled=True
        ).astype(jnp.float32),
        lax.psum_scatter(
            down_term.astype(jnp.bfloat16), ("dp", "seq"), scatter_dimension=0, tiled=True
        ).astype(jnp.float32),
        lax.psum_scatter(
            attn_gain_term.astype(jnp.bfloat16), ("dp", "seq"), scatter_dimension=0, tiled=True
        ).astype(jnp.float32),
        lax.psum_scatter(
            ffn_gain_term.astype(jnp.bfloat16), ("dp", "seq"), scatter_dimension=0, tiled=True
        ).astype(jnp.float32),
    )
    k_grad, v_grad = (
        lax.psum_scatter(k_term, ("dp", "seq", "tensor"), scatter_dimension=0, tiled=True),
        lax.psum_scatter(v_term, ("dp", "seq", "tensor"), scatter_dimension=0, tiled=True),
    )
    q_bias_grad, k_bias_grad, v_bias_grad = lax.psum(
        (q_bias_term, k_bias_term, v_bias_term), ("dp", "seq", "tensor")
    )
    return (
        layer_out,
        token_grad,
        q_grad,
        q_bias_grad,
        k_grad,
        k_bias_grad,
        v_grad,
        v_bias_grad,
        o_grad,
        attn_gain_grad,
        ffn_gain_grad,
        gate_grad,
        up_grad,
        down_grad,
    )


def solution(mesh):
    in_specs = (
        P("dp", "seq", None),
        P("dp", None),
        P("dp", "seq", None),
        P(None, "tensor"),
        P("tensor"),
        P(),
        P(),
        P(),
        P(),
        P(None, "tensor"),
        P(),
        P(),
        P(None, "tensor"),
        P(None, "tensor"),
        P(None, "tensor"),
    )
    out_specs = (
        P("dp", "seq", None),
        P("dp", "seq", None),
        P(("dp", "seq"), "tensor"),
        P(),
        P(("dp", "seq", "tensor"), None),
        P(),
        P(("dp", "seq", "tensor"), None),
        P(),
        P(("dp", "seq"), "tensor"),
        P(("dp", "seq")),
        P(("dp", "seq")),
        P(("dp", "seq"), "tensor"),
        P(("dp", "seq"), "tensor"),
        P(("dp", "seq"), "tensor"),
    )
    return jax.shard_map(body, mesh=mesh, in_specs=in_specs, out_specs=out_specs, check_vma=False)
```

profile of v0, /device:TPU:0, one launch (start us, length us, event | category | flops | bytes accessed | tf_op | source)
XLA Modules:
  0.0 1334.4 jit_solution(9977446160524837445)
XLA Ops:
  19.8 3.2 convolution_add_fusion.1
  25.0 3.6 convolution_add_fusion
  31.2 3.8 copy.139
  50.5 28.0 %all-gather.5.cloned.1.call-done = bf16[2,2048,128]{2,1,0:T(8,128)(2,1)} async-done(((bf16[2,512,128]{2,1,0:T(8,128)(2,1)}), bf16[2,2048,128]{2,1,0:T(8,128)(2,1)}) %all-gather.5.cloned.1.call-update) | async-done | bytes 1048592 | tf_op jit(solution)/shard_map/all_gather | solution.py:147
  78.5 49.8 %while.28 = (s32[]{:T(128)}, bf16[2,512,3,128]{1,3,2,0:T(8,128)(2,1)}, f32[2,3,512]{2,1,0:T(4,128)}, bf16[2,2048,128]{2,1,0:T(8,128)(2,1)}, s32[2,512]{1,0:T(2,1...) while((s32[]{:T(128)}, ...), condition=%wide.region_7.8_spmd.clone, body=%wide.region_4.7_spmd.clone.sunk | while | flops 1651702784 | bytes 54458632 | solution.py:162
  80.2 7.0 fusion.190
  87.2 7.4 fusion.191
  94.7 7.0 fusion.192
  104.9 7.1 fusion.190
  112.0 7.4 fusion.191
  119.4 7.0 fusion.192
  131.6 3.5 convolution_convert_fusion.4
  135.3 4.1 fusion.83
  139.4 63.9 %all-reduce.9.cloned.1.call-done = bf16[1024,1536]{1,0:T(8,128)(2,1)} async-done(((bf16[1024,1536]{1,0:T(8,128)(2,1)}), bf16[1024,1536]{1,0:T(8,128)(2,1)}) %all-reduce.9.cloned.1.call-update) | async-done | bytes 3145744 | tf_op jit(solution)/shard_map/psum | solution.py:164
  203.2 4.1 multiply_reduce_fusion
  209.1 13.1 fusion.127
  222.2 9.7 fusion.126
  231.9 20.2 %multiply_convert_fusion = (bf16[1024,2240]{0,1:T(8,128)(2,1)}, bf16[1024,2240]{0,1:T(8,128)(2,1)}, bf16[1024,2240]{0,1:T(8,128)(2,1)}) fusion(f32[1024,2240]{0,1:T(8,128)} %fusion.126, f32[1024,2240]{0,1:T(8,128)} %fusion.127, bf16[1024,1536]{1,0:T(8,128)(2,1)S(1)} %copy-done.31, bf16[1536,2240]{0,1:T(8,128)(2,1)} %param.33), kind=kOutput, calls=%fused_computation.82 | convolution fusion | flops 7080837120 | bytes 42139648 | tf_op jit(solution)/shard_map/dot_general | solution.py:69
  252.1 11.9 fusion.128
  264.0 11.5 add_convert_fusion.1
  275.6 68.6 %all-reduce.11.cloned.1.call-done = bf16[1024,1536]{1,0:T(8,128)(2,1)} async-done(((bf16[1024,1536]{1,0:T(8,128)(2,1)}), bf16[1024,1536]{1,0:T(8,128)(2,1)}) %all-reduce.11.cloned.1.call-update) | async-done | bytes 3145744 | tf_op jit(solution)/shard_map/psum | solution.py:189
  344.2 6.9 fusion.81
  351.1 4.7 fusion.80
  360.7 53.7 %while.29 = (s32[]{:T(128)}, f32[2,512,3,128]{1,3,2,0:T(8,128)}, bf16[2,2048,128]{2,1,0:T(8,128)(2,1)}, bf16[2,2048,128]{2,1,0:T(8,128)(2,1)}, bf16[2,2048,128]{...) while((s32[]{:T(128)}, f32[2,512,3,128]{1,3,2,0:T(8,128)}, ...), condition=%wide.region_15.16_spmd.clone, body=%wide.region_13.15_spmd.clone.sunk | while | flops 4077321216 | bytes 132994376 | solution.py:220
  365.0 4.3 fusion.207
  369.3 7.0 fusion.203
  376.3 7.1 fusion.204
  391.6 4.3 fusion.207
  395.9 7.0 fusion.203
  403.0 7.1 fusion.204
  415.1 5.9 convolution_convert_fusion.5
  421.2 20.6 %reduce-scatter.10.cloned.1.call-done = bf16[2,512,128]{2,1,0:T(8,128)(2,1)} async-done(((bf16[2,2048,128]{2,1,0:T(8,128)(2,1)}), bf16[2,512,128]{2,1,0:T(8,128)(2,1)}) %reduce-scatter.10.cloned.1.call-update) | async-done | bytes 262160 | tf_op jit(solution)/shard_map/reduce_scatter | solution.py:224
  441.9 4.4 fusion.89
  451.1 19.5 %reduce-scatter.12.cloned.1.call-done = bf16[2,512,128]{2,1,0:T(8,128)(2,1)} async-done(((bf16[2,2048,128]{2,1,0:T(8,128)(2,1)}), bf16[2,512,128]{2,1,0:T(8,128)(2,1)}) %reduce-scatter.12.cloned.1.call-update) | async-done | bytes 262160 | tf_op jit(solution)/shard_map/reduce_scatter | solution.py:227
  478.9 12.5 convolution_convert_fusion.3
  500.9 12.4 convolution_convert_fusion
  513.4 12.3 convolution_convert_fusion.1
  525.8 12.3 convolution_convert_fusion.2
  565.7 39.2 %all-reduce.2 = (f32[1536]{0:T(1024)}, f32[256]{0:T(256)}, f32[256]{0:T(256)}) all-reduce(f32[1536]{0:T(1024)S(1)} %mul.447, f32[256]{0:T(256)S(1)} %get-tuple-element.408, f32[256]{0:T(256)S(1)} %get-tuple-element.407), channel_id=1, replica_groups=mesh['dp'=2,'seq'=4,'tensor'=4] {'dp','seq','tensor'}, use_global_device_ids=true, to_apply=%region_22.23 | all-reduce | flops 2048 | bytes 16384 | tf_op jit(solution)/shard_map/psum | solution.py:296
  608.2 116.7 %all-reduce.13.cloned.1.call-done = (bf16[1024,1536]{1,0:T(8,128)(2,1)}, bf16[1024,1536]{1,0:T(8,128)(2,1)}) async-done(((bf16[1024,1536]{1,0:T(8,128)(2,1)}, bf16[1024,1536]{1,0:T(8,128)(2,1)}), (bf16[1024,1536]{1,0:T(8,128)(2,1)}, bf16[1024,1536]{1,0:T(8,128)(2,1)})) %all-reduce.13.cloned.1.call-update) | async-done | bytes 6291472 | tf_op jit(solution)/shard_map/psum | solution.py:176
  724.9 4.1 fusion.82
  729.1 23.2 %all-reduce.3 = (bf16[1536]{0:T(1024)(128)(2,1)S(1)}, bf16[1536]{0:T(1024)(128)(2,1)S(1)}) all-reduce(bf16[1536]{0:T(1024)(128)(2,1)S(1)} %get-tuple-element.319, bf16[1536]{0:T(1024)(128)(2,1)S(1)} %copy-done.59), channel_id=8, replica_groups=mesh['dp'=2,'seq'=4,'tensor'=4] {'dp','seq'}, use_global_device_ids=true, to_apply=%region_31.32.clone | all-reduce | flops 3072 | bytes 12288
  753.5 11.3 fusion.77
  764.8 93.6 %reduce-scatter.26.cloned.1.call-done = bf16[192,2240]{1,0:T(8,128)(2,1)} async-done(((bf16[1536,2240]{1,0:T(8,128)(2,1)}), bf16[192,2240]{1,0:T(8,128)(2,1)}) %reduce-scatter.26.cloned.1.call-update) | async-done | bytes 860176 | tf_op jit(solution)/shard_map/reduce_scatter | solution.py:282
  860.9 129.8 %reduce-scatter.24.cloned.1.call-done = bf16[192,2240]{1,0:T(8,128)(2,1)} async-done(((bf16[1536,2240]{1,0:T(8,128)(2,1)}), bf16[192,2240]{1,0:T(8,128)(2,1)}) %reduce-scatter.24.cloned.1.call-update) | async-done | bytes 860176 | tf_op jit(solution)/shard_map/reduce_scatter | solution.py:279
  993.2 129.1 %reduce-scatter.22.cloned.1.call-done = bf16[192,2240]{1,0:T(8,128)(2,1)} async-done(((bf16[1536,2240]{1,0:T(8,128)(2,1)}), bf16[192,2240]{1,0:T(8,128)(2,1)}) %reduce-scatter.22.cloned.1.call-update) | async-done | bytes 860176 | tf_op jit(solution)/shard_map/reduce_scatter | solution.py:276
  1124.8 100.3 %reduce-scatter.18.cloned.1.call-done = f32[48,256]{1,0:T(8,128)} async-done(((f32[1536,256]{1,0:T(8,128)}), f32[48,256]{1,0:T(8,128)}) %reduce-scatter.18.cloned.1.call-update) | async-done | bytes 49168 | tf_op jit(solution)/shard_map/reduce_scatter | solution.py:294
  1225.1 102.6 %reduce-scatter.16.cloned.1.call-done = f32[48,256]{1,0:T(8,128)} async-done(((f32[1536,256]{1,0:T(8,128)}), f32[48,256]{1,0:T(8,128)}) %reduce-scatter.16.cloned.1.call-update) | async-done | bytes 49168 | tf_op jit(solution)/shard_map/reduce_scatter | solution.py:293
  (320 shorter events, 127.1 us)
Async XLA Ops:
  7.2 124.4 %copy-start = (bf16[1536,384]{1,0:T(8,128)(2,1)S(1)}, bf16[1536,384]{1,0:T(8,128)(2,1)}, u32[]{:S(2)}) copy-start(bf16[1536,384]{1,0:T(8,128)(2,1)} %param.28) | copy-start | bytes 3538948
  7.2 9.2 copy-start.50
  7.2 43.3 %all-gather.3.cloned.1.call-start = ((), (), s32[]{:S(2)}) async-start(), calls=%async_computation.9 | async-start | bytes 1310720 | tf_op jit(solution)/shard_map/all_gather | solution.py:148
  10.0 8.2 copy-start.63
  10.0 8.7 copy-start.66
  10.0 9.7 copy-start.43
  10.6 12.4 copy-start.56
  11.3 11.7 copy-start.48
  16.4 8.6 copy-start.65
  18.1 60.4 %all-gather.5.cloned.1.call-start = ((), (), s32[]{:S(2)}) async-start(), calls=%async_computation.10 | async-start | bytes 1310720 | tf_op jit(solution)/shard_map/all_gather | solution.py:147
  18.6 10.1 copy-start.58
  18.7 10.0 copy-start.64
  25.0 178.3 %all-reduce.9.cloned.1.call-start = ((), (), s32[]{:S(2)}) async-start(), calls=%async_computation.11 | async-start | bytes 6291456 | tf_op jit(solution)/shard_map/psum | solution.py:164
  36.3 11.9 copy-start.21
  87.2 7.4 copy-start.19
  87.2 7.4 copy-start.45
  111.9 7.4 copy-start.19
  111.9 7.4 copy-start.45
  135.2 209.1 %all-reduce.11.cloned.1.call-start = ((), (), s32[]{:S(2)}) async-start(), calls=%async_computation.12 | async-start | bytes 6291456 | tf_op jit(solution)/shard_map/psum | solution.py:189
  207.9 14.3 %slice-start = ((s8[6881280]{0:T(1024)(128)(4,1)}), s8[4194304]{0:T(1024)(128)(4,1)S(1)}, s32[]{:S(2)}) async-start(s8[6881280]{0:T(1024)(128)(4,1)} %bitcast.355), calls=%async_computation.23 | async-start | bytes 8388608
  209.1 13.1 copy-start.29
  209.1 13.1 slice-start.1
  222.2 9.7 copy-start.31
  252.1 11.9 copy-start.68
  275.6 166.3 %reduce-scatter.10.cloned.1.call-start = ((), (), s32[]{:S(2)}) async-start(), calls=%async_computation.13 | async-start | bytes 1310720 | tf_op jit(solution)/shard_map/reduce_scatter | solution.py:224
  376.3 7.1 copy-start.39
  402.9 7.1 copy-start.39
  414.5 56.1 %reduce-scatter.12.cloned.1.call-start = ((), (), s32[]{:S(2)}) async-start(), calls=%async_computation.14 | async-start | bytes 1310720 | tf_op jit(solution)/shard_map/reduce_scatter | solution.py:227
  415.0 26.8 %copy-start.49 = (f32[1536]{0:T(1024)S(1)}, f32[1536]{0:T(1024)}, u32[]{:S(2)}) copy-start(f32[1536]{0:T(1024)} %copy-done.48) | copy-start | bytes 18436
  415.1 26.8 %copy-start.61 = (f32[2,512]{1,0:T(2,128)S(1)}, f32[2,512]{1,0:T(2,128)}, u32[]{:S(2)}) copy-start(f32[2,512]{1,0:T(2,128)} %get-tuple-element.403) | copy-start | bytes 12292
  415.1 189.8 %reduce-scatter.20.cloned.1.call-start = ((), (), s32[]{:S(2)}) async-start(), calls=%async_computation.18 | async-start | bytes 1327104 | tf_op jit(solution)/shard_map/reduce_scatter | solution.py:273
  421.0 25.4 %copy-start.11 = (f32[2,512,3,128]{1,3,2,0:T(8,128)S(1)}, f32[2,512,3,128]{1,3,2,0:T(8,128)}, u32[]{:S(2)}) copy-start(f32[2,512,3,128]{1,3,2,0:T(8,128)} %get-tuple-element.138) | copy-start | bytes 4718596
  421.0 185.5 %reduce-scatter.14.cloned.1.call-start = ((), (), s32[]{:S(2)}) async-start(), calls=%async_computation.15 | async-start | bytes 1327104 | tf_op jit(solution)/shard_map/reduce_scatter | solution.py:270
  441.9 28.7 %collective-permute-start = (bf16[2,512,128]{2,1,0:T(8,128)(2,1)}, bf16[2,512,128]{2,1,0:T(8,128)(2,1)S(1)}, u32[]{:S(2)}, u32[]{:S(2)}) collective-permute-start(bf16[2,512,128]{2,1,0:T(8,128)(2,1)} %reduce-scatter.10.cloned.1.call-done), channel_id=1, source_target_pairs={{0,1},{1,0},{2,3},{3,2},{4,5},{5,4},{6,7},{7,6},{8,9},{9,8},{10,11... | collective-permute-start | bytes 786440 | tf_op jit(solution)/shard_map/ppermute | solution.py:24
  441.9 28.7 %copy-start.41 = (bf16[2,512,128]{2,1,0:T(8,128)(2,1)S(1)}, bf16[2,512,128]{2,1,0:T(8,128)(2,1)}, u32[]{:S(2)}) copy-start(bf16[2,512,128]{2,1,0:T(8,128)(2,1)} %reduce-scatter.10.cloned.1.call-done) | copy-start | bytes 786436
  441.9 29.6 %copy-start.35 = (f32[1024,64]{0,1:T(8,128)S(1)}, f32[1024,64]{0,1:T(8,128)}, u32[]{:S(2)}) copy-start(f32[1024,64]{0,1:T(8,128)} %copy-done.34) | copy-start | bytes 786436
  447.9 26.3 %copy-start.26 = (f32[1024,128]{0,1:T(8,128)S(1)}, f32[1024,128]{0,1:T(8,128)}, u32[]{:S(2)}) copy-start(f32[1024,128]{0,1:T(8,128)} %get-tuple-element.397) | copy-start | bytes 1572868
  470.6 22.9 %collective-permute-start.1 = (bf16[2,512,128]{2,1,0:T(8,128)(2,1)}, bf16[2,512,128]{2,1,0:T(8,128)(2,1)}, u32[]{:S(2)}, u32[]{:S(2)}) collective-permute-start(bf16[2,512,128]{2,1,0:T(8,128)(2,1)} %reduce-scatter.12.cloned.1.call-done), channel_id=1, source_target_pairs={{0,1},{1,0},{2,3},{3,2},{4,5},{5,4},{6,7},{7,6},{8,9},{9,8},{10,11... | collective-permute-start | bytes 786440 | tf_op jit(solution)/shard_map/ppermute | solution.py:24
  478.9 246.1 %all-reduce.13.cloned.1.call-start = ((), (), s32[]{:S(2)}) async-start(), calls=%async_computation.22 | async-start | bytes 12582912 | tf_op jit(solution)/shard_map/psum | solution.py:176
  500.5 358.0 %reduce-scatter.26.cloned.1.call-start = ((), (), s32[]{:S(2)}) async-start(), calls=%async_computation.21 | async-start | bytes 7962624 | tf_op jit(solution)/shard_map/reduce_scatter | solution.py:282
  513.3 477.4 %reduce-scatter.24.cloned.1.call-start = ((), (), s32[]{:S(2)}) async-start(), calls=%async_computation.20 | async-start | bytes 7962624 | tf_op jit(solution)/shard_map/reduce_scatter | solution.py:279
  525.7 596.6 %reduce-scatter.22.cloned.1.call-start = ((), (), s32[]{:S(2)}) async-start(), calls=%async_computation.19 | async-start | bytes 7962624 | tf_op jit(solution)/shard_map/reduce_scatter | solution.py:276
  538.1 687.0 %reduce-scatter.18.cloned.1.call-start = ((), (), s32[]{:S(2)}) async-start(), calls=%async_computation.17 | async-start | bytes 1622016 | tf_op jit(solution)/shard_map/reduce_scatter | solution.py:294
  552.2 775.5 %reduce-scatter.16.cloned.1.call-start = ((), (), s32[]{:S(2)}) async-start(), calls=%async_computation.16 | async-start | bytes 1622016 | tf_op jit(solution)/shard_map/reduce_scatter | solution.py:293
  555.1 8.0 copy-start.23
  558.2 166.7 %copy-start.57 = (f32[1,4,2,128]{3,1,2,0:T(4,128)S(1)}, f32[1,4,2,128]{3,1,2,0:T(4,128)}, u32[]{:S(2)}) copy-start(f32[1,4,2,128]{3,1,2,0:T(4,128)} %copy-done.56) | copy-start | bytes 12292
  563.1 166.0 %copy-start.59 = (bf16[1536]{0:T(1024)(128)(2,1)S(1)}, bf16[1536]{0:T(1024)(128)(2,1)}, u32[]{:S(2)}) copy-start(bf16[1536]{0:T(1024)(128)(2,1)} %get-tuple-element.317) | copy-start | bytes 9220
  753.5 574.2 %copy-start.1 = (bf16[1536,384]{1,0:T(8,128)(2,1)S(1)}, bf16[1536,384]{1,0:T(8,128)(2,1)}, u32[]{:S(2)}) copy-start(bf16[1536,384]{1,0:T(8,128)(2,1)} %param.28) | copy-start | bytes 3538948
  (50 other events, 160.9 us)
Sparse Core Ops, SparseCore 0:
  18.2 30.6 all-gather.2
  51.0 27.4 all-gather.4
  135.3 67.9 all-reduce.8
  275.7 68.4 all-reduce.10
  414.6 27.2 reduce-scatter.9
  444.7 25.8 reduce-scatter.11
  473.9 62.6 reduce-scatter.19
  540.0 63.0 reduce-scatter.13
  606.1 118.7 all-reduce.12
  728.4 129.9 reduce-scatter.25
  862.6 128.0 reduce-scatter.23
  994.3 128.0 reduce-scatter.21
  1129.0 96.0 reduce-scatter.17
  1231.6 96.0 reduce-scatter.15
where the time goes:
time: 1340 us; the launch traced here: 1330 us
  waiting for transfers between devices  873 us (65%)
  matrix products  213 us (16%)
  other arithmetic  116 us (9%)
  blocking collectives  62.4 us (5%)
  local copies, waits for them, and re-layouts  52 us (4%)
  between operations  15.7 us (1%)
    reduce_scatter x1, waiting for transfers between devices, body(): lax.psum_scatter(up_term.astype(jnp.bfloat16), ('dp', 'seq'), scatter_dim...  130 us
    reduce_scatter x1, waiting for transfers between devices, body(): lax.psum_scatter(gate_term.astype(jnp.bfloat16), ('dp', 'seq'), scatter_d...  129 us
    psum x1, waiting for transfers between devices, body(): lax.psum(matmul_nt(hidden, down_weight).astype(jnp.bfloat16), 'tensor')  117 us
    reduce_scatter x1, waiting for transfers between devices, body(): lax.psum_scatter(k_term, ('dp', 'seq', 'tensor'), scatter_dimension=0, ti...  103 us
    reduce_scatter x1, waiting for transfers between devices, body(): lax.psum_scatter(v_term, ('dp', 'seq', 'tensor'), scatter_dimension=0, ti...  100 us
    reduce_scatter x1, waiting for transfers between devices, body(): lax.psum_scatter(down_term.astype(jnp.bfloat16), ('dp', 'seq'), scatter_d...  93.6 us
    psum x1, waiting for transfers between devices, body(): lax.psum((matmul_nt(grad_gate, gate_weight) + matmul_nt(grad_up, up_weigh...  68.6 us
    psum x1, waiting for transfers between devices, body(): lax.psum(matmul_nt(mixed_flat, o_weight).astype(jnp.bfloat16), 'tensor')  63.9 us
  transfers between devices with their start and end apart: 16, of which 11 were waited for; matrix products, arithmetic and copies ran while one was open for 13% of the time, Pallas kernels for 0%

commit v1 on v0

v1 whole, which is shorter than its diff:
```python
import functools
import math

import jax
import jax.numpy as jnp
from jax import lax
from jax.experimental import pallas as pl
from jax.experimental.pallas import tpu as pltpu
from jax.sharding import PartitionSpec as P

KVH = 2
HD = 128
MOST = 1024
EPS = 1e-06
ROPE_BASE = 10000.0
NEG_FILL = -1e30
Q_BLOCK = 256
K_BLOCK = 256
MIB = 1 << 20
SCALE = 1.0 / math.sqrt(HD)


def to_bf(value):
    return value.astype(jnp.bfloat16)


def to_f(value):
    return value.astype(jnp.float32)


def dot(left, right, left_dim=1, right_dim=0):
    return lax.dot_general(
        left,
        right,
        (((left_dim,), (right_dim,)), ((), ())),
        preferred_element_type=jnp.float32,
    )


def flipped(axis, bit):
    return [(i, i ^ (1 << bit)) for i in range(lax.axis_size(axis))]


def core_swap(value):
    return lax.ppermute(value, "tensor", flipped("tensor", 0))


def chip_swap(value):
    return lax.ppermute(value, "tensor", flipped("tensor", 1))


def shifted(value, hops):
    count = lax.axis_size("seq")
    route = [(i, i + hops) for i in range(count) if 0 <= i + hops < count]
    return lax.ppermute(value, "seq", route)


def first_kernel(core_ref, tok_ref, gain_ref, w_ref, b_ref, cos_ref, sin_ref, h_ref, q_ref, kv_ref):
    x = to_f(tok_ref[...])
    factor = lax.rsqrt(jnp.mean(x * x, axis=-1, keepdims=True) + EPS)
    h = to_bf(x * factor * gain_ref[...])
    h_ref[...] = h
    lin = dot(h, w_ref[...]) + b_ref[...]
    cosine = cos_ref[...]
    sine = sin_ref[...]
    heads = q_ref.shape[1] // HD
    for head in range(heads):
        part = lin[:, head * HD : (head + 1) * HD]
        q_ref[:, head * HD : (head + 1) * HD] = to_bf(
            part * cosine + pltpu.roll(part, HD // 2, 1) * sine
        )
    part = lin[:, heads * HD :]
    is_key = core_ref[0] == 0
    kv_ref[...] = to_bf(
        part * jnp.where(is_key, cosine, 1.0)
        + pltpu.roll(part, HD // 2, 1) * jnp.where(is_key, sine, 0.0)
    )


def first(core, tokens, gain, weight, bias, cosine, sine):
    total, width = tokens.shape
    columns = weight.shape[1]
    block = total // 4
    half = 2

    def flip(i, core_ref):
        return (lax.rem(i + core_ref[0] * half, 4), 0)

    def at(i, core_ref):
        return (i, 0)

    def whole(i, core_ref):
        return (0, 0)

    return pl.pallas_call(
        first_kernel,
        grid_spec=pltpu.PrefetchScalarGridSpec(
            num_scalar_prefetch=1,
            grid=(4,),
            in_specs=[
                pl.BlockSpec((block, width), flip),
                pl.BlockSpec((1, width), whole),
                pl.BlockSpec((width, columns), whole),
                pl.BlockSpec((1, columns), whole),
                pl.BlockSpec((block, HD), at),
                pl.BlockSpec((block, HD), at),
            ],
            out_specs=[
                pl.BlockSpec((block, width), at),
                pl.BlockSpec((block, columns - HD), at),
                pl.BlockSpec((block, HD), at),
            ],
        ),
        out_shape=[
            jax.ShapeDtypeStruct((total, width), jnp.bfloat16),
            jax.ShapeDtypeStruct((total, columns - HD), jnp.bfloat16),
            jax.ShapeDtypeStruct((total, HD), jnp.bfloat16),
        ],
        compiler_params=pltpu.CompilerParams(vmem_limit_bytes=24 * MIB),
        cost_estimate=pl.CostEstimate(
            flops=2 * total * width * columns, bytes_accessed=9 * MIB, transcendentals=0
        ),
        name="first",
    )(core, tokens, gain, weight, bias, cosine, sine)


def stacked(ref, start, count, heads):
    return jnp.concatenate(
        [ref[0, pl.ds(start, count), h * HD : (h + 1) * HD] for h in range(heads)], axis=0
    )


def bounds(start_ref, index, heads, reach):
    first_key = jnp.concatenate(
        [start_ref[0, :, pl.ds(index * Q_BLOCK, Q_BLOCK)]] * heads, axis=1
    )
    place = reach + index * Q_BLOCK + lax.broadcasted_iota(jnp.int32, (1, Q_BLOCK), 1)
    return first_key, jnp.concatenate([place] * heads, axis=1)


def attend_kernel(heads, blocks, reach, low_ref, q_ref, k_ref, v_ref, start_ref, o_ref, lse_ref, acc):
    row = pl.program_id(0)
    wide = heads * Q_BLOCK
    for index in range(blocks):
        q = stacked(q_ref, index * Q_BLOCK, Q_BLOCK, heads)
        first_key, place = bounds(start_ref, index, heads, reach)
        acc[...] = jnp.zeros_like(acc)

        def step(j, carry):
            top, total = carry
            keys = pl.ds(pl.multiple_of(j * K_BLOCK, K_BLOCK), K_BLOCK)
            s = dot(k_ref[0, keys], q, 1, 1) * SCALE
            key = j * K_BLOCK + lax.broadcasted_iota(jnp.int32, (K_BLOCK, wide), 0)
            s = jnp.where((key >= first_key) & (key <= place), s, NEG_FILL)
            later = jnp.maximum(top, jnp.max(s, axis=0, keepdims=True))
            p = jnp.exp(s - later)
            fade = jnp.exp(top - later)
            total = total * fade + jnp.sum(p, axis=0, keepdims=True)
            acc[...] = acc[...] * fade + dot(v_ref[0, keys], to_bf(p), 0, 0)
            return later, total

        last = (reach + (index + 1) * Q_BLOCK - 1) // K_BLOCK + 1
        top, total = lax.fori_loop(
            low_ref[row, index],
            last,
            step,
            (jnp.full((1, wide), NEG_FILL, jnp.float32), jnp.zeros((1, wide), jnp.float32)),
        )
        out = to_bf((acc[...] / total).T)
        for h in range(heads):
            o_ref[0, index * Q_BLOCK : (index + 1) * Q_BLOCK, h * HD : (h + 1) * HD] = out[
                h * Q_BLOCK : (h + 1) * Q_BLOCK
            ]
        lse_ref[0, index : index + 1, :] = top + jnp.log(total)


def attend(low, q, k, v, start, reach):
    rows, local, columns = q.shape
    window = k.shape[1]
    heads = columns // HD
    blocks = local // Q_BLOCK

    def at(i, low_ref):
        return (i, 0, 0)

    return pl.pallas_call(
        functools.partial(attend_kernel, heads, blocks, reach),
        grid_spec=pltpu.PrefetchScalarGridSpec(
            num_scalar_prefetch=1,
            grid=(rows,),
            in_specs=[
                pl.BlockSpec((1, local, columns), at),
                pl.BlockSpec((1, window, HD), at),
                pl.BlockSpec((1, window, HD), at),
                pl.BlockSpec((1, 1, local), at),
            ],
            out_specs=[
                pl.BlockSpec((1, local, columns), at),
                pl.BlockSpec((1, blocks, heads * Q_BLOCK), at),
            ],
            scratch_shapes=[pltpu.VMEM((HD, heads * Q_BLOCK), jnp.float32)],
        ),
        out_shape=[
            jax.ShapeDtypeStruct((rows, local, columns), jnp.bfloat16),
            jax.ShapeDtypeStruct((rows, blocks, heads * Q_BLOCK), jnp.float32),
        ],
        compiler_params=pltpu.CompilerParams(vmem_limit_bytes=24 * MIB),
        cost_estimate=pl.CostEstimate(
            flops=12_000_000_000, bytes_accessed=4 * MIB, transcendentals=rows * local * window
        ),
        name="attend",
    )(low, q, k, v, start)


def attend_back_kernel(
    heads, blocks, reach, low_ref, core_ref, q_ref, k_ref, v_ref, g_ref, o_ref, lse_ref, start_ref, cos_ref,
    sin_ref, gq_ref, both_ref, acc, gk, gv
):
    row = pl.program_id(0)
    wide = heads * Q_BLOCK
    gk[...] = jnp.zeros_like(gk)
    gv[...] = jnp.zeros_like(gv)
    for index in range(blocks):
        q = stacked(q_ref, index * Q_BLOCK, Q_BLOCK, heads)
        g = stacked(g_ref, index * Q_BLOCK, Q_BLOCK, heads)
        o = stacked(o_ref, index * Q_BLOCK, Q_BLOCK, heads)
        inner = jnp.sum((to_f(g) * to_f(o)).T, axis=0, keepdims=True)
        lse = lse_ref[0, index : index + 1, :]
        first_key, place = bounds(start_ref, index, heads, reach)
        acc[...] = jnp.zeros_like(acc)

        def step(j, carry):
            keys = pl.ds(pl.multiple_of(j * K_BLOCK, K_BLOCK), K_BLOCK)
            k = k_ref[0, keys]
            s = dot(k, q, 1, 1) * SCALE
            key = j * K_BLOCK + lax.broadcasted_iota(jnp.int32, (K_BLOCK, wide), 0)
            p = jnp.where((key >= first_key) & (key <= place), jnp.exp(s - lse), 0.0)
            gp = dot(v_ref[0, keys], g, 1, 1)
            gs = to_bf(p * (gp - inner))
            gv[keys] += dot(to_bf(p), g)
            gk[keys] += dot(gs, q)
            acc[...] += dot(k, gs, 0, 0)
            return carry

        last = (reach + (index + 1) * Q_BLOCK - 1) // K_BLOCK + 1
        lax.fori_loop(low_ref[row, index], last, step, 0)
        gq = acc[...].T * SCALE
        here = slice(index * Q_BLOCK, (index + 1) * Q_BLOCK)
        cosine, sine = cos_ref[0, here], sin_ref[0, here]
        for h in range(heads):
            part = gq[h * Q_BLOCK : (h + 1) * Q_BLOCK]
            gq_ref[0, here, h * HD : (h + 1) * HD] = to_bf(
                part * cosine + pltpu.roll(part * sine, HD // 2, 1)
            )
    core = core_ref[0]
    both_ref[core, 0] = to_bf(gk[...] * SCALE)
    both_ref[1 - core, 0] = to_bf(gv[...])


def attend_back(low, core, q, k, v, grad, out, lse, start, cosine, sine, reach):
    rows, local, columns = q.shape
    window = k.shape[1]
    heads = columns // HD
    blocks = local // Q_BLOCK

    def at(i, *refs):
        return (i, 0, 0)

    return pl.pallas_call(
        functools.partial(attend_back_kernel, heads, blocks, reach),
        grid_spec=pltpu.PrefetchScalarGridSpec(
            num_scalar_prefetch=2,
            grid=(rows,),
            in_specs=[
                pl.BlockSpec((1, local, columns), at),
                pl.BlockSpec((1, window, HD), at),
                pl.BlockSpec((1, window, HD), at),
                pl.BlockSpec((1, local, columns), at),
                pl.BlockSpec((1, local, columns), at),
                pl.BlockSpec((1, blocks, heads * Q_BLOCK), at),
                pl.BlockSpec((1, 1, local), at),
                pl.BlockSpec((1, local, HD), at),
                pl.BlockSpec((1, local, HD), at),
            ],
            out_specs=[
                pl.BlockSpec((1, local, columns), at),
                pl.BlockSpec((2, 1, window, HD), lambda i, *refs: (0, i, 0, 0)),
            ],
            scratch_shapes=[
                pltpu.VMEM((HD, heads * Q_BLOCK), jnp.float32),
                pltpu.VMEM((window, HD), jnp.float32),
                pltpu.VMEM((window, HD), jnp.float32),
            ],
        ),
        out_shape=[
            jax.ShapeDtypeStruct((rows, local, columns), jnp.bfloat16),
            jax.ShapeDtypeStruct((2, rows, window, HD), jnp.bfloat16),
        ],
        compiler_params=pltpu.CompilerParams(vmem_limit_bytes=24 * MIB),
        cost_estimate=pl.CostEstimate(
            flops=20_000_000_000, bytes_accessed=6 * MIB, transcendentals=rows * local * window
        ),
        name="attend_back",
    )(low, core, q, k, v, grad, out, lse, start, cosine, sine)


def gated_kernel(h_ref, gh_ref, gw_ref, uw_ref, hid_ref, gg_ref, gu_ref):
    h = h_ref[...]
    gate = dot(h, gw_ref[...])
    up = dot(h, uw_ref[...])
    grad = to_f(gh_ref[...])
    sigma = 1.0 / (1.0 + jnp.exp(-gate))
    swish = gate * sigma
    hid_ref[...] = to_bf(swish * up)
    gu_ref[...] = to_bf(grad * swish)
    gg_ref[...] = to_bf(grad * up * sigma * (1.0 + gate * (1.0 - sigma)))


def gated(h, grad_hidden, gate_weight, up_weight):
    total, width = h.shape
    hidden = gate_weight.shape[1]
    tile = 256
    steps = pl.cdiv(hidden, tile)
    column = pl.BlockSpec((total, tile), lambda i: (0, i))
    weight = pl.BlockSpec((width, tile), lambda i: (0, i))
    shape = jax.ShapeDtypeStruct((total, hidden), jnp.bfloat16)
    return pl.pallas_call(
        gated_kernel,
        grid=(steps,),
        in_specs=[pl.BlockSpec((total, width), lambda i: (0, 0)), column, weight, weight],
        out_specs=[column] * 3,
        out_shape=[shape] * 3,
        compiler_params=pltpu.CompilerParams(vmem_limit_bytes=40 * MIB),
        cost_estimate=pl.CostEstimate(
            flops=4 * total * width * hidden, bytes_accessed=45 * MIB, transcendentals=total * hidden
        ),
        name="gated",
    )(h, grad_hidden, gate_weight, up_weight)


def tensor_sum(half_of):
    sent = core_swap(to_bf(half_of(1, None)))
    mine = to_bf(half_of(0, sent))
    return to_f(mine) + to_f(chip_swap(mine))


def rows_sum(left, right, dp_index, extra=None):
    count = lax.axis_size("dp")
    width = left.shape[1]
    if count != 2:
        whole = to_bf(dot(left, right, 0, 0))
        if extra is not None:
            share = jnp.concatenate(
                [whole.reshape(count, width // count, -1), jnp.broadcast_to(extra, (count,) + extra.shape)], axis=1
            )
            return lax.psum_scatter(share, "dp", scatter_dimension=0, tiled=False)
        return lax.psum_scatter(whole, "dp", scatter_dimension=0, tiled=True)
    part = width // 2
    other = lax.dynamic_slice_in_dim(left, (1 - dp_index) * part, part, 1)
    own = lax.dynamic_slice_in_dim(left, dp_index * part, part, 1)
    send = to_bf(dot(other, right, 0, 0))
    if extra is not None:
        send = jnp.concatenate([send, extra], axis=0)
    come = lax.ppermute(send, "dp", flipped("dp", 0))
    total = to_bf(dot(own, right, 0, 0) + to_f(come[:part]))
    if extra is not None:
        total = jnp.concatenate([total, to_bf(to_f(extra) + to_f(come[part:]))], axis=0)
    return total


def seq_scatter(value):
    return to_f(lax.psum_scatter(value, "seq", scatter_dimension=0, tiled=True))


def body(
    tokens,
    lengths,
    cotangent,
    q_weight,
    q_bias,
    k_weight,
    k_bias,
    v_weight,
    v_bias,
    o_weight,
    attn_gain,
    ffn_gain,
    gate_weight,
    up_weight,
    down_weight,
):
    rows, local, width = tokens.shape
    total = rows * local
    half = total // 2
    heads = q_weight.shape[1] // HD
    ranks = lax.axis_size("tensor")
    seqs = lax.axis_size("seq")
    rank = lax.axis_index("tensor")
    dp_index = lax.axis_index("dp")
    seq_index = lax.axis_index("seq")
    core = lax.rem(rank, 2)
    head = lax.div(rank, 2)
    core_one = core.reshape(1)
    hops = min(seqs - 1, -(-(MOST - 1) // local))
    reach = hops * local

    def own_first(value):
        turned = jnp.concatenate([value[rows // 2 :], value[: rows // 2]], axis=0)
        return jnp.where(core == 0, value, turned)

    slots = jnp.arange(lengths.shape[1], dtype=jnp.int32)
    lens = own_first(lengths)
    ends = jnp.sum(jnp.where(slots[None, :] <= slots[:, None], lens[:, None, :], 0), axis=2)
    place = seq_index * local + jnp.arange(local, dtype=jnp.int32)
    begun = jnp.max(
        jnp.where(ends[:, None, :] <= place[None, :, None], ends[:, None, :], 0), axis=2
    )
    valid = to_f(place[None, :] < ends[:, -2:-1])
    position = (place[None, :] - begun).reshape(total, 1)
    freqs = ROPE_BASE ** (-(jnp.arange(HD // 2, dtype=jnp.float32) * 2.0) / HD)
    angles = to_f(position) * freqs[None, :]
    cosine, sine = jnp.cos(angles), jnp.sin(angles)
    cosine = jnp.concatenate([cosine, cosine], axis=1)
    sine = jnp.concatenate([-sine, sine], axis=1)
    start = begun - (seq_index * local - reach)
    low = jnp.maximum(lax.div(jnp.maximum(start[:, ::Q_BLOCK], 0), K_BLOCK), 0)
    start = start.reshape(rows, 1, local)

    key_side = core == 0
    kv_weight = jnp.where(
        key_side,
        lax.dynamic_slice_in_dim(k_weight, head * HD, HD, 1),
        lax.dynamic_slice_in_dim(v_weight, head * HD, HD, 1),
    )
    kv_bias = jnp.where(
        key_side,
        lax.dynamic_slice_in_dim(k_bias, head * HD, HD, 0),
        lax.dynamic_slice_in_dim(v_bias, head * HD, HD, 0),
    )
    weight = jnp.concatenate([q_weight, kv_weight], axis=1)
    bias = to_f(jnp.concatenate([q_bias, kv_bias])).reshape(1, -1)
    gain_one = to_f(attn_gain).reshape(1, width)
    gain_two = to_f(ffn_gain).reshape(1, width)

    h_one, q_rot, kv = first(
        core_one, tokens.reshape(total, width), gain_one, weight, bias, cosine, sine
    )
    kv = kv.reshape(rows, local, HD)
    span = jnp.concatenate([shifted(kv, h) for h in range(hops, 0, -1)] + [kv], axis=1)
    mate = core_swap(span)
    mate = jnp.concatenate([mate[rows // 2 :], mate[: rows // 2]], axis=0)
    k_span = jnp.where(key_side, span, mate)
    v_span = jnp.where(key_side, mate, span)
    q_rows = q_rot.reshape(rows, local, heads * HD)
    mixed_rows, lse = attend(low, q_rows, k_span, v_span, start, reach)
    mixed = mixed_rows.reshape(total, heads * HD)

    grad_out = to_f(cotangent) * valid_rows(valid, core, rows)[:, :, None]
    grad_out = own_first(grad_out).reshape(total, width)
    grad_ffn = to_bf(grad_out)

    def branch_half(index, extra):
        out = dot(mixed[index * half : (index + 1) * half], o_weight, 1, 1)
        return out if extra is None else out + to_f(extra)

    branch = tensor_sum(branch_half)
    mine = to_f(lax.dynamic_slice_in_dim(tokens, core * (rows // 2), rows // 2, 0)).reshape(half, width)
    grad_mine = grad_out[:half]
    middle = mine + branch
    factor_two = lax.rsqrt(jnp.mean(middle * middle, axis=-1, keepdims=True) + EPS)
    normed_two = middle * factor_two
    h_two_mine = to_bf(normed_two * gain_two)
    h_two = jnp.concatenate([h_two_mine, core_swap(h_two_mine)], axis=0)

    grad_hidden = to_bf(dot(grad_ffn, down_weight))
    hidden, grad_gate, grad_up = gated(h_two, grad_hidden, gate_weight, up_weight)

    down_rows = rows_sum(grad_ffn, hidden, dp_index)
    down_grad = seq_scatter(down_rows)

    def grad_half(index, extra):
        here = slice(index * half, (index + 1) * half)
        out = dot(grad_gate[here], gate_weight, 1, 1) + dot(grad_up[here], up_weight, 1, 1)
        return out if extra is None else out + to_f(extra)

    grad_h_two = tensor_sum(grad_half)
    gate_rows = rows_sum(h_two, grad_gate, dp_index)
    up_rows = rows_sum(h_two, grad_up, dp_index)
    gate_grad = seq_scatter(gate_rows)
    up_grad = seq_scatter(up_rows)

    weighted = grad_h_two * gain_two
    inner = jnp.mean(weighted * normed_two, axis=-1, keepdims=True)
    grad_middle = grad_mine + factor_two * (weighted - normed_two * inner)
    branch_mine = to_bf(grad_middle)
    grad_branch = jnp.concatenate([branch_mine, core_swap(branch_mine)], axis=0)
    grad_mixed = to_bf(dot(grad_branch, o_weight)).reshape(rows, local, heads * HD)
    out_rows = rows_sum(grad_branch, mixed, dp_index)
    o_grad = seq_scatter(out_rows)

    grad_q_rows, both = attend_back(
        low,
        core_one,
        q_rows,
        k_span,
        v_span,
        grad_mixed,
        mixed_rows,
        lse,
        start,
        cosine.reshape(rows, local, HD),
        sine.reshape(rows, local, HD),
        reach,
    )
    come = core_swap(both[1])
    come = jnp.concatenate([come[rows // 2 :], come[: rows // 2]], axis=0)
    span_grad = to_f(both[0]) + to_f(come)
    grad_kv = span_grad[:, reach:]
    for h in range(1, hops + 1):
        there = to_bf(span_grad[:, reach - h * local : reach - (h - 1) * local])
        grad_kv = grad_kv + to_f(shifted(there, -h))
    grad_kv = grad_kv.reshape(total, HD)
    turned = grad_kv * sine
    turned = jnp.concatenate([turned[:, HD // 2 :], turned[:, : HD // 2]], axis=1)
    grad_kv = to_bf(jnp.where(key_side, grad_kv * cosine + turned, grad_kv))
    grad_qkv = jnp.concatenate([grad_q_rows.reshape(total, heads * HD), grad_kv], axis=1)

    bias_sum = jnp.sum(to_f(grad_qkv), axis=0, keepdims=True)
    bias_high = to_bf(bias_sum)
    bias_low = to_bf(bias_sum - to_f(bias_high))
    pad = 16
    bias_rows = jnp.concatenate(
        [bias_high, bias_low, jnp.zeros((pad - 2, bias_sum.shape[1]), jnp.bfloat16)], axis=0
    )
    qkv_rows = rows_sum(h_one, grad_qkv, dp_index)
    qkv_grad = seq_scatter(qkv_rows)

    def one_half(index, extra):
        out = dot(grad_qkv[index * half : (index + 1) * half], weight, 1, 1)
        return out if extra is None else out + to_f(extra)

    grad_h_one = tensor_sum(one_half)
    factor_one = lax.rsqrt(jnp.mean(mine * mine, axis=-1, keepdims=True) + EPS)
    normed_one = mine * factor_one
    weighted = grad_h_one * gain_one
    inner = jnp.mean(weighted * normed_one, axis=-1, keepdims=True)
    token_mine = grad_middle + factor_one * (weighted - normed_one * inner)
    token_mate = core_swap(token_mine)
    token_grad = jnp.where(
        key_side,
        jnp.concatenate([token_mine, token_mate], axis=0),
        jnp.concatenate([token_mate, token_mine], axis=0),
    ).reshape(rows, local, width)

    def ffn_half(index, extra):
        out = dot(hidden[index * half : (index + 1) * half], down_weight, 1, 1)
        return out if extra is None else out + to_f(extra)

    layer_mine = to_bf(middle + tensor_sum(ffn_half))
    layer_mate = core_swap(layer_mine)
    layer_out = jnp.where(
        key_side,
        jnp.concatenate([layer_mine, layer_mate], axis=0),
        jnp.concatenate([layer_mate, layer_mine], axis=0),
    ).reshape(rows, local, width)

    share = qkv_grad.shape[0]
    begin = (dp_index * seqs + seq_index) * share

    def rows_of(value):
        return to_f(lax.dynamic_slice_in_dim(value, begin, share, 0))

    attn_term = jnp.sum(rows_of(weight) * qkv_grad, axis=1)
    ffn_term = jnp.sum(rows_of(gate_weight) * gate_grad + rows_of(up_weight) * up_grad, axis=1)
    ffn_gain_grad, attn_gain_grad = lax.psum((ffn_term, attn_term), "tensor")
    attn_gain_grad = attn_gain_grad / lax.dynamic_slice_in_dim(gain_one[0], begin, share, 0)
    ffn_gain_grad = ffn_gain_grad / lax.dynamic_slice_in_dim(gain_two[0], begin, share, 0)
    q_grad = qkv_grad[:, : heads * HD]
    kv_parts = lax.all_to_all(qkv_grad[:, heads * HD :], "tensor", 0, 0, tiled=True)
    kv_parts = kv_parts.reshape(KVH, 2, share // ranks, HD)
    k_grad = jnp.concatenate([kv_parts[i, 0] for i in range(KVH)], axis=1)
    v_grad = jnp.concatenate([kv_parts[i, 1] for i in range(KVH)], axis=1)
    rank_pick = to_f(jnp.arange(ranks, dtype=jnp.int32) == rank)
    bias_all = lax.psum(rank_pick[:, None] * bias_sum, ("dp", "seq", "tensor"))
    q_bias_grad = bias_all[:, : heads * HD].reshape(-1)
    kv_bias = bias_all[:, heads * HD :].reshape(KVH, 2, HD)
    k_bias_grad = kv_bias[:, 0].reshape(-1)
    v_bias_grad = kv_bias[:, 1].reshape(-1)
    return (
        layer_out,
        token_grad,
        q_grad,
        q_bias_grad,
        k_grad,
        k_bias_grad,
        v_grad,
        v_bias_grad,
        o_grad,
        attn_gain_grad,
        ffn_gain_grad,
        gate_grad,
        up_grad,
        down_grad,
    )


def valid_rows(valid, core, rows):
    turned = jnp.concatenate([valid[rows // 2 :], valid[: rows // 2]], axis=0)
    return jnp.where(core == 0, valid, turned)


def solution(mesh):
    in_specs = (
        P("dp", "seq", None),
        P("dp", None),
        P("dp", "seq", None),
        P(None, "tensor"),
        P("tensor"),
        P(),
        P(),
        P(),
        P(),
        P(None, "tensor"),
        P(),
        P(),
        P(None, "tensor"),
        P(None, "tensor"),
        P(None, "tensor"),
    )
    out_specs = (
        P("dp", "seq", None),
        P("dp", "seq", None),
        P(("dp", "seq"), "tensor"),
        P(),
        P(("dp", "seq", "tensor"), None),
        P(),
        P(("dp", "seq", "tensor"), None),
        P(),
        P(("dp", "seq"), "tensor"),
        P(("dp", "seq")),
        P(("dp", "seq")),
        P(("dp", "seq"), "tensor"),
        P(("dp", "seq"), "tensor"),
        P(("dp", "seq"), "tensor"),
    )
    return jax.shard_map(body, mesh=mesh, in_specs=in_specs, out_specs=out_specs, check_vma=False)
```

time: 1340 us -> 768 us (0.57)
  waiting for transfers between devices: 873 us -> 386 us
  matrix products: 213 us -> 116 us
  other arithmetic: 116 us -> 57.2 us
  Pallas kernels: 0 us -> 38.2 us
  starting transfers between devices: 1.34 us -> 30 us
    reduce_scatter x9 -> x5, waiting for transfers between devices: 596 us -> 0.01 us  [seq_scatter(): return to_f(lax.psum_scatter(value, 'seq', scatter_dimension=0, tiled=True))]
    ppermute x2 -> x23, waiting for transfers between devices: 0.01 us -> 385 us  [the longest x5 243 us: rows_sum(): come = lax.ppermute(send, 'dp', flipped('dp', 0))]
    psum x3 -> x0, waiting for transfers between devices: 249 us -> none  [the longest x1 117 us: body(): lax.psum(matmul_nt(hidden, down_weight).astype(jnp.bfloat16), 'tensor')]
    dot_general x35 -> x22, matrix products: 213 us -> 116 us  [dot(): lax.dot_general(left, right, (((left_dim,), (right_dim,)), ((), ())), pre...]
    pallas_call x0 -> x4, Pallas kernels: none -> 38.2 us  [the longest x1 22.7 us: gated(): pl.pallas_call(gated_kernel, grid=(steps,), in_specs=[pl.BlockSpec((total...]
    all_gather x2 -> x0, waiting for transfers between devices: 28 us -> none  [the longest x1 28 us: body(): lax.all_gather(k_rot, 'seq', axis=1, tiled=True)]
    reduce_sum x10 -> x6, other arithmetic: 34.1 us -> 7.5 us  [the longest x1 4.21 us: body(): jnp.sum(rows_of(gate_weight) * gate_grad + rows_of(up_weight) * up_grad,...]
    ppermute x2 -> x23, starting transfers between devices: 0.01 us -> 26.1 us  [the longest x4 12.3 us: shifted(): return lax.ppermute(value, 'seq', route)]
  transfers between devices with their start and end apart: 16 -> 29, of which waited for: 11 -> 14; matrix products, arithmetic and copies ran while one was open for 13% -> 23% of each run, Pallas kernels for 0% -> 0%
where the time goes in v1:
time: 768 us; the launch traced here: 763 us
  waiting for transfers between devices  386 us (50%)
  matrix products  116 us (15%)
  blocking collectives  61.8 us (8%)
  local copies, waits for them, and re-layouts  58.9 us (8%)
  other arithmetic  57.2 us (7%)
  Pallas kernels  38.2 us (5%)
  starting transfers between devices  30 us (4%)
  between operations  14.9 us (2%)
    ppermute x5, waiting for transfers between devices, rows_sum(): come = lax.ppermute(send, 'dp', flipped('dp', 0))  243 us
    ppermute x4, waiting for transfers between devices, chip_swap(): return lax.ppermute(value, 'tensor', flipped('tensor', 1))  129 us
    dot_general x22, matrix products, dot(): lax.dot_general(left, right, (((left_dim,), (right_dim,)), ((), ())), pre...  116 us
    psum x1, blocking collectives, body(): bias_all = lax.psum(rank_pick[:, None] * bias_sum, ('dp', 'seq', 'tensor'))  55.9 us
    unnamed x111, local copies, waits for them, and re-layouts  25.6 us
    pallas_call x1, Pallas kernels, gated(): pl.pallas_call(gated_kernel, grid=(steps,), in_specs=[pl.BlockSpec((total...  22.7 us
    ppermute x3, local copies, waits for them, and re-layouts, rows_sum(): come = lax.ppermute(send, 'dp', flipped('dp', 0))  17.1 us
  transfers between devices with their start and end apart: 29, of which 14 were waited for; matrix products, arithmetic and copies ran while one was open for 23% of the time, Pallas kernels for 0%

profile of v1, /device:TPU:0, one launch (start us, length us, event | category | flops | bytes accessed | tf_op | source)
XLA Modules:
  0.0 763.3 jit_solution(10346191695303360809)
XLA Ops:
  11.1 3.0 fusion.70
  17.9 3.6 first.1
  23.1 5.9 collective-permute-start
  29.0 3.7 collective-permute-start.1
  32.7 3.1 collective-permute-done
  35.8 3.8 collective-permute-done.1
  44.6 4.7 attend.1
  59.8 3.7 fusion.93
  63.5 30.8 %collective-permute-done.4 = bf16[512,1536]{1,0:T(8,128)(2,1)S(1)} collective-permute-done((bf16[512,1536]{1,0:T(8,128)(2,1)S(1)}, bf16[512,1536]{1,0:T(8,128)(2,1)S(1)}, u32[]{:S(2)}, u32[]{:S(2)}) %collective-permute-start.4) | collective-permute-done | bytes 1572896 | tf_op jit(solution)/shard_map/ppermute | solution.py:49
  99.0 8.9 %convolution_convert_fusion = bf16[1024,2240]{0,1:T(8,128)(2,1)} fusion(bf16[1024,1536]{1,0:T(8,128)(2,1)S(1)} %bitcast.101, bf16[1536,2240]{0,1:T(8,128)(2,1)S(1)} %bitcast.112), kind=kOutput, calls=%fused_computation.6 | convolution fusion | flops 7048724480 | bytes 14614528 | tf_op jit(solution)/shard_map/dot_general | solution.py:32
  107.9 6.6 copy.63.gh_ref
  114.6 10.2 %copy.64.gw_ref = bf16[1536,2240]{1,0:T(8,128)(2,1)} copy(bf16[1536,2240]{0,1:T(8,128)(2,1)} %param.27) | data formatting | bytes 13762560 | tf_op args[12]
  124.8 9.6 %copy.65.uw_ref = bf16[1536,2240]{1,0:T(8,128)(2,1)} copy(bf16[1536,2240]{0,1:T(8,128)(2,1)} %param.28) | data formatting | bytes 13762560 | tf_op args[13]
  136.6 22.7 %gated.1 = (bf16[1024,2240]{1,0:T(8,128)(2,1)S(1)}, bf16[1024,2240]{1,0:T(8,128)(2,1)S(1)}, bf16[1024,2240]{1,0:T(8,128)(2,1)}) custom-call(bf16[1024,1536]{1,0:T(8,128)(2,1)S(1)} %pad_maximum_fusion.h_ref, bf16[1024,2240]{1,0:T(8,128)(2,1)} %copy.63.gh_ref, bf16[1536,2240]{1,0:T(8,128)(2,1)} %copy.64.gw_ref, bf16[1536,2240]{1,0:T(8,128)(2,1)} %copy.65.uw_ref), custom_call_target="tpu_custom_call" | custom-call | flops 14092861440 | bytes 47185920 | tf_op jit(solution)/shard_map/gated/pallas_call | solution.py:327
  159.4 7.4 fusion.12
  166.8 6.9 fusion.11
  174.3 3.8 convolution_convert_fusion.5
  178.2 7.3 fusion.15
  185.5 8.1 %fusion.10 = bf16[512,1536]{1,0:T(8,128)(2,1)S(1)} fusion(bf16[512,1536]{1,0:T(8,128)(2,1)} %collective-permute-done.9, f32[512,1536]{1,0:T(8,128)} %fusion.15, bf16[1536,2240]{0,1:T(8,128)(2,1)} %param.27, bf16[1024,2240]{1,0:T(8,128)(2,1)S(1)} %get-tuple-element.28), kind=kOutput, calls=%fused_computation.47 | convolution fusion | flops 3526361088 | bytes 15532032 | tf_op jit(solution)/shard_map/dot_general | solution.py:32
  195.2 3.8 add_convert_fusion.5
  199.7 31.3 %collective-permute-done.10 = bf16[512,1536]{1,0:T(8,128)(2,1)S(1)} collective-permute-done((bf16[512,1536]{1,0:T(8,128)(2,1)S(1)}, bf16[512,1536]{1,0:T(8,128)(2,1)S(1)}, u32[]{:S(2)}, u32[]{:S(2)}) %collective-permute-start.10) | collective-permute-done | bytes 1572896 | tf_op jit(solution)/shard_map/ppermute | solution.py:49
  231.8 32.4 %collective-permute-done.7 = bf16[512,1536]{1,0:T(8,128)(2,1)S(1)} collective-permute-done((bf16[512,1536]{1,0:T(8,128)(2,1)S(1)}, bf16[512,1536]{1,0:T(8,128)(2,1)S(1)}, u32[]{:S(2)}, u32[]{:S(2)}) %collective-permute-start.7) | collective-permute-done | bytes 1572896 | tf_op jit(solution)/shard_map/ppermute | solution.py:49
  264.2 4.4 fusion.91
  272.4 3.8 fusion.39
  276.2 7.1 attend_back.1
  283.7 5.4 convolution_convert_fusion.1
  298.5 80.1 %collective-permute-done.19 = bf16[768,384]{1,0:T(8,128)(2,1)S(1)} collective-permute-done((bf16[768,384]{1,0:T(8,128)(2,1)S(1)}, bf16[768,384]{1,0:T(8,128)(2,1)S(1)}, u32[]{:S(2)}, u32[]{:S(2)}) %collective-permute-start.19) | collective-permute-done | bytes 589856 | tf_op jit(solution)/shard_map/ppermute | solution.py:364
  378.6 3.2 fusion.46
  388.2 17.4 %collective-permute-done.18 = bf16[768,512]{1,0:T(8,128)(2,1)S(1)} collective-permute-done((bf16[768,512]{1,0:T(8,128)(2,1)S(1)}, bf16[768,512]{1,0:T(8,128)(2,1)S(1)}, u32[]{:S(2)}, u32[]{:S(2)}) %collective-permute-start.18) | collective-permute-done | bytes 786464 | tf_op jit(solution)/shard_map/ppermute | solution.py:364
  407.6 5.7 copy.70
  413.3 9.6 %add_convert_fusion = bf16[768,2240]{1,0:T(8,128)(2,1)} fusion(bf16[768,2240]{1,0:T(8,128)(2,1)} %copy.70, bf16[1024,2240]{1,0:T(8,128)(2,1)} %copy-done.12, bf16[1024,1536]{1,0:T(8,128)(2,1)} %bitcast.102, s32[]{:T(128)S(6)} %select_n.148), kind=kOutput, calls=%fused_computation | convolution fusion | flops 3528376320 | bytes 13271044 | tf_op jit(solution)/shard_map/dot_general | solution.py:32
  422.9 6.6 convolution_convert_fusion.2
  431.2 73.5 %collective-permute-done.21 = bf16[768,2240]{0,1:T(8,128)(2,1)} collective-permute-done((bf16[768,2240]{0,1:T(8,128)(2,1)S(1)}, bf16[768,2240]{0,1:T(8,128)(2,1)}, u32[]{:S(2)}, u32[]{:S(2)}) %collective-permute-start.21) | collective-permute-done | bytes 3440672 | tf_op jit(solution)/shard_map/ppermute | solution.py:364
  504.7 5.6 copy.69
  510.4 9.7 %add_convert_fusion.1 = bf16[768,2240]{1,0:T(8,128)(2,1)} fusion(bf16[768,2240]{1,0:T(8,128)(2,1)} %copy.69, bf16[1024,2240]{1,0:T(8,128)(2,1)} %get-tuple-element.29, s32[]{:T(128)S(6)} %select_n.148, bf16[512,1536]{1,0:T(8,128)(2,1)} %multiply_convert_fusion, bf16[512,1536]{1,0:T(8,128)(2,1)} %collective-permute-done.5), kind=kOutput, calls=%fused_computation.1 | convolution fusion | flops 3531522048 | bytes 14614532 | tf_op jit(solution)/shard_map/dot_general | solution.py:32
  520.1 6.6 convolution_convert_fusion.3
  528.5 72.5 %collective-permute-done.20 = bf16[768,2240]{0,1:T(8,128)(2,1)} collective-permute-done((bf16[768,2240]{0,1:T(8,128)(2,1)S(1)}, bf16[768,2240]{0,1:T(8,128)(2,1)}, u32[]{:S(2)}, u32[]{:S(2)}) %collective-permute-start.20) | collective-permute-done | bytes 3440672 | tf_op jit(solution)/shard_map/ppermute | solution.py:364
  601.0 5.8 copy.67
  606.8 3.2 convolution_convert_fusion.4
  610.0 8.6 %add_convert_fusion.2 = bf16[768,2240]{1,0:T(8,128)(2,1)} fusion(bf16[768,2240]{1,0:T(8,128)(2,1)S(1)} %copy-done.26, bf16[1024,2240]{1,0:T(8,128)(2,1)} %copy-done.15, s32[]{:T(128)S(6)} %select_n.148, bf16[512,1536]{1,0:T(8,128)(2,1)} %multiply_convert_fusion, bf16[512,1536]{1,0:T(8,128)(2,1)} %collective-permute-done.5), kind=kOutput, calls=%fused_computation.2 | convolution fusion | flops 3531522048 | bytes 14614532 | tf_op jit(solution)/shard_map/dot_general | solution.py:32
  618.8 3.1 add_convert_fusion.3
  623.8 35.0 %collective-permute-done.16 = bf16[512,1536]{1,0:T(8,128)(2,1)S(1)} collective-permute-done((bf16[512,1536]{1,0:T(8,128)(2,1)S(1)}, bf16[512,1536]{1,0:T(8,128)(2,1)S(1)}, u32[]{:S(2)}, u32[]{:S(2)}) %collective-permute-start.16) | collective-permute-done | bytes 1572896 | tf_op jit(solution)/shard_map/ppermute | solution.py:49
  662.5 3.5 maximum_select_fusion.2
  666.3 55.9 %psum.21 = f32[4,512]{1,0:T(4,128)S(1)} all-reduce(f32[4,512]{1,0:T(4,128)S(1)} %broadcast_multiply_fusion), channel_id=1, replica_groups=mesh['dp'=2,'seq'=4,'tensor'=4] {'dp','seq','tensor'}, use_global_device_ids=true, to_apply=%region_8.9 | all-reduce | flops 2048 | bytes 16384 | tf_op jit(solution)/shard_map/psum | solution.py:584
  726.4 3.5 all-to-all-start
  738.0 4.2 add_reduce_fusion
  742.2 5.9 all-reduce
  749.4 7.1 maximum_select_fusion.1
  (236 shorter events, 79.9 us)
Async XLA Ops:
  7.2 42.2 %copy-start = (bf16[1536,384]{1,0:T(8,128)(2,1)S(1)}, bf16[1536,384]{1,0:T(8,128)(2,1)}, u32[]{:S(2)}) copy-start(bf16[1536,384]{1,0:T(8,128)(2,1)} %param.24) | copy-start | bytes 3538948
  7.2 716.1 %reduce-scatter.8.cloned.1.call-start = ((), (), s32[]{:S(2)}) async-start(), calls=%async_computation.7 | async-start | bytes 737280 | tf_op jit(solution)/shard_map/reduce_scatter | solution.py:372
  16.3 24.2 %copy-start.4 = (f32[1024,128]{1,0:T(8,128)}, f32[1024,128]{1,0:T(8,128)S(1)}, u32[]{:S(2)}) copy-start(f32[1024,128]{1,0:T(8,128)S(1)} %get-tuple-element.80.sin_ref) | copy-start | bytes 1572868
  23.1 21.5 %copy-start.10 = (bf16[1024,384]{1,0:T(8,128)(2,1)}, bf16[1024,384]{1,0:T(8,128)(2,1)S(1)}, u32[]{:S(2)}) copy-start(bf16[1024,384]{1,0:T(8,128)(2,1)S(1)} %get-tuple-element.24) | copy-start | bytes 2359300
  23.1 12.7 %collective-permute-start = (bf16[2,512,128]{2,1,0:T(8,128)(2,1)S(1)}, bf16[2,512,128]{2,1,0:T(8,128)(2,1)S(1)}, u32[]{:S(2)}, u32[]{:S(2)}) collective-permute-start(bf16[2,512,128]{2,1,0:T(8,128)(2,1)S(1)} %bitcast.80), channel_id=1, source_target_pairs={{0,8},{4,12},{1,9},{5,13},{2,10},{6,14},{3,11},{7,15},{16,24},{20,... | collective-permute-start | bytes 786440 | tf_op jit(solution)/shard_map/ppermute | solution.py:55
  29.0 10.5 %collective-permute-start.1 = (bf16[2,512,128]{2,1,0:T(8,128)(2,1)S(1)}, bf16[2,512,128]{2,1,0:T(8,128)(2,1)S(1)}, u32[]{:S(2)}, u32[]{:S(2)}) collective-permute-start(bf16[2,512,128]{2,1,0:T(8,128)(2,1)S(1)} %bitcast.81), channel_id=1, source_target_pairs={{0,4},{4,8},{8,12},{1,5},{5,9},{9,13},{2,6},{6,10},{10,14},{3,7},{... | collective-permute-start | bytes 786440 | tf_op jit(solution)/shard_map/ppermute | solution.py:55
  40.5 2.6 collective-permute-start.2
  51.6 3.8 collective-permute-start.3
  57.8 36.5 %collective-permute-start.4 = (bf16[512,1536]{1,0:T(8,128)(2,1)S(1)}, bf16[512,1536]{1,0:T(8,128)(2,1)S(1)}, u32[]{:S(2)}, u32[]{:S(2)}) collective-permute-start(bf16[512,1536]{1,0:T(8,128)(2,1)S(1)} %add_convert_fusion.6), channel_id=1, source_target_pairs={{0,2},{1,3},{2,0},{3,1},{4,6},{5,7},{6,4},{7,5},{8,10},{9,11},{10,... | collective-permute-start | bytes 4718600 | tf_op jit(solution)/shard_map/ppermute | solution.py:49
  59.3 39.6 %slice-start.6 = ((s8[6881280]{0:T(1024)(128)(4,1)}), s8[4194304]{0:T(1024)(128)(4,1)S(1)}, s32[]{:S(2)}) async-start(s8[6881280]{0:T(1024)(128)(4,1)} %bitcast.111), calls=%async_computation.17 | async-start | bytes 8388608
  59.8 34.5 %copy-start.2 = (bf16[2,512,1536]{2,1,0:T(8,128)(2,1)S(1)}, bf16[2,512,1536]{2,1,0:T(8,128)(2,1)}, u32[]{:S(2)}) copy-start(bf16[2,512,1536]{2,1,0:T(8,128)(2,1)} %param.15) | copy-start | bytes 9437188
  59.8 39.2 %slice-start.7 = ((s8[6881280]{0:T(1024)(128)(4,1)}), s8[2686976]{0:T(1024)(128)(4,1)S(1)}, s32[]{:S(2)}) async-start(s8[6881280]{0:T(1024)(128)(4,1)} %bitcast.111), calls=%async_computation.18 | async-start | bytes 5373952
  63.5 35.5 %copy-start.27 = (bf16[2,512,1536]{2,1,0:T(8,128)(2,1)}, bf16[2,512,1536]{2,1,0:T(8,128)(2,1)S(1)}, u32[]{:S(2)}) copy-start(bf16[2,512,1536]{2,1,0:T(8,128)(2,1)S(1)} %get-tuple-element.41) | copy-start | bytes 9437188
  99.0 35.4 %collective-permute-start.5 = (bf16[512,1536]{1,0:T(8,128)(2,1)}, bf16[512,1536]{1,0:T(8,128)(2,1)}, u32[]{:S(2)}, u32[]{:S(2)}) collective-permute-start(bf16[512,1536]{1,0:T(8,128)(2,1)} %multiply_convert_fusion), channel_id=1, source_target_pairs={{0,1},{1,0},{2,3},{3,2},{4,5},{5,4},{6,7},{7,6},{8,9},{9,8},{10,11... | collective-permute-start | bytes 4718600 | tf_op jit(solution)/shard_map/ppermute | solution.py:45
  134.3 25.0 %slice-start.4 = ((s8[6881280]{0:T(1024)(128)(4,1)}), s8[4194304]{0:T(1024)(128)(4,1)S(1)}, s32[]{:S(2)}) async-start(s8[6881280]{0:T(1024)(128)(4,1)} %bitcast.98), calls=%async_computation.15 | async-start | bytes 8388608
  136.6 22.8 %slice-start.5 = ((s8[6881280]{0:T(1024)(128)(4,1)}), s8[2686976]{0:T(1024)(128)(4,1)S(1)}, s32[]{:S(2)}) async-start(s8[6881280]{0:T(1024)(128)(4,1)} %bitcast.98), calls=%async_computation.16 | async-start | bytes 5373952
  159.3 26.2 %copy-start.15 = (bf16[1024,2240]{1,0:T(8,128)(2,1)}, bf16[1024,2240]{1,0:T(8,128)(2,1)S(1)}, u32[]{:S(2)}) copy-start(bf16[1024,2240]{1,0:T(8,128)(2,1)S(1)} %get-tuple-element.28) | copy-start | bytes 13762564
  159.4 35.9 %copy-start.12 = (bf16[1024,2240]{1,0:T(8,128)(2,1)}, bf16[1024,2240]{1,0:T(8,128)(2,1)S(1)}, u32[]{:S(2)}) copy-start(bf16[1024,2240]{1,0:T(8,128)(2,1)S(1)} %get-tuple-element.27) | copy-start | bytes 13762564
  173.7 11.8 %collective-permute-start.9 = (bf16[512,1536]{1,0:T(8,128)(2,1)S(1)}, bf16[512,1536]{1,0:T(8,128)(2,1)}, u32[]{:S(2)}, u32[]{:S(2)}) collective-permute-start(bf16[512,1536]{1,0:T(8,128)(2,1)S(1)} %fusion.11), channel_id=1, source_target_pairs={{0,1},{1,0},{2,3},{3,2},{4,5},{5,4},{6,7},{7,6},{8,9},{9,8},{10,11... | collective-permute-start | bytes 4718600 | tf_op jit(solution)/shard_map/ppermute | solution.py:45
  178.1 17.1 %collective-permute-start.6 = (bf16[512,1536]{1,0:T(8,128)(2,1)S(1)}, bf16[512,1536]{1,0:T(8,128)(2,1)S(1)}, u32[]{:S(2)}, u32[]{:S(2)}) collective-permute-start(bf16[512,1536]{1,0:T(8,128)(2,1)S(1)} %convolution_convert_fusion.5), channel_id=1, source_target_pairs={{0,1},{1,0},{2,3},{3,2},{4,5},{5,4},{6,7},{7,6},{8,9},{9,8},{10,11... | collective-permute-start | bytes 4718600 | tf_op jit(solution)/shard_map/ppermute | solution.py:45
  185.5 78.7 %slice-start.2 = ((s8[6291456]{0:T(1024)(128)(4,1)}), s8[2097152]{0:T(1024)(128)(4,1)S(1)}, s32[]{:S(2)}) async-start(s8[6291456]{0:T(1024)(128)(4,1)} %bitcast.96), calls=%async_computation.13 | async-start | bytes 4194304
  193.6 37.3 %copy-start.17 = (f32[512,1536]{1,0:T(8,128)S(1)}, f32[512,1536]{1,0:T(8,128)}, u32[]{:S(2)}) copy-start(f32[512,1536]{1,0:T(8,128)} %copy-done.16) | copy-start | bytes 9437188
  193.6 70.6 %slice-start.3 = ((s8[6291456]{0:T(1024)(128)(4,1)}), s8[4194304]{0:T(1024)(128)(4,1)S(1)}, s32[]{:S(2)}) async-start(s8[6291456]{0:T(1024)(128)(4,1)} %bitcast.96), calls=%async_computation.14 | async-start | bytes 8388608
  193.6 37.3 %collective-permute-start.10 = (bf16[512,1536]{1,0:T(8,128)(2,1)S(1)}, bf16[512,1536]{1,0:T(8,128)(2,1)S(1)}, u32[]{:S(2)}, u32[]{:S(2)}) collective-permute-start(bf16[512,1536]{1,0:T(8,128)(2,1)S(1)} %fusion.10), channel_id=1, source_target_pairs={{0,2},{1,3},{2,0},{3,1},{4,6},{5,7},{6,4},{7,5},{8,10},{9,11},{10,... | collective-permute-start | bytes 4718600 | tf_op jit(solution)/shard_map/ppermute | solution.py:49
  199.1 65.1 %collective-permute-start.7 = (bf16[512,1536]{1,0:T(8,128)(2,1)S(1)}, bf16[512,1536]{1,0:T(8,128)(2,1)S(1)}, u32[]{:S(2)}, u32[]{:S(2)}) collective-permute-start(bf16[512,1536]{1,0:T(8,128)(2,1)S(1)} %add_convert_fusion.5), channel_id=1, source_target_pairs={{0,2},{1,3},{2,0},{3,1},{4,6},{5,7},{6,4},{7,5},{8,10},{9,11},{10,... | collective-permute-start | bytes 4718600 | tf_op jit(solution)/shard_map/ppermute | solution.py:49
  268.6 3.8 collective-permute-start.11
  283.4 10.1 %collective-permute-start.12 = (bf16[2,1536,128]{2,1,0:T(8,128)(2,1)S(1)}, bf16[2,1536,128]{2,1,0:T(8,128)(2,1)S(1)}, u32[]{:S(2)}, u32[]{:S(2)}) collective-permute-start(bf16[2,1536,128]{2,1,0:T(8,128)(2,1)S(1)} %slice_bitcast_fusion.1), channel_id=1, source_target_pairs={{0,1},{1,0},{2,3},{3,2},{4,5},{5,4},{6,7},{7,6},{8,9},{9,8},{10,11... | collective-permute-start | bytes 2359304 | tf_op jit(solution)/shard_map/ppermute | solution.py:45
  289.1 118.6 %collective-permute-start.22 = (bf16[768,2240]{0,1:T(8,128)(2,1)}, bf16[768,2240]{0,1:T(8,128)(2,1)}, u32[]{:S(2)}, u32[]{:S(2)}) collective-permute-start(bf16[768,2240]{0,1:T(8,128)(2,1)} %convolution_convert_fusion.1), channel_id=1, source_target_pairs={{0,16},{16,0},{1,17},{17,1},{2,18},{18,2},{3,19},{19,3},{4,20},{20... | collective-permute-start | bytes 10321928 | tf_op jit(solution)/shard_map/ppermute | solution.py:364
  293.1 85.5 %collective-permute-start.19 = (bf16[768,384]{1,0:T(8,128)(2,1)S(1)}, bf16[768,384]{1,0:T(8,128)(2,1)S(1)}, u32[]{:S(2)}, u32[]{:S(2)}) collective-permute-start(bf16[768,384]{1,0:T(8,128)(2,1)S(1)} %fusion.49), channel_id=1, source_target_pairs={{0,16},{16,0},{1,17},{17,1},{2,18},{18,2},{3,19},{19,3},{4,20},{20... | collective-permute-start | bytes 1769480 | tf_op jit(solution)/shard_map/ppermute | solution.py:364
  295.8 86.3 %collective-permute-start.13 = (bf16[2,512,128]{2,1,0:T(8,128)(2,1)}, bf16[2,512,128]{2,1,0:T(8,128)(2,1)S(1)}, u32[]{:S(2)}, u32[]{:S(2)}) collective-permute-start(bf16[2,512,128]{2,1,0:T(8,128)(2,1)} %get-tuple-element.53), channel_id=1, source_target_pairs={{4,0},{8,4},{12,8},{5,1},{9,5},{13,9},{6,2},{10,6},{14,10},{7,3},{... | collective-permute-start | bytes 786440 | tf_op jit(solution)/shard_map/ppermute | solution.py:55
  297.1 86.2 %copy-start.5 = (f32[1024,128]{1,0:T(8,128)S(1)}, f32[1024,128]{1,0:T(8,128)}, u32[]{:S(2)}) copy-start(f32[1024,128]{1,0:T(8,128)} %copy-done.4) | copy-start | bytes 1572868
  297.1 85.0 %collective-permute-start.14 = (bf16[2,512,128]{2,1,0:T(8,128)(2,1)}, bf16[2,512,128]{2,1,0:T(8,128)(2,1)}, u32[]{:S(2)}, u32[]{:S(2)}) collective-permute-start(bf16[2,512,128]{2,1,0:T(8,128)(2,1)} %get-tuple-element.54), channel_id=1, source_target_pairs={{8,0},{12,4},{9,1},{13,5},{10,2},{14,6},{11,3},{15,7},{24,16},{28,... | collective-permute-start | bytes 786440 | tf_op jit(solution)/shard_map/ppermute | solution.py:55
  381.8 343.1 %reduce-scatter.6.cloned.1.call-start = ((), (), s32[]{:S(2)}) async-start(), calls=%async_computation.6 | async-start | bytes 983040 | tf_op jit(solution)/shard_map/reduce_scatter | solution.py:372
  386.5 19.1 %collective-permute-start.18 = (bf16[768,512]{1,0:T(8,128)(2,1)S(1)}, bf16[768,512]{1,0:T(8,128)(2,1)S(1)}, u32[]{:S(2)}, u32[]{:S(2)}) collective-permute-start(bf16[768,512]{1,0:T(8,128)(2,1)S(1)} %fusion.40), channel_id=1, source_target_pairs={{0,16},{16,0},{1,17},{17,1},{2,18},{18,2},{3,19},{19,3},{4,20},{20... | collective-permute-start | bytes 2359304 | tf_op jit(solution)/shard_map/ppermute | solution.py:364
  407.6 327.9 %reduce-scatter.14.cloned.1.call-start = ((), (), s32[]{:S(2)}) async-start(), calls=%async_computation.10 | async-start | bytes 4423680 | tf_op jit(solution)/shard_map/reduce_scatter | solution.py:372
  422.9 315.1 %reduce-scatter.12.cloned.1.call-start = ((), (), s32[]{:S(2)}) async-start(), calls=%async_computation.9 | async-start | bytes 4423680 | tf_op jit(solution)/shard_map/reduce_scatter | solution.py:372
  429.5 75.2 %collective-permute-start.21 = (bf16[768,2240]{0,1:T(8,128)(2,1)S(1)}, bf16[768,2240]{0,1:T(8,128)(2,1)}, u32[]{:S(2)}, u32[]{:S(2)}) collective-permute-start(bf16[768,2240]{0,1:T(8,128)(2,1)S(1)} %convolution_convert_fusion.2), channel_id=1, source_target_pairs={{0,16},{16,0},{1,17},{17,1},{2,18},{18,2},{3,19},{19,3},{4,20},{20... | collective-permute-start | bytes 10321928 | tf_op jit(solution)/shard_map/ppermute | solution.py:364
  520.1 217.9 %reduce-scatter.10.cloned.1.call-start = ((), (), s32[]{:S(2)}) async-start(), calls=%async_computation.8 | async-start | bytes 4423680 | tf_op jit(solution)/shard_map/reduce_scatter | solution.py:372
  526.8 80.0 %copy-start.22 = (bf16[1536,384]{1,0:T(8,128)(2,1)S(1)}, bf16[1536,384]{1,0:T(8,128)(2,1)}, u32[]{:S(2)}) copy-start(bf16[1536,384]{1,0:T(8,128)(2,1)} %param.18) | copy-start | bytes 3538948
  526.8 80.0 %copy-start.25 = (bf16[1536,128]{1,0:T(8,128)(2,1)S(1)}, bf16[1536,128]{1,0:T(8,128)(2,1)}, u32[]{:S(2)}) copy-start(bf16[1536,128]{1,0:T(8,128)(2,1)} %copy-done.24) | copy-start | bytes 1179652
  526.8 74.2 %collective-permute-start.20 = (bf16[768,2240]{0,1:T(8,128)(2,1)S(1)}, bf16[768,2240]{0,1:T(8,128)(2,1)}, u32[]{:S(2)}, u32[]{:S(2)}) collective-permute-start(bf16[768,2240]{0,1:T(8,128)(2,1)S(1)} %convolution_convert_fusion.3), channel_id=1, source_target_pairs={{0,16},{16,0},{1,17},{17,1},{2,18},{18,2},{3,19},{19,3},{4,20},{20... | collective-permute-start | bytes 10321928 | tf_op jit(solution)/shard_map/ppermute | solution.py:364
  610.0 8.7 %collective-permute-start.15 = (bf16[512,1536]{1,0:T(8,128)(2,1)}, bf16[512,1536]{1,0:T(8,128)(2,1)}, u32[]{:S(2)}, u32[]{:S(2)}) collective-permute-start(bf16[512,1536]{1,0:T(8,128)(2,1)} %convolution_convert_fusion.4), channel_id=1, source_target_pairs={{0,1},{1,0},{2,3},{3,2},{4,5},{5,4},{6,7},{7,6},{8,9},{9,8},{10,11... | collective-permute-start | bytes 4718600 | tf_op jit(solution)/shard_map/ppermute | solution.py:45
  618.7 40.0 %copy-start.3 = (bf16[2,512,1536]{2,1,0:T(8,128)(2,1)S(1)}, bf16[2,512,1536]{2,1,0:T(8,128)(2,1)}, u32[]{:S(2)}) copy-start(bf16[2,512,1536]{2,1,0:T(8,128)(2,1)} %param.15) | copy-start | bytes 9437188
  621.9 37.8 %copy-start.19 = (f32[512,1536]{1,0:T(8,128)S(1)}, f32[512,1536]{1,0:T(8,128)}, u32[]{:S(2)}) copy-start(f32[512,1536]{1,0:T(8,128)} %get-tuple-element.40) | copy-start | bytes 9437188
  621.9 36.9 %collective-permute-start.16 = (bf16[512,1536]{1,0:T(8,128)(2,1)S(1)}, bf16[512,1536]{1,0:T(8,128)(2,1)S(1)}, u32[]{:S(2)}, u32[]{:S(2)}) collective-permute-start(bf16[512,1536]{1,0:T(8,128)(2,1)S(1)} %add_convert_fusion.3), channel_id=1, source_target_pairs={{0,2},{1,3},{2,0},{3,1},{4,6},{5,7},{6,4},{7,5},{8,10},{9,11},{10,... | collective-permute-start | bytes 4718600 | tf_op jit(solution)/shard_map/ppermute | solution.py:49
  623.5 39.0 %collective-permute-start.8 = (bf16[512,1536]{1,0:T(8,128)(2,1)S(1)}, bf16[512,1536]{1,0:T(8,128)(2,1)}, u32[]{:S(2)}, u32[]{:S(2)}) collective-permute-start(bf16[512,1536]{1,0:T(8,128)(2,1)S(1)} %copy-done.20), channel_id=1, source_target_pairs={{0,1},{1,0},{2,3},{3,2},{4,5},{5,4},{6,7},{7,6},{8,9},{9,8},{10,11... | collective-permute-start | bytes 4718600 | tf_op jit(solution)/shard_map/ppermute | solution.py:45
  662.5 87.0 %collective-permute-start.17 = (f32[512,1536]{1,0:T(8,128)}, f32[512,1536]{1,0:T(8,128)}, u32[]{:S(2)}, u32[]{:S(2)}) collective-permute-start(f32[512,1536]{1,0:T(8,128)} %fusion.6), channel_id=1, source_target_pairs={{0,1},{1,0},{2,3},{3,2},{4,5},{5,4},{6,7},{7,6},{8,9},{9,8},{10,11... | collective-permute-start | bytes 9437192 | tf_op jit(solution)/shard_map/ppermute | solution.py:45
  726.4 7.8 %all-to-all-start = ((f32[4,48,128]{2,1,0:T(8,128)}), f32[4,48,128]{2,1,0:T(8,128)S(1)}, u32[]{:S(2)}, u32[]{:S(2)}) async-start(f32[4,48,128]{2,1,0:T(8,128)} %bitcast.18), calls=%async_computation.1 | async-start | bytes 196608 | tf_op jit(solution)/shard_map/all_to_all | solution.py:579
  (35 other events, 204.3 us)
Sparse Core Ops, SparseCore 0:
  382.0 36.0 reduce-scatter.7
  420.4 24.6 reduce-scatter.5
  447.5 65.5 reduce-scatter.13
  520.2 80.6 reduce-scatter.11
  618.8 81.3 reduce-scatter.9

commit v2 on v1

v2 whole, which is shorter than its diff:
```python
import functools
import math

import jax
import jax.numpy as jnp
from jax import lax
from jax.experimental import pallas as pl
from jax.experimental.pallas import tpu as pltpu
from jax.sharding import PartitionSpec as P

KVH = 2
HD = 128
MOST = 1024
EPS = 1e-06
ROPE_BASE = 10000.0
NEG_FILL = -1e30
Q_BLOCK = 256
K_BLOCK = 256
MIB = 1 << 20
LIGHT = 1000
TILE = 256
SCALE = 1.0 / math.sqrt(HD)


def to_bf(value):
    return value.astype(jnp.bfloat16)


def to_f(value):
    return value.astype(jnp.float32)


def dot(left, right, left_dim=1, right_dim=0):
    return lax.dot_general(
        left,
        right,
        (((left_dim,), (right_dim,)), ((), ())),
        preferred_element_type=jnp.float32,
    )


def flipped(axis, bit):
    return [(i, i ^ (1 << bit)) for i in range(lax.axis_size(axis))]


def core_swap(value):
    return lax.ppermute(value, "tensor", flipped("tensor", 0))


def chip_swap(value):
    return lax.ppermute(value, "tensor", flipped("tensor", 1))


def shifted(value, hops):
    count = lax.axis_size("seq")
    route = [(i, i + hops) for i in range(count) if 0 <= i + hops < count]
    return lax.ppermute(value, "seq", route)


def cost(flops, read):
    return pl.CostEstimate(flops=flops // LIGHT, bytes_accessed=read // LIGHT, transcendentals=0)


class Order:
    def __init__(self):
        self.mark = None

    def __call__(self, kernel, args, in_specs, out_specs, out_shape, grid, flops, read, name, scalars=(), scratch=()):
        anchor = [] if self.mark is None else [self.mark]
        count = len(scalars) + len(args)
        outs = len(out_shape)

        def run(*refs):
            rest = refs[count + len(anchor) :]
            kernel(*refs[:count], *rest[:outs], *rest[outs + 1 :])
            rest[outs][...] = jnp.zeros(rest[outs].shape, jnp.float32)

        *results, self.mark = pl.pallas_call(
            run,
            grid_spec=pltpu.PrefetchScalarGridSpec(
                num_scalar_prefetch=len(scalars),
                grid=grid,
                in_specs=list(in_specs) + anchors(len(anchor)),
                out_specs=list(out_specs) + [mark_spec()],
                scratch_shapes=list(scratch),
            ),
            out_shape=list(out_shape) + [MARK],
            compiler_params=pltpu.CompilerParams(vmem_limit_bytes=32 * MIB),
            cost_estimate=cost(flops, read),
            name=name,
        )(*scalars, *args, *anchor)
        return results


def first_kernel(core_ref, tok_ref, gain_ref, w_ref, b_ref, cos_ref, sin_ref, h_ref, q_ref, kv_ref):
    x = to_f(tok_ref[...])
    factor = lax.rsqrt(jnp.mean(x * x, axis=-1, keepdims=True) + EPS)
    h = to_bf(x * factor * gain_ref[...])
    h_ref[...] = h
    lin = dot(h, w_ref[...]) + b_ref[...]
    cosine = cos_ref[...]
    sine = sin_ref[...]
    heads = q_ref.shape[1] // HD
    for head in range(heads):
        part = lin[:, head * HD : (head + 1) * HD]
        q_ref[:, head * HD : (head + 1) * HD] = to_bf(
            part * cosine + pltpu.roll(part, HD // 2, 1) * sine
        )
    part = lin[:, heads * HD :]
    is_key = core_ref[0] == 0
    kv_ref[...] = to_bf(
        part * jnp.where(is_key, cosine, 1.0)
        + pltpu.roll(part, HD // 2, 1) * jnp.where(is_key, sine, 0.0)
    )


def first(core, tokens, gain, weight, bias, cosine, sine):
    total, width = tokens.shape
    columns = weight.shape[1]
    block = total // 4
    half = 2

    def flip(i, core_ref):
        return (lax.rem(i + core_ref[0] * half, 4), 0)

    def at(i, core_ref):
        return (i, 0)

    def whole(i, core_ref):
        return (0, 0)

    return pl.pallas_call(
        first_kernel,
        grid_spec=pltpu.PrefetchScalarGridSpec(
            num_scalar_prefetch=1,
            grid=(4,),
            in_specs=[
                pl.BlockSpec((block, width), flip),
                pl.BlockSpec((1, width), whole),
                pl.BlockSpec((width, columns), whole),
                pl.BlockSpec((1, columns), whole),
                pl.BlockSpec((block, HD), at),
                pl.BlockSpec((block, HD), at),
            ],
            out_specs=[
                pl.BlockSpec((block, width), at),
                pl.BlockSpec((block, columns - HD), at),
                pl.BlockSpec((block, HD), at),
            ],
        ),
        out_shape=[
            jax.ShapeDtypeStruct((total, width), jnp.bfloat16),
            jax.ShapeDtypeStruct((total, columns - HD), jnp.bfloat16),
            jax.ShapeDtypeStruct((total, HD), jnp.bfloat16),
        ],
        compiler_params=pltpu.CompilerParams(vmem_limit_bytes=24 * MIB),
        cost_estimate=cost(2 * total * width * columns, 9 * MIB),
        name="first",
    )(core, tokens, gain, weight, bias, cosine, sine)


def stacked(ref, start, count, heads):
    return jnp.concatenate(
        [ref[0, pl.ds(start, count), h * HD : (h + 1) * HD] for h in range(heads)], axis=0
    )


def bounds(start_ref, index, heads, reach):
    first_key = jnp.concatenate(
        [start_ref[0, :, pl.ds(index * Q_BLOCK, Q_BLOCK)]] * heads, axis=1
    )
    place = reach + index * Q_BLOCK + lax.broadcasted_iota(jnp.int32, (1, Q_BLOCK), 1)
    return first_key, jnp.concatenate([place] * heads, axis=1)


def gather_span(core, refs, span):
    count = len(refs) // 2
    local = refs[0].shape[1]
    for i in range(count):
        here = slice(i * local, (i + 1) * local)
        span[core, here] = refs[i][0]
        span[1 - core, here] = refs[count + i][0]


def attend_kernel(heads, blocks, pieces, low_ref, core_ref, q_ref, start_ref, *refs):
    o_ref, lse_ref, acc, span = refs[2 * pieces :]
    row = pl.program_id(0)
    wide = heads * Q_BLOCK
    reach = (pieces - 1) * q_ref.shape[1]
    gather_span(core_ref[0], refs[: 2 * pieces], span)
    for index in range(blocks):
        q = stacked(q_ref, index * Q_BLOCK, Q_BLOCK, heads)
        first_key, place = bounds(start_ref, index, heads, reach)
        acc[...] = jnp.zeros_like(acc)

        def step(j, carry):
            top, total = carry
            keys = pl.ds(pl.multiple_of(j * K_BLOCK, K_BLOCK), K_BLOCK)
            s = dot(span[0, keys], q, 1, 1) * SCALE
            key = j * K_BLOCK + lax.broadcasted_iota(jnp.int32, (K_BLOCK, wide), 0)
            s = jnp.where((key >= first_key) & (key <= place), s, NEG_FILL)
            later = jnp.maximum(top, jnp.max(s, axis=0, keepdims=True))
            p = jnp.exp(s - later)
            fade = jnp.exp(top - later)
            total = total * fade + jnp.sum(p, axis=0, keepdims=True)
            acc[...] = acc[...] * fade + dot(span[1, keys], to_bf(p), 0, 0)
            return later, total

        last = (reach + (index + 1) * Q_BLOCK - 1) // K_BLOCK + 1
        top, total = lax.fori_loop(
            low_ref[row, index],
            last,
            step,
            (jnp.full((1, wide), NEG_FILL, jnp.float32), jnp.zeros((1, wide), jnp.float32)),
        )
        out = to_bf((acc[...] / total).T)
        for h in range(heads):
            o_ref[0, index * Q_BLOCK : (index + 1) * Q_BLOCK, h * HD : (h + 1) * HD] = out[
                h * Q_BLOCK : (h + 1) * Q_BLOCK
            ]
        lse_ref[0, index : index + 1, :] = top + jnp.log(total)


def span_specs(rows, local, pieces):
    near = pl.BlockSpec((1, local, HD), lambda i, *refs: (i, 0, 0))
    far = pl.BlockSpec((1, local, HD), lambda i, *refs: (lax.rem(i + rows // 2, rows), 0, 0))
    return [near] * pieces + [far] * pieces


def attend(low, core, q, start, span, mate):
    rows, local, columns = q.shape
    pieces = len(span)
    heads = columns // HD
    blocks = local // Q_BLOCK

    def at(i, *refs):
        return (i, 0, 0)

    return pl.pallas_call(
        functools.partial(attend_kernel, heads, blocks, pieces),
        grid_spec=pltpu.PrefetchScalarGridSpec(
            num_scalar_prefetch=2,
            grid=(rows,),
            in_specs=[pl.BlockSpec((1, local, columns), at), pl.BlockSpec((1, 1, local), at)]
            + span_specs(rows, local, pieces),
            out_specs=[
                pl.BlockSpec((1, local, columns), at),
                pl.BlockSpec((1, blocks, heads * Q_BLOCK), at),
            ],
            scratch_shapes=[
                pltpu.VMEM((HD, heads * Q_BLOCK), jnp.float32),
                pltpu.VMEM((2, pieces * local, HD), jnp.bfloat16),
            ],
        ),
        out_shape=[
            jax.ShapeDtypeStruct((rows, local, columns), jnp.bfloat16),
            jax.ShapeDtypeStruct((rows, blocks, heads * Q_BLOCK), jnp.float32),
        ],
        compiler_params=pltpu.CompilerParams(vmem_limit_bytes=24 * MIB),
        cost_estimate=cost(8_000_000_000, 4 * MIB),
        name="attend",
    )(low, core, q, start, *span, *mate)


def attend_back_kernel(
    heads, blocks, pieces, low_ref, core_ref, q_ref, start_ref, g_ref, o_ref, lse_ref, cos_ref, sin_ref, *refs
):
    gq_ref, both_ref, acc, gk, gv, span = refs[2 * pieces :]
    row = pl.program_id(0)
    wide = heads * Q_BLOCK
    reach = (pieces - 1) * q_ref.shape[1]
    core = core_ref[0]
    gather_span(core, refs[: 2 * pieces], span)
    gk[...] = jnp.zeros_like(gk)
    gv[...] = jnp.zeros_like(gv)
    for index in range(blocks):
        q = stacked(q_ref, index * Q_BLOCK, Q_BLOCK, heads)
        g = stacked(g_ref, index * Q_BLOCK, Q_BLOCK, heads)
        o = stacked(o_ref, index * Q_BLOCK, Q_BLOCK, heads)
        inner = jnp.sum((to_f(g) * to_f(o)).T, axis=0, keepdims=True)
        lse = lse_ref[0, index : index + 1, :]
        first_key, place = bounds(start_ref, index, heads, reach)
        acc[...] = jnp.zeros_like(acc)

        def step(j, carry):
            keys = pl.ds(pl.multiple_of(j * K_BLOCK, K_BLOCK), K_BLOCK)
            k = span[0, keys]
            s = dot(k, q, 1, 1) * SCALE
            key = j * K_BLOCK + lax.broadcasted_iota(jnp.int32, (K_BLOCK, wide), 0)
            p = jnp.where((key >= first_key) & (key <= place), jnp.exp(s - lse), 0.0)
            gp = dot(span[1, keys], g, 1, 1)
            gs = to_bf(p * (gp - inner))
            gv[keys] += dot(to_bf(p), g)
            gk[keys] += dot(gs, q)
            acc[...] += dot(k, gs, 0, 0)
            return carry

        last = (reach + (index + 1) * Q_BLOCK - 1) // K_BLOCK + 1
        lax.fori_loop(low_ref[row, index], last, step, 0)
        gq = acc[...].T * SCALE
        here = slice(index * Q_BLOCK, (index + 1) * Q_BLOCK)
        cosine, sine = cos_ref[here], sin_ref[here]
        for h in range(heads):
            part = gq[h * Q_BLOCK : (h + 1) * Q_BLOCK]
            gq_ref[0, here, h * HD : (h + 1) * HD] = to_bf(
                part * cosine + pltpu.roll(part * sine, HD // 2, 1)
            )
    both_ref[core, 0] = to_bf(gk[...] * SCALE)
    both_ref[1 - core, 0] = to_bf(gv[...])


def attend_back(order, low, core, q, start, span, mate, grad, out, lse, cosine, sine):
    rows, local, columns = q.shape
    pieces = len(span)
    window = pieces * local
    heads = columns // HD
    blocks = local // Q_BLOCK

    def at(i, *refs):
        return (i, 0, 0)

    table = pl.BlockSpec((local, HD), lambda i, *refs: (i, 0))
    tokens = pl.BlockSpec((1, local, columns), at)
    return order(
        functools.partial(attend_back_kernel, heads, blocks, pieces),
        [q, start, grad, out, lse, cosine, sine, *span, *mate],
        [
            tokens,
            pl.BlockSpec((1, 1, local), at),
            tokens,
            tokens,
            pl.BlockSpec((1, blocks, heads * Q_BLOCK), at),
            table,
            table,
        ]
        + span_specs(rows, local, pieces),
        [tokens, pl.BlockSpec((2, 1, window, HD), lambda i, *refs: (0, i, 0, 0))],
        [
            jax.ShapeDtypeStruct((rows, local, columns), jnp.bfloat16),
            jax.ShapeDtypeStruct((2, rows, window, HD), jnp.bfloat16),
        ],
        (rows,),
        20_000_000_000,
        6 * MIB,
        "attend_back",
        scalars=(low, core),
        scratch=[
            pltpu.VMEM((HD, heads * Q_BLOCK), jnp.float32),
            pltpu.VMEM((window, HD), jnp.float32),
            pltpu.VMEM((window, HD), jnp.float32),
            pltpu.VMEM((2, window, HD), jnp.bfloat16),
        ],
    )


def fold_kernel(both_ref, come_ref, own_ref, *send_refs):
    local = own_ref.shape[1]
    total = to_f(both_ref[0, 0]) + to_f(come_ref[0])
    reach = total.shape[0] - local
    own_ref[0] = total[reach:]
    for hop, ref in enumerate(send_refs, 1):
        ref[0] = to_bf(total[reach - hop * local : reach - (hop - 1) * local])


def fold(order, both, come, local):
    rows, window = both.shape[1:3]
    hops = window // local - 1
    out = pl.BlockSpec((1, local, HD), lambda i: (i, 0, 0))
    return order(
        fold_kernel,
        [both, come],
        [
            pl.BlockSpec((1, 1, window, HD), lambda i: (0, i, 0, 0)),
            pl.BlockSpec((1, window, HD), lambda i: (lax.rem(i + rows // 2, rows), 0, 0)),
        ],
        [out] * (hops + 1),
        [jax.ShapeDtypeStruct((rows, local, HD), jnp.float32)]
        + [jax.ShapeDtypeStruct((rows, local, HD), jnp.bfloat16)] * hops,
        (rows,),
        0,
        4 * MIB,
        "fold",
    )


def join_kernel(hops, core_ref, gq_ref, cos_ref, sin_ref, own_ref, *refs):
    out_ref, sum_ref = refs[-2:]
    columns = gq_ref.shape[2]
    grad = own_ref[0]
    for ref in refs[:hops]:
        grad = grad + to_f(ref[0])
    is_key = core_ref[0] == 0
    cosine = jnp.where(is_key, cos_ref[...], 1.0)
    sine = jnp.where(is_key, sin_ref[...], 0.0)
    kv = to_bf(grad * cosine + pltpu.roll(grad * sine, HD // 2, 1))
    q = gq_ref[0]
    out_ref[:, :columns] = q
    out_ref[:, columns:] = kv

    @pl.when(pl.program_id(0) == 0)
    def _():
        sum_ref[...] = jnp.zeros(sum_ref.shape, jnp.float32)

    sum_ref[:, :columns] += jnp.sum(to_f(q), axis=0, keepdims=True)
    sum_ref[:, columns:] += jnp.sum(to_f(kv), axis=0, keepdims=True)


def join(order, core, grad_q, own, comes, cosine, sine):
    rows, local, columns = grad_q.shape
    wide = columns + HD

    def at(i, *refs):
        return (i, 0, 0)

    piece = pl.BlockSpec((1, local, HD), at)
    table = pl.BlockSpec((local, HD), lambda i, *refs: (i, 0))
    return order(
        functools.partial(join_kernel, len(comes)),
        [grad_q, cosine, sine, own, *comes],
        [pl.BlockSpec((1, local, columns), at), table, table, piece] + [piece] * len(comes),
        [
            pl.BlockSpec((local, wide), lambda i, *refs: (i, 0)),
            pl.BlockSpec((8, wide), lambda i, *refs: (0, 0)),
        ],
        [
            jax.ShapeDtypeStruct((rows * local, wide), jnp.bfloat16),
            jax.ShapeDtypeStruct((8, wide), jnp.float32),
        ],
        (rows,),
        0,
        4 * MIB,
        "join",
        scalars=(core,),
    )


def mixed_back_kernel(near_ref, far_ref, w_ref, out_ref):
    half = near_ref.shape[0]
    out_ref[:half] = to_bf(dot(near_ref[...], w_ref[...]))
    out_ref[half:] = to_bf(dot(far_ref[...], w_ref[...]))


def mixed_back(order, near, far, weight):
    half, width = near.shape
    columns = weight.shape[1]

    def whole(i):
        return (0, 0)

    return order(
        mixed_back_kernel,
        [near, far, weight],
        [
            pl.BlockSpec((half, width), whole),
            pl.BlockSpec((half, width), whole),
            pl.BlockSpec((width, columns), whole),
        ],
        [pl.BlockSpec((2 * half, columns), whole)],
        [jax.ShapeDtypeStruct((2 * half, columns), jnp.bfloat16)],
        (1,),
        4 * half * width * columns,
        6 * MIB,
        "mixed_back",
    )[0]


def place_kernel(core_ref, near_ref, far_ref, out_ref):
    near = pl.program_id(0) < 2

    @pl.when(near)
    def _():
        out_ref[...] = near_ref[...]

    @pl.when(jnp.logical_not(near))
    def _():
        out_ref[...] = far_ref[...]


def place(order, core, near, far):
    half, width = near.shape
    block = half // 2
    return order(
        place_kernel,
        [near, far],
        [
            pl.BlockSpec((block, width), lambda i, core_ref: (jnp.minimum(i, 1), 0)),
            pl.BlockSpec((block, width), lambda i, core_ref: (jnp.maximum(i - 2, 0), 0)),
        ],
        [pl.BlockSpec((block, width), lambda i, core_ref: (lax.rem(i + core_ref[0] * 2, 4), 0))],
        [jax.ShapeDtypeStruct((2 * half, width), near.dtype)],
        (4,),
        0,
        8 * half * width,
        "place",
        scalars=(core,),
    )[0]


def anchors(count):
    return [pl.BlockSpec(memory_space=pl.ANY)] * count


MARK = jax.ShapeDtypeStruct((8, HD), jnp.float32)


def mark_spec():
    return pl.BlockSpec((8, HD), lambda *refs: (0, 0))


def grad_hidden_kernel(g_ref, w_ref, out_ref):
    out_ref[...] = to_bf(dot(g_ref[...], w_ref[...], 1, 1))


def grad_hidden_of(order, grad, weight):
    total, width = grad.shape
    hidden = weight.shape[0]
    return order(
        grad_hidden_kernel,
        [grad, weight],
        [pl.BlockSpec((total, width), lambda i: (0, 0)), pl.BlockSpec((TILE, width), lambda i: (i, 0))],
        [pl.BlockSpec((total, TILE), lambda i: (0, i))],
        [jax.ShapeDtypeStruct((total, hidden), jnp.bfloat16)],
        (pl.cdiv(hidden, TILE),),
        2 * total * width * hidden,
        15 * MIB,
        "grad_hidden",
    )[0]


def gated_kernel(h_ref, far_ref, gh_ref, gw_ref, uw_ref, hid_ref, gg_ref, gu_ref):
    half = h_ref.shape[0]
    for part, ref in enumerate((h_ref, far_ref)):
        here = slice(part * half, (part + 1) * half)
        h = ref[...]
        gate = dot(h, gw_ref[...], 1, 1)
        up = dot(h, uw_ref[...], 1, 1)
        grad = to_f(gh_ref[here])
        sigma = 1.0 / (1.0 + jnp.exp(-gate))
        swish = gate * sigma
        hid_ref[here] = to_bf(swish * up)
        gu_ref[here] = to_bf(grad * swish)
        gg_ref[here] = to_bf(grad * up * sigma * (1.0 + gate * (1.0 - sigma)))


def gated(order, near, far, grad_hidden, gate_weight, up_weight):
    half, width = near.shape
    total = 2 * half
    hidden = gate_weight.shape[0]
    column = pl.BlockSpec((total, TILE), lambda i: (0, i))
    weight = pl.BlockSpec((TILE, width), lambda i: (i, 0))
    whole = pl.BlockSpec((half, width), lambda i: (0, 0))
    shape = jax.ShapeDtypeStruct((total, hidden), jnp.bfloat16)
    return order(
        gated_kernel,
        [near, far, grad_hidden, gate_weight, up_weight],
        [whole, whole, column, weight, weight],
        [column] * 3,
        [shape] * 3,
        (pl.cdiv(hidden, TILE),),
        4 * total * width * hidden,
        30 * MIB,
        "gated",
    )


def share_kernel(columns, skip, extra, halves, pick_ref, blocks_ref, left_ref, right_ref, *refs):
    out = dot(left_ref[...], right_ref[...])
    if extra:
        out = out + to_f(refs[0][...])
        refs = refs[1:]
    tile = out.shape[1]
    spot = (pl.program_id(0) + skip) * tile + lax.broadcasted_iota(jnp.int32, (1, tile), 1)
    out = to_bf(jnp.where(spot < columns, out, 0.0))
    if not halves:
        refs[0][...] = out
        return
    send_ref, keep_ref, rows = refs
    rows[...] = out
    share = send_ref.shape[0] // (2 * halves)
    for i in range(2 * halves):
        here = slice(i * share, (i + 1) * share)
        send_ref[here] = rows[pl.ds(pl.multiple_of(blocks_ref[i] * share, share), share)]
        keep_ref[here] = rows[pl.ds(pl.multiple_of(blocks_ref[2 * halves + i] * share, share), share)]


def share_of(order, left, right, part, pick, span, tile=0, extra=None, blocks=None):
    tokens, columns = right.shape
    tile = tile or TILE
    skip, count = span
    column = pl.BlockSpec((part, tile), lambda i, *refs: (0, i))
    extras = [] if extra is None else [extra]
    scratch = []
    outs, shapes = [column], [jax.ShapeDtypeStruct((part, count * tile), jnp.bfloat16)]
    halves = 0
    if blocks is None:
        blocks = jnp.zeros((1,), jnp.int32)
    else:
        halves = blocks.shape[0] // 4
        outs = [pl.BlockSpec((part // 2, tile), lambda i, *refs: (0, i))] * 2
        shapes = [jax.ShapeDtypeStruct((part // 2, count * tile), jnp.bfloat16)] * 2
        scratch = [pltpu.VMEM((part, tile), jnp.bfloat16)]
    result = order(
        functools.partial(share_kernel, columns, skip, len(extras), halves),
        [left, right, *extras],
        [
            pl.BlockSpec((part, tokens), lambda i, pick_ref, blocks_ref: (pick_ref[0], 0)),
            pl.BlockSpec((tokens, tile), lambda i, *refs: (0, i + skip)),
        ]
        + [column] * len(extras),
        outs,
        shapes,
        (count,),
        2 * part * tokens * count * tile,
        2 * (part * tokens + (part + tokens) * count * tile),
        "share",
        scalars=(jnp.asarray(pick, jnp.int32).reshape(1), blocks),
        scratch=scratch,
    )
    return result if halves else result[0]


def relay_kernel(keep_ref, come_ref, out_ref):
    out_ref[...] = to_bf(to_f(keep_ref[...]) + to_f(come_ref[...]))


def relay(order, keep, come, share):
    rows, columns = keep.shape
    pair = pl.BlockSpec((share, columns), lambda i: (2 * i + 1, 0))
    return order(
        relay_kernel,
        [keep, come],
        [pair, pair],
        [pl.BlockSpec((share, columns), lambda i: (i, 0))],
        [jax.ShapeDtypeStruct((rows // 2, columns), jnp.bfloat16)],
        (rows // (2 * share),),
        0,
        3 * rows * columns,
        "relay",
    )[0]


def settle_kernel(pick_ref, keep_ref, come_ref, last_ref, out_ref):
    out_ref[...] = to_bf(to_f(keep_ref[...]) + to_f(come_ref[...]) + to_f(last_ref[...]))


def settle(order, keep, come, last, pick):
    share = last.shape[0] // 2
    columns = keep.shape[1]
    pair = pl.BlockSpec((share, columns), lambda i, pick_ref: (2 * pick_ref[0], 0))
    return order(
        settle_kernel,
        [keep, come, last],
        [pair, pair, pl.BlockSpec((share, columns), lambda i, pick_ref: (pick_ref[0], 0))],
        [pl.BlockSpec((share, columns), lambda i, pick_ref: (0, 0))],
        [jax.ShapeDtypeStruct((share, columns), jnp.bfloat16)],
        (1,),
        0,
        8 * share * columns,
        "settle",
        scalars=(pick.reshape(1),),
    )[0]


def narrow_kernel(pairs, extra, right_dim, *refs):
    out = dot(refs[0][...], refs[1][...], 1, right_dim)
    for i in range(1, pairs):
        out = out + dot(refs[2 * i][...], refs[2 * i + 1][...], 1, right_dim)
    if extra:
        out = out + to_f(refs[2 * pairs][...])
    refs[-1][...] = to_bf(out)


def narrow(order, pairs, index, extra=None, right_dim=0):
    total, hidden = pairs[0][0].shape
    width = pairs[0][1].shape[1 - right_dim]
    half = total // 2
    column = pl.BlockSpec((half, TILE), lambda i: (0, i))
    extras = [] if extra is None else [extra]
    right = (
        pl.BlockSpec((TILE, hidden), lambda i: (i, 0))
        if right_dim
        else pl.BlockSpec((hidden, TILE), lambda i: (0, i))
    )
    return order(
        functools.partial(narrow_kernel, len(pairs), len(extras), right_dim),
        [item for pair in pairs for item in pair] + extras,
        [pl.BlockSpec((half, hidden), lambda i: (index, 0)), right] * len(pairs) + [column] * len(extras),
        [column],
        [jax.ShapeDtypeStruct((half, width), jnp.bfloat16)],
        (width // TILE,),
        2 * len(pairs) * half * width * hidden,
        2 * len(pairs) * (half + width) * hidden + 2 * half * width,
        "narrow",
    )[0]


def turn_kernel(near_ref, far_ref, out_ref):
    half = near_ref.shape[0]
    out_ref[:, :half] = near_ref[...].T
    out_ref[:, half:] = far_ref[...].T


def turn(order, near, far=None):
    half, width = near.shape
    far_index = 0
    if far is None:
        half, far, far_index = half // 2, near, 1
    return order(
        turn_kernel,
        [near, far],
        [
            pl.BlockSpec((half, TILE), lambda i: (0, i)),
            pl.BlockSpec((half, TILE), lambda i: (far_index, i)),
        ],
        [pl.BlockSpec((TILE, 2 * half), lambda i: (i, 0))],
        [jax.ShapeDtypeStruct((width, 2 * half), jnp.bfloat16)],
        (width // TILE,),
        0,
        8 * half * width,
        "turn",
    )[0]


def grad_out_kernel(core_ref, cot_ref, valid_ref, out_ref, turned_ref):
    out = to_bf(to_f(cot_ref[...]) * valid_ref[...])
    out_ref[...] = out
    turned_ref[...] = out.T


def grad_out_of(order, core, cotangent, valid):
    total, width = cotangent.shape
    block = total // 4
    return order(
        grad_out_kernel,
        [cotangent, valid],
        [
            pl.BlockSpec((block, width), lambda i, core_ref: (lax.rem(i + core_ref[0] * 2, 4), 0)),
            pl.BlockSpec((block, 1), lambda i, core_ref: (i, 0)),
        ],
        [
            pl.BlockSpec((block, width), lambda i, core_ref: (i, 0)),
            pl.BlockSpec((width, block), lambda i, core_ref: (0, i)),
        ],
        [
            jax.ShapeDtypeStruct((total, width), jnp.bfloat16),
            jax.ShapeDtypeStruct((width, total), jnp.bfloat16),
        ],
        (4,),
        0,
        6 * total * width,
        "grad_out",
        scalars=(core,),
    )


def middle_kernel(core_ref, tok_ref, mine_ref, come_ref, gain_ref, mid_ref, h_ref):
    middle = to_f(tok_ref[...]) + (to_f(mine_ref[...]) + to_f(come_ref[...]))
    factor = lax.rsqrt(jnp.mean(middle * middle, axis=-1, keepdims=True) + EPS)
    mid_ref[...] = middle
    h_ref[...] = to_bf(middle * factor * gain_ref[...])


def middle_of(order, core, tokens, mine, come, gain):
    half, width = mine.shape
    block = half // 4
    at = pl.BlockSpec((block, width), lambda i, core_ref: (i, 0))
    return order(
        middle_kernel,
        [tokens, mine, come, gain],
        [
            pl.BlockSpec((block, width), lambda i, core_ref: (core_ref[0] * 4 + i, 0)),
            at,
            at,
            pl.BlockSpec((1, width), lambda i, core_ref: (0, 0)),
        ],
        [at, at],
        [jax.ShapeDtypeStruct((half, width), jnp.float32), jax.ShapeDtypeStruct((half, width), jnp.bfloat16)],
        (4,),
        0,
        9 * MIB,
        "middle",
        scalars=(core,),
    )


def norm_back_kernel(core_ref, mine_ref, come_ref, x_ref, gain_ref, up_ref, *refs):
    grad = to_f(mine_ref[...]) + to_f(come_ref[...])
    x = to_f(x_ref[...])
    factor = lax.rsqrt(jnp.mean(x * x, axis=-1, keepdims=True) + EPS)
    normed = x * factor
    weighted = grad * gain_ref[...]
    inner = jnp.mean(weighted * normed, axis=-1, keepdims=True)
    out = to_f(up_ref[...]) + factor * (weighted - normed * inner)
    refs[0][...] = out
    if len(refs) > 1:
        refs[1][...] = to_bf(out)


def norm_back(order, core, mine, come, x, gain, up, by_core):
    half, width = mine.shape
    block = half // 4
    at = pl.BlockSpec((block, width), lambda i, core_ref: (i, 0))
    picked = pl.BlockSpec((block, width), lambda i, core_ref: (core_ref[0] * 4 + i, 0))
    shapes = [jax.ShapeDtypeStruct((half, width), jnp.float32)]
    if not by_core:
        shapes.append(jax.ShapeDtypeStruct((half, width), jnp.bfloat16))
    return order(
        norm_back_kernel,
        [mine, come, x, gain, up],
        [at, at, picked if by_core else at, pl.BlockSpec((1, width), lambda i, core_ref: (0, 0)), at],
        [at] * len(shapes),
        shapes,
        (4,),
        0,
        10 * MIB,
        "norm_back",
        scalars=(core,),
    )


def layer_kernel(middle_ref, mine_ref, come_ref, out_ref):
    out_ref[...] = to_bf(middle_ref[...] + (to_f(mine_ref[...]) + to_f(come_ref[...])))


def layer_of(order, middle, mine, come):
    half, width = mine.shape
    at = pl.BlockSpec((half // 4, width), lambda i: (i, 0))
    return order(
        layer_kernel,
        [middle, mine, come],
        [at] * 3,
        [at],
        [jax.ShapeDtypeStruct((half, width), jnp.bfloat16)],
        (4,),
        0,
        5 * MIB,
        "layer",
    )[0]


def tensor_gather(value, rank):
    mate = core_swap(value)
    pair = jnp.where(lax.rem(rank, 2) == 0, jnp.stack([value, mate]), jnp.stack([mate, value]))
    come = chip_swap(pair)
    return jnp.where(
        lax.div(rank, 2) == 0,
        jnp.concatenate([pair, come], axis=0),
        jnp.concatenate([come, pair], axis=0),
    )


def body(
    tokens,
    lengths,
    cotangent,
    q_weight,
    q_bias,
    k_weight,
    k_bias,
    v_weight,
    v_bias,
    o_weight,
    attn_gain,
    ffn_gain,
    gate_weight,
    up_weight,
    down_weight,
):
    rows, local, width = tokens.shape
    total = rows * local
    half = total // 2
    heads = q_weight.shape[1] // HD
    ranks = lax.axis_size("tensor")
    seqs = lax.axis_size("seq")
    rank = lax.axis_index("tensor")
    dp_index = lax.axis_index("dp")
    seq_index = lax.axis_index("seq")
    core = lax.rem(rank, 2)
    head = lax.div(rank, 2)
    core_one = core.reshape(1)
    hops = min(seqs - 1, -(-(MOST - 1) // local))
    reach = hops * local

    def own_first(value):
        turned = jnp.concatenate([value[rows // 2 :], value[: rows // 2]], axis=0)
        return jnp.where(core == 0, value, turned)

    slots = jnp.arange(lengths.shape[1], dtype=jnp.int32)
    lens = own_first(lengths)
    ends = jnp.sum(jnp.where(slots[None, :] <= slots[:, None], lens[:, None, :], 0), axis=2)
    spot = seq_index * local + jnp.arange(local, dtype=jnp.int32)
    begun = jnp.max(
        jnp.where(ends[:, None, :] <= spot[None, :, None], ends[:, None, :], 0), axis=2
    )
    valid = to_f(spot[None, :] < ends[:, -2:-1])
    position = (spot[None, :] - begun).reshape(total, 1)
    freqs = ROPE_BASE ** (-(jnp.arange(HD // 2, dtype=jnp.float32) * 2.0) / HD)
    angles = to_f(position) * freqs[None, :]
    cosine, sine = jnp.cos(angles), jnp.sin(angles)
    cosine = jnp.concatenate([cosine, cosine], axis=1)
    sine = jnp.concatenate([-sine, sine], axis=1)
    start = begun - (seq_index * local - reach)
    low = jnp.maximum(lax.div(jnp.maximum(start[:, ::Q_BLOCK], 0), K_BLOCK), 0)
    start = start.reshape(rows, 1, local)

    key_side = core == 0
    kv_weight = jnp.where(
        key_side,
        lax.dynamic_slice_in_dim(k_weight, head * HD, HD, 1),
        lax.dynamic_slice_in_dim(v_weight, head * HD, HD, 1),
    )
    kv_bias = jnp.where(
        key_side,
        lax.dynamic_slice_in_dim(k_bias, head * HD, HD, 0),
        lax.dynamic_slice_in_dim(v_bias, head * HD, HD, 0),
    )
    weight = jnp.concatenate([q_weight, kv_weight], axis=1)
    bias = to_f(jnp.concatenate([q_bias, kv_bias])).reshape(1, -1)
    gain_one = to_f(attn_gain).reshape(1, width)
    gain_two = to_f(ffn_gain).reshape(1, width)

    h_one, q_rot, kv = first(
        core_one, tokens.reshape(total, width), gain_one, weight, bias, cosine, sine
    )
    kv = kv.reshape(rows, local, HD)
    span = [shifted(kv, h) for h in range(hops, 0, -1)] + [kv]
    mate = [core_swap(piece) for piece in span]
    q_rows = q_rot.reshape(rows, local, heads * HD)
    mixed_rows, lse = attend(low, core_one, q_rows, start, span, mate)
    mixed = mixed_rows.reshape(total, heads * HD)

    order = Order()
    flat_tokens = tokens.reshape(total, width)
    dps = lax.axis_size("dp")
    near_pair = dps == 2 and seqs == 4
    part = width // dps
    share = part // seqs
    gate_t, up_t, down_t = gate_weight.T, up_weight.T, down_weight.T
    units = gate_t.shape[0]
    tiles = -(-units // TILE)
    cut = (tiles + 1) // 2
    one, two = seq_index ^ 1, seq_index ^ 2
    three = seq_index ^ 3
    quad = jnp.stack([one, three, seq_index, two])
    wide = jnp.stack([one, three, one + seqs, three + seqs, seq_index, two, seq_index + seqs, two + seqs])

    class Rows:
        def __init__(self, left_t, right, span, tile=TILE):
            self.args = (left_t, right)
            self.span, self.tile = span, tile
            if near_pair:
                sent = share_of(order, left_t, right, part, 1 - dp_index, span, tile)
                self.come = lax.ppermute(sent, "dp", flipped("dp", 0))
            else:
                self.whole = share_of(order, left_t, right, width, 0, span, tile)

        def own(self):
            if near_pair:
                send, self.keep = share_of(
                    order, *self.args, part, dp_index, self.span, self.tile, self.come, quad
                )
                self.come = lax.ppermute(send, "seq", flipped("seq", 0))

        def relay(self):
            if near_pair:
                sent = relay(order, self.keep, self.come, share)
                self.last = lax.ppermute(sent, "seq", flipped("seq", 1))

        def result(self):
            if near_pair:
                return to_f(self.keep[:share]) + to_f(self.come[:share]) + to_f(self.last)
            return to_f(lax.psum_scatter(self.whole, ("dp", "seq"), scatter_dimension=0, tiled=True))

    class SeqFirst(Rows):
        def __init__(self, left_t, right, span, tile=TILE):
            self.near = near_pair
            if near_pair:
                send, self.keep = share_of(order, left_t, right, width, 0, span, tile, None, wide)
                self.come = lax.ppermute(send, "seq", flipped("seq", 0))
            else:
                super().__init__(left_t, right, span, tile)

        def settle(self):
            if near_pair:
                sent = settle(order, self.keep, self.come, self.last, 1 - dp_index)
                self.mine = settle(order, self.keep, self.come, self.last, dp_index)
                self.final = lax.ppermute(sent, "dp", flipped("dp", 0))

        def result(self):
            return to_f(self.mine) + to_f(self.final) if near_pair else super().result()

    sent = narrow(order, [(mixed, o_weight)], 1, None, 1)
    mine = narrow(order, [(mixed, o_weight)], 0, core_swap(sent), 1)
    come = chip_swap(mine)
    grad_ffn, grad_ffn_t = grad_out_of(
        order, core_one, cotangent.reshape(total, width), valid.reshape(total, 1)
    )
    grad_hidden = grad_hidden_of(order, grad_ffn, down_t)
    h_one_t = turn(order, h_one)
    middle, h_two_mine = middle_of(order, core_one, flat_tokens, mine, come, gain_two)
    h_two_mate = core_swap(h_two_mine)
    hidden, grad_gate, grad_up = gated(order, h_two_mine, h_two_mate, grad_hidden, gate_t, up_t)

    down_a = Rows(grad_ffn_t, hidden, (0, cut))
    down_b = SeqFirst(grad_ffn_t, hidden, (cut, tiles - cut))
    pairs = [(grad_gate, gate_t), (grad_up, up_t)]
    sent = narrow(order, pairs, 1)
    mine = narrow(order, pairs, 0, core_swap(sent))
    come = chip_swap(mine)
    h_two_t = turn(order, h_two_mine, h_two_mate)
    gate_a = Rows(h_two_t, grad_gate, (0, cut))
    gate_b = Rows(h_two_t, grad_gate, (cut, tiles - cut))
    up_a = Rows(h_two_t, grad_up, (0, cut))
    ffn_sent = narrow(order, [(hidden, down_t)], 1)
    down_b.relay()
    down_a.own()
    grad_middle, branch_mine = norm_back(order, core_one, mine, come, middle, gain_two, grad_ffn, False)
    branch_mate = core_swap(branch_mine)
    grad_mixed = mixed_back(order, branch_mine, branch_mate, o_weight).reshape(rows, local, heads * HD)
    grad_q_rows, both = attend_back(
        order, low, core_one, q_rows, start, span, mate, grad_mixed, mixed_rows, lse, cosine, sine
    )
    both_come = core_swap(both[1])
    ffn_mine = narrow(order, [(hidden, down_t)], 0, core_swap(ffn_sent))
    ffn_come = chip_swap(ffn_mine)
    own_kv, *kv_sends = fold(order, both, both_come, local)
    kv_comes = [shifted(piece, -hop) for hop, piece in enumerate(kv_sends, 1)]
    branch_t = turn(order, branch_mine, branch_mate)
    out = Rows(branch_t, mixed, (0, heads), HD)
    down_b.settle() if near_pair else None
    down_a.relay()
    gate_a.own()
    grad_qkv, bias_sum = join(order, core_one, grad_q_rows, own_kv, kv_comes, cosine, sine)
    sent = narrow(order, [(grad_qkv, weight)], 1, None, 1)
    mine = narrow(order, [(grad_qkv, weight)], 0, core_swap(sent), 1)
    come = chip_swap(mine)
    qkv = Rows(h_one_t, grad_qkv, (0, grad_qkv.shape[1] // TILE))
    up_b = Rows(h_two_t, grad_up, (cut, tiles - cut))
    gate_b.own()
    gate_a.relay()
    (token_mine,) = norm_back(order, core_one, mine, come, flat_tokens, gain_one, grad_middle, True)
    token_mate = core_swap(token_mine)
    layer_mine = layer_of(order, middle, ffn_mine, ffn_come)
    layer_mate = core_swap(layer_mine)
    up_a.own()
    gate_b.relay()
    out.own()
    token_grad = place(order, core_one, token_mine, token_mate).reshape(rows, local, width)
    layer_out = place(order, core_one, layer_mine, layer_mate).reshape(rows, local, width)
    up_a.relay()
    out.relay()
    qkv.own()
    qkv.relay()
    up_b.own()
    up_b.relay()
    if near_pair:
        bias_all = bias_sum + lax.ppermute(bias_sum, "dp", flipped("dp", 0))
        bias_all = bias_all + lax.ppermute(bias_all, "seq", flipped("seq", 0))
        bias_all = bias_all + lax.ppermute(bias_all, "seq", flipped("seq", 1))
        bias_all = bias_all[:1]
    else:
        bias_all = lax.psum(bias_sum[:1], ("dp", "seq"))
    qkv_grad = qkv.result()
    o_grad = out.result()
    down_grad = jnp.concatenate([down_a.result(), down_b.result()], axis=1)[:, :units]
    gate_grad = jnp.concatenate([gate_a.result(), gate_b.result()], axis=1)[:, :units]
    up_grad = jnp.concatenate([up_a.result(), up_b.result()], axis=1)[:, :units]

    begin = (dp_index * seqs + seq_index) * share

    def rows_of(value):
        return to_f(lax.dynamic_slice_in_dim(value, begin, share, 0))

    attn_term = jnp.sum(rows_of(weight) * qkv_grad, axis=1)
    ffn_term = jnp.sum(rows_of(gate_weight) * gate_grad + rows_of(up_weight) * up_grad, axis=1)
    columns = heads * HD
    room = -(-share // HD) * HD - share
    terms = jnp.pad(jnp.stack([ffn_term, attn_term]), ((0, 0), (0, room))).reshape(-1, HD)
    packed = jnp.concatenate([qkv_grad[:, columns:], bias_all.reshape(-1, HD), terms], axis=0)
    gathered = tensor_gather(packed, rank)
    term_rows = terms.shape[0]
    bias_count = bias_all.shape[1] // HD
    terms = gathered[:, share + bias_count :].reshape(ranks, 2, -1)[:, :, :share]
    ffn_gain_grad, attn_gain_grad = terms[0] + terms[1] + (terms[2] + terms[3])
    attn_gain_grad = attn_gain_grad / lax.dynamic_slice_in_dim(gain_one[0], begin, share, 0)
    ffn_gain_grad = ffn_gain_grad / lax.dynamic_slice_in_dim(gain_two[0], begin, share, 0)
    q_grad = qkv_grad[:, :columns]
    kv_parts = lax.dynamic_slice_in_dim(gathered, rank * (share // ranks), share // ranks, 1)
    k_grad = jnp.concatenate([kv_parts[2 * i] for i in range(KVH)], axis=1)
    v_grad = jnp.concatenate([kv_parts[2 * i + 1] for i in range(KVH)], axis=1)
    biases = gathered[:, share : share + bias_count]
    q_bias_grad = biases[:, :heads].reshape(-1)
    k_bias_grad = biases[0::2, heads].reshape(-1)
    v_bias_grad = biases[1::2, heads].reshape(-1)
    return (
        layer_out,
        token_grad,
        q_grad,
        q_bias_grad,
        k_grad,
        k_bias_grad,
        v_grad,
        v_bias_grad,
        o_grad,
        attn_gain_grad,
        ffn_gain_grad,
        gate_grad,
        up_grad,
        down_grad,
    )


def solution(mesh):
    in_specs = (
        P("dp", "seq", None),
        P("dp", None),
        P("dp", "seq", None),
        P(None, "tensor"),
        P("tensor"),
        P(),
        P(),
        P(),
        P(),
        P(None, "tensor"),
        P(),
        P(),
        P(None, "tensor"),
        P(None, "tensor"),
        P(None, "tensor"),
    )
    out_specs = (
        P("dp", "seq", None),
        P("dp", "seq", None),
        P(("dp", "seq"), "tensor"),
        P(),
        P(("dp", "seq", "tensor"), None),
        P(),
        P(("dp", "seq", "tensor"), None),
        P(),
        P(("dp", "seq"), "tensor"),
        P(("dp", "seq")),
        P(("dp", "seq")),
        P(("dp", "seq"), "tensor"),
        P(("dp", "seq"), "tensor"),
        P(("dp", "seq"), "tensor"),
    )
    return jax.shard_map(body, mesh=mesh, in_specs=in_specs, out_specs=out_specs, check_vma=False)
```

time: 768 us -> 590 us (0.77)
  Pallas kernels: 38.2 us -> 197 us
  waiting for transfers between devices: 386 us -> 231 us
  matrix products: 116 us -> 0 us
  blocking collectives: 61.8 us -> 0 us
  starting transfers between devices: 30 us -> 69.7 us
  other arithmetic: 57.2 us -> 20.3 us
  between operations: 14.9 us -> 2.12 us
  local copies, waits for them, and re-layouts: 58.9 us -> 68 us
    pallas_call x3 -> x50, Pallas kernels: 34.6 us -> 194 us  [the longest x49 188 us: __call__(): pl.pallas_call(run, grid_spec=pltpu.PrefetchScalarGridSpec(num_scalar_pre...]
    dot_general x22 -> x0, matrix products: 116 us -> none  [dot(): lax.dot_general(left, right, (((left_dim,), (right_dim,)), ((), ())), pre...]
    ppermute x5 -> x27, waiting for transfers between devices: 243 us -> 158 us  [the longest x8 50.1 us: relay(): self.last = lax.ppermute(sent, 'seq', flipped('seq', 1))]
    ppermute x4 -> x5, waiting for transfers between devices: 129 us -> 45.5 us  [chip_swap(): return lax.ppermute(value, 'tensor', flipped('tensor', 1))]
    psum x2 -> x0, blocking collectives: 61.8 us -> none  [the longest x1 55.9 us: body(): bias_all = lax.psum(rank_pick[:, None] * bias_sum, ('dp', 'seq', 'tensor'))]
    ppermute x5 -> x27, starting transfers between devices: 7.17 us -> 48.5 us  [the longest x7 16.6 us: own(): self.come = lax.ppermute(send, 'seq', flipped('seq', 0))]
    unnamed x111 -> x259, local copies, waits for them, and re-layouts: 25.6 us -> 58.9 us
    ppermute x3 -> x0, local copies, waits for them, and re-layouts: 17.1 us -> none  [rows_sum(): come = lax.ppermute(send, 'dp', flipped('dp', 0))]
  transfers between devices with their start and end apart: 29 -> 49, of which waited for: 14 -> 28; matrix products, arithmetic and copies ran while one was open for 23% -> 4% of each run, Pallas kernels for 0% -> 22%
where the time goes in v2:
time: 590 us; the launch traced here: 589 us
  waiting for transfers between devices  231 us (39%)
  Pallas kernels  197 us (33%)
  starting transfers between devices  69.7 us (12%)
  local copies, waits for them, and re-layouts  68 us (12%)
  other arithmetic  20.3 us (3%)
    pallas_call x49, Pallas kernels, __call__(): pl.pallas_call(run, grid_spec=pltpu.PrefetchScalarGridSpec(num_scalar_pre...  188 us
    unnamed x259, local copies, waits for them, and re-layouts  58.9 us
    ppermute x8, waiting for transfers between devices, relay(): self.last = lax.ppermute(sent, 'seq', flipped('seq', 1))  50.1 us
    ppermute x5, waiting for transfers between devices, chip_swap(): return lax.ppermute(value, 'tensor', flipped('tensor', 1))  45.5 us
    ppermute x7, waiting for transfers between devices, own(): self.come = lax.ppermute(send, 'seq', flipped('seq', 0))  44.7 us
    ppermute x7, waiting for transfers between devices, __init__(): self.come = lax.ppermute(sent, 'dp', flipped('dp', 0))  24 us
    ppermute x1, waiting for transfers between devices, settle(): self.final = lax.ppermute(sent, 'dp', flipped('dp', 0))  17 us
    ppermute x7, starting transfers between devices, own(): self.come = lax.ppermute(send, 'seq', flipped('seq', 0))  16.6 us
  transfers between devices with their start and end apart: 49, of which 28 were waited for; matrix products, arithmetic and copies ran while one was open for 4% of the time, Pallas kernels for 22%

profile of v2, /device:TPU:0, one launch (start us, length us, event | category | flops | bytes accessed | tf_op | source)
XLA Modules:
  0.0 588.8 jit_solution(13169743538724169271)
XLA Ops:
  11.4 3.6 first.1
  17.5 6.6 %collective-permute-start = (bf16[2,512,128]{2,1,0:T(8,128)(2,1)S(1)}, bf16[2,512,128]{2,1,0:T(8,128)(2,1)}, u32[]{:S(2)}, u32[]{:S(2)}) collective-permute-start(bf16[2,512,128]{2,1,0:T(8,128)(2,1)S(1)} %bitcast.81), channel_id=1, source_target_pairs={{0,8},{4,12},{1,9},{5,13},{2,10},{6,14},{3,11},{7,15},{16,24},{20,... | collective-permute-start | bytes 786440 | tf_op jit(solution)/shard_map/ppermute | solution.py:57
  24.2 4.2 collective-permute-start.1
  30.1 3.9 collective-permute-done.1.refs_1_.refs_10_
  37.0 6.2 %attend.1 = (bf16[2,512,384]{2,1,0:T(8,128)(2,1)S(1)}, f32[2,2,768]{2,1,0:T(2,128)S(1)}) custom-call(s32[2,2]{1,0:T(2,128)S(1)} %shift-right-logical_maximum_fusion.low_ref.refs_0_, s32[1]{0:T(128)} %bitcast.core_ref.refs_0_.refs_1_, bf16[2,512,384]{2,1,0:T(8,128)(2,1)S(1)} %bitcast.78, s32[2,1,512]{2,1,0:T(1,128)S(1)} %sub.48.start_ref.refs_3_, ...), custom_call_target="tpu_custom_call" | custom-call | flops 8000000 | bytes 4194 | tf_op jit(solution)/shard_map/attend/pallas_call | solution.py:239
  48.8 3.5 narrow.9
  61.7 4.1 copy-done.4
  65.8 9.3 %grad_hidden.1 = (bf16[1024,2240]{1,0:T(8,128)(2,1)S(1)}, f32[8,128]{1,0:T(8,128)S(1)}) custom-call(bf16[1024,1536]{1,0:T(8,128)(2,1)S(1)} %get-tuple-element.141.refs_0_.refs_5_, bf16[2240,1536]{1,0:T(8,128)(2,1)S(1)} %bitcast.63, f32[8,128]{1,0:T(8,128)S(1)} %get-tuple-element.142.refs_2_), custom_call_target="tpu_custom_call" | custom-call | flops 7046430 | bytes 15728 | tf_op jit(solution)/shard_map/grad_hidden/pallas_call | solution.py:78
  79.0 10.1 %collective-permute-done.6.refs_3_ = bf16[512,1536]{1,0:T(8,128)(2,1)} collective-permute-done((bf16[512,1536]{1,0:T(8,128)(2,1)}, bf16[512,1536]{1,0:T(8,128)(2,1)}, u32[]{:S(2)}, u32[]{:S(2)}) %collective-permute-start.6) | collective-permute-done | bytes 1572896 | tf_op jit(solution)/shard_map/ppermute | solution.py:51
  89.1 4.5 middle.1
  95.3 3.5 collective-permute-done.7.refs_1_
  101.7 22.2 %gated.1 = (bf16[1024,2240]{1,0:T(8,128)(2,1)S(1)}, bf16[1024,2240]{1,0:T(8,128)(2,1)S(1)}, bf16[1024,2240]{1,0:T(8,128)(2,1)S(1)}, f32[8,128]{1,0:T(8,128)S(1)}) custom-call(bf16[512,1536]{1,0:T(8,128)(2,1)} %get-tuple-element.146.refs_0_, bf16[512,1536]{1,0:T(8,128)(2,1)S(1)} %collective-permute-done.7.refs_1_, bf16[1024,2240]{1,0:T(8,128)(2,1)S(1)} %copy-done.47, ...), custom_call_target="tpu_custom_call" | custom-call | flops 14092861 | bytes 31457 | tf_op jit(solution)/shard_map/gated/pallas_call | solution.py:78
  124.0 4.5 share.15
  128.5 5.8 share.16
  136.5 10.6 %narrow.10 = (bf16[512,1536]{1,0:T(8,128)(2,1)S(1)}, f32[8,128]{1,0:T(8,128)S(1)}) custom-call(bf16[1024,2240]{1,0:T(8,128)(2,1)S(1)} %get-tuple-element.150.refs_0_.refs_3_, bf16[2240,1536]{1,0:T(8,128)(2,1)S(1)} %bitcast.61, bf16[1024,2240]{1,0:T(8,128)(2,1)S(1)} %get-tuple-element.151.refs_2_.refs_3_, bf16[2240,1536]{1,0:T(8,128)(2,1)} %bitcast.88, ...), custom_call_target="tpu_custom_call" | custom-call | flops 7046430 | bytes 19922 | tf_op jit(solution)/shard_map/narrow/pallas_call | solution.py:78
  148.8 10.6 %collective-permute-start.12 = (bf16[768,1024]{1,0:T(8,128)(2,1)}, bf16[768,1024]{1,0:T(8,128)(2,1)}, u32[]{:S(2)}, u32[]{:S(2)}) collective-permute-start(bf16[768,1024]{1,0:T(8,128)(2,1)} %get-tuple-element.168), channel_id=1, source_target_pairs={{0,4},{4,0},{8,12},{12,8},{1,5},{5,1},{9,13},{13,9},{2,6},{6,2},{1... | collective-permute-start | bytes 4718600 | tf_op jit(solution)/shard_map/ppermute | solution.py:979
  159.4 11.0 %narrow.11 = (bf16[512,1536]{1,0:T(8,128)(2,1)}, f32[8,128]{1,0:T(8,128)S(1)}) custom-call(bf16[1024,2240]{1,0:T(8,128)(2,1)S(1)} %get-tuple-element.150.refs_0_.refs_3_, bf16[2240,1536]{1,0:T(8,128)(2,1)S(1)} %bitcast.62, bf16[1024,2240]{1,0:T(8,128)(2,1)S(1)} %get-tuple-element.151.refs_2_.refs_3_, bf16[2240,1536]{1,0:T(8,128)(2,1)} %bitcast.89, ...), custom_call_target="tpu_custom_call" | custom-call | flops 7046430 | bytes 19922 | tf_op jit(solution)/shard_map/narrow/pallas_call | solution.py:78
  171.9 3.7 turn.4
  188.6 5.2 narrow.12
  197.4 5.9 %share.20 = (bf16[384,1280]{1,0:T(8,128)(2,1)S(1)}, bf16[384,1280]{1,0:T(8,128)(2,1)S(1)}, f32[8,128]{1,0:T(8,128)S(1)}) custom-call(s32[1]{0:T(128)} %bitcast.19.refs_0_, s32[4]{0:T(128)S(1)} %pad_add_fusion.refs_1_, bf16[1536,1024]{1,0:T(8,128)(2,1)S(1)} %copy-done.9, bf16[1024,2240]{1,0:T(8,128)(2,1)S(1)} %bitcast.57, ...), custom_call_target="tpu_custom_call" | custom-call | flops 2013265 | bytes 6160 | tf_op jit(solution)/shard_map/share/pallas_call | solution.py:78
  211.1 3.5 norm_back.2
  226.7 8.5 %attend_back.1 = (bf16[2,512,384]{2,1,0:T(8,128)(2,1)S(1)}, bf16[2,2,1536,128]{3,2,1,0:T(8,128)(2,1)S(1)}, f32[8,128]{1,0:T(8,128)S(1)}) custom-call(s32[2,2]{1,0:T(2,128)S(1)} %shift-right-logical_maximum_fusion.low_ref.refs_0_, s32[1]{0:T(128)} %bitcast.core_ref.refs_0_.refs_1_, bf16[2,512,384]{2,1,0:T(8,128)(2,1)S(1)} %bitcast.79, ...), custom_call_target="tpu_custom_call" | custom-call | flops 20000000 | bytes 6291 | tf_op jit(solution)/shard_map/attend_back/pallas_call | solution.py:78
  236.3 8.8 %collective-permute-start.19 = (bf16[384,1280]{1,0:T(8,128)(2,1)S(1)}, bf16[384,1280]{1,0:T(8,128)(2,1)}, u32[]{:S(2)}, u32[]{:S(2)}) collective-permute-start(bf16[384,1280]{1,0:T(8,128)(2,1)S(1)} %copy-done.86), channel_id=1, source_target_pairs={{0,4},{4,0},{8,12},{12,8},{1,5},{5,1},{9,13},{13,9},{2,6},{6,2},{1... | collective-permute-start | bytes 2949128 | tf_op jit(solution)/shard_map/ppermute | solution.py:962
  245.1 7.2 %collective-permute-start.20 = (bf16[384,1024]{1,0:T(8,128)(2,1)}, bf16[384,1024]{1,0:T(8,128)(2,1)S(1)}, u32[]{:S(2)}, u32[]{:S(2)}) collective-permute-start(bf16[384,1024]{1,0:T(8,128)(2,1)} %get-tuple-element.188), channel_id=1, source_target_pairs={{0,8},{4,12},{8,0},{12,4},{1,9},{5,13},{9,1},{13,5},{2,10},{6,14},... | collective-permute-start | bytes 2359304 | tf_op jit(solution)/shard_map/ppermute | solution.py:967
  252.4 6.0 %narrow.13 = (bf16[512,1536]{1,0:T(8,128)(2,1)}, f32[8,128]{1,0:T(8,128)S(1)}) custom-call(bf16[1024,2240]{1,0:T(8,128)(2,1)S(1)} %bitcast.57, bf16[2240,1536]{1,0:T(8,128)(2,1)S(1)} %bitcast.69, bf16[512,1536]{1,0:T(8,128)(2,1)S(1)} %collective-permute-done.9.refs_2_, f32[8,128]{1,0:T(8,128)S(1)} %get-tuple-element.177.refs_3_), custom_call_target="tpu_custom_call" | custom-call | flops 3523215 | bytes 10747 | tf_op jit(solution)/shard_map/narrow/pallas_call | solution.py:78
  265.7 17.9 %collective-permute-done.20.refs_3_ = bf16[384,1024]{1,0:T(8,128)(2,1)S(1)} collective-permute-done((bf16[384,1024]{1,0:T(8,128)(2,1)}, bf16[384,1024]{1,0:T(8,128)(2,1)S(1)}, u32[]{:S(2)}, u32[]{:S(2)}) %collective-permute-start.20) | collective-permute-done | bytes 786464 | tf_op jit(solution)/shard_map/ppermute | solution.py:967
  289.0 6.2 %share.22 = (bf16[384,1280]{1,0:T(8,128)(2,1)}, bf16[384,1280]{1,0:T(8,128)(2,1)S(1)}, f32[8,128]{1,0:T(8,128)S(1)}) custom-call(s32[1]{0:T(128)} %bitcast.19.refs_0_, s32[4]{0:T(128)S(1)} %pad_add_fusion.refs_1_, bf16[1536,1024]{1,0:T(8,128)(2,1)S(1)} %get-tuple-element.159.refs_2_, bf16[1024,2240]{1,0:T(8,128)(2,1)S(1)} %bitcast.55, ...), custom_call_target="tpu_custom_call" | custom-call | flops 2013265 | bytes 6160 | tf_op jit(solution)/shard_map/share/pallas_call | solution.py:78
  295.2 9.1 %collective-permute-done.17.refs_6_ = bf16[2,512,128]{2,1,0:T(8,128)(2,1)S(1)} collective-permute-done((bf16[2,512,128]{2,1,0:T(8,128)(2,1)S(1)}, bf16[2,512,128]{2,1,0:T(8,128)(2,1)S(1)}, u32[]{:S(2)}, u32[]{:S(2)}) %collective-permute-start.17) | collective-permute-done | bytes 262176 | tf_op jit(solution)/shard_map/ppermute | solution.py:57
  321.8 22.3 %collective-permute-done.24.refs_4_ = bf16[768,1024]{1,0:T(8,128)(2,1)S(1)} collective-permute-done((bf16[768,1024]{1,0:T(8,128)(2,1)S(1)}, bf16[768,1024]{1,0:T(8,128)(2,1)S(1)}, u32[]{:S(2)}, u32[]{:S(2)}) %collective-permute-start.24) | collective-permute-done | bytes 1572896 | tf_op jit(solution)/shard_map/ppermute | solution.py:953
  344.1 4.1 share.25
  353.4 29.7 %collective-permute-done.14.refs_2_ = bf16[512,1536]{1,0:T(8,128)(2,1)S(1)} collective-permute-done((bf16[512,1536]{1,0:T(8,128)(2,1)}, bf16[512,1536]{1,0:T(8,128)(2,1)S(1)}, u32[]{:S(2)}, u32[]{:S(2)}) %collective-permute-start.14) | collective-permute-done | bytes 1572896 | tf_op jit(solution)/shard_map/ppermute | solution.py:51
  383.1 3.9 layer.1
  389.1 9.9 %collective-permute-done.35 = f32[8,512]{1,0:T(8,128)S(1)} collective-permute-done((f32[8,512]{1,0:T(8,128)S(1)}, f32[8,512]{1,0:T(8,128)S(1)}, u32[]{:S(2)}, u32[]{:S(2)}) %collective-permute-start.35) | collective-permute-done | bytes 16416 | tf_op jit(solution)/shard_map/ppermute | solution.py:1057
  401.1 6.8 %collective-permute-done.36 = f32[8,512]{1,0:T(8,128)S(1)} collective-permute-done((f32[8,512]{1,0:T(8,128)S(1)}, f32[8,512]{1,0:T(8,128)S(1)}, u32[]{:S(2)}, u32[]{:S(2)}) %collective-permute-start.36) | collective-permute-done | bytes 16416 | tf_op jit(solution)/shard_map/ppermute | solution.py:1058
  408.0 4.8 collective-permute-done.37
  414.6 17.0 %collective-permute-done.48 = bf16[192,1024]{1,0:T(8,128)(2,1)S(1)} collective-permute-done((bf16[192,1024]{1,0:T(8,128)(2,1)S(1)}, bf16[192,1024]{1,0:T(8,128)(2,1)S(1)}, u32[]{:S(2)}, u32[]{:S(2)}) %collective-permute-start.48) | collective-permute-done | bytes 393248 | tf_op jit(solution)/shard_map/ppermute | solution.py:987
  431.9 4.7 share.26
  441.7 4.5 constant_dynamic-slice_fusion
  459.5 6.4 %place.2 = (f32[1024,1536]{1,0:T(8,128)}, f32[8,128]{1,0:T(8,128)S(1)}) custom-call(s32[1]{0:T(128)} %bitcast.core_ref.refs_0_.refs_1_, f32[512,1536]{1,0:T(8,128)} %get-tuple-element.214.refs_1_, f32[512,1536]{1,0:T(8,128)} %collective-permute-done.26.refs_2_, f32[8,128]{1,0:T(8,128)S(1)} %get-tuple-element.222.refs_3_), custom_call_target="tpu_custom_call" | custom-call | bytes 6291 | tf_op jit(solution)/shard_map/place/pallas_call | solution.py:78
  466.0 4.9 place.3
  475.0 6.8 %collective-permute-done.31.refs_1_ = bf16[384,384]{1,0:T(8,128)(2,1)S(1)} collective-permute-done((bf16[384,384]{1,0:T(8,128)(2,1)S(1)}, bf16[384,384]{1,0:T(8,128)(2,1)S(1)}, u32[]{:S(2)}, u32[]{:S(2)}) %collective-permute-start.31) | collective-permute-done | bytes 294944 | tf_op jit(solution)/shard_map/ppermute | solution.py:962
  493.7 10.8 %collective-permute-done.33.refs_1_ = bf16[384,512]{1,0:T(8,128)(2,1)S(1)} collective-permute-done((bf16[384,512]{1,0:T(8,128)(2,1)S(1)}, bf16[384,512]{1,0:T(8,128)(2,1)S(1)}, u32[]{:S(2)}, u32[]{:S(2)}) %collective-permute-start.33) | collective-permute-done | bytes 393248 | tf_op jit(solution)/shard_map/ppermute | solution.py:962
  504.6 4.9 share.29
  509.7 6.7 %collective-permute-done.38 = bf16[192,1280]{1,0:T(8,128)(2,1)S(1)} collective-permute-done((bf16[192,1280]{1,0:T(8,128)(2,1)S(1)}, bf16[192,1280]{1,0:T(8,128)(2,1)S(1)}, u32[]{:S(2)}, u32[]{:S(2)}) %collective-permute-start.38) | collective-permute-done | bytes 491552 | tf_op jit(solution)/shard_map/ppermute | solution.py:967
  516.5 8.8 %collective-permute-done.39 = bf16[192,1024]{1,0:T(8,128)(2,1)S(1)} collective-permute-done((bf16[192,1024]{1,0:T(8,128)(2,1)S(1)}, bf16[192,1024]{1,0:T(8,128)(2,1)S(1)}, u32[]{:S(2)}, u32[]{:S(2)}) %collective-permute-start.39) | collective-permute-done | bytes 393248 | tf_op jit(solution)/shard_map/ppermute | solution.py:967
  529.6 24.1 %collective-permute-done.42.refs_1_ = bf16[384,1024]{1,0:T(8,128)(2,1)S(1)} collective-permute-done((bf16[384,1024]{1,0:T(8,128)(2,1)S(1)}, bf16[384,1024]{1,0:T(8,128)(2,1)S(1)}, u32[]{:S(2)}, u32[]{:S(2)}) %collective-permute-start.42) | collective-permute-done | bytes 786464 | tf_op jit(solution)/shard_map/ppermute | solution.py:962
  555.7 16.6 %collective-permute-done.43 = bf16[192,1024]{1,0:T(8,128)(2,1)S(1)} collective-permute-done((bf16[192,1024]{1,0:T(8,128)(2,1)S(1)}, bf16[192,1024]{1,0:T(8,128)(2,1)S(1)}, u32[]{:S(2)}, u32[]{:S(2)}) %collective-permute-start.43) | collective-permute-done | bytes 393248 | tf_op jit(solution)/shard_map/ppermute | solution.py:967
  581.5 3.5 collective-permute-done.45
  (426 shorter events, 179.3 us)
Async XLA Ops:
  17.5 12.6 %collective-permute-start = (bf16[2,512,128]{2,1,0:T(8,128)(2,1)S(1)}, bf16[2,512,128]{2,1,0:T(8,128)(2,1)}, u32[]{:S(2)}, u32[]{:S(2)}) collective-permute-start(bf16[2,512,128]{2,1,0:T(8,128)(2,1)S(1)} %bitcast.81), channel_id=1, source_target_pairs={{0,8},{4,12},{1,9},{5,13},{2,10},{6,14},{3,11},{7,15},{16,24},{20,... | collective-permute-start | bytes 786440 | tf_op jit(solution)/shard_map/ppermute | solution.py:57
  24.2 9.8 %collective-permute-start.1 = (bf16[2,512,128]{2,1,0:T(8,128)(2,1)S(1)}, bf16[2,512,128]{2,1,0:T(8,128)(2,1)}, u32[]{:S(2)}, u32[]{:S(2)}) collective-permute-start(bf16[2,512,128]{2,1,0:T(8,128)(2,1)S(1)} %bitcast.82), channel_id=1, source_target_pairs={{0,4},{4,8},{8,12},{1,5},{5,9},{9,13},{2,6},{6,10},{10,14},{3,7},{... | collective-permute-start | bytes 786440 | tf_op jit(solution)/shard_map/ppermute | solution.py:57
  28.4 5.8 collective-permute-start.4
  30.1 4.0 collective-permute-start.2
  45.4 3.5 collective-permute-start.5
  52.4 36.7 %collective-permute-start.6 = (bf16[512,1536]{1,0:T(8,128)(2,1)}, bf16[512,1536]{1,0:T(8,128)(2,1)}, u32[]{:S(2)}, u32[]{:S(2)}) collective-permute-start(bf16[512,1536]{1,0:T(8,128)(2,1)} %get-tuple-element.138.refs_2_), channel_id=1, source_target_pairs={{0,2},{1,3},{2,0},{3,1},{4,6},{5,7},{6,4},{7,5},{8,10},{9,11},{10,... | collective-permute-start | bytes 4718600 | tf_op jit(solution)/shard_map/ppermute | solution.py:51
  95.2 3.6 collective-permute-start.7
  147.1 12.3 %collective-permute-start.8 = (bf16[512,1536]{1,0:T(8,128)(2,1)S(1)}, bf16[512,1536]{1,0:T(8,128)(2,1)S(1)}, u32[]{:S(2)}, u32[]{:S(2)}) collective-permute-start(bf16[512,1536]{1,0:T(8,128)(2,1)S(1)} %get-tuple-element.156), channel_id=1, source_target_pairs={{0,1},{1,0},{2,3},{3,2},{4,5},{5,4},{6,7},{7,6},{8,9},{9,8},{10,11... | collective-permute-start | bytes 4718600 | tf_op jit(solution)/shard_map/ppermute | solution.py:47
  147.3 50.1 %collective-permute-start.11 = (bf16[768,1280]{1,0:T(8,128)(2,1)}, bf16[768,1280]{1,0:T(8,128)(2,1)}, u32[]{:S(2)}, u32[]{:S(2)}) collective-permute-start(bf16[768,1280]{1,0:T(8,128)(2,1)} %get-tuple-element.166), channel_id=1, source_target_pairs={{0,16},{16,0},{1,17},{17,1},{2,18},{18,2},{3,19},{19,3},{4,20},{20... | collective-permute-start | bytes 5898248 | tf_op jit(solution)/shard_map/ppermute | solution.py:953
  148.8 45.5 %collective-permute-start.12 = (bf16[768,1024]{1,0:T(8,128)(2,1)}, bf16[768,1024]{1,0:T(8,128)(2,1)}, u32[]{:S(2)}, u32[]{:S(2)}) collective-permute-start(bf16[768,1024]{1,0:T(8,128)(2,1)} %get-tuple-element.168), channel_id=1, source_target_pairs={{0,4},{4,0},{8,12},{12,8},{1,5},{5,1},{9,13},{13,9},{2,6},{6,2},{1... | collective-permute-start | bytes 4718600 | tf_op jit(solution)/shard_map/ppermute | solution.py:979
  170.3 36.3 %collective-permute-start.10 = (bf16[512,1536]{1,0:T(8,128)(2,1)}, bf16[512,1536]{1,0:T(8,128)(2,1)S(1)}, u32[]{:S(2)}, u32[]{:S(2)}) collective-permute-start(bf16[512,1536]{1,0:T(8,128)(2,1)} %get-tuple-element.165.refs_1_), channel_id=1, source_target_pairs={{0,2},{1,3},{2,0},{3,1},{4,6},{5,7},{6,4},{7,5},{8,10},{9,11},{10,... | collective-permute-start | bytes 4718600 | tf_op jit(solution)/shard_map/ppermute | solution.py:51
  216.2 3.4 collective-permute-start.13
  217.4 71.5 %collective-permute-start.18 = (bf16[768,1280]{1,0:T(8,128)(2,1)}, bf16[768,1280]{1,0:T(8,128)(2,1)}, u32[]{:S(2)}, u32[]{:S(2)}) collective-permute-start(bf16[768,1280]{1,0:T(8,128)(2,1)} %copy-done.81), channel_id=1, source_target_pairs={{0,16},{16,0},{1,17},{17,1},{2,18},{18,2},{3,19},{19,3},{4,20},{20... | collective-permute-start | bytes 5898248 | tf_op jit(solution)/shard_map/ppermute | solution.py:953
  217.9 34.4 %collective-permute-start.9 = (bf16[512,1536]{1,0:T(8,128)(2,1)}, bf16[512,1536]{1,0:T(8,128)(2,1)S(1)}, u32[]{:S(2)}, u32[]{:S(2)}) collective-permute-start(bf16[512,1536]{1,0:T(8,128)(2,1)} %copy-done.84), channel_id=1, source_target_pairs={{0,1},{1,0},{2,3},{3,2},{4,5},{5,4},{6,7},{7,6},{8,9},{9,8},{10,11... | collective-permute-start | bytes 4718600 | tf_op jit(solution)/shard_map/ppermute | solution.py:47
  236.1 22.3 %collective-permute-start.15 = (bf16[2,1536,128]{2,1,0:T(8,128)(2,1)S(1)}, bf16[2,1536,128]{2,1,0:T(8,128)(2,1)S(1)}, u32[]{:S(2)}, u32[]{:S(2)}) collective-permute-start(bf16[2,1536,128]{2,1,0:T(8,128)(2,1)S(1)} %slice_bitcast_fusion), channel_id=1, source_target_pairs={{0,1},{1,0},{2,3},{3,2},{4,5},{5,4},{6,7},{7,6},{8,9},{9,8},{10,11... | collective-permute-start | bytes 2359304 | tf_op jit(solution)/shard_map/ppermute | solution.py:47
  236.3 50.5 %collective-permute-start.19 = (bf16[384,1280]{1,0:T(8,128)(2,1)S(1)}, bf16[384,1280]{1,0:T(8,128)(2,1)}, u32[]{:S(2)}, u32[]{:S(2)}) collective-permute-start(bf16[384,1280]{1,0:T(8,128)(2,1)S(1)} %copy-done.86), channel_id=1, source_target_pairs={{0,4},{4,0},{8,12},{12,8},{1,5},{5,1},{9,13},{13,9},{2,6},{6,2},{1... | collective-permute-start | bytes 2949128 | tf_op jit(solution)/shard_map/ppermute | solution.py:962
  245.1 38.5 %collective-permute-start.20 = (bf16[384,1024]{1,0:T(8,128)(2,1)}, bf16[384,1024]{1,0:T(8,128)(2,1)S(1)}, u32[]{:S(2)}, u32[]{:S(2)}) collective-permute-start(bf16[384,1024]{1,0:T(8,128)(2,1)} %get-tuple-element.188), channel_id=1, source_target_pairs={{0,8},{4,12},{8,0},{12,4},{1,9},{5,13},{9,1},{13,5},{2,10},{6,14},... | collective-permute-start | bytes 2359304 | tf_op jit(solution)/shard_map/ppermute | solution.py:967
  258.7 36.6 %collective-permute-start.16 = (bf16[2,512,128]{2,1,0:T(8,128)(2,1)S(1)}, bf16[2,512,128]{2,1,0:T(8,128)(2,1)S(1)}, u32[]{:S(2)}, u32[]{:S(2)}) collective-permute-start(bf16[2,512,128]{2,1,0:T(8,128)(2,1)S(1)} %get-tuple-element.183), channel_id=1, source_target_pairs={{4,0},{8,4},{12,8},{5,1},{9,5},{13,9},{6,2},{10,6},{14,10},{7,3},{... | collective-permute-start | bytes 786440 | tf_op jit(solution)/shard_map/ppermute | solution.py:57
  260.1 44.2 %collective-permute-start.17 = (bf16[2,512,128]{2,1,0:T(8,128)(2,1)S(1)}, bf16[2,512,128]{2,1,0:T(8,128)(2,1)S(1)}, u32[]{:S(2)}, u32[]{:S(2)}) collective-permute-start(bf16[2,512,128]{2,1,0:T(8,128)(2,1)S(1)} %get-tuple-element.184), channel_id=1, source_target_pairs={{8,0},{12,4},{9,1},{13,5},{10,2},{14,6},{11,3},{15,7},{24,16},{28,... | collective-permute-start | bytes 786440 | tf_op jit(solution)/shard_map/ppermute | solution.py:57
  307.2 3.5 collective-permute-start.21
  307.3 36.8 %collective-permute-start.24 = (bf16[768,1024]{1,0:T(8,128)(2,1)S(1)}, bf16[768,1024]{1,0:T(8,128)(2,1)S(1)}, u32[]{:S(2)}, u32[]{:S(2)}) collective-permute-start(bf16[768,1024]{1,0:T(8,128)(2,1)S(1)} %copy-done.83), channel_id=1, source_target_pairs={{0,16},{16,0},{1,17},{17,1},{2,18},{18,2},{3,19},{19,3},{4,20},{20... | collective-permute-start | bytes 4718600 | tf_op jit(solution)/shard_map/ppermute | solution.py:953
  312.9 37.3 %collective-permute-start.22 = (bf16[512,1536]{1,0:T(8,128)(2,1)S(1)}, bf16[512,1536]{1,0:T(8,128)(2,1)S(1)}, u32[]{:S(2)}, u32[]{:S(2)}) collective-permute-start(bf16[512,1536]{1,0:T(8,128)(2,1)S(1)} %get-tuple-element.201.refs_1_), channel_id=1, source_target_pairs={{0,2},{1,3},{2,0},{3,1},{4,6},{5,7},{6,4},{7,5},{8,10},{9,11},{10,... | collective-permute-start | bytes 4718600 | tf_op jit(solution)/shard_map/ppermute | solution.py:51
  314.4 33.8 %collective-permute-start.23 = (bf16[384,1280]{1,0:T(8,128)(2,1)}, bf16[384,1280]{1,0:T(8,128)(2,1)S(1)}, u32[]{:S(2)}, u32[]{:S(2)}) collective-permute-start(bf16[384,1280]{1,0:T(8,128)(2,1)} %get-tuple-element.204), channel_id=1, source_target_pairs={{0,4},{4,0},{8,12},{12,8},{1,5},{5,1},{9,13},{13,9},{2,6},{6,2},{1... | collective-permute-start | bytes 2949128 | tf_op jit(solution)/shard_map/ppermute | solution.py:962
  316.6 66.5 %collective-permute-start.14 = (bf16[512,1536]{1,0:T(8,128)(2,1)}, bf16[512,1536]{1,0:T(8,128)(2,1)S(1)}, u32[]{:S(2)}, u32[]{:S(2)}) collective-permute-start(bf16[512,1536]{1,0:T(8,128)(2,1)} %get-tuple-element.178.refs_1_), channel_id=1, source_target_pairs={{0,2},{1,3},{2,0},{3,1},{4,6},{5,7},{6,4},{7,5},{8,10},{9,11},{10,... | collective-permute-start | bytes 4718600 | tf_op jit(solution)/shard_map/ppermute | solution.py:51
  353.4 104.5 %collective-permute-start.26 = (f32[512,1536]{1,0:T(8,128)}, f32[512,1536]{1,0:T(8,128)}, u32[]{:S(2)}, u32[]{:S(2)}) collective-permute-start(f32[512,1536]{1,0:T(8,128)} %get-tuple-element.214.refs_1_), channel_id=1, source_target_pairs={{0,1},{1,0},{2,3},{3,2},{4,5},{5,4},{6,7},{7,6},{8,9},{9,8},{10,11... | collective-permute-start | bytes 9437192 | tf_op jit(solution)/shard_map/ppermute | solution.py:47
  353.4 54.5 %collective-permute-start.29 = (bf16[768,1280]{1,0:T(8,128)(2,1)S(1)}, bf16[768,1280]{1,0:T(8,128)(2,1)S(1)}, u32[]{:S(2)}, u32[]{:S(2)}) collective-permute-start(bf16[768,1280]{1,0:T(8,128)(2,1)S(1)} %copy-done.80), channel_id=1, source_target_pairs={{0,16},{16,0},{1,17},{17,1},{2,18},{18,2},{3,19},{19,3},{4,20},{20... | collective-permute-start | bytes 5898248 | tf_op jit(solution)/shard_map/ppermute | solution.py:953
  387.0 52.9 %collective-permute-start.25 = (bf16[512,1536]{1,0:T(8,128)(2,1)}, bf16[512,1536]{1,0:T(8,128)(2,1)}, u32[]{:S(2)}, u32[]{:S(2)}) collective-permute-start(bf16[512,1536]{1,0:T(8,128)(2,1)} %get-tuple-element.213.refs_1_), channel_id=1, source_target_pairs={{0,1},{1,0},{2,3},{3,2},{4,5},{5,4},{6,7},{7,6},{8,9},{9,8},{10,11... | collective-permute-start | bytes 4718600 | tf_op jit(solution)/shard_map/ppermute | solution.py:47
  387.0 52.9 %collective-permute-start.28 = (bf16[384,1024]{1,0:T(8,128)(2,1)}, bf16[384,1024]{1,0:T(8,128)(2,1)}, u32[]{:S(2)}, u32[]{:S(2)}) collective-permute-start(bf16[384,1024]{1,0:T(8,128)(2,1)} %get-tuple-element.217), channel_id=1, source_target_pairs={{0,4},{4,0},{8,12},{12,8},{1,5},{5,1},{9,13},{13,9},{2,6},{6,2},{1... | collective-permute-start | bytes 2359304 | tf_op jit(solution)/shard_map/ppermute | solution.py:962
  389.1 9.9 %collective-permute-start.35 = (f32[8,512]{1,0:T(8,128)S(1)}, f32[8,512]{1,0:T(8,128)S(1)}, u32[]{:S(2)}, u32[]{:S(2)}) collective-permute-start(f32[8,512]{1,0:T(8,128)S(1)} %get-tuple-element.238), channel_id=1, source_target_pairs={{0,16},{16,0},{1,17},{17,1},{2,18},{18,2},{3,19},{19,3},{4,20},{20... | collective-permute-start | bytes 49160 | tf_op jit(solution)/shard_map/ppermute | solution.py:1057
  399.0 8.9 %collective-permute-start.36 = (f32[8,512]{1,0:T(8,128)S(1)}, f32[8,512]{1,0:T(8,128)S(1)}, u32[]{:S(2)}, u32[]{:S(2)}) collective-permute-start(f32[8,512]{1,0:T(8,128)S(1)} %add.126), channel_id=1, source_target_pairs={{0,4},{4,0},{8,12},{12,8},{1,5},{5,1},{9,13},{13,9},{2,6},{6,2},{1... | collective-permute-start | bytes 49160 | tf_op jit(solution)/shard_map/ppermute | solution.py:1058
  407.9 29.6 %collective-permute-start.27 = (bf16[768,384]{1,0:T(8,128)(2,1)S(1)}, bf16[768,384]{1,0:T(8,128)(2,1)S(1)}, u32[]{:S(2)}, u32[]{:S(2)}) collective-permute-start(bf16[768,384]{1,0:T(8,128)(2,1)S(1)} %copy-done.89), channel_id=1, source_target_pairs={{0,16},{16,0},{1,17},{17,1},{2,18},{18,2},{3,19},{19,3},{4,20},{20... | collective-permute-start | bytes 1769480 | tf_op jit(solution)/shard_map/ppermute | solution.py:953
  407.9 4.9 collective-permute-start.37
  412.8 18.8 %collective-permute-start.48 = (bf16[192,1024]{1,0:T(8,128)(2,1)S(1)}, bf16[192,1024]{1,0:T(8,128)(2,1)S(1)}, u32[]{:S(2)}, u32[]{:S(2)}) collective-permute-start(bf16[192,1024]{1,0:T(8,128)(2,1)S(1)} %copy-done.94), channel_id=1, source_target_pairs={{0,16},{16,0},{1,17},{17,1},{2,18},{18,2},{3,19},{19,3},{4,20},{20... | collective-permute-start | bytes 1179656 | tf_op jit(solution)/shard_map/ppermute | solution.py:987
  431.6 73.0 %collective-permute-start.41 = (bf16[768,1024]{1,0:T(8,128)(2,1)}, bf16[768,1024]{1,0:T(8,128)(2,1)}, u32[]{:S(2)}, u32[]{:S(2)}) collective-permute-start(bf16[768,1024]{1,0:T(8,128)(2,1)} %get-tuple-element.242), channel_id=1, source_target_pairs={{0,16},{16,0},{1,17},{17,1},{2,18},{18,2},{3,19},{19,3},{4,20},{20... | collective-permute-start | bytes 4718600 | tf_op jit(solution)/shard_map/ppermute | solution.py:953
  438.3 35.5 %collective-permute-start.32 = (bf16[384,1280]{1,0:T(8,128)(2,1)}, bf16[384,1280]{1,0:T(8,128)(2,1)}, u32[]{:S(2)}, u32[]{:S(2)}) collective-permute-start(bf16[384,1280]{1,0:T(8,128)(2,1)} %get-tuple-element.230), channel_id=1, source_target_pairs={{0,4},{4,0},{8,12},{12,8},{1,5},{5,1},{9,13},{13,9},{2,6},{6,2},{1... | collective-permute-start | bytes 2949128 | tf_op jit(solution)/shard_map/ppermute | solution.py:962
  439.9 48.6 %collective-permute-start.47 = (bf16[192,1280]{1,0:T(8,128)(2,1)}, bf16[192,1280]{1,0:T(8,128)(2,1)}, u32[]{:S(2)}, u32[]{:S(2)}) collective-permute-start(bf16[192,1280]{1,0:T(8,128)(2,1)} %copy-done.90), channel_id=1, source_target_pairs={{0,8},{4,12},{8,0},{12,4},{1,9},{5,13},{9,1},{13,5},{2,10},{6,14},... | collective-permute-start | bytes 1474568 | tf_op jit(solution)/shard_map/ppermute | solution.py:967
  439.9 44.3 %collective-permute-start.30 = (bf16[768,512]{1,0:T(8,128)(2,1)}, bf16[768,512]{1,0:T(8,128)(2,1)}, u32[]{:S(2)}, u32[]{:S(2)}) collective-permute-start(bf16[768,512]{1,0:T(8,128)(2,1)} %copy-done.87), channel_id=1, source_target_pairs={{0,16},{16,0},{1,17},{17,1},{2,18},{18,2},{3,19},{19,3},{4,20},{20... | collective-permute-start | bytes 2359304 | tf_op jit(solution)/shard_map/ppermute | solution.py:953
  458.0 23.9 %collective-permute-start.31 = (bf16[384,384]{1,0:T(8,128)(2,1)S(1)}, bf16[384,384]{1,0:T(8,128)(2,1)S(1)}, u32[]{:S(2)}, u32[]{:S(2)}) collective-permute-start(bf16[384,384]{1,0:T(8,128)(2,1)S(1)} %get-tuple-element.228), channel_id=1, source_target_pairs={{0,4},{4,0},{8,12},{12,8},{1,5},{5,1},{9,13},{13,9},{2,6},{6,2},{1... | collective-permute-start | bytes 884744 | tf_op jit(solution)/shard_map/ppermute | solution.py:962
  473.9 42.5 %collective-permute-start.38 = (bf16[192,1280]{1,0:T(8,128)(2,1)S(1)}, bf16[192,1280]{1,0:T(8,128)(2,1)S(1)}, u32[]{:S(2)}, u32[]{:S(2)}) collective-permute-start(bf16[192,1280]{1,0:T(8,128)(2,1)S(1)} %copy-done.92), channel_id=1, source_target_pairs={{0,8},{4,12},{8,0},{12,4},{1,9},{5,13},{9,1},{13,5},{2,10},{6,14},... | collective-permute-start | bytes 1474568 | tf_op jit(solution)/shard_map/ppermute | solution.py:967
  487.1 17.4 %collective-permute-start.33 = (bf16[384,512]{1,0:T(8,128)(2,1)S(1)}, bf16[384,512]{1,0:T(8,128)(2,1)S(1)}, u32[]{:S(2)}, u32[]{:S(2)}) collective-permute-start(bf16[384,512]{1,0:T(8,128)(2,1)S(1)} %get-tuple-element.235), channel_id=1, source_target_pairs={{0,4},{4,0},{8,12},{12,8},{1,5},{5,1},{9,13},{13,9},{2,6},{6,2},{1... | collective-permute-start | bytes 1179656 | tf_op jit(solution)/shard_map/ppermute | solution.py:962
  490.8 34.6 %collective-permute-start.39 = (bf16[192,1024]{1,0:T(8,128)(2,1)S(1)}, bf16[192,1024]{1,0:T(8,128)(2,1)S(1)}, u32[]{:S(2)}, u32[]{:S(2)}) collective-permute-start(bf16[192,1024]{1,0:T(8,128)(2,1)S(1)} %get-tuple-element.240), channel_id=1, source_target_pairs={{0,8},{4,12},{8,0},{12,4},{1,9},{5,13},{9,1},{13,5},{2,10},{6,14},... | collective-permute-start | bytes 1179656 | tf_op jit(solution)/shard_map/ppermute | solution.py:967
  490.8 63.5 %collective-permute-start.40 = (bf16[192,1280]{1,0:T(8,128)(2,1)S(1)}, bf16[192,1280]{1,0:T(8,128)(2,1)S(1)}, u32[]{:S(2)}, u32[]{:S(2)}) collective-permute-start(bf16[192,1280]{1,0:T(8,128)(2,1)S(1)} %get-tuple-element.241), channel_id=1, source_target_pairs={{0,8},{4,12},{8,0},{12,4},{1,9},{5,13},{9,1},{13,5},{2,10},{6,14},... | collective-permute-start | bytes 1474568 | tf_op jit(solution)/shard_map/ppermute | solution.py:967
  509.6 44.0 %collective-permute-start.42 = (bf16[384,1024]{1,0:T(8,128)(2,1)S(1)}, bf16[384,1024]{1,0:T(8,128)(2,1)S(1)}, u32[]{:S(2)}, u32[]{:S(2)}) collective-permute-start(bf16[384,1024]{1,0:T(8,128)(2,1)S(1)} %get-tuple-element.245), channel_id=1, source_target_pairs={{0,4},{4,0},{8,12},{12,8},{1,5},{5,1},{9,13},{13,9},{2,6},{6,2},{1... | collective-permute-start | bytes 2359304 | tf_op jit(solution)/shard_map/ppermute | solution.py:962
  526.6 52.5 %collective-permute-start.46 = (bf16[192,384]{1,0:T(8,128)(2,1)}, bf16[192,384]{1,0:T(8,128)(2,1)}, u32[]{:S(2)}, u32[]{:S(2)}) collective-permute-start(bf16[192,384]{1,0:T(8,128)(2,1)} %get-tuple-element.248), channel_id=1, source_target_pairs={{0,8},{4,12},{8,0},{12,4},{1,9},{5,13},{9,1},{13,5},{2,10},{6,14},... | collective-permute-start | bytes 442376 | tf_op jit(solution)/shard_map/ppermute | solution.py:967
  526.7 28.8 %collective-permute-start.34 = (bf16[192,512]{1,0:T(8,128)(2,1)S(1)}, bf16[192,512]{1,0:T(8,128)(2,1)S(1)}, u32[]{:S(2)}, u32[]{:S(2)}) collective-permute-start(bf16[192,512]{1,0:T(8,128)(2,1)S(1)} %get-tuple-element.237), channel_id=1, source_target_pairs={{0,8},{4,12},{8,0},{12,4},{1,9},{5,13},{9,1},{13,5},{2,10},{6,14},... | collective-permute-start | bytes 589832 | tf_op jit(solution)/shard_map/ppermute | solution.py:967
  554.2 18.1 %collective-permute-start.43 = (bf16[192,1024]{1,0:T(8,128)(2,1)S(1)}, bf16[192,1024]{1,0:T(8,128)(2,1)S(1)}, u32[]{:S(2)}, u32[]{:S(2)}) collective-permute-start(bf16[192,1024]{1,0:T(8,128)(2,1)S(1)} %get-tuple-element.247), channel_id=1, source_target_pairs={{0,8},{4,12},{8,0},{12,4},{1,9},{5,13},{9,1},{13,5},{2,10},{6,14},... | collective-permute-start | bytes 1179656 | tf_op jit(solution)/shard_map/ppermute | solution.py:967
  574.9 2.6 collective-permute-start.44
  577.5 7.5 %collective-permute-start.45 = (f32[2,200,128]{2,1,0:T(8,128)S(1)}, f32[2,200,128]{2,1,0:T(8,128)S(1)}, u32[]{:S(2)}, u32[]{:S(2)}) collective-permute-start(f32[2,200,128]{2,1,0:T(8,128)S(1)} %maximum_select_fusion.1), channel_id=1, source_target_pairs={{0,2},{1,3},{2,0},{3,1},{4,6},{5,7},{6,4},{7,5},{8,10},{9,11},{10,... | collective-permute-start | bytes 614408 | tf_op jit(solution)/shard_map/ppermute | solution.py:51
  (128 other events, 1322.5 us)

commit v3 on v2

--- a/solution.py
+++ b/solution.py
@@ -19,6 +19,7 @@
 MIB = 1 << 20
 LIGHT = 1000
 TILE = 256
+PIECES = 2
 SCALE = 1.0 / math.sqrt(HD)
 
 
@@ -51,6 +52,14 @@
     return lax.ppermute(value, "tensor", flipped("tensor", 1))
 
 
+def core_swaps(values):
+    return [core_swap(value) for value in values]
+
+
+def chip_swaps(values):
+    return [chip_swap(value) for value in values]
+
+
 def shifted(value, hops):
     count = lax.axis_size("seq")
     route = [(i, i + hops) for i in range(count) if 0 <= i + hops < count]
@@ -64,9 +73,14 @@
 class Order:
     def __init__(self):
         self.mark = None
+        self.touched = []
+
+    def arrived(self, *values):
+        self.touched.extend(values)
 
     def __call__(self, kernel, args, in_specs, out_specs, out_shape, grid, flops, read, name, scalars=(), scratch=()):
-        anchor = [] if self.mark is None else [self.mark]
+        anchor = ([] if self.mark is None else [self.mark]) + self.touched
+        self.touched = []
         count = len(scalars) + len(args)
         outs = len(out_shape)
 
@@ -265,7 +279,7 @@
 def attend_back_kernel(
     heads, blocks, pieces, low_ref, core_ref, q_ref, start_ref, g_ref, o_ref, lse_ref, cos_ref, sin_ref, *refs
 ):
-    gq_ref, both_ref, acc, gk, gv, span = refs[2 * pieces :]
+    gq_ref, keep_ref, *sends, acc, gk, gv, span = refs[2 * pieces :]
     row = pl.program_id(0)
     wide = heads * Q_BLOCK
     reach = (pieces - 1) * q_ref.shape[1]
@@ -305,8 +319,15 @@
             gq_ref[0, here, h * HD : (h + 1) * HD] = to_bf(
                 part * cosine + pltpu.roll(part * sine, HD // 2, 1)
             )
-    both_ref[core, 0] = to_bf(gk[...] * SCALE)
-    both_ref[1 - core, 0] = to_bf(gv[...])
+    is_key = core == 0
+    keys, values = gk[...] * SCALE, gv[...]
+    keep_ref[0] = to_bf(jnp.where(is_key, keys, values))
+    sent = to_bf(jnp.where(is_key, values, keys))
+    for i, ref in enumerate(sends):
+
+        @pl.when(row == i)
+        def _(ref=ref):
+            ref[0] = sent
 
 
 def attend_back(order, low, core, q, start, span, mate, grad, out, lse, cosine, sine):
@@ -334,11 +355,13 @@
             table,
         ]
         + span_specs(rows, local, pieces),
-        [tokens, pl.BlockSpec((2, 1, window, HD), lambda i, *refs: (0, i, 0, 0))],
+        [tokens, pl.BlockSpec((1, window, HD), at)]
+        + [pl.BlockSpec((1, window, HD), lambda i, *refs: (0, 0, 0))] * rows,
         [
             jax.ShapeDtypeStruct((rows, local, columns), jnp.bfloat16),
-            jax.ShapeDtypeStruct((2, rows, window, HD), jnp.bfloat16),
-        ],
+            jax.ShapeDtypeStruct((rows, window, HD), jnp.bfloat16),
+        ]
+        + [jax.ShapeDtypeStruct((1, window, HD), jnp.bfloat16)] * rows,
         (rows,),
         20_000_000_000,
         6 * MIB,
@@ -353,26 +376,28 @@
     )
 
 
-def fold_kernel(both_ref, come_ref, own_ref, *send_refs):
+def fold_kernel(rows, keep_ref, *refs):
+    comes, own_ref, send_refs = refs[:rows], refs[rows], refs[rows + 1 :]
     local = own_ref.shape[1]
-    total = to_f(both_ref[0, 0]) + to_f(come_ref[0])
+    come = comes[0][0]
+    for i in range(1, rows):
+        come = jnp.where(pl.program_id(0) == i, comes[i][0], come)
+    total = to_f(keep_ref[0]) + to_f(come)
     reach = total.shape[0] - local
     own_ref[0] = total[reach:]
     for hop, ref in enumerate(send_refs, 1):
         ref[0] = to_bf(total[reach - hop * local : reach - (hop - 1) * local])
 
 
-def fold(order, both, come, local):
-    rows, window = both.shape[1:3]
+def fold(order, keep, comes, local):
+    rows, window = keep.shape[:2]
     hops = window // local - 1
     out = pl.BlockSpec((1, local, HD), lambda i: (i, 0, 0))
     return order(
-        fold_kernel,
-        [both, come],
-        [
-            pl.BlockSpec((1, 1, window, HD), lambda i: (0, i, 0, 0)),
-            pl.BlockSpec((1, window, HD), lambda i: (lax.rem(i + rows // 2, rows), 0, 0)),
-        ],
+        functools.partial(fold_kernel, rows),
+        [keep, *comes],
+        [pl.BlockSpec((1, window, HD), lambda i: (i, 0, 0))]
+        + [pl.BlockSpec((1, window, HD), lambda i: (0, 0, 0))] * rows,
         [out] * (hops + 1),
         [jax.ShapeDtypeStruct((rows, local, HD), jnp.float32)]
         + [jax.ShapeDtypeStruct((rows, local, HD), jnp.bfloat16)] * hops,
@@ -381,6 +406,45 @@
         4 * MIB,
         "fold",
     )
+
+
+def carry_kernel(piece_ref, come_ref, out_ref):
+    out_ref[...] = to_bf(to_f(piece_ref[...]) + to_f(come_ref[...]))
+
+
+def carry(order, piece, come):
+    rows, local, columns = piece.shape
+    at = pl.BlockSpec((1, local, columns), lambda i: (i, 0, 0))
+    return order(
+        carry_kernel,
+        [piece, come],
+        [at, at],
+        [at],
+        [jax.ShapeDtypeStruct(piece.shape, jnp.bfloat16)],
+        (rows,),
+        0,
+        2 * MIB,
+        "carry",
+    )[0]
+
+
+def bias_kernel(left_ref, right_ref, out_ref):
+    out_ref[...] = left_ref[...] + right_ref[...]
+
+
+def bias_add(order, left, right):
+    whole = pl.BlockSpec(left.shape, lambda i: (0, 0))
+    return order(
+        bias_kernel,
+        [left, right],
+        [whole, whole],
+        [whole],
+        [jax.ShapeDtypeStruct(left.shape, jnp.float32)],
+        (1,),
+        0,
+        MIB,
+        "bias",
+    )[0]
 
 
 def join_kernel(hops, core_ref, gq_ref, cos_ref, sin_ref, own_ref, *refs):
@@ -434,14 +498,15 @@
     )
 
 
-def mixed_back_kernel(near_ref, far_ref, w_ref, out_ref):
-    half = near_ref.shape[0]
-    out_ref[:half] = to_bf(dot(near_ref[...], w_ref[...]))
-    out_ref[half:] = to_bf(dot(far_ref[...], w_ref[...]))
-
-
-def mixed_back(order, near, far, weight):
-    half, width = near.shape
+def mixed_back_kernel(w_ref, *refs):
+    rows = refs[0].shape[0]
+    for i, ref in enumerate(refs[:-1]):
+        refs[-1][i * rows : (i + 1) * rows] = to_bf(dot(ref[...], w_ref[...]))
+
+
+def mixed_back(order, pieces, weight):
+    rows, width = pieces[0].shape
+    total = rows * len(pieces)
     columns = weight.shape[1]
 
     def whole(i):
@@ -449,48 +514,37 @@
 
     return order(
         mixed_back_kernel,
-        [near, far, weight],
-        [
-            pl.BlockSpec((half, width), whole),
-            pl.BlockSpec((half, width), whole),
-            pl.BlockSpec((width, columns), whole),
-        ],
-        [pl.BlockSpec((2 * half, columns), whole)],
-        [jax.ShapeDtypeStruct((2 * half, columns), jnp.bfloat16)],
+        [weight, *pieces],
+        [pl.BlockSpec((width, columns), whole)] + [pl.BlockSpec((rows, width), whole)] * len(pieces),
+        [pl.BlockSpec((total, columns), whole)],
+        [jax.ShapeDtypeStruct((total, columns), jnp.bfloat16)],
         (1,),
-        4 * half * width * columns,
+        2 * total * width * columns,
         6 * MIB,
         "mixed_back",
     )[0]
 
 
-def place_kernel(core_ref, near_ref, far_ref, out_ref):
-    near = pl.program_id(0) < 2
-
-    @pl.when(near)
-    def _():
-        out_ref[...] = near_ref[...]
-
-    @pl.when(jnp.logical_not(near))
-    def _():
-        out_ref[...] = far_ref[...]
-
-
-def place(order, core, near, far):
-    half, width = near.shape
-    block = half // 2
+def place_kernel(core_ref, *refs):
+    for i, ref in enumerate(refs[:-1]):
+
+        @pl.when(pl.program_id(0) == i)
+        def _(ref=ref):
+            refs[-1][...] = ref[...]
+
+
+def place(order, core, pieces):
+    rows, width = pieces[0].shape
+    count = len(pieces)
     return order(
         place_kernel,
-        [near, far],
-        [
-            pl.BlockSpec((block, width), lambda i, core_ref: (jnp.minimum(i, 1), 0)),
-            pl.BlockSpec((block, width), lambda i, core_ref: (jnp.maximum(i - 2, 0), 0)),
-        ],
-        [pl.BlockSpec((block, width), lambda i, core_ref: (lax.rem(i + core_ref[0] * 2, 4), 0))],
-        [jax.ShapeDtypeStruct((2 * half, width), near.dtype)],
-        (4,),
+        list(pieces),
+        [pl.BlockSpec((rows, width), lambda i, core_ref: (0, 0))] * count,
+        [pl.BlockSpec((rows, width), lambda i, core_ref: (lax.rem(i + core_ref[0] * (count // 2), count), 0))],
+        [jax.ShapeDtypeStruct((rows * count, width), pieces[0].dtype)],
+        (count,),
         0,
-        8 * half * width,
+        8 * rows * width,
         "place",
         scalars=(core,),
     )[0]
@@ -527,10 +581,11 @@
     )[0]
 
 
-def gated_kernel(h_ref, far_ref, gh_ref, gw_ref, uw_ref, hid_ref, gg_ref, gu_ref):
-    half = h_ref.shape[0]
-    for part, ref in enumerate((h_ref, far_ref)):
-        here = slice(part * half, (part + 1) * half)
+def gated_kernel(gh_ref, gw_ref, uw_ref, *refs):
+    hid_ref, gg_ref, gu_ref = refs[-3:]
+    rows = refs[0].shape[0]
+    for part, ref in enumerate(refs[:-3]):
+        here = slice(part * rows, (part + 1) * rows)
         h = ref[...]
         gate = dot(h, gw_ref[...], 1, 1)
         up = dot(h, uw_ref[...], 1, 1)
@@ -542,18 +597,17 @@
         gg_ref[here] = to_bf(grad * up * sigma * (1.0 + gate * (1.0 - sigma)))
 
 
-def gated(order, near, far, grad_hidden, gate_weight, up_weight):
-    half, width = near.shape
-    total = 2 * half
+def gated(order, pieces, grad_hidden, gate_weight, up_weight):
+    rows, width = pieces[0].shape
+    total = rows * len(pieces)
     hidden = gate_weight.shape[0]
     column = pl.BlockSpec((total, TILE), lambda i: (0, i))
     weight = pl.BlockSpec((TILE, width), lambda i: (i, 0))
-    whole = pl.BlockSpec((half, width), lambda i: (0, 0))
     shape = jax.ShapeDtypeStruct((total, hidden), jnp.bfloat16)
     return order(
         gated_kernel,
-        [near, far, grad_hidden, gate_weight, up_weight],
-        [whole, whole, column, weight, weight],
+        [grad_hidden, gate_weight, up_weight, *pieces],
+        [column, weight, weight] + [pl.BlockSpec((rows, width), lambda i: (0, 0))] * len(pieces),
         [column] * 3,
         [shape] * 3,
         (pl.cdiv(hidden, TILE),),
@@ -661,62 +715,85 @@
     )[0]
 
 
-def narrow_kernel(pairs, extra, right_dim, *refs):
+def narrow_kernel(pairs, extras, right_dim, *refs):
     out = dot(refs[0][...], refs[1][...], 1, right_dim)
     for i in range(1, pairs):
         out = out + dot(refs[2 * i][...], refs[2 * i + 1][...], 1, right_dim)
-    if extra:
-        out = out + to_f(refs[2 * pairs][...])
-    refs[-1][...] = to_bf(out)
-
-
-def narrow(order, pairs, index, extra=None, right_dim=0):
+    extra = refs[2 * pairs : 2 * pairs + extras]
+    outs = refs[2 * pairs + extras :]
+    if extras:
+        out = out + jnp.concatenate([to_f(ref[...]) for ref in extra], axis=0)
+    rows = outs[0].shape[0]
+    for i, ref in enumerate(outs):
+        ref[...] = to_bf(out[i * rows : (i + 1) * rows])
+
+
+def narrow(order, pairs, index, extra=(), right_dim=0):
     total, hidden = pairs[0][0].shape
     width = pairs[0][1].shape[1 - right_dim]
     half = total // 2
-    column = pl.BlockSpec((half, TILE), lambda i: (0, i))
-    extras = [] if extra is None else [extra]
+    piece = half // PIECES
+    column = pl.BlockSpec((piece, TILE), lambda i: (0, i))
     right = (
         pl.BlockSpec((TILE, hidden), lambda i: (i, 0))
         if right_dim
         else pl.BlockSpec((hidden, TILE), lambda i: (0, i))
     )
     return order(
-        functools.partial(narrow_kernel, len(pairs), len(extras), right_dim),
-        [item for pair in pairs for item in pair] + extras,
-        [pl.BlockSpec((half, hidden), lambda i: (index, 0)), right] * len(pairs) + [column] * len(extras),
-        [column],
-        [jax.ShapeDtypeStruct((half, width), jnp.bfloat16)],
+        functools.partial(narrow_kernel, len(pairs), len(extra), right_dim),
+        [item for pair in pairs for item in pair] + list(extra),
+        [pl.BlockSpec((half, hidden), lambda i: (index, 0)), right] * len(pairs) + [column] * len(extra),
+        [column] * PIECES,
+        [jax.ShapeDtypeStruct((piece, width), jnp.bfloat16)] * PIECES,
         (width // TILE,),
         2 * len(pairs) * half * width * hidden,
         2 * len(pairs) * (half + width) * hidden + 2 * half * width,
         "narrow",
-    )[0]
-
-
-def turn_kernel(near_ref, far_ref, out_ref):
-    half = near_ref.shape[0]
-    out_ref[:, :half] = near_ref[...].T
-    out_ref[:, half:] = far_ref[...].T
-
-
-def turn(order, near, far=None):
-    half, width = near.shape
-    far_index = 0
-    if far is None:
-        half, far, far_index = half // 2, near, 1
+    )
+
+
+def piece_specs(piece, width, block):
+    steps = piece // block
+    return [
+        pl.BlockSpec((block, width), lambda i, *refs, j=j: (jnp.clip(i - j * steps, 0, steps - 1), 0))
+        for j in range(PIECES)
+    ]
+
+
+def pick_piece(refs):
+    value = refs[0][...]
+    for j, ref in enumerate(refs[1:], 1):
+        value = jnp.where(pl.program_id(0) >= 4 * j // len(refs), ref[...], value)
+    return value
+
+
+def put_piece(refs, value):
+    steps = 4 // len(refs)
+    for j, ref in enumerate(refs):
+
+        @pl.when(lax.div(pl.program_id(0), steps) == j)
+        def _(ref=ref):
+            ref[...] = value
+
+
+def turn_kernel(*refs):
+    rows = refs[0].shape[0]
+    for i, ref in enumerate(refs[:-1]):
+        refs[-1][:, i * rows : (i + 1) * rows] = ref[...].T
+
+
+def turn(order, pieces):
+    rows, width = pieces[0].shape
+    total = rows * len(pieces)
     return order(
         turn_kernel,
-        [near, far],
-        [
-            pl.BlockSpec((half, TILE), lambda i: (0, i)),
-            pl.BlockSpec((half, TILE), lambda i: (far_index, i)),
-        ],
-        [pl.BlockSpec((TILE, 2 * half), lambda i: (i, 0))],
-        [jax.ShapeDtypeStruct((width, 2 * half), jnp.bfloat16)],
+        list(pieces),
+        [pl.BlockSpec((rows, TILE), lambda i: (0, i))] * len(pieces),
+        [pl.BlockSpec((TILE, total), lambda i: (i, 0))],
+        [jax.ShapeDtypeStruct((width, total), jnp.bfloat16)],
         (width // TILE,),
         0,
-        8 * half * width,
+        4 * total * width,
         "turn",
     )[0]
 
@@ -753,62 +830,74 @@
     )
 
 
-def middle_kernel(core_ref, tok_ref, mine_ref, come_ref, gain_ref, mid_ref, h_ref):
-    middle = to_f(tok_ref[...]) + (to_f(mine_ref[...]) + to_f(come_ref[...]))
+def middle_kernel(core_ref, tok_ref, gain_ref, *refs):
+    mine, come = pick_piece(refs[:PIECES]), pick_piece(refs[PIECES : 2 * PIECES])
+    mid_ref, *h_refs = refs[2 * PIECES :]
+    middle = to_f(tok_ref[...]) + (to_f(mine) + to_f(come))
     factor = lax.rsqrt(jnp.mean(middle * middle, axis=-1, keepdims=True) + EPS)
     mid_ref[...] = middle
-    h_ref[...] = to_bf(middle * factor * gain_ref[...])
+    put_piece(h_refs, to_bf(middle * factor * gain_ref[...]))
 
 
 def middle_of(order, core, tokens, mine, come, gain):
-    half, width = mine.shape
+    piece, width = mine[0].shape
+    half = piece * PIECES
     block = half // 4
-    at = pl.BlockSpec((block, width), lambda i, core_ref: (i, 0))
-    return order(
+    specs = piece_specs(piece, width, block)
+    middle, *h = order(
         middle_kernel,
-        [tokens, mine, come, gain],
+        [tokens, gain, *mine, *come],
         [
             pl.BlockSpec((block, width), lambda i, core_ref: (core_ref[0] * 4 + i, 0)),
-            at,
-            at,
             pl.BlockSpec((1, width), lambda i, core_ref: (0, 0)),
-        ],
-        [at, at],
-        [jax.ShapeDtypeStruct((half, width), jnp.float32), jax.ShapeDtypeStruct((half, width), jnp.bfloat16)],
+        ]
+        + specs * 2,
+        [pl.BlockSpec((block, width), lambda i, core_ref: (i, 0))] + specs,
+        [jax.ShapeDtypeStruct((half, width), jnp.float32)]
+        + [jax.ShapeDtypeStruct((piece, width), jnp.bfloat16)] * PIECES,
         (4,),
         0,
         9 * MIB,
         "middle",
         scalars=(core,),
     )
-
-
-def norm_back_kernel(core_ref, mine_ref, come_ref, x_ref, gain_ref, up_ref, *refs):
-    grad = to_f(mine_ref[...]) + to_f(come_ref[...])
+    return middle, h
+
+
+def norm_back_kernel(core_ref, x_ref, gain_ref, up_ref, *refs):
+    mine, come = pick_piece(refs[:PIECES]), pick_piece(refs[PIECES : 2 * PIECES])
+    outs = refs[2 * PIECES :]
+    grad = to_f(mine) + to_f(come)
     x = to_f(x_ref[...])
     factor = lax.rsqrt(jnp.mean(x * x, axis=-1, keepdims=True) + EPS)
     normed = x * factor
     weighted = grad * gain_ref[...]
     inner = jnp.mean(weighted * normed, axis=-1, keepdims=True)
     out = to_f(up_ref[...]) + factor * (weighted - normed * inner)
-    refs[0][...] = out
-    if len(refs) > 1:
-        refs[1][...] = to_bf(out)
+    if len(outs) > PIECES:
+        outs[0][...] = out
+        put_piece(outs[1:], to_bf(out))
+    else:
+        put_piece(outs, out)
 
 
 def norm_back(order, core, mine, come, x, gain, up, by_core):
-    half, width = mine.shape
+    piece, width = mine[0].shape
+    half = piece * PIECES
     block = half // 4
     at = pl.BlockSpec((block, width), lambda i, core_ref: (i, 0))
     picked = pl.BlockSpec((block, width), lambda i, core_ref: (core_ref[0] * 4 + i, 0))
-    shapes = [jax.ShapeDtypeStruct((half, width), jnp.float32)]
-    if not by_core:
-        shapes.append(jax.ShapeDtypeStruct((half, width), jnp.bfloat16))
+    specs = piece_specs(piece, width, block)
+    if by_core:
+        shapes = [jax.ShapeDtypeStruct((piece, width), jnp.float32)] * PIECES
+    else:
+        shapes = [jax.ShapeDtypeStruct((half, width), jnp.float32)]
+        shapes += [jax.ShapeDtypeStruct((piece, width), jnp.bfloat16)] * PIECES
     return order(
         norm_back_kernel,
-        [mine, come, x, gain, up],
-        [at, at, picked if by_core else at, pl.BlockSpec((1, width), lambda i, core_ref: (0, 0)), at],
-        [at] * len(shapes),
+        [x, gain, up, *mine, *come],
+        [picked if by_core else at, pl.BlockSpec((1, width), lambda i, core_ref: (0, 0)), at] + specs * 2,
+        specs if by_core else [at] + specs,
         shapes,
         (4,),
         0,
@@ -818,24 +907,26 @@
     )
 
 
-def layer_kernel(middle_ref, mine_ref, come_ref, out_ref):
-    out_ref[...] = to_bf(middle_ref[...] + (to_f(mine_ref[...]) + to_f(come_ref[...])))
+def layer_kernel(middle_ref, *refs):
+    mine, come = pick_piece(refs[:PIECES]), pick_piece(refs[PIECES : 2 * PIECES])
+    put_piece(refs[2 * PIECES :], to_bf(middle_ref[...] + (to_f(mine) + to_f(come))))
 
 
 def layer_of(order, middle, mine, come):
-    half, width = mine.shape
-    at = pl.BlockSpec((half // 4, width), lambda i: (i, 0))
+    piece, width = mine[0].shape
+    block = piece * PIECES // 4
+    specs = piece_specs(piece, width, block)
     return order(
         layer_kernel,
-        [middle, mine, come],
-        [at] * 3,
-        [at],
-        [jax.ShapeDtypeStruct((half, width), jnp.bfloat16)],
+        [middle, *mine, *come],
+        [pl.BlockSpec((block, width), lambda i: (i, 0))] + specs * 2,
+        specs,
+        [jax.ShapeDtypeStruct((piece, width), jnp.bfloat16)] * PIECES,
         (4,),
         0,
         5 * MIB,
         "layer",
-    )[0]
+    )
 
 
 def tensor_gather(value, rank):
@@ -939,6 +1030,7 @@
     units = gate_t.shape[0]
     tiles = -(-units // TILE)
     cut = (tiles + 1) // 2
+    long = cut
     one, two = seq_index ^ 1, seq_index ^ 2
     three = seq_index ^ 3
     quad = jnp.stack([one, three, seq_index, two])
@@ -966,6 +1058,10 @@
                 sent = relay(order, self.keep, self.come, share)
                 self.last = lax.ppermute(sent, "seq", flipped("seq", 1))
 
+        def settled(self):
+            if near_pair:
+                order.arrived(self.last)
+
         def result(self):
             if near_pair:
                 return to_f(self.keep[:share]) + to_f(self.come[:share]) + to_f(self.last)
@@ -986,78 +1082,96 @@
                 self.mine = settle(order, self.keep, self.come, self.last, dp_index)
                 self.final = lax.ppermute(sent, "dp", flipped("dp", 0))
 
+        def placed(self):
+            if near_pair:
+                order.arrived(self.final)
+
         def result(self):
             return to_f(self.mine) + to_f(self.final) if near_pair else super().result()
 
-    sent = narrow(order, [(mixed, o_weight)], 1, None, 1)
-    mine = narrow(order, [(mixed, o_weight)], 0, core_swap(sent), 1)
-    come = chip_swap(mine)
+    sent = core_swaps(narrow(order, [(mixed, o_weight)], 1, (), 1))
+    mine = narrow(order, [(mixed, o_weight)], 0, sent, 1)
+    come = chip_swaps(mine)
     grad_ffn, grad_ffn_t = grad_out_of(
         order, core_one, cotangent.reshape(total, width), valid.reshape(total, 1)
     )
     grad_hidden = grad_hidden_of(order, grad_ffn, down_t)
-    h_one_t = turn(order, h_one)
-    middle, h_two_mine = middle_of(order, core_one, flat_tokens, mine, come, gain_two)
-    h_two_mate = core_swap(h_two_mine)
-    hidden, grad_gate, grad_up = gated(order, h_two_mine, h_two_mate, grad_hidden, gate_t, up_t)
+    h_one_t = turn(order, [h_one])
+    middle, h_two = middle_of(order, core_one, flat_tokens, mine, come, gain_two)
+    h_two += core_swaps(h_two)
+    hidden, grad_gate, grad_up = gated(order, h_two, grad_hidden, gate_t, up_t)
 
     down_a = Rows(grad_ffn_t, hidden, (0, cut))
     down_b = SeqFirst(grad_ffn_t, hidden, (cut, tiles - cut))
     pairs = [(grad_gate, gate_t), (grad_up, up_t)]
-    sent = narrow(order, pairs, 1)
-    mine = narrow(order, pairs, 0, core_swap(sent))
-    come = chip_swap(mine)
-    h_two_t = turn(order, h_two_mine, h_two_mate)
-    gate_a = Rows(h_two_t, grad_gate, (0, cut))
-    gate_b = Rows(h_two_t, grad_gate, (cut, tiles - cut))
-    up_a = Rows(h_two_t, grad_up, (0, cut))
-    ffn_sent = narrow(order, [(hidden, down_t)], 1)
+    sent = core_swaps(narrow(order, pairs, 1))
+    mine = narrow(order, pairs, 0, sent)
+    come = chip_swaps(mine)
+    h_two_t = turn(order, h_two)
+    gate_a = Rows(h_two_t, grad_gate, (0, long))
     down_b.relay()
     down_a.own()
-    grad_middle, branch_mine = norm_back(order, core_one, mine, come, middle, gain_two, grad_ffn, False)
-    branch_mate = core_swap(branch_mine)
-    grad_mixed = mixed_back(order, branch_mine, branch_mate, o_weight).reshape(rows, local, heads * HD)
-    grad_q_rows, both = attend_back(
+    grad_middle, *branch = norm_back(order, core_one, mine, come, middle, gain_two, grad_ffn, False)
+    branch += core_swaps(branch)
+    grad_mixed = mixed_back(order, branch, o_weight).reshape(rows, local, heads * HD)
+    gate_b = Rows(h_two_t, grad_gate, (long, tiles - long))
+    grad_q_rows, keep, *sends = attend_back(
         order, low, core_one, q_rows, start, span, mate, grad_mixed, mixed_rows, lse, cosine, sine
     )
-    both_come = core_swap(both[1])
-    ffn_mine = narrow(order, [(hidden, down_t)], 0, core_swap(ffn_sent))
-    ffn_come = chip_swap(ffn_mine)
-    own_kv, *kv_sends = fold(order, both, both_come, local)
-    kv_comes = [shifted(piece, -hop) for hop, piece in enumerate(kv_sends, 1)]
-    branch_t = turn(order, branch_mine, branch_mate)
+    comes = core_swaps([sends[(i + rows // 2) % rows] for i in range(rows)])
+    branch_t = turn(order, branch)
+    own_kv, *pieces = fold(order, keep, comes, local)
+    moving = shifted(pieces[-1], -1) if pieces else None
+    down_b.settled()
+    gate_a.own()
+    for piece in pieces[-2::-1]:
+        moving = shifted(carry(order, piece, moving), -1)
+    down_a.relay()
+    grad_qkv, bias_sum = join(
+        order, core_one, grad_q_rows, own_kv, [] if moving is None else [moving], cosine, sine
+    )
+    up_a = Rows(h_two_t, grad_up, (0, cut))
+    sent = core_swaps(narrow(order, [(grad_qkv, weight)], 1, (), 1))
+    gate_a.relay()
+    gate_b.own()
+    mine = narrow(order, [(grad_qkv, weight)], 0, sent, 1)
+    come = chip_swaps(mine)
+    up_b = Rows(h_two_t, grad_up, (cut, tiles - cut))
+    ffn_sent = core_swaps(narrow(order, [(hidden, down_t)], 1))
+    qkv = Rows(h_one_t, grad_qkv, (0, grad_qkv.shape[1] // TILE))
+    ffn_mine = narrow(order, [(hidden, down_t)], 0, ffn_sent)
+    ffn_come = chip_swaps(ffn_mine)
     out = Rows(branch_t, mixed, (0, heads), HD)
-    down_b.settle() if near_pair else None
-    down_a.relay()
-    gate_a.own()
-    grad_qkv, bias_sum = join(order, core_one, grad_q_rows, own_kv, kv_comes, cosine, sine)
-    sent = narrow(order, [(grad_qkv, weight)], 1, None, 1)
-    mine = narrow(order, [(grad_qkv, weight)], 0, core_swap(sent), 1)
-    come = chip_swap(mine)
-    qkv = Rows(h_one_t, grad_qkv, (0, grad_qkv.shape[1] // TILE))
-    up_b = Rows(h_two_t, grad_up, (cut, tiles - cut))
-    gate_b.own()
-    gate_a.relay()
-    (token_mine,) = norm_back(order, core_one, mine, come, flat_tokens, gain_one, grad_middle, True)
-    token_mate = core_swap(token_mine)
-    layer_mine = layer_of(order, middle, ffn_mine, ffn_come)
-    layer_mate = core_swap(layer_mine)
+    down_a.settled()
+    gate_a.settled()
+    gate_b.relay()
     up_a.own()
-    gate_b.relay()
+    token = norm_back(order, core_one, mine, come, flat_tokens, gain_one, grad_middle, True)
+    token += core_swaps(token)
+    down_b.settle()
+    gate_b.settled()
+    up_b.own()
+    up_a.relay()
+    token_grad = place(order, core_one, token).reshape(rows, local, width)
+    qkv.own()
+    down_b.placed()
+    up_b.relay()
+    up_a.settled()
+    layer = layer_of(order, middle, ffn_mine, ffn_come)
+    layer += core_swaps(layer)
     out.own()
-    token_grad = place(order, core_one, token_mine, token_mate).reshape(rows, local, width)
-    layer_out = place(order, core_one, layer_mine, layer_mate).reshape(rows, local, width)
-    up_a.relay()
+    if near_pair:
+        bias_come = lax.ppermute(bias_sum, "dp", flipped("dp", 0))
+        bias_all = bias_add(order, bias_sum, bias_come)
+        bias_come = lax.ppermute(bias_all, "seq", flipped("seq", 0))
+    qkv.relay()
+    layer_out = place(order, core_one, layer).reshape(rows, local, width)
+    up_b.settled()
     out.relay()
-    qkv.own()
-    qkv.relay()
-    up_b.own()
-    up_b.relay()
     if near_pair:
-        bias_all = bias_sum + lax.ppermute(bias_sum, "dp", flipped("dp", 0))
-        bias_all = bias_all + lax.ppermute(bias_all, "seq", flipped("seq", 0))
-        bias_all = bias_all + lax.ppermute(bias_all, "seq", flipped("seq", 1))
-        bias_all = bias_all[:1]
+        bias_all = bias_add(order, bias_all, bias_come)
+        bias_come = lax.ppermute(bias_all, "seq", flipped("seq", 1))
+        bias_all = (bias_all + bias_come)[:1]
     else:
         bias_all = lax.psum(bias_sum[:1], ("dp", "seq"))
     qkv_grad = qkv.result()

time: 590 us -> 549 us (0.931)
  waiting for transfers between devices: 231 us -> 174 us
  local copies, waits for them, and re-layouts: 68 us -> 83.7 us
    ppermute x7, waiting for transfers between devices: 44.7 us -> 7.54 us  [own(): self.come = lax.ppermute(send, 'seq', flipped('seq', 0))]
    ppermute x7, waiting for transfers between devices: 24 us -> 0.02 us  [__init__(): self.come = lax.ppermute(sent, 'dp', flipped('dp', 0))]
    ppermute x8, waiting for transfers between devices: 50.1 us -> 71.7 us  [relay(): self.last = lax.ppermute(sent, 'seq', flipped('seq', 1))]
    ppermute x3, waiting for transfers between devices: 21.5 us -> 1.78 us  [the longest x1 1.78 us: body(): bias_come = lax.ppermute(bias_all, 'seq', flipped('seq', 1))]
    ppermute x4, waiting for transfers between devices: 14.7 us -> 34.3 us  [shifted(): return lax.ppermute(value, 'seq', route)]
    ppermute x5 -> x9, waiting for transfers between devices: 45.5 us -> 28.8 us  [chip_swap(): return lax.ppermute(value, 'tensor', flipped('tensor', 1))]
    unnamed x259, local copies, waits for them, and re-layouts: 58.9 us -> 74.1 us
    ppermute x7, starting transfers between devices: 16.6 us -> 2.45 us  [own(): self.come = lax.ppermute(send, 'seq', flipped('seq', 0))]
  transfers between devices with their start and end apart: 49 -> 62, of which waited for: 28 -> 27; matrix products, arithmetic and copies ran while one was open for 4% -> 4% of each run, Pallas kernels for 22% -> 28%
where the time goes in v3:
time: 549 us; the launch traced here: 545 us
  Pallas kernels  197 us (36%)
  waiting for transfers between devices  174 us (32%)
  local copies, waits for them, and re-layouts  83.7 us (15%)
  starting transfers between devices  68.5 us (12%)
  other arithmetic  19.1 us (3%)
    pallas_call x52, Pallas kernels, __call__(): pl.pallas_call(run, grid_spec=pltpu.PrefetchScalarGridSpec(num_scalar_pre...  187 us
    unnamed x259, local copies, waits for them, and re-layouts  74.1 us
    ppermute x8, waiting for transfers between devices, relay(): self.last = lax.ppermute(sent, 'seq', flipped('seq', 1))  71.7 us
    ppermute x4, waiting for transfers between devices, shifted(): return lax.ppermute(value, 'seq', route)  34.3 us
    ppermute x9, waiting for transfers between devices, chip_swap(): return lax.ppermute(value, 'tensor', flipped('tensor', 1))  28.8 us
    ppermute x8, starting transfers between devices, relay(): self.last = lax.ppermute(sent, 'seq', flipped('seq', 1))  16.5 us
    ppermute x4, starting transfers between devices, shifted(): return lax.ppermute(value, 'seq', route)  13.9 us
    ppermute x1, waiting for transfers between devices, __init__(): self.come = lax.ppermute(send, 'seq', flipped('seq', 0))  11.4 us
  transfers between devices with their start and end apart: 62, of which 27 were waited for; matrix products, arithmetic and copies ran while one was open for 4% of the time, Pallas kernels for 28%

profile of v3, /device:TPU:0, one launch (start us, length us, event | category | flops | bytes accessed | tf_op | source)
XLA Modules:
  0.0 544.8 jit_solution(15569245653624647035)
XLA Ops:
  12.5 3.8 first.1
  18.9 6.6 %collective-permute-start = (bf16[2,512,128]{2,1,0:T(8,128)(2,1)S(1)}, bf16[2,512,128]{2,1,0:T(8,128)(2,1)}, u32[]{:S(2)}, u32[]{:S(2)}) collective-permute-start(bf16[2,512,128]{2,1,0:T(8,128)(2,1)S(1)} %bitcast.73), channel_id=1, source_target_pairs={{0,8},{4,12},{1,9},{5,13},{2,10},{6,14},{3,11},{7,15},{16,24},{20,... | collective-permute-start | bytes 786440 | tf_op jit(solution)/shard_map/ppermute | solution.py:66
  25.5 4.7 collective-permute-start.1
  31.4 3.9 collective-permute-done.1.refs_1_.refs_10_
  38.3 6.1 %attend.1 = (bf16[2,512,384]{2,1,0:T(8,128)(2,1)S(1)}, f32[2,2,768]{2,1,0:T(2,128)S(1)}) custom-call(s32[2,2]{1,0:T(2,128)S(1)} %shift-right-logical_maximum_fusion.low_ref.refs_0_, s32[1]{0:T(128)} %bitcast.core_ref.refs_0_.refs_1_, bf16[2,512,384]{2,1,0:T(8,128)(2,1)S(1)} %bitcast.70, s32[2,1,512]{2,1,0:T(1,128)S(1)} %sub.48.start_ref.refs_3_, ...), custom_call_target="tpu_custom_call" | custom-call | flops 8000000 | bytes 4194 | tf_op jit(solution)/shard_map/attend/pallas_call | solution.py:253
  50.0 3.4 narrow.9
  63.3 4.1 copy-done.7
  67.4 9.3 %grad_hidden.1 = (bf16[1024,2240]{1,0:T(8,128)(2,1)S(1)}, f32[8,128]{1,0:T(8,128)S(1)}) custom-call(bf16[1024,1536]{1,0:T(8,128)(2,1)S(1)} %get-tuple-element.163.refs_0_.refs_3_, bf16[2240,1536]{1,0:T(8,128)(2,1)S(1)} %bitcast.59, f32[8,128]{1,0:T(8,128)S(1)} %get-tuple-element.164.refs_2_), custom_call_target="tpu_custom_call" | custom-call | flops 7046430 | bytes 15728 | tf_op jit(solution)/shard_map/grad_hidden/pallas_call | solution.py:92
  82.0 8.1 %collective-permute-done.8.refs_6_ = bf16[256,1536]{1,0:T(8,128)(2,1)} collective-permute-done((bf16[256,1536]{1,0:T(8,128)(2,1)}, bf16[256,1536]{1,0:T(8,128)(2,1)}, u32[]{:S(2)}, u32[]{:S(2)}) %collective-permute-start.8) | collective-permute-done | bytes 786464 | tf_op jit(solution)/shard_map/ppermute | solution.py:52
  90.2 4.9 middle.1
  105.9 21.0 %gated.1 = (bf16[1024,2240]{1,0:T(8,128)(2,1)S(1)}, bf16[1024,2240]{1,0:T(8,128)(2,1)S(1)}, bf16[1024,2240]{1,0:T(8,128)(2,1)S(1)}, f32[8,128]{1,0:T(8,128)S(1)}) custom-call(bf16[1024,2240]{1,0:T(8,128)(2,1)S(1)} %copy-done.48, bf16[2240,1536]{1,0:T(8,128)(2,1)} %bitcast.56, bf16[2240,1536]{1,0:T(8,128)(2,1)} %bitcast.79, ...), custom_call_target="tpu_custom_call" | custom-call | flops 14092861 | bytes 31457 | tf_op jit(solution)/shard_map/gated/pallas_call | solution.py:92
  129.1 4.7 share.15
  139.4 5.8 %share.16 = (bf16[768,1024]{1,0:T(8,128)(2,1)}, bf16[768,1024]{1,0:T(8,128)(2,1)S(1)}, f32[8,128]{1,0:T(8,128)S(1)}) custom-call(s32[1]{0:T(128)} %constant.55.clone.1.refs_1_.refs_0_, s32[8]{0:T(128)S(1)} %stack.65.refs_1_, bf16[1536,1024]{1,0:T(8,128)(2,1)S(1)} %copy-done.13, bf16[1024,2240]{1,0:T(8,128)(2,1)S(1)} %copy-done.5, ...), custom_call_target="tpu_custom_call" | custom-call | flops 3221225 | bytes 8388 | tf_op jit(solution)/shard_map/share/pallas_call | solution.py:92
  151.1 10.2 %narrow.10 = (bf16[256,1536]{1,0:T(8,128)(2,1)S(1)}, bf16[256,1536]{1,0:T(8,128)(2,1)S(1)}, f32[8,128]{1,0:T(8,128)S(1)}) custom-call(bf16[1024,2240]{1,0:T(8,128)(2,1)S(1)} %copy-done.3, bf16[2240,1536]{1,0:T(8,128)(2,1)S(1)} %bitcast.57, bf16[1024,2240]{1,0:T(8,128)(2,1)S(1)} %copy-done.1, bf16[2240,1536]{1,0:T(8,128)(2,1)} %bitcast.80, ...), custom_call_target="tpu_custom_call" | custom-call | flops 7046430 | bytes 19922 | tf_op jit(solution)/shard_map/narrow/pallas_call | solution.py:92
  161.8 9.6 %collective-permute-start.16 = (bf16[768,1024]{1,0:T(8,128)(2,1)}, bf16[768,1024]{1,0:T(8,128)(2,1)S(1)}, u32[]{:S(2)}, u32[]{:S(2)}) collective-permute-start(bf16[768,1024]{1,0:T(8,128)(2,1)} %get-tuple-element.188), channel_id=1, source_target_pairs={{0,4},{4,0},{8,12},{12,8},{1,5},{5,1},{9,13},{13,9},{2,6},{6,2},{1... | collective-permute-start | bytes 4718600 | tf_op jit(solution)/shard_map/ppermute | solution.py:1075
  171.5 11.1 %narrow.11 = (bf16[256,1536]{1,0:T(8,128)(2,1)}, bf16[256,1536]{1,0:T(8,128)(2,1)}, f32[8,128]{1,0:T(8,128)S(1)}) custom-call(bf16[1024,2240]{1,0:T(8,128)(2,1)S(1)} %copy-done.3, bf16[2240,1536]{1,0:T(8,128)(2,1)S(1)} %bitcast.58, bf16[1024,2240]{1,0:T(8,128)(2,1)S(1)} %copy-done.1, bf16[2240,1536]{1,0:T(8,128)(2,1)} %bitcast.81, ...), custom_call_target="tpu_custom_call" | custom-call | flops 7046430 | bytes 19922 | tf_op jit(solution)/shard_map/narrow/pallas_call | solution.py:92
  184.7 3.8 turn.4
  188.5 4.3 share.17
  194.9 11.4 %collective-permute-done.16.refs_1_.refs_2_ = bf16[768,1024]{1,0:T(8,128)(2,1)S(1)} collective-permute-done((bf16[768,1024]{1,0:T(8,128)(2,1)}, bf16[768,1024]{1,0:T(8,128)(2,1)S(1)}, u32[]{:S(2)}, u32[]{:S(2)}) %collective-permute-start.16) | collective-permute-done | bytes 1572896 | tf_op jit(solution)/shard_map/ppermute | solution.py:1075
  206.6 7.2 %share.18 = (bf16[384,1280]{1,0:T(8,128)(2,1)}, bf16[384,1280]{1,0:T(8,128)(2,1)S(1)}, f32[8,128]{1,0:T(8,128)S(1)}) custom-call(s32[1]{0:T(128)} %bitcast.19.refs_0_, s32[4]{0:T(128)S(1)} %pad_add_fusion.refs_1_, bf16[1536,1024]{1,0:T(8,128)(2,1)S(1)} %copy-done.14, bf16[1024,2240]{1,0:T(8,128)(2,1)S(1)} %bitcast.55, ...), custom_call_target="tpu_custom_call" | custom-call | flops 2013265 | bytes 6160 | tf_op jit(solution)/shard_map/share/pallas_call | solution.py:92
  213.9 5.3 collective-permute-done.14.refs_7_
  221.0 4.2 norm_back.2
  236.9 8.9 %attend_back.1 = (bf16[2,512,384]{2,1,0:T(8,128)(2,1)S(1)}, bf16[2,1536,128]{2,1,0:T(8,128)(2,1)S(1)}, bf16[1,1536,128]{2,1,0:T(8,128)(2,1)S(1)}, bf16[1,1536,128]{2,1,0:T(8,128)(2,1)S(1)}, f32[8,128]{1,0:T(8,128)S(1)}) custom-call(s32[2,2]{1,0:T(2,128)S(1)} %shift-right-logical_maximum_fusion.low_ref.refs_0_, s32[1]{0:T(128)} %bitcast.core_ref.refs_0_.refs_1_, ...), custom_call_target="tpu_custom_call" | custom-call | flops 20000000 | bytes 6291 | tf_op jit(solution)/shard_map/attend_back/pallas_call | solution.py:92
  246.8 9.8 %collective-permute-start.23 = (bf16[384,1024]{1,0:T(8,128)(2,1)S(1)}, bf16[384,1024]{1,0:T(8,128)(2,1)S(1)}, u32[]{:S(2)}, u32[]{:S(2)}) collective-permute-start(bf16[384,1024]{1,0:T(8,128)(2,1)S(1)} %copy-done.96), channel_id=1, source_target_pairs={{0,8},{4,12},{8,0},{12,4},{1,9},{5,13},{9,1},{13,5},{2,10},{6,14},... | collective-permute-start | bytes 2359304 | tf_op jit(solution)/shard_map/ppermute | solution.py:1059
  256.7 5.2 collective-permute-start.28
  265.0 26.3 %collective-permute-done.23.refs_6_.refs_3_ = bf16[384,1024]{1,0:T(8,128)(2,1)S(1)} collective-permute-done((bf16[384,1024]{1,0:T(8,128)(2,1)S(1)}, bf16[384,1024]{1,0:T(8,128)(2,1)S(1)}, u32[]{:S(2)}, u32[]{:S(2)}) %collective-permute-start.23) | collective-permute-done | bytes 786464 | tf_op jit(solution)/shard_map/ppermute | solution.py:1059
  291.3 5.6 %share.20 = (bf16[384,1280]{1,0:T(8,128)(2,1)S(1)}, bf16[384,1280]{1,0:T(8,128)(2,1)S(1)}, f32[8,128]{1,0:T(8,128)S(1)}) custom-call(s32[1]{0:T(128)} %bitcast.19.refs_0_, s32[4]{0:T(128)S(1)} %pad_add_fusion.refs_1_, bf16[1536,1024]{1,0:T(8,128)(2,1)S(1)} %get-tuple-element.183.refs_2_, bf16[1024,2240]{1,0:T(8,128)(2,1)S(1)} %bitcast.53, ...), custom_call_target="tpu_custom_call" | custom-call | flops 2013265 | bytes 6160 | tf_op jit(solution)/shard_map/share/pallas_call | solution.py:92
  297.0 6.8 %collective-permute-done.21.refs_1_ = bf16[2,512,128]{2,1,0:T(8,128)(2,1)S(1)} collective-permute-done((bf16[2,512,128]{2,1,0:T(8,128)(2,1)S(1)}, bf16[2,512,128]{2,1,0:T(8,128)(2,1)S(1)}, u32[]{:S(2)}, u32[]{:S(2)}) %collective-permute-start.21) | collective-permute-done | bytes 262176 | tf_op jit(solution)/shard_map/ppermute | solution.py:66
  307.2 22.5 %collective-permute-done.24.refs_5_ = bf16[2,512,128]{2,1,0:T(8,128)(2,1)S(1)} collective-permute-done((bf16[2,512,128]{2,1,0:T(8,128)(2,1)S(1)}, bf16[2,512,128]{2,1,0:T(8,128)(2,1)S(1)}, u32[]{:S(2)}, u32[]{:S(2)}) %collective-permute-start.24) | collective-permute-done | bytes 262176 | tf_op jit(solution)/shard_map/ppermute | solution.py:66
  330.5 4.2 share.21
  337.4 3.7 collective-permute-start.39
  341.3 4.7 share.22
  346.0 3.6 narrow.13
  355.9 5.3 narrow.14
  362.0 23.5 %collective-permute-done.40.refs_4_ = bf16[192,1280]{1,0:T(8,128)(2,1)S(1)} collective-permute-done((bf16[192,1280]{1,0:T(8,128)(2,1)S(1)}, bf16[192,1280]{1,0:T(8,128)(2,1)S(1)}, u32[]{:S(2)}, u32[]{:S(2)}) %collective-permute-start.40) | collective-permute-done | bytes 491552 | tf_op jit(solution)/shard_map/ppermute | solution.py:1059
  392.8 5.4 narrow.15
  401.4 6.2 %share.26 = (bf16[384,1280]{1,0:T(8,128)(2,1)}, bf16[384,1280]{1,0:T(8,128)(2,1)S(1)}, f32[8,128]{1,0:T(8,128)S(1)}) custom-call(s32[1]{0:T(128)} %bitcast.19.refs_0_, s32[4]{0:T(128)S(1)} %pad_add_fusion.refs_1_, bf16[1536,1024]{1,0:T(8,128)(2,1)S(1)} %get-tuple-element.183.refs_2_, bf16[1024,2240]{1,0:T(8,128)(2,1)S(1)} %copy-done.1, ...), custom_call_target="tpu_custom_call" | custom-call | flops 2013265 | bytes 6160 | tf_op jit(solution)/shard_map/share/pallas_call | solution.py:92
  412.0 10.1 %collective-permute-done.36.refs_7_ = bf16[256,1536]{1,0:T(8,128)(2,1)} collective-permute-done((bf16[256,1536]{1,0:T(8,128)(2,1)}, bf16[256,1536]{1,0:T(8,128)(2,1)}, u32[]{:S(2)}, u32[]{:S(2)}) %collective-permute-start.36) | collective-permute-done | bytes 786464 | tf_op jit(solution)/shard_map/ppermute | solution.py:52
  426.6 5.5 %norm_back.3 = (f32[256,1536]{1,0:T(8,128)}, f32[256,1536]{1,0:T(8,128)}, f32[8,128]{1,0:T(8,128)S(1)}) custom-call(s32[1]{0:T(128)} %bitcast.core_ref.refs_0_.refs_1_, bf16[1024,1536]{1,0:T(8,128)(2,1)S(1)} %bitcast.64, f32[1,1536]{1,0:T(1,128)S(1)} %reshape.206.gain_ref.refs_2_, f32[512,1536]{1,0:T(8,128)S(1)} %copy-done.66, ...), custom_call_target="tpu_custom_call" | custom-call | bytes 10485 | tf_op jit(solution)/shard_map/norm_back/pallas_call | solution.py:92
  432.6 4.5 constant_dynamic-slice_fusion
  455.0 4.8 share.27
  462.3 8.4 %collective-permute-done.47.refs_3_ = bf16[192,1024]{1,0:T(8,128)(2,1)S(1)} collective-permute-done((bf16[192,1024]{1,0:T(8,128)(2,1)S(1)}, bf16[192,1024]{1,0:T(8,128)(2,1)S(1)}, u32[]{:S(2)}, u32[]{:S(2)}) %collective-permute-start.47) | collective-permute-done | bytes 393248 | tf_op jit(solution)/shard_map/ppermute | solution.py:1083
  472.0 6.1 %place.2 = (f32[1024,1536]{1,0:T(8,128)}, f32[8,128]{1,0:T(8,128)S(1)}) custom-call(s32[1]{0:T(128)} %bitcast.core_ref.refs_0_.refs_1_, f32[256,1536]{1,0:T(8,128)} %get-tuple-element.259.refs_1_, f32[256,1536]{1,0:T(8,128)} %get-tuple-element.260.refs_2_, f32[256,1536]{1,0:T(8,128)} %collective-permute-done.44.refs_3_, ...), custom_call_target="tpu_custom_call" | custom-call | bytes 3145 | tf_op jit(solution)/shard_map/place/pallas_call | solution.py:92
  487.4 7.0 %collective-permute-done.48.refs_6_ = bf16[192,1280]{1,0:T(8,128)(2,1)S(1)} collective-permute-done((bf16[192,1280]{1,0:T(8,128)(2,1)S(1)}, bf16[192,1280]{1,0:T(8,128)(2,1)S(1)}, u32[]{:S(2)}, u32[]{:S(2)}) %collective-permute-start.48) | collective-permute-done | bytes 491552 | tf_op jit(solution)/shard_map/ppermute | solution.py:1059
  501.0 4.3 collective-permute-done.51.refs_1_
  505.4 7.9 %collective-permute-done.57.refs_3_ = bf16[192,1024]{1,0:T(8,128)(2,1)S(1)} collective-permute-done((bf16[192,1024]{1,0:T(8,128)(2,1)S(1)}, bf16[192,1024]{1,0:T(8,128)(2,1)S(1)}, u32[]{:S(2)}, u32[]{:S(2)}) %collective-permute-start.57) | collective-permute-done | bytes 393248 | tf_op jit(solution)/shard_map/ppermute | solution.py:1059
  515.7 6.0 %collective-permute-done.54 = bf16[192,512]{1,0:T(8,128)(2,1)S(1)} collective-permute-done((bf16[192,512]{1,0:T(8,128)(2,1)S(1)}, bf16[192,512]{1,0:T(8,128)(2,1)S(1)}, u32[]{:S(2)}, u32[]{:S(2)}) %collective-permute-start.54) | collective-permute-done | bytes 196640 | tf_op jit(solution)/shard_map/ppermute | solution.py:1059
  534.0 5.3 collective-permute-done.60
  (449 shorter events, 177.2 us)
Async XLA Ops:
  18.9 12.5 %collective-permute-start = (bf16[2,512,128]{2,1,0:T(8,128)(2,1)S(1)}, bf16[2,512,128]{2,1,0:T(8,128)(2,1)}, u32[]{:S(2)}, u32[]{:S(2)}) collective-permute-start(bf16[2,512,128]{2,1,0:T(8,128)(2,1)S(1)} %bitcast.73), channel_id=1, source_target_pairs={{0,8},{4,12},{1,9},{5,13},{2,10},{6,14},{3,11},{7,15},{16,24},{20,... | collective-permute-start | bytes 786440 | tf_op jit(solution)/shard_map/ppermute | solution.py:66
  25.5 9.8 %collective-permute-start.1 = (bf16[2,512,128]{2,1,0:T(8,128)(2,1)S(1)}, bf16[2,512,128]{2,1,0:T(8,128)(2,1)}, u32[]{:S(2)}, u32[]{:S(2)}) collective-permute-start(bf16[2,512,128]{2,1,0:T(8,128)(2,1)S(1)} %bitcast.74), channel_id=1, source_target_pairs={{0,4},{4,8},{8,12},{1,5},{5,9},{9,13},{2,6},{6,10},{10,14},{3,7},{... | collective-permute-start | bytes 786440 | tf_op jit(solution)/shard_map/ppermute | solution.py:66
  53.4 28.6 %collective-permute-start.7 = (bf16[256,1536]{1,0:T(8,128)(2,1)}, bf16[256,1536]{1,0:T(8,128)(2,1)}, u32[]{:S(2)}, u32[]{:S(2)}) collective-permute-start(bf16[256,1536]{1,0:T(8,128)(2,1)} %get-tuple-element.159.refs_3_), channel_id=1, source_target_pairs={{0,2},{1,3},{2,0},{3,1},{4,6},{5,7},{6,4},{7,5},{8,10},{9,11},{10,... | collective-permute-start | bytes 2359304 | tf_op jit(solution)/shard_map/ppermute | solution.py:52
  54.9 35.2 %collective-permute-start.8 = (bf16[256,1536]{1,0:T(8,128)(2,1)}, bf16[256,1536]{1,0:T(8,128)(2,1)}, u32[]{:S(2)}, u32[]{:S(2)}) collective-permute-start(bf16[256,1536]{1,0:T(8,128)(2,1)} %get-tuple-element.160.refs_4_), channel_id=1, source_target_pairs={{0,2},{1,3},{2,0},{3,1},{4,6},{5,7},{6,4},{7,5},{8,10},{9,11},{10,... | collective-permute-start | bytes 2359304 | tf_op jit(solution)/shard_map/ppermute | solution.py:52
  136.0 70.6 %collective-permute-start.15 = (bf16[768,1280]{1,0:T(8,128)(2,1)}, bf16[768,1280]{1,0:T(8,128)(2,1)}, u32[]{:S(2)}, u32[]{:S(2)}) collective-permute-start(bf16[768,1280]{1,0:T(8,128)(2,1)} %get-tuple-element.186), channel_id=1, source_target_pairs={{0,16},{16,0},{1,17},{17,1},{2,18},{18,2},{3,19},{19,3},{4,20},{20... | collective-permute-start | bytes 5898248 | tf_op jit(solution)/shard_map/ppermute | solution.py:1045
  161.3 10.2 %collective-permute-start.11 = (bf16[256,1536]{1,0:T(8,128)(2,1)S(1)}, bf16[256,1536]{1,0:T(8,128)(2,1)S(1)}, u32[]{:S(2)}, u32[]{:S(2)}) collective-permute-start(bf16[256,1536]{1,0:T(8,128)(2,1)S(1)} %get-tuple-element.179), channel_id=1, source_target_pairs={{0,1},{1,0},{2,3},{3,2},{4,5},{5,4},{6,7},{7,6},{8,9},{9,8},{10,11... | collective-permute-start | bytes 2359304 | tf_op jit(solution)/shard_map/ppermute | solution.py:48
  161.3 10.1 %collective-permute-start.12 = (bf16[256,1536]{1,0:T(8,128)(2,1)S(1)}, bf16[256,1536]{1,0:T(8,128)(2,1)S(1)}, u32[]{:S(2)}, u32[]{:S(2)}) collective-permute-start(bf16[256,1536]{1,0:T(8,128)(2,1)S(1)} %get-tuple-element.180), channel_id=1, source_target_pairs={{0,1},{1,0},{2,3},{3,2},{4,5},{5,4},{6,7},{7,6},{8,9},{9,8},{10,11... | collective-permute-start | bytes 2359304 | tf_op jit(solution)/shard_map/ppermute | solution.py:48
  161.8 44.5 %collective-permute-start.16 = (bf16[768,1024]{1,0:T(8,128)(2,1)}, bf16[768,1024]{1,0:T(8,128)(2,1)S(1)}, u32[]{:S(2)}, u32[]{:S(2)}) collective-permute-start(bf16[768,1024]{1,0:T(8,128)(2,1)} %get-tuple-element.188), channel_id=1, source_target_pairs={{0,4},{4,0},{8,12},{12,8},{1,5},{5,1},{9,13},{13,9},{2,6},{6,2},{1... | collective-permute-start | bytes 4718600 | tf_op jit(solution)/shard_map/ppermute | solution.py:1075
  182.6 31.2 %collective-permute-start.13 = (bf16[256,1536]{1,0:T(8,128)(2,1)}, bf16[256,1536]{1,0:T(8,128)(2,1)}, u32[]{:S(2)}, u32[]{:S(2)}) collective-permute-start(bf16[256,1536]{1,0:T(8,128)(2,1)} %get-tuple-element.184.refs_4_), channel_id=1, source_target_pairs={{0,2},{1,3},{2,0},{3,1},{4,6},{5,7},{6,4},{7,5},{8,10},{9,11},{10,... | collective-permute-start | bytes 2359304 | tf_op jit(solution)/shard_map/ppermute | solution.py:52
  184.1 35.0 %collective-permute-start.14 = (bf16[256,1536]{1,0:T(8,128)(2,1)}, bf16[256,1536]{1,0:T(8,128)(2,1)}, u32[]{:S(2)}, u32[]{:S(2)}) collective-permute-start(bf16[256,1536]{1,0:T(8,128)(2,1)} %get-tuple-element.185.refs_5_), channel_id=1, source_target_pairs={{0,2},{1,3},{2,0},{3,1},{4,6},{5,7},{6,4},{7,5},{8,10},{9,11},{10,... | collective-permute-start | bytes 2359304 | tf_op jit(solution)/shard_map/ppermute | solution.py:52
  192.8 98.5 %collective-permute-start.22 = (bf16[768,1280]{1,0:T(8,128)(2,1)}, bf16[768,1280]{1,0:T(8,128)(2,1)}, u32[]{:S(2)}, u32[]{:S(2)}) collective-permute-start(bf16[768,1280]{1,0:T(8,128)(2,1)} %get-tuple-element.209), channel_id=1, source_target_pairs={{0,16},{16,0},{1,17},{17,1},{2,18},{18,2},{3,19},{19,3},{4,20},{20... | collective-permute-start | bytes 5898248 | tf_op jit(solution)/shard_map/ppermute | solution.py:1045
  246.7 10.0 %collective-permute-start.19 = (bf16[1,1536,128]{2,1,0:T(8,128)(2,1)S(1)}, bf16[1,1536,128]{2,1,0:T(8,128)(2,1)S(1)}, u32[]{:S(2)}, u32[]{:S(2)}) collective-permute-start(bf16[1,1536,128]{2,1,0:T(8,128)(2,1)S(1)} %get-tuple-element.202), channel_id=1, source_target_pairs={{0,1},{1,0},{2,3},{3,2},{4,5},{5,4},{6,7},{7,6},{8,9},{9,8},{10,11... | collective-permute-start | bytes 1179656 | tf_op jit(solution)/shard_map/ppermute | solution.py:48
  246.8 44.5 %collective-permute-start.23 = (bf16[384,1024]{1,0:T(8,128)(2,1)S(1)}, bf16[384,1024]{1,0:T(8,128)(2,1)S(1)}, u32[]{:S(2)}, u32[]{:S(2)}) collective-permute-start(bf16[384,1024]{1,0:T(8,128)(2,1)S(1)} %copy-done.96), channel_id=1, source_target_pairs={{0,8},{4,12},{8,0},{12,4},{1,9},{5,13},{9,1},{13,5},{2,10},{6,14},... | collective-permute-start | bytes 2359304 | tf_op jit(solution)/shard_map/ppermute | solution.py:1059
  256.6 48.6 %collective-permute-start.25 = (bf16[384,1280]{1,0:T(8,128)(2,1)}, bf16[384,1280]{1,0:T(8,128)(2,1)}, u32[]{:S(2)}, u32[]{:S(2)}) collective-permute-start(bf16[384,1280]{1,0:T(8,128)(2,1)} %get-tuple-element.215), channel_id=1, source_target_pairs={{0,4},{4,0},{8,12},{12,8},{1,5},{5,1},{9,13},{13,9},{2,6},{6,2},{1... | collective-permute-start | bytes 2949128 | tf_op jit(solution)/shard_map/ppermute | solution.py:1054
  256.7 84.6 %collective-permute-start.28 = (bf16[768,1024]{1,0:T(8,128)(2,1)}, bf16[768,1024]{1,0:T(8,128)(2,1)}, u32[]{:S(2)}, u32[]{:S(2)}) collective-permute-start(bf16[768,1024]{1,0:T(8,128)(2,1)} %get-tuple-element.223), channel_id=1, source_target_pairs={{0,16},{16,0},{1,17},{17,1},{2,18},{18,2},{3,19},{19,3},{4,20},{20... | collective-permute-start | bytes 4718600 | tf_op jit(solution)/shard_map/ppermute | solution.py:1045
  263.7 40.1 %collective-permute-start.21 = (bf16[2,512,128]{2,1,0:T(8,128)(2,1)S(1)}, bf16[2,512,128]{2,1,0:T(8,128)(2,1)S(1)}, u32[]{:S(2)}, u32[]{:S(2)}) collective-permute-start(bf16[2,512,128]{2,1,0:T(8,128)(2,1)S(1)} %get-tuple-element.208), channel_id=1, source_target_pairs={{4,0},{8,4},{12,8},{5,1},{9,5},{13,9},{6,2},{10,6},{14,10},{7,3},{... | collective-permute-start | bytes 786440 | tf_op jit(solution)/shard_map/ppermute | solution.py:66
  297.0 40.5 %collective-permute-start.29 = (bf16[384,1280]{1,0:T(8,128)(2,1)S(1)}, bf16[384,1280]{1,0:T(8,128)(2,1)S(1)}, u32[]{:S(2)}, u32[]{:S(2)}) collective-permute-start(bf16[384,1280]{1,0:T(8,128)(2,1)S(1)} %get-tuple-element.225), channel_id=1, source_target_pairs={{0,4},{4,0},{8,12},{12,8},{1,5},{5,1},{9,13},{13,9},{2,6},{6,2},{1... | collective-permute-start | bytes 2949128 | tf_op jit(solution)/shard_map/ppermute | solution.py:1054
  303.9 25.7 %collective-permute-start.24 = (bf16[2,512,128]{2,1,0:T(8,128)(2,1)S(1)}, bf16[2,512,128]{2,1,0:T(8,128)(2,1)S(1)}, u32[]{:S(2)}, u32[]{:S(2)}) collective-permute-start(bf16[2,512,128]{2,1,0:T(8,128)(2,1)S(1)} %get-tuple-element.213), channel_id=1, source_target_pairs={{4,0},{8,4},{12,8},{5,1},{9,5},{13,9},{6,2},{10,6},{14,10},{7,3},{... | collective-permute-start | bytes 786440 | tf_op jit(solution)/shard_map/ppermute | solution.py:66
  336.9 9.1 %collective-permute-start.26 = (bf16[256,1536]{1,0:T(8,128)(2,1)S(1)}, bf16[256,1536]{1,0:T(8,128)(2,1)S(1)}, u32[]{:S(2)}, u32[]{:S(2)}) collective-permute-start(bf16[256,1536]{1,0:T(8,128)(2,1)S(1)} %get-tuple-element.221), channel_id=1, source_target_pairs={{0,1},{1,0},{2,3},{3,2},{4,5},{5,4},{6,7},{7,6},{8,9},{9,8},{10,11... | collective-permute-start | bytes 2359304 | tf_op jit(solution)/shard_map/ppermute | solution.py:48
  336.9 9.0 %collective-permute-start.27 = (bf16[256,1536]{1,0:T(8,128)(2,1)S(1)}, bf16[256,1536]{1,0:T(8,128)(2,1)S(1)}, u32[]{:S(2)}, u32[]{:S(2)}) collective-permute-start(bf16[256,1536]{1,0:T(8,128)(2,1)S(1)} %get-tuple-element.222), channel_id=1, source_target_pairs={{0,1},{1,0},{2,3},{3,2},{4,5},{5,4},{6,7},{7,6},{8,9},{9,8},{10,11... | collective-permute-start | bytes 2359304 | tf_op jit(solution)/shard_map/ppermute | solution.py:48
  337.4 63.9 %collective-permute-start.37 = (bf16[768,1280]{1,0:T(8,128)(2,1)}, bf16[768,1280]{1,0:T(8,128)(2,1)}, u32[]{:S(2)}, u32[]{:S(2)}) collective-permute-start(bf16[768,1280]{1,0:T(8,128)(2,1)} %get-tuple-element.242), channel_id=1, source_target_pairs={{0,16},{16,0},{1,17},{17,1},{2,18},{18,2},{3,19},{19,3},{4,20},{20... | collective-permute-start | bytes 5898248 | tf_op jit(solution)/shard_map/ppermute | solution.py:1045
  337.4 24.6 %collective-permute-start.39 = (bf16[192,1280]{1,0:T(8,128)(2,1)}, bf16[192,1280]{1,0:T(8,128)(2,1)S(1)}, u32[]{:S(2)}, u32[]{:S(2)}) collective-permute-start(bf16[192,1280]{1,0:T(8,128)(2,1)} %get-tuple-element.248), channel_id=1, source_target_pairs={{0,8},{4,12},{8,0},{12,4},{1,9},{5,13},{9,1},{13,5},{2,10},{6,14},... | collective-permute-start | bytes 1474568 | tf_op jit(solution)/shard_map/ppermute | solution.py:1059
  361.2 25.8 %collective-permute-start.30 = (bf16[256,1536]{1,0:T(8,128)(2,1)S(1)}, bf16[256,1536]{1,0:T(8,128)(2,1)S(1)}, u32[]{:S(2)}, u32[]{:S(2)}) collective-permute-start(bf16[256,1536]{1,0:T(8,128)(2,1)S(1)} %get-tuple-element.231), channel_id=1, source_target_pairs={{0,1},{1,0},{2,3},{3,2},{4,5},{5,4},{6,7},{7,6},{8,9},{9,8},{10,11... | collective-permute-start | bytes 2359304 | tf_op jit(solution)/shard_map/ppermute | solution.py:48
  361.3 26.2 %collective-permute-start.31 = (bf16[256,1536]{1,0:T(8,128)(2,1)S(1)}, bf16[256,1536]{1,0:T(8,128)(2,1)S(1)}, u32[]{:S(2)}, u32[]{:S(2)}) collective-permute-start(bf16[256,1536]{1,0:T(8,128)(2,1)S(1)} %get-tuple-element.232), channel_id=1, source_target_pairs={{0,1},{1,0},{2,3},{3,2},{4,5},{5,4},{6,7},{7,6},{8,9},{9,8},{10,11... | collective-permute-start | bytes 2359304 | tf_op jit(solution)/shard_map/ppermute | solution.py:48
  361.8 23.7 %collective-permute-start.40 = (bf16[192,1280]{1,0:T(8,128)(2,1)S(1)}, bf16[192,1280]{1,0:T(8,128)(2,1)S(1)}, u32[]{:S(2)}, u32[]{:S(2)}) collective-permute-start(bf16[192,1280]{1,0:T(8,128)(2,1)S(1)} %get-tuple-element.249), channel_id=1, source_target_pairs={{0,8},{4,12},{8,0},{12,4},{1,9},{5,13},{9,1},{13,5},{2,10},{6,14},... | collective-permute-start | bytes 1474568 | tf_op jit(solution)/shard_map/ppermute | solution.py:1059
  362.0 38.3 %collective-permute-start.38 = (bf16[384,1024]{1,0:T(8,128)(2,1)S(1)}, bf16[384,1024]{1,0:T(8,128)(2,1)S(1)}, u32[]{:S(2)}, u32[]{:S(2)}) collective-permute-start(bf16[384,1024]{1,0:T(8,128)(2,1)S(1)} %copy-done.98), channel_id=1, source_target_pairs={{0,4},{4,0},{8,12},{12,8},{1,5},{5,1},{9,13},{13,9},{2,6},{6,2},{1... | collective-permute-start | bytes 2359304 | tf_op jit(solution)/shard_map/ppermute | solution.py:1054
  385.5 25.4 %collective-permute-start.35 = (bf16[256,1536]{1,0:T(8,128)(2,1)}, bf16[256,1536]{1,0:T(8,128)(2,1)}, u32[]{:S(2)}, u32[]{:S(2)}) collective-permute-start(bf16[256,1536]{1,0:T(8,128)(2,1)} %get-tuple-element.240.refs_4_), channel_id=1, source_target_pairs={{0,2},{1,3},{2,0},{3,1},{4,6},{5,7},{6,4},{7,5},{8,10},{9,11},{10,... | collective-permute-start | bytes 2359304 | tf_op jit(solution)/shard_map/ppermute | solution.py:52
  387.0 35.1 %collective-permute-start.36 = (bf16[256,1536]{1,0:T(8,128)(2,1)}, bf16[256,1536]{1,0:T(8,128)(2,1)}, u32[]{:S(2)}, u32[]{:S(2)}) collective-permute-start(bf16[256,1536]{1,0:T(8,128)(2,1)} %get-tuple-element.241.refs_5_), channel_id=1, source_target_pairs={{0,2},{1,3},{2,0},{3,1},{4,6},{5,7},{6,4},{7,5},{8,10},{9,11},{10,... | collective-permute-start | bytes 2359304 | tf_op jit(solution)/shard_map/ppermute | solution.py:52
  387.6 64.9 %collective-permute-start.34 = (bf16[768,1024]{1,0:T(8,128)(2,1)}, bf16[768,1024]{1,0:T(8,128)(2,1)}, u32[]{:S(2)}, u32[]{:S(2)}) collective-permute-start(bf16[768,1024]{1,0:T(8,128)(2,1)} %get-tuple-element.238), channel_id=1, source_target_pairs={{0,16},{16,0},{1,17},{17,1},{2,18},{18,2},{3,19},{19,3},{4,20},{20... | collective-permute-start | bytes 4718600 | tf_op jit(solution)/shard_map/ppermute | solution.py:1045
  401.4 30.7 %collective-permute-start.41 = (bf16[192,1024]{1,0:T(8,128)(2,1)}, bf16[192,1024]{1,0:T(8,128)(2,1)S(1)}, u32[]{:S(2)}, u32[]{:S(2)}) collective-permute-start(bf16[192,1024]{1,0:T(8,128)(2,1)} %get-tuple-element.255), channel_id=1, source_target_pairs={{0,8},{4,12},{8,0},{12,4},{1,9},{5,13},{9,1},{13,5},{2,10},{6,14},... | collective-permute-start | bytes 1179656 | tf_op jit(solution)/shard_map/ppermute | solution.py:1059
  409.2 50.8 %collective-permute-start.46 = (bf16[384,1280]{1,0:T(8,128)(2,1)}, bf16[384,1280]{1,0:T(8,128)(2,1)}, u32[]{:S(2)}, u32[]{:S(2)}) collective-permute-start(bf16[384,1280]{1,0:T(8,128)(2,1)} %get-tuple-element.262), channel_id=1, source_target_pairs={{0,4},{4,0},{8,12},{12,8},{1,5},{5,1},{9,13},{13,9},{2,6},{6,2},{1... | collective-permute-start | bytes 2949128 | tf_op jit(solution)/shard_map/ppermute | solution.py:1054
  410.9 48.9 %collective-permute-start.43 = (bf16[768,512]{1,0:T(8,128)(2,1)}, bf16[768,512]{1,0:T(8,128)(2,1)}, u32[]{:S(2)}, u32[]{:S(2)}) collective-permute-start(bf16[768,512]{1,0:T(8,128)(2,1)} %copy-done.94), channel_id=1, source_target_pairs={{0,16},{16,0},{1,17},{17,1},{2,18},{18,2},{3,19},{19,3},{4,20},{20... | collective-permute-start | bytes 2359304 | tf_op jit(solution)/shard_map/ppermute | solution.py:1045
  432.1 38.8 %collective-permute-start.44 = (f32[256,1536]{1,0:T(8,128)}, f32[256,1536]{1,0:T(8,128)}, u32[]{:S(2)}, u32[]{:S(2)}) collective-permute-start(f32[256,1536]{1,0:T(8,128)} %get-tuple-element.259.refs_1_), channel_id=1, source_target_pairs={{0,1},{1,0},{2,3},{3,2},{4,5},{5,4},{6,7},{7,6},{8,9},{9,8},{10,11... | collective-permute-start | bytes 4718600 | tf_op jit(solution)/shard_map/ppermute | solution.py:48
  432.1 39.4 %collective-permute-start.45 = (f32[256,1536]{1,0:T(8,128)}, f32[256,1536]{1,0:T(8,128)}, u32[]{:S(2)}, u32[]{:S(2)}) collective-permute-start(f32[256,1536]{1,0:T(8,128)} %get-tuple-element.260.refs_2_), channel_id=1, source_target_pairs={{0,1},{1,0},{2,3},{3,2},{4,5},{5,4},{6,7},{7,6},{8,9},{9,8},{10,11... | collective-permute-start | bytes 4718600 | tf_op jit(solution)/shard_map/ppermute | solution.py:48
  453.5 33.8 %collective-permute-start.32 = (bf16[256,1536]{1,0:T(8,128)(2,1)S(1)}, bf16[256,1536]{1,0:T(8,128)(2,1)S(1)}, u32[]{:S(2)}, u32[]{:S(2)}) collective-permute-start(bf16[256,1536]{1,0:T(8,128)(2,1)S(1)} %copy-done.87), channel_id=1, source_target_pairs={{0,2},{1,3},{2,0},{3,1},{4,6},{5,7},{6,4},{7,5},{8,10},{9,11},{10,... | collective-permute-start | bytes 2359304 | tf_op jit(solution)/shard_map/ppermute | solution.py:52
  459.8 10.9 %collective-permute-start.47 = (bf16[192,1024]{1,0:T(8,128)(2,1)S(1)}, bf16[192,1024]{1,0:T(8,128)(2,1)S(1)}, u32[]{:S(2)}, u32[]{:S(2)}) collective-permute-start(bf16[192,1024]{1,0:T(8,128)(2,1)S(1)} %get-tuple-element.267), channel_id=1, source_target_pairs={{0,16},{16,0},{1,17},{17,1},{2,18},{18,2},{3,19},{19,3},{4,20},{20... | collective-permute-start | bytes 1179656 | tf_op jit(solution)/shard_map/ppermute | solution.py:1083
  460.0 24.4 %collective-permute-start.42 = (bf16[384,1024]{1,0:T(8,128)(2,1)S(1)}, bf16[384,1024]{1,0:T(8,128)(2,1)S(1)}, u32[]{:S(2)}, u32[]{:S(2)}) collective-permute-start(bf16[384,1024]{1,0:T(8,128)(2,1)S(1)} %get-tuple-element.257), channel_id=1, source_target_pairs={{0,4},{4,0},{8,12},{12,8},{1,5},{5,1},{9,13},{13,9},{2,6},{6,2},{1... | collective-permute-start | bytes 2359304 | tf_op jit(solution)/shard_map/ppermute | solution.py:1054
  470.7 23.6 %collective-permute-start.48 = (bf16[192,1280]{1,0:T(8,128)(2,1)S(1)}, bf16[192,1280]{1,0:T(8,128)(2,1)S(1)}, u32[]{:S(2)}, u32[]{:S(2)}) collective-permute-start(bf16[192,1280]{1,0:T(8,128)(2,1)S(1)} %get-tuple-element.269), channel_id=1, source_target_pairs={{0,8},{4,12},{8,0},{12,4},{1,9},{5,13},{9,1},{13,5},{2,10},{6,14},... | collective-permute-start | bytes 1474568 | tf_op jit(solution)/shard_map/ppermute | solution.py:1059
  470.9 24.6 %collective-permute-start.33 = (bf16[256,1536]{1,0:T(8,128)(2,1)S(1)}, bf16[256,1536]{1,0:T(8,128)(2,1)S(1)}, u32[]{:S(2)}, u32[]{:S(2)}) collective-permute-start(bf16[256,1536]{1,0:T(8,128)(2,1)S(1)} %copy-done.89), channel_id=1, source_target_pairs={{0,2},{1,3},{2,0},{3,1},{4,6},{5,7},{6,4},{7,5},{8,10},{9,11},{10,... | collective-permute-start | bytes 2359304 | tf_op jit(solution)/shard_map/ppermute | solution.py:52
  471.5 25.5 %collective-permute-start.53 = (bf16[768,384]{1,0:T(8,128)(2,1)S(1)}, bf16[768,384]{1,0:T(8,128)(2,1)S(1)}, u32[]{:S(2)}, u32[]{:S(2)}) collective-permute-start(bf16[768,384]{1,0:T(8,128)(2,1)S(1)} %copy-done.100), channel_id=1, source_target_pairs={{0,16},{16,0},{1,17},{17,1},{2,18},{18,2},{3,19},{19,3},{4,20},{20... | collective-permute-start | bytes 1769480 | tf_op jit(solution)/shard_map/ppermute | solution.py:1045
  484.4 16.1 %collective-permute-start.52 = (f32[8,512]{1,0:T(8,128)S(1)}, f32[8,512]{1,0:T(8,128)S(1)}, u32[]{:S(2)}, u32[]{:S(2)}) collective-permute-start(f32[8,512]{1,0:T(8,128)S(1)} %copy-done.91), channel_id=1, source_target_pairs={{0,16},{16,0},{1,17},{17,1},{2,18},{18,2},{3,19},{19,3},{4,20},{20... | collective-permute-start | bytes 49160 | tf_op jit(solution)/shard_map/ppermute | solution.py:1164
  487.3 18.0 %collective-permute-start.51 = (bf16[384,512]{1,0:T(8,128)(2,1)S(1)}, bf16[384,512]{1,0:T(8,128)(2,1)S(1)}, u32[]{:S(2)}, u32[]{:S(2)}) collective-permute-start(bf16[384,512]{1,0:T(8,128)(2,1)S(1)} %get-tuple-element.273), channel_id=1, source_target_pairs={{0,4},{4,0},{8,12},{12,8},{1,5},{5,1},{9,13},{13,9},{2,6},{6,2},{1... | collective-permute-start | bytes 1179656 | tf_op jit(solution)/shard_map/ppermute | solution.py:1054
  494.4 18.9 %collective-permute-start.57 = (bf16[192,1024]{1,0:T(8,128)(2,1)S(1)}, bf16[192,1024]{1,0:T(8,128)(2,1)S(1)}, u32[]{:S(2)}, u32[]{:S(2)}) collective-permute-start(bf16[192,1024]{1,0:T(8,128)(2,1)S(1)} %get-tuple-element.287), channel_id=1, source_target_pairs={{0,8},{4,12},{8,0},{12,4},{1,9},{5,13},{9,1},{13,5},{2,10},{6,14},... | collective-permute-start | bytes 1179656 | tf_op jit(solution)/shard_map/ppermute | solution.py:1059
  496.9 25.0 %collective-permute-start.49 = (bf16[256,1536]{1,0:T(8,128)(2,1)S(1)}, bf16[256,1536]{1,0:T(8,128)(2,1)S(1)}, u32[]{:S(2)}, u32[]{:S(2)}) collective-permute-start(bf16[256,1536]{1,0:T(8,128)(2,1)S(1)} %get-tuple-element.270.refs_1_), channel_id=1, source_target_pairs={{0,1},{1,0},{2,3},{3,2},{4,5},{5,4},{6,7},{7,6},{8,9},{9,8},{10,11... | collective-permute-start | bytes 2359304 | tf_op jit(solution)/shard_map/ppermute | solution.py:48
  497.0 24.9 %collective-permute-start.50 = (bf16[256,1536]{1,0:T(8,128)(2,1)S(1)}, bf16[256,1536]{1,0:T(8,128)(2,1)S(1)}, u32[]{:S(2)}, u32[]{:S(2)}) collective-permute-start(bf16[256,1536]{1,0:T(8,128)(2,1)S(1)} %get-tuple-element.271.refs_2_), channel_id=1, source_target_pairs={{0,1},{1,0},{2,3},{3,2},{4,5},{5,4},{6,7},{7,6},{8,9},{9,8},{10,11... | collective-permute-start | bytes 2359304 | tf_op jit(solution)/shard_map/ppermute | solution.py:48
  500.5 23.6 %collective-permute-start.56 = (bf16[384,384]{1,0:T(8,128)(2,1)S(1)}, bf16[384,384]{1,0:T(8,128)(2,1)S(1)}, u32[]{:S(2)}, u32[]{:S(2)}) collective-permute-start(bf16[384,384]{1,0:T(8,128)(2,1)S(1)} %get-tuple-element.285), channel_id=1, source_target_pairs={{0,4},{4,0},{8,12},{12,8},{1,5},{5,1},{9,13},{13,9},{2,6},{6,2},{1... | collective-permute-start | bytes 884744 | tf_op jit(solution)/shard_map/ppermute | solution.py:1054
  505.3 18.9 %collective-permute-start.55 = (f32[8,512]{1,0:T(8,128)S(1)}, f32[8,512]{1,0:T(8,128)S(1)}, u32[]{:S(2)}, u32[]{:S(2)}) collective-permute-start(f32[8,512]{1,0:T(8,128)S(1)} %get-tuple-element.283.refs_0_), channel_id=1, source_target_pairs={{0,4},{4,0},{8,12},{12,8},{1,5},{5,1},{9,13},{13,9},{2,6},{6,2},{1... | collective-permute-start | bytes 49160 | tf_op jit(solution)/shard_map/ppermute | solution.py:1166
  513.2 8.5 %collective-permute-start.54 = (bf16[192,512]{1,0:T(8,128)(2,1)S(1)}, bf16[192,512]{1,0:T(8,128)(2,1)S(1)}, u32[]{:S(2)}, u32[]{:S(2)}) collective-permute-start(bf16[192,512]{1,0:T(8,128)(2,1)S(1)} %get-tuple-element.282), channel_id=1, source_target_pairs={{0,8},{4,12},{8,0},{12,4},{1,9},{5,13},{9,1},{13,5},{2,10},{6,14},... | collective-permute-start | bytes 589832 | tf_op jit(solution)/shard_map/ppermute | solution.py:1059
  (141 other events, 1046.2 us)

commit v4 on v3

--- a/solution.py
+++ b/solution.py
@@ -167,7 +167,7 @@
             jax.ShapeDtypeStruct((total, columns - HD), jnp.bfloat16),
             jax.ShapeDtypeStruct((total, HD), jnp.bfloat16),
         ],
-        compiler_params=pltpu.CompilerParams(vmem_limit_bytes=24 * MIB),
+        compiler_params=pltpu.CompilerParams(vmem_limit_bytes=32 * MIB),
         cost_estimate=cost(2 * total * width * columns, 9 * MIB),
         name="first",
     )(core, tokens, gain, weight, bias, cosine, sine)
@@ -270,7 +270,7 @@
             jax.ShapeDtypeStruct((rows, local, columns), jnp.bfloat16),
             jax.ShapeDtypeStruct((rows, blocks, heads * Q_BLOCK), jnp.float32),
         ],
-        compiler_params=pltpu.CompilerParams(vmem_limit_bytes=24 * MIB),
+        compiler_params=pltpu.CompilerParams(vmem_limit_bytes=32 * MIB),
         cost_estimate=cost(8_000_000_000, 4 * MIB),
         name="attend",
     )(low, core, q, start, *span, *mate)
@@ -617,60 +617,76 @@
     )
 
 
-def share_kernel(columns, skip, extra, halves, pick_ref, blocks_ref, left_ref, right_ref, *refs):
-    out = dot(left_ref[...], right_ref[...])
+def share_kernel(plan, lefts, rights, extra, halves, pick_ref, blocks_ref, *refs):
+    step = pl.program_id(0)
+    left_refs, right_refs = refs[:lefts], refs[lefts : lefts + rights]
+    refs = refs[lefts + rights :]
     if extra:
-        out = out + to_f(refs[0][...])
-        refs = refs[1:]
-    tile = out.shape[1]
-    spot = (pl.program_id(0) + skip) * tile + lax.broadcasted_iota(jnp.int32, (1, tile), 1)
-    out = to_bf(jnp.where(spot < columns, out, 0.0))
-    if not halves:
-        refs[0][...] = out
-        return
-    send_ref, keep_ref, rows = refs
-    rows[...] = out
-    share = send_ref.shape[0] // (2 * halves)
-    for i in range(2 * halves):
-        here = slice(i * share, (i + 1) * share)
-        send_ref[here] = rows[pl.ds(pl.multiple_of(blocks_ref[i] * share, share), share)]
-        keep_ref[here] = rows[pl.ds(pl.multiple_of(blocks_ref[2 * halves + i] * share, share), share)]
-
-
-def share_of(order, left, right, part, pick, span, tile=0, extra=None, blocks=None):
-    tokens, columns = right.shape
-    tile = tile or TILE
-    skip, count = span
-    column = pl.BlockSpec((part, tile), lambda i, *refs: (0, i))
+        extra_ref, refs = refs[0], refs[1:]
+    for left, right, begin, end, shift, columns, target in plan:
+
+        @pl.when((step >= begin) & (step < end))
+        def _(left=left, right=right, shift=shift, columns=columns, target=target):
+            out = dot(left_refs[left][...], right_refs[right][...])
+            if extra:
+                out = out + to_f(extra_ref[...])
+            tile = out.shape[1]
+            spot = (step + shift) * tile + lax.broadcasted_iota(jnp.int32, (1, tile), 1)
+            out = to_bf(jnp.where(spot < columns, out, 0.0))
+            if not halves:
+                refs[target][...] = out
+                return
+            send_ref, keep_ref, rows = refs
+            rows[...] = out
+            share = send_ref.shape[0] // (2 * halves)
+            for i in range(2 * halves):
+                here = slice(i * share, (i + 1) * share)
+                send_ref[here] = rows[pl.ds(pl.multiple_of(blocks_ref[i] * share, share), share)]
+                keep_ref[here] = rows[pl.ds(pl.multiple_of(blocks_ref[2 * halves + i] * share, share), share)]
+
+
+def clipped(rows, tile, begin, count, shift=0):
+    return pl.BlockSpec((rows, tile), lambda i, *refs: (0, jnp.clip(i - begin, 0, count - 1) + shift))
+
+
+def share_of(order, lefts, rights, parts, part, pick, tile, extra=None, blocks=None):
+    tokens = lefts[0].shape[1]
+    plan, at = [], 0
+    starts, sizes, right_at = {}, {}, {}
+    for left, right, skip, count, target in parts:
+        plan.append((left, right, at, at + count, skip - at, rights[right].shape[1], target))
+        starts.setdefault(target, at)
+        sizes[target] = sizes.get(target, 0) + count
+        first, tiles, low = right_at.get(right, (at, 0, skip))
+        right_at[right] = (first, tiles + count, low)
+        at += count
+    halves = 0
     extras = [] if extra is None else [extra]
     scratch = []
-    outs, shapes = [column], [jax.ShapeDtypeStruct((part, count * tile), jnp.bfloat16)]
-    halves = 0
     if blocks is None:
         blocks = jnp.zeros((1,), jnp.int32)
+        outs = [clipped(part, tile, starts[t], sizes[t]) for t in sorted(sizes)]
+        shapes = [jax.ShapeDtypeStruct((part, sizes[t] * tile), jnp.bfloat16) for t in sorted(sizes)]
     else:
         halves = blocks.shape[0] // 4
-        outs = [pl.BlockSpec((part // 2, tile), lambda i, *refs: (0, i))] * 2
-        shapes = [jax.ShapeDtypeStruct((part // 2, count * tile), jnp.bfloat16)] * 2
+        outs = [clipped(part // 2, tile, 0, at)] * 2
+        shapes = [jax.ShapeDtypeStruct((part // 2, at * tile), jnp.bfloat16)] * 2
         scratch = [pltpu.VMEM((part, tile), jnp.bfloat16)]
-    result = order(
-        functools.partial(share_kernel, columns, skip, len(extras), halves),
-        [left, right, *extras],
-        [
-            pl.BlockSpec((part, tokens), lambda i, pick_ref, blocks_ref: (pick_ref[0], 0)),
-            pl.BlockSpec((tokens, tile), lambda i, *refs: (0, i + skip)),
-        ]
-        + [column] * len(extras),
+    return order(
+        functools.partial(share_kernel, plan, len(lefts), len(rights), len(extras), halves),
+        [*lefts, *rights, *extras],
+        [pl.BlockSpec((part, tokens), lambda i, pick_ref, blocks_ref: (pick_ref[0], 0))] * len(lefts)
+        + [clipped(tokens, tile, *right_at[r]) for r in range(len(rights))]
+        + [clipped(part, tile, 0, at)] * len(extras),
         outs,
         shapes,
-        (count,),
-        2 * part * tokens * count * tile,
-        2 * (part * tokens + (part + tokens) * count * tile),
+        (at,),
+        2 * part * tokens * at * tile,
+        2 * (part * tokens + (part + tokens) * at * tile),
         "share",
         scalars=(jnp.asarray(pick, jnp.int32).reshape(1), blocks),
         scratch=scratch,
     )
-    return result if halves else result[0]
 
 
 def relay_kernel(keep_ref, come_ref, out_ref):
@@ -693,26 +709,91 @@
     )[0]
 
 
-def settle_kernel(pick_ref, keep_ref, come_ref, last_ref, out_ref):
-    out_ref[...] = to_bf(to_f(keep_ref[...]) + to_f(come_ref[...]) + to_f(last_ref[...]))
-
-
-def settle(order, keep, come, last, pick):
+def settle_kernel(pick_ref, keep_ref, come_ref, last_ref, sent_ref, mine_ref):
+    out = to_bf(to_f(keep_ref[...]) + to_f(come_ref[...]) + to_f(last_ref[...]))
+
+    @pl.when(pl.program_id(0) == 0)
+    def _():
+        sent_ref[...] = out
+
+    @pl.when(pl.program_id(0) == 1)
+    def _():
+        mine_ref[...] = out
+
+
+def settle(order, keep, come, last, picks):
     share = last.shape[0] // 2
     columns = keep.shape[1]
-    pair = pl.BlockSpec((share, columns), lambda i, pick_ref: (2 * pick_ref[0], 0))
+    pair = pl.BlockSpec((share, columns), lambda i, pick_ref: (2 * pick_ref[i], 0))
+    whole = pl.BlockSpec((share, columns), lambda i, pick_ref: (0, 0))
     return order(
         settle_kernel,
         [keep, come, last],
-        [pair, pair, pl.BlockSpec((share, columns), lambda i, pick_ref: (pick_ref[0], 0))],
-        [pl.BlockSpec((share, columns), lambda i, pick_ref: (0, 0))],
-        [jax.ShapeDtypeStruct((share, columns), jnp.bfloat16)],
-        (1,),
+        [pair, pair, pl.BlockSpec((share, columns), lambda i, pick_ref: (pick_ref[i], 0))],
+        [whole] * 2,
+        [jax.ShapeDtypeStruct((share, columns), jnp.bfloat16)] * 2,
+        (2,),
         0,
-        8 * share * columns,
+        16 * share * columns,
         "settle",
-        scalars=(pick.reshape(1),),
-    )[0]
+        scalars=(picks,),
+    )
+
+
+def finish_kernel(plan, columns, gains, *refs):
+    out_ref = refs[-2] if gains else refs[-1]
+    step = pl.program_id(0)
+    tile = out_ref.shape[1]
+    for begin, end, first, count in plan:
+
+        @pl.when((step >= begin) & (step < end))
+        def _(first=first, count=count):
+            out = to_f(refs[first][...])
+            for ref in refs[first + 1 : first + count]:
+                out = out + to_f(ref[...])
+            out_ref[...] = out
+            if gains:
+                spot = step * tile + lax.broadcasted_iota(jnp.int32, (1, tile), 1)
+                terms = jnp.where(spot < columns, out * to_f(refs[-3][...]), 0.0)
+                total = terms[:, :HD]
+                for i in range(HD, tile, HD):
+                    total = total + terms[:, i : i + HD]
+
+                @pl.when(step == 0)
+                def _():
+                    refs[-1][...] = total
+
+                @pl.when(step > 0)
+                def _():
+                    refs[-1][...] += total
+
+
+def finish(order, chunks, share, columns, tile, weight=None):
+    plan, specs, args, at = [], [], [], 0
+    for chunk in chunks:
+        count = chunk[0].shape[1] // tile
+        plan.append((at, at + count, len(args), len(chunk)))
+        specs += [clipped(share, tile, at, count)] * len(chunk)
+        args += chunk
+        at += count
+    column = pl.BlockSpec((share, tile), lambda i: (0, i))
+    outs, shapes = [column], [jax.ShapeDtypeStruct((share, columns), jnp.float32)]
+    if weight is not None:
+        args.append(weight)
+        specs.append(column)
+        outs.append(pl.BlockSpec((share, HD), lambda i: (0, 0)))
+        shapes.append(jax.ShapeDtypeStruct((share, HD), jnp.float32))
+    return order(
+        functools.partial(finish_kernel, plan, columns, weight is not None),
+        args,
+        specs,
+        outs,
+        shapes,
+        (at,),
+        0,
+        14 * share * columns,
+        "finish",
+    )
 
 
 def narrow_kernel(pairs, extras, right_dim, *refs):
@@ -1030,27 +1111,32 @@
     units = gate_t.shape[0]
     tiles = -(-units // TILE)
     cut = (tiles + 1) // 2
-    long = cut
+    long = -(-2 * tiles // 3)
     one, two = seq_index ^ 1, seq_index ^ 2
     three = seq_index ^ 3
     quad = jnp.stack([one, three, seq_index, two])
     wide = jnp.stack([one, three, one + seqs, three + seqs, seq_index, two, seq_index + seqs, two + seqs])
 
+    begin = (dp_index * seqs + seq_index) * share
+
+    def rows_of(value):
+        return lax.dynamic_slice_in_dim(value, begin, share, 0)
+
     class Rows:
-        def __init__(self, left_t, right, span, tile=TILE):
-            self.args = (left_t, right)
-            self.span, self.tile = span, tile
-            if near_pair:
-                sent = share_of(order, left_t, right, part, 1 - dp_index, span, tile)
-                self.come = lax.ppermute(sent, "dp", flipped("dp", 0))
-            else:
-                self.whole = share_of(order, left_t, right, width, 0, span, tile)
+        def __init__(self, lefts, rights, parts, tile=TILE, sent=None):
+            self.args = (order, lefts, rights, parts)
+            self.tile = tile
+            if not near_pair:
+                (whole,) = share_of(*self.args, width, 0, tile)
+                self.whole = lax.psum_scatter(whole, ("dp", "seq"), scatter_dimension=0, tiled=True)
+                return
+            if sent is None:
+                (sent,) = share_of(*self.args, part, 1 - dp_index, tile)
+            self.come = lax.ppermute(sent, "dp", flipped("dp", 0))
 
         def own(self):
             if near_pair:
-                send, self.keep = share_of(
-                    order, *self.args, part, dp_index, self.span, self.tile, self.come, quad
-                )
+                send, self.keep = share_of(*self.args, part, dp_index, self.tile, self.come, quad)
                 self.come = lax.ppermute(send, "seq", flipped("seq", 0))
 
         def relay(self):
@@ -1063,31 +1149,25 @@
                 order.arrived(self.last)
 
         def result(self):
-            if near_pair:
-                return to_f(self.keep[:share]) + to_f(self.come[:share]) + to_f(self.last)
-            return to_f(lax.psum_scatter(self.whole, ("dp", "seq"), scatter_dimension=0, tiled=True))
+            return [self.keep, self.come, self.last] if near_pair else [self.whole]
 
     class SeqFirst(Rows):
-        def __init__(self, left_t, right, span, tile=TILE):
-            self.near = near_pair
-            if near_pair:
-                send, self.keep = share_of(order, left_t, right, width, 0, span, tile, None, wide)
-                self.come = lax.ppermute(send, "seq", flipped("seq", 0))
-            else:
-                super().__init__(left_t, right, span, tile)
+        def __init__(self, lefts, rights, parts, tile=TILE):
+            if not near_pair:
+                super().__init__(lefts, rights, parts, tile)
+                return
+            send, self.keep = share_of(order, lefts, rights, parts, width, 0, tile, None, wide)
+            self.come = lax.ppermute(send, "seq", flipped("seq", 0))
 
         def settle(self):
             if near_pair:
-                sent = settle(order, self.keep, self.come, self.last, 1 - dp_index)
-                self.mine = settle(order, self.keep, self.come, self.last, dp_index)
+                sent, self.mine = settle(
+                    order, self.keep, self.come, self.last, jnp.stack([1 - dp_index, dp_index])
+                )
                 self.final = lax.ppermute(sent, "dp", flipped("dp", 0))
 
-        def placed(self):
-            if near_pair:
-                order.arrived(self.final)
-
         def result(self):
-            return to_f(self.mine) + to_f(self.final) if near_pair else super().result()
+            return [self.mine, self.final] if near_pair else [self.whole]
 
     sent = core_swaps(narrow(order, [(mixed, o_weight)], 1, (), 1))
     mine = narrow(order, [(mixed, o_weight)], 0, sent, 1)
@@ -1095,26 +1175,50 @@
     grad_ffn, grad_ffn_t = grad_out_of(
         order, core_one, cotangent.reshape(total, width), valid.reshape(total, 1)
     )
+    gate_rows, up_rows = rows_of(gate_weight), rows_of(up_weight)
+    order.arrived(gate_rows, up_rows)
     grad_hidden = grad_hidden_of(order, grad_ffn, down_t)
     h_one_t = turn(order, [h_one])
     middle, h_two = middle_of(order, core_one, flat_tokens, mine, come, gain_two)
     h_two += core_swaps(h_two)
     hidden, grad_gate, grad_up = gated(order, h_two, grad_hidden, gate_t, up_t)
 
-    down_a = Rows(grad_ffn_t, hidden, (0, cut))
-    down_b = SeqFirst(grad_ffn_t, hidden, (cut, tiles - cut))
+    down_a = Rows([grad_ffn_t], [hidden], [(0, 0, 0, long, 0)])
+    down_b = SeqFirst([grad_ffn_t], [hidden], [(0, 0, long, tiles - long, 0)])
     pairs = [(grad_gate, gate_t), (grad_up, up_t)]
     sent = core_swaps(narrow(order, pairs, 1))
     mine = narrow(order, pairs, 0, sent)
     come = chip_swaps(mine)
     h_two_t = turn(order, h_two)
-    gate_a = Rows(h_two_t, grad_gate, (0, long))
+    up_cut = long
+    if near_pair:
+        sends = share_of(
+            order,
+            [h_two_t],
+            [grad_gate, grad_up],
+            [
+                (0, 0, 0, tiles, 0),
+                (0, 1, 0, up_cut, 1),
+                (0, 1, up_cut, tiles - up_cut, 2),
+            ],
+            part,
+            1 - dp_index,
+            TILE,
+        )
+    else:
+        sends = [None] * 3
+
+    def half_rows(right, begin, end, sent):
+        return Rows([h_two_t], [right], [(0, 0, begin, end - begin, 0)], TILE, sent)
+
+    gate = half_rows(grad_gate, 0, tiles, sends[0])
     down_b.relay()
     down_a.own()
+    up_a = half_rows(grad_up, 0, up_cut, sends[1])
+    up_b = half_rows(grad_up, up_cut, tiles, sends[2])
     grad_middle, *branch = norm_back(order, core_one, mine, come, middle, gain_two, grad_ffn, False)
     branch += core_swaps(branch)
     grad_mixed = mixed_back(order, branch, o_weight).reshape(rows, local, heads * HD)
-    gate_b = Rows(h_two_t, grad_gate, (long, tiles - long))
     grad_q_rows, keep, *sends = attend_back(
         order, low, core_one, q_rows, start, span, mate, grad_mixed, mixed_rows, lse, cosine, sine
     )
@@ -1123,70 +1227,55 @@
     own_kv, *pieces = fold(order, keep, comes, local)
     moving = shifted(pieces[-1], -1) if pieces else None
     down_b.settled()
-    gate_a.own()
     for piece in pieces[-2::-1]:
         moving = shifted(carry(order, piece, moving), -1)
-    down_a.relay()
     grad_qkv, bias_sum = join(
         order, core_one, grad_q_rows, own_kv, [] if moving is None else [moving], cosine, sine
     )
-    up_a = Rows(h_two_t, grad_up, (0, cut))
     sent = core_swaps(narrow(order, [(grad_qkv, weight)], 1, (), 1))
-    gate_a.relay()
-    gate_b.own()
+    down_a.relay()
     mine = narrow(order, [(grad_qkv, weight)], 0, sent, 1)
     come = chip_swaps(mine)
-    up_b = Rows(h_two_t, grad_up, (cut, tiles - cut))
+    last_parts = [(0, 0, 0, grad_qkv.shape[1] // HD, 0), (1, 1, 0, heads, 0)]
+    last = Rows([h_one_t, branch_t], [grad_qkv, mixed], last_parts, HD)
+    gate.own()
+    token = norm_back(order, core_one, mine, come, flat_tokens, gain_one, grad_middle, True)
+    token += core_swaps(token)
+    token_grad = place(order, core_one, token).reshape(rows, local, width)
+    gate.relay()
+    up_a.own()
     ffn_sent = core_swaps(narrow(order, [(hidden, down_t)], 1))
-    qkv = Rows(h_one_t, grad_qkv, (0, grad_qkv.shape[1] // TILE))
+    if near_pair:
+        down_b.settle()
     ffn_mine = narrow(order, [(hidden, down_t)], 0, ffn_sent)
     ffn_come = chip_swaps(ffn_mine)
-    out = Rows(branch_t, mixed, (0, heads), HD)
-    down_a.settled()
-    gate_a.settled()
-    gate_b.relay()
-    up_a.own()
-    token = norm_back(order, core_one, mine, come, flat_tokens, gain_one, grad_middle, True)
-    token += core_swaps(token)
-    down_b.settle()
-    gate_b.settled()
     up_b.own()
+    (down_grad,) = finish(order, [down_a.result(), down_b.result()], share, units, TILE)
     up_a.relay()
-    token_grad = place(order, core_one, token).reshape(rows, local, width)
-    qkv.own()
-    down_b.placed()
+    last.own()
+    gate_grad, gate_term = finish(order, [gate.result()], share, units, TILE, gate_rows)
     up_b.relay()
-    up_a.settled()
     layer = layer_of(order, middle, ffn_mine, ffn_come)
     layer += core_swaps(layer)
-    out.own()
     if near_pair:
         bias_come = lax.ppermute(bias_sum, "dp", flipped("dp", 0))
         bias_all = bias_add(order, bias_sum, bias_come)
         bias_come = lax.ppermute(bias_all, "seq", flipped("seq", 0))
-    qkv.relay()
+    last.relay()
     layer_out = place(order, core_one, layer).reshape(rows, local, width)
-    up_b.settled()
-    out.relay()
     if near_pair:
         bias_all = bias_add(order, bias_all, bias_come)
         bias_come = lax.ppermute(bias_all, "seq", flipped("seq", 1))
         bias_all = (bias_all + bias_come)[:1]
     else:
         bias_all = lax.psum(bias_sum[:1], ("dp", "seq"))
-    qkv_grad = qkv.result()
-    o_grad = out.result()
-    down_grad = jnp.concatenate([down_a.result(), down_b.result()], axis=1)[:, :units]
-    gate_grad = jnp.concatenate([gate_a.result(), gate_b.result()], axis=1)[:, :units]
-    up_grad = jnp.concatenate([up_a.result(), up_b.result()], axis=1)[:, :units]
-
-    begin = (dp_index * seqs + seq_index) * share
-
-    def rows_of(value):
-        return to_f(lax.dynamic_slice_in_dim(value, begin, share, 0))
-
-    attn_term = jnp.sum(rows_of(weight) * qkv_grad, axis=1)
-    ffn_term = jnp.sum(rows_of(gate_weight) * gate_grad + rows_of(up_weight) * up_grad, axis=1)
+    up_grad, up_term = finish(order, [up_a.result(), up_b.result()], share, units, TILE, up_rows)
+    wide_columns = grad_qkv.shape[1]
+    (last_grad,) = finish(order, [last.result()], share, wide_columns + heads * HD, HD)
+    qkv_grad, o_grad = last_grad[:, :wide_columns], last_grad[:, wide_columns:]
+
+    attn_term = jnp.sum(to_f(rows_of(weight)) * qkv_grad, axis=1)
+    ffn_term = jnp.sum(gate_term + up_term, axis=1)
     columns = heads * HD
     room = -(-share // HD) * HD - share
     terms = jnp.pad(jnp.stack([ffn_term, attn_term]), ((0, 0), (0, room))).reshape(-1, HD)

time: 549 us -> 559 us (1.018)
  waiting for transfers between devices: 174 us -> 192 us
  Pallas kernels: 197 us -> 211 us
  other arithmetic: 19.1 us -> 7.88 us
  local copies, waits for them, and re-layouts: 83.7 us -> 74.8 us
    ppermute x1, waiting for transfers between devices: 0.01 us -> 14.9 us  [body(): bias_come = lax.ppermute(bias_all, 'seq', flipped('seq', 0))]
    pallas_call x52 -> x47, Pallas kernels: 187 us -> 201 us  [__call__(): pl.pallas_call(run, grid_spec=pltpu.PrefetchScalarGridSpec(num_scalar_pre...]
    ppermute x7 -> x5, waiting for transfers between devices: 7.54 us -> 19.5 us  [own(): self.come = lax.ppermute(send, 'seq', flipped('seq', 0))]
    ppermute x1, waiting for transfers between devices: 11.4 us -> 0.01 us  [__init__(): self.come = lax.ppermute(send, 'seq', flipped('seq', 0))]
    unnamed x259 -> x201, local copies, waits for them, and re-layouts: 74.1 us -> 65.6 us
    ppermute x1, waiting for transfers between devices: 8.43 us -> 0.01 us  [settle(): self.final = lax.ppermute(sent, 'dp', flipped('dp', 0))]
    ppermute x22, waiting for transfers between devices: 9.78 us -> 17.3 us  [core_swap(): return lax.ppermute(value, 'tensor', flipped('tensor', 0))]
    ppermute x8 -> x6, waiting for transfers between devices: 71.7 us -> 77.9 us  [relay(): self.last = lax.ppermute(sent, 'seq', flipped('seq', 1))]
  transfers between devices with their start and end apart: 62 -> 56, of which waited for: 27 -> 29; matrix products, arithmetic and copies ran while one was open for 4% -> 2% of each run, Pallas kernels for 28% -> 29%
where the time goes in v4:
time: 559 us; the launch traced here: 558 us
  Pallas kernels  211 us (38%)
  waiting for transfers between devices  192 us (34%)
  local copies, waits for them, and re-layouts  74.8 us (13%)
  starting transfers between devices  70.4 us (13%)
  other arithmetic  7.88 us (1%)
    pallas_call x47, Pallas kernels, __call__(): pl.pallas_call(run, grid_spec=pltpu.PrefetchScalarGridSpec(num_scalar_pre...  201 us
    ppermute x6, waiting for transfers between devices, relay(): self.last = lax.ppermute(sent, 'seq', flipped('seq', 1))  77.9 us
    unnamed x201, local copies, waits for them, and re-layouts  65.6 us
    ppermute x4, waiting for transfers between devices, shifted(): return lax.ppermute(value, 'seq', route)  36.3 us
    ppermute x9, waiting for transfers between devices, chip_swap(): return lax.ppermute(value, 'tensor', flipped('tensor', 1))  23.1 us
    ppermute x5, waiting for transfers between devices, own(): self.come = lax.ppermute(send, 'seq', flipped('seq', 0))  19.5 us
    ppermute x6, starting transfers between devices, relay(): self.last = lax.ppermute(sent, 'seq', flipped('seq', 1))  19.2 us
    ppermute x22, waiting for transfers between devices, core_swap(): return lax.ppermute(value, 'tensor', flipped('tensor', 0))  17.3 us
  transfers between devices with their start and end apart: 56, of which 29 were waited for; matrix products, arithmetic and copies ran while one was open for 2% of the time, Pallas kernels for 29%

profile of v4, /device:TPU:0, one launch (start us, length us, event | category | flops | bytes accessed | tf_op | source)
XLA Modules:
  0.0 557.9 jit_solution(8933249643803768450)
XLA Ops:
  3.9 3.1 fusion.1
  11.4 3.6 first.1
  17.6 6.6 %collective-permute-start = (bf16[2,512,128]{2,1,0:T(8,128)(2,1)S(1)}, bf16[2,512,128]{2,1,0:T(8,128)(2,1)}, u32[]{:S(2)}, u32[]{:S(2)}) collective-permute-start(bf16[2,512,128]{2,1,0:T(8,128)(2,1)S(1)} %bitcast.73), channel_id=1, source_target_pairs={{0,8},{4,12},{1,9},{5,13},{2,10},{6,14},{3,11},{7,15},{16,24},{20,... | collective-permute-start | bytes 786440 | tf_op jit(solution)/shard_map/ppermute | solution.py:66
  24.2 4.2 collective-permute-start.1
  30.1 3.9 collective-permute-done.1.refs_1_.refs_10_
  37.0 6.2 %attend.1 = (bf16[2,512,384]{2,1,0:T(8,128)(2,1)S(1)}, f32[2,2,768]{2,1,0:T(2,128)S(1)}) custom-call(s32[2,2]{1,0:T(2,128)S(1)} %shift-right-logical_maximum_fusion.low_ref.refs_0_, s32[1]{0:T(128)} %bitcast.core_ref.refs_0_.refs_1_, bf16[2,512,384]{2,1,0:T(8,128)(2,1)S(1)} %bitcast.70, s32[2,1,512]{2,1,0:T(1,128)S(1)} %sub.44.start_ref.refs_3_, ...), custom_call_target="tpu_custom_call" | custom-call | flops 8000000 | bytes 4194 | tf_op jit(solution)/shard_map/attend/pallas_call | solution.py:253
  48.9 3.6 narrow.9
  55.8 4.5 constant_dynamic-slice_fusion
  71.5 4.1 copy-done.8
  75.6 9.3 %grad_hidden.1 = (bf16[1024,2240]{1,0:T(8,128)(2,1)S(1)}, f32[8,128]{1,0:T(8,128)S(1)}) custom-call(bf16[1024,1536]{1,0:T(8,128)(2,1)S(1)} %get-tuple-element.156.refs_0_.refs_3_, bf16[2240,1536]{1,0:T(8,128)(2,1)S(1)} %bitcast.57, f32[8,128]{1,0:T(8,128)S(1)} %get-tuple-element.157.refs_2_, bf16[192,2240]{1,0:T(8,128)(2,1)S(1)} %copy-done.40, ...), custom_call_target="tpu_custom_call" | custom-call | flops 7046430 | bytes 15728 | tf_op jit(solution)/shard_map/grad_hidden/pallas_call | solution.py:92
  89.2 5.4 middle.1
  102.4 21.5 %gated.1 = (bf16[1024,2240]{1,0:T(8,128)(2,1)S(1)}, bf16[1024,2240]{1,0:T(8,128)(2,1)S(1)}, bf16[1024,2240]{1,0:T(8,128)(2,1)S(1)}, f32[8,128]{1,0:T(8,128)S(1)}) custom-call(bf16[1024,2240]{1,0:T(8,128)(2,1)S(1)} %copy-done.55, bf16[2240,1536]{1,0:T(8,128)(2,1)} %bitcast.54, bf16[2240,1536]{1,0:T(8,128)(2,1)} %bitcast.79, ...), custom_call_target="tpu_custom_call" | custom-call | flops 14092861 | bytes 31457 | tf_op jit(solution)/shard_map/gated/pallas_call | solution.py:92
  126.0 5.4 share.9
  139.4 4.7 share.10
  149.9 10.1 %narrow.10 = (bf16[256,1536]{1,0:T(8,128)(2,1)S(1)}, bf16[256,1536]{1,0:T(8,128)(2,1)S(1)}, f32[8,128]{1,0:T(8,128)S(1)}) custom-call(bf16[1024,2240]{1,0:T(8,128)(2,1)S(1)} %copy-done.5, bf16[2240,1536]{1,0:T(8,128)(2,1)S(1)} %bitcast.55, bf16[1024,2240]{1,0:T(8,128)(2,1)S(1)} %copy-done.1, bf16[2240,1536]{1,0:T(8,128)(2,1)} %bitcast.80, ...), custom_call_target="tpu_custom_call" | custom-call | flops 7046430 | bytes 19922 | tf_op jit(solution)/shard_map/narrow/pallas_call | solution.py:92
  160.6 10.6 %collective-permute-start.18 = (bf16[768,768]{1,0:T(8,128)(2,1)}, bf16[768,768]{1,0:T(8,128)(2,1)}, u32[]{:S(2)}, u32[]{:S(2)}) collective-permute-start(bf16[768,768]{1,0:T(8,128)(2,1)} %get-tuple-element.185), channel_id=1, source_target_pairs={{0,4},{4,0},{8,12},{12,8},{1,5},{5,1},{9,13},{13,9},{2,6},{6,2},{1... | collective-permute-start | bytes 3538952 | tf_op jit(solution)/shard_map/ppermute | solution.py:1160
  171.2 10.9 %narrow.11 = (bf16[256,1536]{1,0:T(8,128)(2,1)}, bf16[256,1536]{1,0:T(8,128)(2,1)}, f32[8,128]{1,0:T(8,128)S(1)}) custom-call(bf16[1024,2240]{1,0:T(8,128)(2,1)S(1)} %copy-done.5, bf16[2240,1536]{1,0:T(8,128)(2,1)S(1)} %bitcast.56, bf16[1024,2240]{1,0:T(8,128)(2,1)S(1)} %copy-done.1, bf16[2240,1536]{1,0:T(8,128)(2,1)} %bitcast.81, ...), custom_call_target="tpu_custom_call" | custom-call | flops 7046430 | bytes 19922 | tf_op jit(solution)/shard_map/narrow/pallas_call | solution.py:92
  184.1 4.2 turn.4
  190.8 14.2 %share.11 = (bf16[768,2304]{1,0:T(8,128)(2,1)}, bf16[768,1536]{1,0:T(8,128)(2,1)}, bf16[768,768]{1,0:T(8,128)(2,1)}, f32[8,128]{1,0:T(8,128)S(1)}) custom-call(s32[1]{0:T(128)} %bitcast.19.refs_0_, s32[1]{0:T(128)} %constant.60.clone.1.refs_1_.refs_0_, bf16[1536,1024]{1,0:T(8,128)(2,1)S(1)} %get-tuple-element.176.refs_2_, bf16[1024,2240]{1,0:T(8,128)(2,1)S(1)} %copy-done.6, ...), custom_call_target="tpu_custom_call" | custom-call | flops 7247757 | bytes 18087 | tf_op jit(solution)/shard_map/share/pallas_call | solution.py:92
  206.3 6.8 %share.12 = (bf16[384,1536]{1,0:T(8,128)(2,1)S(1)}, bf16[384,1536]{1,0:T(8,128)(2,1)S(1)}, f32[8,128]{1,0:T(8,128)S(1)}) custom-call(s32[1]{0:T(128)} %bitcast.10.refs_0_, s32[4]{0:T(128)S(1)} %pad_add_fusion.refs_1_, bf16[1536,1024]{1,0:T(8,128)(2,1)S(1)} %copy-done.13, bf16[1024,2240]{1,0:T(8,128)(2,1)S(1)} %bitcast.51, ...), custom_call_target="tpu_custom_call" | custom-call | flops 2415919 | bytes 7077 | tf_op jit(solution)/shard_map/share/pallas_call | solution.py:92
  215.2 3.3 collective-permute-done.16.refs_7_
  220.4 4.1 norm_back.2
  231.5 8.8 %attend_back.1 = (bf16[2,512,384]{2,1,0:T(8,128)(2,1)S(1)}, bf16[2,1536,128]{2,1,0:T(8,128)(2,1)S(1)}, bf16[1,1536,128]{2,1,0:T(8,128)(2,1)S(1)}, bf16[1,1536,128]{2,1,0:T(8,128)(2,1)S(1)}, f32[8,128]{1,0:T(8,128)S(1)}) custom-call(s32[2,2]{1,0:T(2,128)S(1)} %shift-right-logical_maximum_fusion.low_ref.refs_0_, s32[1]{0:T(128)} %bitcast.core_ref.refs_0_.refs_1_, ...), custom_call_target="tpu_custom_call" | custom-call | flops 20000000 | bytes 6291 | tf_op jit(solution)/shard_map/attend_back/pallas_call | solution.py:92
  240.9 13.3 %collective-permute-start.24 = (bf16[384,768]{1,0:T(8,128)(2,1)S(1)}, bf16[384,768]{1,0:T(8,128)(2,1)S(1)}, u32[]{:S(2)}, u32[]{:S(2)}) collective-permute-start(bf16[384,768]{1,0:T(8,128)(2,1)S(1)} %copy-done.78), channel_id=1, source_target_pairs={{0,8},{4,12},{8,0},{12,4},{1,9},{5,13},{9,1},{13,5},{2,10},{6,14},... | collective-permute-start | bytes 1769480 | tf_op jit(solution)/shard_map/ppermute | solution.py:1145
  261.6 17.2 %collective-permute-done.24.refs_3_ = bf16[384,768]{1,0:T(8,128)(2,1)S(1)} collective-permute-done((bf16[384,768]{1,0:T(8,128)(2,1)S(1)}, bf16[384,768]{1,0:T(8,128)(2,1)S(1)}, u32[]{:S(2)}, u32[]{:S(2)}) %collective-permute-start.24) | collective-permute-done | bytes 589856 | tf_op jit(solution)/shard_map/ppermute | solution.py:1145
  282.7 28.2 %collective-permute-done.25.refs_5_ = bf16[2,512,128]{2,1,0:T(8,128)(2,1)S(1)} collective-permute-done((bf16[2,512,128]{2,1,0:T(8,128)(2,1)S(1)}, bf16[2,512,128]{2,1,0:T(8,128)(2,1)S(1)}, u32[]{:S(2)}, u32[]{:S(2)}) %collective-permute-start.25) | collective-permute-done | bytes 262176 | tf_op jit(solution)/shard_map/ppermute | solution.py:66
  318.4 3.4 narrow.13
  329.1 5.4 share.13
  334.5 9.7 %share.14 = (bf16[384,2304]{1,0:T(8,128)(2,1)}, bf16[384,2304]{1,0:T(8,128)(2,1)S(1)}, f32[8,128]{1,0:T(8,128)S(1)}) custom-call(s32[1]{0:T(128)} %bitcast.10.refs_0_, s32[4]{0:T(128)S(1)} %pad_add_fusion.refs_1_, bf16[1536,1024]{1,0:T(8,128)(2,1)S(1)} %get-tuple-element.176.refs_2_, bf16[1024,2240]{1,0:T(8,128)(2,1)S(1)} %bitcast.53, ...), custom_call_target="tpu_custom_call" | custom-call | flops 3623878 | bytes 9830 | tf_op jit(solution)/shard_map/share/pallas_call | solution.py:92
  344.1 14.4 %collective-permute-done.31.refs_7_ = bf16[256,1536]{1,0:T(8,128)(2,1)} collective-permute-done((bf16[256,1536]{1,0:T(8,128)(2,1)}, bf16[256,1536]{1,0:T(8,128)(2,1)}, u32[]{:S(2)}, u32[]{:S(2)}) %collective-permute-start.31) | collective-permute-done | bytes 786464 | tf_op jit(solution)/shard_map/ppermute | solution.py:52
  360.5 4.1 norm_back.3
  374.8 9.4 %collective-permute-done.29.refs_1_ = bf16[384,2304]{1,0:T(8,128)(2,1)S(1)} collective-permute-done((bf16[384,2304]{1,0:T(8,128)(2,1)}, bf16[384,2304]{1,0:T(8,128)(2,1)S(1)}, u32[]{:S(2)}, u32[]{:S(2)}) %collective-permute-start.29) | collective-permute-done | bytes 1769504 | tf_op jit(solution)/shard_map/ppermute | solution.py:1140
  388.0 7.6 %share.15 = (bf16[384,1536]{1,0:T(8,128)(2,1)}, bf16[384,1536]{1,0:T(8,128)(2,1)S(1)}, f32[8,128]{1,0:T(8,128)S(1)}) custom-call(s32[1]{0:T(128)} %bitcast.10.refs_0_, s32[4]{0:T(128)S(1)} %pad_add_fusion.refs_1_, bf16[1536,1024]{1,0:T(8,128)(2,1)S(1)} %get-tuple-element.176.refs_2_, bf16[1024,2240]{1,0:T(8,128)(2,1)S(1)} %copy-done.1, ...), custom_call_target="tpu_custom_call" | custom-call | flops 2415919 | bytes 7077 | tf_op jit(solution)/shard_map/share/pallas_call | solution.py:92
  395.6 5.3 narrow.14
  408.7 6.1 %narrow.15 = (bf16[256,1536]{1,0:T(8,128)(2,1)}, bf16[256,1536]{1,0:T(8,128)(2,1)}, f32[8,128]{1,0:T(8,128)S(1)}) custom-call(bf16[1024,2240]{1,0:T(8,128)(2,1)S(1)} %bitcast.51, bf16[2240,1536]{1,0:T(8,128)(2,1)S(1)} %bitcast.61, bf16[256,1536]{1,0:T(8,128)(2,1)S(1)} %collective-permute-done.34.refs_2_, ...), custom_call_target="tpu_custom_call" | custom-call | flops 3523215 | bytes 10747 | tf_op jit(solution)/shard_map/narrow/pallas_call | solution.py:92
  414.7 25.8 %collective-permute-done.43.refs_2_ = bf16[192,1536]{1,0:T(8,128)(2,1)S(1)} collective-permute-done((bf16[192,1536]{1,0:T(8,128)(2,1)S(1)}, bf16[192,1536]{1,0:T(8,128)(2,1)S(1)}, u32[]{:S(2)}, u32[]{:S(2)}) %collective-permute-start.43) | collective-permute-done | bytes 589856 | tf_op jit(solution)/shard_map/ppermute | solution.py:1145
  442.6 4.2 share.16
  448.1 3.8 finish.4
  453.4 5.8 %share.17 = (bf16[384,896]{1,0:T(8,128)(2,1)S(1)}, bf16[384,896]{1,0:T(8,128)(2,1)S(1)}, f32[8,128]{1,0:T(8,128)S(1)}) custom-call(s32[1]{0:T(128)} %bitcast.10.refs_0_, s32[4]{0:T(128)S(1)} %pad_add_fusion.refs_1_, bf16[1536,1024]{1,0:T(8,128)(2,1)S(1)} %copy-done.26, bf16[1536,1024]{1,0:T(8,128)(2,1)S(1)} %copy-done.29, bf16[1024,512]{1,0:T(8,128)(2,1)S(1)} %copy-done.20, ...), custom_call_target="tpu_custom_call" | custom-call | flops 1409286 | bytes 4784 | tf_op jit(solution)/shard_map/share/pallas_call | solution.py:92
  460.1 9.1 %collective-permute-done.40.refs_2_ = bf16[192,2304]{1,0:T(8,128)(2,1)} collective-permute-done((bf16[192,2304]{1,0:T(8,128)(2,1)}, bf16[192,2304]{1,0:T(8,128)(2,1)}, u32[]{:S(2)}, u32[]{:S(2)}) %collective-permute-start.40) | collective-permute-done | bytes 884768 | tf_op jit(solution)/shard_map/ppermute | solution.py:1145
  469.2 6.2 %finish.5 = (f32[192,2240]{1,0:T(8,128)}, f32[192,128]{1,0:T(8,128)S(1)}, f32[8,128]{1,0:T(8,128)S(1)}) custom-call(bf16[384,2304]{1,0:T(8,128)(2,1)S(1)} %copy-done.43, bf16[384,2304]{1,0:T(8,128)(2,1)S(1)} %copy-done.46, bf16[192,2304]{1,0:T(8,128)(2,1)} %collective-permute-done.40.refs_2_, bf16[192,2240]{1,0:T(8,128)(2,1)S(1)} %copy-done.41, ...), custom_call_target="tpu_custom_call" | custom-call | bytes 6021 | tf_op jit(solution)/shard_map/finish/pallas_call | solution.py:92
  475.4 4.9 collective-permute-done.39.refs_1_.refs_4_
  484.4 3.5 collective-permute-done.48.refs_1_
  487.8 5.1 collective-permute-done.47.refs_1_
  498.2 14.9 %collective-permute-done.52.refs_1_ = f32[8,512]{1,0:T(8,128)S(1)} collective-permute-done((f32[8,512]{1,0:T(8,128)S(1)}, f32[8,512]{1,0:T(8,128)S(1)}, u32[]{:S(2)}, u32[]{:S(2)}) %collective-permute-start.52) | collective-permute-done | bytes 16416 | tf_op jit(solution)/shard_map/ppermute | solution.py:1263
  513.9 25.8 %collective-permute-done.51.refs_5_ = bf16[192,768]{1,0:T(8,128)(2,1)S(1)} collective-permute-done((bf16[192,768]{1,0:T(8,128)(2,1)S(1)}, bf16[192,768]{1,0:T(8,128)(2,1)S(1)}, u32[]{:S(2)}, u32[]{:S(2)}) %collective-permute-start.51) | collective-permute-done | bytes 294944 | tf_op jit(solution)/shard_map/ppermute | solution.py:1145
  539.7 4.0 finish.6
  549.3 4.8 collective-permute-done.55
  (367 shorter events, 154.8 us)
Async XLA Ops:
  17.6 12.5 %collective-permute-start = (bf16[2,512,128]{2,1,0:T(8,128)(2,1)S(1)}, bf16[2,512,128]{2,1,0:T(8,128)(2,1)}, u32[]{:S(2)}, u32[]{:S(2)}) collective-permute-start(bf16[2,512,128]{2,1,0:T(8,128)(2,1)S(1)} %bitcast.73), channel_id=1, source_target_pairs={{0,8},{4,12},{1,9},{5,13},{2,10},{6,14},{3,11},{7,15},{16,24},{20,... | collective-permute-start | bytes 786440 | tf_op jit(solution)/shard_map/ppermute | solution.py:66
  24.2 9.8 %collective-permute-start.1 = (bf16[2,512,128]{2,1,0:T(8,128)(2,1)S(1)}, bf16[2,512,128]{2,1,0:T(8,128)(2,1)}, u32[]{:S(2)}, u32[]{:S(2)}) collective-permute-start(bf16[2,512,128]{2,1,0:T(8,128)(2,1)S(1)} %bitcast.74), channel_id=1, source_target_pairs={{0,4},{4,8},{8,12},{1,5},{5,9},{9,13},{2,6},{6,10},{10,14},{3,7},{... | collective-permute-start | bytes 786440 | tf_op jit(solution)/shard_map/ppermute | solution.py:66
  28.4 5.8 %collective-permute-start.4 = (bf16[2,512,128]{2,1,0:T(8,128)(2,1)S(1)}, bf16[2,512,128]{2,1,0:T(8,128)(2,1)}, u32[]{:S(2)}, u32[]{:S(2)}) collective-permute-start(bf16[2,512,128]{2,1,0:T(8,128)(2,1)S(1)} %bitcast.75), channel_id=1, source_target_pairs={{0,1},{1,0},{2,3},{3,2},{4,5},{5,4},{6,7},{7,6},{8,9},{9,8},{10,11... | collective-permute-start | bytes 786440 | tf_op jit(solution)/shard_map/ppermute | solution.py:48
  30.1 4.1 collective-permute-start.2
  52.5 36.2 %collective-permute-start.7 = (bf16[256,1536]{1,0:T(8,128)(2,1)}, bf16[256,1536]{1,0:T(8,128)(2,1)}, u32[]{:S(2)}, u32[]{:S(2)}) collective-permute-start(bf16[256,1536]{1,0:T(8,128)(2,1)} %get-tuple-element.152.refs_3_), channel_id=1, source_target_pairs={{0,2},{1,3},{2,0},{3,1},{4,6},{5,7},{6,4},{7,5},{8,10},{9,11},{10,... | collective-permute-start | bytes 2359304 | tf_op jit(solution)/shard_map/ppermute | solution.py:52
  54.0 35.3 %collective-permute-start.8 = (bf16[256,1536]{1,0:T(8,128)(2,1)}, bf16[256,1536]{1,0:T(8,128)(2,1)}, u32[]{:S(2)}, u32[]{:S(2)}) collective-permute-start(bf16[256,1536]{1,0:T(8,128)(2,1)} %get-tuple-element.153.refs_4_), channel_id=1, source_target_pairs={{0,2},{1,3},{2,0},{3,1},{4,6},{5,7},{6,4},{7,5},{8,10},{9,11},{10,... | collective-permute-start | bytes 2359304 | tf_op jit(solution)/shard_map/ppermute | solution.py:52
  96.3 3.7 collective-permute-start.9
  133.6 72.6 %collective-permute-start.17 = (bf16[768,1536]{1,0:T(8,128)(2,1)}, bf16[768,1536]{1,0:T(8,128)(2,1)}, u32[]{:S(2)}, u32[]{:S(2)}) collective-permute-start(bf16[768,1536]{1,0:T(8,128)(2,1)} %get-tuple-element.183), channel_id=1, source_target_pairs={{0,16},{16,0},{1,17},{17,1},{2,18},{18,2},{3,19},{19,3},{4,20},{20... | collective-permute-start | bytes 7077896 | tf_op jit(solution)/shard_map/ppermute | solution.py:1135
  160.0 11.1 %collective-permute-start.11 = (bf16[256,1536]{1,0:T(8,128)(2,1)S(1)}, bf16[256,1536]{1,0:T(8,128)(2,1)S(1)}, u32[]{:S(2)}, u32[]{:S(2)}) collective-permute-start(bf16[256,1536]{1,0:T(8,128)(2,1)S(1)} %get-tuple-element.172), channel_id=1, source_target_pairs={{0,1},{1,0},{2,3},{3,2},{4,5},{5,4},{6,7},{7,6},{8,9},{9,8},{10,11... | collective-permute-start | bytes 2359304 | tf_op jit(solution)/shard_map/ppermute | solution.py:48
  160.1 11.1 %collective-permute-start.12 = (bf16[256,1536]{1,0:T(8,128)(2,1)S(1)}, bf16[256,1536]{1,0:T(8,128)(2,1)S(1)}, u32[]{:S(2)}, u32[]{:S(2)}) collective-permute-start(bf16[256,1536]{1,0:T(8,128)(2,1)S(1)} %get-tuple-element.173), channel_id=1, source_target_pairs={{0,1},{1,0},{2,3},{3,2},{4,5},{5,4},{6,7},{7,6},{8,9},{9,8},{10,11... | collective-permute-start | bytes 2359304 | tf_op jit(solution)/shard_map/ppermute | solution.py:48
  160.6 44.5 %collective-permute-start.18 = (bf16[768,768]{1,0:T(8,128)(2,1)}, bf16[768,768]{1,0:T(8,128)(2,1)}, u32[]{:S(2)}, u32[]{:S(2)}) collective-permute-start(bf16[768,768]{1,0:T(8,128)(2,1)} %get-tuple-element.185), channel_id=1, source_target_pairs={{0,4},{4,0},{8,12},{12,8},{1,5},{5,1},{9,13},{13,9},{2,6},{6,2},{1... | collective-permute-start | bytes 3538952 | tf_op jit(solution)/shard_map/ppermute | solution.py:1160
  182.1 33.1 %collective-permute-start.15 = (bf16[256,1536]{1,0:T(8,128)(2,1)}, bf16[256,1536]{1,0:T(8,128)(2,1)}, u32[]{:S(2)}, u32[]{:S(2)}) collective-permute-start(bf16[256,1536]{1,0:T(8,128)(2,1)} %get-tuple-element.181.refs_4_), channel_id=1, source_target_pairs={{0,2},{1,3},{2,0},{3,1},{4,6},{5,7},{6,4},{7,5},{8,10},{9,11},{10,... | collective-permute-start | bytes 2359304 | tf_op jit(solution)/shard_map/ppermute | solution.py:52
  183.6 34.9 %collective-permute-start.16 = (bf16[256,1536]{1,0:T(8,128)(2,1)}, bf16[256,1536]{1,0:T(8,128)(2,1)}, u32[]{:S(2)}, u32[]{:S(2)}) collective-permute-start(bf16[256,1536]{1,0:T(8,128)(2,1)} %get-tuple-element.182.refs_5_), channel_id=1, source_target_pairs={{0,2},{1,3},{2,0},{3,1},{4,6},{5,7},{6,4},{7,5},{8,10},{9,11},{10,... | collective-permute-start | bytes 2359304 | tf_op jit(solution)/shard_map/ppermute | solution.py:52
  205.0 129.5 %collective-permute-start.14 = (bf16[768,2304]{1,0:T(8,128)(2,1)}, bf16[768,2304]{1,0:T(8,128)(2,1)}, u32[]{:S(2)}, u32[]{:S(2)}) collective-permute-start(bf16[768,2304]{1,0:T(8,128)(2,1)} %get-tuple-element.179), channel_id=1, source_target_pairs={{0,16},{16,0},{1,17},{17,1},{2,18},{18,2},{3,19},{19,3},{4,20},{20... | collective-permute-start | bytes 10616840 | tf_op jit(solution)/shard_map/ppermute | solution.py:1135
  226.2 3.4 collective-permute-start.20
  240.3 17.0 %collective-permute-start.21 = (bf16[1,1536,128]{2,1,0:T(8,128)(2,1)S(1)}, bf16[1,1536,128]{2,1,0:T(8,128)(2,1)S(1)}, u32[]{:S(2)}, u32[]{:S(2)}) collective-permute-start(bf16[1,1536,128]{2,1,0:T(8,128)(2,1)S(1)} %get-tuple-element.199), channel_id=1, source_target_pairs={{0,1},{1,0},{2,3},{3,2},{4,5},{5,4},{6,7},{7,6},{8,9},{9,8},{10,11... | collective-permute-start | bytes 1179656 | tf_op jit(solution)/shard_map/ppermute | solution.py:48
  240.5 16.8 %collective-permute-start.22 = (bf16[1,1536,128]{2,1,0:T(8,128)(2,1)S(1)}, bf16[1,1536,128]{2,1,0:T(8,128)(2,1)S(1)}, u32[]{:S(2)}, u32[]{:S(2)}) collective-permute-start(bf16[1,1536,128]{2,1,0:T(8,128)(2,1)S(1)} %get-tuple-element.200), channel_id=1, source_target_pairs={{0,1},{1,0},{2,3},{3,2},{4,5},{5,4},{6,7},{7,6},{8,9},{9,8},{10,11... | collective-permute-start | bytes 1179656 | tf_op jit(solution)/shard_map/ppermute | solution.py:48
  240.9 37.9 %collective-permute-start.24 = (bf16[384,768]{1,0:T(8,128)(2,1)S(1)}, bf16[384,768]{1,0:T(8,128)(2,1)S(1)}, u32[]{:S(2)}, u32[]{:S(2)}) collective-permute-start(bf16[384,768]{1,0:T(8,128)(2,1)S(1)} %copy-done.78), channel_id=1, source_target_pairs={{0,8},{4,12},{8,0},{12,4},{1,9},{5,13},{9,1},{13,5},{2,10},{6,14},... | collective-permute-start | bytes 1769480 | tf_op jit(solution)/shard_map/ppermute | solution.py:1145
  257.6 23.6 %collective-permute-start.23 = (bf16[2,512,128]{2,1,0:T(8,128)(2,1)S(1)}, bf16[2,512,128]{2,1,0:T(8,128)(2,1)S(1)}, u32[]{:S(2)}, u32[]{:S(2)}) collective-permute-start(bf16[2,512,128]{2,1,0:T(8,128)(2,1)S(1)} %get-tuple-element.204), channel_id=1, source_target_pairs={{4,0},{8,4},{12,8},{5,1},{9,5},{13,9},{6,2},{10,6},{14,10},{7,3},{... | collective-permute-start | bytes 786440 | tf_op jit(solution)/shard_map/ppermute | solution.py:66
  258.9 56.6 %collective-permute-start.28 = (bf16[384,1536]{1,0:T(8,128)(2,1)S(1)}, bf16[384,1536]{1,0:T(8,128)(2,1)S(1)}, u32[]{:S(2)}, u32[]{:S(2)}) collective-permute-start(bf16[384,1536]{1,0:T(8,128)(2,1)S(1)} %copy-done.74), channel_id=1, source_target_pairs={{0,4},{4,0},{8,12},{12,8},{1,5},{5,1},{9,13},{13,9},{2,6},{6,2},{1... | collective-permute-start | bytes 3538952 | tf_op jit(solution)/shard_map/ppermute | solution.py:1140
  281.3 29.7 %collective-permute-start.25 = (bf16[2,512,128]{2,1,0:T(8,128)(2,1)S(1)}, bf16[2,512,128]{2,1,0:T(8,128)(2,1)S(1)}, u32[]{:S(2)}, u32[]{:S(2)}) collective-permute-start(bf16[2,512,128]{2,1,0:T(8,128)(2,1)S(1)} %get-tuple-element.207), channel_id=1, source_target_pairs={{4,0},{8,4},{12,8},{5,1},{9,5},{13,9},{6,2},{10,6},{14,10},{7,3},{... | collective-permute-start | bytes 786440 | tf_op jit(solution)/shard_map/ppermute | solution.py:66
  315.0 3.4 collective-permute-start.27
  321.8 22.3 %collective-permute-start.30 = (bf16[256,1536]{1,0:T(8,128)(2,1)}, bf16[256,1536]{1,0:T(8,128)(2,1)}, u32[]{:S(2)}, u32[]{:S(2)}) collective-permute-start(bf16[256,1536]{1,0:T(8,128)(2,1)} %get-tuple-element.222.refs_4_), channel_id=1, source_target_pairs={{0,2},{1,3},{2,0},{3,1},{4,6},{5,7},{6,4},{7,5},{8,10},{9,11},{10,... | collective-permute-start | bytes 2359304 | tf_op jit(solution)/shard_map/ppermute | solution.py:52
  323.4 35.2 %collective-permute-start.31 = (bf16[256,1536]{1,0:T(8,128)(2,1)}, bf16[256,1536]{1,0:T(8,128)(2,1)}, u32[]{:S(2)}, u32[]{:S(2)}) collective-permute-start(bf16[256,1536]{1,0:T(8,128)(2,1)} %get-tuple-element.223.refs_5_), channel_id=1, source_target_pairs={{0,2},{1,3},{2,0},{3,1},{4,6},{5,7},{6,4},{7,5},{8,10},{9,11},{10,... | collective-permute-start | bytes 2359304 | tf_op jit(solution)/shard_map/ppermute | solution.py:52
  323.9 64.2 %collective-permute-start.13 = (bf16[768,1536]{1,0:T(8,128)(2,1)}, bf16[768,1536]{1,0:T(8,128)(2,1)}, u32[]{:S(2)}, u32[]{:S(2)}) collective-permute-start(bf16[768,1536]{1,0:T(8,128)(2,1)} %get-tuple-element.178), channel_id=1, source_target_pairs={{0,16},{16,0},{1,17},{17,1},{2,18},{18,2},{3,19},{19,3},{4,20},{20... | collective-permute-start | bytes 7077896 | tf_op jit(solution)/shard_map/ppermute | solution.py:1135
  344.1 40.0 %collective-permute-start.29 = (bf16[384,2304]{1,0:T(8,128)(2,1)}, bf16[384,2304]{1,0:T(8,128)(2,1)S(1)}, u32[]{:S(2)}, u32[]{:S(2)}) collective-permute-start(bf16[384,2304]{1,0:T(8,128)(2,1)} %get-tuple-element.220), channel_id=1, source_target_pairs={{0,4},{4,0},{8,12},{12,8},{1,5},{5,1},{9,13},{13,9},{2,6},{6,2},{1... | collective-permute-start | bytes 5308424 | tf_op jit(solution)/shard_map/ppermute | solution.py:1140
  364.6 3.5 collective-permute-start.32
  365.8 4.5 collective-permute-start.33
  366.3 35.9 %collective-permute-start.38 = (bf16[768,768]{1,0:T(8,128)(2,1)}, bf16[768,768]{1,0:T(8,128)(2,1)}, u32[]{:S(2)}, u32[]{:S(2)}) collective-permute-start(bf16[768,768]{1,0:T(8,128)(2,1)} %get-tuple-element.237), channel_id=1, source_target_pairs={{0,16},{16,0},{1,17},{17,1},{2,18},{18,2},{3,19},{19,3},{4,20},{20... | collective-permute-start | bytes 3538952 | tf_op jit(solution)/shard_map/ppermute | solution.py:1135
  401.0 45.8 %collective-permute-start.42 = (bf16[384,1536]{1,0:T(8,128)(2,1)}, bf16[384,1536]{1,0:T(8,128)(2,1)S(1)}, u32[]{:S(2)}, u32[]{:S(2)}) collective-permute-start(bf16[384,1536]{1,0:T(8,128)(2,1)} %get-tuple-element.244), channel_id=1, source_target_pairs={{0,4},{4,0},{8,12},{12,8},{1,5},{5,1},{9,13},{13,9},{2,6},{6,2},{1... | collective-permute-start | bytes 3538952 | tf_op jit(solution)/shard_map/ppermute | solution.py:1140
  401.4 4.4 collective-permute-start.35
  401.5 50.5 %collective-permute-start.41 = (bf16[768,896]{1,0:T(8,128)(2,1)}, bf16[768,896]{1,0:T(8,128)(2,1)S(1)}, u32[]{:S(2)}, u32[]{:S(2)}) collective-permute-start(bf16[768,896]{1,0:T(8,128)(2,1)} %get-tuple-element.242), channel_id=1, source_target_pairs={{0,16},{16,0},{1,17},{17,1},{2,18},{18,2},{3,19},{19,3},{4,20},{20... | collective-permute-start | bytes 4128776 | tf_op jit(solution)/shard_map/ppermute | solution.py:1135
  402.2 38.4 %collective-permute-start.43 = (bf16[192,1536]{1,0:T(8,128)(2,1)S(1)}, bf16[192,1536]{1,0:T(8,128)(2,1)S(1)}, u32[]{:S(2)}, u32[]{:S(2)}) collective-permute-start(bf16[192,1536]{1,0:T(8,128)(2,1)S(1)} %copy-done.76), channel_id=1, source_target_pairs={{0,8},{4,12},{8,0},{12,4},{1,9},{5,13},{9,1},{13,5},{2,10},{6,14},... | collective-permute-start | bytes 1769480 | tf_op jit(solution)/shard_map/ppermute | solution.py:1145
  404.2 37.8 %collective-permute-start.44 = (bf16[192,768]{1,0:T(8,128)(2,1)S(1)}, bf16[192,768]{1,0:T(8,128)(2,1)S(1)}, u32[]{:S(2)}, u32[]{:S(2)}) collective-permute-start(bf16[192,768]{1,0:T(8,128)(2,1)S(1)} %get-tuple-element.247), channel_id=1, source_target_pairs={{0,16},{16,0},{1,17},{17,1},{2,18},{18,2},{3,19},{19,3},{4,20},{20... | collective-permute-start | bytes 884744 | tf_op jit(solution)/shard_map/ppermute | solution.py:1167
  405.8 63.4 %collective-permute-start.40 = (bf16[192,2304]{1,0:T(8,128)(2,1)}, bf16[192,2304]{1,0:T(8,128)(2,1)}, u32[]{:S(2)}, u32[]{:S(2)}) collective-permute-start(bf16[192,2304]{1,0:T(8,128)(2,1)} %get-tuple-element.241), channel_id=1, source_target_pairs={{0,8},{4,12},{8,0},{12,4},{1,9},{5,13},{9,1},{13,5},{2,10},{6,14},... | collective-permute-start | bytes 2654216 | tf_op jit(solution)/shard_map/ppermute | solution.py:1145
  440.6 39.8 %collective-permute-start.36 = (bf16[256,1536]{1,0:T(8,128)(2,1)}, bf16[256,1536]{1,0:T(8,128)(2,1)S(1)}, u32[]{:S(2)}, u32[]{:S(2)}) collective-permute-start(bf16[256,1536]{1,0:T(8,128)(2,1)} %get-tuple-element.235.refs_1_), channel_id=1, source_target_pairs={{0,2},{1,3},{2,0},{3,1},{4,6},{5,7},{6,4},{7,5},{8,10},{9,11},{10,... | collective-permute-start | bytes 2359304 | tf_op jit(solution)/shard_map/ppermute | solution.py:52
  442.1 38.3 %collective-permute-start.37 = (bf16[256,1536]{1,0:T(8,128)(2,1)}, bf16[256,1536]{1,0:T(8,128)(2,1)S(1)}, u32[]{:S(2)}, u32[]{:S(2)}) collective-permute-start(bf16[256,1536]{1,0:T(8,128)(2,1)} %get-tuple-element.236.refs_2_), channel_id=1, source_target_pairs={{0,2},{1,3},{2,0},{3,1},{4,6},{5,7},{6,4},{7,5},{8,10},{9,11},{10,... | collective-permute-start | bytes 2359304 | tf_op jit(solution)/shard_map/ppermute | solution.py:52
  446.9 33.5 %collective-permute-start.39 = (bf16[384,768]{1,0:T(8,128)(2,1)S(1)}, bf16[384,768]{1,0:T(8,128)(2,1)S(1)}, u32[]{:S(2)}, u32[]{:S(2)}) collective-permute-start(bf16[384,768]{1,0:T(8,128)(2,1)S(1)} %get-tuple-element.240), channel_id=1, source_target_pairs={{0,4},{4,0},{8,12},{12,8},{1,5},{5,1},{9,13},{13,9},{2,6},{6,2},{1... | collective-permute-start | bytes 1769480 | tf_op jit(solution)/shard_map/ppermute | solution.py:1140
  459.2 33.8 %collective-permute-start.47 = (bf16[384,896]{1,0:T(8,128)(2,1)S(1)}, bf16[384,896]{1,0:T(8,128)(2,1)S(1)}, u32[]{:S(2)}, u32[]{:S(2)}) collective-permute-start(bf16[384,896]{1,0:T(8,128)(2,1)S(1)} %get-tuple-element.257), channel_id=1, source_target_pairs={{0,4},{4,0},{8,12},{12,8},{1,5},{5,1},{9,13},{13,9},{2,6},{6,2},{1... | collective-permute-start | bytes 2064392 | tf_op jit(solution)/shard_map/ppermute | solution.py:1140
  483.5 12.5 %collective-permute-start.45 = (bf16[256,1536]{1,0:T(8,128)(2,1)S(1)}, bf16[256,1536]{1,0:T(8,128)(2,1)S(1)}, u32[]{:S(2)}, u32[]{:S(2)}) collective-permute-start(bf16[256,1536]{1,0:T(8,128)(2,1)S(1)} %get-tuple-element.254.refs_1_), channel_id=1, source_target_pairs={{0,1},{1,0},{2,3},{3,2},{4,5},{5,4},{6,7},{7,6},{8,9},{9,8},{10,11... | collective-permute-start | bytes 2359304 | tf_op jit(solution)/shard_map/ppermute | solution.py:48
  483.6 12.5 %collective-permute-start.46 = (bf16[256,1536]{1,0:T(8,128)(2,1)S(1)}, bf16[256,1536]{1,0:T(8,128)(2,1)S(1)}, u32[]{:S(2)}, u32[]{:S(2)}) collective-permute-start(bf16[256,1536]{1,0:T(8,128)(2,1)S(1)} %get-tuple-element.255.refs_2_), channel_id=1, source_target_pairs={{0,1},{1,0},{2,3},{3,2},{4,5},{5,4},{6,7},{7,6},{8,9},{9,8},{10,11... | collective-permute-start | bytes 2359304 | tf_op jit(solution)/shard_map/ppermute | solution.py:48
  484.1 55.7 %collective-permute-start.50 = (bf16[192,1536]{1,0:T(8,128)(2,1)S(1)}, bf16[192,1536]{1,0:T(8,128)(2,1)S(1)}, u32[]{:S(2)}, u32[]{:S(2)}) collective-permute-start(bf16[192,1536]{1,0:T(8,128)(2,1)S(1)} %get-tuple-element.265), channel_id=1, source_target_pairs={{0,8},{4,12},{8,0},{12,4},{1,9},{5,13},{9,1},{13,5},{2,10},{6,14},... | collective-permute-start | bytes 1769480 | tf_op jit(solution)/shard_map/ppermute | solution.py:1145
  484.1 3.7 collective-permute-start.48
  493.1 50.7 %collective-permute-start.49 = (bf16[192,896]{1,0:T(8,128)(2,1)S(1)}, bf16[192,896]{1,0:T(8,128)(2,1)S(1)}, u32[]{:S(2)}, u32[]{:S(2)}) collective-permute-start(bf16[192,896]{1,0:T(8,128)(2,1)S(1)} %get-tuple-element.264), channel_id=1, source_target_pairs={{0,8},{4,12},{8,0},{12,4},{1,9},{5,13},{9,1},{13,5},{2,10},{6,14},... | collective-permute-start | bytes 1032200 | tf_op jit(solution)/shard_map/ppermute | solution.py:1145
  493.1 46.6 %collective-permute-start.51 = (bf16[192,768]{1,0:T(8,128)(2,1)S(1)}, bf16[192,768]{1,0:T(8,128)(2,1)S(1)}, u32[]{:S(2)}, u32[]{:S(2)}) collective-permute-start(bf16[192,768]{1,0:T(8,128)(2,1)S(1)} %get-tuple-element.266), channel_id=1, source_target_pairs={{0,8},{4,12},{8,0},{12,4},{1,9},{5,13},{9,1},{13,5},{2,10},{6,14},... | collective-permute-start | bytes 884744 | tf_op jit(solution)/shard_map/ppermute | solution.py:1145
  496.0 17.1 %collective-permute-start.52 = (f32[8,512]{1,0:T(8,128)S(1)}, f32[8,512]{1,0:T(8,128)S(1)}, u32[]{:S(2)}, u32[]{:S(2)}) collective-permute-start(f32[8,512]{1,0:T(8,128)S(1)} %get-tuple-element.267.refs_0_), channel_id=1, source_target_pairs={{0,4},{4,0},{8,12},{12,8},{1,5},{5,1},{9,13},{13,9},{2,6},{6,2},{1... | collective-permute-start | bytes 49160 | tf_op jit(solution)/shard_map/ppermute | solution.py:1263
  513.2 32.2 %collective-permute-start.53 = (f32[8,512]{1,0:T(8,128)S(1)}, f32[8,512]{1,0:T(8,128)S(1)}, u32[]{:S(2)}, u32[]{:S(2)}) collective-permute-start(f32[8,512]{1,0:T(8,128)S(1)} %get-tuple-element.272), channel_id=1, source_target_pairs={{0,8},{4,12},{8,0},{12,4},{1,9},{5,13},{9,1},{13,5},{2,10},{6,14},... | collective-permute-start | bytes 49160 | tf_op jit(solution)/shard_map/ppermute | solution.py:1268
  546.9 7.2 %collective-permute-start.55 = (f32[2,200,128]{2,1,0:T(8,128)S(1)}, f32[2,200,128]{2,1,0:T(8,128)S(1)}, u32[]{:S(2)}, u32[]{:S(2)}) collective-permute-start(f32[2,200,128]{2,1,0:T(8,128)S(1)} %maximum_select_fusion.1), channel_id=1, source_target_pairs={{0,2},{1,3},{2,0},{3,1},{4,6},{5,7},{6,4},{7,5},{8,10},{9,11},{10,... | collective-permute-start | bytes 614408 | tf_op jit(solution)/shard_map/ppermute | solution.py:52
  (106 other events, 730.5 us)

commit v5 on v4

--- a/solution.py
+++ b/solution.py
@@ -707,37 +707,6 @@
         3 * rows * columns,
         "relay",
     )[0]
-
-
-def settle_kernel(pick_ref, keep_ref, come_ref, last_ref, sent_ref, mine_ref):
-    out = to_bf(to_f(keep_ref[...]) + to_f(come_ref[...]) + to_f(last_ref[...]))
-
-    @pl.when(pl.program_id(0) == 0)
-    def _():
-        sent_ref[...] = out
-
-    @pl.when(pl.program_id(0) == 1)
-    def _():
-        mine_ref[...] = out
-
-
-def settle(order, keep, come, last, picks):
-    share = last.shape[0] // 2
-    columns = keep.shape[1]
-    pair = pl.BlockSpec((share, columns), lambda i, pick_ref: (2 * pick_ref[i], 0))
-    whole = pl.BlockSpec((share, columns), lambda i, pick_ref: (0, 0))
-    return order(
-        settle_kernel,
-        [keep, come, last],
-        [pair, pair, pl.BlockSpec((share, columns), lambda i, pick_ref: (pick_ref[i], 0))],
-        [whole] * 2,
-        [jax.ShapeDtypeStruct((share, columns), jnp.bfloat16)] * 2,
-        (2,),
-        0,
-        16 * share * columns,
-        "settle",
-        scalars=(picks,),
-    )
 
 
 def finish_kernel(plan, columns, gains, *refs):
@@ -1115,7 +1084,6 @@
     one, two = seq_index ^ 1, seq_index ^ 2
     three = seq_index ^ 3
     quad = jnp.stack([one, three, seq_index, two])
-    wide = jnp.stack([one, three, one + seqs, three + seqs, seq_index, two, seq_index + seqs, two + seqs])
 
     begin = (dp_index * seqs + seq_index) * share
 
@@ -1151,23 +1119,17 @@
         def result(self):
             return [self.keep, self.come, self.last] if near_pair else [self.whole]
 
-    class SeqFirst(Rows):
-        def __init__(self, lefts, rights, parts, tile=TILE):
-            if not near_pair:
-                super().__init__(lefts, rights, parts, tile)
-                return
-            send, self.keep = share_of(order, lefts, rights, parts, width, 0, tile, None, wide)
-            self.come = lax.ppermute(send, "seq", flipped("seq", 0))
-
-        def settle(self):
+    class Scattered(Rows):
+        def own(self):
             if near_pair:
-                sent, self.mine = settle(
-                    order, self.keep, self.come, self.last, jnp.stack([1 - dp_index, dp_index])
-                )
-                self.final = lax.ppermute(sent, "dp", flipped("dp", 0))
+                (mine,) = share_of(*self.args, part, dp_index, self.tile, self.come)
+                self.whole = lax.psum_scatter(mine, "seq", scatter_dimension=0, tiled=True)
+
+        def settled(self):
+            order.arrived(self.whole)
 
         def result(self):
-            return [self.mine, self.final] if near_pair else [self.whole]
+            return [self.whole]
 
     sent = core_swaps(narrow(order, [(mixed, o_weight)], 1, (), 1))
     mine = narrow(order, [(mixed, o_weight)], 0, sent, 1)
@@ -1183,24 +1145,18 @@
     h_two += core_swaps(h_two)
     hidden, grad_gate, grad_up = gated(order, h_two, grad_hidden, gate_t, up_t)
 
-    down_a = Rows([grad_ffn_t], [hidden], [(0, 0, 0, long, 0)])
-    down_b = SeqFirst([grad_ffn_t], [hidden], [(0, 0, long, tiles - long, 0)])
+    down = Rows([grad_ffn_t], [hidden], [(0, 0, 0, tiles, 0)])
     pairs = [(grad_gate, gate_t), (grad_up, up_t)]
     sent = core_swaps(narrow(order, pairs, 1))
     mine = narrow(order, pairs, 0, sent)
     come = chip_swaps(mine)
     h_two_t = turn(order, h_two)
-    up_cut = long
     if near_pair:
         sends = share_of(
             order,
             [h_two_t],
             [grad_gate, grad_up],
-            [
-                (0, 0, 0, tiles, 0),
-                (0, 1, 0, up_cut, 1),
-                (0, 1, up_cut, tiles - up_cut, 2),
-            ],
+            [(0, 0, 0, tiles, 0), (0, 1, 0, long, 1), (0, 1, long, tiles - long, 2)],
             part,
             1 - dp_index,
             TILE,
@@ -1208,14 +1164,13 @@
     else:
         sends = [None] * 3
 
-    def half_rows(right, begin, end, sent):
-        return Rows([h_two_t], [right], [(0, 0, begin, end - begin, 0)], TILE, sent)
-
-    gate = half_rows(grad_gate, 0, tiles, sends[0])
-    down_b.relay()
-    down_a.own()
-    up_a = half_rows(grad_up, 0, up_cut, sends[1])
-    up_b = half_rows(grad_up, up_cut, tiles, sends[2])
+    def half_rows(kind, right, begin, end, sent):
+        return kind([h_two_t], [right], [(0, 0, begin, end - begin, 0)], TILE, sent)
+
+    gate = half_rows(Scattered, grad_gate, 0, tiles, sends[0])
+    up_a = half_rows(Rows, grad_up, 0, long, sends[1])
+    up_b = half_rows(Rows, grad_up, long, tiles, sends[2])
+    down.own()
     grad_middle, *branch = norm_back(order, core_one, mine, come, middle, gain_two, grad_ffn, False)
     branch += core_swaps(branch)
     grad_mixed = mixed_back(order, branch, o_weight).reshape(rows, local, heads * HD)
@@ -1226,43 +1181,41 @@
     branch_t = turn(order, branch)
     own_kv, *pieces = fold(order, keep, comes, local)
     moving = shifted(pieces[-1], -1) if pieces else None
-    down_b.settled()
+    ffn_sent = core_swaps(narrow(order, [(hidden, down_t)], 1))
+    down.relay()
     for piece in pieces[-2::-1]:
         moving = shifted(carry(order, piece, moving), -1)
+    ffn_mine = narrow(order, [(hidden, down_t)], 0, ffn_sent)
     grad_qkv, bias_sum = join(
         order, core_one, grad_q_rows, own_kv, [] if moving is None else [moving], cosine, sine
     )
     sent = core_swaps(narrow(order, [(grad_qkv, weight)], 1, (), 1))
-    down_a.relay()
+    last_parts = [(0, 0, 0, grad_qkv.shape[1] // HD, 0), (1, 1, 0, heads, 0)]
+    last = Rows([h_one_t, branch_t], [grad_qkv, mixed], last_parts, HD)
     mine = narrow(order, [(grad_qkv, weight)], 0, sent, 1)
     come = chip_swaps(mine)
-    last_parts = [(0, 0, 0, grad_qkv.shape[1] // HD, 0), (1, 1, 0, heads, 0)]
-    last = Rows([h_one_t, branch_t], [grad_qkv, mixed], last_parts, HD)
     gate.own()
     token = norm_back(order, core_one, mine, come, flat_tokens, gain_one, grad_middle, True)
     token += core_swaps(token)
+    ffn_come = chip_swaps(ffn_mine)
     token_grad = place(order, core_one, token).reshape(rows, local, width)
-    gate.relay()
     up_a.own()
-    ffn_sent = core_swaps(narrow(order, [(hidden, down_t)], 1))
-    if near_pair:
-        down_b.settle()
-    ffn_mine = narrow(order, [(hidden, down_t)], 0, ffn_sent)
-    ffn_come = chip_swaps(ffn_mine)
-    up_b.own()
-    (down_grad,) = finish(order, [down_a.result(), down_b.result()], share, units, TILE)
-    up_a.relay()
-    last.own()
-    gate_grad, gate_term = finish(order, [gate.result()], share, units, TILE, gate_rows)
-    up_b.relay()
+    (down_grad,) = finish(order, [down.result()], share, units, TILE)
     layer = layer_of(order, middle, ffn_mine, ffn_come)
     layer += core_swaps(layer)
+    last.own()
+    layer_out = place(order, core_one, layer).reshape(rows, local, width)
+    up_a.relay()
+    up_b.own()
+    last.relay()
     if near_pair:
         bias_come = lax.ppermute(bias_sum, "dp", flipped("dp", 0))
         bias_all = bias_add(order, bias_sum, bias_come)
         bias_come = lax.ppermute(bias_all, "seq", flipped("seq", 0))
-    last.relay()
-    layer_out = place(order, core_one, layer).reshape(rows, local, width)
+    up_b.relay()
+    gate_grad, gate_term = finish(order, [gate.result()], share, units, TILE, gate_rows)
+    wide_columns = grad_qkv.shape[1]
+    (last_grad,) = finish(order, [last.result()], share, wide_columns + heads * HD, HD)
     if near_pair:
         bias_all = bias_add(order, bias_all, bias_come)
         bias_come = lax.ppermute(bias_all, "seq", flipped("seq", 1))
@@ -1270,8 +1223,6 @@
     else:
         bias_all = lax.psum(bias_sum[:1], ("dp", "seq"))
     up_grad, up_term = finish(order, [up_a.result(), up_b.result()], share, units, TILE, up_rows)
-    wide_columns = grad_qkv.shape[1]
-    (last_grad,) = finish(order, [last.result()], share, wide_columns + heads * HD, HD)
     qkv_grad, o_grad = last_grad[:, :wide_columns], last_grad[:, wide_columns:]
 
     attn_term = jnp.sum(to_f(rows_of(weight)) * qkv_grad, axis=1)

time: 559 us -> 553 us (0.989)
  between operations: 1.81 us -> 15.3 us
  local copies, waits for them, and re-layouts: 74.8 us -> 64.4 us
  starting transfers between devices: 70.4 us -> 61.1 us
    ppermute x5, waiting for transfers between devices: 0.06 us -> 38.6 us  [__init__(): self.come = lax.ppermute(sent, 'dp', flipped('dp', 0))]
    ppermute x4, waiting for transfers between devices: 36.3 us -> 9.56 us  [shifted(): return lax.ppermute(value, 'seq', route)]
    ppermute x6 -> x4, waiting for transfers between devices: 77.9 us -> 52.6 us  [relay(): self.last = lax.ppermute(sent, 'seq', flipped('seq', 1))]
    ppermute x5 -> x4, waiting for transfers between devices: 19.5 us -> 37 us  [own(): self.come = lax.ppermute(send, 'seq', flipped('seq', 0))]
    ppermute x1, waiting for transfers between devices: 14.9 us -> 0.01 us  [body(): bias_come = lax.ppermute(bias_all, 'seq', flipped('seq', 0))]
    ppermute x6 -> x4, starting transfers between devices: 19.2 us -> 6.5 us  [relay(): self.last = lax.ppermute(sent, 'seq', flipped('seq', 1))]
    ppermute x2 -> x0, starting transfers between devices: 12.1 us -> none  [the longest x1 10.6 us: __init__(): self.come = lax.ppermute(send, 'seq', flipped('seq', 0))]
    ppermute x9, waiting for transfers between devices: 23.1 us -> 34.8 us  [chip_swap(): return lax.ppermute(value, 'tensor', flipped('tensor', 1))]
  transfers between devices with their start and end apart: 56 -> 52, of which waited for: 29 -> 27; matrix products, arithmetic and copies ran while one was open for 2% -> 2% of each run, Pallas kernels for 29% -> 27%
where the time goes in v5:
time: 553 us; the launch traced here: 550 us
  Pallas kernels  206 us (37%)
  waiting for transfers between devices  191 us (35%)
  local copies, waits for them, and re-layouts  64.4 us (12%)
  starting transfers between devices  61.1 us (11%)
  between operations  15.3 us (3%)
  other arithmetic  12.2 us (2%)
    pallas_call x43, Pallas kernels, __call__(): pl.pallas_call(run, grid_spec=pltpu.PrefetchScalarGridSpec(num_scalar_pre...  197 us
    unnamed x207, local copies, waits for them, and re-layouts  55.3 us
    ppermute x4, waiting for transfers between devices, relay(): self.last = lax.ppermute(sent, 'seq', flipped('seq', 1))  52.6 us
    ppermute x5, waiting for transfers between devices, __init__(): self.come = lax.ppermute(sent, 'dp', flipped('dp', 0))  38.6 us
    ppermute x4, waiting for transfers between devices, own(): self.come = lax.ppermute(send, 'seq', flipped('seq', 0))  37 us
    ppermute x9, waiting for transfers between devices, chip_swap(): return lax.ppermute(value, 'tensor', flipped('tensor', 1))  34.8 us
    ppermute x22, waiting for transfers between devices, core_swap(): return lax.ppermute(value, 'tensor', flipped('tensor', 0))  15.1 us
    ppermute x4, starting transfers between devices, own(): self.come = lax.ppermute(send, 'seq', flipped('seq', 0))  13.6 us
  transfers between devices with their start and end apart: 52, of which 27 were waited for; matrix products, arithmetic and copies ran while one was open for 2% of the time, Pallas kernels for 27%

profile of v5, /device:TPU:0, one launch (start us, length us, event | category | flops | bytes accessed | tf_op | source)
XLA Modules:
  0.0 550.2 jit_solution(10101733306243772581)
XLA Ops:
  10.4 3.1 fusion.1
  17.3 3.6 first.1
  23.5 6.6 %collective-permute-start = (bf16[2,512,128]{2,1,0:T(8,128)(2,1)S(1)}, bf16[2,512,128]{2,1,0:T(8,128)(2,1)}, u32[]{:S(2)}, u32[]{:S(2)}) collective-permute-start(bf16[2,512,128]{2,1,0:T(8,128)(2,1)S(1)} %bitcast.73), channel_id=1, source_target_pairs={{0,8},{4,12},{1,9},{5,13},{2,10},{6,14},{3,11},{7,15},{16,24},{20,... | collective-permute-start | bytes 786440 | tf_op jit(solution)/shard_map/ppermute | solution.py:66
  30.1 4.2 collective-permute-start.1
  36.1 3.9 collective-permute-done.1.refs_1_.refs_10_
  43.0 6.1 %attend.1 = (bf16[2,512,384]{2,1,0:T(8,128)(2,1)S(1)}, f32[2,2,768]{2,1,0:T(2,128)S(1)}) custom-call(s32[2,2]{1,0:T(2,128)S(1)} %shift-right-logical_maximum_fusion.low_ref.refs_0_, s32[1]{0:T(128)} %bitcast.core_ref.refs_0_.refs_1_, bf16[2,512,384]{2,1,0:T(8,128)(2,1)S(1)} %bitcast.70, s32[2,1,512]{2,1,0:T(1,128)S(1)} %sub.43.start_ref.refs_3_, ...), custom_call_target="tpu_custom_call" | custom-call | flops 8000000 | bytes 4194 | tf_op jit(solution)/shard_map/attend/pallas_call | solution.py:253
  54.7 3.4 narrow.9
  61.4 4.5 constant_dynamic-slice_fusion
  77.2 4.1 copy-done.4
  81.3 9.3 %grad_hidden.1 = (bf16[1024,2240]{1,0:T(8,128)(2,1)S(1)}, f32[8,128]{1,0:T(8,128)S(1)}) custom-call(bf16[1024,1536]{1,0:T(8,128)(2,1)S(1)} %get-tuple-element.145.refs_0_.refs_3_, bf16[2240,1536]{1,0:T(8,128)(2,1)S(1)} %bitcast.57, f32[8,128]{1,0:T(8,128)S(1)} %get-tuple-element.146.refs_2_, bf16[192,2240]{1,0:T(8,128)(2,1)S(1)} %copy-done.35, ...), custom_call_target="tpu_custom_call" | custom-call | flops 7046430 | bytes 15728 | tf_op jit(solution)/shard_map/grad_hidden/pallas_call | solution.py:92
  96.0 4.9 middle.1
  110.9 21.0 %gated.1 = (bf16[1024,2240]{1,0:T(8,128)(2,1)S(1)}, bf16[1024,2240]{1,0:T(8,128)(2,1)S(1)}, bf16[1024,2240]{1,0:T(8,128)(2,1)S(1)}, f32[8,128]{1,0:T(8,128)S(1)}) custom-call(bf16[1024,2240]{1,0:T(8,128)(2,1)S(1)} %copy-done.42, bf16[2240,1536]{1,0:T(8,128)(2,1)} %bitcast.52, bf16[2240,1536]{1,0:T(8,128)(2,1)} %bitcast.79, ...), custom_call_target="tpu_custom_call" | custom-call | flops 14092861 | bytes 31457 | tf_op jit(solution)/shard_map/gated/pallas_call | solution.py:92
  132.0 8.3 %share.8 = (bf16[768,2304]{1,0:T(8,128)(2,1)}, f32[8,128]{1,0:T(8,128)S(1)}) custom-call(s32[1]{0:T(128)} %bitcast.10.refs_0_, s32[1]{0:T(128)} %constant.58.clone.1.refs_1_, bf16[1536,1024]{1,0:T(8,128)(2,1)S(1)} %copy-done.27, bf16[1024,2240]{1,0:T(8,128)(2,1)S(1)} %get-tuple-element.154.refs_3_.refs_0_, f32[8,128]{1,0:T(8,128)S(1)} %get-tuple-element.158.refs_4_), custom_call_target="tpu_custom_call" | custom-call | flops 3623878 | bytes 9830 | tf_op jit(solution)/shard_map/share/pallas_call | solution.py:92
  144.0 10.1 %narrow.10 = (bf16[256,1536]{1,0:T(8,128)(2,1)S(1)}, bf16[256,1536]{1,0:T(8,128)(2,1)S(1)}, f32[8,128]{1,0:T(8,128)S(1)}) custom-call(bf16[1024,2240]{1,0:T(8,128)(2,1)S(1)} %get-tuple-element.155.refs_0_.refs_3_, bf16[2240,1536]{1,0:T(8,128)(2,1)S(1)} %bitcast.55, bf16[1024,2240]{1,0:T(8,128)(2,1)S(1)} %get-tuple-element.156.refs_2_.refs_4_.refs_3_, ...), custom_call_target="tpu_custom_call" | custom-call | flops 7046430 | bytes 19922 | tf_op jit(solution)/shard_map/narrow/pallas_call | solution.py:92
  157.6 11.1 %narrow.11 = (bf16[256,1536]{1,0:T(8,128)(2,1)}, bf16[256,1536]{1,0:T(8,128)(2,1)}, f32[8,128]{1,0:T(8,128)S(1)}) custom-call(bf16[1024,2240]{1,0:T(8,128)(2,1)S(1)} %get-tuple-element.155.refs_0_.refs_3_, bf16[2240,1536]{1,0:T(8,128)(2,1)S(1)} %bitcast.56, bf16[1024,2240]{1,0:T(8,128)(2,1)S(1)} %get-tuple-element.156.refs_2_.refs_4_.refs_3_, ...), custom_call_target="tpu_custom_call" | custom-call | flops 7046430 | bytes 19922 | tf_op jit(solution)/shard_map/narrow/pallas_call | solution.py:92
  170.7 3.8 turn.4
  174.5 13.9 %share.9 = (bf16[768,2304]{1,0:T(8,128)(2,1)}, bf16[768,1536]{1,0:T(8,128)(2,1)S(1)}, bf16[768,768]{1,0:T(8,128)(2,1)}, f32[8,128]{1,0:T(8,128)S(1)}) custom-call(s32[1]{0:T(128)} %bitcast.10.refs_0_, s32[1]{0:T(128)} %constant.58.clone.1.refs_1_, bf16[1536,1024]{1,0:T(8,128)(2,1)S(1)} %get-tuple-element.167.refs_2_, ...), custom_call_target="tpu_custom_call" | custom-call | flops 7247757 | bytes 18087 | tf_op jit(solution)/shard_map/share/pallas_call | solution.py:92
  190.4 31.7 %collective-permute-done.15.refs_4_ = bf16[768,2304]{1,0:T(8,128)(2,1)} collective-permute-done((bf16[768,2304]{1,0:T(8,128)(2,1)}, bf16[768,2304]{1,0:T(8,128)(2,1)}, u32[]{:S(2)}, u32[]{:S(2)}) %collective-permute-start.15) | collective-permute-done | bytes 3538976 | tf_op jit(solution)/shard_map/ppermute | solution.py:1103
  226.4 9.9 %share.10 = (bf16[384,2304]{1,0:T(8,128)(2,1)}, bf16[384,2304]{1,0:T(8,128)(2,1)S(1)}, f32[8,128]{1,0:T(8,128)S(1)}) custom-call(s32[1]{0:T(128)} %bitcast.11.refs_0_, s32[4]{0:T(128)S(1)} %pad_add_fusion.refs_1_, bf16[1536,1024]{1,0:T(8,128)(2,1)S(1)} %copy-done.28, bf16[1024,2240]{1,0:T(8,128)(2,1)S(1)} %copy-done.3, ...), custom_call_target="tpu_custom_call" | custom-call | flops 3623878 | bytes 9830 | tf_op jit(solution)/shard_map/share/pallas_call | solution.py:92
  236.3 11.7 %collective-permute-start.23 = (bf16[384,2304]{1,0:T(8,128)(2,1)}, bf16[384,2304]{1,0:T(8,128)(2,1)}, u32[]{:S(2)}, u32[]{:S(2)}) collective-permute-start(bf16[384,2304]{1,0:T(8,128)(2,1)} %get-tuple-element.188), channel_id=1, source_target_pairs={{0,4},{4,0},{8,12},{12,8},{1,5},{5,1},{9,13},{13,9},{2,6},{6,2},{1... | collective-permute-start | bytes 5308424 | tf_op jit(solution)/shard_map/ppermute | solution.py:1108
  248.1 4.2 norm_back.2
  257.7 9.1 %attend_back.1 = (bf16[2,512,384]{2,1,0:T(8,128)(2,1)S(1)}, bf16[2,1536,128]{2,1,0:T(8,128)(2,1)S(1)}, bf16[1,1536,128]{2,1,0:T(8,128)(2,1)S(1)}, bf16[1,1536,128]{2,1,0:T(8,128)(2,1)S(1)}, f32[8,128]{1,0:T(8,128)S(1)}) custom-call(s32[2,2]{1,0:T(2,128)S(1)} %shift-right-logical_maximum_fusion.low_ref.refs_0_, s32[1]{0:T(128)} %bitcast.core_ref.refs_0_.refs_1_, ...), custom_call_target="tpu_custom_call" | custom-call | flops 20000000 | bytes 6291 | tf_op jit(solution)/shard_map/attend_back/pallas_call | solution.py:92
  269.5 5.3 narrow.12
  276.7 10.0 %collective-permute-done.23.refs_1_ = bf16[384,2304]{1,0:T(8,128)(2,1)} collective-permute-done((bf16[384,2304]{1,0:T(8,128)(2,1)}, bf16[384,2304]{1,0:T(8,128)(2,1)}, u32[]{:S(2)}, u32[]{:S(2)}) %collective-permute-start.23) | collective-permute-done | bytes 1769504 | tf_op jit(solution)/shard_map/ppermute | solution.py:1108
  292.6 6.3 %narrow.13 = (bf16[256,1536]{1,0:T(8,128)(2,1)}, bf16[256,1536]{1,0:T(8,128)(2,1)}, f32[8,128]{1,0:T(8,128)S(1)}) custom-call(bf16[1024,2240]{1,0:T(8,128)(2,1)S(1)} %bitcast.51, bf16[2240,1536]{1,0:T(8,128)(2,1)S(1)} %bitcast.61, bf16[256,1536]{1,0:T(8,128)(2,1)S(1)} %collective-permute-done.20.refs_2_, ...), custom_call_target="tpu_custom_call" | custom-call | flops 3523215 | bytes 10747 | tf_op jit(solution)/shard_map/narrow/pallas_call | solution.py:92
  304.0 5.3 share.11
  313.4 8.3 %share.12 = (bf16[768,2304]{1,0:T(8,128)(2,1)S(1)}, f32[8,128]{1,0:T(8,128)S(1)}) custom-call(s32[1]{0:T(128)} %bitcast.11.refs_0_, s32[1]{0:T(128)} %constant.58.clone.1.refs_1_, bf16[1536,1024]{1,0:T(8,128)(2,1)S(1)} %get-tuple-element.167.refs_2_, bf16[1024,2240]{1,0:T(8,128)(2,1)S(1)} %bitcast.49, bf16[768,2304]{1,0:T(8,128)(2,1)} %collective-permute-done.33.refs_4_, ...), custom_call_target="tpu_custom_call" | custom-call | flops 3623878 | bytes 9830 | tf_op jit(solution)/shard_map/share/pallas_call | solution.py:92
  326.8 4.4 collective-permute-start.27
  331.2 14.0 %collective-permute-done.31.refs_6_ = bf16[256,1536]{1,0:T(8,128)(2,1)S(1)} collective-permute-done((bf16[256,1536]{1,0:T(8,128)(2,1)S(1)}, bf16[256,1536]{1,0:T(8,128)(2,1)S(1)}, u32[]{:S(2)}, u32[]{:S(2)}) %collective-permute-start.31) | collective-permute-done | bytes 786464 | tf_op jit(solution)/shard_map/ppermute | solution.py:52
  345.2 16.0 %collective-permute-done.32.refs_7_ = bf16[256,1536]{1,0:T(8,128)(2,1)S(1)} collective-permute-done((bf16[256,1536]{1,0:T(8,128)(2,1)S(1)}, bf16[256,1536]{1,0:T(8,128)(2,1)S(1)}, u32[]{:S(2)}, u32[]{:S(2)}) %collective-permute-start.32) | collective-permute-done | bytes 786464 | tf_op jit(solution)/shard_map/ppermute | solution.py:52
  367.6 4.6 collective-permute-start.26
  376.6 3.2 place.2
  379.8 3.8 collective-permute-done.27.refs_4_
  383.6 5.4 share.13
  390.8 40.8 %collective-permute-done.26.refs_2_ = bf16[192,2304]{1,0:T(8,128)(2,1)S(1)} collective-permute-done((bf16[192,2304]{1,0:T(8,128)(2,1)S(1)}, bf16[192,2304]{1,0:T(8,128)(2,1)S(1)}, u32[]{:S(2)}, u32[]{:S(2)}) %collective-permute-start.26) | collective-permute-done | bytes 884768 | tf_op jit(solution)/shard_map/ppermute | solution.py:1113
  433.1 5.9 %finish.4 = (f32[192,2240]{1,0:T(8,128)}, f32[8,128]{1,0:T(8,128)S(1)}) custom-call(bf16[384,2304]{1,0:T(8,128)(2,1)S(1)} %copy-done.40, bf16[384,2304]{1,0:T(8,128)(2,1)} %collective-permute-done.23.refs_1_, bf16[192,2304]{1,0:T(8,128)(2,1)S(1)} %collective-permute-done.26.refs_2_, f32[8,128]{1,0:T(8,128)S(1)} %get-tuple-element.218.refs_3_), custom_call_target="tpu_custom_call" | custom-call | bytes 6021 | tf_op jit(solution)/shard_map/finish/pallas_call | solution.py:92
  441.1 3.4 layer.1
  447.5 5.8 %share.14 = (bf16[384,896]{1,0:T(8,128)(2,1)S(1)}, bf16[384,896]{1,0:T(8,128)(2,1)S(1)}, f32[8,128]{1,0:T(8,128)S(1)}) custom-call(s32[1]{0:T(128)} %bitcast.11.refs_0_, s32[4]{0:T(128)S(1)} %pad_add_fusion.refs_1_, bf16[1536,1024]{1,0:T(8,128)(2,1)S(1)} %copy-done.18, bf16[1536,1024]{1,0:T(8,128)(2,1)S(1)} %copy-done.23, bf16[1024,512]{1,0:T(8,128)(2,1)S(1)} %copy-done.15, ...), custom_call_target="tpu_custom_call" | custom-call | flops 1409286 | bytes 4784 | tf_op jit(solution)/shard_map/share/pallas_call | solution.py:92
  456.6 3.1 collective-permute-done.40.refs_4_
  459.7 2.7 share.15
  464.5 19.9 %collective-permute-done.39.refs_1_ = bf16[384,896]{1,0:T(8,128)(2,1)S(1)} collective-permute-done((bf16[384,896]{1,0:T(8,128)(2,1)S(1)}, bf16[384,896]{1,0:T(8,128)(2,1)S(1)}, u32[]{:S(2)}, u32[]{:S(2)}) %collective-permute-start.39) | collective-permute-done | bytes 688160 | tf_op jit(solution)/shard_map/ppermute | solution.py:1108
  485.9 3.2 collective-permute-done.44.refs_1_
  489.1 7.1 %collective-permute-done.43.refs_1_.refs_4_ = bf16[384,768]{1,0:T(8,128)(2,1)S(1)} collective-permute-done((bf16[384,768]{1,0:T(8,128)(2,1)S(1)}, bf16[384,768]{1,0:T(8,128)(2,1)S(1)}, u32[]{:S(2)}, u32[]{:S(2)}) %collective-permute-start.43) | collective-permute-done | bytes 589856 | tf_op jit(solution)/shard_map/ppermute | solution.py:1108
  501.6 3.7 finish.5
  505.3 11.8 %collective-permute-done.42.refs_2_ = bf16[192,896]{1,0:T(8,128)(2,1)} collective-permute-done((bf16[192,896]{1,0:T(8,128)(2,1)}, bf16[192,896]{1,0:T(8,128)(2,1)}, u32[]{:S(2)}, u32[]{:S(2)}) %collective-permute-start.42) | collective-permute-done | bytes 344096 | tf_op jit(solution)/shard_map/ppermute | solution.py:1113
  519.3 3.5 finish.6
  524.7 5.4 finish.7
  534.8 4.8 collective-permute-done.50
  (362 shorter events, 138.5 us)
Async XLA Ops:
  7.2 492.6 %reduce-scatter.2.cloned.1.call-start = ((), (), s32[]{:S(2)}) async-start(), calls=%async_computation.1 | async-start | bytes 4423680 | tf_op jit(solution)/shard_map/reduce_scatter | solution.py:1126
  23.5 12.5 %collective-permute-start = (bf16[2,512,128]{2,1,0:T(8,128)(2,1)S(1)}, bf16[2,512,128]{2,1,0:T(8,128)(2,1)}, u32[]{:S(2)}, u32[]{:S(2)}) collective-permute-start(bf16[2,512,128]{2,1,0:T(8,128)(2,1)S(1)} %bitcast.73), channel_id=1, source_target_pairs={{0,8},{4,12},{1,9},{5,13},{2,10},{6,14},{3,11},{7,15},{16,24},{20,... | collective-permute-start | bytes 786440 | tf_op jit(solution)/shard_map/ppermute | solution.py:66
  30.1 9.8 %collective-permute-start.1 = (bf16[2,512,128]{2,1,0:T(8,128)(2,1)S(1)}, bf16[2,512,128]{2,1,0:T(8,128)(2,1)}, u32[]{:S(2)}, u32[]{:S(2)}) collective-permute-start(bf16[2,512,128]{2,1,0:T(8,128)(2,1)S(1)} %bitcast.74), channel_id=1, source_target_pairs={{0,4},{4,8},{8,12},{1,5},{5,9},{9,13},{2,6},{6,10},{10,14},{3,7},{... | collective-permute-start | bytes 786440 | tf_op jit(solution)/shard_map/ppermute | solution.py:66
  34.3 5.8 %collective-permute-start.4 = (bf16[2,512,128]{2,1,0:T(8,128)(2,1)S(1)}, bf16[2,512,128]{2,1,0:T(8,128)(2,1)}, u32[]{:S(2)}, u32[]{:S(2)}) collective-permute-start(bf16[2,512,128]{2,1,0:T(8,128)(2,1)S(1)} %bitcast.75), channel_id=1, source_target_pairs={{0,1},{1,0},{2,3},{3,2},{4,5},{5,4},{6,7},{7,6},{8,9},{9,8},{10,11... | collective-permute-start | bytes 786440 | tf_op jit(solution)/shard_map/ppermute | solution.py:48
  36.0 4.0 collective-permute-start.2
  51.2 2.4 collective-permute-start.5
  51.4 3.3 collective-permute-start.6
  58.1 37.9 %collective-permute-start.7 = (bf16[256,1536]{1,0:T(8,128)(2,1)}, bf16[256,1536]{1,0:T(8,128)(2,1)}, u32[]{:S(2)}, u32[]{:S(2)}) collective-permute-start(bf16[256,1536]{1,0:T(8,128)(2,1)} %get-tuple-element.141.refs_3_), channel_id=1, source_target_pairs={{0,2},{1,3},{2,0},{3,1},{4,6},{5,7},{6,4},{7,5},{8,10},{9,11},{10,... | collective-permute-start | bytes 2359304 | tf_op jit(solution)/shard_map/ppermute | solution.py:52
  59.6 36.4 %collective-permute-start.8 = (bf16[256,1536]{1,0:T(8,128)(2,1)}, bf16[256,1536]{1,0:T(8,128)(2,1)}, u32[]{:S(2)}, u32[]{:S(2)}) collective-permute-start(bf16[256,1536]{1,0:T(8,128)(2,1)} %get-tuple-element.142.refs_4_), channel_id=1, source_target_pairs={{0,2},{1,3},{2,0},{3,1},{4,6},{5,7},{6,4},{7,5},{8,10},{9,11},{10,... | collective-permute-start | bytes 2359304 | tf_op jit(solution)/shard_map/ppermute | solution.py:52
  102.6 2.5 collective-permute-start.10
  102.6 3.6 collective-permute-start.9
  142.4 79.7 %collective-permute-start.15 = (bf16[768,2304]{1,0:T(8,128)(2,1)}, bf16[768,2304]{1,0:T(8,128)(2,1)}, u32[]{:S(2)}, u32[]{:S(2)}) collective-permute-start(bf16[768,2304]{1,0:T(8,128)(2,1)} %get-tuple-element.165), channel_id=1, source_target_pairs={{0,16},{16,0},{1,17},{17,1},{2,18},{18,2},{3,19},{19,3},{4,20},{20... | collective-permute-start | bytes 10616840 | tf_op jit(solution)/shard_map/ppermute | solution.py:1103
  154.1 2.4 collective-permute-start.11
  154.2 3.4 collective-permute-start.12
  168.6 79.4 %collective-permute-start.13 = (bf16[256,1536]{1,0:T(8,128)(2,1)}, bf16[256,1536]{1,0:T(8,128)(2,1)}, u32[]{:S(2)}, u32[]{:S(2)}) collective-permute-start(bf16[256,1536]{1,0:T(8,128)(2,1)} %get-tuple-element.163.refs_4_), channel_id=1, source_target_pairs={{0,2},{1,3},{2,0},{3,1},{4,6},{5,7},{6,4},{7,5},{8,10},{9,11},{10,... | collective-permute-start | bytes 2359304 | tf_op jit(solution)/shard_map/ppermute | solution.py:52
  170.2 77.9 %collective-permute-start.14 = (bf16[256,1536]{1,0:T(8,128)(2,1)}, bf16[256,1536]{1,0:T(8,128)(2,1)}, u32[]{:S(2)}, u32[]{:S(2)}) collective-permute-start(bf16[256,1536]{1,0:T(8,128)(2,1)} %get-tuple-element.164.refs_5_), channel_id=1, source_target_pairs={{0,2},{1,3},{2,0},{3,1},{4,6},{5,7},{6,4},{7,5},{8,10},{9,11},{10,... | collective-permute-start | bytes 2359304 | tf_op jit(solution)/shard_map/ppermute | solution.py:52
  189.9 123.6 %collective-permute-start.33 = (bf16[768,2304]{1,0:T(8,128)(2,1)}, bf16[768,2304]{1,0:T(8,128)(2,1)}, u32[]{:S(2)}, u32[]{:S(2)}) collective-permute-start(bf16[768,2304]{1,0:T(8,128)(2,1)} %get-tuple-element.211), channel_id=1, source_target_pairs={{0,16},{16,0},{1,17},{17,1},{2,18},{18,2},{3,19},{19,3},{4,20},{20... | collective-permute-start | bytes 10616840 | tf_op jit(solution)/shard_map/ppermute | solution.py:1103
  236.3 50.3 %collective-permute-start.23 = (bf16[384,2304]{1,0:T(8,128)(2,1)}, bf16[384,2304]{1,0:T(8,128)(2,1)}, u32[]{:S(2)}, u32[]{:S(2)}) collective-permute-start(bf16[384,2304]{1,0:T(8,128)(2,1)} %get-tuple-element.188), channel_id=1, source_target_pairs={{0,4},{4,0},{8,12},{12,8},{1,5},{5,1},{9,13},{13,9},{2,6},{6,2},{1... | collective-permute-start | bytes 5308424 | tf_op jit(solution)/shard_map/ppermute | solution.py:1108
  252.4 2.4 collective-permute-start.16
  252.4 3.4 collective-permute-start.17
  274.8 17.7 %collective-permute-start.20 = (bf16[256,1536]{1,0:T(8,128)(2,1)S(1)}, bf16[256,1536]{1,0:T(8,128)(2,1)S(1)}, u32[]{:S(2)}, u32[]{:S(2)}) collective-permute-start(bf16[256,1536]{1,0:T(8,128)(2,1)S(1)} %get-tuple-element.183), channel_id=1, source_target_pairs={{0,1},{1,0},{2,3},{3,2},{4,5},{5,4},{6,7},{7,6},{8,9},{9,8},{10,11... | collective-permute-start | bytes 2359304 | tf_op jit(solution)/shard_map/ppermute | solution.py:48
  275.0 17.5 %collective-permute-start.21 = (bf16[256,1536]{1,0:T(8,128)(2,1)S(1)}, bf16[256,1536]{1,0:T(8,128)(2,1)S(1)}, u32[]{:S(2)}, u32[]{:S(2)}) collective-permute-start(bf16[256,1536]{1,0:T(8,128)(2,1)S(1)} %get-tuple-element.184), channel_id=1, source_target_pairs={{0,1},{1,0},{2,3},{3,2},{4,5},{5,4},{6,7},{7,6},{8,9},{9,8},{10,11... | collective-permute-start | bytes 2359304 | tf_op jit(solution)/shard_map/ppermute | solution.py:48
  275.4 15.8 %collective-permute-start.22 = (bf16[2,512,128]{2,1,0:T(8,128)(2,1)S(1)}, bf16[2,512,128]{2,1,0:T(8,128)(2,1)S(1)}, u32[]{:S(2)}, u32[]{:S(2)}) collective-permute-start(bf16[2,512,128]{2,1,0:T(8,128)(2,1)S(1)} %get-tuple-element.186), channel_id=1, source_target_pairs={{4,0},{8,4},{12,8},{5,1},{9,5},{13,9},{6,2},{10,6},{14,10},{7,3},{... | collective-permute-start | bytes 786440 | tf_op jit(solution)/shard_map/ppermute | solution.py:66
  291.2 9.3 %collective-permute-start.28 = (bf16[2,512,128]{2,1,0:T(8,128)(2,1)S(1)}, bf16[2,512,128]{2,1,0:T(8,128)(2,1)S(1)}, u32[]{:S(2)}, u32[]{:S(2)}) collective-permute-start(bf16[2,512,128]{2,1,0:T(8,128)(2,1)S(1)} %get-tuple-element.199), channel_id=1, source_target_pairs={{4,0},{8,4},{12,8},{5,1},{9,5},{13,9},{6,2},{10,6},{14,10},{7,3},{... | collective-permute-start | bytes 786440 | tf_op jit(solution)/shard_map/ppermute | solution.py:66
  303.4 5.9 %collective-permute-start.29 = (bf16[256,1536]{1,0:T(8,128)(2,1)S(1)}, bf16[256,1536]{1,0:T(8,128)(2,1)S(1)}, u32[]{:S(2)}, u32[]{:S(2)}) collective-permute-start(bf16[256,1536]{1,0:T(8,128)(2,1)S(1)} %get-tuple-element.203), channel_id=1, source_target_pairs={{0,1},{1,0},{2,3},{3,2},{4,5},{5,4},{6,7},{7,6},{8,9},{9,8},{10,11... | collective-permute-start | bytes 2359304 | tf_op jit(solution)/shard_map/ppermute | solution.py:48
  303.4 5.9 %collective-permute-start.30 = (bf16[256,1536]{1,0:T(8,128)(2,1)S(1)}, bf16[256,1536]{1,0:T(8,128)(2,1)S(1)}, u32[]{:S(2)}, u32[]{:S(2)}) collective-permute-start(bf16[256,1536]{1,0:T(8,128)(2,1)S(1)} %get-tuple-element.204), channel_id=1, source_target_pairs={{0,1},{1,0},{2,3},{3,2},{4,5},{5,4},{6,7},{7,6},{8,9},{9,8},{10,11... | collective-permute-start | bytes 2359304 | tf_op jit(solution)/shard_map/ppermute | solution.py:48
  324.8 20.4 %collective-permute-start.31 = (bf16[256,1536]{1,0:T(8,128)(2,1)S(1)}, bf16[256,1536]{1,0:T(8,128)(2,1)S(1)}, u32[]{:S(2)}, u32[]{:S(2)}) collective-permute-start(bf16[256,1536]{1,0:T(8,128)(2,1)S(1)} %copy-done.70), channel_id=1, source_target_pairs={{0,2},{1,3},{2,0},{3,1},{4,6},{5,7},{6,4},{7,5},{8,10},{9,11},{10,... | collective-permute-start | bytes 2359304 | tf_op jit(solution)/shard_map/ppermute | solution.py:52
  326.3 34.9 %collective-permute-start.32 = (bf16[256,1536]{1,0:T(8,128)(2,1)S(1)}, bf16[256,1536]{1,0:T(8,128)(2,1)S(1)}, u32[]{:S(2)}, u32[]{:S(2)}) collective-permute-start(bf16[256,1536]{1,0:T(8,128)(2,1)S(1)} %copy-done.72), channel_id=1, source_target_pairs={{0,2},{1,3},{2,0},{3,1},{4,6},{5,7},{6,4},{7,5},{8,10},{9,11},{10,... | collective-permute-start | bytes 2359304 | tf_op jit(solution)/shard_map/ppermute | solution.py:52
  326.8 56.7 %collective-permute-start.27 = (bf16[768,1536]{1,0:T(8,128)(2,1)}, bf16[768,1536]{1,0:T(8,128)(2,1)S(1)}, u32[]{:S(2)}, u32[]{:S(2)}) collective-permute-start(bf16[768,1536]{1,0:T(8,128)(2,1)} %copy-done.79), channel_id=1, source_target_pairs={{0,16},{16,0},{1,17},{17,1},{2,18},{18,2},{3,19},{19,3},{4,20},{20... | collective-permute-start | bytes 7077896 | tf_op jit(solution)/shard_map/ppermute | solution.py:1103
  367.1 7.5 %collective-permute-start.34 = (f32[256,1536]{1,0:T(8,128)S(1)}, f32[256,1536]{1,0:T(8,128)S(1)}, u32[]{:S(2)}, u32[]{:S(2)}) collective-permute-start(f32[256,1536]{1,0:T(8,128)S(1)} %get-tuple-element.214.refs_1_), channel_id=1, source_target_pairs={{0,1},{1,0},{2,3},{3,2},{4,5},{5,4},{6,7},{7,6},{8,9},{9,8},{10,11... | collective-permute-start | bytes 4718600 | tf_op jit(solution)/shard_map/ppermute | solution.py:48
  367.1 9.0 %collective-permute-start.35 = (f32[256,1536]{1,0:T(8,128)S(1)}, f32[256,1536]{1,0:T(8,128)S(1)}, u32[]{:S(2)}, u32[]{:S(2)}) collective-permute-start(f32[256,1536]{1,0:T(8,128)S(1)} %get-tuple-element.215.refs_2_), channel_id=1, source_target_pairs={{0,1},{1,0},{2,3},{3,2},{4,5},{5,4},{6,7},{7,6},{8,9},{9,8},{10,11... | collective-permute-start | bytes 4718600 | tf_op jit(solution)/shard_map/ppermute | solution.py:48
  367.6 64.0 %collective-permute-start.26 = (bf16[192,2304]{1,0:T(8,128)(2,1)S(1)}, bf16[192,2304]{1,0:T(8,128)(2,1)S(1)}, u32[]{:S(2)}, u32[]{:S(2)}) collective-permute-start(bf16[192,2304]{1,0:T(8,128)(2,1)S(1)} %copy-done.81), channel_id=1, source_target_pairs={{0,8},{4,12},{8,0},{12,4},{1,9},{5,13},{9,1},{13,5},{2,10},{6,14},... | collective-permute-start | bytes 2654216 | tf_op jit(solution)/shard_map/ppermute | solution.py:1113
  372.3 72.8 %collective-permute-start.38 = (bf16[768,896]{1,0:T(8,128)(2,1)}, bf16[768,896]{1,0:T(8,128)(2,1)S(1)}, u32[]{:S(2)}, u32[]{:S(2)}) collective-permute-start(bf16[768,896]{1,0:T(8,128)(2,1)} %get-tuple-element.222), channel_id=1, source_target_pairs={{0,16},{16,0},{1,17},{17,1},{2,18},{18,2},{3,19},{19,3},{4,20},{20... | collective-permute-start | bytes 4128776 | tf_op jit(solution)/shard_map/ppermute | solution.py:1103
  374.6 64.4 %collective-permute-start.24 = (bf16[256,1536]{1,0:T(8,128)(2,1)}, bf16[256,1536]{1,0:T(8,128)(2,1)S(1)}, u32[]{:S(2)}, u32[]{:S(2)}) collective-permute-start(bf16[256,1536]{1,0:T(8,128)(2,1)} %get-tuple-element.192.refs_1_), channel_id=1, source_target_pairs={{0,2},{1,3},{2,0},{3,1},{4,6},{5,7},{6,4},{7,5},{8,10},{9,11},{10,... | collective-permute-start | bytes 2359304 | tf_op jit(solution)/shard_map/ppermute | solution.py:52
  376.1 63.8 %collective-permute-start.25 = (bf16[256,1536]{1,0:T(8,128)(2,1)}, bf16[256,1536]{1,0:T(8,128)(2,1)}, u32[]{:S(2)}, u32[]{:S(2)}) collective-permute-start(bf16[256,1536]{1,0:T(8,128)(2,1)} %get-tuple-element.193.refs_2_), channel_id=1, source_target_pairs={{0,2},{1,3},{2,0},{3,1},{4,6},{5,7},{6,4},{7,5},{8,10},{9,11},{10,... | collective-permute-start | bytes 2359304 | tf_op jit(solution)/shard_map/ppermute | solution.py:52
  389.0 66.6 %collective-permute-start.41 = (bf16[384,1536]{1,0:T(8,128)(2,1)}, bf16[384,1536]{1,0:T(8,128)(2,1)S(1)}, u32[]{:S(2)}, u32[]{:S(2)}) collective-permute-start(bf16[384,1536]{1,0:T(8,128)(2,1)} %get-tuple-element.231), channel_id=1, source_target_pairs={{0,4},{4,0},{8,12},{12,8},{1,5},{5,1},{9,13},{13,9},{2,6},{6,2},{1... | collective-permute-start | bytes 3538952 | tf_op jit(solution)/shard_map/ppermute | solution.py:1108
  431.6 28.1 %collective-permute-start.40 = (bf16[768,768]{1,0:T(8,128)(2,1)}, bf16[768,768]{1,0:T(8,128)(2,1)S(1)}, u32[]{:S(2)}, u32[]{:S(2)}) collective-permute-start(bf16[768,768]{1,0:T(8,128)(2,1)} %get-tuple-element.229), channel_id=1, source_target_pairs={{0,16},{16,0},{1,17},{17,1},{2,18},{18,2},{3,19},{19,3},{4,20},{20... | collective-permute-start | bytes 3538952 | tf_op jit(solution)/shard_map/ppermute | solution.py:1103
  444.5 8.9 %collective-permute-start.36 = (bf16[256,1536]{1,0:T(8,128)(2,1)S(1)}, bf16[256,1536]{1,0:T(8,128)(2,1)S(1)}, u32[]{:S(2)}, u32[]{:S(2)}) collective-permute-start(bf16[256,1536]{1,0:T(8,128)(2,1)S(1)} %get-tuple-element.220.refs_1_), channel_id=1, source_target_pairs={{0,1},{1,0},{2,3},{3,2},{4,5},{5,4},{6,7},{7,6},{8,9},{9,8},{10,11... | collective-permute-start | bytes 2359304 | tf_op jit(solution)/shard_map/ppermute | solution.py:48
  444.6 8.8 %collective-permute-start.37 = (bf16[256,1536]{1,0:T(8,128)(2,1)S(1)}, bf16[256,1536]{1,0:T(8,128)(2,1)S(1)}, u32[]{:S(2)}, u32[]{:S(2)}) collective-permute-start(bf16[256,1536]{1,0:T(8,128)(2,1)S(1)} %get-tuple-element.221.refs_2_), channel_id=1, source_target_pairs={{0,1},{1,0},{2,3},{3,2},{4,5},{5,4},{6,7},{7,6},{8,9},{9,8},{10,11... | collective-permute-start | bytes 2359304 | tf_op jit(solution)/shard_map/ppermute | solution.py:48
  453.3 31.0 %collective-permute-start.39 = (bf16[384,896]{1,0:T(8,128)(2,1)S(1)}, bf16[384,896]{1,0:T(8,128)(2,1)S(1)}, u32[]{:S(2)}, u32[]{:S(2)}) collective-permute-start(bf16[384,896]{1,0:T(8,128)(2,1)S(1)} %get-tuple-element.228), channel_id=1, source_target_pairs={{0,4},{4,0},{8,12},{12,8},{1,5},{5,1},{9,13},{13,9},{2,6},{6,2},{1... | collective-permute-start | bytes 2064392 | tf_op jit(solution)/shard_map/ppermute | solution.py:1108
  462.5 33.7 %collective-permute-start.43 = (bf16[384,768]{1,0:T(8,128)(2,1)S(1)}, bf16[384,768]{1,0:T(8,128)(2,1)S(1)}, u32[]{:S(2)}, u32[]{:S(2)}) collective-permute-start(bf16[384,768]{1,0:T(8,128)(2,1)S(1)} %get-tuple-element.238), channel_id=1, source_target_pairs={{0,4},{4,0},{8,12},{12,8},{1,5},{5,1},{9,13},{13,9},{2,6},{6,2},{1... | collective-permute-start | bytes 1769480 | tf_op jit(solution)/shard_map/ppermute | solution.py:1108
  462.6 62.0 %collective-permute-start.47 = (bf16[192,1536]{1,0:T(8,128)(2,1)}, bf16[192,1536]{1,0:T(8,128)(2,1)}, u32[]{:S(2)}, u32[]{:S(2)}) collective-permute-start(bf16[192,1536]{1,0:T(8,128)(2,1)} %get-tuple-element.249), channel_id=1, source_target_pairs={{0,8},{4,12},{8,0},{12,4},{1,9},{5,13},{9,1},{13,5},{2,10},{6,14},... | collective-permute-start | bytes 1769480 | tf_op jit(solution)/shard_map/ppermute | solution.py:1113
  485.3 31.7 %collective-permute-start.42 = (bf16[192,896]{1,0:T(8,128)(2,1)}, bf16[192,896]{1,0:T(8,128)(2,1)}, u32[]{:S(2)}, u32[]{:S(2)}) collective-permute-start(bf16[192,896]{1,0:T(8,128)(2,1)} %get-tuple-element.235), channel_id=1, source_target_pairs={{0,8},{4,12},{8,0},{12,4},{1,9},{5,13},{9,1},{13,5},{2,10},{6,14},... | collective-permute-start | bytes 1032200 | tf_op jit(solution)/shard_map/ppermute | solution.py:1113
  485.3 3.7 collective-permute-start.44
  497.7 26.9 %collective-permute-start.48 = (bf16[192,768]{1,0:T(8,128)(2,1)}, bf16[192,768]{1,0:T(8,128)(2,1)S(1)}, u32[]{:S(2)}, u32[]{:S(2)}) collective-permute-start(bf16[192,768]{1,0:T(8,128)(2,1)} %get-tuple-element.250), channel_id=1, source_target_pairs={{0,8},{4,12},{8,0},{12,4},{1,9},{5,13},{9,1},{13,5},{2,10},{6,14},... | collective-permute-start | bytes 884744 | tf_op jit(solution)/shard_map/ppermute | solution.py:1113
  497.8 25.1 %collective-permute-start.45 = (f32[8,512]{1,0:T(8,128)S(1)}, f32[8,512]{1,0:T(8,128)}, u32[]{:S(2)}, u32[]{:S(2)}) collective-permute-start(f32[8,512]{1,0:T(8,128)S(1)} %get-tuple-element.245.refs_0_), channel_id=1, source_target_pairs={{0,4},{4,0},{8,12},{12,8},{1,5},{5,1},{9,13},{13,9},{2,6},{6,2},{1... | collective-permute-start | bytes 49160 | tf_op jit(solution)/shard_map/ppermute | solution.py:1214
  523.5 6.7 %collective-permute-start.46 = (f32[8,512]{1,0:T(8,128)S(1)}, f32[8,512]{1,0:T(8,128)}, u32[]{:S(2)}, u32[]{:S(2)}) collective-permute-start(f32[8,512]{1,0:T(8,128)S(1)} %get-tuple-element.247), channel_id=1, source_target_pairs={{0,8},{4,12},{8,0},{12,4},{1,9},{5,13},{9,1},{13,5},{2,10},{6,14},... | collective-permute-start | bytes 49160 | tf_op jit(solution)/shard_map/ppermute | solution.py:1221
  532.4 7.2 %collective-permute-start.50 = (f32[2,200,128]{2,1,0:T(8,128)S(1)}, f32[2,200,128]{2,1,0:T(8,128)S(1)}, u32[]{:S(2)}, u32[]{:S(2)}) collective-permute-start(f32[2,200,128]{2,1,0:T(8,128)S(1)} %maximum_select_fusion.1), channel_id=1, source_target_pairs={{0,2},{1,3},{2,0},{3,1},{4,6},{5,7},{6,4},{7,5},{8,10},{9,11},{10,... | collective-permute-start | bytes 614408 | tf_op jit(solution)/shard_map/ppermute | solution.py:52
  (105 other events, 1219.8 us)
Sparse Core Ops, SparseCore 0:
  323.8 87.9 reduce-scatter.1

commit v6 on v5

--- a/solution.py
+++ b/solution.py
@@ -279,7 +279,7 @@
 def attend_back_kernel(
     heads, blocks, pieces, low_ref, core_ref, q_ref, start_ref, g_ref, o_ref, lse_ref, cos_ref, sin_ref, *refs
 ):
-    gq_ref, keep_ref, *sends, acc, gk, gv, span = refs[2 * pieces :]
+    gq_ref, keep_ref, send_ref, acc, gk, gv, span = refs[2 * pieces :]
     row = pl.program_id(0)
     wide = heads * Q_BLOCK
     reach = (pieces - 1) * q_ref.shape[1]
@@ -322,12 +322,7 @@
     is_key = core == 0
     keys, values = gk[...] * SCALE, gv[...]
     keep_ref[0] = to_bf(jnp.where(is_key, keys, values))
-    sent = to_bf(jnp.where(is_key, values, keys))
-    for i, ref in enumerate(sends):
-
-        @pl.when(row == i)
-        def _(ref=ref):
-            ref[0] = sent
+    send_ref[0] = to_bf(jnp.where(is_key, values, keys))
 
 
 def attend_back(order, low, core, q, start, span, mate, grad, out, lse, cosine, sine):
@@ -355,13 +350,12 @@
             table,
         ]
         + span_specs(rows, local, pieces),
-        [tokens, pl.BlockSpec((1, window, HD), at)]
-        + [pl.BlockSpec((1, window, HD), lambda i, *refs: (0, 0, 0))] * rows,
+        [tokens, pl.BlockSpec((1, window, HD), at), pl.BlockSpec((1, window, HD), at)],
         [
             jax.ShapeDtypeStruct((rows, local, columns), jnp.bfloat16),
             jax.ShapeDtypeStruct((rows, window, HD), jnp.bfloat16),
-        ]
-        + [jax.ShapeDtypeStruct((1, window, HD), jnp.bfloat16)] * rows,
+            jax.ShapeDtypeStruct((rows, window, HD), jnp.bfloat16),
+        ],
         (rows,),
         20_000_000_000,
         6 * MIB,
@@ -376,28 +370,26 @@
     )
 
 
-def fold_kernel(rows, keep_ref, *refs):
-    comes, own_ref, send_refs = refs[:rows], refs[rows], refs[rows + 1 :]
+def fold_kernel(keep_ref, come_ref, own_ref, *send_refs):
     local = own_ref.shape[1]
-    come = comes[0][0]
-    for i in range(1, rows):
-        come = jnp.where(pl.program_id(0) == i, comes[i][0], come)
-    total = to_f(keep_ref[0]) + to_f(come)
+    total = to_f(keep_ref[0]) + to_f(come_ref[0])
     reach = total.shape[0] - local
     own_ref[0] = total[reach:]
     for hop, ref in enumerate(send_refs, 1):
         ref[0] = to_bf(total[reach - hop * local : reach - (hop - 1) * local])
 
 
-def fold(order, keep, comes, local):
+def fold(order, keep, come, local):
     rows, window = keep.shape[:2]
     hops = window // local - 1
     out = pl.BlockSpec((1, local, HD), lambda i: (i, 0, 0))
     return order(
-        functools.partial(fold_kernel, rows),
-        [keep, *comes],
-        [pl.BlockSpec((1, window, HD), lambda i: (i, 0, 0))]
-        + [pl.BlockSpec((1, window, HD), lambda i: (0, 0, 0))] * rows,
+        fold_kernel,
+        [keep, come],
+        [
+            pl.BlockSpec((1, window, HD), lambda i: (i, 0, 0)),
+            pl.BlockSpec((1, window, HD), lambda i: (lax.rem(i + rows // 2, rows), 0, 0)),
+        ],
         [out] * (hops + 1),
         [jax.ShapeDtypeStruct((rows, local, HD), jnp.float32)]
         + [jax.ShapeDtypeStruct((rows, local, HD), jnp.bfloat16)] * hops,
@@ -617,7 +609,7 @@
     )
 
 
-def share_kernel(plan, lefts, rights, extra, halves, pick_ref, blocks_ref, *refs):
+def share_kernel(plan, lefts, rights, extra, halves, groups, pick_ref, blocks_ref, *refs):
     step = pl.program_id(0)
     left_refs, right_refs = refs[:lefts], refs[lefts : lefts + rights]
     refs = refs[lefts + rights :]
@@ -633,6 +625,14 @@
             tile = out.shape[1]
             spot = (step + shift) * tile + lax.broadcasted_iota(jnp.int32, (1, tile), 1)
             out = to_bf(jnp.where(spot < columns, out, 0.0))
+            if groups:
+                share = out.shape[0] // (groups[0] * groups[1])
+                for i in range(groups[0]):
+                    for j in range(groups[1]):
+                        here = (j * groups[0] + i) * share
+                        there = (i * groups[1] + j) * share
+                        refs[target][here : here + share] = out[there : there + share]
+                return
             if not halves:
                 refs[target][...] = out
                 return
@@ -649,7 +649,7 @@
     return pl.BlockSpec((rows, tile), lambda i, *refs: (0, jnp.clip(i - begin, 0, count - 1) + shift))
 
 
-def share_of(order, lefts, rights, parts, part, pick, tile, extra=None, blocks=None):
+def share_of(order, lefts, rights, parts, part, pick, tile, extra=None, blocks=None, groups=None):
     tokens = lefts[0].shape[1]
     plan, at = [], 0
     starts, sizes, right_at = {}, {}, {}
@@ -673,7 +673,7 @@
         shapes = [jax.ShapeDtypeStruct((part // 2, at * tile), jnp.bfloat16)] * 2
         scratch = [pltpu.VMEM((part, tile), jnp.bfloat16)]
     return order(
-        functools.partial(share_kernel, plan, len(lefts), len(rights), len(extras), halves),
+        functools.partial(share_kernel, plan, len(lefts), len(rights), len(extras), halves, groups),
         [*lefts, *rights, *extras],
         [pl.BlockSpec((part, tokens), lambda i, pick_ref, blocks_ref: (pick_ref[0], 0))] * len(lefts)
         + [clipped(tokens, tile, *right_at[r]) for r in range(len(rights))]
@@ -1119,6 +1119,27 @@
         def result(self):
             return [self.keep, self.come, self.last] if near_pair else [self.whole]
 
+    class SeqFirst(Rows):
+        def __init__(self, lefts, rights, parts, tile=TILE):
+            if not near_pair:
+                super().__init__(lefts, rights, parts, tile)
+                return
+            (whole,) = share_of(order, lefts, rights, parts, width, 0, tile, None, None, (dps, seqs))
+            self.mine = lax.psum_scatter(whole, "seq", scatter_dimension=0, tiled=True)
+
+        def across(self):
+            if near_pair:
+                sent = lax.dynamic_slice_in_dim(self.mine, (1 - dp_index) * share, share, 0)
+                self.mine = lax.dynamic_slice_in_dim(self.mine, dp_index * share, share, 0)
+                self.come = lax.ppermute(sent, "dp", flipped("dp", 0))
+
+        def settled(self):
+            if near_pair:
+                order.arrived(self.come)
+
+        def result(self):
+            return [self.mine, self.come] if near_pair else [self.whole]
+
     class Scattered(Rows):
         def own(self):
             if near_pair:
@@ -1145,7 +1166,8 @@
     h_two += core_swaps(h_two)
     hidden, grad_gate, grad_up = gated(order, h_two, grad_hidden, gate_t, up_t)
 
-    down = Rows([grad_ffn_t], [hidden], [(0, 0, 0, tiles, 0)])
+    down_b = SeqFirst([grad_ffn_t], [hidden], [(0, 0, cut, tiles - cut, 0)])
+    down_a = Rows([grad_ffn_t], [hidden], [(0, 0, 0, cut, 0)])
     pairs = [(grad_gate, gate_t), (grad_up, up_t)]
     sent = core_swaps(narrow(order, pairs, 1))
     mine = narrow(order, pairs, 0, sent)
@@ -1170,22 +1192,20 @@
     gate = half_rows(Scattered, grad_gate, 0, tiles, sends[0])
     up_a = half_rows(Rows, grad_up, 0, long, sends[1])
     up_b = half_rows(Rows, grad_up, long, tiles, sends[2])
-    down.own()
+    down_a.own()
     grad_middle, *branch = norm_back(order, core_one, mine, come, middle, gain_two, grad_ffn, False)
     branch += core_swaps(branch)
     grad_mixed = mixed_back(order, branch, o_weight).reshape(rows, local, heads * HD)
-    grad_q_rows, keep, *sends = attend_back(
+    grad_q_rows, keep, sent = attend_back(
         order, low, core_one, q_rows, start, span, mate, grad_mixed, mixed_rows, lse, cosine, sine
     )
-    comes = core_swaps([sends[(i + rows // 2) % rows] for i in range(rows)])
+    both_come = core_swap(sent)
     branch_t = turn(order, branch)
-    own_kv, *pieces = fold(order, keep, comes, local)
+    own_kv, *pieces = fold(order, keep, both_come, local)
     moving = shifted(pieces[-1], -1) if pieces else None
     ffn_sent = core_swaps(narrow(order, [(hidden, down_t)], 1))
-    down.relay()
     for piece in pieces[-2::-1]:
         moving = shifted(carry(order, piece, moving), -1)
-    ffn_mine = narrow(order, [(hidden, down_t)], 0, ffn_sent)
     grad_qkv, bias_sum = join(
         order, core_one, grad_q_rows, own_kv, [] if moving is None else [moving], cosine, sine
     )
@@ -1194,20 +1214,25 @@
     last = Rows([h_one_t, branch_t], [grad_qkv, mixed], last_parts, HD)
     mine = narrow(order, [(grad_qkv, weight)], 0, sent, 1)
     come = chip_swaps(mine)
+    down_a.relay()
     gate.own()
+    ffn_mine = narrow(order, [(hidden, down_t)], 0, ffn_sent)
     token = norm_back(order, core_one, mine, come, flat_tokens, gain_one, grad_middle, True)
     token += core_swaps(token)
     ffn_come = chip_swaps(ffn_mine)
     token_grad = place(order, core_one, token).reshape(rows, local, width)
     up_a.own()
-    (down_grad,) = finish(order, [down.result()], share, units, TILE)
+    down_a.settled()
     layer = layer_of(order, middle, ffn_mine, ffn_come)
     layer += core_swaps(layer)
+    down_b.across()
     last.own()
     layer_out = place(order, core_one, layer).reshape(rows, local, width)
     up_a.relay()
+    down_b.settled()
     up_b.own()
     last.relay()
+    (down_grad,) = finish(order, [down_a.result(), down_b.result()], share, units, TILE)
     if near_pair:
         bias_come = lax.ppermute(bias_sum, "dp", flipped("dp", 0))
         bias_all = bias_add(order, bias_sum, bias_come)

time: 553 us -> 516 us (0.933)
  waiting for transfers between devices: 191 us -> 171 us
  starting transfers between devices: 61.1 us -> 46.6 us
  local copies, waits for them, and re-layouts: 64.4 us -> 76.5 us
  Pallas kernels: 206 us -> 195 us
    ppermute x5, waiting for transfers between devices: 38.6 us -> 7.36 us  [__init__(): self.come = lax.ppermute(sent, 'dp', flipped('dp', 0))]
    ppermute x4, waiting for transfers between devices: 9.56 us -> 30.5 us  [shifted(): return lax.ppermute(value, 'seq', route)]
    ppermute x4, waiting for transfers between devices: 37 us -> 24.4 us  [own(): self.come = lax.ppermute(send, 'seq', flipped('seq', 0))]
    pallas_call x43 -> x44, Pallas kernels: 197 us -> 186 us  [__call__(): pl.pallas_call(run, grid_spec=pltpu.PrefetchScalarGridSpec(num_scalar_pre...]
    unnamed x207 -> x219, local copies, waits for them, and re-layouts: 55.3 us -> 66.3 us
    ppermute x4, starting transfers between devices: 13.6 us -> 2.85 us  [own(): self.come = lax.ppermute(send, 'seq', flipped('seq', 0))]
    ppermute x0 -> x1, waiting for transfers between devices: none -> 7.33 us  [across(): self.come = lax.ppermute(sent, 'dp', flipped('dp', 0))]
    ppermute x5, starting transfers between devices: 10.2 us -> 3.56 us  [__init__(): self.come = lax.ppermute(sent, 'dp', flipped('dp', 0))]
  transfers between devices with their start and end apart: 52 -> 53, of which waited for: 27 -> 31; matrix products, arithmetic and copies ran while one was open for 2% -> 3% of each run, Pallas kernels for 27% -> 29%
where the time goes in v6:
time: 516 us; the launch traced here: 514 us
  Pallas kernels  195 us (38%)
  waiting for transfers between devices  171 us (33%)
  local copies, waits for them, and re-layouts  76.5 us (15%)
  starting transfers between devices  46.6 us (9%)
  between operations  15.5 us (3%)
  other arithmetic  9.38 us (2%)
    pallas_call x44, Pallas kernels, __call__(): pl.pallas_call(run, grid_spec=pltpu.PrefetchScalarGridSpec(num_scalar_pre...  186 us
    unnamed x219, local copies, waits for them, and re-layouts  66.3 us
    ppermute x4, waiting for transfers between devices, relay(): self.last = lax.ppermute(sent, 'seq', flipped('seq', 1))  46.5 us
    ppermute x9, waiting for transfers between devices, chip_swap(): return lax.ppermute(value, 'tensor', flipped('tensor', 1))  35.2 us
    ppermute x4, waiting for transfers between devices, shifted(): return lax.ppermute(value, 'seq', route)  30.5 us
    ppermute x4, waiting for transfers between devices, own(): self.come = lax.ppermute(send, 'seq', flipped('seq', 0))  24.4 us
    ppermute x21, waiting for transfers between devices, core_swap(): return lax.ppermute(value, 'tensor', flipped('tensor', 0))  19.5 us
    ppermute x4, starting transfers between devices, shifted(): return lax.ppermute(value, 'seq', route)  13 us
  transfers between devices with their start and end apart: 53, of which 31 were waited for; matrix products, arithmetic and copies ran while one was open for 3% of the time, Pallas kernels for 29%

profile of v6, /device:TPU:0, one launch (start us, length us, event | category | flops | bytes accessed | tf_op | source)
XLA Modules:
  0.0 514.3 jit_solution(12601859946675111174)
XLA Ops:
  17.2 3.6 first.1
  23.4 5.6 %collective-permute-start.1 = (bf16[2,512,128]{2,1,0:T(8,128)(2,1)S(1)}, bf16[2,512,128]{2,1,0:T(8,128)(2,1)}, u32[]{:S(2)}, u32[]{:S(2)}) collective-permute-start(bf16[2,512,128]{2,1,0:T(8,128)(2,1)S(1)} %bitcast.79), channel_id=1, source_target_pairs={{0,4},{4,8},{8,12},{1,5},{5,9},{9,13},{2,6},{6,10},{10,14},{3,7},{... | collective-permute-start | bytes 786440 | tf_op jit(solution)/shard_map/ppermute | solution.py:66
  29.0 4.5 collective-permute-start
  34.5 4.3 collective-permute-done.refs_0_.refs_9_
  41.9 6.1 %attend.1 = (bf16[2,512,384]{2,1,0:T(8,128)(2,1)S(1)}, f32[2,2,768]{2,1,0:T(2,128)S(1)}) custom-call(s32[2,2]{1,0:T(2,128)S(1)} %shift-right-logical_maximum_fusion.low_ref.refs_0_, s32[1]{0:T(128)} %bitcast.core_ref.refs_0_.refs_1_, bf16[2,512,384]{2,1,0:T(8,128)(2,1)S(1)} %bitcast.76, s32[2,1,512]{2,1,0:T(1,128)S(1)} %sub.44.start_ref.refs_3_, ...), custom_call_target="tpu_custom_call" | custom-call | flops 8000000 | bytes 4194 | tf_op jit(solution)/shard_map/attend/pallas_call | solution.py:253
  53.6 3.5 narrow.9
  60.4 4.5 constant_dynamic-slice_fusion.2
  74.6 5.2 %copy-done.9 = bf16[1536,2240]{0,1:T(8,128)(2,1)S(1)} copy-done((bf16[1536,2240]{0,1:T(8,128)(2,1)S(1)}, bf16[1536,2240]{0,1:T(8,128)(2,1)}, u32[]{:S(2)}) %copy-start.9) | copy-done | bytes 6881304
  79.8 9.3 %grad_hidden.1 = (bf16[1024,2240]{1,0:T(8,128)(2,1)S(1)}, f32[8,128]{1,0:T(8,128)S(1)}) custom-call(bf16[1024,1536]{1,0:T(8,128)(2,1)S(1)} %get-tuple-element.146.refs_0_.refs_3_, bf16[2240,1536]{1,0:T(8,128)(2,1)S(1)} %bitcast.63, f32[8,128]{1,0:T(8,128)S(1)} %get-tuple-element.147.refs_2_, bf16[192,2240]{1,0:T(8,128)(2,1)S(1)} %copy-done.41, ...), custom_call_target="tpu_custom_call" | custom-call | flops 7046430 | bytes 15728 | tf_op jit(solution)/shard_map/grad_hidden/pallas_call | solution.py:92
  93.8 3.8 middle.1
  103.5 20.3 %gated.1 = (bf16[1024,2240]{1,0:T(8,128)(2,1)S(1)}, bf16[1024,2240]{1,0:T(8,128)(2,1)S(1)}, bf16[1024,2240]{1,0:T(8,128)(2,1)S(1)}, f32[8,128]{1,0:T(8,128)S(1)}) custom-call(bf16[1024,2240]{1,0:T(8,128)(2,1)S(1)} %copy-done.49, bf16[2240,1536]{1,0:T(8,128)(2,1)} %bitcast.60, bf16[2240,1536]{1,0:T(8,128)(2,1)} %bitcast.85, ...), custom_call_target="tpu_custom_call" | custom-call | flops 14092861 | bytes 31457 | tf_op jit(solution)/shard_map/gated/pallas_call | solution.py:92
  126.0 4.6 share.9
  139.1 4.2 share.10
  147.1 3.0 copy-done.7
  150.1 10.3 %narrow.10 = (bf16[256,1536]{1,0:T(8,128)(2,1)S(1)}, bf16[256,1536]{1,0:T(8,128)(2,1)S(1)}, f32[8,128]{1,0:T(8,128)S(1)}) custom-call(bf16[1024,2240]{1,0:T(8,128)(2,1)S(1)} %copy-done.6, bf16[2240,1536]{1,0:T(8,128)(2,1)S(1)} %bitcast.61, bf16[1024,2240]{1,0:T(8,128)(2,1)S(1)} %bitcast.47, bf16[2240,1536]{1,0:T(8,128)(2,1)} %bitcast.86, ...), custom_call_target="tpu_custom_call" | custom-call | flops 7046430 | bytes 19922 | tf_op jit(solution)/shard_map/narrow/pallas_call | solution.py:92
  163.9 3.2 copy-done.8
  167.0 11.1 %narrow.11 = (bf16[256,1536]{1,0:T(8,128)(2,1)}, bf16[256,1536]{1,0:T(8,128)(2,1)}, f32[8,128]{1,0:T(8,128)S(1)}) custom-call(bf16[1024,2240]{1,0:T(8,128)(2,1)S(1)} %bitcast.55, bf16[2240,1536]{1,0:T(8,128)(2,1)S(1)} %bitcast.62, bf16[1024,2240]{1,0:T(8,128)(2,1)S(1)} %bitcast.47, bf16[2240,1536]{1,0:T(8,128)(2,1)} %bitcast.87, ...), custom_call_target="tpu_custom_call" | custom-call | flops 7046430 | bytes 19922 | tf_op jit(solution)/shard_map/narrow/pallas_call | solution.py:92
  181.6 13.7 %share.11 = (bf16[768,2304]{1,0:T(8,128)(2,1)}, bf16[768,1536]{1,0:T(8,128)(2,1)S(1)}, bf16[768,768]{1,0:T(8,128)(2,1)}, f32[8,128]{1,0:T(8,128)S(1)}) custom-call(s32[1]{0:T(128)} %bitcast.10.refs_0_, s32[1]{0:T(128)} %constant.59.clone.1.refs_0_.refs_1_, bf16[1536,1024]{1,0:T(8,128)(2,1)S(1)} %get-tuple-element.169.refs_2_, ...), custom_call_target="tpu_custom_call" | custom-call | flops 7247757 | bytes 18087 | tf_op jit(solution)/shard_map/share/pallas_call | solution.py:92
  201.7 5.9 %share.12 = (bf16[384,1280]{1,0:T(8,128)(2,1)S(1)}, bf16[384,1280]{1,0:T(8,128)(2,1)S(1)}, f32[8,128]{1,0:T(8,128)S(1)}) custom-call(s32[1]{0:T(128)} %bitcast.11.refs_0_, s32[4]{0:T(128)S(1)} %pad_add_fusion.refs_1_, bf16[1536,1024]{1,0:T(8,128)(2,1)S(1)} %copy-done.17, bf16[1024,2240]{1,0:T(8,128)(2,1)S(1)} %copy-done.3, ...), custom_call_target="tpu_custom_call" | custom-call | flops 2013265 | bytes 6160 | tf_op jit(solution)/shard_map/share/pallas_call | solution.py:92
  207.6 7.2 %collective-permute-done.14.refs_7_ = bf16[256,1536]{1,0:T(8,128)(2,1)} collective-permute-done((bf16[256,1536]{1,0:T(8,128)(2,1)}, bf16[256,1536]{1,0:T(8,128)(2,1)}, u32[]{:S(2)}, u32[]{:S(2)}) %collective-permute-start.14) | collective-permute-done | bytes 786464 | tf_op jit(solution)/shard_map/ppermute | solution.py:52
  214.8 4.0 norm_back.2
  224.3 9.0 %attend_back.1 = (bf16[2,512,384]{2,1,0:T(8,128)(2,1)S(1)}, bf16[2,1536,128]{2,1,0:T(8,128)(2,1)S(1)}, bf16[2,1536,128]{2,1,0:T(8,128)(2,1)S(1)}, f32[8,128]{1,0:T(8,128)S(1)}) custom-call(s32[2,2]{1,0:T(2,128)S(1)} %shift-right-logical_maximum_fusion.low_ref.refs_0_, s32[1]{0:T(128)} %bitcast.core_ref.refs_0_.refs_1_, bf16[2,512,384]{2,1,0:T(8,128)(2,1)S(1)} %bitcast.77, ...), custom_call_target="tpu_custom_call" | custom-call | flops 20000000 | bytes 6291 | tf_op jit(solution)/shard_map/attend_back/pallas_call | solution.py:92
  237.2 5.3 %narrow.12 = (bf16[256,1536]{1,0:T(8,128)(2,1)S(1)}, bf16[256,1536]{1,0:T(8,128)(2,1)S(1)}, f32[8,128]{1,0:T(8,128)S(1)}) custom-call(bf16[1024,2240]{1,0:T(8,128)(2,1)S(1)} %bitcast.53, bf16[2240,1536]{1,0:T(8,128)(2,1)S(1)} %bitcast.66, f32[8,128]{1,0:T(8,128)S(1)} %get-tuple-element.183.refs_2_), custom_call_target="tpu_custom_call" | custom-call | flops 3523215 | bytes 10747 | tf_op jit(solution)/shard_map/narrow/pallas_call | solution.py:92
  242.6 18.4 %collective-permute-done.23.refs_1_ = bf16[2,512,128]{2,1,0:T(8,128)(2,1)S(1)} collective-permute-done((bf16[2,512,128]{2,1,0:T(8,128)(2,1)S(1)}, bf16[2,512,128]{2,1,0:T(8,128)(2,1)S(1)}, u32[]{:S(2)}, u32[]{:S(2)}) %collective-permute-start.23) | collective-permute-done | bytes 262176 | tf_op jit(solution)/shard_map/ppermute | solution.py:66
  262.6 2.7 collective-permute-start.22
  265.3 6.8 %collective-permute-done.24.refs_5_ = bf16[2,512,128]{2,1,0:T(8,128)(2,1)S(1)} collective-permute-done((bf16[2,512,128]{2,1,0:T(8,128)(2,1)S(1)}, bf16[2,512,128]{2,1,0:T(8,128)(2,1)S(1)}, u32[]{:S(2)}, u32[]{:S(2)}) %collective-permute-start.24) | collective-permute-done | bytes 262176 | tf_op jit(solution)/shard_map/ppermute | solution.py:66
  275.5 5.3 %share.13 = (bf16[768,896]{1,0:T(8,128)(2,1)}, f32[8,128]{1,0:T(8,128)S(1)}) custom-call(s32[1]{0:T(128)} %bitcast.10.refs_0_, s32[1]{0:T(128)} %constant.59.clone.1.refs_0_.refs_1_, bf16[1536,1024]{1,0:T(8,128)(2,1)S(1)} %copy-done.29, bf16[1536,1024]{1,0:T(8,128)(2,1)S(1)} %get-tuple-element.201.refs_3_, ...), custom_call_target="tpu_custom_call" | custom-call | flops 1409286 | bytes 4784 | tf_op jit(solution)/shard_map/share/pallas_call | solution.py:92
  283.2 8.7 %collective-permute-done.22.refs_1_ = bf16[384,1280]{1,0:T(8,128)(2,1)S(1)} collective-permute-done((bf16[384,1280]{1,0:T(8,128)(2,1)S(1)}, bf16[384,1280]{1,0:T(8,128)(2,1)S(1)}, u32[]{:S(2)}, u32[]{:S(2)}) %collective-permute-start.22) | collective-permute-done | bytes 983072 | tf_op jit(solution)/shard_map/ppermute | solution.py:1108
  293.0 8.3 %share.14 = (bf16[768,2304]{1,0:T(8,128)(2,1)S(1)}, f32[8,128]{1,0:T(8,128)S(1)}) custom-call(s32[1]{0:T(128)} %bitcast.11.refs_0_, s32[1]{0:T(128)} %constant.59.clone.1.refs_0_.refs_1_, bf16[1536,1024]{1,0:T(8,128)(2,1)S(1)} %copy-done.12, bf16[1024,2240]{1,0:T(8,128)(2,1)S(1)} %bitcast.59, bf16[768,2304]{1,0:T(8,128)(2,1)} %collective-permute-done.21.refs_4_, ...), custom_call_target="tpu_custom_call" | custom-call | flops 3623878 | bytes 9830 | tf_op jit(solution)/shard_map/share/pallas_call | solution.py:92
  309.3 3.3 copy-done.10
  312.6 5.4 %narrow.15 = (bf16[256,1536]{1,0:T(8,128)(2,1)S(1)}, bf16[256,1536]{1,0:T(8,128)(2,1)S(1)}, f32[8,128]{1,0:T(8,128)S(1)}) custom-call(bf16[1024,2240]{1,0:T(8,128)(2,1)S(1)} %copy-done.4, bf16[2240,1536]{1,0:T(8,128)(2,1)S(1)} %bitcast.67, bf16[256,1536]{1,0:T(8,128)(2,1)S(1)} %collective-permute-done.19.refs_2_, ...), custom_call_target="tpu_custom_call" | custom-call | flops 3523215 | bytes 10747 | tf_op jit(solution)/shard_map/narrow/pallas_call | solution.py:92
  318.0 6.4 %collective-permute-done.30.refs_6_ = bf16[256,1536]{1,0:T(8,128)(2,1)S(1)} collective-permute-done((bf16[256,1536]{1,0:T(8,128)(2,1)}, bf16[256,1536]{1,0:T(8,128)(2,1)S(1)}, u32[]{:S(2)}, u32[]{:S(2)}) %collective-permute-start.30) | collective-permute-done | bytes 786464 | tf_op jit(solution)/shard_map/ppermute | solution.py:52
  324.4 16.0 %collective-permute-done.31.refs_7_ = bf16[256,1536]{1,0:T(8,128)(2,1)S(1)} collective-permute-done((bf16[256,1536]{1,0:T(8,128)(2,1)}, bf16[256,1536]{1,0:T(8,128)(2,1)S(1)}, u32[]{:S(2)}, u32[]{:S(2)}) %collective-permute-start.31) | collective-permute-done | bytes 786464 | tf_op jit(solution)/shard_map/ppermute | solution.py:52
  348.3 4.1 collective-permute-start.34
  352.4 3.0 place.2
  355.4 4.8 collective-permute-done.29.refs_4_
  360.2 5.4 %share.15 = (bf16[384,1536]{1,0:T(8,128)(2,1)}, bf16[384,1536]{1,0:T(8,128)(2,1)S(1)}, f32[8,128]{1,0:T(8,128)S(1)}) custom-call(s32[1]{0:T(128)} %bitcast.11.refs_0_, s32[4]{0:T(128)S(1)} %pad_add_fusion.refs_1_, bf16[1536,1024]{1,0:T(8,128)(2,1)S(1)} %copy-done.12, bf16[1024,2240]{1,0:T(8,128)(2,1)S(1)} %bitcast.49, ...), custom_call_target="tpu_custom_call" | custom-call | flops 2415919 | bytes 7077 | tf_op jit(solution)/shard_map/share/pallas_call | solution.py:92
  365.7 27.1 %collective-permute-done.34.refs_6_.refs_2_ = bf16[192,1280]{1,0:T(8,128)(2,1)S(1)} collective-permute-done((bf16[192,1280]{1,0:T(8,128)(2,1)S(1)}, bf16[192,1280]{1,0:T(8,128)(2,1)S(1)}, u32[]{:S(2)}, u32[]{:S(2)}) %collective-permute-start.34) | collective-permute-done | bytes 491552 | tf_op jit(solution)/shard_map/ppermute | solution.py:1113
  405.7 7.1 %share.16 = (bf16[384,896]{1,0:T(8,128)(2,1)S(1)}, bf16[384,896]{1,0:T(8,128)(2,1)S(1)}, f32[8,128]{1,0:T(8,128)S(1)}) custom-call(s32[1]{0:T(128)} %bitcast.11.refs_0_, s32[4]{0:T(128)S(1)} %pad_add_fusion.refs_1_, bf16[1536,1024]{1,0:T(8,128)(2,1)S(1)} %copy-done.30, bf16[1536,1024]{1,0:T(8,128)(2,1)S(1)} %copy-done.32, bf16[1024,512]{1,0:T(8,128)(2,1)S(1)} %copy-done.24, ...), custom_call_target="tpu_custom_call" | custom-call | flops 1409286 | bytes 4784 | tf_op jit(solution)/shard_map/share/pallas_call | solution.py:92
  413.0 4.4 place.3
  422.0 7.3 %collective-permute-done.41.refs_6_.refs_4_ = bf16[192,1024]{1,0:T(8,128)(2,1)S(1)} collective-permute-done((bf16[192,1024]{1,0:T(8,128)(2,1)S(1)}, bf16[192,1024]{1,0:T(8,128)(2,1)S(1)}, u32[]{:S(2)}, u32[]{:S(2)}) %collective-permute-start.41) | collective-permute-done | bytes 393248 | tf_op jit(solution)/shard_map/ppermute | solution.py:1134
  429.3 4.1 share.17
  439.0 3.8 finish.4
  442.8 15.8 %collective-permute-done.43.refs_1_.refs_4_ = bf16[384,768]{1,0:T(8,128)(2,1)S(1)} collective-permute-done((bf16[384,768]{1,0:T(8,128)(2,1)S(1)}, bf16[384,768]{1,0:T(8,128)(2,1)S(1)}, u32[]{:S(2)}, u32[]{:S(2)}) %collective-permute-start.43) | collective-permute-done | bytes 589856 | tf_op jit(solution)/shard_map/ppermute | solution.py:1108
  463.5 3.7 finish.5
  467.2 17.4 %collective-permute-done.42.refs_2_ = bf16[192,896]{1,0:T(8,128)(2,1)S(1)} collective-permute-done((bf16[192,896]{1,0:T(8,128)(2,1)}, bf16[192,896]{1,0:T(8,128)(2,1)S(1)}, u32[]{:S(2)}, u32[]{:S(2)}) %collective-permute-start.42) | collective-permute-done | bytes 344096 | tf_op jit(solution)/shard_map/ppermute | solution.py:1113
  489.5 5.4 %finish.7 = (f32[192,2240]{1,0:T(8,128)}, f32[192,128]{1,0:T(8,128)S(1)}, f32[8,128]{1,0:T(8,128)}) custom-call(bf16[384,1536]{1,0:T(8,128)(2,1)S(1)} %copy-done.47, bf16[384,1536]{1,0:T(8,128)(2,1)} %collective-permute-done.40.refs_1_, bf16[192,1536]{1,0:T(8,128)(2,1)S(1)} %collective-permute-done.47.refs_2_, bf16[384,768]{1,0:T(8,128)(2,1)S(1)} %copy-done.73, ...), custom_call_target="tpu_custom_call" | custom-call | bytes 6021 | tf_op jit(solution)/shard_map/finish/pallas_call | solution.py:92
  499.0 4.6 collective-permute-done.50
  (382 shorter events, 147.3 us)
Async XLA Ops:
  7.2 390.2 %reduce-scatter.3.cloned.1.call-start = ((), (), s32[]{:S(2)}) async-start(), calls=%async_computation.2 | async-start | bytes 3932160 | tf_op jit(solution)/shard_map/reduce_scatter | solution.py:1128
  23.4 11.1 %collective-permute-start.1 = (bf16[2,512,128]{2,1,0:T(8,128)(2,1)S(1)}, bf16[2,512,128]{2,1,0:T(8,128)(2,1)}, u32[]{:S(2)}, u32[]{:S(2)}) collective-permute-start(bf16[2,512,128]{2,1,0:T(8,128)(2,1)S(1)} %bitcast.79), channel_id=1, source_target_pairs={{0,4},{4,8},{8,12},{1,5},{5,9},{9,13},{2,6},{6,10},{10,14},{3,7},{... | collective-permute-start | bytes 786440 | tf_op jit(solution)/shard_map/ppermute | solution.py:66
  29.0 9.8 %collective-permute-start = (bf16[2,512,128]{2,1,0:T(8,128)(2,1)S(1)}, bf16[2,512,128]{2,1,0:T(8,128)(2,1)}, u32[]{:S(2)}, u32[]{:S(2)}) collective-permute-start(bf16[2,512,128]{2,1,0:T(8,128)(2,1)S(1)} %bitcast.80), channel_id=1, source_target_pairs={{0,8},{4,12},{1,9},{5,13},{2,10},{6,14},{3,11},{7,15},{16,24},{20,... | collective-permute-start | bytes 786440 | tf_op jit(solution)/shard_map/ppermute | solution.py:66
  33.5 5.5 %collective-permute-start.4 = (bf16[2,512,128]{2,1,0:T(8,128)(2,1)S(1)}, bf16[2,512,128]{2,1,0:T(8,128)(2,1)}, u32[]{:S(2)}, u32[]{:S(2)}) collective-permute-start(bf16[2,512,128]{2,1,0:T(8,128)(2,1)S(1)} %bitcast.81), channel_id=1, source_target_pairs={{0,1},{1,0},{2,3},{3,2},{4,5},{5,4},{6,7},{7,6},{8,9},{9,8},{10,11... | collective-permute-start | bytes 786440 | tf_op jit(solution)/shard_map/ppermute | solution.py:48
  34.5 4.5 collective-permute-start.3
  50.1 2.4 collective-permute-start.5
  50.3 3.3 collective-permute-start.6
  57.0 35.8 %collective-permute-start.7 = (bf16[256,1536]{1,0:T(8,128)(2,1)}, bf16[256,1536]{1,0:T(8,128)(2,1)}, u32[]{:S(2)}, u32[]{:S(2)}) collective-permute-start(bf16[256,1536]{1,0:T(8,128)(2,1)} %get-tuple-element.142.refs_3_), channel_id=1, source_target_pairs={{0,2},{1,3},{2,0},{3,1},{4,6},{5,7},{6,4},{7,5},{8,10},{9,11},{10,... | collective-permute-start | bytes 2359304 | tf_op jit(solution)/shard_map/ppermute | solution.py:52
  58.5 35.3 %collective-permute-start.8 = (bf16[256,1536]{1,0:T(8,128)(2,1)}, bf16[256,1536]{1,0:T(8,128)(2,1)}, u32[]{:S(2)}, u32[]{:S(2)}) collective-permute-start(bf16[256,1536]{1,0:T(8,128)(2,1)} %get-tuple-element.143.refs_4_), channel_id=1, source_target_pairs={{0,2},{1,3},{2,0},{3,1},{4,6},{5,7},{6,4},{7,5},{8,10},{9,11},{10,... | collective-permute-start | bytes 2359304 | tf_op jit(solution)/shard_map/ppermute | solution.py:52
  97.7 2.4 collective-permute-start.9
  97.7 3.4 collective-permute-start.10
  134.5 327.8 %reduce-scatter.5.cloned.1.call-start = ((), (), s32[]{:S(2)}) async-start(), calls=%async_computation.3 | async-start | bytes 4423680 | tf_op jit(solution)/shard_map/reduce_scatter | solution.py:1147
  143.3 54.2 %collective-permute-start.15 = (bf16[768,1280]{1,0:T(8,128)(2,1)}, bf16[768,1280]{1,0:T(8,128)(2,1)}, u32[]{:S(2)}, u32[]{:S(2)}) collective-permute-start(bf16[768,1280]{1,0:T(8,128)(2,1)} %get-tuple-element.167), channel_id=1, source_target_pairs={{0,16},{16,0},{1,17},{17,1},{2,18},{18,2},{3,19},{19,3},{4,20},{20... | collective-permute-start | bytes 5898248 | tf_op jit(solution)/shard_map/ppermute | solution.py:1103
  160.4 3.4 collective-permute-start.12
  178.1 29.6 %collective-permute-start.13 = (bf16[256,1536]{1,0:T(8,128)(2,1)}, bf16[256,1536]{1,0:T(8,128)(2,1)S(1)}, u32[]{:S(2)}, u32[]{:S(2)}) collective-permute-start(bf16[256,1536]{1,0:T(8,128)(2,1)} %get-tuple-element.165.refs_4_), channel_id=1, source_target_pairs={{0,2},{1,3},{2,0},{3,1},{4,6},{5,7},{6,4},{7,5},{8,10},{9,11},{10,... | collective-permute-start | bytes 2359304 | tf_op jit(solution)/shard_map/ppermute | solution.py:52
  179.6 35.2 %collective-permute-start.14 = (bf16[256,1536]{1,0:T(8,128)(2,1)}, bf16[256,1536]{1,0:T(8,128)(2,1)}, u32[]{:S(2)}, u32[]{:S(2)}) collective-permute-start(bf16[256,1536]{1,0:T(8,128)(2,1)} %get-tuple-element.166.refs_5_), channel_id=1, source_target_pairs={{0,2},{1,3},{2,0},{3,1},{4,6},{5,7},{6,4},{7,5},{8,10},{9,11},{10,... | collective-permute-start | bytes 2359304 | tf_op jit(solution)/shard_map/ppermute | solution.py:52
  196.8 96.2 %collective-permute-start.21 = (bf16[768,2304]{1,0:T(8,128)(2,1)}, bf16[768,2304]{1,0:T(8,128)(2,1)}, u32[]{:S(2)}, u32[]{:S(2)}) collective-permute-start(bf16[768,2304]{1,0:T(8,128)(2,1)} %get-tuple-element.186), channel_id=1, source_target_pairs={{0,16},{16,0},{1,17},{17,1},{2,18},{18,2},{3,19},{19,3},{4,20},{20... | collective-permute-start | bytes 10616840 | tf_op jit(solution)/shard_map/ppermute | solution.py:1103
  219.0 3.4 collective-permute-start.17
  235.9 25.0 %collective-permute-start.23 = (bf16[2,512,128]{2,1,0:T(8,128)(2,1)S(1)}, bf16[2,512,128]{2,1,0:T(8,128)(2,1)S(1)}, u32[]{:S(2)}, u32[]{:S(2)}) collective-permute-start(bf16[2,512,128]{2,1,0:T(8,128)(2,1)S(1)} %get-tuple-element.192), channel_id=1, source_target_pairs={{4,0},{8,4},{12,8},{5,1},{9,5},{13,9},{6,2},{10,6},{14,10},{7,3},{... | collective-permute-start | bytes 786440 | tf_op jit(solution)/shard_map/ppermute | solution.py:66
  261.0 11.1 %collective-permute-start.24 = (bf16[2,512,128]{2,1,0:T(8,128)(2,1)S(1)}, bf16[2,512,128]{2,1,0:T(8,128)(2,1)S(1)}, u32[]{:S(2)}, u32[]{:S(2)}) collective-permute-start(bf16[2,512,128]{2,1,0:T(8,128)(2,1)S(1)} %get-tuple-element.194), channel_id=1, source_target_pairs={{4,0},{8,4},{12,8},{5,1},{9,5},{13,9},{6,2},{10,6},{14,10},{7,3},{... | collective-permute-start | bytes 786440 | tf_op jit(solution)/shard_map/ppermute | solution.py:66
  262.6 29.3 %collective-permute-start.22 = (bf16[384,1280]{1,0:T(8,128)(2,1)S(1)}, bf16[384,1280]{1,0:T(8,128)(2,1)S(1)}, u32[]{:S(2)}, u32[]{:S(2)}) collective-permute-start(bf16[384,1280]{1,0:T(8,128)(2,1)S(1)} %get-tuple-element.188), channel_id=1, source_target_pairs={{0,4},{4,0},{8,12},{12,8},{1,5},{5,1},{9,13},{13,9},{2,6},{6,2},{1... | collective-permute-start | bytes 2949128 | tf_op jit(solution)/shard_map/ppermute | solution.py:1108
  275.0 5.9 %collective-permute-start.25 = (bf16[256,1536]{1,0:T(8,128)(2,1)S(1)}, bf16[256,1536]{1,0:T(8,128)(2,1)S(1)}, u32[]{:S(2)}, u32[]{:S(2)}) collective-permute-start(bf16[256,1536]{1,0:T(8,128)(2,1)S(1)} %get-tuple-element.198), channel_id=1, source_target_pairs={{0,1},{1,0},{2,3},{3,2},{4,5},{5,4},{6,7},{7,6},{8,9},{9,8},{10,11... | collective-permute-start | bytes 2359304 | tf_op jit(solution)/shard_map/ppermute | solution.py:48
  275.0 5.9 %collective-permute-start.26 = (bf16[256,1536]{1,0:T(8,128)(2,1)S(1)}, bf16[256,1536]{1,0:T(8,128)(2,1)S(1)}, u32[]{:S(2)}, u32[]{:S(2)}) collective-permute-start(bf16[256,1536]{1,0:T(8,128)(2,1)S(1)} %get-tuple-element.199), channel_id=1, source_target_pairs={{0,1},{1,0},{2,3},{3,2},{4,5},{5,4},{6,7},{7,6},{8,9},{9,8},{10,11... | collective-permute-start | bytes 2359304 | tf_op jit(solution)/shard_map/ppermute | solution.py:48
  303.2 2.6 collective-permute-start.19
  303.3 3.6 collective-permute-start.20
  303.8 20.6 %collective-permute-start.30 = (bf16[256,1536]{1,0:T(8,128)(2,1)}, bf16[256,1536]{1,0:T(8,128)(2,1)S(1)}, u32[]{:S(2)}, u32[]{:S(2)}) collective-permute-start(bf16[256,1536]{1,0:T(8,128)(2,1)} %copy-done.78), channel_id=1, source_target_pairs={{0,2},{1,3},{2,0},{3,1},{4,6},{5,7},{6,4},{7,5},{8,10},{9,11},{10,... | collective-permute-start | bytes 2359304 | tf_op jit(solution)/shard_map/ppermute | solution.py:52
  305.3 35.1 %collective-permute-start.31 = (bf16[256,1536]{1,0:T(8,128)(2,1)}, bf16[256,1536]{1,0:T(8,128)(2,1)S(1)}, u32[]{:S(2)}, u32[]{:S(2)}) collective-permute-start(bf16[256,1536]{1,0:T(8,128)(2,1)} %copy-done.80), channel_id=1, source_target_pairs={{0,2},{1,3},{2,0},{3,1},{4,6},{5,7},{6,4},{7,5},{8,10},{9,11},{10,... | collective-permute-start | bytes 2359304 | tf_op jit(solution)/shard_map/ppermute | solution.py:52
  305.8 54.4 %collective-permute-start.29 = (bf16[768,1536]{1,0:T(8,128)(2,1)}, bf16[768,1536]{1,0:T(8,128)(2,1)S(1)}, u32[]{:S(2)}, u32[]{:S(2)}) collective-permute-start(bf16[768,1536]{1,0:T(8,128)(2,1)} %copy-done.82), channel_id=1, source_target_pairs={{0,16},{16,0},{1,17},{17,1},{2,18},{18,2},{3,19},{19,3},{4,20},{20... | collective-permute-start | bytes 7077896 | tf_op jit(solution)/shard_map/ppermute | solution.py:1103
  342.5 3.5 collective-permute-start.32
  342.6 5.6 %collective-permute-start.33 = (f32[256,1536]{1,0:T(8,128)S(1)}, f32[256,1536]{1,0:T(8,128)S(1)}, u32[]{:S(2)}, u32[]{:S(2)}) collective-permute-start(f32[256,1536]{1,0:T(8,128)S(1)} %get-tuple-element.215.refs_2_), channel_id=1, source_target_pairs={{0,1},{1,0},{2,3},{3,2},{4,5},{5,4},{6,7},{7,6},{8,9},{9,8},{10,11... | collective-permute-start | bytes 4718600 | tf_op jit(solution)/shard_map/ppermute | solution.py:48
  343.1 51.2 %collective-permute-start.27 = (bf16[256,1536]{1,0:T(8,128)(2,1)S(1)}, bf16[256,1536]{1,0:T(8,128)(2,1)S(1)}, u32[]{:S(2)}, u32[]{:S(2)}) collective-permute-start(bf16[256,1536]{1,0:T(8,128)(2,1)S(1)} %get-tuple-element.207.refs_1_), channel_id=1, source_target_pairs={{0,2},{1,3},{2,0},{3,1},{4,6},{5,7},{6,4},{7,5},{8,10},{9,11},{10,... | collective-permute-start | bytes 2359304 | tf_op jit(solution)/shard_map/ppermute | solution.py:52
  344.6 49.7 %collective-permute-start.28 = (bf16[256,1536]{1,0:T(8,128)(2,1)S(1)}, bf16[256,1536]{1,0:T(8,128)(2,1)S(1)}, u32[]{:S(2)}, u32[]{:S(2)}) collective-permute-start(bf16[256,1536]{1,0:T(8,128)(2,1)S(1)} %get-tuple-element.208.refs_2_), channel_id=1, source_target_pairs={{0,2},{1,3},{2,0},{3,1},{4,6},{5,7},{6,4},{7,5},{8,10},{9,11},{10,... | collective-permute-start | bytes 2359304 | tf_op jit(solution)/shard_map/ppermute | solution.py:52
  346.0 52.6 %collective-permute-start.37 = (bf16[768,896]{1,0:T(8,128)(2,1)}, bf16[768,896]{1,0:T(8,128)(2,1)}, u32[]{:S(2)}, u32[]{:S(2)}) collective-permute-start(bf16[768,896]{1,0:T(8,128)(2,1)} %get-tuple-element.222), channel_id=1, source_target_pairs={{0,16},{16,0},{1,17},{17,1},{2,18},{18,2},{3,19},{19,3},{4,20},{20... | collective-permute-start | bytes 4128776 | tf_op jit(solution)/shard_map/ppermute | solution.py:1103
  348.3 44.5 %collective-permute-start.34 = (bf16[192,1280]{1,0:T(8,128)(2,1)S(1)}, bf16[192,1280]{1,0:T(8,128)(2,1)S(1)}, u32[]{:S(2)}, u32[]{:S(2)}) collective-permute-start(bf16[192,1280]{1,0:T(8,128)(2,1)S(1)} %copy-done.86), channel_id=1, source_target_pairs={{0,8},{4,12},{8,0},{12,4},{1,9},{5,13},{9,1},{13,5},{2,10},{6,14},... | collective-permute-start | bytes 1474568 | tf_op jit(solution)/shard_map/ppermute | solution.py:1113
  365.7 51.7 %collective-permute-start.40 = (bf16[384,1536]{1,0:T(8,128)(2,1)}, bf16[384,1536]{1,0:T(8,128)(2,1)}, u32[]{:S(2)}, u32[]{:S(2)}) collective-permute-start(bf16[384,1536]{1,0:T(8,128)(2,1)} %get-tuple-element.231), channel_id=1, source_target_pairs={{0,4},{4,0},{8,12},{12,8},{1,5},{5,1},{9,13},{13,9},{2,6},{6,2},{1... | collective-permute-start | bytes 3538952 | tf_op jit(solution)/shard_map/ppermute | solution.py:1108
  392.8 29.2 %collective-permute-start.39 = (bf16[768,768]{1,0:T(8,128)(2,1)}, bf16[768,768]{1,0:T(8,128)(2,1)}, u32[]{:S(2)}, u32[]{:S(2)}) collective-permute-start(bf16[768,768]{1,0:T(8,128)(2,1)} %get-tuple-element.229), channel_id=1, source_target_pairs={{0,16},{16,0},{1,17},{17,1},{2,18},{18,2},{3,19},{19,3},{4,20},{20... | collective-permute-start | bytes 3538952 | tf_op jit(solution)/shard_map/ppermute | solution.py:1103
  396.9 16.0 %collective-permute-start.35 = (bf16[256,1536]{1,0:T(8,128)(2,1)}, bf16[256,1536]{1,0:T(8,128)(2,1)}, u32[]{:S(2)}, u32[]{:S(2)}) collective-permute-start(bf16[256,1536]{1,0:T(8,128)(2,1)} %get-tuple-element.220.refs_1_), channel_id=1, source_target_pairs={{0,1},{1,0},{2,3},{3,2},{4,5},{5,4},{6,7},{7,6},{8,9},{9,8},{10,11... | collective-permute-start | bytes 2359304 | tf_op jit(solution)/shard_map/ppermute | solution.py:48
  396.9 16.1 %collective-permute-start.36 = (bf16[256,1536]{1,0:T(8,128)(2,1)}, bf16[256,1536]{1,0:T(8,128)(2,1)}, u32[]{:S(2)}, u32[]{:S(2)}) collective-permute-start(bf16[256,1536]{1,0:T(8,128)(2,1)} %get-tuple-element.221.refs_2_), channel_id=1, source_target_pairs={{0,1},{1,0},{2,3},{3,2},{4,5},{5,4},{6,7},{7,6},{8,9},{9,8},{10,11... | collective-permute-start | bytes 2359304 | tf_op jit(solution)/shard_map/ppermute | solution.py:48
  398.6 30.7 %collective-permute-start.41 = (bf16[192,1024]{1,0:T(8,128)(2,1)S(1)}, bf16[192,1024]{1,0:T(8,128)(2,1)S(1)}, u32[]{:S(2)}, u32[]{:S(2)}) collective-permute-start(bf16[192,1024]{1,0:T(8,128)(2,1)S(1)} %get-tuple-element.259), channel_id=1, source_target_pairs={{0,16},{16,0},{1,17},{17,1},{2,18},{18,2},{3,19},{19,3},{4,20},{20... | collective-permute-start | bytes 1179656 | tf_op jit(solution)/shard_map/ppermute | solution.py:1134
  412.9 22.3 %collective-permute-start.38 = (bf16[384,896]{1,0:T(8,128)(2,1)S(1)}, bf16[384,896]{1,0:T(8,128)(2,1)S(1)}, u32[]{:S(2)}, u32[]{:S(2)}) collective-permute-start(bf16[384,896]{1,0:T(8,128)(2,1)S(1)} %get-tuple-element.228), channel_id=1, source_target_pairs={{0,4},{4,0},{8,12},{12,8},{1,5},{5,1},{9,13},{13,9},{2,6},{6,2},{1... | collective-permute-start | bytes 2064392 | tf_op jit(solution)/shard_map/ppermute | solution.py:1108
  433.4 25.1 %collective-permute-start.43 = (bf16[384,768]{1,0:T(8,128)(2,1)S(1)}, bf16[384,768]{1,0:T(8,128)(2,1)S(1)}, u32[]{:S(2)}, u32[]{:S(2)}) collective-permute-start(bf16[384,768]{1,0:T(8,128)(2,1)S(1)} %get-tuple-element.239), channel_id=1, source_target_pairs={{0,4},{4,0},{8,12},{12,8},{1,5},{5,1},{9,13},{13,9},{2,6},{6,2},{1... | collective-permute-start | bytes 1769480 | tf_op jit(solution)/shard_map/ppermute | solution.py:1108
  433.5 54.0 %collective-permute-start.47 = (bf16[192,1536]{1,0:T(8,128)(2,1)}, bf16[192,1536]{1,0:T(8,128)(2,1)S(1)}, u32[]{:S(2)}, u32[]{:S(2)}) collective-permute-start(bf16[192,1536]{1,0:T(8,128)(2,1)} %get-tuple-element.251), channel_id=1, source_target_pairs={{0,8},{4,12},{8,0},{12,4},{1,9},{5,13},{9,1},{13,5},{2,10},{6,14},... | collective-permute-start | bytes 1769480 | tf_op jit(solution)/shard_map/ppermute | solution.py:1113
  436.2 48.4 %collective-permute-start.42 = (bf16[192,896]{1,0:T(8,128)(2,1)}, bf16[192,896]{1,0:T(8,128)(2,1)S(1)}, u32[]{:S(2)}, u32[]{:S(2)}) collective-permute-start(bf16[192,896]{1,0:T(8,128)(2,1)} %get-tuple-element.236), channel_id=1, source_target_pairs={{0,8},{4,12},{8,0},{12,4},{1,9},{5,13},{9,1},{13,5},{2,10},{6,14},... | collective-permute-start | bytes 1032200 | tf_op jit(solution)/shard_map/ppermute | solution.py:1113
  437.4 5.3 %collective-permute-start.44 = (f32[8,512]{1,0:T(8,128)S(1)}, f32[8,512]{1,0:T(8,128)S(1)}, u32[]{:S(2)}, u32[]{:S(2)}) collective-permute-start(f32[8,512]{1,0:T(8,128)S(1)} %get-tuple-element.240.refs_0_), channel_id=1, source_target_pairs={{0,16},{16,0},{1,17},{17,1},{2,18},{18,2},{3,19},{19,3},{4,20},{20... | collective-permute-start | bytes 49160 | tf_op jit(solution)/shard_map/ppermute | solution.py:1237
  459.3 30.1 %collective-permute-start.48 = (bf16[192,768]{1,0:T(8,128)(2,1)}, bf16[192,768]{1,0:T(8,128)(2,1)S(1)}, u32[]{:S(2)}, u32[]{:S(2)}) collective-permute-start(bf16[192,768]{1,0:T(8,128)(2,1)} %get-tuple-element.252), channel_id=1, source_target_pairs={{0,8},{4,12},{8,0},{12,4},{1,9},{5,13},{9,1},{13,5},{2,10},{6,14},... | collective-permute-start | bytes 884744 | tf_op jit(solution)/shard_map/ppermute | solution.py:1113
  459.8 26.5 %collective-permute-start.45 = (f32[8,512]{1,0:T(8,128)S(1)}, f32[8,512]{1,0:T(8,128)S(1)}, u32[]{:S(2)}, u32[]{:S(2)}) collective-permute-start(f32[8,512]{1,0:T(8,128)S(1)} %get-tuple-element.247.refs_0_), channel_id=1, source_target_pairs={{0,4},{4,0},{8,12},{12,8},{1,5},{5,1},{9,13},{13,9},{2,6},{6,2},{1... | collective-permute-start | bytes 49160 | tf_op jit(solution)/shard_map/ppermute | solution.py:1239
  486.3 8.7 %collective-permute-start.46 = (f32[8,512]{1,0:T(8,128)S(1)}, f32[8,512]{1,0:T(8,128)S(1)}, u32[]{:S(2)}, u32[]{:S(2)}) collective-permute-start(f32[8,512]{1,0:T(8,128)S(1)} %get-tuple-element.249), channel_id=1, source_target_pairs={{0,8},{4,12},{8,0},{12,4},{1,9},{5,13},{9,1},{13,5},{2,10},{6,14},... | collective-permute-start | bytes 49160 | tf_op jit(solution)/shard_map/ppermute | solution.py:1246
  496.4 7.2 %collective-permute-start.50 = (f32[2,200,128]{2,1,0:T(8,128)S(1)}, f32[2,200,128]{2,1,0:T(8,128)S(1)}, u32[]{:S(2)}, u32[]{:S(2)}) collective-permute-start(f32[2,200,128]{2,1,0:T(8,128)S(1)} %maximum_select_fusion.1), channel_id=1, source_target_pairs={{0,2},{1,3},{2,0},{3,1},{4,6},{5,7},{6,4},{7,5},{8,10},{9,11},{10,... | collective-permute-start | bytes 614408 | tf_op jit(solution)/shard_map/ppermute | solution.py:52
  (112 other events, 1407.0 us)
Sparse Core Ops, SparseCore 0:
  134.7 73.6 reduce-scatter.2
  303.4 87.0 reduce-scatter.4

commit v7 on v6

--- a/solution.py
+++ b/solution.py
@@ -20,6 +20,7 @@
 LIGHT = 1000
 TILE = 256
 PIECES = 2
+LARGE = MIB
 SCALE = 1.0 / math.sqrt(HD)
 
 
@@ -68,6 +69,12 @@
 
 def cost(flops, read):
     return pl.CostEstimate(flops=flops // LIGHT, bytes_accessed=read // LIGHT, transcendentals=0)
+
+
+def placed(shape):
+    if math.prod(shape.shape) * shape.dtype.itemsize < LARGE:
+        return shape
+    return pltpu.HBM(shape.shape, shape.dtype)
 
 
 class Order:
@@ -98,7 +105,7 @@
                 out_specs=list(out_specs) + [mark_spec()],
                 scratch_shapes=list(scratch),
             ),
-            out_shape=list(out_shape) + [MARK],
+            out_shape=[placed(shape) for shape in out_shape] + [MARK],
             compiler_params=pltpu.CompilerParams(vmem_limit_bytes=32 * MIB),
             cost_estimate=cost(flops, read),
             name=name,
@@ -241,7 +248,7 @@
     return [near] * pieces + [far] * pieces
 
 
-def attend(low, core, q, start, span, mate):
+def attend(order, low, core, q, start, span, mate):
     rows, local, columns = q.shape
     pieces = len(span)
     heads = columns // HD
@@ -250,30 +257,26 @@
     def at(i, *refs):
         return (i, 0, 0)
 
-    return pl.pallas_call(
+    return order(
         functools.partial(attend_kernel, heads, blocks, pieces),
-        grid_spec=pltpu.PrefetchScalarGridSpec(
-            num_scalar_prefetch=2,
-            grid=(rows,),
-            in_specs=[pl.BlockSpec((1, local, columns), at), pl.BlockSpec((1, 1, local), at)]
-            + span_specs(rows, local, pieces),
-            out_specs=[
-                pl.BlockSpec((1, local, columns), at),
-                pl.BlockSpec((1, blocks, heads * Q_BLOCK), at),
-            ],
-            scratch_shapes=[
-                pltpu.VMEM((HD, heads * Q_BLOCK), jnp.float32),
-                pltpu.VMEM((2, pieces * local, HD), jnp.bfloat16),
-            ],
-        ),
-        out_shape=[
+        [q, start, *span, *mate],
+        [pl.BlockSpec((1, local, columns), at), pl.BlockSpec((1, 1, local), at)]
+        + span_specs(rows, local, pieces),
+        [pl.BlockSpec((1, local, columns), at), pl.BlockSpec((1, blocks, heads * Q_BLOCK), at)],
+        [
             jax.ShapeDtypeStruct((rows, local, columns), jnp.bfloat16),
             jax.ShapeDtypeStruct((rows, blocks, heads * Q_BLOCK), jnp.float32),
         ],
-        compiler_params=pltpu.CompilerParams(vmem_limit_bytes=32 * MIB),
-        cost_estimate=cost(8_000_000_000, 4 * MIB),
-        name="attend",
-    )(low, core, q, start, *span, *mate)
+        (rows,),
+        8_000_000_000,
+        4 * MIB,
+        "attend",
+        scalars=(low, core),
+        scratch=[
+            pltpu.VMEM((HD, heads * Q_BLOCK), jnp.float32),
+            pltpu.VMEM((2, pieces * local, HD), jnp.bfloat16),
+        ],
+    )
 
 
 def attend_back_kernel(
@@ -575,10 +578,8 @@
 
 def gated_kernel(gh_ref, gw_ref, uw_ref, *refs):
     hid_ref, gg_ref, gu_ref = refs[-3:]
-    rows = refs[0].shape[0]
-    for part, ref in enumerate(refs[:-3]):
-        here = slice(part * rows, (part + 1) * rows)
-        h = ref[...]
+    for here in (slice(0, hid_ref.shape[0]),):
+        h = jnp.concatenate([ref[...] for ref in refs[:-3]], axis=0)
         gate = dot(h, gw_ref[...], 1, 1)
         up = dot(h, uw_ref[...], 1, 1)
         grad = to_f(gh_ref[here])
@@ -589,7 +590,7 @@
         gg_ref[here] = to_bf(grad * up * sigma * (1.0 + gate * (1.0 - sigma)))
 
 
-def gated(order, pieces, grad_hidden, gate_weight, up_weight):
+def gated(order, pieces, grad_hidden, index, gate_weight, up_weight):
     rows, width = pieces[0].shape
     total = rows * len(pieces)
     hidden = gate_weight.shape[0]
@@ -599,7 +600,8 @@
     return order(
         gated_kernel,
         [grad_hidden, gate_weight, up_weight, *pieces],
-        [column, weight, weight] + [pl.BlockSpec((rows, width), lambda i: (0, 0))] * len(pieces),
+        [pl.BlockSpec((total, TILE), lambda i: (index, i)), weight, weight]
+        + [pl.BlockSpec((rows, width), lambda i: (0, 0))] * len(pieces),
         [column] * 3,
         [shape] * 3,
         (pl.cdiv(hidden, TILE),),
@@ -611,15 +613,20 @@
 
 def share_kernel(plan, lefts, rights, extra, halves, groups, pick_ref, blocks_ref, *refs):
     step = pl.program_id(0)
-    left_refs, right_refs = refs[:lefts], refs[lefts : lefts + rights]
-    refs = refs[lefts + rights :]
+    left_refs, refs = refs[:lefts], refs[lefts:]
+    right_refs = []
+    for count in rights:
+        right_refs.append(refs[:count])
+        refs = refs[count:]
     if extra:
         extra_ref, refs = refs[0], refs[1:]
     for left, right, begin, end, shift, columns, target in plan:
 
         @pl.when((step >= begin) & (step < end))
         def _(left=left, right=right, shift=shift, columns=columns, target=target):
-            out = dot(left_refs[left][...], right_refs[right][...])
+            out = dot(
+                left_refs[left][...], jnp.concatenate([ref[...] for ref in right_refs[right]], axis=0)
+            )
             if extra:
                 out = out + to_f(extra_ref[...])
             tile = out.shape[1]
@@ -654,7 +661,7 @@
     plan, at = [], 0
     starts, sizes, right_at = {}, {}, {}
     for left, right, skip, count, target in parts:
-        plan.append((left, right, at, at + count, skip - at, rights[right].shape[1], target))
+        plan.append((left, right, at, at + count, skip - at, rights[right][0].shape[1], target))
         starts.setdefault(target, at)
         sizes[target] = sizes.get(target, 0) + count
         first, tiles, low = right_at.get(right, (at, 0, skip))
@@ -673,10 +680,10 @@
         shapes = [jax.ShapeDtypeStruct((part // 2, at * tile), jnp.bfloat16)] * 2
         scratch = [pltpu.VMEM((part, tile), jnp.bfloat16)]
     return order(
-        functools.partial(share_kernel, plan, len(lefts), len(rights), len(extras), halves, groups),
-        [*lefts, *rights, *extras],
+        functools.partial(share_kernel, plan, len(lefts), [len(r) for r in rights], len(extras), halves, groups),
+        [*lefts, *[block for right in rights for block in right], *extras],
         [pl.BlockSpec((part, tokens), lambda i, pick_ref, blocks_ref: (pick_ref[0], 0))] * len(lefts)
-        + [clipped(tokens, tile, *right_at[r]) for r in range(len(rights))]
+        + [clipped(block.shape[0], tile, *right_at[r]) for r, right in enumerate(rights) for block in right]
         + [clipped(part, tile, 0, at)] * len(extras),
         outs,
         shapes,
@@ -766,33 +773,41 @@
 
 
 def narrow_kernel(pairs, extras, right_dim, *refs):
-    out = dot(refs[0][...], refs[1][...], 1, right_dim)
-    for i in range(1, pairs):
-        out = out + dot(refs[2 * i][...], refs[2 * i + 1][...], 1, right_dim)
-    extra = refs[2 * pairs : 2 * pairs + extras]
-    outs = refs[2 * pairs + extras :]
+    out = 0.0
+    for i in range(pairs):
+        left = jnp.concatenate([ref[...] for ref in refs[:PIECES]], axis=0)
+        out = out + dot(left, refs[PIECES][...], 1, right_dim)
+        refs = refs[PIECES + 1 :]
+    outs = refs[extras:]
     if extras:
-        out = out + jnp.concatenate([to_f(ref[...]) for ref in extra], axis=0)
+        out = out + jnp.concatenate([to_f(ref[...]) for ref in refs[:extras]], axis=0)
     rows = outs[0].shape[0]
     for i, ref in enumerate(outs):
         ref[...] = to_bf(out[i * rows : (i + 1) * rows])
 
 
-def narrow(order, pairs, index, extra=(), right_dim=0):
-    total, hidden = pairs[0][0].shape
+def narrow(order, pairs, extra=(), right_dim=0):
+    piece = pairs[0][0][0][1]
+    hidden = pairs[0][0][0][0].shape[1]
     width = pairs[0][1].shape[1 - right_dim]
-    half = total // 2
-    piece = half // PIECES
+    half = piece * PIECES
     column = pl.BlockSpec((piece, TILE), lambda i: (0, i))
     right = (
         pl.BlockSpec((TILE, hidden), lambda i: (i, 0))
         if right_dim
         else pl.BlockSpec((hidden, TILE), lambda i: (0, i))
     )
+    args, specs = [], []
+    for lefts, weight in pairs:
+        for array, rows, index in lefts:
+            args.append(array)
+            specs.append(pl.BlockSpec((rows, hidden), lambda i, index=index: (index, 0)))
+        args.append(weight)
+        specs.append(right)
     return order(
         functools.partial(narrow_kernel, len(pairs), len(extra), right_dim),
-        [item for pair in pairs for item in pair] + list(extra),
-        [pl.BlockSpec((half, hidden), lambda i: (index, 0)), right] * len(pairs) + [column] * len(extra),
+        args + list(extra),
+        specs + [column] * len(extra),
         [column] * PIECES,
         [jax.ShapeDtypeStruct((piece, width), jnp.bfloat16)] * PIECES,
         (width // TILE,),
@@ -800,6 +815,15 @@
         2 * len(pairs) * (half + width) * hidden + 2 * half * width,
         "narrow",
     )
+
+
+def half_of(array, index):
+    rows = array.shape[0] // (2 * PIECES)
+    return [(array, rows, index * PIECES + j) for j in range(PIECES)]
+
+
+def sides_of(arrays, index):
+    return [(array, array.shape[0] // 2, index) for array in arrays]
 
 
 def piece_specs(piece, width, block):
@@ -861,8 +885,11 @@
         grad_out_kernel,
         [cotangent, valid],
         [
-            pl.BlockSpec((block, width), lambda i, core_ref: (lax.rem(i + core_ref[0] * 2, 4), 0)),
-            pl.BlockSpec((block, 1), lambda i, core_ref: (i, 0)),
+            pl.BlockSpec(
+                (block, width),
+                lambda i, core_ref: (lax.rem(i + core_ref[0], 2) * 2 + lax.div(i, 2), 0),
+            ),
+            pl.BlockSpec((block, 1), lambda i, core_ref: (lax.rem(i, 2) * 2 + lax.div(i, 2), 0)),
         ],
         [
             pl.BlockSpec((block, width), lambda i, core_ref: (i, 0)),
@@ -880,74 +907,83 @@
     )
 
 
-def middle_kernel(core_ref, tok_ref, gain_ref, *refs):
-    mine, come = pick_piece(refs[:PIECES]), pick_piece(refs[PIECES : 2 * PIECES])
-    mid_ref, *h_refs = refs[2 * PIECES :]
-    middle = to_f(tok_ref[...]) + (to_f(mine) + to_f(come))
+def middle_kernel(core_ref, tok_ref, gain_ref, mine_ref, come_ref, mid_ref, *h_refs):
+    middle = to_f(tok_ref[...]) + (to_f(mine_ref[...]) + to_f(come_ref[...]))
     factor = lax.rsqrt(jnp.mean(middle * middle, axis=-1, keepdims=True) + EPS)
     mid_ref[...] = middle
-    put_piece(h_refs, to_bf(middle * factor * gain_ref[...]))
-
-
-def middle_of(order, core, tokens, mine, come, gain):
-    piece, width = mine[0].shape
-    half = piece * PIECES
-    block = half // 4
-    specs = piece_specs(piece, width, block)
-    middle, *h = order(
+    h = to_bf(middle * factor * gain_ref[...])
+    for i, ref in enumerate(h_refs):
+
+        @pl.when(pl.program_id(0) == i)
+        def _(ref=ref):
+            ref[...] = h
+
+
+def middle_of(order, core, tokens, mine, come, gain, index):
+    piece, width = mine.shape
+    block = piece // 2
+    at = pl.BlockSpec((block, width), lambda i, core_ref: (i, 0))
+    return order(
         middle_kernel,
-        [tokens, gain, *mine, *come],
+        [tokens, gain, mine, come],
         [
-            pl.BlockSpec((block, width), lambda i, core_ref: (core_ref[0] * 4 + i, 0)),
+            pl.BlockSpec((block, width), lambda i, core_ref: ((core_ref[0] * PIECES + index) * 2 + i, 0)),
             pl.BlockSpec((1, width), lambda i, core_ref: (0, 0)),
-        ]
-        + specs * 2,
-        [pl.BlockSpec((block, width), lambda i, core_ref: (i, 0))] + specs,
-        [jax.ShapeDtypeStruct((half, width), jnp.float32)]
-        + [jax.ShapeDtypeStruct((piece, width), jnp.bfloat16)] * PIECES,
-        (4,),
+            at,
+            at,
+        ],
+        [at] + [pl.BlockSpec((block, width), lambda i, core_ref: (0, 0))] * 2,
+        [jax.ShapeDtypeStruct((piece, width), jnp.float32)]
+        + [jax.ShapeDtypeStruct((block, width), jnp.bfloat16)] * 2,
+        (2,),
         0,
-        9 * MIB,
+        5 * MIB,
         "middle",
         scalars=(core,),
     )
-    return middle, h
-
-
-def norm_back_kernel(core_ref, x_ref, gain_ref, up_ref, *refs):
+
+
+def norm_back_kernel(last, core_ref, gain_ref, up_ref, *refs):
+    xs = 1 if last else PIECES
+    x, refs = to_f(pick_piece(refs[:xs])), refs[xs:]
     mine, come = pick_piece(refs[:PIECES]), pick_piece(refs[PIECES : 2 * PIECES])
     outs = refs[2 * PIECES :]
     grad = to_f(mine) + to_f(come)
-    x = to_f(x_ref[...])
     factor = lax.rsqrt(jnp.mean(x * x, axis=-1, keepdims=True) + EPS)
     normed = x * factor
     weighted = grad * gain_ref[...]
     inner = jnp.mean(weighted * normed, axis=-1, keepdims=True)
     out = to_f(up_ref[...]) + factor * (weighted - normed * inner)
-    if len(outs) > PIECES:
+    if last:
+        put_piece(outs, out)
+    else:
         outs[0][...] = out
         put_piece(outs[1:], to_bf(out))
-    else:
-        put_piece(outs, out)
-
-
-def norm_back(order, core, mine, come, x, gain, up, by_core):
+
+
+def norm_back(order, core, mine, come, x, gain, up, last):
     piece, width = mine[0].shape
     half = piece * PIECES
     block = half // 4
     at = pl.BlockSpec((block, width), lambda i, core_ref: (i, 0))
-    picked = pl.BlockSpec((block, width), lambda i, core_ref: (core_ref[0] * 4 + i, 0))
+    gain_at = pl.BlockSpec((1, width), lambda i, core_ref: (0, 0))
     specs = piece_specs(piece, width, block)
-    if by_core:
+    steps = piece // block
+    if last:
+        args = [gain, up, x]
+        front = [gain_at, at, pl.BlockSpec((block, width), lambda i, core_ref: (core_ref[0] * 4 + i, 0))]
         shapes = [jax.ShapeDtypeStruct((piece, width), jnp.float32)] * PIECES
     else:
+        args = [gain, up, *x]
+        between = pl.BlockSpec((block, width), lambda i, core_ref: (i + lax.div(i, steps) * steps, 0))
+        front = [gain_at, between] + specs
         shapes = [jax.ShapeDtypeStruct((half, width), jnp.float32)]
         shapes += [jax.ShapeDtypeStruct((piece, width), jnp.bfloat16)] * PIECES
     return order(
-        norm_back_kernel,
-        [x, gain, up, *mine, *come],
-        [picked if by_core else at, pl.BlockSpec((1, width), lambda i, core_ref: (0, 0)), at] + specs * 2,
-        specs if by_core else [at] + specs,
+        functools.partial(norm_back_kernel, last),
+        [*args, *mine, *come],
+        front + specs * 2,
+        specs if last else [at] + specs,
         shapes,
         (4,),
         0,
@@ -957,9 +993,9 @@
     )
 
 
-def layer_kernel(middle_ref, *refs):
-    mine, come = pick_piece(refs[:PIECES]), pick_piece(refs[PIECES : 2 * PIECES])
-    put_piece(refs[2 * PIECES :], to_bf(middle_ref[...] + (to_f(mine) + to_f(come))))
+def layer_kernel(*refs):
+    middle, mine, come = (pick_piece(refs[i * PIECES : (i + 1) * PIECES]) for i in range(3))
+    put_piece(refs[3 * PIECES :], to_bf(middle + (to_f(mine) + to_f(come))))
 
 
 def layer_of(order, middle, mine, come):
@@ -968,8 +1004,8 @@
     specs = piece_specs(piece, width, block)
     return order(
         layer_kernel,
-        [middle, *mine, *come],
-        [pl.BlockSpec((block, width), lambda i: (i, 0))] + specs * 2,
+        [*middle, *mine, *come],
+        specs * 3,
         specs,
         [jax.ShapeDtypeStruct((piece, width), jnp.bfloat16)] * PIECES,
         (4,),
@@ -1067,9 +1103,6 @@
     span = [shifted(kv, h) for h in range(hops, 0, -1)] + [kv]
     mate = [core_swap(piece) for piece in span]
     q_rows = q_rot.reshape(rows, local, heads * HD)
-    mixed_rows, lse = attend(low, core_one, q_rows, start, span, mate)
-    mixed = mixed_rows.reshape(total, heads * HD)
-
     order = Order()
     flat_tokens = tokens.reshape(total, width)
     dps = lax.axis_size("dp")
@@ -1152,25 +1185,34 @@
         def result(self):
             return [self.whole]
 
-    sent = core_swaps(narrow(order, [(mixed, o_weight)], 1, (), 1))
-    mine = narrow(order, [(mixed, o_weight)], 0, sent, 1)
-    come = chip_swaps(mine)
+    gate_rows, up_rows = rows_of(gate_weight), rows_of(up_weight)
+    order.arrived(kv)
     grad_ffn, grad_ffn_t = grad_out_of(
         order, core_one, cotangent.reshape(total, width), valid.reshape(total, 1)
     )
-    gate_rows, up_rows = rows_of(gate_weight), rows_of(up_weight)
-    order.arrived(gate_rows, up_rows)
     grad_hidden = grad_hidden_of(order, grad_ffn, down_t)
     h_one_t = turn(order, [h_one])
-    middle, h_two = middle_of(order, core_one, flat_tokens, mine, come, gain_two)
-    h_two += core_swaps(h_two)
-    hidden, grad_gate, grad_up = gated(order, h_two, grad_hidden, gate_t, up_t)
+    mixed_rows, lse = attend(order, low, core_one, q_rows, start, span, mate)
+    mixed = mixed_rows.reshape(total, heads * HD)
+    sent = core_swaps(narrow(order, [(half_of(mixed, 1), o_weight)], (), 1))
+    mine = narrow(order, [(half_of(mixed, 0), o_weight)], sent, 1)
+    come = chip_swaps(mine)
+    order.arrived(gate_rows, up_rows)
+    middle, h_two, ffn = [], [], []
+    for i in range(PIECES):
+        middle_part, *h_pair = middle_of(order, core_one, flat_tokens, mine[i], come[i], gain_two, i)
+        middle.append(middle_part)
+        h_pair += core_swaps(h_pair)
+        h_two += h_pair
+        ffn.append(gated(order, h_pair, grad_hidden, i, gate_t, up_t))
+    hidden, grad_gate, grad_up = (list(parts) for parts in zip(*ffn))
 
     down_b = SeqFirst([grad_ffn_t], [hidden], [(0, 0, cut, tiles - cut, 0)])
     down_a = Rows([grad_ffn_t], [hidden], [(0, 0, 0, cut, 0)])
-    pairs = [(grad_gate, gate_t), (grad_up, up_t)]
-    sent = core_swaps(narrow(order, pairs, 1))
-    mine = narrow(order, pairs, 0, sent)
+    sent = core_swaps(
+        narrow(order, [(sides_of(grad_gate, 1), gate_t), (sides_of(grad_up, 1), up_t)])
+    )
+    mine = narrow(order, [(sides_of(grad_gate, 0), gate_t), (sides_of(grad_up, 0), up_t)], sent)
     come = chip_swaps(mine)
     h_two_t = turn(order, h_two)
     if near_pair:
@@ -1203,29 +1245,29 @@
     branch_t = turn(order, branch)
     own_kv, *pieces = fold(order, keep, both_come, local)
     moving = shifted(pieces[-1], -1) if pieces else None
-    ffn_sent = core_swaps(narrow(order, [(hidden, down_t)], 1))
+    ffn_sent = core_swaps(narrow(order, [(sides_of(hidden, 1), down_t)]))
     for piece in pieces[-2::-1]:
         moving = shifted(carry(order, piece, moving), -1)
     grad_qkv, bias_sum = join(
         order, core_one, grad_q_rows, own_kv, [] if moving is None else [moving], cosine, sine
     )
-    sent = core_swaps(narrow(order, [(grad_qkv, weight)], 1, (), 1))
+    sent = core_swaps(narrow(order, [(half_of(grad_qkv, 1), weight)], (), 1))
     last_parts = [(0, 0, 0, grad_qkv.shape[1] // HD, 0), (1, 1, 0, heads, 0)]
-    last = Rows([h_one_t, branch_t], [grad_qkv, mixed], last_parts, HD)
-    mine = narrow(order, [(grad_qkv, weight)], 0, sent, 1)
+    last = Rows([h_one_t, branch_t], [[grad_qkv], [mixed]], last_parts, HD)
+    mine = narrow(order, [(half_of(grad_qkv, 0), weight)], sent, 1)
     come = chip_swaps(mine)
+    gate.own()
+    ffn_mine = narrow(order, [(sides_of(hidden, 0), down_t)], ffn_sent)
     down_a.relay()
-    gate.own()
-    ffn_mine = narrow(order, [(hidden, down_t)], 0, ffn_sent)
     token = norm_back(order, core_one, mine, come, flat_tokens, gain_one, grad_middle, True)
     token += core_swaps(token)
     ffn_come = chip_swaps(ffn_mine)
     token_grad = place(order, core_one, token).reshape(rows, local, width)
     up_a.own()
-    down_a.settled()
     layer = layer_of(order, middle, ffn_mine, ffn_come)
     layer += core_swaps(layer)
     down_b.across()
+    down_a.settled()
     last.own()
     layer_out = place(order, core_one, layer).reshape(rows, local, width)
     up_a.relay()

time: 516 us -> 537 us (1.041)
  Pallas kernels: 195 us -> 217 us
    ppermute x4, waiting for transfers between devices: 24.4 us -> 57.9 us  [own(): self.come = lax.ppermute(send, 'seq', flipped('seq', 0))]
    pallas_call x44 -> x47, Pallas kernels: 186 us -> 213 us  [__call__(): pl.pallas_call(run, grid_spec=pltpu.PrefetchScalarGridSpec(num_scalar_pre...]
    ppermute x4, waiting for transfers between devices: 46.5 us -> 22.1 us  [relay(): self.last = lax.ppermute(sent, 'seq', flipped('seq', 1))]
    ppermute x5, waiting for transfers between devices: 7.36 us -> 0.33 us  [__init__(): self.come = lax.ppermute(sent, 'dp', flipped('dp', 0))]
    pallas_call x1 -> x0, Pallas kernels: 6.07 us -> none  [attend(): pl.pallas_call(functools.partial(attend_kernel, heads, blocks, pieces), g...]
    ppermute x21 -> x23, waiting for transfers between devices: 19.5 us -> 17.2 us  [core_swap(): return lax.ppermute(value, 'tensor', flipped('tensor', 0))]
    unnamed x219 -> x243, local copies, waits for them, and re-layouts: 66.3 us -> 67.7 us
  transfers between devices with their start and end apart: 53 -> 55, of which waited for: 31 -> 28; matrix products, arithmetic and copies ran while one was open for 3% -> 2% of each run, Pallas kernels for 29% -> 34%
where the time goes in v7:
time: 537 us; the launch traced here: 530 us
  Pallas kernels  217 us (40%)
  waiting for transfers between devices  167 us (31%)
  local copies, waits for them, and re-layouts  77.5 us (14%)
  starting transfers between devices  43.8 us (8%)
  between operations  15.8 us (3%)
  other arithmetic  9.27 us (2%)
    pallas_call x47, Pallas kernels, __call__(): pl.pallas_call(run, grid_spec=pltpu.PrefetchScalarGridSpec(num_scalar_pre...  213 us
    unnamed x243, local copies, waits for them, and re-layouts  67.7 us
    ppermute x4, waiting for transfers between devices, own(): self.come = lax.ppermute(send, 'seq', flipped('seq', 0))  57.9 us
    ppermute x4, waiting for transfers between devices, shifted(): return lax.ppermute(value, 'seq', route)  31.4 us
    ppermute x9, waiting for transfers between devices, chip_swap(): return lax.ppermute(value, 'tensor', flipped('tensor', 1))  30.3 us
    ppermute x4, waiting for transfers between devices, relay(): self.last = lax.ppermute(sent, 'seq', flipped('seq', 1))  22.1 us
    ppermute x23, waiting for transfers between devices, core_swap(): return lax.ppermute(value, 'tensor', flipped('tensor', 0))  17.2 us
    ppermute x4, starting transfers between devices, shifted(): return lax.ppermute(value, 'seq', route)  13.1 us
  transfers between devices with their start and end apart: 55, of which 28 were waited for; matrix products, arithmetic and copies ran while one was open for 2% of the time, Pallas kernels for 34%

profile of v7, /device:TPU:0, one launch (start us, length us, event | category | flops | bytes accessed | tf_op | source)
XLA Modules:
  0.0 530.0 jit_solution(3024655809242600454)
XLA Ops:
  17.2 3.6 first.1
  21.7 5.7 %collective-permute-start.1 = (bf16[2,512,128]{2,1,0:T(8,128)(2,1)S(1)}, bf16[2,512,128]{2,1,0:T(8,128)(2,1)}, u32[]{:S(2)}, u32[]{:S(2)}) collective-permute-start(bf16[2,512,128]{2,1,0:T(8,128)(2,1)S(1)} %bitcast.74), channel_id=1, source_target_pairs={{0,4},{4,8},{8,12},{1,5},{5,9},{9,13},{2,6},{6,10},{10,14},{3,7},{... | collective-permute-start | bytes 786440 | tf_op jit(solution)/shard_map/ppermute | solution.py:67
  27.3 4.6 collective-permute-start
  32.8 4.3 collective-permute-done.refs_4_.refs_9_
  41.3 3.5 grad_out.1
  49.6 10.0 %grad_hidden.1 = (bf16[1024,2240]{1,0:T(8,128)(2,1)}, f32[8,128]{1,0:T(8,128)S(1)}) custom-call(bf16[1024,1536]{1,0:T(8,128)(2,1)S(1)} %copy-done.44, bf16[2240,1536]{1,0:T(8,128)(2,1)S(1)} %bitcast.56, f32[8,128]{1,0:T(8,128)S(1)} %get-tuple-element.149.refs_2_), custom_call_target="tpu_custom_call" | custom-call | flops 7046430 | bytes 15728 | tf_op jit(solution)/shard_map/grad_hidden/pallas_call | solution.py:99
  59.6 3.5 turn.3
  63.1 6.1 %attend.1 = (bf16[2,512,384]{2,1,0:T(8,128)(2,1)S(1)}, f32[2,2,768]{2,1,0:T(2,128)S(1)}, f32[8,128]{1,0:T(8,128)S(1)}) custom-call(s32[2,2]{1,0:T(2,128)S(1)} %shift-right-logical_maximum_fusion.refs_0_, s32[1]{0:T(128)} %bitcast.core_ref.refs_0_.refs_1_, bf16[2,512,384]{2,1,0:T(8,128)(2,1)S(1)} %bitcast.71, s32[2,1,512]{2,1,0:T(1,128)S(1)} %sub.44.refs_3_, ...), custom_call_target="tpu_custom_call" | custom-call | flops 8000000 | bytes 4194 | tf_op jit(solution)/shard_map/attend/pallas_call | solution.py:99
  74.9 3.5 narrow.9
  80.5 4.1 constant_dynamic-slice_fusion.2
  88.6 10.5 %collective-permute-done.7.refs_4_ = bf16[256,1536]{1,0:T(8,128)(2,1)} collective-permute-done((bf16[256,1536]{1,0:T(8,128)(2,1)}, bf16[256,1536]{1,0:T(8,128)(2,1)}, u32[]{:S(2)}, u32[]{:S(2)}) %collective-permute-start.7) | collective-permute-done | bytes 786464 | tf_op jit(solution)/shard_map/ppermute | solution.py:53
  108.5 3.1 copy-done
  114.6 11.9 %gated.2 = (bf16[512,2240]{1,0:T(8,128)(2,1)}, bf16[512,2240]{1,0:T(8,128)(2,1)}, bf16[512,2240]{1,0:T(8,128)(2,1)}, f32[8,128]{1,0:T(8,128)S(1)}) custom-call(bf16[1024,2240]{1,0:T(8,128)(2,1)S(1)} %copy-done.39, bf16[2240,1536]{1,0:T(8,128)(2,1)S(1)} %bitcast.50, bf16[2240,1536]{1,0:T(8,128)(2,1)S(1)} %bitcast.48, ...), custom_call_target="tpu_custom_call" | custom-call | flops 7046430 | bytes 31457 | tf_op jit(solution)/shard_map/gated/pallas_call | solution.py:99
  131.6 12.0 %gated.3 = (bf16[512,2240]{1,0:T(8,128)(2,1)}, bf16[512,2240]{1,0:T(8,128)(2,1)}, bf16[512,2240]{1,0:T(8,128)(2,1)}, f32[8,128]{1,0:T(8,128)S(1)}) custom-call(bf16[1024,2240]{1,0:T(8,128)(2,1)S(1)} %copy-done.39, bf16[2240,1536]{1,0:T(8,128)(2,1)S(1)} %bitcast.53, bf16[2240,1536]{1,0:T(8,128)(2,1)S(1)} %bitcast.49, ...), custom_call_target="tpu_custom_call" | custom-call | flops 7046430 | bytes 31457 | tf_op jit(solution)/shard_map/gated/pallas_call | solution.py:99
  145.3 5.3 share.9
  156.0 4.2 share.10
  166.5 10.5 %narrow.10 = (bf16[256,1536]{1,0:T(8,128)(2,1)S(1)}, bf16[256,1536]{1,0:T(8,128)(2,1)S(1)}, f32[8,128]{1,0:T(8,128)S(1)}) custom-call(bf16[512,2240]{1,0:T(8,128)(2,1)S(1)} %copy-done.27, bf16[512,2240]{1,0:T(8,128)(2,1)S(1)} %copy-done.29, bf16[2240,1536]{1,0:T(8,128)(2,1)S(1)} %bitcast.54, bf16[512,2240]{1,0:T(8,128)(2,1)S(1)} %copy-done.5, ...), custom_call_target="tpu_custom_call" | custom-call | flops 7046430 | bytes 19922 | tf_op jit(solution)/shard_map/narrow/pallas_call | solution.py:99
  180.5 11.1 %narrow.11 = (bf16[256,1536]{1,0:T(8,128)(2,1)}, bf16[256,1536]{1,0:T(8,128)(2,1)}, f32[8,128]{1,0:T(8,128)S(1)}) custom-call(bf16[512,2240]{1,0:T(8,128)(2,1)S(1)} %copy-done.27, bf16[512,2240]{1,0:T(8,128)(2,1)S(1)} %copy-done.29, bf16[2240,1536]{1,0:T(8,128)(2,1)S(1)} %bitcast.55, bf16[512,2240]{1,0:T(8,128)(2,1)S(1)} %copy-done.5, ...), custom_call_target="tpu_custom_call" | custom-call | flops 7046430 | bytes 19922 | tf_op jit(solution)/shard_map/narrow/pallas_call | solution.py:99
  193.6 3.5 turn.4
  199.1 13.8 %share.11 = (bf16[768,2304]{1,0:T(8,128)(2,1)}, bf16[768,1536]{1,0:T(8,128)(2,1)}, bf16[768,768]{1,0:T(8,128)(2,1)}, f32[8,128]{1,0:T(8,128)S(1)}) custom-call(s32[1]{0:T(128)} %bitcast.10.refs_0_, s32[1]{0:T(128)} %constant.59.clone.1.refs_0_.refs_1_, bf16[1536,1024]{1,0:T(8,128)(2,1)S(1)} %copy-done.23, bf16[512,2240]{1,0:T(8,128)(2,1)S(1)} %copy-done.27, ...), custom_call_target="tpu_custom_call" | custom-call | flops 7247757 | bytes 18087 | tf_op jit(solution)/shard_map/share/pallas_call | solution.py:99
  218.3 5.9 %share.12 = (bf16[384,1280]{1,0:T(8,128)(2,1)S(1)}, bf16[384,1280]{1,0:T(8,128)(2,1)S(1)}, f32[8,128]{1,0:T(8,128)S(1)}) custom-call(s32[1]{0:T(128)} %bitcast.11.refs_0_, s32[4]{0:T(128)S(1)} %pad_add_fusion.refs_1_, bf16[1536,1024]{1,0:T(8,128)(2,1)S(1)} %copy-done.36, bf16[512,2240]{1,0:T(8,128)(2,1)S(1)} %copy-done.11, bf16[512,2240]{1,0:T(8,128)(2,1)S(1)} %copy-done.16, ...), custom_call_target="tpu_custom_call" | custom-call | flops 2013265 | bytes 6160 | tf_op jit(solution)/shard_map/share/pallas_call | solution.py:99
  228.3 5.7 %norm_back.2 = (f32[512,1536]{1,0:T(8,128)}, bf16[256,1536]{1,0:T(8,128)(2,1)S(1)}, bf16[256,1536]{1,0:T(8,128)(2,1)S(1)}, f32[8,128]{1,0:T(8,128)S(1)}) custom-call(s32[1]{0:T(128)} %bitcast.core_ref.refs_0_.refs_1_, f32[1,1536]{1,0:T(1,128)S(1)} %reshape.197.refs_2_.refs_1_, bf16[1024,1536]{1,0:T(8,128)(2,1)S(1)} %copy-done.45, ...), custom_call_target="tpu_custom_call" | custom-call | bytes 10485 | tf_op jit(solution)/shard_map/norm_back/pallas_call | solution.py:99
  239.3 9.0 %attend_back.1 = (bf16[2,512,384]{2,1,0:T(8,128)(2,1)S(1)}, bf16[2,1536,128]{2,1,0:T(8,128)(2,1)S(1)}, bf16[2,1536,128]{2,1,0:T(8,128)(2,1)S(1)}, f32[8,128]{1,0:T(8,128)S(1)}) custom-call(s32[2,2]{1,0:T(2,128)S(1)} %shift-right-logical_maximum_fusion.refs_0_, s32[1]{0:T(128)} %bitcast.core_ref.refs_0_.refs_1_, bf16[2,512,384]{2,1,0:T(8,128)(2,1)S(1)} %bitcast.72, ...), custom_call_target="tpu_custom_call" | custom-call | flops 20000000 | bytes 6291 | tf_op jit(solution)/shard_map/attend_back/pallas_call | solution.py:99
  248.5 3.4 turn.5
  253.5 5.3 %narrow.12 = (bf16[256,1536]{1,0:T(8,128)(2,1)S(1)}, bf16[256,1536]{1,0:T(8,128)(2,1)S(1)}, f32[8,128]{1,0:T(8,128)S(1)}) custom-call(bf16[512,2240]{1,0:T(8,128)(2,1)S(1)} %copy-done.12, bf16[512,2240]{1,0:T(8,128)(2,1)S(1)} %copy-done.17, bf16[2240,1536]{1,0:T(8,128)(2,1)S(1)} %bitcast.59, f32[8,128]{1,0:T(8,128)S(1)} %get-tuple-element.201.refs_3_), custom_call_target="tpu_custom_call" | custom-call | flops 3523215 | bytes 10747 | tf_op jit(solution)/shard_map/narrow/pallas_call | solution.py:99
  258.9 16.0 %collective-permute-done.24.refs_1_ = bf16[2,512,128]{2,1,0:T(8,128)(2,1)S(1)} collective-permute-done((bf16[2,512,128]{2,1,0:T(8,128)(2,1)S(1)}, bf16[2,512,128]{2,1,0:T(8,128)(2,1)S(1)}, u32[]{:S(2)}, u32[]{:S(2)}) %collective-permute-start.24) | collective-permute-done | bytes 262176 | tf_op jit(solution)/shard_map/ppermute | solution.py:67
  276.5 10.5 %collective-permute-done.25.refs_5_ = bf16[2,512,128]{2,1,0:T(8,128)(2,1)S(1)} collective-permute-done((bf16[2,512,128]{2,1,0:T(8,128)(2,1)S(1)}, bf16[2,512,128]{2,1,0:T(8,128)(2,1)S(1)}, u32[]{:S(2)}, u32[]{:S(2)}) %collective-permute-start.25) | collective-permute-done | bytes 262176 | tf_op jit(solution)/shard_map/ppermute | solution.py:67
  292.3 5.5 %share.13 = (bf16[768,896]{1,0:T(8,128)(2,1)}, f32[8,128]{1,0:T(8,128)S(1)}) custom-call(s32[1]{0:T(128)} %bitcast.10.refs_0_, s32[1]{0:T(128)} %constant.59.clone.1.refs_0_.refs_1_, bf16[1536,1024]{1,0:T(8,128)(2,1)S(1)} %copy-done.40, bf16[1536,1024]{1,0:T(8,128)(2,1)S(1)} %copy-done.42, bf16[1024,512]{1,0:T(8,128)(2,1)S(1)} %copy-done.32, ...), custom_call_target="tpu_custom_call" | custom-call | flops 1409286 | bytes 4784 | tf_op jit(solution)/shard_map/share/pallas_call | solution.py:99
  300.1 9.7 %share.14 = (bf16[768,2304]{1,0:T(8,128)(2,1)}, f32[8,128]{1,0:T(8,128)S(1)}) custom-call(s32[1]{0:T(128)} %bitcast.11.refs_0_, s32[1]{0:T(128)} %constant.59.clone.1.refs_0_.refs_1_, bf16[1536,1024]{1,0:T(8,128)(2,1)S(1)} %copy-done.24, bf16[512,2240]{1,0:T(8,128)(2,1)S(1)} %copy-done.28, bf16[512,2240]{1,0:T(8,128)(2,1)S(1)} %copy-done.30, ...), custom_call_target="tpu_custom_call" | custom-call | flops 3623878 | bytes 9830 | tf_op jit(solution)/shard_map/share/pallas_call | solution.py:99
  314.3 3.6 copy-done.4
  321.3 5.4 %narrow.15 = (bf16[256,1536]{1,0:T(8,128)(2,1)S(1)}, bf16[256,1536]{1,0:T(8,128)(2,1)S(1)}, f32[8,128]{1,0:T(8,128)S(1)}) custom-call(bf16[512,2240]{1,0:T(8,128)(2,1)S(1)} %copy-done.13, bf16[512,2240]{1,0:T(8,128)(2,1)S(1)} %copy-done.18, bf16[2240,1536]{1,0:T(8,128)(2,1)S(1)} %bitcast.60, bf16[256,1536]{1,0:T(8,128)(2,1)S(1)} %collective-permute-done.21.refs_3_, ...), custom_call_target="tpu_custom_call" | custom-call | flops 3523215 | bytes 10747 | tf_op jit(solution)/shard_map/narrow/pallas_call | solution.py:99
  326.7 40.9 %collective-permute-done.33.refs_1_ = bf16[384,1280]{1,0:T(8,128)(2,1)S(1)} collective-permute-done((bf16[384,1280]{1,0:T(8,128)(2,1)}, bf16[384,1280]{1,0:T(8,128)(2,1)S(1)}, u32[]{:S(2)}, u32[]{:S(2)}) %collective-permute-start.33) | collective-permute-done | bytes 983072 | tf_op jit(solution)/shard_map/ppermute | solution.py:1141
  367.8 3.7 norm_back.3
  382.4 3.3 place.2
  387.2 5.6 %share.15 = (bf16[384,1536]{1,0:T(8,128)(2,1)}, bf16[384,1536]{1,0:T(8,128)(2,1)}, f32[8,128]{1,0:T(8,128)S(1)}) custom-call(s32[1]{0:T(128)} %bitcast.11.refs_0_, s32[4]{0:T(128)S(1)} %pad_add_fusion.refs_1_, bf16[1536,1024]{1,0:T(8,128)(2,1)S(1)} %copy-done.25, bf16[512,2240]{1,0:T(8,128)(2,1)S(1)} %copy-done.5, bf16[512,2240]{1,0:T(8,128)(2,1)S(1)} %copy-done.7, ...), custom_call_target="tpu_custom_call" | custom-call | flops 2415919 | bytes 7077 | tf_op jit(solution)/shard_map/share/pallas_call | solution.py:99
  395.5 12.8 %collective-permute-done.29.refs_5_ = bf16[256,1536]{1,0:T(8,128)(2,1)S(1)} collective-permute-done((bf16[256,1536]{1,0:T(8,128)(2,1)S(1)}, bf16[256,1536]{1,0:T(8,128)(2,1)S(1)}, u32[]{:S(2)}, u32[]{:S(2)}) %collective-permute-start.29) | collective-permute-done | bytes 786464 | tf_op jit(solution)/shard_map/ppermute | solution.py:53
  419.9 7.1 %share.16 = (bf16[384,896]{1,0:T(8,128)(2,1)S(1)}, bf16[384,896]{1,0:T(8,128)(2,1)S(1)}, f32[8,128]{1,0:T(8,128)S(1)}) custom-call(s32[1]{0:T(128)} %bitcast.11.refs_0_, s32[4]{0:T(128)S(1)} %pad_add_fusion.refs_1_, bf16[1536,1024]{1,0:T(8,128)(2,1)S(1)} %copy-done.41, bf16[1536,1024]{1,0:T(8,128)(2,1)S(1)} %copy-done.43, bf16[1024,512]{1,0:T(8,128)(2,1)S(1)} %copy-done.33, ...), custom_call_target="tpu_custom_call" | custom-call | flops 1409286 | bytes 4784 | tf_op jit(solution)/shard_map/share/pallas_call | solution.py:99
  427.2 4.2 place.3
  433.8 7.5 %collective-permute-done.43.refs_7_.refs_4_ = bf16[192,1024]{1,0:T(8,128)(2,1)S(1)} collective-permute-done((bf16[192,1024]{1,0:T(8,128)(2,1)S(1)}, bf16[192,1024]{1,0:T(8,128)(2,1)S(1)}, u32[]{:S(2)}, u32[]{:S(2)}) %collective-permute-start.43) | collective-permute-done | bytes 393248 | tf_op jit(solution)/shard_map/ppermute | solution.py:1167
  441.3 4.1 share.17
  445.5 4.9 collective-permute-start.49
  451.5 3.8 finish.4
  455.2 17.0 %collective-permute-done.45.refs_1_.refs_4_ = bf16[384,768]{1,0:T(8,128)(2,1)S(1)} collective-permute-done((bf16[384,768]{1,0:T(8,128)(2,1)S(1)}, bf16[384,768]{1,0:T(8,128)(2,1)S(1)}, u32[]{:S(2)}, u32[]{:S(2)}) %collective-permute-start.45) | collective-permute-done | bytes 589856 | tf_op jit(solution)/shard_map/ppermute | solution.py:1141
  476.2 3.7 finish.5
  479.9 18.6 %collective-permute-done.44.refs_2_ = bf16[192,896]{1,0:T(8,128)(2,1)S(1)} collective-permute-done((bf16[192,896]{1,0:T(8,128)(2,1)}, bf16[192,896]{1,0:T(8,128)(2,1)S(1)}, u32[]{:S(2)}, u32[]{:S(2)}) %collective-permute-start.44) | collective-permute-done | bytes 344096 | tf_op jit(solution)/shard_map/ppermute | solution.py:1146
  500.3 3.5 collective-permute-done.50.refs_5_
  503.8 6.3 %finish.7 = (f32[192,2240]{1,0:T(8,128)}, f32[192,128]{1,0:T(8,128)S(1)}, f32[8,128]{1,0:T(8,128)}) custom-call(bf16[384,1536]{1,0:T(8,128)(2,1)S(1)} %copy-done.61, bf16[384,1536]{1,0:T(8,128)(2,1)} %collective-permute-done.42.refs_1_, bf16[192,1536]{1,0:T(8,128)(2,1)} %collective-permute-done.49.refs_2_, bf16[384,768]{1,0:T(8,128)(2,1)S(1)} %copy-done.75, ...), custom_call_target="tpu_custom_call" | custom-call | bytes 6021 | tf_op jit(solution)/shard_map/finish/pallas_call | solution.py:99
  514.0 4.9 collective-permute-done.52
  (406 shorter events, 147.9 us)
Async XLA Ops:
  7.2 405.4 %reduce-scatter.3.cloned.1.call-start = ((), (), s32[]{:S(2)}) async-start(), calls=%async_computation.2 | async-start | bytes 3932160 | tf_op jit(solution)/shard_map/reduce_scatter | solution.py:1161
  21.7 11.1 %collective-permute-start.1 = (bf16[2,512,128]{2,1,0:T(8,128)(2,1)S(1)}, bf16[2,512,128]{2,1,0:T(8,128)(2,1)}, u32[]{:S(2)}, u32[]{:S(2)}) collective-permute-start(bf16[2,512,128]{2,1,0:T(8,128)(2,1)S(1)} %bitcast.74), channel_id=1, source_target_pairs={{0,4},{4,8},{8,12},{1,5},{5,9},{9,13},{2,6},{6,10},{10,14},{3,7},{... | collective-permute-start | bytes 786440 | tf_op jit(solution)/shard_map/ppermute | solution.py:67
  27.3 9.8 %collective-permute-start = (bf16[2,512,128]{2,1,0:T(8,128)(2,1)S(1)}, bf16[2,512,128]{2,1,0:T(8,128)(2,1)}, u32[]{:S(2)}, u32[]{:S(2)}) collective-permute-start(bf16[2,512,128]{2,1,0:T(8,128)(2,1)S(1)} %bitcast.75), channel_id=1, source_target_pairs={{0,8},{4,12},{1,9},{5,13},{2,10},{6,14},{3,11},{7,15},{16,24},{20,... | collective-permute-start | bytes 786440 | tf_op jit(solution)/shard_map/ppermute | solution.py:67
  32.0 31.1 %collective-permute-start.4 = (bf16[2,512,128]{2,1,0:T(8,128)(2,1)S(1)}, bf16[2,512,128]{2,1,0:T(8,128)(2,1)}, u32[]{:S(2)}, u32[]{:S(2)}) collective-permute-start(bf16[2,512,128]{2,1,0:T(8,128)(2,1)S(1)} %bitcast.76), channel_id=1, source_target_pairs={{0,1},{1,0},{2,3},{3,2},{4,5},{5,4},{6,7},{7,6},{8,9},{9,8},{10,11... | collective-permute-start | bytes 786440 | tf_op jit(solution)/shard_map/ppermute | solution.py:49
  32.8 30.3 %collective-permute-start.3 = (bf16[2,512,128]{2,1,0:T(8,128)(2,1)}, bf16[2,512,128]{2,1,0:T(8,128)(2,1)}, u32[]{:S(2)}, u32[]{:S(2)}) collective-permute-start(bf16[2,512,128]{2,1,0:T(8,128)(2,1)} %collective-permute-done.1.refs_5_.refs_10_), channel_id=1, source_target_pairs={{0,1},{1,0},{2,3},{3,2},{4,5},{5,4},{6,7},{7,6},{8,9},{9,8},{10,11... | collective-permute-start | bytes 786440 | tf_op jit(solution)/shard_map/ppermute | solution.py:49
  37.1 25.9 %collective-permute-start.2 = (bf16[2,512,128]{2,1,0:T(8,128)(2,1)}, bf16[2,512,128]{2,1,0:T(8,128)(2,1)}, u32[]{:S(2)}, u32[]{:S(2)}) collective-permute-start(bf16[2,512,128]{2,1,0:T(8,128)(2,1)} %collective-permute-done.refs_4_.refs_9_), channel_id=1, source_target_pairs={{0,1},{1,0},{2,3},{3,2},{4,5},{5,4},{6,7},{7,6},{8,9},{9,8},{10,11... | collective-permute-start | bytes 786440 | tf_op jit(solution)/shard_map/ppermute | solution.py:49
  71.3 2.5 collective-permute-start.5
  71.9 3.0 collective-permute-start.6
  78.4 20.7 %collective-permute-start.7 = (bf16[256,1536]{1,0:T(8,128)(2,1)}, bf16[256,1536]{1,0:T(8,128)(2,1)}, u32[]{:S(2)}, u32[]{:S(2)}) collective-permute-start(bf16[256,1536]{1,0:T(8,128)(2,1)} %get-tuple-element.157.refs_3_), channel_id=1, source_target_pairs={{0,2},{1,3},{2,0},{3,1},{4,6},{5,7},{6,4},{7,5},{8,10},{9,11},{10,... | collective-permute-start | bytes 2359304 | tf_op jit(solution)/shard_map/ppermute | solution.py:53
  79.9 46.5 %collective-permute-start.8 = (bf16[256,1536]{1,0:T(8,128)(2,1)}, bf16[256,1536]{1,0:T(8,128)(2,1)}, u32[]{:S(2)}, u32[]{:S(2)}) collective-permute-start(bf16[256,1536]{1,0:T(8,128)(2,1)} %get-tuple-element.160.refs_3_), channel_id=1, source_target_pairs={{0,2},{1,3},{2,0},{3,1},{4,6},{5,7},{6,4},{7,5},{8,10},{9,11},{10,... | collective-permute-start | bytes 2359304 | tf_op jit(solution)/shard_map/ppermute | solution.py:53
  150.6 324.5 %reduce-scatter.5.cloned.1.call-start = ((), (), s32[]{:S(2)}) async-start(), calls=%async_computation.3 | async-start | bytes 4423680 | tf_op jit(solution)/shard_map/reduce_scatter | solution.py:1180
  160.3 52.7 %collective-permute-start.17 = (bf16[768,1280]{1,0:T(8,128)(2,1)}, bf16[768,1280]{1,0:T(8,128)(2,1)}, u32[]{:S(2)}, u32[]{:S(2)}) collective-permute-start(bf16[768,1280]{1,0:T(8,128)(2,1)} %get-tuple-element.185), channel_id=1, source_target_pairs={{0,16},{16,0},{1,17},{17,1},{2,18},{18,2},{3,19},{19,3},{4,20},{20... | collective-permute-start | bytes 5898248 | tf_op jit(solution)/shard_map/ppermute | solution.py:1136
  177.0 3.4 collective-permute-start.14
  191.5 34.6 %collective-permute-start.15 = (bf16[256,1536]{1,0:T(8,128)(2,1)}, bf16[256,1536]{1,0:T(8,128)(2,1)}, u32[]{:S(2)}, u32[]{:S(2)}) collective-permute-start(bf16[256,1536]{1,0:T(8,128)(2,1)} %get-tuple-element.183.refs_5_), channel_id=1, source_target_pairs={{0,2},{1,3},{2,0},{3,1},{4,6},{5,7},{6,4},{7,5},{8,10},{9,11},{10,... | collective-permute-start | bytes 2359304 | tf_op jit(solution)/shard_map/ppermute | solution.py:53
  192.9 35.4 %collective-permute-start.16 = (bf16[256,1536]{1,0:T(8,128)(2,1)}, bf16[256,1536]{1,0:T(8,128)(2,1)}, u32[]{:S(2)}, u32[]{:S(2)}) collective-permute-start(bf16[256,1536]{1,0:T(8,128)(2,1)} %get-tuple-element.184.refs_6_), channel_id=1, source_target_pairs={{0,2},{1,3},{2,0},{3,1},{4,6},{5,7},{6,4},{7,5},{8,10},{9,11},{10,... | collective-permute-start | bytes 2359304 | tf_op jit(solution)/shard_map/ppermute | solution.py:53
  212.8 87.3 %collective-permute-start.23 = (bf16[768,2304]{1,0:T(8,128)(2,1)}, bf16[768,2304]{1,0:T(8,128)(2,1)}, u32[]{:S(2)}, u32[]{:S(2)}) collective-permute-start(bf16[768,2304]{1,0:T(8,128)(2,1)} %get-tuple-element.204), channel_id=1, source_target_pairs={{0,16},{16,0},{1,17},{17,1},{2,18},{18,2},{3,19},{19,3},{4,20},{20... | collective-permute-start | bytes 10616840 | tf_op jit(solution)/shard_map/ppermute | solution.py:1136
  234.0 3.4 collective-permute-start.19
  248.3 3.6 collective-permute-start.20
  252.1 22.7 %collective-permute-start.24 = (bf16[2,512,128]{2,1,0:T(8,128)(2,1)S(1)}, bf16[2,512,128]{2,1,0:T(8,128)(2,1)S(1)}, u32[]{:S(2)}, u32[]{:S(2)}) collective-permute-start(bf16[2,512,128]{2,1,0:T(8,128)(2,1)S(1)} %get-tuple-element.208), channel_id=1, source_target_pairs={{4,0},{8,4},{12,8},{5,1},{9,5},{13,9},{6,2},{10,6},{14,10},{7,3},{... | collective-permute-start | bytes 786440 | tf_op jit(solution)/shard_map/ppermute | solution.py:67
  274.9 12.1 %collective-permute-start.25 = (bf16[2,512,128]{2,1,0:T(8,128)(2,1)S(1)}, bf16[2,512,128]{2,1,0:T(8,128)(2,1)S(1)}, u32[]{:S(2)}, u32[]{:S(2)}) collective-permute-start(bf16[2,512,128]{2,1,0:T(8,128)(2,1)S(1)} %get-tuple-element.210), channel_id=1, source_target_pairs={{4,0},{8,4},{12,8},{5,1},{9,5},{13,9},{6,2},{10,6},{14,10},{7,3},{... | collective-permute-start | bytes 786440 | tf_op jit(solution)/shard_map/ppermute | solution.py:67
  291.7 6.1 %collective-permute-start.26 = (bf16[256,1536]{1,0:T(8,128)(2,1)S(1)}, bf16[256,1536]{1,0:T(8,128)(2,1)S(1)}, u32[]{:S(2)}, u32[]{:S(2)}) collective-permute-start(bf16[256,1536]{1,0:T(8,128)(2,1)S(1)} %get-tuple-element.214), channel_id=1, source_target_pairs={{0,1},{1,0},{2,3},{3,2},{4,5},{5,4},{6,7},{7,6},{8,9},{9,8},{10,11... | collective-permute-start | bytes 2359304 | tf_op jit(solution)/shard_map/ppermute | solution.py:49
  291.7 6.0 %collective-permute-start.27 = (bf16[256,1536]{1,0:T(8,128)(2,1)S(1)}, bf16[256,1536]{1,0:T(8,128)(2,1)S(1)}, u32[]{:S(2)}, u32[]{:S(2)}) collective-permute-start(bf16[256,1536]{1,0:T(8,128)(2,1)S(1)} %get-tuple-element.215), channel_id=1, source_target_pairs={{0,1},{1,0},{2,3},{3,2},{4,5},{5,4},{6,7},{7,6},{8,9},{9,8},{10,11... | collective-permute-start | bytes 2359304 | tf_op jit(solution)/shard_map/ppermute | solution.py:49
  309.9 4.1 collective-permute-start.21
  310.0 57.6 %collective-permute-start.33 = (bf16[384,1280]{1,0:T(8,128)(2,1)}, bf16[384,1280]{1,0:T(8,128)(2,1)S(1)}, u32[]{:S(2)}, u32[]{:S(2)}) collective-permute-start(bf16[384,1280]{1,0:T(8,128)(2,1)} %copy-done.108), channel_id=1, source_target_pairs={{0,4},{4,0},{8,12},{12,8},{1,5},{5,1},{9,13},{13,9},{2,6},{6,2},{1... | collective-permute-start | bytes 2949128 | tf_op jit(solution)/shard_map/ppermute | solution.py:1141
  311.8 2.5 collective-permute-start.22
  312.0 55.8 %collective-permute-start.31 = (bf16[256,1536]{1,0:T(8,128)(2,1)}, bf16[256,1536]{1,0:T(8,128)(2,1)S(1)}, u32[]{:S(2)}, u32[]{:S(2)}) collective-permute-start(bf16[256,1536]{1,0:T(8,128)(2,1)} %copy-done.104), channel_id=1, source_target_pairs={{0,2},{1,3},{2,0},{3,1},{4,6},{5,7},{6,4},{7,5},{8,10},{9,11},{10,... | collective-permute-start | bytes 2359304 | tf_op jit(solution)/shard_map/ppermute | solution.py:53
  313.4 54.3 %collective-permute-start.32 = (bf16[256,1536]{1,0:T(8,128)(2,1)}, bf16[256,1536]{1,0:T(8,128)(2,1)S(1)}, u32[]{:S(2)}, u32[]{:S(2)}) collective-permute-start(bf16[256,1536]{1,0:T(8,128)(2,1)} %copy-done.106), channel_id=1, source_target_pairs={{0,2},{1,3},{2,0},{3,1},{4,6},{5,7},{6,4},{7,5},{8,10},{9,11},{10,... | collective-permute-start | bytes 2359304 | tf_op jit(solution)/shard_map/ppermute | solution.py:53
  314.0 71.7 %collective-permute-start.30 = (bf16[768,1536]{1,0:T(8,128)(2,1)}, bf16[768,1536]{1,0:T(8,128)(2,1)S(1)}, u32[]{:S(2)}, u32[]{:S(2)}) collective-permute-start(bf16[768,1536]{1,0:T(8,128)(2,1)} %get-tuple-element.224), channel_id=1, source_target_pairs={{0,16},{16,0},{1,17},{17,1},{2,18},{18,2},{3,19},{19,3},{4,20},{20... | collective-permute-start | bytes 7077896 | tf_op jit(solution)/shard_map/ppermute | solution.py:1136
  371.5 3.6 collective-permute-start.34
  371.5 5.9 %collective-permute-start.35 = (f32[256,1536]{1,0:T(8,128)}, f32[256,1536]{1,0:T(8,128)S(1)}, u32[]{:S(2)}, u32[]{:S(2)}) collective-permute-start(f32[256,1536]{1,0:T(8,128)} %get-tuple-element.233.refs_2_), channel_id=1, source_target_pairs={{0,1},{1,0},{2,3},{3,2},{4,5},{5,4},{6,7},{7,6},{8,9},{9,8},{10,11... | collective-permute-start | bytes 4718600 | tf_op jit(solution)/shard_map/ppermute | solution.py:49
  372.0 23.5 %collective-permute-start.28 = (bf16[256,1536]{1,0:T(8,128)(2,1)S(1)}, bf16[256,1536]{1,0:T(8,128)(2,1)S(1)}, u32[]{:S(2)}, u32[]{:S(2)}) collective-permute-start(bf16[256,1536]{1,0:T(8,128)(2,1)S(1)} %get-tuple-element.222.refs_2_), channel_id=1, source_target_pairs={{0,2},{1,3},{2,0},{3,1},{4,6},{5,7},{6,4},{7,5},{8,10},{9,11},{10,... | collective-permute-start | bytes 2359304 | tf_op jit(solution)/shard_map/ppermute | solution.py:53
  373.6 34.7 %collective-permute-start.29 = (bf16[256,1536]{1,0:T(8,128)(2,1)S(1)}, bf16[256,1536]{1,0:T(8,128)(2,1)S(1)}, u32[]{:S(2)}, u32[]{:S(2)}) collective-permute-start(bf16[256,1536]{1,0:T(8,128)(2,1)S(1)} %get-tuple-element.223.refs_3_), channel_id=1, source_target_pairs={{0,2},{1,3},{2,0},{3,1},{4,6},{5,7},{6,4},{7,5},{8,10},{9,11},{10,... | collective-permute-start | bytes 2359304 | tf_op jit(solution)/shard_map/ppermute | solution.py:53
  375.1 38.7 %collective-permute-start.38 = (bf16[768,896]{1,0:T(8,128)(2,1)}, bf16[768,896]{1,0:T(8,128)(2,1)}, u32[]{:S(2)}, u32[]{:S(2)}) collective-permute-start(bf16[768,896]{1,0:T(8,128)(2,1)} %get-tuple-element.239), channel_id=1, source_target_pairs={{0,16},{16,0},{1,17},{17,1},{2,18},{18,2},{3,19},{19,3},{4,20},{20... | collective-permute-start | bytes 4128776 | tf_op jit(solution)/shard_map/ppermute | solution.py:1136
  377.4 34.0 %collective-permute-start.39 = (bf16[192,1280]{1,0:T(8,128)(2,1)S(1)}, bf16[192,1280]{1,0:T(8,128)(2,1)S(1)}, u32[]{:S(2)}, u32[]{:S(2)}) collective-permute-start(bf16[192,1280]{1,0:T(8,128)(2,1)S(1)} %get-tuple-element.241), channel_id=1, source_target_pairs={{0,8},{4,12},{8,0},{12,4},{1,9},{5,13},{9,1},{13,5},{2,10},{6,14},... | collective-permute-start | bytes 1474568 | tf_op jit(solution)/shard_map/ppermute | solution.py:1146
  392.8 38.6 %collective-permute-start.42 = (bf16[384,1536]{1,0:T(8,128)(2,1)}, bf16[384,1536]{1,0:T(8,128)(2,1)}, u32[]{:S(2)}, u32[]{:S(2)}) collective-permute-start(bf16[384,1536]{1,0:T(8,128)(2,1)} %get-tuple-element.249), channel_id=1, source_target_pairs={{0,4},{4,0},{8,12},{12,8},{1,5},{5,1},{9,13},{13,9},{2,6},{6,2},{1... | collective-permute-start | bytes 3538952 | tf_op jit(solution)/shard_map/ppermute | solution.py:1141
  395.5 38.3 %collective-permute-start.41 = (bf16[768,768]{1,0:T(8,128)(2,1)}, bf16[768,768]{1,0:T(8,128)(2,1)}, u32[]{:S(2)}, u32[]{:S(2)}) collective-permute-start(bf16[768,768]{1,0:T(8,128)(2,1)} %get-tuple-element.247), channel_id=1, source_target_pairs={{0,16},{16,0},{1,17},{17,1},{2,18},{18,2},{3,19},{19,3},{4,20},{20... | collective-permute-start | bytes 3538952 | tf_op jit(solution)/shard_map/ppermute | solution.py:1136
  411.3 15.7 %collective-permute-start.36 = (bf16[256,1536]{1,0:T(8,128)(2,1)}, bf16[256,1536]{1,0:T(8,128)(2,1)}, u32[]{:S(2)}, u32[]{:S(2)}) collective-permute-start(bf16[256,1536]{1,0:T(8,128)(2,1)} %get-tuple-element.237.refs_1_), channel_id=1, source_target_pairs={{0,1},{1,0},{2,3},{3,2},{4,5},{5,4},{6,7},{7,6},{8,9},{9,8},{10,11... | collective-permute-start | bytes 2359304 | tf_op jit(solution)/shard_map/ppermute | solution.py:49
  412.1 15.0 %collective-permute-start.37 = (bf16[256,1536]{1,0:T(8,128)(2,1)}, bf16[256,1536]{1,0:T(8,128)(2,1)}, u32[]{:S(2)}, u32[]{:S(2)}) collective-permute-start(bf16[256,1536]{1,0:T(8,128)(2,1)} %get-tuple-element.238.refs_2_), channel_id=1, source_target_pairs={{0,1},{1,0},{2,3},{3,2},{4,5},{5,4},{6,7},{7,6},{8,9},{9,8},{10,11... | collective-permute-start | bytes 2359304 | tf_op jit(solution)/shard_map/ppermute | solution.py:49
  413.8 27.5 %collective-permute-start.43 = (bf16[192,1024]{1,0:T(8,128)(2,1)S(1)}, bf16[192,1024]{1,0:T(8,128)(2,1)S(1)}, u32[]{:S(2)}, u32[]{:S(2)}) collective-permute-start(bf16[192,1024]{1,0:T(8,128)(2,1)S(1)} %get-tuple-element.277), channel_id=1, source_target_pairs={{0,16},{16,0},{1,17},{17,1},{2,18},{18,2},{3,19},{19,3},{4,20},{20... | collective-permute-start | bytes 1179656 | tf_op jit(solution)/shard_map/ppermute | solution.py:1167
  427.1 23.3 %collective-permute-start.40 = (bf16[384,896]{1,0:T(8,128)(2,1)S(1)}, bf16[384,896]{1,0:T(8,128)(2,1)S(1)}, u32[]{:S(2)}, u32[]{:S(2)}) collective-permute-start(bf16[384,896]{1,0:T(8,128)(2,1)S(1)} %get-tuple-element.246), channel_id=1, source_target_pairs={{0,4},{4,0},{8,12},{12,8},{1,5},{5,1},{9,13},{13,9},{2,6},{6,2},{1... | collective-permute-start | bytes 2064392 | tf_op jit(solution)/shard_map/ppermute | solution.py:1141
  445.4 26.8 %collective-permute-start.45 = (bf16[384,768]{1,0:T(8,128)(2,1)S(1)}, bf16[384,768]{1,0:T(8,128)(2,1)S(1)}, u32[]{:S(2)}, u32[]{:S(2)}) collective-permute-start(bf16[384,768]{1,0:T(8,128)(2,1)S(1)} %get-tuple-element.257), channel_id=1, source_target_pairs={{0,4},{4,0},{8,12},{12,8},{1,5},{5,1},{9,13},{13,9},{2,6},{6,2},{1... | collective-permute-start | bytes 1769480 | tf_op jit(solution)/shard_map/ppermute | solution.py:1141
  445.5 54.8 %collective-permute-start.49 = (bf16[192,1536]{1,0:T(8,128)(2,1)}, bf16[192,1536]{1,0:T(8,128)(2,1)}, u32[]{:S(2)}, u32[]{:S(2)}) collective-permute-start(bf16[192,1536]{1,0:T(8,128)(2,1)} %get-tuple-element.269), channel_id=1, source_target_pairs={{0,8},{4,12},{8,0},{12,4},{1,9},{5,13},{9,1},{13,5},{2,10},{6,14},... | collective-permute-start | bytes 1769480 | tf_op jit(solution)/shard_map/ppermute | solution.py:1146
  451.2 47.3 %collective-permute-start.44 = (bf16[192,896]{1,0:T(8,128)(2,1)}, bf16[192,896]{1,0:T(8,128)(2,1)S(1)}, u32[]{:S(2)}, u32[]{:S(2)}) collective-permute-start(bf16[192,896]{1,0:T(8,128)(2,1)} %get-tuple-element.254), channel_id=1, source_target_pairs={{0,8},{4,12},{8,0},{12,4},{1,9},{5,13},{9,1},{13,5},{2,10},{6,14},... | collective-permute-start | bytes 1032200 | tf_op jit(solution)/shard_map/ppermute | solution.py:1146
  451.2 4.1 collective-permute-start.46
  473.1 30.7 %collective-permute-start.50 = (bf16[192,768]{1,0:T(8,128)(2,1)}, bf16[192,768]{1,0:T(8,128)(2,1)}, u32[]{:S(2)}, u32[]{:S(2)}) collective-permute-start(bf16[192,768]{1,0:T(8,128)(2,1)} %get-tuple-element.270), channel_id=1, source_target_pairs={{0,8},{4,12},{8,0},{12,4},{1,9},{5,13},{9,1},{13,5},{2,10},{6,14},... | collective-permute-start | bytes 884744 | tf_op jit(solution)/shard_map/ppermute | solution.py:1146
  473.1 26.0 %collective-permute-start.47 = (f32[8,512]{1,0:T(8,128)S(1)}, f32[8,512]{1,0:T(8,128)S(1)}, u32[]{:S(2)}, u32[]{:S(2)}) collective-permute-start(f32[8,512]{1,0:T(8,128)S(1)} %get-tuple-element.265.refs_0_), channel_id=1, source_target_pairs={{0,4},{4,0},{8,12},{12,8},{1,5},{5,1},{9,13},{13,9},{2,6},{6,2},{1... | collective-permute-start | bytes 49160 | tf_op jit(solution)/shard_map/ppermute | solution.py:1281
  499.1 11.2 %collective-permute-start.48 = (f32[8,512]{1,0:T(8,128)S(1)}, f32[8,512]{1,0:T(8,128)S(1)}, u32[]{:S(2)}, u32[]{:S(2)}) collective-permute-start(f32[8,512]{1,0:T(8,128)S(1)} %get-tuple-element.267), channel_id=1, source_target_pairs={{0,8},{4,12},{8,0},{12,4},{1,9},{5,13},{9,1},{13,5},{2,10},{6,14},... | collective-permute-start | bytes 49160 | tf_op jit(solution)/shard_map/ppermute | solution.py:1288
  511.7 7.2 %collective-permute-start.52 = (f32[2,200,128]{2,1,0:T(8,128)S(1)}, f32[2,200,128]{2,1,0:T(8,128)S(1)}, u32[]{:S(2)}, u32[]{:S(2)}) collective-permute-start(f32[2,200,128]{2,1,0:T(8,128)S(1)} %maximum_select_fusion.1), channel_id=1, source_target_pairs={{0,2},{1,3},{2,0},{3,1},{4,6},{5,7},{6,4},{7,5},{8,10},{9,11},{10,... | collective-permute-start | bytes 614408 | tf_op jit(solution)/shard_map/ppermute | solution.py:53
  (126 other events, 1422.8 us)
Sparse Core Ops, SparseCore 0:
  150.7 70.8 reduce-scatter.2
  310.0 92.1 reduce-scatter.4

commit v8 on v7

--- a/solution.py
+++ b/solution.py
@@ -194,21 +194,42 @@
     return first_key, jnp.concatenate([place] * heads, axis=1)
 
 
+def pass_kernel(*refs):
+    for i, ref in enumerate(refs[:-1]):
+        refs[-1][i] = ref[...]
+
+
+def pass_on(order, pieces):
+    rows, local, columns = pieces[0].shape
+    count = len(pieces)
+    return order(
+        pass_kernel,
+        list(pieces),
+        [pl.BlockSpec((1, local, columns), lambda i: (i, 0, 0))] * count,
+        [pl.BlockSpec((count, 1, local, columns), lambda i: (0, i, 0, 0))],
+        [jax.ShapeDtypeStruct((count, rows, local, columns), pieces[0].dtype)],
+        (rows,),
+        0,
+        2 * MIB,
+        "pass",
+    )[0]
+
+
 def gather_span(core, refs, span):
-    count = len(refs) // 2
-    local = refs[0].shape[1]
-    for i in range(count):
-        here = slice(i * local, (i + 1) * local)
-        span[core, here] = refs[i][0]
-        span[1 - core, here] = refs[count + i][0]
+    for side, (moved, own) in ((core, refs[:2]), (1 - core, refs[2:])):
+        local = own.shape[1]
+        hops = moved.shape[0]
+        for i in range(hops):
+            span[side, i * local : (i + 1) * local] = moved[i, 0]
+        span[side, hops * local :] = own[0]
 
 
 def attend_kernel(heads, blocks, pieces, low_ref, core_ref, q_ref, start_ref, *refs):
-    o_ref, lse_ref, acc, span = refs[2 * pieces :]
+    o_ref, lse_ref, acc, span = refs[4:]
     row = pl.program_id(0)
     wide = heads * Q_BLOCK
     reach = (pieces - 1) * q_ref.shape[1]
-    gather_span(core_ref[0], refs[: 2 * pieces], span)
+    gather_span(core_ref[0], refs[:4], span)
     for index in range(blocks):
         q = stacked(q_ref, index * Q_BLOCK, Q_BLOCK, heads)
         first_key, place = bounds(start_ref, index, heads, reach)
@@ -243,14 +264,21 @@
 
 
 def span_specs(rows, local, pieces):
-    near = pl.BlockSpec((1, local, HD), lambda i, *refs: (i, 0, 0))
-    far = pl.BlockSpec((1, local, HD), lambda i, *refs: (lax.rem(i + rows // 2, rows), 0, 0))
-    return [near] * pieces + [far] * pieces
+    def at(turned):
+        def row(i):
+            return lax.rem(i + turned, rows)
+
+        return [
+            pl.BlockSpec((pieces - 1, 1, local, HD), lambda i, *refs: (0, row(i), 0, 0)),
+            pl.BlockSpec((1, local, HD), lambda i, *refs: (row(i), 0, 0)),
+        ]
+
+    return at(0) + at(rows // 2)
 
 
 def attend(order, low, core, q, start, span, mate):
     rows, local, columns = q.shape
-    pieces = len(span)
+    pieces = span[0].shape[0] + 1
     heads = columns // HD
     blocks = local // Q_BLOCK
 
@@ -282,12 +310,12 @@
 def attend_back_kernel(
     heads, blocks, pieces, low_ref, core_ref, q_ref, start_ref, g_ref, o_ref, lse_ref, cos_ref, sin_ref, *refs
 ):
-    gq_ref, keep_ref, send_ref, acc, gk, gv, span = refs[2 * pieces :]
+    gq_ref, keep_ref, send_ref, acc, gk, gv, span = refs[4:]
     row = pl.program_id(0)
     wide = heads * Q_BLOCK
     reach = (pieces - 1) * q_ref.shape[1]
     core = core_ref[0]
-    gather_span(core, refs[: 2 * pieces], span)
+    gather_span(core, refs[:4], span)
     gk[...] = jnp.zeros_like(gk)
     gv[...] = jnp.zeros_like(gv)
     for index in range(blocks):
@@ -330,7 +358,7 @@
 
 def attend_back(order, low, core, q, start, span, mate, grad, out, lse, cosine, sine):
     rows, local, columns = q.shape
-    pieces = len(span)
+    pieces = span[0].shape[0] + 1
     window = pieces * local
     heads = columns // HD
     blocks = local // Q_BLOCK
@@ -1100,8 +1128,8 @@
         core_one, tokens.reshape(total, width), gain_one, weight, bias, cosine, sine
     )
     kv = kv.reshape(rows, local, HD)
-    span = [shifted(kv, h) for h in range(hops, 0, -1)] + [kv]
-    mate = [core_swap(piece) for piece in span]
+    moved = [shifted(kv, h) for h in range(hops, 0, -1)]
+    kv_mate = core_swap(kv)
     q_rows = q_rot.reshape(rows, local, heads * HD)
     order = Order()
     flat_tokens = tokens.reshape(total, width)
@@ -1164,6 +1192,7 @@
             if near_pair:
                 sent = lax.dynamic_slice_in_dim(self.mine, (1 - dp_index) * share, share, 0)
                 self.mine = lax.dynamic_slice_in_dim(self.mine, dp_index * share, share, 0)
+                order.arrived(sent, self.mine)
                 self.come = lax.ppermute(sent, "dp", flipped("dp", 0))
 
         def settled(self):
@@ -1192,6 +1221,8 @@
     )
     grad_hidden = grad_hidden_of(order, grad_ffn, down_t)
     h_one_t = turn(order, [h_one])
+    moved = pass_on(order, moved)
+    span, mate = [moved, kv], [core_swap(moved), kv_mate]
     mixed_rows, lse = attend(order, low, core_one, q_rows, start, span, mate)
     mixed = mixed_rows.reshape(total, heads * HD)
     sent = core_swaps(narrow(order, [(half_of(mixed, 1), o_weight)], (), 1))
@@ -1256,23 +1287,23 @@
     last = Rows([h_one_t, branch_t], [[grad_qkv], [mixed]], last_parts, HD)
     mine = narrow(order, [(half_of(grad_qkv, 0), weight)], sent, 1)
     come = chip_swaps(mine)
+    down_b.across()
+    down_a.relay()
     gate.own()
     ffn_mine = narrow(order, [(sides_of(hidden, 0), down_t)], ffn_sent)
-    down_a.relay()
     token = norm_back(order, core_one, mine, come, flat_tokens, gain_one, grad_middle, True)
     token += core_swaps(token)
     ffn_come = chip_swaps(ffn_mine)
+    up_a.own()
     token_grad = place(order, core_one, token).reshape(rows, local, width)
-    up_a.own()
+    down_a.settled()
     layer = layer_of(order, middle, ffn_mine, ffn_come)
     layer += core_swaps(layer)
-    down_b.across()
-    down_a.settled()
     last.own()
     layer_out = place(order, core_one, layer).reshape(rows, local, width)
     up_a.relay()
+    up_b.own()
     down_b.settled()
-    up_b.own()
     last.relay()
     (down_grad,) = finish(order, [down_a.result(), down_b.result()], share, units, TILE)
     if near_pair:

time: 537 us -> 546 us (1.017)
  waiting for transfers between devices: 167 us -> 154 us
  local copies, waits for them, and re-layouts: 77.5 us -> 89.9 us
    ppermute x4, waiting for transfers between devices: 57.9 us -> 21.9 us  [own(): self.come = lax.ppermute(send, 'seq', flipped('seq', 0))]
    ppermute x4, waiting for transfers between devices: 22.1 us -> 43.8 us  [relay(): self.last = lax.ppermute(sent, 'seq', flipped('seq', 1))]
    ppermute x4, waiting for transfers between devices: 31.4 us -> 14.2 us  [shifted(): return lax.ppermute(value, 'seq', route)]
    ppermute x9, waiting for transfers between devices: 30.3 us -> 46 us  [chip_swap(): return lax.ppermute(value, 'tensor', flipped('tensor', 1))]
    unnamed x243 -> x285, local copies, waits for them, and re-layouts: 67.7 us -> 78 us
    ppermute x5, waiting for transfers between devices: 0.33 us -> 7.7 us  [__init__(): self.come = lax.ppermute(sent, 'dp', flipped('dp', 0))]
    ppermute x23 -> x22, waiting for transfers between devices: 17.2 us -> 14.6 us  [core_swap(): return lax.ppermute(value, 'tensor', flipped('tensor', 0))]
    pallas_call x47 -> x48, Pallas kernels: 213 us -> 215 us  [__call__(): pl.pallas_call(run, grid_spec=pltpu.PrefetchScalarGridSpec(num_scalar_pre...]
  transfers between devices with their start and end apart: 55 -> 54, of which waited for: 28 -> 27; matrix products, arithmetic and copies ran while one was open for 2% -> 3% of each run, Pallas kernels for 34% -> 33%
where the time goes in v8:
time: 546 us; the launch traced here: 538 us
  Pallas kernels  219 us (40%)
  waiting for transfers between devices  154 us (28%)
  local copies, waits for them, and re-layouts  89.9 us (16%)
  starting transfers between devices  47.8 us (9%)
  between operations  15.9 us (3%)
  other arithmetic  11.3 us (2%)
    pallas_call x48, Pallas kernels, __call__(): pl.pallas_call(run, grid_spec=pltpu.PrefetchScalarGridSpec(num_scalar_pre...  215 us
    unnamed x285, local copies, waits for them, and re-layouts  78 us
    ppermute x9, waiting for transfers between devices, chip_swap(): return lax.ppermute(value, 'tensor', flipped('tensor', 1))  46 us
    ppermute x4, waiting for transfers between devices, relay(): self.last = lax.ppermute(sent, 'seq', flipped('seq', 1))  43.8 us
    ppermute x4, waiting for transfers between devices, own(): self.come = lax.ppermute(send, 'seq', flipped('seq', 0))  21.9 us
    ppermute x22, waiting for transfers between devices, core_swap(): return lax.ppermute(value, 'tensor', flipped('tensor', 0))  14.6 us
    ppermute x4, waiting for transfers between devices, shifted(): return lax.ppermute(value, 'seq', route)  14.2 us
    ppermute x4, starting transfers between devices, shifted(): return lax.ppermute(value, 'seq', route)  12.4 us
  transfers between devices with their start and end apart: 54, of which 27 were waited for; matrix products, arithmetic and copies ran while one was open for 3% of the time, Pallas kernels for 33%

profile of v8, /device:TPU:0, one launch (start us, length us, event | category | flops | bytes accessed | tf_op | source)
XLA Modules:
  0.0 537.5 jit_solution(5414981237516149416)
XLA Ops:
  17.7 3.6 first.1
  23.0 4.9 collective-permute-start.1
  28.0 4.7 collective-permute-start
  35.1 3.5 grad_out.1
  43.4 10.0 %grad_hidden.1 = (bf16[1024,2240]{1,0:T(8,128)(2,1)}, f32[8,128]{1,0:T(8,128)S(1)}) custom-call(bf16[1024,1536]{1,0:T(8,128)(2,1)S(1)} %copy-done.43, bf16[2240,1536]{1,0:T(8,128)(2,1)S(1)} %bitcast.56, f32[8,128]{1,0:T(8,128)S(1)} %get-tuple-element.151.refs_2_), custom_call_target="tpu_custom_call" | custom-call | flops 7046430 | bytes 15728 | tf_op jit(solution)/shard_map/grad_hidden/pallas_call | solution.py:99
  65.4 5.0 attend.1
  82.1 4.1 constant_dynamic-slice_fusion.2
  90.2 10.5 %collective-permute-done.6.refs_4_ = bf16[256,1536]{1,0:T(8,128)(2,1)} collective-permute-done((bf16[256,1536]{1,0:T(8,128)(2,1)}, bf16[256,1536]{1,0:T(8,128)(2,1)}, u32[]{:S(2)}, u32[]{:S(2)}) %collective-permute-start.6) | collective-permute-done | bytes 786464 | tf_op jit(solution)/shard_map/ppermute | solution.py:53
  116.2 11.9 %gated.2 = (bf16[512,2240]{1,0:T(8,128)(2,1)}, bf16[512,2240]{1,0:T(8,128)(2,1)}, bf16[512,2240]{1,0:T(8,128)(2,1)}, f32[8,128]{1,0:T(8,128)S(1)}) custom-call(bf16[1024,2240]{1,0:T(8,128)(2,1)S(1)} %copy-done.38, bf16[2240,1536]{1,0:T(8,128)(2,1)S(1)} %bitcast.50, bf16[2240,1536]{1,0:T(8,128)(2,1)S(1)} %bitcast.48, ...), custom_call_target="tpu_custom_call" | custom-call | flops 7046430 | bytes 31457 | tf_op jit(solution)/shard_map/gated/pallas_call | solution.py:99
  133.2 12.0 %gated.3 = (bf16[512,2240]{1,0:T(8,128)(2,1)}, bf16[512,2240]{1,0:T(8,128)(2,1)}, bf16[512,2240]{1,0:T(8,128)(2,1)}, f32[8,128]{1,0:T(8,128)S(1)}) custom-call(bf16[1024,2240]{1,0:T(8,128)(2,1)S(1)} %copy-done.38, bf16[2240,1536]{1,0:T(8,128)(2,1)S(1)} %bitcast.53, bf16[2240,1536]{1,0:T(8,128)(2,1)S(1)} %bitcast.49, ...), custom_call_target="tpu_custom_call" | custom-call | flops 7046430 | bytes 31457 | tf_op jit(solution)/shard_map/gated/pallas_call | solution.py:99
  146.9 5.3 share.9
  157.7 4.2 share.10
  168.1 10.1 %narrow.10 = (bf16[256,1536]{1,0:T(8,128)(2,1)S(1)}, bf16[256,1536]{1,0:T(8,128)(2,1)S(1)}, f32[8,128]{1,0:T(8,128)S(1)}) custom-call(bf16[512,2240]{1,0:T(8,128)(2,1)S(1)} %copy-done.25, bf16[512,2240]{1,0:T(8,128)(2,1)S(1)} %copy-done.27, bf16[2240,1536]{1,0:T(8,128)(2,1)S(1)} %bitcast.54, bf16[512,2240]{1,0:T(8,128)(2,1)S(1)} %copy-done.5, ...), custom_call_target="tpu_custom_call" | custom-call | flops 7046430 | bytes 19922 | tf_op jit(solution)/shard_map/narrow/pallas_call | solution.py:99
  181.8 11.1 %narrow.11 = (bf16[256,1536]{1,0:T(8,128)(2,1)}, bf16[256,1536]{1,0:T(8,128)(2,1)}, f32[8,128]{1,0:T(8,128)S(1)}) custom-call(bf16[512,2240]{1,0:T(8,128)(2,1)S(1)} %copy-done.25, bf16[512,2240]{1,0:T(8,128)(2,1)S(1)} %copy-done.27, bf16[2240,1536]{1,0:T(8,128)(2,1)S(1)} %bitcast.55, bf16[512,2240]{1,0:T(8,128)(2,1)S(1)} %copy-done.5, ...), custom_call_target="tpu_custom_call" | custom-call | flops 7046430 | bytes 19922 | tf_op jit(solution)/shard_map/narrow/pallas_call | solution.py:99
  194.9 3.5 turn.4
  200.3 13.7 %share.11 = (bf16[768,2304]{1,0:T(8,128)(2,1)}, bf16[768,1536]{1,0:T(8,128)(2,1)}, bf16[768,768]{1,0:T(8,128)(2,1)}, f32[8,128]{1,0:T(8,128)S(1)}) custom-call(s32[1]{0:T(128)} %bitcast.10.refs_0_, s32[1]{0:T(128)} %constant.59.clone.1.refs_0_.refs_1_, bf16[1536,1024]{1,0:T(8,128)(2,1)S(1)} %copy-done.22, bf16[512,2240]{1,0:T(8,128)(2,1)S(1)} %copy-done.25, ...), custom_call_target="tpu_custom_call" | custom-call | flops 7247757 | bytes 18087 | tf_op jit(solution)/shard_map/share/pallas_call | solution.py:99
  219.8 6.5 %share.12 = (bf16[384,1280]{1,0:T(8,128)(2,1)}, bf16[384,1280]{1,0:T(8,128)(2,1)S(1)}, f32[8,128]{1,0:T(8,128)S(1)}) custom-call(s32[1]{0:T(128)} %bitcast.11.refs_0_, s32[4]{0:T(128)S(1)} %pad_add_fusion.refs_1_, bf16[1536,1024]{1,0:T(8,128)(2,1)S(1)} %copy-done.34, bf16[512,2240]{1,0:T(8,128)(2,1)S(1)} %copy-done.10, bf16[512,2240]{1,0:T(8,128)(2,1)S(1)} %copy-done.15, ...), custom_call_target="tpu_custom_call" | custom-call | flops 2013265 | bytes 6160 | tf_op jit(solution)/shard_map/share/pallas_call | solution.py:99
  229.6 5.7 %norm_back.2 = (f32[512,1536]{1,0:T(8,128)}, bf16[256,1536]{1,0:T(8,128)(2,1)S(1)}, bf16[256,1536]{1,0:T(8,128)(2,1)S(1)}, f32[8,128]{1,0:T(8,128)S(1)}) custom-call(s32[1]{0:T(128)} %bitcast.core_ref.refs_0_.refs_1_, f32[1,1536]{1,0:T(1,128)S(1)} %reshape.197.refs_2_.refs_1_, bf16[1024,1536]{1,0:T(8,128)(2,1)S(1)} %copy-done.44, ...), custom_call_target="tpu_custom_call" | custom-call | bytes 10485 | tf_op jit(solution)/shard_map/norm_back/pallas_call | solution.py:99
  240.8 7.6 %attend_back.1 = (bf16[2,512,384]{2,1,0:T(8,128)(2,1)S(1)}, bf16[2,1536,128]{2,1,0:T(8,128)(2,1)S(1)}, bf16[2,1536,128]{2,1,0:T(8,128)(2,1)S(1)}, f32[8,128]{1,0:T(8,128)S(1)}) custom-call(s32[2,2]{1,0:T(2,128)S(1)} %copy-done.124, s32[1]{0:T(128)} %bitcast.core_ref.refs_0_.refs_1_, bf16[2,512,384]{2,1,0:T(8,128)(2,1)S(1)} %bitcast.72, ...), custom_call_target="tpu_custom_call" | custom-call | flops 20000000 | bytes 6291 | tf_op jit(solution)/shard_map/attend_back/pallas_call | solution.py:99
  253.5 5.3 narrow.12
  259.8 7.1 %collective-permute-done.24.refs_1_ = bf16[2,512,128]{2,1,0:T(8,128)(2,1)S(1)} collective-permute-done((bf16[2,512,128]{2,1,0:T(8,128)(2,1)S(1)}, bf16[2,512,128]{2,1,0:T(8,128)(2,1)S(1)}, u32[]{:S(2)}, u32[]{:S(2)}) %collective-permute-start.24) | collective-permute-done | bytes 262176 | tf_op jit(solution)/shard_map/ppermute | solution.py:67
  268.6 3.5 collective-permute-start.23
  272.1 7.0 %collective-permute-done.25.refs_5_ = bf16[2,512,128]{2,1,0:T(8,128)(2,1)S(1)} collective-permute-done((bf16[2,512,128]{2,1,0:T(8,128)(2,1)S(1)}, bf16[2,512,128]{2,1,0:T(8,128)(2,1)S(1)}, u32[]{:S(2)}, u32[]{:S(2)}) %collective-permute-start.25) | collective-permute-done | bytes 262176 | tf_op jit(solution)/shard_map/ppermute | solution.py:67
  281.7 3.5 narrow.13
  290.7 5.4 %share.13 = (bf16[768,896]{1,0:T(8,128)(2,1)}, f32[8,128]{1,0:T(8,128)S(1)}) custom-call(s32[1]{0:T(128)} %bitcast.10.refs_0_, s32[1]{0:T(128)} %constant.59.clone.1.refs_0_.refs_1_, bf16[1536,1024]{1,0:T(8,128)(2,1)S(1)} %copy-done.39, bf16[1536,1024]{1,0:T(8,128)(2,1)S(1)} %copy-done.41, bf16[1024,512]{1,0:T(8,128)(2,1)S(1)} %copy-done.30, ...), custom_call_target="tpu_custom_call" | custom-call | flops 1409286 | bytes 4784 | tf_op jit(solution)/shard_map/share/pallas_call | solution.py:99
  296.1 4.4 narrow.14
  310.5 9.4 %share.14 = (bf16[768,2304]{1,0:T(8,128)(2,1)}, f32[8,128]{1,0:T(8,128)S(1)}) custom-call(s32[1]{0:T(128)} %bitcast.11.refs_0_, s32[1]{0:T(128)} %constant.59.clone.1.refs_0_.refs_1_, bf16[1536,1024]{1,0:T(8,128)(2,1)S(1)} %copy-done.23, bf16[512,2240]{1,0:T(8,128)(2,1)S(1)} %copy-done.26, bf16[512,2240]{1,0:T(8,128)(2,1)S(1)} %copy-done.28, ...), custom_call_target="tpu_custom_call" | custom-call | flops 3623878 | bytes 9830 | tf_op jit(solution)/shard_map/share/pallas_call | solution.py:99
  325.1 3.6 copy-done.4
  332.1 5.4 %narrow.15 = (bf16[256,1536]{1,0:T(8,128)(2,1)S(1)}, bf16[256,1536]{1,0:T(8,128)(2,1)S(1)}, f32[8,128]{1,0:T(8,128)S(1)}) custom-call(bf16[512,2240]{1,0:T(8,128)(2,1)S(1)} %copy-done.12, bf16[512,2240]{1,0:T(8,128)(2,1)S(1)} %copy-done.17, bf16[2240,1536]{1,0:T(8,128)(2,1)S(1)} %bitcast.60, bf16[256,1536]{1,0:T(8,128)(2,1)S(1)} %collective-permute-done.20.refs_3_, ...), custom_call_target="tpu_custom_call" | custom-call | flops 3523215 | bytes 10747 | tf_op jit(solution)/shard_map/narrow/pallas_call | solution.py:99
  338.4 4.2 collective-permute-done.30.refs_6_
  342.6 15.9 %collective-permute-done.31.refs_7_ = bf16[256,1536]{1,0:T(8,128)(2,1)S(1)} collective-permute-done((bf16[256,1536]{1,0:T(8,128)(2,1)}, bf16[256,1536]{1,0:T(8,128)(2,1)S(1)}, u32[]{:S(2)}, u32[]{:S(2)}) %collective-permute-start.31) | collective-permute-done | bytes 786464 | tf_op jit(solution)/shard_map/ppermute | solution.py:53
  358.6 3.7 norm_back.3
  366.6 7.7 %collective-permute-done.34.refs_5_ = bf16[768,1536]{1,0:T(8,128)(2,1)S(1)} collective-permute-done((bf16[768,1536]{1,0:T(8,128)(2,1)}, bf16[768,1536]{1,0:T(8,128)(2,1)S(1)}, u32[]{:S(2)}, u32[]{:S(2)}) %collective-permute-start.34) | collective-permute-done | bytes 2359328 | tf_op jit(solution)/shard_map/ppermute | solution.py:1164
  375.7 32.0 %collective-permute-done.35.refs_7_.refs_2_ = bf16[192,1280]{1,0:T(8,128)(2,1)S(1)} collective-permute-done((bf16[192,1280]{1,0:T(8,128)(2,1)S(1)}, bf16[192,1280]{1,0:T(8,128)(2,1)S(1)}, u32[]{:S(2)}, u32[]{:S(2)}) %collective-permute-start.35) | collective-permute-done | bytes 491552 | tf_op jit(solution)/shard_map/ppermute | solution.py:1174
  409.3 5.7 %share.15 = (bf16[384,1536]{1,0:T(8,128)(2,1)}, bf16[384,1536]{1,0:T(8,128)(2,1)}, f32[8,128]{1,0:T(8,128)S(1)}) custom-call(s32[1]{0:T(128)} %bitcast.11.refs_0_, s32[4]{0:T(128)S(1)} %pad_add_fusion.refs_1_, bf16[1536,1024]{1,0:T(8,128)(2,1)S(1)} %copy-done.24, bf16[512,2240]{1,0:T(8,128)(2,1)S(1)} %copy-done.5, bf16[512,2240]{1,0:T(8,128)(2,1)S(1)} %copy-done.7, ...), custom_call_target="tpu_custom_call" | custom-call | flops 2415919 | bytes 7077 | tf_op jit(solution)/shard_map/share/pallas_call | solution.py:99
  419.9 7.4 %collective-permute-done.29.refs_5_ = bf16[256,1536]{1,0:T(8,128)(2,1)S(1)} collective-permute-done((bf16[256,1536]{1,0:T(8,128)(2,1)S(1)}, bf16[256,1536]{1,0:T(8,128)(2,1)S(1)}, u32[]{:S(2)}, u32[]{:S(2)}) %collective-permute-start.29) | collective-permute-done | bytes 786464 | tf_op jit(solution)/shard_map/ppermute | solution.py:53
  429.7 7.1 %share.16 = (bf16[384,896]{1,0:T(8,128)(2,1)S(1)}, bf16[384,896]{1,0:T(8,128)(2,1)S(1)}, f32[8,128]{1,0:T(8,128)S(1)}) custom-call(s32[1]{0:T(128)} %bitcast.11.refs_0_, s32[4]{0:T(128)S(1)} %pad_add_fusion.refs_1_, bf16[1536,1024]{1,0:T(8,128)(2,1)S(1)} %copy-done.40, bf16[1536,1024]{1,0:T(8,128)(2,1)S(1)} %copy-done.42, bf16[1024,512]{1,0:T(8,128)(2,1)S(1)} %copy-done.31, ...), custom_call_target="tpu_custom_call" | custom-call | flops 1409286 | bytes 4784 | tf_op jit(solution)/shard_map/share/pallas_call | solution.py:99
  439.1 4.9 collective-permute-done.41.refs_1_
  445.2 4.0 share.17
  452.7 5.6 %collective-permute-done.42.refs_3_.refs_4_ = bf16[192,1024]{1,0:T(8,128)(2,1)S(1)} collective-permute-done((bf16[192,1024]{1,0:T(8,128)(2,1)S(1)}, bf16[192,1024]{1,0:T(8,128)(2,1)S(1)}, u32[]{:S(2)}, u32[]{:S(2)}) %collective-permute-start.42) | collective-permute-done | bytes 393248 | tf_op jit(solution)/shard_map/ppermute | solution.py:1196
  458.3 13.1 %collective-permute-done.39.refs_1_ = bf16[384,896]{1,0:T(8,128)(2,1)S(1)} collective-permute-done((bf16[384,896]{1,0:T(8,128)(2,1)S(1)}, bf16[384,896]{1,0:T(8,128)(2,1)S(1)}, u32[]{:S(2)}, u32[]{:S(2)}) %collective-permute-start.39) | collective-permute-done | bytes 688160 | tf_op jit(solution)/shard_map/ppermute | solution.py:1169
  473.9 5.1 finish.4
  479.1 3.9 collective-permute-done.44.refs_1_.refs_4_
  488.4 3.7 finish.5
  492.1 11.8 %collective-permute-done.43.refs_2_ = bf16[192,896]{1,0:T(8,128)(2,1)} collective-permute-done((bf16[192,896]{1,0:T(8,128)(2,1)}, bf16[192,896]{1,0:T(8,128)(2,1)}, u32[]{:S(2)}, u32[]{:S(2)}) %collective-permute-start.43) | collective-permute-done | bytes 344096 | tf_op jit(solution)/shard_map/ppermute | solution.py:1174
  506.1 3.6 finish.6
  511.5 5.4 %finish.7 = (f32[192,2240]{1,0:T(8,128)}, f32[192,128]{1,0:T(8,128)S(1)}, f32[8,128]{1,0:T(8,128)}) custom-call(bf16[384,1536]{1,0:T(8,128)(2,1)S(1)} %copy-done.59, bf16[384,1536]{1,0:T(8,128)(2,1)S(1)} %copy-done.61, bf16[192,1536]{1,0:T(8,128)(2,1)} %collective-permute-done.48.refs_2_, bf16[384,768]{1,0:T(8,128)(2,1)S(1)} %copy-done.78, ...), custom_call_target="tpu_custom_call" | custom-call | bytes 6021 | tf_op jit(solution)/shard_map/finish/pallas_call | solution.py:99
  520.7 5.7 %collective-permute-done.51 = f32[2,200,128]{2,1,0:T(8,128)S(1)} collective-permute-done((f32[2,200,128]{2,1,0:T(8,128)S(1)}, f32[2,200,128]{2,1,0:T(8,128)S(1)}, u32[]{:S(2)}, u32[]{:S(2)}) %collective-permute-start.51) | collective-permute-done | bytes 204832 | tf_op jit(solution)/shard_map/ppermute | solution.py:53
  (447 shorter events, 178.5 us)
Async XLA Ops:
  7.2 295.1 %reduce-scatter.3.cloned.1.call-start = ((), (), s32[]{:S(2)}) async-start(), calls=%async_computation.2 | async-start | bytes 3932160 | tf_op jit(solution)/shard_map/reduce_scatter | solution.py:1189
  23.0 33.6 %collective-permute-start.1 = (bf16[2,512,128]{2,1,0:T(8,128)(2,1)S(1)}, bf16[2,512,128]{2,1,0:T(8,128)(2,1)S(1)}, u32[]{:S(2)}, u32[]{:S(2)}) collective-permute-start(bf16[2,512,128]{2,1,0:T(8,128)(2,1)S(1)} %bitcast.74), channel_id=1, source_target_pairs={{0,4},{4,8},{8,12},{1,5},{5,9},{9,13},{2,6},{6,10},{10,14},{3,7},{... | collective-permute-start | bytes 786440 | tf_op jit(solution)/shard_map/ppermute | solution.py:67
  28.0 28.7 %collective-permute-start = (bf16[2,512,128]{2,1,0:T(8,128)(2,1)S(1)}, bf16[2,512,128]{2,1,0:T(8,128)(2,1)S(1)}, u32[]{:S(2)}, u32[]{:S(2)}) collective-permute-start(bf16[2,512,128]{2,1,0:T(8,128)(2,1)S(1)} %bitcast.75), channel_id=1, source_target_pairs={{0,8},{4,12},{1,9},{5,13},{2,10},{6,14},{3,11},{7,15},{16,24},{20,... | collective-permute-start | bytes 786440 | tf_op jit(solution)/shard_map/ppermute | solution.py:67
  56.8 4.8 collective-permute-start.2
  57.7 3.2 collective-permute-start.3
  73.1 2.4 collective-permute-start.4
  73.2 3.4 collective-permute-start.5
  80.0 20.7 %collective-permute-start.6 = (bf16[256,1536]{1,0:T(8,128)(2,1)}, bf16[256,1536]{1,0:T(8,128)(2,1)}, u32[]{:S(2)}, u32[]{:S(2)}) collective-permute-start(bf16[256,1536]{1,0:T(8,128)(2,1)} %get-tuple-element.161.refs_3_), channel_id=1, source_target_pairs={{0,2},{1,3},{2,0},{3,1},{4,6},{5,7},{6,4},{7,5},{8,10},{9,11},{10,... | collective-permute-start | bytes 2359304 | tf_op jit(solution)/shard_map/ppermute | solution.py:53
  81.5 46.6 %collective-permute-start.7 = (bf16[256,1536]{1,0:T(8,128)(2,1)}, bf16[256,1536]{1,0:T(8,128)(2,1)}, u32[]{:S(2)}, u32[]{:S(2)}) collective-permute-start(bf16[256,1536]{1,0:T(8,128)(2,1)} %get-tuple-element.164.refs_3_), channel_id=1, source_target_pairs={{0,2},{1,3},{2,0},{3,1},{4,6},{5,7},{6,4},{7,5},{8,10},{9,11},{10,... | collective-permute-start | bytes 2359304 | tf_op jit(solution)/shard_map/ppermute | solution.py:53
  152.2 334.3 %reduce-scatter.5.cloned.1.call-start = ((), (), s32[]{:S(2)}) async-start(), calls=%async_computation.3 | async-start | bytes 4423680 | tf_op jit(solution)/shard_map/reduce_scatter | solution.py:1209
  161.9 52.7 %collective-permute-start.16 = (bf16[768,1280]{1,0:T(8,128)(2,1)}, bf16[768,1280]{1,0:T(8,128)(2,1)}, u32[]{:S(2)}, u32[]{:S(2)}) collective-permute-start(bf16[768,1280]{1,0:T(8,128)(2,1)} %get-tuple-element.189), channel_id=1, source_target_pairs={{0,16},{16,0},{1,17},{17,1},{2,18},{18,2},{3,19},{19,3},{4,20},{20... | collective-permute-start | bytes 5898248 | tf_op jit(solution)/shard_map/ppermute | solution.py:1164
  178.3 3.4 collective-permute-start.13
  192.8 34.5 %collective-permute-start.14 = (bf16[256,1536]{1,0:T(8,128)(2,1)}, bf16[256,1536]{1,0:T(8,128)(2,1)}, u32[]{:S(2)}, u32[]{:S(2)}) collective-permute-start(bf16[256,1536]{1,0:T(8,128)(2,1)} %get-tuple-element.187.refs_5_), channel_id=1, source_target_pairs={{0,2},{1,3},{2,0},{3,1},{4,6},{5,7},{6,4},{7,5},{8,10},{9,11},{10,... | collective-permute-start | bytes 2359304 | tf_op jit(solution)/shard_map/ppermute | solution.py:53
  194.4 35.2 %collective-permute-start.15 = (bf16[256,1536]{1,0:T(8,128)(2,1)}, bf16[256,1536]{1,0:T(8,128)(2,1)}, u32[]{:S(2)}, u32[]{:S(2)}) collective-permute-start(bf16[256,1536]{1,0:T(8,128)(2,1)} %get-tuple-element.188.refs_6_), channel_id=1, source_target_pairs={{0,2},{1,3},{2,0},{3,1},{4,6},{5,7},{6,4},{7,5},{8,10},{9,11},{10,... | collective-permute-start | bytes 2359304 | tf_op jit(solution)/shard_map/ppermute | solution.py:53
  214.0 93.1 %collective-permute-start.22 = (bf16[768,2304]{1,0:T(8,128)(2,1)}, bf16[768,2304]{1,0:T(8,128)(2,1)}, u32[]{:S(2)}, u32[]{:S(2)}) collective-permute-start(bf16[768,2304]{1,0:T(8,128)(2,1)} %get-tuple-element.208), channel_id=1, source_target_pairs={{0,16},{16,0},{1,17},{17,1},{2,18},{18,2},{3,19},{19,3},{4,20},{20... | collective-permute-start | bytes 10616840 | tf_op jit(solution)/shard_map/ppermute | solution.py:1164
  235.4 2.4 collective-permute-start.17
  235.5 3.4 collective-permute-start.18
  248.4 3.6 collective-permute-start.19
  252.2 14.7 %collective-permute-start.24 = (bf16[2,512,128]{2,1,0:T(8,128)(2,1)S(1)}, bf16[2,512,128]{2,1,0:T(8,128)(2,1)S(1)}, u32[]{:S(2)}, u32[]{:S(2)}) collective-permute-start(bf16[2,512,128]{2,1,0:T(8,128)(2,1)S(1)} %get-tuple-element.214), channel_id=1, source_target_pairs={{4,0},{8,4},{12,8},{5,1},{9,5},{13,9},{6,2},{10,6},{14,10},{7,3},{... | collective-permute-start | bytes 786440 | tf_op jit(solution)/shard_map/ppermute | solution.py:67
  267.0 12.1 %collective-permute-start.25 = (bf16[2,512,128]{2,1,0:T(8,128)(2,1)S(1)}, bf16[2,512,128]{2,1,0:T(8,128)(2,1)S(1)}, u32[]{:S(2)}, u32[]{:S(2)}) collective-permute-start(bf16[2,512,128]{2,1,0:T(8,128)(2,1)S(1)} %get-tuple-element.216), channel_id=1, source_target_pairs={{4,0},{8,4},{12,8},{5,1},{9,5},{13,9},{6,2},{10,6},{14,10},{7,3},{... | collective-permute-start | bytes 786440 | tf_op jit(solution)/shard_map/ppermute | solution.py:67
  268.6 35.1 %collective-permute-start.23 = (bf16[384,1280]{1,0:T(8,128)(2,1)}, bf16[384,1280]{1,0:T(8,128)(2,1)}, u32[]{:S(2)}, u32[]{:S(2)}) collective-permute-start(bf16[384,1280]{1,0:T(8,128)(2,1)} %get-tuple-element.210), channel_id=1, source_target_pairs={{0,4},{4,0},{8,12},{12,8},{1,5},{5,1},{9,13},{13,9},{2,6},{6,2},{1... | collective-permute-start | bytes 2949128 | tf_op jit(solution)/shard_map/ppermute | solution.py:1169
  285.2 10.9 %collective-permute-start.26 = (bf16[256,1536]{1,0:T(8,128)(2,1)}, bf16[256,1536]{1,0:T(8,128)(2,1)}, u32[]{:S(2)}, u32[]{:S(2)}) collective-permute-start(bf16[256,1536]{1,0:T(8,128)(2,1)} %get-tuple-element.220), channel_id=1, source_target_pairs={{0,1},{1,0},{2,3},{3,2},{4,5},{5,4},{6,7},{7,6},{8,9},{9,8},{10,11... | collective-permute-start | bytes 2359304 | tf_op jit(solution)/shard_map/ppermute | solution.py:49
  285.2 10.9 %collective-permute-start.27 = (bf16[256,1536]{1,0:T(8,128)(2,1)}, bf16[256,1536]{1,0:T(8,128)(2,1)}, u32[]{:S(2)}, u32[]{:S(2)}) collective-permute-start(bf16[256,1536]{1,0:T(8,128)(2,1)} %get-tuple-element.221), channel_id=1, source_target_pairs={{0,1},{1,0},{2,3},{3,2},{4,5},{5,4},{6,7},{7,6},{8,9},{9,8},{10,11... | collective-permute-start | bytes 2359304 | tf_op jit(solution)/shard_map/ppermute | solution.py:49
  319.9 54.4 %collective-permute-start.34 = (bf16[768,1536]{1,0:T(8,128)(2,1)}, bf16[768,1536]{1,0:T(8,128)(2,1)S(1)}, u32[]{:S(2)}, u32[]{:S(2)}) collective-permute-start(bf16[768,1536]{1,0:T(8,128)(2,1)} %get-tuple-element.238), channel_id=1, source_target_pairs={{0,16},{16,0},{1,17},{17,1},{2,18},{18,2},{3,19},{19,3},{4,20},{20... | collective-permute-start | bytes 7077896 | tf_op jit(solution)/shard_map/ppermute | solution.py:1164
  321.5 2.5 collective-permute-start.20
  321.5 3.6 collective-permute-start.21
  322.0 20.6 %collective-permute-start.30 = (bf16[256,1536]{1,0:T(8,128)(2,1)}, bf16[256,1536]{1,0:T(8,128)(2,1)S(1)}, u32[]{:S(2)}, u32[]{:S(2)}) collective-permute-start(bf16[256,1536]{1,0:T(8,128)(2,1)} %copy-done.113), channel_id=1, source_target_pairs={{0,2},{1,3},{2,0},{3,1},{4,6},{5,7},{6,4},{7,5},{8,10},{9,11},{10,... | collective-permute-start | bytes 2359304 | tf_op jit(solution)/shard_map/ppermute | solution.py:53
  323.5 35.0 %collective-permute-start.31 = (bf16[256,1536]{1,0:T(8,128)(2,1)}, bf16[256,1536]{1,0:T(8,128)(2,1)S(1)}, u32[]{:S(2)}, u32[]{:S(2)}) collective-permute-start(bf16[256,1536]{1,0:T(8,128)(2,1)} %copy-done.115), channel_id=1, source_target_pairs={{0,2},{1,3},{2,0},{3,1},{4,6},{5,7},{6,4},{7,5},{8,10},{9,11},{10,... | collective-permute-start | bytes 2359304 | tf_op jit(solution)/shard_map/ppermute | solution.py:53
  362.3 52.7 %collective-permute-start.32 = (f32[256,1536]{1,0:T(8,128)}, f32[256,1536]{1,0:T(8,128)S(1)}, u32[]{:S(2)}, u32[]{:S(2)}) collective-permute-start(f32[256,1536]{1,0:T(8,128)} %get-tuple-element.236.refs_1_), channel_id=1, source_target_pairs={{0,1},{1,0},{2,3},{3,2},{4,5},{5,4},{6,7},{7,6},{8,9},{9,8},{10,11... | collective-permute-start | bytes 4718600 | tf_op jit(solution)/shard_map/ppermute | solution.py:49
  362.3 52.7 %collective-permute-start.33 = (f32[256,1536]{1,0:T(8,128)}, f32[256,1536]{1,0:T(8,128)S(1)}, u32[]{:S(2)}, u32[]{:S(2)}) collective-permute-start(f32[256,1536]{1,0:T(8,128)} %get-tuple-element.237.refs_2_), channel_id=1, source_target_pairs={{0,1},{1,0},{2,3},{3,2},{4,5},{5,4},{6,7},{7,6},{8,9},{9,8},{10,11... | collective-permute-start | bytes 4718600 | tf_op jit(solution)/shard_map/ppermute | solution.py:49
  362.8 45.0 %collective-permute-start.35 = (bf16[192,1280]{1,0:T(8,128)(2,1)S(1)}, bf16[192,1280]{1,0:T(8,128)(2,1)S(1)}, u32[]{:S(2)}, u32[]{:S(2)}) collective-permute-start(bf16[192,1280]{1,0:T(8,128)(2,1)S(1)} %copy-done.130), channel_id=1, source_target_pairs={{0,8},{4,12},{8,0},{12,4},{1,9},{5,13},{9,1},{13,5},{2,10},{6,14},... | collective-permute-start | bytes 1474568 | tf_op jit(solution)/shard_map/ppermute | solution.py:1174
  366.0 63.6 %collective-permute-start.38 = (bf16[768,896]{1,0:T(8,128)(2,1)}, bf16[768,896]{1,0:T(8,128)(2,1)}, u32[]{:S(2)}, u32[]{:S(2)}) collective-permute-start(bf16[768,896]{1,0:T(8,128)(2,1)} %get-tuple-element.245), channel_id=1, source_target_pairs={{0,16},{16,0},{1,17},{17,1},{2,18},{18,2},{3,19},{19,3},{4,20},{20... | collective-permute-start | bytes 4128776 | tf_op jit(solution)/shard_map/ppermute | solution.py:1164
  374.3 45.6 %collective-permute-start.28 = (bf16[256,1536]{1,0:T(8,128)(2,1)S(1)}, bf16[256,1536]{1,0:T(8,128)(2,1)S(1)}, u32[]{:S(2)}, u32[]{:S(2)}) collective-permute-start(bf16[256,1536]{1,0:T(8,128)(2,1)S(1)} %copy-done.118), channel_id=1, source_target_pairs={{0,2},{1,3},{2,0},{3,1},{4,6},{5,7},{6,4},{7,5},{8,10},{9,11},{10,... | collective-permute-start | bytes 2359304 | tf_op jit(solution)/shard_map/ppermute | solution.py:53
  407.8 19.5 %collective-permute-start.29 = (bf16[256,1536]{1,0:T(8,128)(2,1)S(1)}, bf16[256,1536]{1,0:T(8,128)(2,1)S(1)}, u32[]{:S(2)}, u32[]{:S(2)}) collective-permute-start(bf16[256,1536]{1,0:T(8,128)(2,1)S(1)} %get-tuple-element.231.refs_3_), channel_id=1, source_target_pairs={{0,2},{1,3},{2,0},{3,1},{4,6},{5,7},{6,4},{7,5},{8,10},{9,11},{10,... | collective-permute-start | bytes 2359304 | tf_op jit(solution)/shard_map/ppermute | solution.py:53
  415.0 29.1 %collective-permute-start.41 = (bf16[384,1536]{1,0:T(8,128)(2,1)}, bf16[384,1536]{1,0:T(8,128)(2,1)S(1)}, u32[]{:S(2)}, u32[]{:S(2)}) collective-permute-start(bf16[384,1536]{1,0:T(8,128)(2,1)} %get-tuple-element.254), channel_id=1, source_target_pairs={{0,4},{4,0},{8,12},{12,8},{1,5},{5,1},{9,13},{13,9},{2,6},{6,2},{1... | collective-permute-start | bytes 3538952 | tf_op jit(solution)/shard_map/ppermute | solution.py:1169
  415.0 30.2 %collective-permute-start.40 = (bf16[768,768]{1,0:T(8,128)(2,1)}, bf16[768,768]{1,0:T(8,128)(2,1)}, u32[]{:S(2)}, u32[]{:S(2)}) collective-permute-start(bf16[768,768]{1,0:T(8,128)(2,1)} %get-tuple-element.252), channel_id=1, source_target_pairs={{0,16},{16,0},{1,17},{17,1},{2,18},{18,2},{3,19},{19,3},{4,20},{20... | collective-permute-start | bytes 3538952 | tf_op jit(solution)/shard_map/ppermute | solution.py:1164
  429.1 7.8 %collective-permute-start.36 = (bf16[256,1536]{1,0:T(8,128)(2,1)S(1)}, bf16[256,1536]{1,0:T(8,128)(2,1)S(1)}, u32[]{:S(2)}, u32[]{:S(2)}) collective-permute-start(bf16[256,1536]{1,0:T(8,128)(2,1)S(1)} %get-tuple-element.243.refs_1_), channel_id=1, source_target_pairs={{0,1},{1,0},{2,3},{3,2},{4,5},{5,4},{6,7},{7,6},{8,9},{9,8},{10,11... | collective-permute-start | bytes 2359304 | tf_op jit(solution)/shard_map/ppermute | solution.py:49
  429.2 7.8 %collective-permute-start.37 = (bf16[256,1536]{1,0:T(8,128)(2,1)S(1)}, bf16[256,1536]{1,0:T(8,128)(2,1)S(1)}, u32[]{:S(2)}, u32[]{:S(2)}) collective-permute-start(bf16[256,1536]{1,0:T(8,128)(2,1)S(1)} %get-tuple-element.244.refs_2_), channel_id=1, source_target_pairs={{0,1},{1,0},{2,3},{3,2},{4,5},{5,4},{6,7},{7,6},{8,9},{9,8},{10,11... | collective-permute-start | bytes 2359304 | tf_op jit(solution)/shard_map/ppermute | solution.py:49
  436.9 34.6 %collective-permute-start.39 = (bf16[384,896]{1,0:T(8,128)(2,1)S(1)}, bf16[384,896]{1,0:T(8,128)(2,1)S(1)}, u32[]{:S(2)}, u32[]{:S(2)}) collective-permute-start(bf16[384,896]{1,0:T(8,128)(2,1)S(1)} %get-tuple-element.251), channel_id=1, source_target_pairs={{0,4},{4,0},{8,12},{12,8},{1,5},{5,1},{9,13},{13,9},{2,6},{6,2},{1... | collective-permute-start | bytes 2064392 | tf_op jit(solution)/shard_map/ppermute | solution.py:1169
  449.2 33.8 %collective-permute-start.44 = (bf16[384,768]{1,0:T(8,128)(2,1)S(1)}, bf16[384,768]{1,0:T(8,128)(2,1)S(1)}, u32[]{:S(2)}, u32[]{:S(2)}) collective-permute-start(bf16[384,768]{1,0:T(8,128)(2,1)S(1)} %get-tuple-element.261), channel_id=1, source_target_pairs={{0,4},{4,0},{8,12},{12,8},{1,5},{5,1},{9,13},{13,9},{2,6},{6,2},{1... | collective-permute-start | bytes 1769480 | tf_op jit(solution)/shard_map/ppermute | solution.py:1169
  449.3 9.0 %collective-permute-start.42 = (bf16[192,1024]{1,0:T(8,128)(2,1)S(1)}, bf16[192,1024]{1,0:T(8,128)(2,1)S(1)}, u32[]{:S(2)}, u32[]{:S(2)}) collective-permute-start(bf16[192,1024]{1,0:T(8,128)(2,1)S(1)} %copy-done.92), channel_id=1, source_target_pairs={{0,16},{16,0},{1,17},{17,1},{2,18},{18,2},{3,19},{19,3},{4,20},{20... | collective-permute-start | bytes 1179656 | tf_op jit(solution)/shard_map/ppermute | solution.py:1196
  450.8 60.7 %collective-permute-start.48 = (bf16[192,1536]{1,0:T(8,128)(2,1)}, bf16[192,1536]{1,0:T(8,128)(2,1)}, u32[]{:S(2)}, u32[]{:S(2)}) collective-permute-start(bf16[192,1536]{1,0:T(8,128)(2,1)} %get-tuple-element.273), channel_id=1, source_target_pairs={{0,8},{4,12},{8,0},{12,4},{1,9},{5,13},{9,1},{13,5},{2,10},{6,14},... | collective-permute-start | bytes 1769480 | tf_op jit(solution)/shard_map/ppermute | solution.py:1174
  472.4 31.5 %collective-permute-start.43 = (bf16[192,896]{1,0:T(8,128)(2,1)}, bf16[192,896]{1,0:T(8,128)(2,1)}, u32[]{:S(2)}, u32[]{:S(2)}) collective-permute-start(bf16[192,896]{1,0:T(8,128)(2,1)} %get-tuple-element.258), channel_id=1, source_target_pairs={{0,8},{4,12},{8,0},{12,4},{1,9},{5,13},{9,1},{13,5},{2,10},{6,14},... | collective-permute-start | bytes 1032200 | tf_op jit(solution)/shard_map/ppermute | solution.py:1174
  472.4 6.7 %collective-permute-start.45 = (f32[8,512]{1,0:T(8,128)S(1)}, f32[8,512]{1,0:T(8,128)S(1)}, u32[]{:S(2)}, u32[]{:S(2)}) collective-permute-start(f32[8,512]{1,0:T(8,128)S(1)} %copy-done.122), channel_id=1, source_target_pairs={{0,16},{16,0},{1,17},{17,1},{2,18},{18,2},{3,19},{19,3},{4,20},{20... | collective-permute-start | bytes 49160 | tf_op jit(solution)/shard_map/ppermute | solution.py:1310
  484.4 27.0 %collective-permute-start.49 = (bf16[192,768]{1,0:T(8,128)(2,1)}, bf16[192,768]{1,0:T(8,128)(2,1)S(1)}, u32[]{:S(2)}, u32[]{:S(2)}) collective-permute-start(bf16[192,768]{1,0:T(8,128)(2,1)} %get-tuple-element.274), channel_id=1, source_target_pairs={{0,8},{4,12},{8,0},{12,4},{1,9},{5,13},{9,1},{13,5},{2,10},{6,14},... | collective-permute-start | bytes 884744 | tf_op jit(solution)/shard_map/ppermute | solution.py:1174
  484.4 25.2 %collective-permute-start.46 = (f32[8,512]{1,0:T(8,128)S(1)}, f32[8,512]{1,0:T(8,128)}, u32[]{:S(2)}, u32[]{:S(2)}) collective-permute-start(f32[8,512]{1,0:T(8,128)S(1)} %get-tuple-element.269.refs_0_), channel_id=1, source_target_pairs={{0,4},{4,0},{8,12},{12,8},{1,5},{5,1},{9,13},{13,9},{2,6},{6,2},{1... | collective-permute-start | bytes 49160 | tf_op jit(solution)/shard_map/ppermute | solution.py:1312
  510.4 6.7 %collective-permute-start.47 = (f32[8,512]{1,0:T(8,128)S(1)}, f32[8,512]{1,0:T(8,128)}, u32[]{:S(2)}, u32[]{:S(2)}) collective-permute-start(f32[8,512]{1,0:T(8,128)S(1)} %get-tuple-element.271), channel_id=1, source_target_pairs={{0,8},{4,12},{8,0},{12,4},{1,9},{5,13},{9,1},{13,5},{2,10},{6,14},... | collective-permute-start | bytes 49160 | tf_op jit(solution)/shard_map/ppermute | solution.py:1319
  519.2 7.2 %collective-permute-start.51 = (f32[2,200,128]{2,1,0:T(8,128)S(1)}, f32[2,200,128]{2,1,0:T(8,128)S(1)}, u32[]{:S(2)}, u32[]{:S(2)}) collective-permute-start(f32[2,200,128]{2,1,0:T(8,128)S(1)} %maximum_select_fusion.1), channel_id=1, source_target_pairs={{0,2},{1,3},{2,0},{3,1},{4,6},{5,7},{6,4},{7,5},{8,10},{9,11},{10,... | collective-permute-start | bytes 614408 | tf_op jit(solution)/shard_map/ppermute | solution.py:53
  (146 other events, 1420.0 us)
Sparse Core Ops, SparseCore 0:
  152.4 61.8 reduce-scatter.2
  320.0 77.6 reduce-scatter.4

commit v9 on v6

--- a/solution.py
+++ b/solution.py
@@ -1131,6 +1131,7 @@
             if near_pair:
                 sent = lax.dynamic_slice_in_dim(self.mine, (1 - dp_index) * share, share, 0)
                 self.mine = lax.dynamic_slice_in_dim(self.mine, dp_index * share, share, 0)
+                order.arrived(sent, self.mine)
                 self.come = lax.ppermute(sent, "dp", flipped("dp", 0))
 
         def settled(self):
@@ -1201,6 +1202,7 @@
     )
     both_come = core_swap(sent)
     branch_t = turn(order, branch)
+    down_a.relay()
     own_kv, *pieces = fold(order, keep, both_come, local)
     moving = shifted(pieces[-1], -1) if pieces else None
     ffn_sent = core_swaps(narrow(order, [(hidden, down_t)], 1))
@@ -1214,7 +1216,8 @@
     last = Rows([h_one_t, branch_t], [grad_qkv, mixed], last_parts, HD)
     mine = narrow(order, [(grad_qkv, weight)], 0, sent, 1)
     come = chip_swaps(mine)
-    down_a.relay()
+    down_b.across()
+    down_a.settled()
     gate.own()
     ffn_mine = narrow(order, [(hidden, down_t)], 0, ffn_sent)
     token = norm_back(order, core_one, mine, come, flat_tokens, gain_one, grad_middle, True)
@@ -1222,15 +1225,14 @@
     ffn_come = chip_swaps(ffn_mine)
     token_grad = place(order, core_one, token).reshape(rows, local, width)
     up_a.own()
-    down_a.settled()
     layer = layer_of(order, middle, ffn_mine, ffn_come)
     layer += core_swaps(layer)
-    down_b.across()
     last.own()
     layer_out = place(order, core_one, layer).reshape(rows, local, width)
     up_a.relay()
+    up_b.own()
     down_b.settled()
-    up_b.own()
+    up_a.settled()
     last.relay()
     (down_grad,) = finish(order, [down_a.result(), down_b.result()], share, units, TILE)
     if near_pair:

time: 516 us -> 499 us (0.967)
  waiting for transfers between devices: 171 us -> 132 us
  local copies, waits for them, and re-layouts: 76.5 us -> 87.2 us
  starting transfers between devices: 46.6 us -> 56.2 us
    ppermute x4, waiting for transfers between devices: 46.5 us -> 2.66 us  [relay(): self.last = lax.ppermute(sent, 'seq', flipped('seq', 1))]
    ppermute x5, waiting for transfers between devices: 7.36 us -> 30.9 us  [__init__(): self.come = lax.ppermute(sent, 'dp', flipped('dp', 0))]
    ppermute x4, waiting for transfers between devices: 30.5 us -> 16.6 us  [shifted(): return lax.ppermute(value, 'seq', route)]
    unnamed x219 -> x243, local copies, waits for them, and re-layouts: 66.3 us -> 77 us
    ppermute x9, waiting for transfers between devices: 35.2 us -> 45.1 us  [chip_swap(): return lax.ppermute(value, 'tensor', flipped('tensor', 1))]
    ppermute x4, waiting for transfers between devices: 24.4 us -> 14.8 us  [own(): self.come = lax.ppermute(send, 'seq', flipped('seq', 0))]
    ppermute x4, starting transfers between devices: 2.85 us -> 10.1 us  [own(): self.come = lax.ppermute(send, 'seq', flipped('seq', 0))]
    ppermute x21, waiting for transfers between devices: 19.5 us -> 13.4 us  [core_swap(): return lax.ppermute(value, 'tensor', flipped('tensor', 0))]
  transfers between devices with their start and end apart: 53 -> 53, of which waited for: 31 -> 28; matrix products, arithmetic and copies ran while one was open for 3% -> 3% of each run, Pallas kernels for 29% -> 29%
where the time goes in v9:
time: 499 us; the launch traced here: 493 us
  Pallas kernels  193 us (39%)
  waiting for transfers between devices  132 us (26%)
  local copies, waits for them, and re-layouts  87.2 us (17%)
  starting transfers between devices  56.2 us (11%)
  between operations  15.8 us (3%)
  other arithmetic  9.37 us (2%)
    pallas_call x44, Pallas kernels, __call__(): pl.pallas_call(run, grid_spec=pltpu.PrefetchScalarGridSpec(num_scalar_pre...  183 us
    unnamed x243, local copies, waits for them, and re-layouts  77 us
    ppermute x9, waiting for transfers between devices, chip_swap(): return lax.ppermute(value, 'tensor', flipped('tensor', 1))  45.1 us
    ppermute x5, waiting for transfers between devices, __init__(): self.come = lax.ppermute(sent, 'dp', flipped('dp', 0))  30.9 us
    ppermute x4, waiting for transfers between devices, shifted(): return lax.ppermute(value, 'seq', route)  16.6 us
    ppermute x4, waiting for transfers between devices, own(): self.come = lax.ppermute(send, 'seq', flipped('seq', 0))  14.8 us
    ppermute x4, starting transfers between devices, shifted(): return lax.ppermute(value, 'seq', route)  13.4 us
    ppermute x21, waiting for transfers between devices, core_swap(): return lax.ppermute(value, 'tensor', flipped('tensor', 0))  13.4 us
  transfers between devices with their start and end apart: 53, of which 28 were waited for; matrix products, arithmetic and copies ran while one was open for 3% of the time, Pallas kernels for 29%

profile of v9, /device:TPU:0, one launch (start us, length us, event | category | flops | bytes accessed | tf_op | source)
XLA Modules:
  0.0 493.3 jit_solution(6279925211505468243)
XLA Ops:
  17.2 3.6 first.1
  23.4 5.7 %collective-permute-start.1 = (bf16[2,512,128]{2,1,0:T(8,128)(2,1)S(1)}, bf16[2,512,128]{2,1,0:T(8,128)(2,1)}, u32[]{:S(2)}, u32[]{:S(2)}) collective-permute-start(bf16[2,512,128]{2,1,0:T(8,128)(2,1)S(1)} %bitcast.75), channel_id=1, source_target_pairs={{0,4},{4,8},{8,12},{1,5},{5,9},{9,13},{2,6},{6,10},{10,14},{3,7},{... | collective-permute-start | bytes 786440 | tf_op jit(solution)/shard_map/ppermute | solution.py:66
  29.1 4.9 %collective-permute-start = (bf16[2,512,128]{2,1,0:T(8,128)(2,1)S(1)}, bf16[2,512,128]{2,1,0:T(8,128)(2,1)}, u32[]{:S(2)}, u32[]{:S(2)}) collective-permute-start(bf16[2,512,128]{2,1,0:T(8,128)(2,1)S(1)} %bitcast.76), channel_id=1, source_target_pairs={{0,8},{4,12},{1,9},{5,13},{2,10},{6,14},{3,11},{7,15},{16,24},{20,... | collective-permute-start | bytes 786440 | tf_op jit(solution)/shard_map/ppermute | solution.py:66
  34.6 4.3 collective-permute-done.refs_0_.refs_9_
  41.9 6.1 %attend.1 = (bf16[2,512,384]{2,1,0:T(8,128)(2,1)S(1)}, f32[2,2,768]{2,1,0:T(2,128)S(1)}) custom-call(s32[2,2]{1,0:T(2,128)S(1)} %shift-right-logical_maximum_fusion.low_ref.refs_0_, s32[1]{0:T(128)} %bitcast.core_ref.refs_0_.refs_1_, bf16[2,512,384]{2,1,0:T(8,128)(2,1)S(1)} %bitcast.72, s32[2,1,512]{2,1,0:T(1,128)S(1)} %sub.44.start_ref.refs_3_, ...), custom_call_target="tpu_custom_call" | custom-call | flops 8000000 | bytes 4194 | tf_op jit(solution)/shard_map/attend/pallas_call | solution.py:253
  53.6 3.5 narrow.9
  60.4 4.5 constant_dynamic-slice_fusion.2
  74.6 5.2 %copy-done.10 = bf16[1536,2240]{0,1:T(8,128)(2,1)S(1)} copy-done((bf16[1536,2240]{0,1:T(8,128)(2,1)S(1)}, bf16[1536,2240]{0,1:T(8,128)(2,1)}, u32[]{:S(2)}) %copy-start.10) | copy-done | bytes 6881304
  79.8 9.3 %grad_hidden.1 = (bf16[1024,2240]{1,0:T(8,128)(2,1)S(1)}, f32[8,128]{1,0:T(8,128)S(1)}) custom-call(bf16[1024,1536]{1,0:T(8,128)(2,1)S(1)} %get-tuple-element.146.refs_0_.refs_3_, bf16[2240,1536]{1,0:T(8,128)(2,1)S(1)} %bitcast.59, f32[8,128]{1,0:T(8,128)S(1)} %get-tuple-element.147.refs_2_, bf16[192,2240]{1,0:T(8,128)(2,1)S(1)} %copy-done.45, ...), custom_call_target="tpu_custom_call" | custom-call | flops 7046430 | bytes 15728 | tf_op jit(solution)/shard_map/grad_hidden/pallas_call | solution.py:92
  94.5 3.8 middle.1
  104.2 20.3 %gated.1 = (bf16[1024,2240]{1,0:T(8,128)(2,1)S(1)}, bf16[1024,2240]{1,0:T(8,128)(2,1)S(1)}, bf16[1024,2240]{1,0:T(8,128)(2,1)S(1)}, f32[8,128]{1,0:T(8,128)S(1)}) custom-call(bf16[1024,2240]{1,0:T(8,128)(2,1)S(1)} %copy-done.54, bf16[2240,1536]{1,0:T(8,128)(2,1)} %bitcast.56, bf16[2240,1536]{1,0:T(8,128)(2,1)} %bitcast.81, ...), custom_call_target="tpu_custom_call" | custom-call | flops 14092861 | bytes 31457 | tf_op jit(solution)/shard_map/gated/pallas_call | solution.py:92
  126.7 4.6 share.9
  139.7 4.2 share.10
  147.8 3.0 copy-done.8
  150.7 10.4 %narrow.10 = (bf16[256,1536]{1,0:T(8,128)(2,1)S(1)}, bf16[256,1536]{1,0:T(8,128)(2,1)S(1)}, f32[8,128]{1,0:T(8,128)S(1)}) custom-call(bf16[1024,2240]{1,0:T(8,128)(2,1)S(1)} %copy-done.6, bf16[2240,1536]{1,0:T(8,128)(2,1)S(1)} %bitcast.57, bf16[1024,2240]{1,0:T(8,128)(2,1)S(1)} %bitcast.47, bf16[2240,1536]{1,0:T(8,128)(2,1)} %bitcast.82, ...), custom_call_target="tpu_custom_call" | custom-call | flops 7046430 | bytes 19922 | tf_op jit(solution)/shard_map/narrow/pallas_call | solution.py:92
  164.6 3.1 copy-done.9
  167.7 11.1 %narrow.11 = (bf16[256,1536]{1,0:T(8,128)(2,1)}, bf16[256,1536]{1,0:T(8,128)(2,1)}, f32[8,128]{1,0:T(8,128)S(1)}) custom-call(bf16[1024,2240]{1,0:T(8,128)(2,1)S(1)} %bitcast.53, bf16[2240,1536]{1,0:T(8,128)(2,1)S(1)} %bitcast.58, bf16[1024,2240]{1,0:T(8,128)(2,1)S(1)} %bitcast.47, bf16[2240,1536]{1,0:T(8,128)(2,1)} %bitcast.83, ...), custom_call_target="tpu_custom_call" | custom-call | flops 7046430 | bytes 19922 | tf_op jit(solution)/shard_map/narrow/pallas_call | solution.py:92
  182.4 13.6 %share.11 = (bf16[768,2304]{1,0:T(8,128)(2,1)}, bf16[768,1536]{1,0:T(8,128)(2,1)S(1)}, bf16[768,768]{1,0:T(8,128)(2,1)S(1)}, f32[8,128]{1,0:T(8,128)S(1)}) custom-call(s32[1]{0:T(128)} %bitcast.10.refs_0_, s32[1]{0:T(128)} %constant.59.clone.1.refs_0_.refs_1_, bf16[1536,1024]{1,0:T(8,128)(2,1)S(1)} %get-tuple-element.169.refs_2_, ...), custom_call_target="tpu_custom_call" | custom-call | flops 7247757 | bytes 18087 | tf_op jit(solution)/shard_map/share/pallas_call | solution.py:92
  203.2 5.9 %share.12 = (bf16[384,1280]{1,0:T(8,128)(2,1)S(1)}, bf16[384,1280]{1,0:T(8,128)(2,1)S(1)}, f32[8,128]{1,0:T(8,128)S(1)}) custom-call(s32[1]{0:T(128)} %bitcast.11.refs_0_, s32[4]{0:T(128)S(1)} %pad_add_fusion.refs_1_, bf16[1536,1024]{1,0:T(8,128)(2,1)S(1)} %copy-done.18, bf16[1024,2240]{1,0:T(8,128)(2,1)S(1)} %copy-done.3, ...), custom_call_target="tpu_custom_call" | custom-call | flops 2013265 | bytes 6160 | tf_op jit(solution)/shard_map/share/pallas_call | solution.py:92
  209.2 6.4 %collective-permute-done.14.refs_7_ = bf16[256,1536]{1,0:T(8,128)(2,1)} collective-permute-done((bf16[256,1536]{1,0:T(8,128)(2,1)}, bf16[256,1536]{1,0:T(8,128)(2,1)}, u32[]{:S(2)}, u32[]{:S(2)}) %collective-permute-start.14) | collective-permute-done | bytes 786464 | tf_op jit(solution)/shard_map/ppermute | solution.py:52
  215.6 4.0 norm_back.2
  220.2 10.0 %collective-permute-start.19 = (bf16[384,1280]{1,0:T(8,128)(2,1)S(1)}, bf16[384,1280]{1,0:T(8,128)(2,1)S(1)}, u32[]{:S(2)}, u32[]{:S(2)}) collective-permute-start(bf16[384,1280]{1,0:T(8,128)(2,1)S(1)} %get-tuple-element.182), channel_id=1, source_target_pairs={{0,4},{4,0},{8,12},{12,8},{1,5},{5,1},{9,13},{13,9},{2,6},{6,2},{1... | collective-permute-start | bytes 2949128 | tf_op jit(solution)/shard_map/ppermute | solution.py:1108
  232.1 8.9 %attend_back.1 = (bf16[2,512,384]{2,1,0:T(8,128)(2,1)S(1)}, bf16[2,1536,128]{2,1,0:T(8,128)(2,1)S(1)}, bf16[2,1536,128]{2,1,0:T(8,128)(2,1)S(1)}, f32[8,128]{1,0:T(8,128)S(1)}) custom-call(s32[2,2]{1,0:T(2,128)S(1)} %shift-right-logical_maximum_fusion.low_ref.refs_0_, s32[1]{0:T(128)} %bitcast.core_ref.refs_0_.refs_1_, bf16[2,512,384]{2,1,0:T(8,128)(2,1)S(1)} %bitcast.73, ...), custom_call_target="tpu_custom_call" | custom-call | flops 20000000 | bytes 6291 | tf_op jit(solution)/shard_map/attend_back/pallas_call | solution.py:92
  244.2 8.0 %collective-permute-done.19.refs_1_ = bf16[384,1280]{1,0:T(8,128)(2,1)S(1)} collective-permute-done((bf16[384,1280]{1,0:T(8,128)(2,1)S(1)}, bf16[384,1280]{1,0:T(8,128)(2,1)S(1)}, u32[]{:S(2)}, u32[]{:S(2)}) %collective-permute-start.19) | collective-permute-done | bytes 983072 | tf_op jit(solution)/shard_map/ppermute | solution.py:1108
  254.9 5.3 %narrow.12 = (bf16[256,1536]{1,0:T(8,128)(2,1)S(1)}, bf16[256,1536]{1,0:T(8,128)(2,1)S(1)}, f32[8,128]{1,0:T(8,128)S(1)}) custom-call(bf16[1024,2240]{1,0:T(8,128)(2,1)S(1)} %bitcast.51, bf16[2240,1536]{1,0:T(8,128)(2,1)S(1)} %bitcast.62, f32[8,128]{1,0:T(8,128)S(1)} %get-tuple-element.186.refs_2_), custom_call_target="tpu_custom_call" | custom-call | flops 3523215 | bytes 10747 | tf_op jit(solution)/shard_map/narrow/pallas_call | solution.py:92
  260.2 3.1 collective-permute-done.23.refs_1_
  264.9 8.8 %collective-permute-done.24.refs_5_ = bf16[2,512,128]{2,1,0:T(8,128)(2,1)S(1)} collective-permute-done((bf16[2,512,128]{2,1,0:T(8,128)(2,1)S(1)}, bf16[2,512,128]{2,1,0:T(8,128)(2,1)S(1)}, u32[]{:S(2)}, u32[]{:S(2)}) %collective-permute-start.24) | collective-permute-done | bytes 262176 | tf_op jit(solution)/shard_map/ppermute | solution.py:66
  274.4 3.4 narrow.13
  284.5 5.3 %share.13 = (bf16[768,896]{1,0:T(8,128)(2,1)}, f32[8,128]{1,0:T(8,128)S(1)}) custom-call(s32[1]{0:T(128)} %bitcast.10.refs_0_, s32[1]{0:T(128)} %constant.59.clone.1.refs_0_.refs_1_, bf16[1536,1024]{1,0:T(8,128)(2,1)S(1)} %copy-done.29, bf16[1536,1024]{1,0:T(8,128)(2,1)S(1)} %copy-done.35, bf16[1024,512]{1,0:T(8,128)(2,1)S(1)} %get-tuple-element.197.refs_0_.refs_4_, ...), custom_call_target="tpu_custom_call" | custom-call | flops 1409286 | bytes 4784 | tf_op jit(solution)/shard_map/share/pallas_call | solution.py:92
  306.4 8.3 %share.14 = (bf16[768,2304]{1,0:T(8,128)(2,1)S(1)}, f32[8,128]{1,0:T(8,128)S(1)}) custom-call(s32[1]{0:T(128)} %bitcast.11.refs_0_, s32[1]{0:T(128)} %constant.59.clone.1.refs_0_.refs_1_, bf16[1536,1024]{1,0:T(8,128)(2,1)S(1)} %copy-done.13, bf16[1024,2240]{1,0:T(8,128)(2,1)S(1)} %copy-done.7, bf16[768,2304]{1,0:T(8,128)(2,1)} %collective-permute-done.22.refs_4_, ...), custom_call_target="tpu_custom_call" | custom-call | flops 3623878 | bytes 9830 | tf_op jit(solution)/shard_map/share/pallas_call | solution.py:92
  320.6 3.0 copy-done.4
  326.6 5.4 %narrow.15 = (bf16[256,1536]{1,0:T(8,128)(2,1)S(1)}, bf16[256,1536]{1,0:T(8,128)(2,1)S(1)}, f32[8,128]{1,0:T(8,128)S(1)}) custom-call(bf16[1024,2240]{1,0:T(8,128)(2,1)S(1)} %copy-done.4, bf16[2240,1536]{1,0:T(8,128)(2,1)S(1)} %bitcast.63, bf16[256,1536]{1,0:T(8,128)(2,1)S(1)} %collective-permute-done.20.refs_2_, ...), custom_call_target="tpu_custom_call" | custom-call | flops 3523215 | bytes 10747 | tf_op jit(solution)/shard_map/narrow/pallas_call | solution.py:92
  332.0 5.7 %collective-permute-done.31.refs_6_ = bf16[256,1536]{1,0:T(8,128)(2,1)S(1)} collective-permute-done((bf16[256,1536]{1,0:T(8,128)(2,1)}, bf16[256,1536]{1,0:T(8,128)(2,1)S(1)}, u32[]{:S(2)}, u32[]{:S(2)}) %collective-permute-start.31) | collective-permute-done | bytes 786464 | tf_op jit(solution)/shard_map/ppermute | solution.py:52
  337.7 16.0 %collective-permute-done.32.refs_7_ = bf16[256,1536]{1,0:T(8,128)(2,1)S(1)} collective-permute-done((bf16[256,1536]{1,0:T(8,128)(2,1)}, bf16[256,1536]{1,0:T(8,128)(2,1)S(1)}, u32[]{:S(2)}, u32[]{:S(2)}) %collective-permute-start.32) | collective-permute-done | bytes 786464 | tf_op jit(solution)/shard_map/ppermute | solution.py:52
  361.5 3.0 place.2
  364.6 8.9 %collective-permute-done.30.refs_4_ = bf16[768,1536]{1,0:T(8,128)(2,1)S(1)} collective-permute-done((bf16[768,1536]{1,0:T(8,128)(2,1)}, bf16[768,1536]{1,0:T(8,128)(2,1)S(1)}, u32[]{:S(2)}, u32[]{:S(2)}) %collective-permute-start.30) | collective-permute-done | bytes 2359328 | tf_op jit(solution)/shard_map/ppermute | solution.py:1103
  373.6 5.4 %share.15 = (bf16[384,1536]{1,0:T(8,128)(2,1)}, bf16[384,1536]{1,0:T(8,128)(2,1)S(1)}, f32[8,128]{1,0:T(8,128)S(1)}) custom-call(s32[1]{0:T(128)} %bitcast.11.refs_0_, s32[4]{0:T(128)S(1)} %pad_add_fusion.refs_1_, bf16[1536,1024]{1,0:T(8,128)(2,1)S(1)} %copy-done.13, bf16[1024,2240]{1,0:T(8,128)(2,1)S(1)} %bitcast.49, ...), custom_call_target="tpu_custom_call" | custom-call | flops 2415919 | bytes 7077 | tf_op jit(solution)/shard_map/share/pallas_call | solution.py:92
  380.5 12.3 %collective-permute-done.29.refs_4_ = bf16[256,1536]{1,0:T(8,128)(2,1)S(1)} collective-permute-done((bf16[256,1536]{1,0:T(8,128)(2,1)S(1)}, bf16[256,1536]{1,0:T(8,128)(2,1)S(1)}, u32[]{:S(2)}, u32[]{:S(2)}) %collective-permute-start.29) | collective-permute-done | bytes 786464 | tf_op jit(solution)/shard_map/ppermute | solution.py:52
  394.6 8.4 %collective-permute-done.37.refs_6_ = bf16[768,896]{1,0:T(8,128)(2,1)S(1)} collective-permute-done((bf16[768,896]{1,0:T(8,128)(2,1)}, bf16[768,896]{1,0:T(8,128)(2,1)S(1)}, u32[]{:S(2)}, u32[]{:S(2)}) %collective-permute-start.37) | collective-permute-done | bytes 1376288 | tf_op jit(solution)/shard_map/ppermute | solution.py:1103
  403.0 5.8 %share.16 = (bf16[384,896]{1,0:T(8,128)(2,1)S(1)}, bf16[384,896]{1,0:T(8,128)(2,1)S(1)}, f32[8,128]{1,0:T(8,128)S(1)}) custom-call(s32[1]{0:T(128)} %bitcast.11.refs_0_, s32[4]{0:T(128)S(1)} %pad_add_fusion.refs_1_, bf16[1536,1024]{1,0:T(8,128)(2,1)S(1)} %copy-done.30, bf16[1536,1024]{1,0:T(8,128)(2,1)S(1)} %copy-done.36, bf16[1024,512]{1,0:T(8,128)(2,1)S(1)} %copy-done.27, ...), custom_call_target="tpu_custom_call" | custom-call | flops 1409286 | bytes 4784 | tf_op jit(solution)/shard_map/share/pallas_call | solution.py:92
  413.2 13.6 %collective-permute-done.39.refs_4_ = bf16[768,768]{1,0:T(8,128)(2,1)S(1)} collective-permute-done((bf16[768,768]{1,0:T(8,128)(2,1)S(1)}, bf16[768,768]{1,0:T(8,128)(2,1)S(1)}, u32[]{:S(2)}, u32[]{:S(2)}) %collective-permute-start.39) | collective-permute-done | bytes 1179680 | tf_op jit(solution)/shard_map/ppermute | solution.py:1103
  431.2 8.2 %collective-permute-done.41.refs_3_.refs_4_ = bf16[192,1024]{1,0:T(8,128)(2,1)S(1)} collective-permute-done((bf16[192,1024]{1,0:T(8,128)(2,1)S(1)}, bf16[192,1024]{1,0:T(8,128)(2,1)S(1)}, u32[]{:S(2)}, u32[]{:S(2)}) %collective-permute-start.41) | collective-permute-done | bytes 393248 | tf_op jit(solution)/shard_map/ppermute | solution.py:1135
  443.4 5.2 %finish.4 = (f32[192,2240]{1,0:T(8,128)}, f32[8,128]{1,0:T(8,128)S(1)}) custom-call(bf16[384,1280]{1,0:T(8,128)(2,1)S(1)} %copy-done.56, bf16[384,1280]{1,0:T(8,128)(2,1)S(1)} %copy-done.58, bf16[192,1280]{1,0:T(8,128)(2,1)} %collective-permute-done.27.refs_8_.refs_2_, bf16[192,1024]{1,0:T(8,128)(2,1)S(1)} %get-tuple-element.258.refs_7_.refs_3_, ...), custom_call_target="tpu_custom_call" | custom-call | bytes 6021 | tf_op jit(solution)/shard_map/finish/pallas_call | solution.py:92
  448.6 6.7 %collective-permute-done.44.refs_1_.refs_4_ = bf16[384,768]{1,0:T(8,128)(2,1)S(1)} collective-permute-done((bf16[384,768]{1,0:T(8,128)(2,1)S(1)}, bf16[384,768]{1,0:T(8,128)(2,1)S(1)}, u32[]{:S(2)}, u32[]{:S(2)}) %collective-permute-start.44) | collective-permute-done | bytes 589856 | tf_op jit(solution)/shard_map/ppermute | solution.py:1108
  459.9 3.7 finish.5
  463.6 3.5 finish.6
  469.6 4.1 finish.7
  477.6 4.8 collective-permute-done.50
  (404 shorter events, 155.5 us)
Async XLA Ops:
  7.2 292.6 %reduce-scatter.3.cloned.1.call-start = ((), (), s32[]{:S(2)}) async-start(), calls=%async_computation.2 | async-start | bytes 3932160 | tf_op jit(solution)/shard_map/reduce_scatter | solution.py:1128
  23.4 11.1 %collective-permute-start.1 = (bf16[2,512,128]{2,1,0:T(8,128)(2,1)S(1)}, bf16[2,512,128]{2,1,0:T(8,128)(2,1)}, u32[]{:S(2)}, u32[]{:S(2)}) collective-permute-start(bf16[2,512,128]{2,1,0:T(8,128)(2,1)S(1)} %bitcast.75), channel_id=1, source_target_pairs={{0,4},{4,8},{8,12},{1,5},{5,9},{9,13},{2,6},{6,10},{10,14},{3,7},{... | collective-permute-start | bytes 786440 | tf_op jit(solution)/shard_map/ppermute | solution.py:66
  29.1 9.8 %collective-permute-start = (bf16[2,512,128]{2,1,0:T(8,128)(2,1)S(1)}, bf16[2,512,128]{2,1,0:T(8,128)(2,1)}, u32[]{:S(2)}, u32[]{:S(2)}) collective-permute-start(bf16[2,512,128]{2,1,0:T(8,128)(2,1)S(1)} %bitcast.76), channel_id=1, source_target_pairs={{0,8},{4,12},{1,9},{5,13},{2,10},{6,14},{3,11},{7,15},{16,24},{20,... | collective-permute-start | bytes 786440 | tf_op jit(solution)/shard_map/ppermute | solution.py:66
  34.0 5.0 %collective-permute-start.4 = (bf16[2,512,128]{2,1,0:T(8,128)(2,1)S(1)}, bf16[2,512,128]{2,1,0:T(8,128)(2,1)}, u32[]{:S(2)}, u32[]{:S(2)}) collective-permute-start(bf16[2,512,128]{2,1,0:T(8,128)(2,1)S(1)} %bitcast.77), channel_id=1, source_target_pairs={{0,1},{1,0},{2,3},{3,2},{4,5},{5,4},{6,7},{7,6},{8,9},{9,8},{10,11... | collective-permute-start | bytes 786440 | tf_op jit(solution)/shard_map/ppermute | solution.py:48
  34.5 4.5 collective-permute-start.3
  50.3 3.3 collective-permute-start.6
  57.1 37.5 %collective-permute-start.7 = (bf16[256,1536]{1,0:T(8,128)(2,1)}, bf16[256,1536]{1,0:T(8,128)(2,1)}, u32[]{:S(2)}, u32[]{:S(2)}) collective-permute-start(bf16[256,1536]{1,0:T(8,128)(2,1)} %get-tuple-element.142.refs_3_), channel_id=1, source_target_pairs={{0,2},{1,3},{2,0},{3,1},{4,6},{5,7},{6,4},{7,5},{8,10},{9,11},{10,... | collective-permute-start | bytes 2359304 | tf_op jit(solution)/shard_map/ppermute | solution.py:52
  58.6 36.0 %collective-permute-start.8 = (bf16[256,1536]{1,0:T(8,128)(2,1)}, bf16[256,1536]{1,0:T(8,128)(2,1)}, u32[]{:S(2)}, u32[]{:S(2)}) collective-permute-start(bf16[256,1536]{1,0:T(8,128)(2,1)} %get-tuple-element.143.refs_4_), channel_id=1, source_target_pairs={{0,2},{1,3},{2,0},{3,1},{4,6},{5,7},{6,4},{7,5},{8,10},{9,11},{10,... | collective-permute-start | bytes 2359304 | tf_op jit(solution)/shard_map/ppermute | solution.py:52
  98.4 3.4 collective-permute-start.10
  135.2 323.5 %reduce-scatter.5.cloned.1.call-start = ((), (), s32[]{:S(2)}) async-start(), calls=%async_computation.3 | async-start | bytes 4423680 | tf_op jit(solution)/shard_map/reduce_scatter | solution.py:1148
  143.9 55.0 %collective-permute-start.15 = (bf16[768,1280]{1,0:T(8,128)(2,1)}, bf16[768,1280]{1,0:T(8,128)(2,1)}, u32[]{:S(2)}, u32[]{:S(2)}) collective-permute-start(bf16[768,1280]{1,0:T(8,128)(2,1)} %get-tuple-element.167), channel_id=1, source_target_pairs={{0,16},{16,0},{1,17},{17,1},{2,18},{18,2},{3,19},{19,3},{4,20},{20... | collective-permute-start | bytes 5898248 | tf_op jit(solution)/shard_map/ppermute | solution.py:1103
  161.2 3.4 collective-permute-start.12
  178.8 30.4 %collective-permute-start.13 = (bf16[256,1536]{1,0:T(8,128)(2,1)}, bf16[256,1536]{1,0:T(8,128)(2,1)S(1)}, u32[]{:S(2)}, u32[]{:S(2)}) collective-permute-start(bf16[256,1536]{1,0:T(8,128)(2,1)} %get-tuple-element.165.refs_4_), channel_id=1, source_target_pairs={{0,2},{1,3},{2,0},{3,1},{4,6},{5,7},{6,4},{7,5},{8,10},{9,11},{10,... | collective-permute-start | bytes 2359304 | tf_op jit(solution)/shard_map/ppermute | solution.py:52
  180.2 35.4 %collective-permute-start.14 = (bf16[256,1536]{1,0:T(8,128)(2,1)}, bf16[256,1536]{1,0:T(8,128)(2,1)}, u32[]{:S(2)}, u32[]{:S(2)}) collective-permute-start(bf16[256,1536]{1,0:T(8,128)(2,1)} %get-tuple-element.166.refs_5_), channel_id=1, source_target_pairs={{0,2},{1,3},{2,0},{3,1},{4,6},{5,7},{6,4},{7,5},{8,10},{9,11},{10,... | collective-permute-start | bytes 2359304 | tf_op jit(solution)/shard_map/ppermute | solution.py:52
  198.4 104.9 %collective-permute-start.22 = (bf16[768,2304]{1,0:T(8,128)(2,1)}, bf16[768,2304]{1,0:T(8,128)(2,1)}, u32[]{:S(2)}, u32[]{:S(2)}) collective-permute-start(bf16[768,2304]{1,0:T(8,128)(2,1)} %get-tuple-element.189), channel_id=1, source_target_pairs={{0,16},{16,0},{1,17},{17,1},{2,18},{18,2},{3,19},{19,3},{4,20},{20... | collective-permute-start | bytes 10616840 | tf_op jit(solution)/shard_map/ppermute | solution.py:1103
  219.7 10.6 %collective-permute-start.16 = (bf16[256,1536]{1,0:T(8,128)(2,1)S(1)}, bf16[256,1536]{1,0:T(8,128)(2,1)S(1)}, u32[]{:S(2)}, u32[]{:S(2)}) collective-permute-start(bf16[256,1536]{1,0:T(8,128)(2,1)S(1)} %get-tuple-element.173.refs_1_.refs_0_), channel_id=1, source_target_pairs={{0,1},{1,0},{2,3},{3,2},{4,5},{5,4},{6,7},{7,6},{8,9},{9,8},{10,11... | collective-permute-start | bytes 2359304 | tf_op jit(solution)/shard_map/ppermute | solution.py:48
  219.7 10.5 %collective-permute-start.17 = (bf16[256,1536]{1,0:T(8,128)(2,1)S(1)}, bf16[256,1536]{1,0:T(8,128)(2,1)S(1)}, u32[]{:S(2)}, u32[]{:S(2)}) collective-permute-start(bf16[256,1536]{1,0:T(8,128)(2,1)S(1)} %get-tuple-element.174.refs_2_.refs_1_), channel_id=1, source_target_pairs={{0,1},{1,0},{2,3},{3,2},{4,5},{5,4},{6,7},{7,6},{8,9},{9,8},{10,11... | collective-permute-start | bytes 2359304 | tf_op jit(solution)/shard_map/ppermute | solution.py:48
  220.2 32.0 %collective-permute-start.19 = (bf16[384,1280]{1,0:T(8,128)(2,1)S(1)}, bf16[384,1280]{1,0:T(8,128)(2,1)S(1)}, u32[]{:S(2)}, u32[]{:S(2)}) collective-permute-start(bf16[384,1280]{1,0:T(8,128)(2,1)S(1)} %get-tuple-element.182), channel_id=1, source_target_pairs={{0,4},{4,0},{8,12},{12,8},{1,5},{5,1},{9,13},{13,9},{2,6},{6,2},{1... | collective-permute-start | bytes 2949128 | tf_op jit(solution)/shard_map/ppermute | solution.py:1108
  241.0 12.3 %collective-permute-start.18 = (bf16[2,1536,128]{2,1,0:T(8,128)(2,1)S(1)}, bf16[2,1536,128]{2,1,0:T(8,128)(2,1)S(1)}, u32[]{:S(2)}, u32[]{:S(2)}) collective-permute-start(bf16[2,1536,128]{2,1,0:T(8,128)(2,1)S(1)} %get-tuple-element.180), channel_id=1, source_target_pairs={{0,1},{1,0},{2,3},{3,2},{4,5},{5,4},{6,7},{7,6},{8,9},{9,8},{10,11... | collective-permute-start | bytes 2359304 | tf_op jit(solution)/shard_map/ppermute | solution.py:48
  253.5 9.8 %collective-permute-start.23 = (bf16[2,512,128]{2,1,0:T(8,128)(2,1)S(1)}, bf16[2,512,128]{2,1,0:T(8,128)(2,1)S(1)}, u32[]{:S(2)}, u32[]{:S(2)}) collective-permute-start(bf16[2,512,128]{2,1,0:T(8,128)(2,1)S(1)} %get-tuple-element.193), channel_id=1, source_target_pairs={{4,0},{8,4},{12,8},{5,1},{9,5},{13,9},{6,2},{10,6},{14,10},{7,3},{... | collective-permute-start | bytes 786440 | tf_op jit(solution)/shard_map/ppermute | solution.py:66
  263.4 10.3 %collective-permute-start.24 = (bf16[2,512,128]{2,1,0:T(8,128)(2,1)S(1)}, bf16[2,512,128]{2,1,0:T(8,128)(2,1)S(1)}, u32[]{:S(2)}, u32[]{:S(2)}) collective-permute-start(bf16[2,512,128]{2,1,0:T(8,128)(2,1)S(1)} %get-tuple-element.195), channel_id=1, source_target_pairs={{4,0},{8,4},{12,8},{5,1},{9,5},{13,9},{6,2},{10,6},{14,10},{7,3},{... | collective-permute-start | bytes 786440 | tf_op jit(solution)/shard_map/ppermute | solution.py:66
  277.8 12.0 %collective-permute-start.25 = (bf16[256,1536]{1,0:T(8,128)(2,1)}, bf16[256,1536]{1,0:T(8,128)(2,1)S(1)}, u32[]{:S(2)}, u32[]{:S(2)}) collective-permute-start(bf16[256,1536]{1,0:T(8,128)(2,1)} %get-tuple-element.199), channel_id=1, source_target_pairs={{0,1},{1,0},{2,3},{3,2},{4,5},{5,4},{6,7},{7,6},{8,9},{9,8},{10,11... | collective-permute-start | bytes 2359304 | tf_op jit(solution)/shard_map/ppermute | solution.py:48
  277.9 12.9 %collective-permute-start.26 = (bf16[256,1536]{1,0:T(8,128)(2,1)}, bf16[256,1536]{1,0:T(8,128)(2,1)S(1)}, u32[]{:S(2)}, u32[]{:S(2)}) collective-permute-start(bf16[256,1536]{1,0:T(8,128)(2,1)} %get-tuple-element.200), channel_id=1, source_target_pairs={{0,1},{1,0},{2,3},{3,2},{4,5},{5,4},{6,7},{7,6},{8,9},{9,8},{10,11... | collective-permute-start | bytes 2359304 | tf_op jit(solution)/shard_map/ppermute | solution.py:48
  278.4 25.0 %collective-permute-start.27 = (bf16[192,1280]{1,0:T(8,128)(2,1)}, bf16[192,1280]{1,0:T(8,128)(2,1)}, u32[]{:S(2)}, u32[]{:S(2)}) collective-permute-start(bf16[192,1280]{1,0:T(8,128)(2,1)} %get-tuple-element.207), channel_id=1, source_target_pairs={{0,8},{4,12},{8,0},{12,4},{1,9},{5,13},{9,1},{13,5},{2,10},{6,14},... | collective-permute-start | bytes 1474568 | tf_op jit(solution)/shard_map/ppermute | solution.py:1113
  316.5 4.1 collective-permute-start.20
  316.6 4.0 collective-permute-start.21
  317.1 20.6 %collective-permute-start.31 = (bf16[256,1536]{1,0:T(8,128)(2,1)}, bf16[256,1536]{1,0:T(8,128)(2,1)S(1)}, u32[]{:S(2)}, u32[]{:S(2)}) collective-permute-start(bf16[256,1536]{1,0:T(8,128)(2,1)} %copy-done.85), channel_id=1, source_target_pairs={{0,2},{1,3},{2,0},{3,1},{4,6},{5,7},{6,4},{7,5},{8,10},{9,11},{10,... | collective-permute-start | bytes 2359304 | tf_op jit(solution)/shard_map/ppermute | solution.py:52
  318.6 35.1 %collective-permute-start.32 = (bf16[256,1536]{1,0:T(8,128)(2,1)}, bf16[256,1536]{1,0:T(8,128)(2,1)S(1)}, u32[]{:S(2)}, u32[]{:S(2)}) collective-permute-start(bf16[256,1536]{1,0:T(8,128)(2,1)} %copy-done.87), channel_id=1, source_target_pairs={{0,2},{1,3},{2,0},{3,1},{4,6},{5,7},{6,4},{7,5},{8,10},{9,11},{10,... | collective-permute-start | bytes 2359304 | tf_op jit(solution)/shard_map/ppermute | solution.py:52
  319.1 54.4 %collective-permute-start.30 = (bf16[768,1536]{1,0:T(8,128)(2,1)}, bf16[768,1536]{1,0:T(8,128)(2,1)S(1)}, u32[]{:S(2)}, u32[]{:S(2)}) collective-permute-start(bf16[768,1536]{1,0:T(8,128)(2,1)} %copy-done.97), channel_id=1, source_target_pairs={{0,16},{16,0},{1,17},{17,1},{2,18},{18,2},{3,19},{19,3},{4,20},{20... | collective-permute-start | bytes 7077896 | tf_op jit(solution)/shard_map/ppermute | solution.py:1103
  355.8 3.5 collective-permute-start.33
  355.9 5.6 %collective-permute-start.34 = (f32[256,1536]{1,0:T(8,128)S(1)}, f32[256,1536]{1,0:T(8,128)S(1)}, u32[]{:S(2)}, u32[]{:S(2)}) collective-permute-start(f32[256,1536]{1,0:T(8,128)S(1)} %get-tuple-element.217.refs_2_), channel_id=1, source_target_pairs={{0,1},{1,0},{2,3},{3,2},{4,5},{5,4},{6,7},{7,6},{8,9},{9,8},{10,11... | collective-permute-start | bytes 4718600 | tf_op jit(solution)/shard_map/ppermute | solution.py:48
  356.4 24.1 %collective-permute-start.28 = (bf16[256,1536]{1,0:T(8,128)(2,1)S(1)}, bf16[256,1536]{1,0:T(8,128)(2,1)S(1)}, u32[]{:S(2)}, u32[]{:S(2)}) collective-permute-start(bf16[256,1536]{1,0:T(8,128)(2,1)S(1)} %get-tuple-element.209.refs_1_), channel_id=1, source_target_pairs={{0,2},{1,3},{2,0},{3,1},{4,6},{5,7},{6,4},{7,5},{8,10},{9,11},{10,... | collective-permute-start | bytes 2359304 | tf_op jit(solution)/shard_map/ppermute | solution.py:52
  357.9 34.9 %collective-permute-start.29 = (bf16[256,1536]{1,0:T(8,128)(2,1)S(1)}, bf16[256,1536]{1,0:T(8,128)(2,1)S(1)}, u32[]{:S(2)}, u32[]{:S(2)}) collective-permute-start(bf16[256,1536]{1,0:T(8,128)(2,1)S(1)} %get-tuple-element.210.refs_2_), channel_id=1, source_target_pairs={{0,2},{1,3},{2,0},{3,1},{4,6},{5,7},{6,4},{7,5},{8,10},{9,11},{10,... | collective-permute-start | bytes 2359304 | tf_op jit(solution)/shard_map/ppermute | solution.py:52
  359.3 43.7 %collective-permute-start.37 = (bf16[768,896]{1,0:T(8,128)(2,1)}, bf16[768,896]{1,0:T(8,128)(2,1)S(1)}, u32[]{:S(2)}, u32[]{:S(2)}) collective-permute-start(bf16[768,896]{1,0:T(8,128)(2,1)} %get-tuple-element.223), channel_id=1, source_target_pairs={{0,16},{16,0},{1,17},{17,1},{2,18},{18,2},{3,19},{19,3},{4,20},{20... | collective-permute-start | bytes 4128776 | tf_op jit(solution)/shard_map/ppermute | solution.py:1103
  379.0 32.2 %collective-permute-start.40 = (bf16[384,1536]{1,0:T(8,128)(2,1)}, bf16[384,1536]{1,0:T(8,128)(2,1)S(1)}, u32[]{:S(2)}, u32[]{:S(2)}) collective-permute-start(bf16[384,1536]{1,0:T(8,128)(2,1)} %get-tuple-element.232), channel_id=1, source_target_pairs={{0,4},{4,0},{8,12},{12,8},{1,5},{5,1},{9,13},{13,9},{2,6},{6,2},{1... | collective-permute-start | bytes 3538952 | tf_op jit(solution)/shard_map/ppermute | solution.py:1108
  379.0 47.8 %collective-permute-start.39 = (bf16[768,768]{1,0:T(8,128)(2,1)S(1)}, bf16[768,768]{1,0:T(8,128)(2,1)S(1)}, u32[]{:S(2)}, u32[]{:S(2)}) collective-permute-start(bf16[768,768]{1,0:T(8,128)(2,1)S(1)} %copy-done.99), channel_id=1, source_target_pairs={{0,16},{16,0},{1,17},{17,1},{2,18},{18,2},{3,19},{19,3},{4,20},{20... | collective-permute-start | bytes 3538952 | tf_op jit(solution)/shard_map/ppermute | solution.py:1103
  394.0 14.9 %collective-permute-start.35 = (bf16[256,1536]{1,0:T(8,128)(2,1)S(1)}, bf16[256,1536]{1,0:T(8,128)(2,1)S(1)}, u32[]{:S(2)}, u32[]{:S(2)}) collective-permute-start(bf16[256,1536]{1,0:T(8,128)(2,1)S(1)} %get-tuple-element.221.refs_1_), channel_id=1, source_target_pairs={{0,1},{1,0},{2,3},{3,2},{4,5},{5,4},{6,7},{7,6},{8,9},{9,8},{10,11... | collective-permute-start | bytes 2359304 | tf_op jit(solution)/shard_map/ppermute | solution.py:48
  394.1 14.9 %collective-permute-start.36 = (bf16[256,1536]{1,0:T(8,128)(2,1)S(1)}, bf16[256,1536]{1,0:T(8,128)(2,1)S(1)}, u32[]{:S(2)}, u32[]{:S(2)}) collective-permute-start(bf16[256,1536]{1,0:T(8,128)(2,1)S(1)} %get-tuple-element.222.refs_2_), channel_id=1, source_target_pairs={{0,1},{1,0},{2,3},{3,2},{4,5},{5,4},{6,7},{7,6},{8,9},{9,8},{10,11... | collective-permute-start | bytes 2359304 | tf_op jit(solution)/shard_map/ppermute | solution.py:48
  408.9 30.7 %collective-permute-start.38 = (bf16[384,896]{1,0:T(8,128)(2,1)S(1)}, bf16[384,896]{1,0:T(8,128)(2,1)S(1)}, u32[]{:S(2)}, u32[]{:S(2)}) collective-permute-start(bf16[384,896]{1,0:T(8,128)(2,1)S(1)} %get-tuple-element.229), channel_id=1, source_target_pairs={{0,4},{4,0},{8,12},{12,8},{1,5},{5,1},{9,13},{13,9},{2,6},{6,2},{1... | collective-permute-start | bytes 2064392 | tf_op jit(solution)/shard_map/ppermute | solution.py:1108
  411.3 28.2 %collective-permute-start.42 = (bf16[192,1536]{1,0:T(8,128)(2,1)S(1)}, bf16[192,1536]{1,0:T(8,128)(2,1)S(1)}, u32[]{:S(2)}, u32[]{:S(2)}) collective-permute-start(bf16[192,1536]{1,0:T(8,128)(2,1)S(1)} %get-tuple-element.236), channel_id=1, source_target_pairs={{0,8},{4,12},{8,0},{12,4},{1,9},{5,13},{9,1},{13,5},{2,10},{6,14},... | collective-permute-start | bytes 1769480 | tf_op jit(solution)/shard_map/ppermute | solution.py:1113
  429.6 25.7 %collective-permute-start.44 = (bf16[384,768]{1,0:T(8,128)(2,1)S(1)}, bf16[384,768]{1,0:T(8,128)(2,1)S(1)}, u32[]{:S(2)}, u32[]{:S(2)}) collective-permute-start(bf16[384,768]{1,0:T(8,128)(2,1)S(1)} %get-tuple-element.240), channel_id=1, source_target_pairs={{0,4},{4,0},{8,12},{12,8},{1,5},{5,1},{9,13},{13,9},{2,6},{6,2},{1... | collective-permute-start | bytes 1769480 | tf_op jit(solution)/shard_map/ppermute | solution.py:1108
  429.7 9.7 %collective-permute-start.41 = (bf16[192,1024]{1,0:T(8,128)(2,1)S(1)}, bf16[192,1024]{1,0:T(8,128)(2,1)S(1)}, u32[]{:S(2)}, u32[]{:S(2)}) collective-permute-start(bf16[192,1024]{1,0:T(8,128)(2,1)S(1)} %copy-done.83), channel_id=1, source_target_pairs={{0,16},{16,0},{1,17},{17,1},{2,18},{18,2},{3,19},{19,3},{4,20},{20... | collective-permute-start | bytes 1179656 | tf_op jit(solution)/shard_map/ppermute | solution.py:1135
  440.5 23.1 %collective-permute-start.43 = (bf16[192,896]{1,0:T(8,128)(2,1)}, bf16[192,896]{1,0:T(8,128)(2,1)}, u32[]{:S(2)}, u32[]{:S(2)}) collective-permute-start(bf16[192,896]{1,0:T(8,128)(2,1)} %get-tuple-element.237), channel_id=1, source_target_pairs={{0,8},{4,12},{8,0},{12,4},{1,9},{5,13},{9,1},{13,5},{2,10},{6,14},... | collective-permute-start | bytes 1032200 | tf_op jit(solution)/shard_map/ppermute | solution.py:1113
  441.9 6.7 %collective-permute-start.45 = (f32[8,512]{1,0:T(8,128)S(1)}, f32[8,512]{1,0:T(8,128)S(1)}, u32[]{:S(2)}, u32[]{:S(2)}) collective-permute-start(f32[8,512]{1,0:T(8,128)S(1)} %copy-done.94), channel_id=1, source_target_pairs={{0,16},{16,0},{1,17},{17,1},{2,18},{18,2},{3,19},{19,3},{4,20},{20... | collective-permute-start | bytes 49160 | tf_op jit(solution)/shard_map/ppermute | solution.py:1239
  456.0 13.5 %collective-permute-start.48 = (bf16[192,768]{1,0:T(8,128)(2,1)}, bf16[192,768]{1,0:T(8,128)(2,1)S(1)}, u32[]{:S(2)}, u32[]{:S(2)}) collective-permute-start(bf16[192,768]{1,0:T(8,128)(2,1)} %get-tuple-element.252), channel_id=1, source_target_pairs={{0,8},{4,12},{8,0},{12,4},{1,9},{5,13},{9,1},{13,5},{2,10},{6,14},... | collective-permute-start | bytes 884744 | tf_op jit(solution)/shard_map/ppermute | solution.py:1113
  456.2 10.9 %collective-permute-start.46 = (f32[8,512]{1,0:T(8,128)S(1)}, f32[8,512]{1,0:T(8,128)}, u32[]{:S(2)}, u32[]{:S(2)}) collective-permute-start(f32[8,512]{1,0:T(8,128)S(1)} %get-tuple-element.248.refs_0_), channel_id=1, source_target_pairs={{0,4},{4,0},{8,12},{12,8},{1,5},{5,1},{9,13},{13,9},{2,6},{6,2},{1... | collective-permute-start | bytes 49160 | tf_op jit(solution)/shard_map/ppermute | solution.py:1241
  467.9 5.9 %collective-permute-start.47 = (f32[8,512]{1,0:T(8,128)S(1)}, f32[8,512]{1,0:T(8,128)S(1)}, u32[]{:S(2)}, u32[]{:S(2)}) collective-permute-start(f32[8,512]{1,0:T(8,128)S(1)} %get-tuple-element.250), channel_id=1, source_target_pairs={{0,8},{4,12},{8,0},{12,4},{1,9},{5,13},{9,1},{13,5},{2,10},{6,14},... | collective-permute-start | bytes 49160 | tf_op jit(solution)/shard_map/ppermute | solution.py:1248
  475.2 7.2 %collective-permute-start.50 = (f32[2,200,128]{2,1,0:T(8,128)S(1)}, f32[2,200,128]{2,1,0:T(8,128)S(1)}, u32[]{:S(2)}, u32[]{:S(2)}) collective-permute-start(f32[2,200,128]{2,1,0:T(8,128)S(1)} %maximum_select_fusion.1), channel_id=1, source_target_pairs={{0,2},{1,3},{2,0},{3,1},{4,6},{5,7},{6,4},{7,5},{8,10},{9,11},{10,... | collective-permute-start | bytes 614408 | tf_op jit(solution)/shard_map/ppermute | solution.py:52
  (124 other events, 1326.8 us)
Sparse Core Ops, SparseCore 0:
  135.4 71.0 reduce-scatter.2
  316.7 66.1 reduce-scatter.4

commit v10 on v9

--- a/solution.py
+++ b/solution.py
@@ -1212,24 +1212,24 @@
         order, core_one, grad_q_rows, own_kv, [] if moving is None else [moving], cosine, sine
     )
     sent = core_swaps(narrow(order, [(grad_qkv, weight)], 1, (), 1))
+    down_b.across()
+    gate.own()
+    mine = narrow(order, [(grad_qkv, weight)], 0, sent, 1)
+    come = chip_swaps(mine)
     last_parts = [(0, 0, 0, grad_qkv.shape[1] // HD, 0), (1, 1, 0, heads, 0)]
     last = Rows([h_one_t, branch_t], [grad_qkv, mixed], last_parts, HD)
-    mine = narrow(order, [(grad_qkv, weight)], 0, sent, 1)
-    come = chip_swaps(mine)
-    down_b.across()
-    down_a.settled()
-    gate.own()
     ffn_mine = narrow(order, [(hidden, down_t)], 0, ffn_sent)
     token = norm_back(order, core_one, mine, come, flat_tokens, gain_one, grad_middle, True)
     token += core_swaps(token)
     ffn_come = chip_swaps(ffn_mine)
+    up_a.own()
     token_grad = place(order, core_one, token).reshape(rows, local, width)
-    up_a.own()
     layer = layer_of(order, middle, ffn_mine, ffn_come)
     layer += core_swaps(layer)
     last.own()
     layer_out = place(order, core_one, layer).reshape(rows, local, width)
     up_a.relay()
+    down_a.settled()
     up_b.own()
     down_b.settled()
     up_a.settled()

time: 499 us -> 512 us (1.026)
  waiting for transfers between devices: 132 us -> 148 us
    ppermute x4, waiting for transfers between devices: 2.66 us -> 19.2 us  [relay(): self.last = lax.ppermute(sent, 'seq', flipped('seq', 1))]
    ppermute x5, waiting for transfers between devices: 30.9 us -> 23.6 us  [__init__(): self.come = lax.ppermute(sent, 'dp', flipped('dp', 0))]
    ppermute x9, waiting for transfers between devices: 45.1 us -> 52.2 us  [chip_swap(): return lax.ppermute(value, 'tensor', flipped('tensor', 1))]
    unnamed x243 -> x241, local copies, waits for them, and re-layouts: 77 us -> 80.1 us
  transfers between devices with their start and end apart: 53 -> 53, of which waited for: 28 -> 29; matrix products, arithmetic and copies ran while one was open for 3% -> 3% of each run, Pallas kernels for 29% -> 27%
where the time goes in v10:
time: 512 us; the launch traced here: 507 us
  Pallas kernels  189 us (37%)
  waiting for transfers between devices  148 us (29%)
  local copies, waits for them, and re-layouts  90.3 us (18%)
  starting transfers between devices  54.3 us (11%)
  between operations  15.5 us (3%)
  other arithmetic  9.37 us (2%)
    pallas_call x44, Pallas kernels, __call__(): pl.pallas_call(run, grid_spec=pltpu.PrefetchScalarGridSpec(num_scalar_pre...  180 us
    unnamed x241, local copies, waits for them, and re-layouts  80.1 us
    ppermute x9, waiting for transfers between devices, chip_swap(): return lax.ppermute(value, 'tensor', flipped('tensor', 1))  52.2 us
    ppermute x5, waiting for transfers between devices, __init__(): self.come = lax.ppermute(sent, 'dp', flipped('dp', 0))  23.6 us
    ppermute x4, waiting for transfers between devices, relay(): self.last = lax.ppermute(sent, 'seq', flipped('seq', 1))  19.2 us
    ppermute x4, waiting for transfers between devices, own(): self.come = lax.ppermute(send, 'seq', flipped('seq', 0))  16.9 us
    ppermute x4, waiting for transfers between devices, shifted(): return lax.ppermute(value, 'seq', route)  16.1 us
    ppermute x4, starting transfers between devices, shifted(): return lax.ppermute(value, 'seq', route)  13 us
  transfers between devices with their start and end apart: 53, of which 29 were waited for; matrix products, arithmetic and copies ran while one was open for 3% of the time, Pallas kernels for 27%

profile of v10, /device:TPU:0, one launch (start us, length us, event | category | flops | bytes accessed | tf_op | source)
XLA Modules:
  0.0 507.0 jit_solution(5852747400335136741)
XLA Ops:
  17.2 3.6 first.1
  23.4 5.6 %collective-permute-start.1 = (bf16[2,512,128]{2,1,0:T(8,128)(2,1)S(1)}, bf16[2,512,128]{2,1,0:T(8,128)(2,1)}, u32[]{:S(2)}, u32[]{:S(2)}) collective-permute-start(bf16[2,512,128]{2,1,0:T(8,128)(2,1)S(1)} %bitcast.77), channel_id=1, source_target_pairs={{0,4},{4,8},{8,12},{1,5},{5,9},{9,13},{2,6},{6,10},{10,14},{3,7},{... | collective-permute-start | bytes 786440 | tf_op jit(solution)/shard_map/ppermute | solution.py:66
  29.1 4.5 collective-permute-start
  34.5 4.3 collective-permute-done.refs_0_.refs_9_
  41.9 6.1 %attend.1 = (bf16[2,512,384]{2,1,0:T(8,128)(2,1)S(1)}, f32[2,2,768]{2,1,0:T(2,128)S(1)}) custom-call(s32[2,2]{1,0:T(2,128)S(1)} %shift-right-logical_maximum_fusion.low_ref.refs_0_, s32[1]{0:T(128)} %bitcast.core_ref.refs_0_.refs_1_, bf16[2,512,384]{2,1,0:T(8,128)(2,1)S(1)} %bitcast.74, s32[2,1,512]{2,1,0:T(1,128)S(1)} %sub.44.start_ref.refs_3_, ...), custom_call_target="tpu_custom_call" | custom-call | flops 8000000 | bytes 4194 | tf_op jit(solution)/shard_map/attend/pallas_call | solution.py:253
  53.6 3.5 narrow.9
  60.4 4.5 constant_dynamic-slice_fusion.2
  74.6 5.2 %copy-done.9 = bf16[1536,2240]{0,1:T(8,128)(2,1)S(1)} copy-done((bf16[1536,2240]{0,1:T(8,128)(2,1)S(1)}, bf16[1536,2240]{0,1:T(8,128)(2,1)}, u32[]{:S(2)}) %copy-start.9) | copy-done | bytes 6881304
  79.8 9.3 %grad_hidden.1 = (bf16[1024,2240]{1,0:T(8,128)(2,1)S(1)}, f32[8,128]{1,0:T(8,128)S(1)}) custom-call(bf16[1024,1536]{1,0:T(8,128)(2,1)S(1)} %get-tuple-element.146.refs_0_.refs_3_, bf16[2240,1536]{1,0:T(8,128)(2,1)S(1)} %bitcast.61, f32[8,128]{1,0:T(8,128)S(1)} %get-tuple-element.147.refs_2_, bf16[192,2240]{1,0:T(8,128)(2,1)S(1)} %copy-done.46, ...), custom_call_target="tpu_custom_call" | custom-call | flops 7046430 | bytes 15728 | tf_op jit(solution)/shard_map/grad_hidden/pallas_call | solution.py:92
  94.5 3.8 middle.1
  104.1 20.3 %gated.1 = (bf16[1024,2240]{1,0:T(8,128)(2,1)S(1)}, bf16[1024,2240]{1,0:T(8,128)(2,1)S(1)}, bf16[1024,2240]{1,0:T(8,128)(2,1)S(1)}, f32[8,128]{1,0:T(8,128)S(1)}) custom-call(bf16[1024,2240]{1,0:T(8,128)(2,1)S(1)} %copy-done.55, bf16[2240,1536]{1,0:T(8,128)(2,1)} %bitcast.58, bf16[2240,1536]{1,0:T(8,128)(2,1)} %bitcast.83, ...), custom_call_target="tpu_custom_call" | custom-call | flops 14092861 | bytes 31457 | tf_op jit(solution)/shard_map/gated/pallas_call | solution.py:92
  126.7 4.6 share.9
  139.7 4.2 share.10
  149.2 10.3 %narrow.10 = (bf16[256,1536]{1,0:T(8,128)(2,1)S(1)}, bf16[256,1536]{1,0:T(8,128)(2,1)S(1)}, f32[8,128]{1,0:T(8,128)S(1)}) custom-call(bf16[1024,2240]{1,0:T(8,128)(2,1)S(1)} %copy-done.5, bf16[2240,1536]{1,0:T(8,128)(2,1)S(1)} %bitcast.59, bf16[1024,2240]{1,0:T(8,128)(2,1)S(1)} %bitcast.47, bf16[2240,1536]{1,0:T(8,128)(2,1)} %bitcast.84, ...), custom_call_target="tpu_custom_call" | custom-call | flops 7046430 | bytes 19922 | tf_op jit(solution)/shard_map/narrow/pallas_call | solution.py:92
  162.9 3.2 copy-done.8
  166.1 11.1 %narrow.11 = (bf16[256,1536]{1,0:T(8,128)(2,1)}, bf16[256,1536]{1,0:T(8,128)(2,1)}, f32[8,128]{1,0:T(8,128)S(1)}) custom-call(bf16[1024,2240]{1,0:T(8,128)(2,1)S(1)} %bitcast.55, bf16[2240,1536]{1,0:T(8,128)(2,1)S(1)} %bitcast.60, bf16[1024,2240]{1,0:T(8,128)(2,1)S(1)} %bitcast.47, bf16[2240,1536]{1,0:T(8,128)(2,1)} %bitcast.85, ...), custom_call_target="tpu_custom_call" | custom-call | flops 7046430 | bytes 19922 | tf_op jit(solution)/shard_map/narrow/pallas_call | solution.py:92
  178.7 13.6 %share.11 = (bf16[768,2304]{1,0:T(8,128)(2,1)}, bf16[768,1536]{1,0:T(8,128)(2,1)S(1)}, bf16[768,768]{1,0:T(8,128)(2,1)S(1)}, f32[8,128]{1,0:T(8,128)S(1)}) custom-call(s32[1]{0:T(128)} %bitcast.10.refs_0_, s32[1]{0:T(128)} %constant.59.clone.1.refs_0_.refs_1_, bf16[1536,1024]{1,0:T(8,128)(2,1)S(1)} %get-tuple-element.169.refs_2_, ...), custom_call_target="tpu_custom_call" | custom-call | flops 7247757 | bytes 18087 | tf_op jit(solution)/shard_map/share/pallas_call | solution.py:92
  197.0 9.0 %collective-permute-done.15.refs_4_ = bf16[768,1280]{1,0:T(8,128)(2,1)} collective-permute-done((bf16[768,1280]{1,0:T(8,128)(2,1)}, bf16[768,1280]{1,0:T(8,128)(2,1)}, u32[]{:S(2)}, u32[]{:S(2)}) %collective-permute-start.15) | collective-permute-done | bytes 1966112 | tf_op jit(solution)/shard_map/ppermute | solution.py:1103
  210.3 5.9 %share.12 = (bf16[384,1280]{1,0:T(8,128)(2,1)S(1)}, bf16[384,1280]{1,0:T(8,128)(2,1)S(1)}, f32[8,128]{1,0:T(8,128)S(1)}) custom-call(s32[1]{0:T(128)} %bitcast.11.refs_0_, s32[4]{0:T(128)S(1)} %pad_add_fusion.refs_1_, bf16[1536,1024]{1,0:T(8,128)(2,1)S(1)} %copy-done.17, bf16[1024,2240]{1,0:T(8,128)(2,1)S(1)} %copy-done.3, ...), custom_call_target="tpu_custom_call" | custom-call | flops 2013265 | bytes 6160 | tf_op jit(solution)/shard_map/share/pallas_call | solution.py:92
  216.2 15.2 %collective-permute-done.14.refs_7_ = bf16[256,1536]{1,0:T(8,128)(2,1)S(1)} collective-permute-done((bf16[256,1536]{1,0:T(8,128)(2,1)}, bf16[256,1536]{1,0:T(8,128)(2,1)S(1)}, u32[]{:S(2)}, u32[]{:S(2)}) %collective-permute-start.14) | collective-permute-done | bytes 786464 | tf_op jit(solution)/shard_map/ppermute | solution.py:52
  231.5 3.8 norm_back.2
  237.5 10.5 %collective-permute-start.19 = (bf16[384,1280]{1,0:T(8,128)(2,1)S(1)}, bf16[384,1280]{1,0:T(8,128)(2,1)S(1)}, u32[]{:S(2)}, u32[]{:S(2)}) collective-permute-start(bf16[384,1280]{1,0:T(8,128)(2,1)S(1)} %get-tuple-element.182), channel_id=1, source_target_pairs={{0,4},{4,0},{8,12},{12,8},{1,5},{5,1},{9,13},{13,9},{2,6},{6,2},{1... | collective-permute-start | bytes 2949128 | tf_op jit(solution)/shard_map/ppermute | solution.py:1108
  249.9 8.9 %attend_back.1 = (bf16[2,512,384]{2,1,0:T(8,128)(2,1)S(1)}, bf16[2,1536,128]{2,1,0:T(8,128)(2,1)S(1)}, bf16[2,1536,128]{2,1,0:T(8,128)(2,1)S(1)}, f32[8,128]{1,0:T(8,128)S(1)}) custom-call(s32[2,2]{1,0:T(2,128)S(1)} %shift-right-logical_maximum_fusion.low_ref.refs_0_, s32[1]{0:T(128)} %bitcast.core_ref.refs_0_.refs_1_, bf16[2,512,384]{2,1,0:T(8,128)(2,1)S(1)} %bitcast.75, ...), custom_call_target="tpu_custom_call" | custom-call | flops 20000000 | bytes 6291 | tf_op jit(solution)/shard_map/attend_back/pallas_call | solution.py:92
  262.0 8.0 %collective-permute-done.19.refs_1_ = bf16[384,1280]{1,0:T(8,128)(2,1)S(1)} collective-permute-done((bf16[384,1280]{1,0:T(8,128)(2,1)S(1)}, bf16[384,1280]{1,0:T(8,128)(2,1)S(1)}, u32[]{:S(2)}, u32[]{:S(2)}) %collective-permute-start.19) | collective-permute-done | bytes 983072 | tf_op jit(solution)/shard_map/ppermute | solution.py:1108
  272.6 5.3 %narrow.12 = (bf16[256,1536]{1,0:T(8,128)(2,1)S(1)}, bf16[256,1536]{1,0:T(8,128)(2,1)S(1)}, f32[8,128]{1,0:T(8,128)S(1)}) custom-call(bf16[1024,2240]{1,0:T(8,128)(2,1)S(1)} %bitcast.51, bf16[2240,1536]{1,0:T(8,128)(2,1)S(1)} %bitcast.64, f32[8,128]{1,0:T(8,128)S(1)} %get-tuple-element.186.refs_2_), custom_call_target="tpu_custom_call" | custom-call | flops 3523215 | bytes 10747 | tf_op jit(solution)/shard_map/narrow/pallas_call | solution.py:92
  282.6 9.4 %collective-permute-done.23.refs_5_ = bf16[2,512,128]{2,1,0:T(8,128)(2,1)S(1)} collective-permute-done((bf16[2,512,128]{2,1,0:T(8,128)(2,1)S(1)}, bf16[2,512,128]{2,1,0:T(8,128)(2,1)S(1)}, u32[]{:S(2)}, u32[]{:S(2)}) %collective-permute-start.23) | collective-permute-done | bytes 262176 | tf_op jit(solution)/shard_map/ppermute | solution.py:66
  304.7 8.3 %share.13 = (bf16[768,2304]{1,0:T(8,128)(2,1)S(1)}, f32[8,128]{1,0:T(8,128)S(1)}) custom-call(s32[1]{0:T(128)} %bitcast.11.refs_0_, s32[1]{0:T(128)} %constant.59.clone.1.refs_0_.refs_1_, bf16[1536,1024]{1,0:T(8,128)(2,1)S(1)} %copy-done.12, bf16[1024,2240]{1,0:T(8,128)(2,1)S(1)} %copy-done.6, bf16[768,2304]{1,0:T(8,128)(2,1)} %collective-permute-done.26.refs_4_, ...), custom_call_target="tpu_custom_call" | custom-call | flops 3623878 | bytes 9830 | tf_op jit(solution)/shard_map/share/pallas_call | solution.py:92
  332.0 5.3 %share.14 = (bf16[768,896]{1,0:T(8,128)(2,1)}, f32[8,128]{1,0:T(8,128)S(1)}) custom-call(s32[1]{0:T(128)} %bitcast.10.refs_0_, s32[1]{0:T(128)} %constant.59.clone.1.refs_0_.refs_1_, bf16[1536,1024]{1,0:T(8,128)(2,1)S(1)} %copy-done.30, bf16[1536,1024]{1,0:T(8,128)(2,1)S(1)} %copy-done.36, bf16[1024,512]{1,0:T(8,128)(2,1)S(1)} %copy-done.27, ...), custom_call_target="tpu_custom_call" | custom-call | flops 1409286 | bytes 4784 | tf_op jit(solution)/shard_map/share/pallas_call | solution.py:92
  337.4 3.0 copy-done.10
  340.4 5.4 %narrow.15 = (bf16[256,1536]{1,0:T(8,128)(2,1)S(1)}, bf16[256,1536]{1,0:T(8,128)(2,1)S(1)}, f32[8,128]{1,0:T(8,128)S(1)}) custom-call(bf16[1024,2240]{1,0:T(8,128)(2,1)S(1)} %bitcast.53, bf16[2240,1536]{1,0:T(8,128)(2,1)S(1)} %bitcast.65, bf16[256,1536]{1,0:T(8,128)(2,1)S(1)} %collective-permute-done.20.refs_2_, ...), custom_call_target="tpu_custom_call" | custom-call | flops 3523215 | bytes 10747 | tf_op jit(solution)/shard_map/narrow/pallas_call | solution.py:92
  345.8 14.5 %collective-permute-done.30.refs_7_ = bf16[256,1536]{1,0:T(8,128)(2,1)S(1)} collective-permute-done((bf16[256,1536]{1,0:T(8,128)(2,1)S(1)}, bf16[256,1536]{1,0:T(8,128)(2,1)S(1)}, u32[]{:S(2)}, u32[]{:S(2)}) %collective-permute-start.30) | collective-permute-done | bytes 786464 | tf_op jit(solution)/shard_map/ppermute | solution.py:52
  364.6 5.2 %collective-permute-done.33.refs_4_ = bf16[768,1536]{1,0:T(8,128)(2,1)S(1)} collective-permute-done((bf16[768,1536]{1,0:T(8,128)(2,1)}, bf16[768,1536]{1,0:T(8,128)(2,1)S(1)}, u32[]{:S(2)}, u32[]{:S(2)}) %collective-permute-start.33) | collective-permute-done | bytes 2359328 | tf_op jit(solution)/shard_map/ppermute | solution.py:1103
  371.2 5.4 %share.15 = (bf16[384,1536]{1,0:T(8,128)(2,1)}, bf16[384,1536]{1,0:T(8,128)(2,1)S(1)}, f32[8,128]{1,0:T(8,128)S(1)}) custom-call(s32[1]{0:T(128)} %bitcast.11.refs_0_, s32[4]{0:T(128)S(1)} %pad_add_fusion.refs_1_, bf16[1536,1024]{1,0:T(8,128)(2,1)S(1)} %copy-done.12, bf16[1024,2240]{1,0:T(8,128)(2,1)S(1)} %bitcast.49, ...), custom_call_target="tpu_custom_call" | custom-call | flops 2415919 | bytes 7077 | tf_op jit(solution)/shard_map/share/pallas_call | solution.py:92
  378.5 3.3 place.2
  383.5 16.0 %collective-permute-done.28.refs_4_ = bf16[256,1536]{1,0:T(8,128)(2,1)S(1)} collective-permute-done((bf16[256,1536]{1,0:T(8,128)(2,1)S(1)}, bf16[256,1536]{1,0:T(8,128)(2,1)S(1)}, u32[]{:S(2)}, u32[]{:S(2)}) %collective-permute-start.28) | collective-permute-done | bytes 786464 | tf_op jit(solution)/shard_map/ppermute | solution.py:52
  404.0 5.8 %share.16 = (bf16[384,896]{1,0:T(8,128)(2,1)S(1)}, bf16[384,896]{1,0:T(8,128)(2,1)S(1)}, f32[8,128]{1,0:T(8,128)S(1)}) custom-call(s32[1]{0:T(128)} %bitcast.11.refs_0_, s32[4]{0:T(128)S(1)} %pad_add_fusion.refs_1_, bf16[1536,1024]{1,0:T(8,128)(2,1)S(1)} %copy-done.31, bf16[1536,1024]{1,0:T(8,128)(2,1)S(1)} %copy-done.37, bf16[1024,512]{1,0:T(8,128)(2,1)S(1)} %copy-done.28, ...), custom_call_target="tpu_custom_call" | custom-call | flops 1409286 | bytes 4784 | tf_op jit(solution)/shard_map/share/pallas_call | solution.py:92
  414.3 9.4 %collective-permute-done.38.refs_4_ = bf16[768,768]{1,0:T(8,128)(2,1)S(1)} collective-permute-done((bf16[768,768]{1,0:T(8,128)(2,1)S(1)}, bf16[768,768]{1,0:T(8,128)(2,1)S(1)}, u32[]{:S(2)}, u32[]{:S(2)}) %collective-permute-start.38) | collective-permute-done | bytes 1179680 | tf_op jit(solution)/shard_map/ppermute | solution.py:1103
  423.6 3.3 collective-permute-done.40.refs_6_.refs_2_
  431.7 7.6 %collective-permute-done.41.refs_3_.refs_4_ = bf16[192,1024]{1,0:T(8,128)(2,1)S(1)} collective-permute-done((bf16[192,1024]{1,0:T(8,128)(2,1)S(1)}, bf16[192,1024]{1,0:T(8,128)(2,1)S(1)}, u32[]{:S(2)}, u32[]{:S(2)}) %collective-permute-start.41) | collective-permute-done | bytes 393248 | tf_op jit(solution)/shard_map/ppermute | solution.py:1135
  439.3 3.7 collective-permute-done.37.refs_1_
  443.0 8.4 %collective-permute-done.42.refs_4_.refs_2_ = bf16[192,1536]{1,0:T(8,128)(2,1)S(1)} collective-permute-done((bf16[192,1536]{1,0:T(8,128)(2,1)S(1)}, bf16[192,1536]{1,0:T(8,128)(2,1)S(1)}, u32[]{:S(2)}, u32[]{:S(2)}) %collective-permute-start.42) | collective-permute-done | bytes 589856 | tf_op jit(solution)/shard_map/ppermute | solution.py:1113
  454.2 3.8 finish.4
  458.0 5.2 %collective-permute-done.44.refs_1_.refs_4_ = bf16[384,768]{1,0:T(8,128)(2,1)S(1)} collective-permute-done((bf16[384,768]{1,0:T(8,128)(2,1)S(1)}, bf16[384,768]{1,0:T(8,128)(2,1)S(1)}, u32[]{:S(2)}, u32[]{:S(2)}) %collective-permute-start.44) | collective-permute-done | bytes 589856 | tf_op jit(solution)/shard_map/ppermute | solution.py:1108
  467.0 3.7 finish.5
  470.7 7.4 %collective-permute-done.43.refs_2_ = bf16[192,896]{1,0:T(8,128)(2,1)} collective-permute-done((bf16[192,896]{1,0:T(8,128)(2,1)}, bf16[192,896]{1,0:T(8,128)(2,1)}, u32[]{:S(2)}, u32[]{:S(2)}) %collective-permute-start.43) | collective-permute-done | bytes 344096 | tf_op jit(solution)/shard_map/ppermute | solution.py:1113
  478.2 3.5 finish.6
  483.5 4.1 finish.7
  491.6 4.8 collective-permute-done.50
  (403 shorter events, 160.9 us)
Async XLA Ops:
  7.2 293.2 %reduce-scatter.3.cloned.1.call-start = ((), (), s32[]{:S(2)}) async-start(), calls=%async_computation.2 | async-start | bytes 3932160 | tf_op jit(solution)/shard_map/reduce_scatter | solution.py:1128
  23.4 11.1 %collective-permute-start.1 = (bf16[2,512,128]{2,1,0:T(8,128)(2,1)S(1)}, bf16[2,512,128]{2,1,0:T(8,128)(2,1)}, u32[]{:S(2)}, u32[]{:S(2)}) collective-permute-start(bf16[2,512,128]{2,1,0:T(8,128)(2,1)S(1)} %bitcast.77), channel_id=1, source_target_pairs={{0,4},{4,8},{8,12},{1,5},{5,9},{9,13},{2,6},{6,10},{10,14},{3,7},{... | collective-permute-start | bytes 786440 | tf_op jit(solution)/shard_map/ppermute | solution.py:66
  29.1 9.8 %collective-permute-start = (bf16[2,512,128]{2,1,0:T(8,128)(2,1)S(1)}, bf16[2,512,128]{2,1,0:T(8,128)(2,1)}, u32[]{:S(2)}, u32[]{:S(2)}) collective-permute-start(bf16[2,512,128]{2,1,0:T(8,128)(2,1)S(1)} %bitcast.78), channel_id=1, source_target_pairs={{0,8},{4,12},{1,9},{5,13},{2,10},{6,14},{3,11},{7,15},{16,24},{20,... | collective-permute-start | bytes 786440 | tf_op jit(solution)/shard_map/ppermute | solution.py:66
  33.6 5.4 %collective-permute-start.4 = (bf16[2,512,128]{2,1,0:T(8,128)(2,1)S(1)}, bf16[2,512,128]{2,1,0:T(8,128)(2,1)}, u32[]{:S(2)}, u32[]{:S(2)}) collective-permute-start(bf16[2,512,128]{2,1,0:T(8,128)(2,1)S(1)} %bitcast.79), channel_id=1, source_target_pairs={{0,1},{1,0},{2,3},{3,2},{4,5},{5,4},{6,7},{7,6},{8,9},{9,8},{10,11... | collective-permute-start | bytes 786440 | tf_op jit(solution)/shard_map/ppermute | solution.py:48
  34.5 4.5 collective-permute-start.3
  50.3 3.3 collective-permute-start.6
  57.1 37.4 %collective-permute-start.7 = (bf16[256,1536]{1,0:T(8,128)(2,1)}, bf16[256,1536]{1,0:T(8,128)(2,1)}, u32[]{:S(2)}, u32[]{:S(2)}) collective-permute-start(bf16[256,1536]{1,0:T(8,128)(2,1)} %get-tuple-element.142.refs_3_), channel_id=1, source_target_pairs={{0,2},{1,3},{2,0},{3,1},{4,6},{5,7},{6,4},{7,5},{8,10},{9,11},{10,... | collective-permute-start | bytes 2359304 | tf_op jit(solution)/shard_map/ppermute | solution.py:52
  58.6 35.9 %collective-permute-start.8 = (bf16[256,1536]{1,0:T(8,128)(2,1)}, bf16[256,1536]{1,0:T(8,128)(2,1)}, u32[]{:S(2)}, u32[]{:S(2)}) collective-permute-start(bf16[256,1536]{1,0:T(8,128)(2,1)} %get-tuple-element.143.refs_4_), channel_id=1, source_target_pairs={{0,2},{1,3},{2,0},{3,1},{4,6},{5,7},{6,4},{7,5},{8,10},{9,11},{10,... | collective-permute-start | bytes 2359304 | tf_op jit(solution)/shard_map/ppermute | solution.py:52
  98.4 3.4 collective-permute-start.10
  135.2 330.6 %reduce-scatter.5.cloned.1.call-start = ((), (), s32[]{:S(2)}) async-start(), calls=%async_computation.3 | async-start | bytes 4423680 | tf_op jit(solution)/shard_map/reduce_scatter | solution.py:1148
  159.7 3.3 collective-permute-start.12
  160.0 46.0 %collective-permute-start.15 = (bf16[768,1280]{1,0:T(8,128)(2,1)}, bf16[768,1280]{1,0:T(8,128)(2,1)}, u32[]{:S(2)}, u32[]{:S(2)}) collective-permute-start(bf16[768,1280]{1,0:T(8,128)(2,1)} %get-tuple-element.167), channel_id=1, source_target_pairs={{0,16},{16,0},{1,17},{17,1},{2,18},{18,2},{3,19},{19,3},{4,20},{20... | collective-permute-start | bytes 5898248 | tf_op jit(solution)/shard_map/ppermute | solution.py:1103
  193.4 108.2 %collective-permute-start.26 = (bf16[768,2304]{1,0:T(8,128)(2,1)}, bf16[768,2304]{1,0:T(8,128)(2,1)}, u32[]{:S(2)}, u32[]{:S(2)}) collective-permute-start(bf16[768,2304]{1,0:T(8,128)(2,1)} %get-tuple-element.202), channel_id=1, source_target_pairs={{0,16},{16,0},{1,17},{17,1},{2,18},{18,2},{3,19},{19,3},{4,20},{20... | collective-permute-start | bytes 10616840 | tf_op jit(solution)/shard_map/ppermute | solution.py:1103
  194.9 21.3 %collective-permute-start.13 = (bf16[256,1536]{1,0:T(8,128)(2,1)}, bf16[256,1536]{1,0:T(8,128)(2,1)S(1)}, u32[]{:S(2)}, u32[]{:S(2)}) collective-permute-start(bf16[256,1536]{1,0:T(8,128)(2,1)} %get-tuple-element.165.refs_4_), channel_id=1, source_target_pairs={{0,2},{1,3},{2,0},{3,1},{4,6},{5,7},{6,4},{7,5},{8,10},{9,11},{10,... | collective-permute-start | bytes 2359304 | tf_op jit(solution)/shard_map/ppermute | solution.py:52
  196.4 35.0 %collective-permute-start.14 = (bf16[256,1536]{1,0:T(8,128)(2,1)}, bf16[256,1536]{1,0:T(8,128)(2,1)S(1)}, u32[]{:S(2)}, u32[]{:S(2)}) collective-permute-start(bf16[256,1536]{1,0:T(8,128)(2,1)} %get-tuple-element.166.refs_5_), channel_id=1, source_target_pairs={{0,2},{1,3},{2,0},{3,1},{4,6},{5,7},{6,4},{7,5},{8,10},{9,11},{10,... | collective-permute-start | bytes 2359304 | tf_op jit(solution)/shard_map/ppermute | solution.py:52
  236.9 11.0 %collective-permute-start.16 = (bf16[256,1536]{1,0:T(8,128)(2,1)S(1)}, bf16[256,1536]{1,0:T(8,128)(2,1)S(1)}, u32[]{:S(2)}, u32[]{:S(2)}) collective-permute-start(bf16[256,1536]{1,0:T(8,128)(2,1)S(1)} %get-tuple-element.173.refs_1_.refs_0_), channel_id=1, source_target_pairs={{0,1},{1,0},{2,3},{3,2},{4,5},{5,4},{6,7},{7,6},{8,9},{9,8},{10,11... | collective-permute-start | bytes 2359304 | tf_op jit(solution)/shard_map/ppermute | solution.py:48
  237.0 11.0 %collective-permute-start.17 = (bf16[256,1536]{1,0:T(8,128)(2,1)S(1)}, bf16[256,1536]{1,0:T(8,128)(2,1)S(1)}, u32[]{:S(2)}, u32[]{:S(2)}) collective-permute-start(bf16[256,1536]{1,0:T(8,128)(2,1)S(1)} %get-tuple-element.174.refs_2_.refs_1_), channel_id=1, source_target_pairs={{0,1},{1,0},{2,3},{3,2},{4,5},{5,4},{6,7},{7,6},{8,9},{9,8},{10,11... | collective-permute-start | bytes 2359304 | tf_op jit(solution)/shard_map/ppermute | solution.py:48
  237.5 32.5 %collective-permute-start.19 = (bf16[384,1280]{1,0:T(8,128)(2,1)S(1)}, bf16[384,1280]{1,0:T(8,128)(2,1)S(1)}, u32[]{:S(2)}, u32[]{:S(2)}) collective-permute-start(bf16[384,1280]{1,0:T(8,128)(2,1)S(1)} %get-tuple-element.182), channel_id=1, source_target_pairs={{0,4},{4,0},{8,12},{12,8},{1,5},{5,1},{9,13},{13,9},{2,6},{6,2},{1... | collective-permute-start | bytes 2949128 | tf_op jit(solution)/shard_map/ppermute | solution.py:1108
  258.8 12.2 %collective-permute-start.18 = (bf16[2,1536,128]{2,1,0:T(8,128)(2,1)S(1)}, bf16[2,1536,128]{2,1,0:T(8,128)(2,1)S(1)}, u32[]{:S(2)}, u32[]{:S(2)}) collective-permute-start(bf16[2,1536,128]{2,1,0:T(8,128)(2,1)S(1)} %get-tuple-element.180), channel_id=1, source_target_pairs={{0,1},{1,0},{2,3},{3,2},{4,5},{5,4},{6,7},{7,6},{8,9},{9,8},{10,11... | collective-permute-start | bytes 2359304 | tf_op jit(solution)/shard_map/ppermute | solution.py:48
  271.2 9.8 %collective-permute-start.22 = (bf16[2,512,128]{2,1,0:T(8,128)(2,1)S(1)}, bf16[2,512,128]{2,1,0:T(8,128)(2,1)S(1)}, u32[]{:S(2)}, u32[]{:S(2)}) collective-permute-start(bf16[2,512,128]{2,1,0:T(8,128)(2,1)S(1)} %get-tuple-element.194), channel_id=1, source_target_pairs={{4,0},{8,4},{12,8},{5,1},{9,5},{13,9},{6,2},{10,6},{14,10},{7,3},{... | collective-permute-start | bytes 786440 | tf_op jit(solution)/shard_map/ppermute | solution.py:66
  281.1 11.0 %collective-permute-start.23 = (bf16[2,512,128]{2,1,0:T(8,128)(2,1)S(1)}, bf16[2,512,128]{2,1,0:T(8,128)(2,1)S(1)}, u32[]{:S(2)}, u32[]{:S(2)}) collective-permute-start(bf16[2,512,128]{2,1,0:T(8,128)(2,1)S(1)} %get-tuple-element.196), channel_id=1, source_target_pairs={{4,0},{8,4},{12,8},{5,1},{9,5},{13,9},{6,2},{10,6},{14,10},{7,3},{... | collective-permute-start | bytes 786440 | tf_op jit(solution)/shard_map/ppermute | solution.py:66
  314.9 2.6 collective-permute-start.24
  314.9 3.6 collective-permute-start.25
  315.4 54.3 %collective-permute-start.33 = (bf16[768,1536]{1,0:T(8,128)(2,1)}, bf16[768,1536]{1,0:T(8,128)(2,1)S(1)}, u32[]{:S(2)}, u32[]{:S(2)}) collective-permute-start(bf16[768,1536]{1,0:T(8,128)(2,1)} %copy-done.90), channel_id=1, source_target_pairs={{0,16},{16,0},{1,17},{17,1},{2,18},{18,2},{3,19},{19,3},{4,20},{20... | collective-permute-start | bytes 7077896 | tf_op jit(solution)/shard_map/ppermute | solution.py:1103
  315.5 21.8 %collective-permute-start.20 = (bf16[256,1536]{1,0:T(8,128)(2,1)}, bf16[256,1536]{1,0:T(8,128)(2,1)S(1)}, u32[]{:S(2)}, u32[]{:S(2)}) collective-permute-start(bf16[256,1536]{1,0:T(8,128)(2,1)} %copy-done.94), channel_id=1, source_target_pairs={{0,1},{1,0},{2,3},{3,2},{4,5},{5,4},{6,7},{7,6},{8,9},{9,8},{10,11... | collective-permute-start | bytes 2359304 | tf_op jit(solution)/shard_map/ppermute | solution.py:48
  315.5 21.8 %collective-permute-start.21 = (bf16[256,1536]{1,0:T(8,128)(2,1)}, bf16[256,1536]{1,0:T(8,128)(2,1)S(1)}, u32[]{:S(2)}, u32[]{:S(2)}) collective-permute-start(bf16[256,1536]{1,0:T(8,128)(2,1)} %copy-done.93), channel_id=1, source_target_pairs={{0,1},{1,0},{2,3},{3,2},{4,5},{5,4},{6,7},{7,6},{8,9},{9,8},{10,11... | collective-permute-start | bytes 2359304 | tf_op jit(solution)/shard_map/ppermute | solution.py:48
  323.7 22.1 %collective-permute-start.29 = (bf16[256,1536]{1,0:T(8,128)(2,1)S(1)}, bf16[256,1536]{1,0:T(8,128)(2,1)S(1)}, u32[]{:S(2)}, u32[]{:S(2)}) collective-permute-start(bf16[256,1536]{1,0:T(8,128)(2,1)S(1)} %get-tuple-element.211.refs_4_), channel_id=1, source_target_pairs={{0,2},{1,3},{2,0},{3,1},{4,6},{5,7},{6,4},{7,5},{8,10},{9,11},{10,... | collective-permute-start | bytes 2359304 | tf_op jit(solution)/shard_map/ppermute | solution.py:52
  325.3 35.0 %collective-permute-start.30 = (bf16[256,1536]{1,0:T(8,128)(2,1)S(1)}, bf16[256,1536]{1,0:T(8,128)(2,1)S(1)}, u32[]{:S(2)}, u32[]{:S(2)}) collective-permute-start(bf16[256,1536]{1,0:T(8,128)(2,1)S(1)} %get-tuple-element.212.refs_5_), channel_id=1, source_target_pairs={{0,2},{1,3},{2,0},{3,1},{4,6},{5,7},{6,4},{7,5},{8,10},{9,11},{10,... | collective-permute-start | bytes 2359304 | tf_op jit(solution)/shard_map/ppermute | solution.py:52
  362.5 14.1 %collective-permute-start.31 = (f32[256,1536]{1,0:T(8,128)S(1)}, f32[256,1536]{1,0:T(8,128)S(1)}, u32[]{:S(2)}, u32[]{:S(2)}) collective-permute-start(f32[256,1536]{1,0:T(8,128)S(1)} %get-tuple-element.214.refs_1_), channel_id=1, source_target_pairs={{0,1},{1,0},{2,3},{3,2},{4,5},{5,4},{6,7},{7,6},{8,9},{9,8},{10,11... | collective-permute-start | bytes 4718600 | tf_op jit(solution)/shard_map/ppermute | solution.py:48
  362.6 15.8 %collective-permute-start.32 = (f32[256,1536]{1,0:T(8,128)S(1)}, f32[256,1536]{1,0:T(8,128)S(1)}, u32[]{:S(2)}, u32[]{:S(2)}) collective-permute-start(f32[256,1536]{1,0:T(8,128)S(1)} %get-tuple-element.215.refs_2_), channel_id=1, source_target_pairs={{0,1},{1,0},{2,3},{3,2},{4,5},{5,4},{6,7},{7,6},{8,9},{9,8},{10,11... | collective-permute-start | bytes 4718600 | tf_op jit(solution)/shard_map/ppermute | solution.py:48
  363.1 38.3 %collective-permute-start.36 = (bf16[768,896]{1,0:T(8,128)(2,1)}, bf16[768,896]{1,0:T(8,128)(2,1)S(1)}, u32[]{:S(2)}, u32[]{:S(2)}) collective-permute-start(bf16[768,896]{1,0:T(8,128)(2,1)} %get-tuple-element.222), channel_id=1, source_target_pairs={{0,16},{16,0},{1,17},{17,1},{2,18},{18,2},{3,19},{19,3},{4,20},{20... | collective-permute-start | bytes 4128776 | tf_op jit(solution)/shard_map/ppermute | solution.py:1103
  363.1 20.4 %collective-permute-start.27 = (bf16[256,1536]{1,0:T(8,128)(2,1)S(1)}, bf16[256,1536]{1,0:T(8,128)(2,1)S(1)}, u32[]{:S(2)}, u32[]{:S(2)}) collective-permute-start(bf16[256,1536]{1,0:T(8,128)(2,1)S(1)} %get-tuple-element.208.refs_1_), channel_id=1, source_target_pairs={{0,2},{1,3},{2,0},{3,1},{4,6},{5,7},{6,4},{7,5},{8,10},{9,11},{10,... | collective-permute-start | bytes 2359304 | tf_op jit(solution)/shard_map/ppermute | solution.py:52
  369.7 29.7 %collective-permute-start.28 = (bf16[256,1536]{1,0:T(8,128)(2,1)S(1)}, bf16[256,1536]{1,0:T(8,128)(2,1)S(1)}, u32[]{:S(2)}, u32[]{:S(2)}) collective-permute-start(bf16[256,1536]{1,0:T(8,128)(2,1)S(1)} %get-tuple-element.209.refs_2_), channel_id=1, source_target_pairs={{0,2},{1,3},{2,0},{3,1},{4,6},{5,7},{6,4},{7,5},{8,10},{9,11},{10,... | collective-permute-start | bytes 2359304 | tf_op jit(solution)/shard_map/ppermute | solution.py:52
  376.7 35.5 %collective-permute-start.39 = (bf16[384,1536]{1,0:T(8,128)(2,1)}, bf16[384,1536]{1,0:T(8,128)(2,1)S(1)}, u32[]{:S(2)}, u32[]{:S(2)}) collective-permute-start(bf16[384,1536]{1,0:T(8,128)(2,1)} %get-tuple-element.231), channel_id=1, source_target_pairs={{0,4},{4,0},{8,12},{12,8},{1,5},{5,1},{9,13},{13,9},{2,6},{6,2},{1... | collective-permute-start | bytes 3538952 | tf_op jit(solution)/shard_map/ppermute | solution.py:1108
  378.4 45.3 %collective-permute-start.38 = (bf16[768,768]{1,0:T(8,128)(2,1)S(1)}, bf16[768,768]{1,0:T(8,128)(2,1)S(1)}, u32[]{:S(2)}, u32[]{:S(2)}) collective-permute-start(bf16[768,768]{1,0:T(8,128)(2,1)S(1)} %copy-done.92), channel_id=1, source_target_pairs={{0,16},{16,0},{1,17},{17,1},{2,18},{18,2},{3,19},{19,3},{4,20},{20... | collective-permute-start | bytes 3538952 | tf_op jit(solution)/shard_map/ppermute | solution.py:1103
  400.8 9.1 %collective-permute-start.34 = (bf16[256,1536]{1,0:T(8,128)(2,1)S(1)}, bf16[256,1536]{1,0:T(8,128)(2,1)S(1)}, u32[]{:S(2)}, u32[]{:S(2)}) collective-permute-start(bf16[256,1536]{1,0:T(8,128)(2,1)S(1)} %get-tuple-element.220.refs_1_), channel_id=1, source_target_pairs={{0,1},{1,0},{2,3},{3,2},{4,5},{5,4},{6,7},{7,6},{8,9},{9,8},{10,11... | collective-permute-start | bytes 2359304 | tf_op jit(solution)/shard_map/ppermute | solution.py:48
  400.9 9.1 %collective-permute-start.35 = (bf16[256,1536]{1,0:T(8,128)(2,1)S(1)}, bf16[256,1536]{1,0:T(8,128)(2,1)S(1)}, u32[]{:S(2)}, u32[]{:S(2)}) collective-permute-start(bf16[256,1536]{1,0:T(8,128)(2,1)S(1)} %get-tuple-element.221.refs_2_), channel_id=1, source_target_pairs={{0,1},{1,0},{2,3},{3,2},{4,5},{5,4},{6,7},{7,6},{8,9},{9,8},{10,11... | collective-permute-start | bytes 2359304 | tf_op jit(solution)/shard_map/ppermute | solution.py:48
  401.4 25.6 %collective-permute-start.40 = (bf16[192,1280]{1,0:T(8,128)(2,1)S(1)}, bf16[192,1280]{1,0:T(8,128)(2,1)S(1)}, u32[]{:S(2)}, u32[]{:S(2)}) collective-permute-start(bf16[192,1280]{1,0:T(8,128)(2,1)S(1)} %copy-done.98), channel_id=1, source_target_pairs={{0,8},{4,12},{8,0},{12,4},{1,9},{5,13},{9,1},{13,5},{2,10},{6,14},... | collective-permute-start | bytes 1474568 | tf_op jit(solution)/shard_map/ppermute | solution.py:1113
  409.9 33.1 %collective-permute-start.37 = (bf16[384,896]{1,0:T(8,128)(2,1)S(1)}, bf16[384,896]{1,0:T(8,128)(2,1)S(1)}, u32[]{:S(2)}, u32[]{:S(2)}) collective-permute-start(bf16[384,896]{1,0:T(8,128)(2,1)S(1)} %get-tuple-element.228), channel_id=1, source_target_pairs={{0,4},{4,0},{8,12},{12,8},{1,5},{5,1},{9,13},{13,9},{2,6},{6,2},{1... | collective-permute-start | bytes 2064392 | tf_op jit(solution)/shard_map/ppermute | solution.py:1108
  412.3 39.1 %collective-permute-start.42 = (bf16[192,1536]{1,0:T(8,128)(2,1)S(1)}, bf16[192,1536]{1,0:T(8,128)(2,1)S(1)}, u32[]{:S(2)}, u32[]{:S(2)}) collective-permute-start(bf16[192,1536]{1,0:T(8,128)(2,1)S(1)} %get-tuple-element.236), channel_id=1, source_target_pairs={{0,8},{4,12},{8,0},{12,4},{1,9},{5,13},{9,1},{13,5},{2,10},{6,14},... | collective-permute-start | bytes 1769480 | tf_op jit(solution)/shard_map/ppermute | solution.py:1113
  429.8 33.4 %collective-permute-start.44 = (bf16[384,768]{1,0:T(8,128)(2,1)S(1)}, bf16[384,768]{1,0:T(8,128)(2,1)S(1)}, u32[]{:S(2)}, u32[]{:S(2)}) collective-permute-start(bf16[384,768]{1,0:T(8,128)(2,1)S(1)} %get-tuple-element.240), channel_id=1, source_target_pairs={{0,4},{4,0},{8,12},{12,8},{1,5},{5,1},{9,13},{13,9},{2,6},{6,2},{1... | collective-permute-start | bytes 1769480 | tf_op jit(solution)/shard_map/ppermute | solution.py:1108
  429.9 9.4 %collective-permute-start.41 = (bf16[192,1024]{1,0:T(8,128)(2,1)S(1)}, bf16[192,1024]{1,0:T(8,128)(2,1)S(1)}, u32[]{:S(2)}, u32[]{:S(2)}) collective-permute-start(bf16[192,1024]{1,0:T(8,128)(2,1)S(1)} %copy-done.84), channel_id=1, source_target_pairs={{0,16},{16,0},{1,17},{17,1},{2,18},{18,2},{3,19},{19,3},{4,20},{20... | collective-permute-start | bytes 1179656 | tf_op jit(solution)/shard_map/ppermute | solution.py:1135
  452.4 25.8 %collective-permute-start.43 = (bf16[192,896]{1,0:T(8,128)(2,1)}, bf16[192,896]{1,0:T(8,128)(2,1)}, u32[]{:S(2)}, u32[]{:S(2)}) collective-permute-start(bf16[192,896]{1,0:T(8,128)(2,1)} %get-tuple-element.237), channel_id=1, source_target_pairs={{0,8},{4,12},{8,0},{12,4},{1,9},{5,13},{9,1},{13,5},{2,10},{6,14},... | collective-permute-start | bytes 1032200 | tf_op jit(solution)/shard_map/ppermute | solution.py:1113
  452.4 5.6 %collective-permute-start.45 = (f32[8,512]{1,0:T(8,128)S(1)}, f32[8,512]{1,0:T(8,128)S(1)}, u32[]{:S(2)}, u32[]{:S(2)}) collective-permute-start(f32[8,512]{1,0:T(8,128)S(1)} %copy-done.87), channel_id=1, source_target_pairs={{0,16},{16,0},{1,17},{17,1},{2,18},{18,2},{3,19},{19,3},{4,20},{20... | collective-permute-start | bytes 49160 | tf_op jit(solution)/shard_map/ppermute | solution.py:1239
  464.0 19.5 %collective-permute-start.48 = (bf16[192,768]{1,0:T(8,128)(2,1)}, bf16[192,768]{1,0:T(8,128)(2,1)S(1)}, u32[]{:S(2)}, u32[]{:S(2)}) collective-permute-start(bf16[192,768]{1,0:T(8,128)(2,1)} %get-tuple-element.252), channel_id=1, source_target_pairs={{0,8},{4,12},{8,0},{12,4},{1,9},{5,13},{9,1},{13,5},{2,10},{6,14},... | collective-permute-start | bytes 884744 | tf_op jit(solution)/shard_map/ppermute | solution.py:1113
  464.0 17.7 %collective-permute-start.46 = (f32[8,512]{1,0:T(8,128)S(1)}, f32[8,512]{1,0:T(8,128)}, u32[]{:S(2)}, u32[]{:S(2)}) collective-permute-start(f32[8,512]{1,0:T(8,128)S(1)} %get-tuple-element.248.refs_0_), channel_id=1, source_target_pairs={{0,4},{4,0},{8,12},{12,8},{1,5},{5,1},{9,13},{13,9},{2,6},{6,2},{1... | collective-permute-start | bytes 49160 | tf_op jit(solution)/shard_map/ppermute | solution.py:1241
  482.4 5.4 %collective-permute-start.47 = (f32[8,512]{1,0:T(8,128)S(1)}, f32[8,512]{1,0:T(8,128)S(1)}, u32[]{:S(2)}, u32[]{:S(2)}) collective-permute-start(f32[8,512]{1,0:T(8,128)S(1)} %get-tuple-element.250), channel_id=1, source_target_pairs={{0,8},{4,12},{8,0},{12,4},{1,9},{5,13},{9,1},{13,5},{2,10},{6,14},... | collective-permute-start | bytes 49160 | tf_op jit(solution)/shard_map/ppermute | solution.py:1248
  489.2 7.2 %collective-permute-start.50 = (f32[2,200,128]{2,1,0:T(8,128)S(1)}, f32[2,200,128]{2,1,0:T(8,128)S(1)}, u32[]{:S(2)}, u32[]{:S(2)}) collective-permute-start(f32[2,200,128]{2,1,0:T(8,128)S(1)} %maximum_select_fusion.1), channel_id=1, source_target_pairs={{0,2},{1,3},{2,0},{3,1},{4,6},{5,7},{6,4},{7,5},{8,10},{9,11},{10,... | collective-permute-start | bytes 614408 | tf_op jit(solution)/shard_map/ppermute | solution.py:52
  (123 other events, 1255.1 us)
Sparse Core Ops, SparseCore 0:
  135.3 71.0 reduce-scatter.2
  315.0 65.7 reduce-scatter.4

commit v11 on v10

--- a/solution.py
+++ b/solution.py
@@ -1213,9 +1213,9 @@
     )
     sent = core_swaps(narrow(order, [(grad_qkv, weight)], 1, (), 1))
     down_b.across()
-    gate.own()
     mine = narrow(order, [(grad_qkv, weight)], 0, sent, 1)
     come = chip_swaps(mine)
+    gate.own()
     last_parts = [(0, 0, 0, grad_qkv.shape[1] // HD, 0), (1, 1, 0, heads, 0)]
     last = Rows([h_one_t, branch_t], [grad_qkv, mixed], last_parts, HD)
     ffn_mine = narrow(order, [(hidden, down_t)], 0, ffn_sent)

time: 512 us -> 496 us (0.969)
  waiting for transfers between devices: 148 us -> 136 us
  Pallas kernels: 189 us -> 198 us
  local copies, waits for them, and re-layouts: 90.3 us -> 83.8 us
    ppermute x9, waiting for transfers between devices: 52.2 us -> 39.5 us  [chip_swap(): return lax.ppermute(value, 'tensor', flipped('tensor', 1))]
    pallas_call x44, Pallas kernels: 180 us -> 189 us  [__call__(): pl.pallas_call(run, grid_spec=pltpu.PrefetchScalarGridSpec(num_scalar_pre...]
    unnamed x241 -> x215, local copies, waits for them, and re-layouts: 80.1 us -> 73.6 us
  transfers between devices with their start and end apart: 53 -> 53, of which waited for: 29 -> 28; matrix products, arithmetic and copies ran while one was open for 3% -> 3% of each run, Pallas kernels for 27% -> 30%
where the time goes in v11:
time: 496 us; the launch traced here: 494 us
  Pallas kernels  198 us (40%)
  waiting for transfers between devices  136 us (27%)
  local copies, waits for them, and re-layouts  83.8 us (17%)
  starting transfers between devices  51.5 us (10%)
  between operations  15.4 us (3%)
  other arithmetic  9.38 us (2%)
    pallas_call x44, Pallas kernels, __call__(): pl.pallas_call(run, grid_spec=pltpu.PrefetchScalarGridSpec(num_scalar_pre...  189 us
    unnamed x215, local copies, waits for them, and re-layouts  73.6 us
    ppermute x9, waiting for transfers between devices, chip_swap(): return lax.ppermute(value, 'tensor', flipped('tensor', 1))  39.5 us
    ppermute x4, waiting for transfers between devices, relay(): self.last = lax.ppermute(sent, 'seq', flipped('seq', 1))  19.5 us
    ppermute x5, waiting for transfers between devices, __init__(): self.come = lax.ppermute(sent, 'dp', flipped('dp', 0))  18.6 us
    ppermute x4, waiting for transfers between devices, own(): self.come = lax.ppermute(send, 'seq', flipped('seq', 0))  17.8 us
    ppermute x4, waiting for transfers between devices, shifted(): return lax.ppermute(value, 'seq', route)  17.6 us
    ppermute x21, waiting for transfers between devices, core_swap(): return lax.ppermute(value, 'tensor', flipped('tensor', 0))  13.8 us
  transfers between devices with their start and end apart: 53, of which 28 were waited for; matrix products, arithmetic and copies ran while one was open for 3% of the time, Pallas kernels for 30%

profile of v11, /device:TPU:0, one launch (start us, length us, event | category | flops | bytes accessed | tf_op | source)
XLA Modules:
  0.0 494.0 jit_solution(15137314151434595657)
XLA Ops:
  17.2 3.6 first.1
  23.4 5.6 %collective-permute-start.1 = (bf16[2,512,128]{2,1,0:T(8,128)(2,1)S(1)}, bf16[2,512,128]{2,1,0:T(8,128)(2,1)}, u32[]{:S(2)}, u32[]{:S(2)}) collective-permute-start(bf16[2,512,128]{2,1,0:T(8,128)(2,1)S(1)} %bitcast.77), channel_id=1, source_target_pairs={{0,4},{4,8},{8,12},{1,5},{5,9},{9,13},{2,6},{6,10},{10,14},{3,7},{... | collective-permute-start | bytes 786440 | tf_op jit(solution)/shard_map/ppermute | solution.py:66
  29.1 4.5 collective-permute-start
  34.5 4.3 collective-permute-done.refs_0_.refs_9_
  41.9 6.1 %attend.1 = (bf16[2,512,384]{2,1,0:T(8,128)(2,1)S(1)}, f32[2,2,768]{2,1,0:T(2,128)S(1)}) custom-call(s32[2,2]{1,0:T(2,128)S(1)} %shift-right-logical_maximum_fusion.low_ref.refs_0_, s32[1]{0:T(128)} %bitcast.core_ref.refs_0_.refs_1_, bf16[2,512,384]{2,1,0:T(8,128)(2,1)S(1)} %bitcast.74, s32[2,1,512]{2,1,0:T(1,128)S(1)} %sub.44.start_ref.refs_3_, ...), custom_call_target="tpu_custom_call" | custom-call | flops 8000000 | bytes 4194 | tf_op jit(solution)/shard_map/attend/pallas_call | solution.py:253
  53.6 3.4 narrow.9
  60.3 4.5 constant_dynamic-slice_fusion.2
  74.6 5.2 %copy-done.9 = bf16[1536,2240]{0,1:T(8,128)(2,1)S(1)} copy-done((bf16[1536,2240]{0,1:T(8,128)(2,1)S(1)}, bf16[1536,2240]{0,1:T(8,128)(2,1)}, u32[]{:S(2)}) %copy-start.9) | copy-done | bytes 6881304
  79.8 9.3 %grad_hidden.1 = (bf16[1024,2240]{1,0:T(8,128)(2,1)S(1)}, f32[8,128]{1,0:T(8,128)S(1)}) custom-call(bf16[1024,1536]{1,0:T(8,128)(2,1)S(1)} %get-tuple-element.146.refs_0_.refs_3_, bf16[2240,1536]{1,0:T(8,128)(2,1)S(1)} %bitcast.61, f32[8,128]{1,0:T(8,128)S(1)} %get-tuple-element.147.refs_2_, bf16[192,2240]{1,0:T(8,128)(2,1)S(1)} %copy-done.40, ...), custom_call_target="tpu_custom_call" | custom-call | flops 7046430 | bytes 15728 | tf_op jit(solution)/shard_map/grad_hidden/pallas_call | solution.py:92
  94.4 3.8 middle.1
  104.1 20.3 %gated.1 = (bf16[1024,2240]{1,0:T(8,128)(2,1)S(1)}, bf16[1024,2240]{1,0:T(8,128)(2,1)S(1)}, bf16[1024,2240]{1,0:T(8,128)(2,1)S(1)}, f32[8,128]{1,0:T(8,128)S(1)}) custom-call(bf16[1024,2240]{1,0:T(8,128)(2,1)S(1)} %copy-done.49, bf16[2240,1536]{1,0:T(8,128)(2,1)} %bitcast.58, bf16[2240,1536]{1,0:T(8,128)(2,1)} %bitcast.83, ...), custom_call_target="tpu_custom_call" | custom-call | flops 14092861 | bytes 31457 | tf_op jit(solution)/shard_map/gated/pallas_call | solution.py:92
  126.6 4.8 share.9
  139.7 4.2 share.10
  150.8 10.3 %narrow.10 = (bf16[256,1536]{1,0:T(8,128)(2,1)S(1)}, bf16[256,1536]{1,0:T(8,128)(2,1)S(1)}, f32[8,128]{1,0:T(8,128)S(1)}) custom-call(bf16[1024,2240]{1,0:T(8,128)(2,1)S(1)} %copy-done.5, bf16[2240,1536]{1,0:T(8,128)(2,1)S(1)} %bitcast.59, bf16[1024,2240]{1,0:T(8,128)(2,1)S(1)} %bitcast.47, bf16[2240,1536]{1,0:T(8,128)(2,1)} %bitcast.84, ...), custom_call_target="tpu_custom_call" | custom-call | flops 7046430 | bytes 19922 | tf_op jit(solution)/shard_map/narrow/pallas_call | solution.py:92
  167.7 11.0 %narrow.11 = (bf16[256,1536]{1,0:T(8,128)(2,1)}, bf16[256,1536]{1,0:T(8,128)(2,1)}, f32[8,128]{1,0:T(8,128)S(1)}) custom-call(bf16[1024,2240]{1,0:T(8,128)(2,1)S(1)} %bitcast.55, bf16[2240,1536]{1,0:T(8,128)(2,1)S(1)} %bitcast.60, bf16[1024,2240]{1,0:T(8,128)(2,1)S(1)} %bitcast.47, bf16[2240,1536]{1,0:T(8,128)(2,1)} %bitcast.85, ...), custom_call_target="tpu_custom_call" | custom-call | flops 7046430 | bytes 19922 | tf_op jit(solution)/shard_map/narrow/pallas_call | solution.py:92
  182.3 13.8 %share.11 = (bf16[768,2304]{1,0:T(8,128)(2,1)}, bf16[768,1536]{1,0:T(8,128)(2,1)S(1)}, bf16[768,768]{1,0:T(8,128)(2,1)}, f32[8,128]{1,0:T(8,128)S(1)}) custom-call(s32[1]{0:T(128)} %bitcast.10.refs_0_, s32[1]{0:T(128)} %constant.59.clone.1.refs_0_.refs_1_, bf16[1536,1024]{1,0:T(8,128)(2,1)S(1)} %get-tuple-element.169.refs_2_, ...), custom_call_target="tpu_custom_call" | custom-call | flops 7247757 | bytes 18087 | tf_op jit(solution)/shard_map/share/pallas_call | solution.py:92
  202.4 5.9 %share.12 = (bf16[384,1280]{1,0:T(8,128)(2,1)S(1)}, bf16[384,1280]{1,0:T(8,128)(2,1)S(1)}, f32[8,128]{1,0:T(8,128)S(1)}) custom-call(s32[1]{0:T(128)} %bitcast.11.refs_0_, s32[4]{0:T(128)S(1)} %pad_add_fusion.refs_1_, bf16[1536,1024]{1,0:T(8,128)(2,1)S(1)} %copy-done.18, bf16[1024,2240]{1,0:T(8,128)(2,1)S(1)} %copy-done.3, ...), custom_call_target="tpu_custom_call" | custom-call | flops 2013265 | bytes 6160 | tf_op jit(solution)/shard_map/share/pallas_call | solution.py:92
  208.4 7.1 %collective-permute-done.14.refs_7_ = bf16[256,1536]{1,0:T(8,128)(2,1)} collective-permute-done((bf16[256,1536]{1,0:T(8,128)(2,1)}, bf16[256,1536]{1,0:T(8,128)(2,1)}, u32[]{:S(2)}, u32[]{:S(2)}) %collective-permute-start.14) | collective-permute-done | bytes 786464 | tf_op jit(solution)/shard_map/ppermute | solution.py:52
  215.5 4.1 norm_back.2
  220.2 9.1 %collective-permute-start.19 = (bf16[384,1280]{1,0:T(8,128)(2,1)S(1)}, bf16[384,1280]{1,0:T(8,128)(2,1)S(1)}, u32[]{:S(2)}, u32[]{:S(2)}) collective-permute-start(bf16[384,1280]{1,0:T(8,128)(2,1)S(1)} %get-tuple-element.182), channel_id=1, source_target_pairs={{0,4},{4,0},{8,12},{12,8},{1,5},{5,1},{9,13},{13,9},{2,6},{6,2},{1... | collective-permute-start | bytes 2949128 | tf_op jit(solution)/shard_map/ppermute | solution.py:1108
  231.3 8.9 %attend_back.1 = (bf16[2,512,384]{2,1,0:T(8,128)(2,1)S(1)}, bf16[2,1536,128]{2,1,0:T(8,128)(2,1)S(1)}, bf16[2,1536,128]{2,1,0:T(8,128)(2,1)S(1)}, f32[8,128]{1,0:T(8,128)S(1)}) custom-call(s32[2,2]{1,0:T(2,128)S(1)} %shift-right-logical_maximum_fusion.low_ref.refs_0_, s32[1]{0:T(128)} %bitcast.core_ref.refs_0_.refs_1_, bf16[2,512,384]{2,1,0:T(8,128)(2,1)S(1)} %bitcast.75, ...), custom_call_target="tpu_custom_call" | custom-call | flops 20000000 | bytes 6291 | tf_op jit(solution)/shard_map/attend_back/pallas_call | solution.py:92
  243.4 7.9 %collective-permute-done.19.refs_1_ = bf16[384,1280]{1,0:T(8,128)(2,1)S(1)} collective-permute-done((bf16[384,1280]{1,0:T(8,128)(2,1)S(1)}, bf16[384,1280]{1,0:T(8,128)(2,1)S(1)}, u32[]{:S(2)}, u32[]{:S(2)}) %collective-permute-start.19) | collective-permute-done | bytes 983072 | tf_op jit(solution)/shard_map/ppermute | solution.py:1108
  254.6 5.3 %narrow.12 = (bf16[256,1536]{1,0:T(8,128)(2,1)S(1)}, bf16[256,1536]{1,0:T(8,128)(2,1)S(1)}, f32[8,128]{1,0:T(8,128)S(1)}) custom-call(bf16[1024,2240]{1,0:T(8,128)(2,1)S(1)} %bitcast.51, bf16[2240,1536]{1,0:T(8,128)(2,1)S(1)} %bitcast.64, f32[8,128]{1,0:T(8,128)S(1)} %get-tuple-element.186.refs_2_), custom_call_target="tpu_custom_call" | custom-call | flops 3523215 | bytes 10747 | tf_op jit(solution)/shard_map/narrow/pallas_call | solution.py:92
  264.7 10.0 %collective-permute-done.23.refs_5_ = bf16[2,512,128]{2,1,0:T(8,128)(2,1)S(1)} collective-permute-done((bf16[2,512,128]{2,1,0:T(8,128)(2,1)S(1)}, bf16[2,512,128]{2,1,0:T(8,128)(2,1)S(1)}, u32[]{:S(2)}, u32[]{:S(2)}) %collective-permute-start.23) | collective-permute-done | bytes 262176 | tf_op jit(solution)/shard_map/ppermute | solution.py:66
  275.4 3.4 narrow.13
  282.6 4.5 narrow.14
  291.3 8.3 %share.13 = (bf16[768,2304]{1,0:T(8,128)(2,1)S(1)}, f32[8,128]{1,0:T(8,128)S(1)}) custom-call(s32[1]{0:T(128)} %bitcast.11.refs_0_, s32[1]{0:T(128)} %constant.59.clone.1.refs_0_.refs_1_, bf16[1536,1024]{1,0:T(8,128)(2,1)S(1)} %copy-done.12, bf16[1024,2240]{1,0:T(8,128)(2,1)S(1)} %copy-done.6, bf16[768,2304]{1,0:T(8,128)(2,1)} %collective-permute-done.24.refs_4_, ...), custom_call_target="tpu_custom_call" | custom-call | flops 3623878 | bytes 9830 | tf_op jit(solution)/shard_map/share/pallas_call | solution.py:92
  308.8 5.3 %share.14 = (bf16[768,896]{1,0:T(8,128)(2,1)}, f32[8,128]{1,0:T(8,128)S(1)}) custom-call(s32[1]{0:T(128)} %bitcast.10.refs_0_, s32[1]{0:T(128)} %constant.59.clone.1.refs_0_.refs_1_, bf16[1536,1024]{1,0:T(8,128)(2,1)S(1)} %copy-done.24, bf16[1536,1024]{1,0:T(8,128)(2,1)S(1)} %copy-done.30, bf16[1024,512]{1,0:T(8,128)(2,1)S(1)} %get-tuple-element.198.refs_0_.refs_4_, ...), custom_call_target="tpu_custom_call" | custom-call | flops 1409286 | bytes 4784 | tf_op jit(solution)/shard_map/share/pallas_call | solution.py:92
  317.1 6.0 %narrow.15 = (bf16[256,1536]{1,0:T(8,128)(2,1)}, bf16[256,1536]{1,0:T(8,128)(2,1)}, f32[8,128]{1,0:T(8,128)S(1)}) custom-call(bf16[1024,2240]{1,0:T(8,128)(2,1)S(1)} %bitcast.53, bf16[2240,1536]{1,0:T(8,128)(2,1)S(1)} %bitcast.65, bf16[256,1536]{1,0:T(8,128)(2,1)S(1)} %collective-permute-done.20.refs_2_, ...), custom_call_target="tpu_custom_call" | custom-call | flops 3523215 | bytes 10747 | tf_op jit(solution)/shard_map/narrow/pallas_call | solution.py:92
  323.2 15.8 %collective-permute-done.30.refs_7_ = bf16[256,1536]{1,0:T(8,128)(2,1)S(1)} collective-permute-done((bf16[256,1536]{1,0:T(8,128)(2,1)}, bf16[256,1536]{1,0:T(8,128)(2,1)S(1)}, u32[]{:S(2)}, u32[]{:S(2)}) %collective-permute-start.30) | collective-permute-done | bytes 786464 | tf_op jit(solution)/shard_map/ppermute | solution.py:52
  346.6 9.3 %collective-permute-done.33.refs_4_ = bf16[768,1536]{1,0:T(8,128)(2,1)} collective-permute-done((bf16[768,1536]{1,0:T(8,128)(2,1)}, bf16[768,1536]{1,0:T(8,128)(2,1)}, u32[]{:S(2)}, u32[]{:S(2)}) %collective-permute-start.33) | collective-permute-done | bytes 2359328 | tf_op jit(solution)/shard_map/ppermute | solution.py:1103
  357.5 7.0 %share.15 = (bf16[384,1536]{1,0:T(8,128)(2,1)}, bf16[384,1536]{1,0:T(8,128)(2,1)S(1)}, f32[8,128]{1,0:T(8,128)S(1)}) custom-call(s32[1]{0:T(128)} %bitcast.11.refs_0_, s32[4]{0:T(128)S(1)} %pad_add_fusion.refs_1_, bf16[1536,1024]{1,0:T(8,128)(2,1)S(1)} %copy-done.13, bf16[1024,2240]{1,0:T(8,128)(2,1)S(1)} %bitcast.49, ...), custom_call_target="tpu_custom_call" | custom-call | flops 2415919 | bytes 7077 | tf_op jit(solution)/shard_map/share/pallas_call | solution.py:92
  366.2 3.3 place.2
  369.5 11.9 %collective-permute-done.28.refs_4_ = bf16[256,1536]{1,0:T(8,128)(2,1)S(1)} collective-permute-done((bf16[256,1536]{1,0:T(8,128)(2,1)}, bf16[256,1536]{1,0:T(8,128)(2,1)S(1)}, u32[]{:S(2)}, u32[]{:S(2)}) %collective-permute-start.28) | collective-permute-done | bytes 786464 | tf_op jit(solution)/shard_map/ppermute | solution.py:52
  383.4 3.5 layer.1
  390.1 5.8 %share.16 = (bf16[384,896]{1,0:T(8,128)(2,1)S(1)}, bf16[384,896]{1,0:T(8,128)(2,1)S(1)}, f32[8,128]{1,0:T(8,128)S(1)}) custom-call(s32[1]{0:T(128)} %bitcast.11.refs_0_, s32[4]{0:T(128)S(1)} %pad_add_fusion.refs_1_, bf16[1536,1024]{1,0:T(8,128)(2,1)S(1)} %copy-done.25, bf16[1536,1024]{1,0:T(8,128)(2,1)S(1)} %copy-done.31, ...), custom_call_target="tpu_custom_call" | custom-call | flops 1409286 | bytes 4784 | tf_op jit(solution)/shard_map/share/pallas_call | solution.py:92
  400.5 9.3 %collective-permute-done.38.refs_4_ = bf16[768,768]{1,0:T(8,128)(2,1)S(1)} collective-permute-done((bf16[768,768]{1,0:T(8,128)(2,1)}, bf16[768,768]{1,0:T(8,128)(2,1)S(1)}, u32[]{:S(2)}, u32[]{:S(2)}) %collective-permute-start.38) | collective-permute-done | bytes 1179680 | tf_op jit(solution)/shard_map/ppermute | solution.py:1103
  409.8 3.4 collective-permute-done.40.refs_6_.refs_2_
  416.8 8.6 %collective-permute-done.41.refs_3_.refs_4_ = bf16[192,1024]{1,0:T(8,128)(2,1)S(1)} collective-permute-done((bf16[192,1024]{1,0:T(8,128)(2,1)S(1)}, bf16[192,1024]{1,0:T(8,128)(2,1)S(1)}, u32[]{:S(2)}, u32[]{:S(2)}) %collective-permute-start.41) | collective-permute-done | bytes 393248 | tf_op jit(solution)/shard_map/ppermute | solution.py:1135
  425.5 3.6 collective-permute-done.37.refs_1_
  429.1 8.6 %collective-permute-done.42.refs_4_.refs_2_ = bf16[192,1536]{1,0:T(8,128)(2,1)S(1)} collective-permute-done((bf16[192,1536]{1,0:T(8,128)(2,1)S(1)}, bf16[192,1536]{1,0:T(8,128)(2,1)S(1)}, u32[]{:S(2)}, u32[]{:S(2)}) %collective-permute-start.42) | collective-permute-done | bytes 589856 | tf_op jit(solution)/shard_map/ppermute | solution.py:1113
  439.3 3.8 finish.4
  443.0 6.2 %collective-permute-done.44.refs_1_.refs_4_ = bf16[384,768]{1,0:T(8,128)(2,1)S(1)} collective-permute-done((bf16[384,768]{1,0:T(8,128)(2,1)S(1)}, bf16[384,768]{1,0:T(8,128)(2,1)S(1)}, u32[]{:S(2)}, u32[]{:S(2)}) %collective-permute-start.44) | collective-permute-done | bytes 589856 | tf_op jit(solution)/shard_map/ppermute | solution.py:1108
  453.4 3.7 finish.5
  457.1 7.3 %collective-permute-done.43.refs_2_ = bf16[192,896]{1,0:T(8,128)(2,1)} collective-permute-done((bf16[192,896]{1,0:T(8,128)(2,1)}, bf16[192,896]{1,0:T(8,128)(2,1)}, u32[]{:S(2)}, u32[]{:S(2)}) %collective-permute-start.43) | collective-permute-done | bytes 344096 | tf_op jit(solution)/shard_map/ppermute | solution.py:1113
  464.4 3.5 finish.6
  469.3 5.2 %finish.7 = (f32[192,2240]{1,0:T(8,128)}, f32[192,128]{1,0:T(8,128)S(1)}, f32[8,128]{1,0:T(8,128)}) custom-call(bf16[384,1536]{1,0:T(8,128)(2,1)S(1)} %copy-done.45, bf16[384,1536]{1,0:T(8,128)(2,1)S(1)} %copy-done.47, bf16[192,1536]{1,0:T(8,128)(2,1)S(1)} %copy-done.71, bf16[384,768]{1,0:T(8,128)(2,1)S(1)} %get-tuple-element.239.refs_0_.refs_3_, ...), custom_call_target="tpu_custom_call" | custom-call | bytes 6021 | tf_op jit(solution)/shard_map/finish/pallas_call | solution.py:92
  478.6 4.8 collective-permute-done.50
  (377 shorter events, 153.3 us)
Async XLA Ops:
  7.2 272.2 %reduce-scatter.3.cloned.1.call-start = ((), (), s32[]{:S(2)}) async-start(), calls=%async_computation.2 | async-start | bytes 3932160 | tf_op jit(solution)/shard_map/reduce_scatter | solution.py:1128
  23.4 11.1 %collective-permute-start.1 = (bf16[2,512,128]{2,1,0:T(8,128)(2,1)S(1)}, bf16[2,512,128]{2,1,0:T(8,128)(2,1)}, u32[]{:S(2)}, u32[]{:S(2)}) collective-permute-start(bf16[2,512,128]{2,1,0:T(8,128)(2,1)S(1)} %bitcast.77), channel_id=1, source_target_pairs={{0,4},{4,8},{8,12},{1,5},{5,9},{9,13},{2,6},{6,10},{10,14},{3,7},{... | collective-permute-start | bytes 786440 | tf_op jit(solution)/shard_map/ppermute | solution.py:66
  29.1 9.8 %collective-permute-start = (bf16[2,512,128]{2,1,0:T(8,128)(2,1)S(1)}, bf16[2,512,128]{2,1,0:T(8,128)(2,1)}, u32[]{:S(2)}, u32[]{:S(2)}) collective-permute-start(bf16[2,512,128]{2,1,0:T(8,128)(2,1)S(1)} %bitcast.78), channel_id=1, source_target_pairs={{0,8},{4,12},{1,9},{5,13},{2,10},{6,14},{3,11},{7,15},{16,24},{20,... | collective-permute-start | bytes 786440 | tf_op jit(solution)/shard_map/ppermute | solution.py:66
  33.5 5.4 %collective-permute-start.4 = (bf16[2,512,128]{2,1,0:T(8,128)(2,1)S(1)}, bf16[2,512,128]{2,1,0:T(8,128)(2,1)}, u32[]{:S(2)}, u32[]{:S(2)}) collective-permute-start(bf16[2,512,128]{2,1,0:T(8,128)(2,1)S(1)} %bitcast.79), channel_id=1, source_target_pairs={{0,1},{1,0},{2,3},{3,2},{4,5},{5,4},{6,7},{7,6},{8,9},{9,8},{10,11... | collective-permute-start | bytes 786440 | tf_op jit(solution)/shard_map/ppermute | solution.py:48
  34.5 4.5 collective-permute-start.3
  50.3 3.3 collective-permute-start.6
  57.0 37.4 %collective-permute-start.7 = (bf16[256,1536]{1,0:T(8,128)(2,1)}, bf16[256,1536]{1,0:T(8,128)(2,1)}, u32[]{:S(2)}, u32[]{:S(2)}) collective-permute-start(bf16[256,1536]{1,0:T(8,128)(2,1)} %get-tuple-element.142.refs_3_), channel_id=1, source_target_pairs={{0,2},{1,3},{2,0},{3,1},{4,6},{5,7},{6,4},{7,5},{8,10},{9,11},{10,... | collective-permute-start | bytes 2359304 | tf_op jit(solution)/shard_map/ppermute | solution.py:52
  58.5 35.9 %collective-permute-start.8 = (bf16[256,1536]{1,0:T(8,128)(2,1)}, bf16[256,1536]{1,0:T(8,128)(2,1)}, u32[]{:S(2)}, u32[]{:S(2)}) collective-permute-start(bf16[256,1536]{1,0:T(8,128)(2,1)} %get-tuple-element.143.refs_4_), channel_id=1, source_target_pairs={{0,2},{1,3},{2,0},{3,1},{4,6},{5,7},{6,4},{7,5},{8,10},{9,11},{10,... | collective-permute-start | bytes 2359304 | tf_op jit(solution)/shard_map/ppermute | solution.py:52
  98.3 3.4 collective-permute-start.10
  135.2 317.0 %reduce-scatter.5.cloned.1.call-start = ((), (), s32[]{:S(2)}) async-start(), calls=%async_computation.3 | async-start | bytes 4423680 | tf_op jit(solution)/shard_map/reduce_scatter | solution.py:1148
  143.9 54.3 %collective-permute-start.15 = (bf16[768,1280]{1,0:T(8,128)(2,1)}, bf16[768,1280]{1,0:T(8,128)(2,1)}, u32[]{:S(2)}, u32[]{:S(2)}) collective-permute-start(bf16[768,1280]{1,0:T(8,128)(2,1)} %get-tuple-element.167), channel_id=1, source_target_pairs={{0,16},{16,0},{1,17},{17,1},{2,18},{18,2},{3,19},{19,3},{4,20},{20... | collective-permute-start | bytes 5898248 | tf_op jit(solution)/shard_map/ppermute | solution.py:1103
  161.1 3.4 collective-permute-start.12
  178.7 29.7 %collective-permute-start.13 = (bf16[256,1536]{1,0:T(8,128)(2,1)}, bf16[256,1536]{1,0:T(8,128)(2,1)S(1)}, u32[]{:S(2)}, u32[]{:S(2)}) collective-permute-start(bf16[256,1536]{1,0:T(8,128)(2,1)} %get-tuple-element.165.refs_4_), channel_id=1, source_target_pairs={{0,2},{1,3},{2,0},{3,1},{4,6},{5,7},{6,4},{7,5},{8,10},{9,11},{10,... | collective-permute-start | bytes 2359304 | tf_op jit(solution)/shard_map/ppermute | solution.py:52
  180.2 35.3 %collective-permute-start.14 = (bf16[256,1536]{1,0:T(8,128)(2,1)}, bf16[256,1536]{1,0:T(8,128)(2,1)}, u32[]{:S(2)}, u32[]{:S(2)}) collective-permute-start(bf16[256,1536]{1,0:T(8,128)(2,1)} %get-tuple-element.166.refs_5_), channel_id=1, source_target_pairs={{0,2},{1,3},{2,0},{3,1},{4,6},{5,7},{6,4},{7,5},{8,10},{9,11},{10,... | collective-permute-start | bytes 2359304 | tf_op jit(solution)/shard_map/ppermute | solution.py:52
  197.6 90.5 %collective-permute-start.24 = (bf16[768,2304]{1,0:T(8,128)(2,1)}, bf16[768,2304]{1,0:T(8,128)(2,1)}, u32[]{:S(2)}, u32[]{:S(2)}) collective-permute-start(bf16[768,2304]{1,0:T(8,128)(2,1)} %get-tuple-element.199), channel_id=1, source_target_pairs={{0,16},{16,0},{1,17},{17,1},{2,18},{18,2},{3,19},{19,3},{4,20},{20... | collective-permute-start | bytes 10616840 | tf_op jit(solution)/shard_map/ppermute | solution.py:1103
  219.6 9.7 %collective-permute-start.16 = (bf16[256,1536]{1,0:T(8,128)(2,1)S(1)}, bf16[256,1536]{1,0:T(8,128)(2,1)S(1)}, u32[]{:S(2)}, u32[]{:S(2)}) collective-permute-start(bf16[256,1536]{1,0:T(8,128)(2,1)S(1)} %get-tuple-element.173.refs_1_.refs_0_), channel_id=1, source_target_pairs={{0,1},{1,0},{2,3},{3,2},{4,5},{5,4},{6,7},{7,6},{8,9},{9,8},{10,11... | collective-permute-start | bytes 2359304 | tf_op jit(solution)/shard_map/ppermute | solution.py:48
  219.7 9.6 %collective-permute-start.17 = (bf16[256,1536]{1,0:T(8,128)(2,1)S(1)}, bf16[256,1536]{1,0:T(8,128)(2,1)S(1)}, u32[]{:S(2)}, u32[]{:S(2)}) collective-permute-start(bf16[256,1536]{1,0:T(8,128)(2,1)S(1)} %get-tuple-element.174.refs_2_.refs_1_), channel_id=1, source_target_pairs={{0,1},{1,0},{2,3},{3,2},{4,5},{5,4},{6,7},{7,6},{8,9},{9,8},{10,11... | collective-permute-start | bytes 2359304 | tf_op jit(solution)/shard_map/ppermute | solution.py:48
  220.2 31.1 %collective-permute-start.19 = (bf16[384,1280]{1,0:T(8,128)(2,1)S(1)}, bf16[384,1280]{1,0:T(8,128)(2,1)S(1)}, u32[]{:S(2)}, u32[]{:S(2)}) collective-permute-start(bf16[384,1280]{1,0:T(8,128)(2,1)S(1)} %get-tuple-element.182), channel_id=1, source_target_pairs={{0,4},{4,0},{8,12},{12,8},{1,5},{5,1},{9,13},{13,9},{2,6},{6,2},{1... | collective-permute-start | bytes 2949128 | tf_op jit(solution)/shard_map/ppermute | solution.py:1108
  240.2 12.9 %collective-permute-start.18 = (bf16[2,1536,128]{2,1,0:T(8,128)(2,1)S(1)}, bf16[2,1536,128]{2,1,0:T(8,128)(2,1)S(1)}, u32[]{:S(2)}, u32[]{:S(2)}) collective-permute-start(bf16[2,1536,128]{2,1,0:T(8,128)(2,1)S(1)} %get-tuple-element.180), channel_id=1, source_target_pairs={{0,1},{1,0},{2,3},{3,2},{4,5},{5,4},{6,7},{7,6},{8,9},{9,8},{10,11... | collective-permute-start | bytes 2359304 | tf_op jit(solution)/shard_map/ppermute | solution.py:48
  253.3 9.8 %collective-permute-start.22 = (bf16[2,512,128]{2,1,0:T(8,128)(2,1)S(1)}, bf16[2,512,128]{2,1,0:T(8,128)(2,1)S(1)}, u32[]{:S(2)}, u32[]{:S(2)}) collective-permute-start(bf16[2,512,128]{2,1,0:T(8,128)(2,1)S(1)} %get-tuple-element.194), channel_id=1, source_target_pairs={{4,0},{8,4},{12,8},{5,1},{9,5},{13,9},{6,2},{10,6},{14,10},{7,3},{... | collective-permute-start | bytes 786440 | tf_op jit(solution)/shard_map/ppermute | solution.py:66
  263.1 11.6 %collective-permute-start.23 = (bf16[2,512,128]{2,1,0:T(8,128)(2,1)S(1)}, bf16[2,512,128]{2,1,0:T(8,128)(2,1)S(1)}, u32[]{:S(2)}, u32[]{:S(2)}) collective-permute-start(bf16[2,512,128]{2,1,0:T(8,128)(2,1)S(1)} %get-tuple-element.196), channel_id=1, source_target_pairs={{4,0},{8,4},{12,8},{5,1},{9,5},{13,9},{6,2},{10,6},{14,10},{7,3},{... | collective-permute-start | bytes 786440 | tf_op jit(solution)/shard_map/ppermute | solution.py:66
  278.8 2.6 collective-permute-start.25
  278.8 3.7 collective-permute-start.26
  301.4 54.5 %collective-permute-start.33 = (bf16[768,1536]{1,0:T(8,128)(2,1)}, bf16[768,1536]{1,0:T(8,128)(2,1)}, u32[]{:S(2)}, u32[]{:S(2)}) collective-permute-start(bf16[768,1536]{1,0:T(8,128)(2,1)} %copy-done.82), channel_id=1, source_target_pairs={{0,16},{16,0},{1,17},{17,1},{2,18},{18,2},{3,19},{19,3},{4,20},{20... | collective-permute-start | bytes 7077896 | tf_op jit(solution)/shard_map/ppermute | solution.py:1103
  301.5 12.5 %collective-permute-start.20 = (bf16[256,1536]{1,0:T(8,128)(2,1)}, bf16[256,1536]{1,0:T(8,128)(2,1)S(1)}, u32[]{:S(2)}, u32[]{:S(2)}) collective-permute-start(bf16[256,1536]{1,0:T(8,128)(2,1)} %copy-done.84), channel_id=1, source_target_pairs={{0,1},{1,0},{2,3},{3,2},{4,5},{5,4},{6,7},{7,6},{8,9},{9,8},{10,11... | collective-permute-start | bytes 2359304 | tf_op jit(solution)/shard_map/ppermute | solution.py:48
  301.7 12.3 %collective-permute-start.21 = (bf16[256,1536]{1,0:T(8,128)(2,1)}, bf16[256,1536]{1,0:T(8,128)(2,1)S(1)}, u32[]{:S(2)}, u32[]{:S(2)}) collective-permute-start(bf16[256,1536]{1,0:T(8,128)(2,1)} %copy-done.83), channel_id=1, source_target_pairs={{0,1},{1,0},{2,3},{3,2},{4,5},{5,4},{6,7},{7,6},{8,9},{9,8},{10,11... | collective-permute-start | bytes 2359304 | tf_op jit(solution)/shard_map/ppermute | solution.py:48
  302.6 20.6 %collective-permute-start.29 = (bf16[256,1536]{1,0:T(8,128)(2,1)S(1)}, bf16[256,1536]{1,0:T(8,128)(2,1)S(1)}, u32[]{:S(2)}, u32[]{:S(2)}) collective-permute-start(bf16[256,1536]{1,0:T(8,128)(2,1)S(1)} %copy-done.77), channel_id=1, source_target_pairs={{0,2},{1,3},{2,0},{3,1},{4,6},{5,7},{6,4},{7,5},{8,10},{9,11},{10,... | collective-permute-start | bytes 2359304 | tf_op jit(solution)/shard_map/ppermute | solution.py:52
  304.1 34.9 %collective-permute-start.30 = (bf16[256,1536]{1,0:T(8,128)(2,1)}, bf16[256,1536]{1,0:T(8,128)(2,1)S(1)}, u32[]{:S(2)}, u32[]{:S(2)}) collective-permute-start(bf16[256,1536]{1,0:T(8,128)(2,1)} %copy-done.78), channel_id=1, source_target_pairs={{0,2},{1,3},{2,0},{3,1},{4,6},{5,7},{6,4},{7,5},{8,10},{9,11},{10,... | collective-permute-start | bytes 2359304 | tf_op jit(solution)/shard_map/ppermute | solution.py:52
  343.2 21.3 %collective-permute-start.31 = (f32[256,1536]{1,0:T(8,128)S(1)}, f32[256,1536]{1,0:T(8,128)S(1)}, u32[]{:S(2)}, u32[]{:S(2)}) collective-permute-start(f32[256,1536]{1,0:T(8,128)S(1)} %get-tuple-element.214.refs_1_), channel_id=1, source_target_pairs={{0,1},{1,0},{2,3},{3,2},{4,5},{5,4},{6,7},{7,6},{8,9},{9,8},{10,11... | collective-permute-start | bytes 4718600 | tf_op jit(solution)/shard_map/ppermute | solution.py:48
  343.2 22.9 %collective-permute-start.32 = (f32[256,1536]{1,0:T(8,128)S(1)}, f32[256,1536]{1,0:T(8,128)S(1)}, u32[]{:S(2)}, u32[]{:S(2)}) collective-permute-start(f32[256,1536]{1,0:T(8,128)S(1)} %get-tuple-element.215.refs_2_), channel_id=1, source_target_pairs={{0,1},{1,0},{2,3},{3,2},{4,5},{5,4},{6,7},{7,6},{8,9},{9,8},{10,11... | collective-permute-start | bytes 4718600 | tf_op jit(solution)/shard_map/ppermute | solution.py:48
  343.7 43.8 %collective-permute-start.36 = (bf16[768,896]{1,0:T(8,128)(2,1)}, bf16[768,896]{1,0:T(8,128)(2,1)S(1)}, u32[]{:S(2)}, u32[]{:S(2)}) collective-permute-start(bf16[768,896]{1,0:T(8,128)(2,1)} %get-tuple-element.222), channel_id=1, source_target_pairs={{0,16},{16,0},{1,17},{17,1},{2,18},{18,2},{3,19},{19,3},{4,20},{20... | collective-permute-start | bytes 4128776 | tf_op jit(solution)/shard_map/ppermute | solution.py:1103
  345.1 24.4 %collective-permute-start.27 = (bf16[256,1536]{1,0:T(8,128)(2,1)}, bf16[256,1536]{1,0:T(8,128)(2,1)S(1)}, u32[]{:S(2)}, u32[]{:S(2)}) collective-permute-start(bf16[256,1536]{1,0:T(8,128)(2,1)} %get-tuple-element.208.refs_1_), channel_id=1, source_target_pairs={{0,2},{1,3},{2,0},{3,1},{4,6},{5,7},{6,4},{7,5},{8,10},{9,11},{10,... | collective-permute-start | bytes 2359304 | tf_op jit(solution)/shard_map/ppermute | solution.py:52
  355.9 25.5 %collective-permute-start.28 = (bf16[256,1536]{1,0:T(8,128)(2,1)}, bf16[256,1536]{1,0:T(8,128)(2,1)S(1)}, u32[]{:S(2)}, u32[]{:S(2)}) collective-permute-start(bf16[256,1536]{1,0:T(8,128)(2,1)} %get-tuple-element.209.refs_2_), channel_id=1, source_target_pairs={{0,2},{1,3},{2,0},{3,1},{4,6},{5,7},{6,4},{7,5},{8,10},{9,11},{10,... | collective-permute-start | bytes 2359304 | tf_op jit(solution)/shard_map/ppermute | solution.py:52
  364.5 33.8 %collective-permute-start.39 = (bf16[384,1536]{1,0:T(8,128)(2,1)}, bf16[384,1536]{1,0:T(8,128)(2,1)S(1)}, u32[]{:S(2)}, u32[]{:S(2)}) collective-permute-start(bf16[384,1536]{1,0:T(8,128)(2,1)} %get-tuple-element.231), channel_id=1, source_target_pairs={{0,4},{4,0},{8,12},{12,8},{1,5},{5,1},{9,13},{13,9},{2,6},{6,2},{1... | collective-permute-start | bytes 3538952 | tf_op jit(solution)/shard_map/ppermute | solution.py:1108
  366.2 43.6 %collective-permute-start.38 = (bf16[768,768]{1,0:T(8,128)(2,1)}, bf16[768,768]{1,0:T(8,128)(2,1)S(1)}, u32[]{:S(2)}, u32[]{:S(2)}) collective-permute-start(bf16[768,768]{1,0:T(8,128)(2,1)} %get-tuple-element.229), channel_id=1, source_target_pairs={{0,16},{16,0},{1,17},{17,1},{2,18},{18,2},{3,19},{19,3},{4,20},{20... | collective-permute-start | bytes 3538952 | tf_op jit(solution)/shard_map/ppermute | solution.py:1103
  387.0 9.0 %collective-permute-start.34 = (bf16[256,1536]{1,0:T(8,128)(2,1)S(1)}, bf16[256,1536]{1,0:T(8,128)(2,1)S(1)}, u32[]{:S(2)}, u32[]{:S(2)}) collective-permute-start(bf16[256,1536]{1,0:T(8,128)(2,1)S(1)} %get-tuple-element.220.refs_1_), channel_id=1, source_target_pairs={{0,1},{1,0},{2,3},{3,2},{4,5},{5,4},{6,7},{7,6},{8,9},{9,8},{10,11... | collective-permute-start | bytes 2359304 | tf_op jit(solution)/shard_map/ppermute | solution.py:48
  387.1 9.0 %collective-permute-start.35 = (bf16[256,1536]{1,0:T(8,128)(2,1)S(1)}, bf16[256,1536]{1,0:T(8,128)(2,1)S(1)}, u32[]{:S(2)}, u32[]{:S(2)}) collective-permute-start(bf16[256,1536]{1,0:T(8,128)(2,1)S(1)} %get-tuple-element.221.refs_2_), channel_id=1, source_target_pairs={{0,1},{1,0},{2,3},{3,2},{4,5},{5,4},{6,7},{7,6},{8,9},{9,8},{10,11... | collective-permute-start | bytes 2359304 | tf_op jit(solution)/shard_map/ppermute | solution.py:48
  387.6 25.6 %collective-permute-start.40 = (bf16[192,1280]{1,0:T(8,128)(2,1)S(1)}, bf16[192,1280]{1,0:T(8,128)(2,1)S(1)}, u32[]{:S(2)}, u32[]{:S(2)}) collective-permute-start(bf16[192,1280]{1,0:T(8,128)(2,1)S(1)} %copy-done.86), channel_id=1, source_target_pairs={{0,8},{4,12},{8,0},{12,4},{1,9},{5,13},{9,1},{13,5},{2,10},{6,14},... | collective-permute-start | bytes 1474568 | tf_op jit(solution)/shard_map/ppermute | solution.py:1113
  395.9 33.1 %collective-permute-start.37 = (bf16[384,896]{1,0:T(8,128)(2,1)S(1)}, bf16[384,896]{1,0:T(8,128)(2,1)S(1)}, u32[]{:S(2)}, u32[]{:S(2)}) collective-permute-start(bf16[384,896]{1,0:T(8,128)(2,1)S(1)} %get-tuple-element.228), channel_id=1, source_target_pairs={{0,4},{4,0},{8,12},{12,8},{1,5},{5,1},{9,13},{13,9},{2,6},{6,2},{1... | collective-permute-start | bytes 2064392 | tf_op jit(solution)/shard_map/ppermute | solution.py:1108
  398.4 39.3 %collective-permute-start.42 = (bf16[192,1536]{1,0:T(8,128)(2,1)S(1)}, bf16[192,1536]{1,0:T(8,128)(2,1)S(1)}, u32[]{:S(2)}, u32[]{:S(2)}) collective-permute-start(bf16[192,1536]{1,0:T(8,128)(2,1)S(1)} %get-tuple-element.236), channel_id=1, source_target_pairs={{0,8},{4,12},{8,0},{12,4},{1,9},{5,13},{9,1},{13,5},{2,10},{6,14},... | collective-permute-start | bytes 1769480 | tf_op jit(solution)/shard_map/ppermute | solution.py:1113
  416.0 33.3 %collective-permute-start.44 = (bf16[384,768]{1,0:T(8,128)(2,1)S(1)}, bf16[384,768]{1,0:T(8,128)(2,1)S(1)}, u32[]{:S(2)}, u32[]{:S(2)}) collective-permute-start(bf16[384,768]{1,0:T(8,128)(2,1)S(1)} %get-tuple-element.240), channel_id=1, source_target_pairs={{0,4},{4,0},{8,12},{12,8},{1,5},{5,1},{9,13},{13,9},{2,6},{6,2},{1... | collective-permute-start | bytes 1769480 | tf_op jit(solution)/shard_map/ppermute | solution.py:1108
  416.1 9.4 %collective-permute-start.41 = (bf16[192,1024]{1,0:T(8,128)(2,1)S(1)}, bf16[192,1024]{1,0:T(8,128)(2,1)S(1)}, u32[]{:S(2)}, u32[]{:S(2)}) collective-permute-start(bf16[192,1024]{1,0:T(8,128)(2,1)S(1)} %copy-done.74), channel_id=1, source_target_pairs={{0,16},{16,0},{1,17},{17,1},{2,18},{18,2},{3,19},{19,3},{4,20},{20... | collective-permute-start | bytes 1179656 | tf_op jit(solution)/shard_map/ppermute | solution.py:1135
  438.5 25.8 %collective-permute-start.43 = (bf16[192,896]{1,0:T(8,128)(2,1)}, bf16[192,896]{1,0:T(8,128)(2,1)}, u32[]{:S(2)}, u32[]{:S(2)}) collective-permute-start(bf16[192,896]{1,0:T(8,128)(2,1)} %get-tuple-element.237), channel_id=1, source_target_pairs={{0,8},{4,12},{8,0},{12,4},{1,9},{5,13},{9,1},{13,5},{2,10},{6,14},... | collective-permute-start | bytes 1032200 | tf_op jit(solution)/shard_map/ppermute | solution.py:1113
  438.5 4.5 collective-permute-start.45
  450.1 19.2 %collective-permute-start.48 = (bf16[192,768]{1,0:T(8,128)(2,1)}, bf16[192,768]{1,0:T(8,128)(2,1)}, u32[]{:S(2)}, u32[]{:S(2)}) collective-permute-start(bf16[192,768]{1,0:T(8,128)(2,1)} %get-tuple-element.252), channel_id=1, source_target_pairs={{0,8},{4,12},{8,0},{12,4},{1,9},{5,13},{9,1},{13,5},{2,10},{6,14},... | collective-permute-start | bytes 884744 | tf_op jit(solution)/shard_map/ppermute | solution.py:1113
  450.1 17.8 %collective-permute-start.46 = (f32[8,512]{1,0:T(8,128)S(1)}, f32[8,512]{1,0:T(8,128)S(1)}, u32[]{:S(2)}, u32[]{:S(2)}) collective-permute-start(f32[8,512]{1,0:T(8,128)S(1)} %get-tuple-element.248.refs_0_), channel_id=1, source_target_pairs={{0,4},{4,0},{8,12},{12,8},{1,5},{5,1},{9,13},{13,9},{2,6},{6,2},{1... | collective-permute-start | bytes 49160 | tf_op jit(solution)/shard_map/ppermute | solution.py:1241
  467.9 6.8 %collective-permute-start.47 = (f32[8,512]{1,0:T(8,128)S(1)}, f32[8,512]{1,0:T(8,128)S(1)}, u32[]{:S(2)}, u32[]{:S(2)}) collective-permute-start(f32[8,512]{1,0:T(8,128)S(1)} %get-tuple-element.250), channel_id=1, source_target_pairs={{0,8},{4,12},{8,0},{12,4},{1,9},{5,13},{9,1},{13,5},{2,10},{6,14},... | collective-permute-start | bytes 49160 | tf_op jit(solution)/shard_map/ppermute | solution.py:1248
  476.1 7.2 %collective-permute-start.50 = (f32[2,200,128]{2,1,0:T(8,128)S(1)}, f32[2,200,128]{2,1,0:T(8,128)S(1)}, u32[]{:S(2)}, u32[]{:S(2)}) collective-permute-start(f32[2,200,128]{2,1,0:T(8,128)S(1)} %maximum_select_fusion.1), channel_id=1, source_target_pairs={{0,2},{1,3},{2,0},{3,1},{4,6},{5,7},{6,4},{7,5},{8,10},{9,11},{10,... | collective-permute-start | bytes 614408 | tf_op jit(solution)/shard_map/ppermute | solution.py:52
  (110 other events, 1114.0 us)
Sparse Core Ops, SparseCore 0:
  135.3 71.6 reduce-scatter.2
  301.6 65.6 reduce-scatter.4

commit v12 on v11

--- a/solution.py
+++ b/solution.py
@@ -1080,7 +1080,7 @@
     units = gate_t.shape[0]
     tiles = -(-units // TILE)
     cut = (tiles + 1) // 2
-    long = -(-2 * tiles // 3)
+    long = max(tiles - 2, 1)
     one, two = seq_index ^ 1, seq_index ^ 2
     three = seq_index ^ 3
     quad = jnp.stack([one, three, seq_index, two])
@@ -1231,15 +1231,14 @@
     up_a.relay()
     down_a.settled()
     up_b.own()
-    down_b.settled()
-    up_a.settled()
     last.relay()
-    (down_grad,) = finish(order, [down_a.result(), down_b.result()], share, units, TILE)
     if near_pair:
         bias_come = lax.ppermute(bias_sum, "dp", flipped("dp", 0))
         bias_all = bias_add(order, bias_sum, bias_come)
         bias_come = lax.ppermute(bias_all, "seq", flipped("seq", 0))
+    up_a.settled()
     up_b.relay()
+    (down_grad,) = finish(order, [down_a.result(), down_b.result()], share, units, TILE)
     gate_grad, gate_term = finish(order, [gate.result()], share, units, TILE, gate_rows)
     wide_columns = grad_qkv.shape[1]
     (last_grad,) = finish(order, [last.result()], share, wide_columns + heads * HD, HD)

time: 496 us -> 515 us (1.038)
  waiting for transfers between devices: 136 us -> 149 us
    ppermute x4, waiting for transfers between devices: 17.8 us -> 28.7 us  [own(): self.come = lax.ppermute(send, 'seq', flipped('seq', 0))]
    ppermute x5, waiting for transfers between devices: 18.6 us -> 28.9 us  [__init__(): self.come = lax.ppermute(sent, 'dp', flipped('dp', 0))]
    ppermute x9, waiting for transfers between devices: 39.5 us -> 30.2 us  [chip_swap(): return lax.ppermute(value, 'tensor', flipped('tensor', 1))]
    ppermute x1, waiting for transfers between devices: 8.62 us -> 0.01 us  [across(): self.come = lax.ppermute(sent, 'dp', flipped('dp', 0))]
    ppermute x4, waiting for transfers between devices: 19.5 us -> 27.5 us  [relay(): self.last = lax.ppermute(sent, 'seq', flipped('seq', 1))]
    ppermute x4, starting transfers between devices: 11 us -> 17.4 us  [own(): self.come = lax.ppermute(send, 'seq', flipped('seq', 0))]
    unnamed x215 -> x225, local copies, waits for them, and re-layouts: 73.6 us -> 74.1 us
  transfers between devices with their start and end apart: 53 -> 53, of which waited for: 28 -> 26; matrix products, arithmetic and copies ran while one was open for 3% -> 3% of each run, Pallas kernels for 30% -> 28%
where the time goes in v12:
time: 515 us; the launch traced here: 512 us
  Pallas kernels  198 us (38%)
  waiting for transfers between devices  149 us (29%)
  local copies, waits for them, and re-layouts  84.3 us (16%)
  starting transfers between devices  55.5 us (11%)
  between operations  15.4 us (3%)
  other arithmetic  9.38 us (2%)
    pallas_call x44, Pallas kernels, __call__(): pl.pallas_call(run, grid_spec=pltpu.PrefetchScalarGridSpec(num_scalar_pre...  189 us
    unnamed x225, local copies, waits for them, and re-layouts  74.1 us
    ppermute x9, waiting for transfers between devices, chip_swap(): return lax.ppermute(value, 'tensor', flipped('tensor', 1))  30.2 us
    ppermute x5, waiting for transfers between devices, __init__(): self.come = lax.ppermute(sent, 'dp', flipped('dp', 0))  28.9 us
    ppermute x4, waiting for transfers between devices, own(): self.come = lax.ppermute(send, 'seq', flipped('seq', 0))  28.7 us
    ppermute x4, waiting for transfers between devices, relay(): self.last = lax.ppermute(sent, 'seq', flipped('seq', 1))  27.5 us
    ppermute x4, starting transfers between devices, own(): self.come = lax.ppermute(send, 'seq', flipped('seq', 0))  17.4 us
    ppermute x4, waiting for transfers between devices, shifted(): return lax.ppermute(value, 'seq', route)  15.2 us
  transfers between devices with their start and end apart: 53, of which 26 were waited for; matrix products, arithmetic and copies ran while one was open for 3% of the time, Pallas kernels for 28%

profile of v12, /device:TPU:0, one launch (start us, length us, event | category | flops | bytes accessed | tf_op | source)
XLA Modules:
  0.0 512.3 jit_solution(13317657604707209865)
XLA Ops:
  17.2 3.6 first.1
  23.4 5.6 %collective-permute-start.1 = (bf16[2,512,128]{2,1,0:T(8,128)(2,1)S(1)}, bf16[2,512,128]{2,1,0:T(8,128)(2,1)}, u32[]{:S(2)}, u32[]{:S(2)}) collective-permute-start(bf16[2,512,128]{2,1,0:T(8,128)(2,1)S(1)} %bitcast.77), channel_id=1, source_target_pairs={{0,4},{4,8},{8,12},{1,5},{5,9},{9,13},{2,6},{6,10},{10,14},{3,7},{... | collective-permute-start | bytes 786440 | tf_op jit(solution)/shard_map/ppermute | solution.py:66
  29.1 4.5 collective-permute-start
  34.6 4.3 collective-permute-done.refs_0_.refs_9_
  41.9 6.1 %attend.1 = (bf16[2,512,384]{2,1,0:T(8,128)(2,1)S(1)}, f32[2,2,768]{2,1,0:T(2,128)S(1)}) custom-call(s32[2,2]{1,0:T(2,128)S(1)} %shift-right-logical_maximum_fusion.low_ref.refs_0_, s32[1]{0:T(128)} %bitcast.core_ref.refs_0_.refs_1_, bf16[2,512,384]{2,1,0:T(8,128)(2,1)S(1)} %bitcast.74, s32[2,1,512]{2,1,0:T(1,128)S(1)} %sub.44.start_ref.refs_3_, ...), custom_call_target="tpu_custom_call" | custom-call | flops 8000000 | bytes 4194 | tf_op jit(solution)/shard_map/attend/pallas_call | solution.py:253
  53.6 3.4 narrow.9
  60.4 4.5 constant_dynamic-slice_fusion.2
  74.6 5.2 %copy-done.9 = bf16[1536,2240]{0,1:T(8,128)(2,1)S(1)} copy-done((bf16[1536,2240]{0,1:T(8,128)(2,1)S(1)}, bf16[1536,2240]{0,1:T(8,128)(2,1)}, u32[]{:S(2)}) %copy-start.9) | copy-done | bytes 6881304
  79.8 9.3 %grad_hidden.1 = (bf16[1024,2240]{1,0:T(8,128)(2,1)S(1)}, f32[8,128]{1,0:T(8,128)S(1)}) custom-call(bf16[1024,1536]{1,0:T(8,128)(2,1)S(1)} %get-tuple-element.146.refs_0_.refs_3_, bf16[2240,1536]{1,0:T(8,128)(2,1)S(1)} %bitcast.61, f32[8,128]{1,0:T(8,128)S(1)} %get-tuple-element.147.refs_2_, bf16[192,2240]{1,0:T(8,128)(2,1)S(1)} %copy-done.40, ...), custom_call_target="tpu_custom_call" | custom-call | flops 7046430 | bytes 15728 | tf_op jit(solution)/shard_map/grad_hidden/pallas_call | solution.py:92
  94.5 3.8 middle.1
  104.1 20.3 %gated.1 = (bf16[1024,2240]{1,0:T(8,128)(2,1)S(1)}, bf16[1024,2240]{1,0:T(8,128)(2,1)S(1)}, bf16[1024,2240]{1,0:T(8,128)(2,1)S(1)}, f32[8,128]{1,0:T(8,128)S(1)}) custom-call(bf16[1024,2240]{1,0:T(8,128)(2,1)S(1)} %copy-done.49, bf16[2240,1536]{1,0:T(8,128)(2,1)} %bitcast.58, bf16[2240,1536]{1,0:T(8,128)(2,1)} %bitcast.83, ...), custom_call_target="tpu_custom_call" | custom-call | flops 14092861 | bytes 31457 | tf_op jit(solution)/shard_map/gated/pallas_call | solution.py:92
  126.6 4.8 share.9
  139.8 4.2 share.10
  150.8 10.6 %narrow.10 = (bf16[256,1536]{1,0:T(8,128)(2,1)S(1)}, bf16[256,1536]{1,0:T(8,128)(2,1)S(1)}, f32[8,128]{1,0:T(8,128)S(1)}) custom-call(bf16[1024,2240]{1,0:T(8,128)(2,1)S(1)} %copy-done.5, bf16[2240,1536]{1,0:T(8,128)(2,1)S(1)} %bitcast.59, bf16[1024,2240]{1,0:T(8,128)(2,1)S(1)} %bitcast.47, bf16[2240,1536]{1,0:T(8,128)(2,1)} %bitcast.84, ...), custom_call_target="tpu_custom_call" | custom-call | flops 7046430 | bytes 19922 | tf_op jit(solution)/shard_map/narrow/pallas_call | solution.py:92
  164.9 3.1 copy-done.8
  168.0 11.1 %narrow.11 = (bf16[256,1536]{1,0:T(8,128)(2,1)}, bf16[256,1536]{1,0:T(8,128)(2,1)}, f32[8,128]{1,0:T(8,128)S(1)}) custom-call(bf16[1024,2240]{1,0:T(8,128)(2,1)S(1)} %bitcast.55, bf16[2240,1536]{1,0:T(8,128)(2,1)S(1)} %bitcast.60, bf16[1024,2240]{1,0:T(8,128)(2,1)S(1)} %bitcast.47, bf16[2240,1536]{1,0:T(8,128)(2,1)} %bitcast.85, ...), custom_call_target="tpu_custom_call" | custom-call | flops 7046430 | bytes 19922 | tf_op jit(solution)/shard_map/narrow/pallas_call | solution.py:92
  182.7 13.7 %share.11 = (bf16[768,2304]{1,0:T(8,128)(2,1)}, bf16[768,1792]{1,0:T(8,128)(2,1)S(1)}, bf16[768,512]{1,0:T(8,128)(2,1)S(1)}, f32[8,128]{1,0:T(8,128)S(1)}) custom-call(s32[1]{0:T(128)} %bitcast.10.refs_0_, s32[1]{0:T(128)} %constant.59.clone.1.refs_0_.refs_1_, bf16[1536,1024]{1,0:T(8,128)(2,1)S(1)} %get-tuple-element.169.refs_2_, ...), custom_call_target="tpu_custom_call" | custom-call | flops 7247757 | bytes 18087 | tf_op jit(solution)/shard_map/share/pallas_call | solution.py:92
  203.4 5.9 %share.12 = (bf16[384,1280]{1,0:T(8,128)(2,1)S(1)}, bf16[384,1280]{1,0:T(8,128)(2,1)S(1)}, f32[8,128]{1,0:T(8,128)S(1)}) custom-call(s32[1]{0:T(128)} %bitcast.11.refs_0_, s32[4]{0:T(128)S(1)} %pad_add_fusion.refs_1_, bf16[1536,1024]{1,0:T(8,128)(2,1)S(1)} %copy-done.18, bf16[1024,2240]{1,0:T(8,128)(2,1)S(1)} %copy-done.3, ...), custom_call_target="tpu_custom_call" | custom-call | flops 2013265 | bytes 6160 | tf_op jit(solution)/shard_map/share/pallas_call | solution.py:92
  209.3 6.6 %collective-permute-done.14.refs_7_ = bf16[256,1536]{1,0:T(8,128)(2,1)} collective-permute-done((bf16[256,1536]{1,0:T(8,128)(2,1)}, bf16[256,1536]{1,0:T(8,128)(2,1)}, u32[]{:S(2)}, u32[]{:S(2)}) %collective-permute-start.14) | collective-permute-done | bytes 786464 | tf_op jit(solution)/shard_map/ppermute | solution.py:52
  215.9 4.1 norm_back.2
  220.6 10.4 %collective-permute-start.19 = (bf16[384,1280]{1,0:T(8,128)(2,1)S(1)}, bf16[384,1280]{1,0:T(8,128)(2,1)S(1)}, u32[]{:S(2)}, u32[]{:S(2)}) collective-permute-start(bf16[384,1280]{1,0:T(8,128)(2,1)S(1)} %get-tuple-element.182), channel_id=1, source_target_pairs={{0,4},{4,0},{8,12},{12,8},{1,5},{5,1},{9,13},{13,9},{2,6},{6,2},{1... | collective-permute-start | bytes 2949128 | tf_op jit(solution)/shard_map/ppermute | solution.py:1108
  232.9 8.9 %attend_back.1 = (bf16[2,512,384]{2,1,0:T(8,128)(2,1)S(1)}, bf16[2,1536,128]{2,1,0:T(8,128)(2,1)S(1)}, bf16[2,1536,128]{2,1,0:T(8,128)(2,1)S(1)}, f32[8,128]{1,0:T(8,128)S(1)}) custom-call(s32[2,2]{1,0:T(2,128)S(1)} %shift-right-logical_maximum_fusion.low_ref.refs_0_, s32[1]{0:T(128)} %bitcast.core_ref.refs_0_.refs_1_, bf16[2,512,384]{2,1,0:T(8,128)(2,1)S(1)} %bitcast.75, ...), custom_call_target="tpu_custom_call" | custom-call | flops 20000000 | bytes 6291 | tf_op jit(solution)/shard_map/attend_back/pallas_call | solution.py:92
  245.0 7.9 %collective-permute-done.19.refs_1_ = bf16[384,1280]{1,0:T(8,128)(2,1)S(1)} collective-permute-done((bf16[384,1280]{1,0:T(8,128)(2,1)S(1)}, bf16[384,1280]{1,0:T(8,128)(2,1)S(1)}, u32[]{:S(2)}, u32[]{:S(2)}) %collective-permute-start.19) | collective-permute-done | bytes 983072 | tf_op jit(solution)/shard_map/ppermute | solution.py:1108
  256.3 5.3 %narrow.12 = (bf16[256,1536]{1,0:T(8,128)(2,1)S(1)}, bf16[256,1536]{1,0:T(8,128)(2,1)S(1)}, f32[8,128]{1,0:T(8,128)S(1)}) custom-call(bf16[1024,2240]{1,0:T(8,128)(2,1)S(1)} %bitcast.51, bf16[2240,1536]{1,0:T(8,128)(2,1)S(1)} %bitcast.64, f32[8,128]{1,0:T(8,128)S(1)} %get-tuple-element.186.refs_2_), custom_call_target="tpu_custom_call" | custom-call | flops 3523215 | bytes 10747 | tf_op jit(solution)/shard_map/narrow/pallas_call | solution.py:92
  266.4 7.7 %collective-permute-done.23.refs_5_ = bf16[2,512,128]{2,1,0:T(8,128)(2,1)S(1)} collective-permute-done((bf16[2,512,128]{2,1,0:T(8,128)(2,1)S(1)}, bf16[2,512,128]{2,1,0:T(8,128)(2,1)S(1)}, u32[]{:S(2)}, u32[]{:S(2)}) %collective-permute-start.23) | collective-permute-done | bytes 262176 | tf_op jit(solution)/shard_map/ppermute | solution.py:66
  274.7 3.4 narrow.13
  281.9 4.4 narrow.14
  290.4 8.3 %share.13 = (bf16[768,2304]{1,0:T(8,128)(2,1)S(1)}, f32[8,128]{1,0:T(8,128)S(1)}) custom-call(s32[1]{0:T(128)} %bitcast.11.refs_0_, s32[1]{0:T(128)} %constant.59.clone.1.refs_0_.refs_1_, bf16[1536,1024]{1,0:T(8,128)(2,1)S(1)} %copy-done.12, bf16[1024,2240]{1,0:T(8,128)(2,1)S(1)} %copy-done.6, bf16[768,2304]{1,0:T(8,128)(2,1)} %collective-permute-done.24.refs_4_, ...), custom_call_target="tpu_custom_call" | custom-call | flops 3623878 | bytes 9830 | tf_op jit(solution)/shard_map/share/pallas_call | solution.py:92
  307.9 5.3 %share.14 = (bf16[768,896]{1,0:T(8,128)(2,1)}, f32[8,128]{1,0:T(8,128)S(1)}) custom-call(s32[1]{0:T(128)} %bitcast.10.refs_0_, s32[1]{0:T(128)} %constant.59.clone.1.refs_0_.refs_1_, bf16[1536,1024]{1,0:T(8,128)(2,1)S(1)} %copy-done.24, bf16[1536,1024]{1,0:T(8,128)(2,1)S(1)} %copy-done.30, bf16[1024,512]{1,0:T(8,128)(2,1)S(1)} %get-tuple-element.198.refs_0_.refs_4_, ...), custom_call_target="tpu_custom_call" | custom-call | flops 1409286 | bytes 4784 | tf_op jit(solution)/shard_map/share/pallas_call | solution.py:92
  316.3 6.0 %narrow.15 = (bf16[256,1536]{1,0:T(8,128)(2,1)}, bf16[256,1536]{1,0:T(8,128)(2,1)}, f32[8,128]{1,0:T(8,128)S(1)}) custom-call(bf16[1024,2240]{1,0:T(8,128)(2,1)S(1)} %bitcast.53, bf16[2240,1536]{1,0:T(8,128)(2,1)S(1)} %bitcast.65, bf16[256,1536]{1,0:T(8,128)(2,1)S(1)} %collective-permute-done.20.refs_2_, ...), custom_call_target="tpu_custom_call" | custom-call | flops 3523215 | bytes 10747 | tf_op jit(solution)/shard_map/narrow/pallas_call | solution.py:92
  322.4 15.8 %collective-permute-done.30.refs_7_ = bf16[256,1536]{1,0:T(8,128)(2,1)S(1)} collective-permute-done((bf16[256,1536]{1,0:T(8,128)(2,1)}, bf16[256,1536]{1,0:T(8,128)(2,1)S(1)}, u32[]{:S(2)}, u32[]{:S(2)}) %collective-permute-start.30) | collective-permute-done | bytes 786464 | tf_op jit(solution)/shard_map/ppermute | solution.py:52
  344.9 17.8 %collective-permute-done.33.refs_4_ = bf16[768,1792]{1,0:T(8,128)(2,1)} collective-permute-done((bf16[768,1792]{1,0:T(8,128)(2,1)}, bf16[768,1792]{1,0:T(8,128)(2,1)}, u32[]{:S(2)}, u32[]{:S(2)}) %collective-permute-start.33) | collective-permute-done | bytes 2752544 | tf_op jit(solution)/shard_map/ppermute | solution.py:1103
  363.4 8.0 %share.15 = (bf16[384,1792]{1,0:T(8,128)(2,1)}, bf16[384,1792]{1,0:T(8,128)(2,1)S(1)}, f32[8,128]{1,0:T(8,128)S(1)}) custom-call(s32[1]{0:T(128)} %bitcast.11.refs_0_, s32[4]{0:T(128)S(1)} %pad_add_fusion.refs_1_, bf16[1536,1024]{1,0:T(8,128)(2,1)S(1)} %copy-done.13, bf16[1024,2240]{1,0:T(8,128)(2,1)S(1)} %bitcast.49, ...), custom_call_target="tpu_custom_call" | custom-call | flops 2818572 | bytes 7995 | tf_op jit(solution)/shard_map/share/pallas_call | solution.py:92
  373.1 3.3 place.2
  379.5 3.5 layer.1
  384.9 11.1 %collective-permute-done.36.refs_6_ = bf16[768,896]{1,0:T(8,128)(2,1)S(1)} collective-permute-done((bf16[768,896]{1,0:T(8,128)(2,1)}, bf16[768,896]{1,0:T(8,128)(2,1)S(1)}, u32[]{:S(2)}, u32[]{:S(2)}) %collective-permute-start.36) | collective-permute-done | bytes 1376288 | tf_op jit(solution)/shard_map/ppermute | solution.py:1103
  396.0 5.8 %share.16 = (bf16[384,896]{1,0:T(8,128)(2,1)S(1)}, bf16[384,896]{1,0:T(8,128)(2,1)S(1)}, f32[8,128]{1,0:T(8,128)S(1)}) custom-call(s32[1]{0:T(128)} %bitcast.11.refs_0_, s32[4]{0:T(128)S(1)} %pad_add_fusion.refs_1_, bf16[1536,1024]{1,0:T(8,128)(2,1)S(1)} %copy-done.25, bf16[1536,1024]{1,0:T(8,128)(2,1)S(1)} %copy-done.31, ...), custom_call_target="tpu_custom_call" | custom-call | flops 1409286 | bytes 4784 | tf_op jit(solution)/shard_map/share/pallas_call | solution.py:92
  406.7 11.4 %collective-permute-done.39.refs_1_ = bf16[384,1792]{1,0:T(8,128)(2,1)S(1)} collective-permute-done((bf16[384,1792]{1,0:T(8,128)(2,1)}, bf16[384,1792]{1,0:T(8,128)(2,1)S(1)}, u32[]{:S(2)}, u32[]{:S(2)}) %collective-permute-start.39) | collective-permute-done | bytes 1376288 | tf_op jit(solution)/shard_map/ppermute | solution.py:1108
  418.4 11.3 %collective-permute-done.40.refs_6_.refs_2_ = bf16[192,1280]{1,0:T(8,128)(2,1)S(1)} collective-permute-done((bf16[192,1280]{1,0:T(8,128)(2,1)S(1)}, bf16[192,1280]{1,0:T(8,128)(2,1)S(1)}, u32[]{:S(2)}, u32[]{:S(2)}) %collective-permute-start.40) | collective-permute-done | bytes 491552 | tf_op jit(solution)/shard_map/ppermute | solution.py:1113
  431.8 3.8 collective-permute-start.43
  438.5 5.1 collective-permute-done.44.refs_1_
  443.6 9.3 %collective-permute-done.43.refs_1_.refs_4_ = bf16[384,512]{1,0:T(8,128)(2,1)S(1)} collective-permute-done((bf16[384,512]{1,0:T(8,128)(2,1)S(1)}, bf16[384,512]{1,0:T(8,128)(2,1)S(1)}, u32[]{:S(2)}, u32[]{:S(2)}) %collective-permute-start.43) | collective-permute-done | bytes 393248 | tf_op jit(solution)/shard_map/ppermute | solution.py:1108
  452.9 16.1 %collective-permute-done.45.refs_3_.refs_2_ = bf16[192,1792]{1,0:T(8,128)(2,1)S(1)} collective-permute-done((bf16[192,1792]{1,0:T(8,128)(2,1)S(1)}, bf16[192,1792]{1,0:T(8,128)(2,1)S(1)}, u32[]{:S(2)}, u32[]{:S(2)}) %collective-permute-start.45) | collective-permute-done | bytes 688160 | tf_op jit(solution)/shard_map/ppermute | solution.py:1113
  472.7 3.8 finish.4
  478.9 3.7 finish.5
  482.7 3.5 finish.6
  488.8 4.0 finish.7
  496.8 4.8 collective-permute-done.50
  (387 shorter events, 152.3 us)
Async XLA Ops:
  7.2 271.5 %reduce-scatter.3.cloned.1.call-start = ((), (), s32[]{:S(2)}) async-start(), calls=%async_computation.2 | async-start | bytes 3932160 | tf_op jit(solution)/shard_map/reduce_scatter | solution.py:1128
  23.4 11.1 %collective-permute-start.1 = (bf16[2,512,128]{2,1,0:T(8,128)(2,1)S(1)}, bf16[2,512,128]{2,1,0:T(8,128)(2,1)}, u32[]{:S(2)}, u32[]{:S(2)}) collective-permute-start(bf16[2,512,128]{2,1,0:T(8,128)(2,1)S(1)} %bitcast.77), channel_id=1, source_target_pairs={{0,4},{4,8},{8,12},{1,5},{5,9},{9,13},{2,6},{6,10},{10,14},{3,7},{... | collective-permute-start | bytes 786440 | tf_op jit(solution)/shard_map/ppermute | solution.py:66
  29.1 9.8 %collective-permute-start = (bf16[2,512,128]{2,1,0:T(8,128)(2,1)S(1)}, bf16[2,512,128]{2,1,0:T(8,128)(2,1)}, u32[]{:S(2)}, u32[]{:S(2)}) collective-permute-start(bf16[2,512,128]{2,1,0:T(8,128)(2,1)S(1)} %bitcast.78), channel_id=1, source_target_pairs={{0,8},{4,12},{1,9},{5,13},{2,10},{6,14},{3,11},{7,15},{16,24},{20,... | collective-permute-start | bytes 786440 | tf_op jit(solution)/shard_map/ppermute | solution.py:66
  33.6 5.4 %collective-permute-start.4 = (bf16[2,512,128]{2,1,0:T(8,128)(2,1)S(1)}, bf16[2,512,128]{2,1,0:T(8,128)(2,1)}, u32[]{:S(2)}, u32[]{:S(2)}) collective-permute-start(bf16[2,512,128]{2,1,0:T(8,128)(2,1)S(1)} %bitcast.79), channel_id=1, source_target_pairs={{0,1},{1,0},{2,3},{3,2},{4,5},{5,4},{6,7},{7,6},{8,9},{9,8},{10,11... | collective-permute-start | bytes 786440 | tf_op jit(solution)/shard_map/ppermute | solution.py:48
  34.6 4.5 collective-permute-start.3
  50.3 3.3 collective-permute-start.6
  57.0 37.4 %collective-permute-start.7 = (bf16[256,1536]{1,0:T(8,128)(2,1)}, bf16[256,1536]{1,0:T(8,128)(2,1)}, u32[]{:S(2)}, u32[]{:S(2)}) collective-permute-start(bf16[256,1536]{1,0:T(8,128)(2,1)} %get-tuple-element.142.refs_3_), channel_id=1, source_target_pairs={{0,2},{1,3},{2,0},{3,1},{4,6},{5,7},{6,4},{7,5},{8,10},{9,11},{10,... | collective-permute-start | bytes 2359304 | tf_op jit(solution)/shard_map/ppermute | solution.py:52
  58.6 35.9 %collective-permute-start.8 = (bf16[256,1536]{1,0:T(8,128)(2,1)}, bf16[256,1536]{1,0:T(8,128)(2,1)}, u32[]{:S(2)}, u32[]{:S(2)}) collective-permute-start(bf16[256,1536]{1,0:T(8,128)(2,1)} %get-tuple-element.143.refs_4_), channel_id=1, source_target_pairs={{0,2},{1,3},{2,0},{3,1},{4,6},{5,7},{6,4},{7,5},{8,10},{9,11},{10,... | collective-permute-start | bytes 2359304 | tf_op jit(solution)/shard_map/ppermute | solution.py:52
  98.4 3.4 collective-permute-start.10
  135.2 341.8 %reduce-scatter.5.cloned.1.call-start = ((), (), s32[]{:S(2)}) async-start(), calls=%async_computation.3 | async-start | bytes 4423680 | tf_op jit(solution)/shard_map/reduce_scatter | solution.py:1148
  144.0 55.1 %collective-permute-start.15 = (bf16[768,1280]{1,0:T(8,128)(2,1)}, bf16[768,1280]{1,0:T(8,128)(2,1)}, u32[]{:S(2)}, u32[]{:S(2)}) collective-permute-start(bf16[768,1280]{1,0:T(8,128)(2,1)} %get-tuple-element.167), channel_id=1, source_target_pairs={{0,16},{16,0},{1,17},{17,1},{2,18},{18,2},{3,19},{19,3},{4,20},{20... | collective-permute-start | bytes 5898248 | tf_op jit(solution)/shard_map/ppermute | solution.py:1103
  161.5 3.4 collective-permute-start.12
  179.1 30.2 %collective-permute-start.13 = (bf16[256,1536]{1,0:T(8,128)(2,1)}, bf16[256,1536]{1,0:T(8,128)(2,1)S(1)}, u32[]{:S(2)}, u32[]{:S(2)}) collective-permute-start(bf16[256,1536]{1,0:T(8,128)(2,1)} %get-tuple-element.165.refs_4_), channel_id=1, source_target_pairs={{0,2},{1,3},{2,0},{3,1},{4,6},{5,7},{6,4},{7,5},{8,10},{9,11},{10,... | collective-permute-start | bytes 2359304 | tf_op jit(solution)/shard_map/ppermute | solution.py:52
  180.6 35.3 %collective-permute-start.14 = (bf16[256,1536]{1,0:T(8,128)(2,1)}, bf16[256,1536]{1,0:T(8,128)(2,1)}, u32[]{:S(2)}, u32[]{:S(2)}) collective-permute-start(bf16[256,1536]{1,0:T(8,128)(2,1)} %get-tuple-element.166.refs_5_), channel_id=1, source_target_pairs={{0,2},{1,3},{2,0},{3,1},{4,6},{5,7},{6,4},{7,5},{8,10},{9,11},{10,... | collective-permute-start | bytes 2359304 | tf_op jit(solution)/shard_map/ppermute | solution.py:52
  198.9 88.3 %collective-permute-start.24 = (bf16[768,2304]{1,0:T(8,128)(2,1)}, bf16[768,2304]{1,0:T(8,128)(2,1)}, u32[]{:S(2)}, u32[]{:S(2)}) collective-permute-start(bf16[768,2304]{1,0:T(8,128)(2,1)} %get-tuple-element.199), channel_id=1, source_target_pairs={{0,16},{16,0},{1,17},{17,1},{2,18},{18,2},{3,19},{19,3},{4,20},{20... | collective-permute-start | bytes 10616840 | tf_op jit(solution)/shard_map/ppermute | solution.py:1103
  220.0 10.9 %collective-permute-start.16 = (bf16[256,1536]{1,0:T(8,128)(2,1)S(1)}, bf16[256,1536]{1,0:T(8,128)(2,1)S(1)}, u32[]{:S(2)}, u32[]{:S(2)}) collective-permute-start(bf16[256,1536]{1,0:T(8,128)(2,1)S(1)} %get-tuple-element.173.refs_1_.refs_0_), channel_id=1, source_target_pairs={{0,1},{1,0},{2,3},{3,2},{4,5},{5,4},{6,7},{7,6},{8,9},{9,8},{10,11... | collective-permute-start | bytes 2359304 | tf_op jit(solution)/shard_map/ppermute | solution.py:48
  220.1 10.9 %collective-permute-start.17 = (bf16[256,1536]{1,0:T(8,128)(2,1)S(1)}, bf16[256,1536]{1,0:T(8,128)(2,1)S(1)}, u32[]{:S(2)}, u32[]{:S(2)}) collective-permute-start(bf16[256,1536]{1,0:T(8,128)(2,1)S(1)} %get-tuple-element.174.refs_2_.refs_1_), channel_id=1, source_target_pairs={{0,1},{1,0},{2,3},{3,2},{4,5},{5,4},{6,7},{7,6},{8,9},{9,8},{10,11... | collective-permute-start | bytes 2359304 | tf_op jit(solution)/shard_map/ppermute | solution.py:48
  220.6 32.4 %collective-permute-start.19 = (bf16[384,1280]{1,0:T(8,128)(2,1)S(1)}, bf16[384,1280]{1,0:T(8,128)(2,1)S(1)}, u32[]{:S(2)}, u32[]{:S(2)}) collective-permute-start(bf16[384,1280]{1,0:T(8,128)(2,1)S(1)} %get-tuple-element.182), channel_id=1, source_target_pairs={{0,4},{4,0},{8,12},{12,8},{1,5},{5,1},{9,13},{13,9},{2,6},{6,2},{1... | collective-permute-start | bytes 2949128 | tf_op jit(solution)/shard_map/ppermute | solution.py:1108
  241.8 12.9 %collective-permute-start.18 = (bf16[2,1536,128]{2,1,0:T(8,128)(2,1)S(1)}, bf16[2,1536,128]{2,1,0:T(8,128)(2,1)S(1)}, u32[]{:S(2)}, u32[]{:S(2)}) collective-permute-start(bf16[2,1536,128]{2,1,0:T(8,128)(2,1)S(1)} %get-tuple-element.180), channel_id=1, source_target_pairs={{0,1},{1,0},{2,3},{3,2},{4,5},{5,4},{6,7},{7,6},{8,9},{9,8},{10,11... | collective-permute-start | bytes 2359304 | tf_op jit(solution)/shard_map/ppermute | solution.py:48
  254.9 9.8 %collective-permute-start.22 = (bf16[2,512,128]{2,1,0:T(8,128)(2,1)S(1)}, bf16[2,512,128]{2,1,0:T(8,128)(2,1)S(1)}, u32[]{:S(2)}, u32[]{:S(2)}) collective-permute-start(bf16[2,512,128]{2,1,0:T(8,128)(2,1)S(1)} %get-tuple-element.194), channel_id=1, source_target_pairs={{4,0},{8,4},{12,8},{5,1},{9,5},{13,9},{6,2},{10,6},{14,10},{7,3},{... | collective-permute-start | bytes 786440 | tf_op jit(solution)/shard_map/ppermute | solution.py:66
  264.8 9.2 %collective-permute-start.23 = (bf16[2,512,128]{2,1,0:T(8,128)(2,1)S(1)}, bf16[2,512,128]{2,1,0:T(8,128)(2,1)S(1)}, u32[]{:S(2)}, u32[]{:S(2)}) collective-permute-start(bf16[2,512,128]{2,1,0:T(8,128)(2,1)S(1)} %get-tuple-element.196), channel_id=1, source_target_pairs={{4,0},{8,4},{12,8},{5,1},{9,5},{13,9},{6,2},{10,6},{14,10},{7,3},{... | collective-permute-start | bytes 786440 | tf_op jit(solution)/shard_map/ppermute | solution.py:66
  278.1 2.6 collective-permute-start.25
  278.1 3.7 collective-permute-start.26
  300.6 62.1 %collective-permute-start.33 = (bf16[768,1792]{1,0:T(8,128)(2,1)}, bf16[768,1792]{1,0:T(8,128)(2,1)}, u32[]{:S(2)}, u32[]{:S(2)}) collective-permute-start(bf16[768,1792]{1,0:T(8,128)(2,1)} %copy-done.84), channel_id=1, source_target_pairs={{0,16},{16,0},{1,17},{17,1},{2,18},{18,2},{3,19},{19,3},{4,20},{20... | collective-permute-start | bytes 8257544 | tf_op jit(solution)/shard_map/ppermute | solution.py:1103
  301.3 11.9 %collective-permute-start.20 = (bf16[256,1536]{1,0:T(8,128)(2,1)}, bf16[256,1536]{1,0:T(8,128)(2,1)S(1)}, u32[]{:S(2)}, u32[]{:S(2)}) collective-permute-start(bf16[256,1536]{1,0:T(8,128)(2,1)} %copy-done.88), channel_id=1, source_target_pairs={{0,1},{1,0},{2,3},{3,2},{4,5},{5,4},{6,7},{7,6},{8,9},{9,8},{10,11... | collective-permute-start | bytes 2359304 | tf_op jit(solution)/shard_map/ppermute | solution.py:48
  301.3 11.9 %collective-permute-start.21 = (bf16[256,1536]{1,0:T(8,128)(2,1)}, bf16[256,1536]{1,0:T(8,128)(2,1)S(1)}, u32[]{:S(2)}, u32[]{:S(2)}) collective-permute-start(bf16[256,1536]{1,0:T(8,128)(2,1)} %copy-done.87), channel_id=1, source_target_pairs={{0,1},{1,0},{2,3},{3,2},{4,5},{5,4},{6,7},{7,6},{8,9},{9,8},{10,11... | collective-permute-start | bytes 2359304 | tf_op jit(solution)/shard_map/ppermute | solution.py:48
  301.8 20.5 %collective-permute-start.29 = (bf16[256,1536]{1,0:T(8,128)(2,1)S(1)}, bf16[256,1536]{1,0:T(8,128)(2,1)S(1)}, u32[]{:S(2)}, u32[]{:S(2)}) collective-permute-start(bf16[256,1536]{1,0:T(8,128)(2,1)S(1)} %copy-done.79), channel_id=1, source_target_pairs={{0,2},{1,3},{2,0},{3,1},{4,6},{5,7},{6,4},{7,5},{8,10},{9,11},{10,... | collective-permute-start | bytes 2359304 | tf_op jit(solution)/shard_map/ppermute | solution.py:52
  303.2 34.9 %collective-permute-start.30 = (bf16[256,1536]{1,0:T(8,128)(2,1)}, bf16[256,1536]{1,0:T(8,128)(2,1)S(1)}, u32[]{:S(2)}, u32[]{:S(2)}) collective-permute-start(bf16[256,1536]{1,0:T(8,128)(2,1)} %copy-done.80), channel_id=1, source_target_pairs={{0,2},{1,3},{2,0},{3,1},{4,6},{5,7},{6,4},{7,5},{8,10},{9,11},{10,... | collective-permute-start | bytes 2359304 | tf_op jit(solution)/shard_map/ppermute | solution.py:52
  342.3 29.0 %collective-permute-start.31 = (f32[256,1536]{1,0:T(8,128)S(1)}, f32[256,1536]{1,0:T(8,128)S(1)}, u32[]{:S(2)}, u32[]{:S(2)}) collective-permute-start(f32[256,1536]{1,0:T(8,128)S(1)} %get-tuple-element.214.refs_1_), channel_id=1, source_target_pairs={{0,1},{1,0},{2,3},{3,2},{4,5},{5,4},{6,7},{7,6},{8,9},{9,8},{10,11... | collective-permute-start | bytes 4718600 | tf_op jit(solution)/shard_map/ppermute | solution.py:48
  342.4 30.7 %collective-permute-start.32 = (f32[256,1536]{1,0:T(8,128)S(1)}, f32[256,1536]{1,0:T(8,128)S(1)}, u32[]{:S(2)}, u32[]{:S(2)}) collective-permute-start(f32[256,1536]{1,0:T(8,128)S(1)} %get-tuple-element.215.refs_2_), channel_id=1, source_target_pairs={{0,1},{1,0},{2,3},{3,2},{4,5},{5,4},{6,7},{7,6},{8,9},{9,8},{10,11... | collective-permute-start | bytes 4718600 | tf_op jit(solution)/shard_map/ppermute | solution.py:48
  342.9 33.5 %collective-permute-start.27 = (bf16[256,1536]{1,0:T(8,128)(2,1)}, bf16[256,1536]{1,0:T(8,128)(2,1)S(1)}, u32[]{:S(2)}, u32[]{:S(2)}) collective-permute-start(bf16[256,1536]{1,0:T(8,128)(2,1)} %get-tuple-element.208.refs_1_), channel_id=1, source_target_pairs={{0,2},{1,3},{2,0},{3,1},{4,6},{5,7},{6,4},{7,5},{8,10},{9,11},{10,... | collective-permute-start | bytes 2359304 | tf_op jit(solution)/shard_map/ppermute | solution.py:52
  344.4 35.1 %collective-permute-start.28 = (bf16[256,1536]{1,0:T(8,128)(2,1)}, bf16[256,1536]{1,0:T(8,128)(2,1)S(1)}, u32[]{:S(2)}, u32[]{:S(2)}) collective-permute-start(bf16[256,1536]{1,0:T(8,128)(2,1)} %get-tuple-element.209.refs_2_), channel_id=1, source_target_pairs={{0,2},{1,3},{2,0},{3,1},{4,6},{5,7},{6,4},{7,5},{8,10},{9,11},{10,... | collective-permute-start | bytes 2359304 | tf_op jit(solution)/shard_map/ppermute | solution.py:52
  362.7 33.3 %collective-permute-start.36 = (bf16[768,896]{1,0:T(8,128)(2,1)}, bf16[768,896]{1,0:T(8,128)(2,1)S(1)}, u32[]{:S(2)}, u32[]{:S(2)}) collective-permute-start(bf16[768,896]{1,0:T(8,128)(2,1)} %get-tuple-element.222), channel_id=1, source_target_pairs={{0,16},{16,0},{1,17},{17,1},{2,18},{18,2},{3,19},{19,3},{4,20},{20... | collective-permute-start | bytes 4128776 | tf_op jit(solution)/shard_map/ppermute | solution.py:1103
  371.3 46.8 %collective-permute-start.39 = (bf16[384,1792]{1,0:T(8,128)(2,1)}, bf16[384,1792]{1,0:T(8,128)(2,1)S(1)}, u32[]{:S(2)}, u32[]{:S(2)}) collective-permute-start(bf16[384,1792]{1,0:T(8,128)(2,1)} %get-tuple-element.231), channel_id=1, source_target_pairs={{0,4},{4,0},{8,12},{12,8},{1,5},{5,1},{9,13},{13,9},{2,6},{6,2},{1... | collective-permute-start | bytes 4128776 | tf_op jit(solution)/shard_map/ppermute | solution.py:1108
  383.0 20.3 %collective-permute-start.34 = (bf16[256,1536]{1,0:T(8,128)(2,1)S(1)}, bf16[256,1536]{1,0:T(8,128)(2,1)S(1)}, u32[]{:S(2)}, u32[]{:S(2)}) collective-permute-start(bf16[256,1536]{1,0:T(8,128)(2,1)S(1)} %get-tuple-element.220.refs_1_), channel_id=1, source_target_pairs={{0,1},{1,0},{2,3},{3,2},{4,5},{5,4},{6,7},{7,6},{8,9},{9,8},{10,11... | collective-permute-start | bytes 2359304 | tf_op jit(solution)/shard_map/ppermute | solution.py:48
  383.1 21.5 %collective-permute-start.35 = (bf16[256,1536]{1,0:T(8,128)(2,1)S(1)}, bf16[256,1536]{1,0:T(8,128)(2,1)S(1)}, u32[]{:S(2)}, u32[]{:S(2)}) collective-permute-start(bf16[256,1536]{1,0:T(8,128)(2,1)S(1)} %get-tuple-element.221.refs_2_), channel_id=1, source_target_pairs={{0,1},{1,0},{2,3},{3,2},{4,5},{5,4},{6,7},{7,6},{8,9},{9,8},{10,11... | collective-permute-start | bytes 2359304 | tf_op jit(solution)/shard_map/ppermute | solution.py:48
  383.6 34.8 %collective-permute-start.38 = (bf16[768,512]{1,0:T(8,128)(2,1)S(1)}, bf16[768,512]{1,0:T(8,128)(2,1)S(1)}, u32[]{:S(2)}, u32[]{:S(2)}) collective-permute-start(bf16[768,512]{1,0:T(8,128)(2,1)S(1)} %copy-done.86), channel_id=1, source_target_pairs={{0,16},{16,0},{1,17},{17,1},{2,18},{18,2},{3,19},{19,3},{4,20},{20... | collective-permute-start | bytes 2359304 | tf_op jit(solution)/shard_map/ppermute | solution.py:1103
  401.8 34.5 %collective-permute-start.37 = (bf16[384,896]{1,0:T(8,128)(2,1)S(1)}, bf16[384,896]{1,0:T(8,128)(2,1)S(1)}, u32[]{:S(2)}, u32[]{:S(2)}) collective-permute-start(bf16[384,896]{1,0:T(8,128)(2,1)S(1)} %get-tuple-element.228), channel_id=1, source_target_pairs={{0,4},{4,0},{8,12},{12,8},{1,5},{5,1},{9,13},{13,9},{2,6},{6,2},{1... | collective-permute-start | bytes 2064392 | tf_op jit(solution)/shard_map/ppermute | solution.py:1108
  403.3 26.5 %collective-permute-start.40 = (bf16[192,1280]{1,0:T(8,128)(2,1)S(1)}, bf16[192,1280]{1,0:T(8,128)(2,1)S(1)}, u32[]{:S(2)}, u32[]{:S(2)}) collective-permute-start(bf16[192,1280]{1,0:T(8,128)(2,1)S(1)} %copy-done.90), channel_id=1, source_target_pairs={{0,8},{4,12},{8,0},{12,4},{1,9},{5,13},{9,1},{13,5},{2,10},{6,14},... | collective-permute-start | bytes 1474568 | tf_op jit(solution)/shard_map/ppermute | solution.py:1113
  418.3 50.7 %collective-permute-start.45 = (bf16[192,1792]{1,0:T(8,128)(2,1)S(1)}, bf16[192,1792]{1,0:T(8,128)(2,1)S(1)}, u32[]{:S(2)}, u32[]{:S(2)}) collective-permute-start(bf16[192,1792]{1,0:T(8,128)(2,1)S(1)} %get-tuple-element.243), channel_id=1, source_target_pairs={{0,8},{4,12},{8,0},{12,4},{1,9},{5,13},{9,1},{13,5},{2,10},{6,14},... | collective-permute-start | bytes 2064392 | tf_op jit(solution)/shard_map/ppermute | solution.py:1113
  431.8 21.1 %collective-permute-start.43 = (bf16[384,512]{1,0:T(8,128)(2,1)S(1)}, bf16[384,512]{1,0:T(8,128)(2,1)S(1)}, u32[]{:S(2)}, u32[]{:S(2)}) collective-permute-start(bf16[384,512]{1,0:T(8,128)(2,1)S(1)} %get-tuple-element.239), channel_id=1, source_target_pairs={{0,4},{4,0},{8,12},{12,8},{1,5},{5,1},{9,13},{13,9},{2,6},{6,2},{1... | collective-permute-start | bytes 1179656 | tf_op jit(solution)/shard_map/ppermute | solution.py:1108
  435.6 37.1 %collective-permute-start.42 = (bf16[192,1024]{1,0:T(8,128)(2,1)S(1)}, bf16[192,1024]{1,0:T(8,128)(2,1)S(1)}, u32[]{:S(2)}, u32[]{:S(2)}) collective-permute-start(bf16[192,1024]{1,0:T(8,128)(2,1)S(1)} %copy-done.74), channel_id=1, source_target_pairs={{0,16},{16,0},{1,17},{17,1},{2,18},{18,2},{3,19},{19,3},{4,20},{20... | collective-permute-start | bytes 1179656 | tf_op jit(solution)/shard_map/ppermute | solution.py:1135
  437.1 45.5 %collective-permute-start.41 = (bf16[192,896]{1,0:T(8,128)(2,1)}, bf16[192,896]{1,0:T(8,128)(2,1)}, u32[]{:S(2)}, u32[]{:S(2)}) collective-permute-start(bf16[192,896]{1,0:T(8,128)(2,1)} %get-tuple-element.236), channel_id=1, source_target_pairs={{0,8},{4,12},{8,0},{12,4},{1,9},{5,13},{9,1},{13,5},{2,10},{6,14},... | collective-permute-start | bytes 1032200 | tf_op jit(solution)/shard_map/ppermute | solution.py:1113
  437.3 6.3 %collective-permute-start.44 = (f32[8,512]{1,0:T(8,128)S(1)}, f32[8,512]{1,0:T(8,128)S(1)}, u32[]{:S(2)}, u32[]{:S(2)}) collective-permute-start(f32[8,512]{1,0:T(8,128)S(1)} %get-tuple-element.240.refs_0_), channel_id=1, source_target_pairs={{0,16},{16,0},{1,17},{17,1},{2,18},{18,2},{3,19},{19,3},{4,20},{20... | collective-permute-start | bytes 49160 | tf_op jit(solution)/shard_map/ppermute | solution.py:1236
  470.5 18.2 %collective-permute-start.48 = (bf16[192,512]{1,0:T(8,128)(2,1)}, bf16[192,512]{1,0:T(8,128)(2,1)S(1)}, u32[]{:S(2)}, u32[]{:S(2)}) collective-permute-start(bf16[192,512]{1,0:T(8,128)(2,1)} %get-tuple-element.252), channel_id=1, source_target_pairs={{0,8},{4,12},{8,0},{12,4},{1,9},{5,13},{9,1},{13,5},{2,10},{6,14},... | collective-permute-start | bytes 589832 | tf_op jit(solution)/shard_map/ppermute | solution.py:1113
  470.5 15.6 %collective-permute-start.46 = (f32[8,512]{1,0:T(8,128)S(1)}, f32[8,512]{1,0:T(8,128)}, u32[]{:S(2)}, u32[]{:S(2)}) collective-permute-start(f32[8,512]{1,0:T(8,128)S(1)} %get-tuple-element.248.refs_0_), channel_id=1, source_target_pairs={{0,4},{4,0},{8,12},{12,8},{1,5},{5,1},{9,13},{13,9},{2,6},{6,2},{1... | collective-permute-start | bytes 49160 | tf_op jit(solution)/shard_map/ppermute | solution.py:1238
  486.9 6.1 %collective-permute-start.47 = (f32[8,512]{1,0:T(8,128)S(1)}, f32[8,512]{1,0:T(8,128)S(1)}, u32[]{:S(2)}, u32[]{:S(2)}) collective-permute-start(f32[8,512]{1,0:T(8,128)S(1)} %get-tuple-element.250), channel_id=1, source_target_pairs={{0,8},{4,12},{8,0},{12,4},{1,9},{5,13},{9,1},{13,5},{2,10},{6,14},... | collective-permute-start | bytes 49160 | tf_op jit(solution)/shard_map/ppermute | solution.py:1247
  494.4 7.2 %collective-permute-start.50 = (f32[2,200,128]{2,1,0:T(8,128)S(1)}, f32[2,200,128]{2,1,0:T(8,128)S(1)}, u32[]{:S(2)}, u32[]{:S(2)}) collective-permute-start(f32[2,200,128]{2,1,0:T(8,128)S(1)} %maximum_select_fusion.1), channel_id=1, source_target_pairs={{0,2},{1,3},{2,0},{3,1},{4,6},{5,7},{6,4},{7,5},{8,10},{9,11},{10,... | collective-permute-start | bytes 614408 | tf_op jit(solution)/shard_map/ppermute | solution.py:52
  (115 other events, 1261.4 us)
Sparse Core Ops, SparseCore 0:
  135.4 70.5 reduce-scatter.2
  300.7 65.6 reduce-scatter.4

commit v13 on v12

--- a/solution.py
+++ b/solution.py
@@ -1219,6 +1219,7 @@
     last_parts = [(0, 0, 0, grad_qkv.shape[1] // HD, 0), (1, 1, 0, heads, 0)]
     last = Rows([h_one_t, branch_t], [grad_qkv, mixed], last_parts, HD)
     ffn_mine = narrow(order, [(hidden, down_t)], 0, ffn_sent)
+    down_a.settled()
     token = norm_back(order, core_one, mine, come, flat_tokens, gain_one, grad_middle, True)
     token += core_swaps(token)
     ffn_come = chip_swaps(ffn_mine)
@@ -1229,7 +1230,6 @@
     last.own()
     layer_out = place(order, core_one, layer).reshape(rows, local, width)
     up_a.relay()
-    down_a.settled()
     up_b.own()
     last.relay()
     if near_pair:

time: 515 us -> 507 us (0.984)
  starting transfers between devices: 55.5 us -> 49.6 us
    ppermute x5, waiting for transfers between devices: 28.9 us -> 9.49 us  [__init__(): self.come = lax.ppermute(sent, 'dp', flipped('dp', 0))]
    ppermute x4, waiting for transfers between devices: 27.5 us -> 35.4 us  [relay(): self.last = lax.ppermute(sent, 'seq', flipped('seq', 1))]
    ppermute x4, starting transfers between devices: 17.4 us -> 10.8 us  [own(): self.come = lax.ppermute(send, 'seq', flipped('seq', 0))]
    unnamed x225 -> x227, local copies, waits for them, and re-layouts: 74.1 us -> 74.9 us
  transfers between devices with their start and end apart: 53 -> 53, of which waited for: 26 -> 24; matrix products, arithmetic and copies ran while one was open for 3% -> 3% of each run, Pallas kernels for 28% -> 29%
where the time goes in v13:
time: 507 us; the launch traced here: 504 us
  Pallas kernels  200 us (39%)
  waiting for transfers between devices  145 us (29%)
  local copies, waits for them, and re-layouts  85.1 us (17%)
  starting transfers between devices  49.6 us (10%)
  between operations  15.5 us (3%)
  other arithmetic  9.38 us (2%)
    pallas_call x44, Pallas kernels, __call__(): pl.pallas_call(run, grid_spec=pltpu.PrefetchScalarGridSpec(num_scalar_pre...  190 us
    unnamed x227, local copies, waits for them, and re-layouts  74.9 us
    ppermute x4, waiting for transfers between devices, relay(): self.last = lax.ppermute(sent, 'seq', flipped('seq', 1))  35.4 us
    ppermute x9, waiting for transfers between devices, chip_swap(): return lax.ppermute(value, 'tensor', flipped('tensor', 1))  34.6 us
    ppermute x4, waiting for transfers between devices, own(): self.come = lax.ppermute(send, 'seq', flipped('seq', 0))  32.7 us
    ppermute x4, waiting for transfers between devices, shifted(): return lax.ppermute(value, 'seq', route)  16.1 us
    ppermute x21, waiting for transfers between devices, core_swap(): return lax.ppermute(value, 'tensor', flipped('tensor', 0))  13.8 us
    ppermute x4, starting transfers between devices, shifted(): return lax.ppermute(value, 'seq', route)  13 us
  transfers between devices with their start and end apart: 53, of which 24 were waited for; matrix products, arithmetic and copies ran while one was open for 3% of the time, Pallas kernels for 29%

profile of v13, /device:TPU:0, one launch (start us, length us, event | category | flops | bytes accessed | tf_op | source)
XLA Modules:
  0.0 504.3 jit_solution(120988246671079986)
XLA Ops:
  17.2 3.6 first.1
  23.4 5.6 %collective-permute-start.1 = (bf16[2,512,128]{2,1,0:T(8,128)(2,1)S(1)}, bf16[2,512,128]{2,1,0:T(8,128)(2,1)}, u32[]{:S(2)}, u32[]{:S(2)}) collective-permute-start(bf16[2,512,128]{2,1,0:T(8,128)(2,1)S(1)} %bitcast.77), channel_id=1, source_target_pairs={{0,4},{4,8},{8,12},{1,5},{5,9},{9,13},{2,6},{6,10},{10,14},{3,7},{... | collective-permute-start | bytes 786440 | tf_op jit(solution)/shard_map/ppermute | solution.py:66
  29.0 4.5 collective-permute-start
  34.5 4.3 collective-permute-done.refs_0_.refs_9_
  41.9 6.1 %attend.1 = (bf16[2,512,384]{2,1,0:T(8,128)(2,1)S(1)}, f32[2,2,768]{2,1,0:T(2,128)S(1)}) custom-call(s32[2,2]{1,0:T(2,128)S(1)} %shift-right-logical_maximum_fusion.low_ref.refs_0_, s32[1]{0:T(128)} %bitcast.core_ref.refs_0_.refs_1_, bf16[2,512,384]{2,1,0:T(8,128)(2,1)S(1)} %bitcast.74, s32[2,1,512]{2,1,0:T(1,128)S(1)} %sub.44.start_ref.refs_3_, ...), custom_call_target="tpu_custom_call" | custom-call | flops 8000000 | bytes 4194 | tf_op jit(solution)/shard_map/attend/pallas_call | solution.py:253
  53.6 3.5 narrow.9
  60.4 4.5 constant_dynamic-slice_fusion.2
  74.6 5.2 %copy-done.9 = bf16[1536,2240]{0,1:T(8,128)(2,1)S(1)} copy-done((bf16[1536,2240]{0,1:T(8,128)(2,1)S(1)}, bf16[1536,2240]{0,1:T(8,128)(2,1)}, u32[]{:S(2)}) %copy-start.9) | copy-done | bytes 6881304
  79.8 9.3 %grad_hidden.1 = (bf16[1024,2240]{1,0:T(8,128)(2,1)S(1)}, f32[8,128]{1,0:T(8,128)S(1)}) custom-call(bf16[1024,1536]{1,0:T(8,128)(2,1)S(1)} %get-tuple-element.146.refs_0_.refs_3_, bf16[2240,1536]{1,0:T(8,128)(2,1)S(1)} %bitcast.61, f32[8,128]{1,0:T(8,128)S(1)} %get-tuple-element.147.refs_2_, bf16[192,2240]{1,0:T(8,128)(2,1)S(1)} %copy-done.40, ...), custom_call_target="tpu_custom_call" | custom-call | flops 7046430 | bytes 15728 | tf_op jit(solution)/shard_map/grad_hidden/pallas_call | solution.py:92
  94.5 3.8 middle.1
  104.2 20.3 %gated.1 = (bf16[1024,2240]{1,0:T(8,128)(2,1)S(1)}, bf16[1024,2240]{1,0:T(8,128)(2,1)S(1)}, bf16[1024,2240]{1,0:T(8,128)(2,1)S(1)}, f32[8,128]{1,0:T(8,128)S(1)}) custom-call(bf16[1024,2240]{1,0:T(8,128)(2,1)S(1)} %copy-done.49, bf16[2240,1536]{1,0:T(8,128)(2,1)} %bitcast.58, bf16[2240,1536]{1,0:T(8,128)(2,1)} %bitcast.83, ...), custom_call_target="tpu_custom_call" | custom-call | flops 14092861 | bytes 31457 | tf_op jit(solution)/shard_map/gated/pallas_call | solution.py:92
  126.7 4.8 share.9
  139.9 4.2 share.10
  147.9 3.0 copy-done.7
  150.9 10.3 %narrow.10 = (bf16[256,1536]{1,0:T(8,128)(2,1)S(1)}, bf16[256,1536]{1,0:T(8,128)(2,1)S(1)}, f32[8,128]{1,0:T(8,128)S(1)}) custom-call(bf16[1024,2240]{1,0:T(8,128)(2,1)S(1)} %copy-done.5, bf16[2240,1536]{1,0:T(8,128)(2,1)S(1)} %bitcast.59, bf16[1024,2240]{1,0:T(8,128)(2,1)S(1)} %bitcast.47, bf16[2240,1536]{1,0:T(8,128)(2,1)} %bitcast.84, ...), custom_call_target="tpu_custom_call" | custom-call | flops 7046430 | bytes 19922 | tf_op jit(solution)/shard_map/narrow/pallas_call | solution.py:92
  164.7 3.1 copy-done.8
  167.8 11.1 %narrow.11 = (bf16[256,1536]{1,0:T(8,128)(2,1)}, bf16[256,1536]{1,0:T(8,128)(2,1)}, f32[8,128]{1,0:T(8,128)S(1)}) custom-call(bf16[1024,2240]{1,0:T(8,128)(2,1)S(1)} %bitcast.55, bf16[2240,1536]{1,0:T(8,128)(2,1)S(1)} %bitcast.60, bf16[1024,2240]{1,0:T(8,128)(2,1)S(1)} %bitcast.47, bf16[2240,1536]{1,0:T(8,128)(2,1)} %bitcast.85, ...), custom_call_target="tpu_custom_call" | custom-call | flops 7046430 | bytes 19922 | tf_op jit(solution)/shard_map/narrow/pallas_call | solution.py:92
  182.4 13.9 %share.11 = (bf16[768,2304]{1,0:T(8,128)(2,1)}, bf16[768,1792]{1,0:T(8,128)(2,1)S(1)}, bf16[768,512]{1,0:T(8,128)(2,1)}, f32[8,128]{1,0:T(8,128)S(1)}) custom-call(s32[1]{0:T(128)} %bitcast.10.refs_0_, s32[1]{0:T(128)} %constant.59.clone.1.refs_0_.refs_1_, bf16[1536,1024]{1,0:T(8,128)(2,1)S(1)} %get-tuple-element.169.refs_2_, ...), custom_call_target="tpu_custom_call" | custom-call | flops 7247757 | bytes 18087 | tf_op jit(solution)/shard_map/share/pallas_call | solution.py:92
  202.9 5.9 %share.12 = (bf16[384,1280]{1,0:T(8,128)(2,1)S(1)}, bf16[384,1280]{1,0:T(8,128)(2,1)S(1)}, f32[8,128]{1,0:T(8,128)S(1)}) custom-call(s32[1]{0:T(128)} %bitcast.11.refs_0_, s32[4]{0:T(128)S(1)} %pad_add_fusion.refs_1_, bf16[1536,1024]{1,0:T(8,128)(2,1)S(1)} %copy-done.18, bf16[1024,2240]{1,0:T(8,128)(2,1)S(1)} %copy-done.3, ...), custom_call_target="tpu_custom_call" | custom-call | flops 2013265 | bytes 6160 | tf_op jit(solution)/shard_map/share/pallas_call | solution.py:92
  208.8 6.9 %collective-permute-done.14.refs_7_ = bf16[256,1536]{1,0:T(8,128)(2,1)} collective-permute-done((bf16[256,1536]{1,0:T(8,128)(2,1)}, bf16[256,1536]{1,0:T(8,128)(2,1)}, u32[]{:S(2)}, u32[]{:S(2)}) %collective-permute-start.14) | collective-permute-done | bytes 786464 | tf_op jit(solution)/shard_map/ppermute | solution.py:52
  215.7 4.1 norm_back.2
  220.4 10.7 %collective-permute-start.19 = (bf16[384,1280]{1,0:T(8,128)(2,1)S(1)}, bf16[384,1280]{1,0:T(8,128)(2,1)S(1)}, u32[]{:S(2)}, u32[]{:S(2)}) collective-permute-start(bf16[384,1280]{1,0:T(8,128)(2,1)S(1)} %get-tuple-element.182), channel_id=1, source_target_pairs={{0,4},{4,0},{8,12},{12,8},{1,5},{5,1},{9,13},{13,9},{2,6},{6,2},{1... | collective-permute-start | bytes 2949128 | tf_op jit(solution)/shard_map/ppermute | solution.py:1108
  233.0 8.9 %attend_back.1 = (bf16[2,512,384]{2,1,0:T(8,128)(2,1)S(1)}, bf16[2,1536,128]{2,1,0:T(8,128)(2,1)S(1)}, bf16[2,1536,128]{2,1,0:T(8,128)(2,1)S(1)}, f32[8,128]{1,0:T(8,128)S(1)}) custom-call(s32[2,2]{1,0:T(2,128)S(1)} %shift-right-logical_maximum_fusion.low_ref.refs_0_, s32[1]{0:T(128)} %bitcast.core_ref.refs_0_.refs_1_, bf16[2,512,384]{2,1,0:T(8,128)(2,1)S(1)} %bitcast.75, ...), custom_call_target="tpu_custom_call" | custom-call | flops 20000000 | bytes 6291 | tf_op jit(solution)/shard_map/attend_back/pallas_call | solution.py:92
  245.1 7.9 %collective-permute-done.19.refs_1_ = bf16[384,1280]{1,0:T(8,128)(2,1)S(1)} collective-permute-done((bf16[384,1280]{1,0:T(8,128)(2,1)S(1)}, bf16[384,1280]{1,0:T(8,128)(2,1)S(1)}, u32[]{:S(2)}, u32[]{:S(2)}) %collective-permute-start.19) | collective-permute-done | bytes 983072 | tf_op jit(solution)/shard_map/ppermute | solution.py:1108
  256.4 5.3 %narrow.12 = (bf16[256,1536]{1,0:T(8,128)(2,1)S(1)}, bf16[256,1536]{1,0:T(8,128)(2,1)S(1)}, f32[8,128]{1,0:T(8,128)S(1)}) custom-call(bf16[1024,2240]{1,0:T(8,128)(2,1)S(1)} %bitcast.51, bf16[2240,1536]{1,0:T(8,128)(2,1)S(1)} %bitcast.64, f32[8,128]{1,0:T(8,128)S(1)} %get-tuple-element.186.refs_2_), custom_call_target="tpu_custom_call" | custom-call | flops 3523215 | bytes 10747 | tf_op jit(solution)/shard_map/narrow/pallas_call | solution.py:92
  266.4 8.5 %collective-permute-done.23.refs_5_ = bf16[2,512,128]{2,1,0:T(8,128)(2,1)S(1)} collective-permute-done((bf16[2,512,128]{2,1,0:T(8,128)(2,1)S(1)}, bf16[2,512,128]{2,1,0:T(8,128)(2,1)S(1)}, u32[]{:S(2)}, u32[]{:S(2)}) %collective-permute-start.23) | collective-permute-done | bytes 262176 | tf_op jit(solution)/shard_map/ppermute | solution.py:66
  275.6 3.4 narrow.13
  282.8 4.4 narrow.14
  291.3 8.3 %share.13 = (bf16[768,2304]{1,0:T(8,128)(2,1)S(1)}, f32[8,128]{1,0:T(8,128)S(1)}) custom-call(s32[1]{0:T(128)} %bitcast.11.refs_0_, s32[1]{0:T(128)} %constant.59.clone.1.refs_0_.refs_1_, bf16[1536,1024]{1,0:T(8,128)(2,1)S(1)} %copy-done.12, bf16[1024,2240]{1,0:T(8,128)(2,1)S(1)} %copy-done.6, bf16[768,2304]{1,0:T(8,128)(2,1)} %collective-permute-done.24.refs_4_, ...), custom_call_target="tpu_custom_call" | custom-call | flops 3623878 | bytes 9830 | tf_op jit(solution)/shard_map/share/pallas_call | solution.py:92
  311.1 5.3 %share.14 = (bf16[768,896]{1,0:T(8,128)(2,1)}, f32[8,128]{1,0:T(8,128)S(1)}) custom-call(s32[1]{0:T(128)} %bitcast.10.refs_0_, s32[1]{0:T(128)} %constant.59.clone.1.refs_0_.refs_1_, bf16[1536,1024]{1,0:T(8,128)(2,1)S(1)} %copy-done.24, bf16[1536,1024]{1,0:T(8,128)(2,1)S(1)} %copy-done.30, bf16[1024,512]{1,0:T(8,128)(2,1)S(1)} %get-tuple-element.198.refs_0_.refs_4_, ...), custom_call_target="tpu_custom_call" | custom-call | flops 1409286 | bytes 4784 | tf_op jit(solution)/shard_map/share/pallas_call | solution.py:92
  316.4 3.0 copy-done.10
  319.4 6.1 %narrow.15 = (bf16[256,1536]{1,0:T(8,128)(2,1)}, bf16[256,1536]{1,0:T(8,128)(2,1)}, f32[8,128]{1,0:T(8,128)S(1)}) custom-call(bf16[1024,2240]{1,0:T(8,128)(2,1)S(1)} %bitcast.53, bf16[2240,1536]{1,0:T(8,128)(2,1)S(1)} %bitcast.65, bf16[256,1536]{1,0:T(8,128)(2,1)S(1)} %collective-permute-done.20.refs_2_, ...), custom_call_target="tpu_custom_call" | custom-call | flops 3523215 | bytes 10747 | tf_op jit(solution)/shard_map/narrow/pallas_call | solution.py:92
  325.5 35.4 %collective-permute-done.31.refs_9_.refs_2_ = bf16[192,1280]{1,0:T(8,128)(2,1)S(1)} collective-permute-done((bf16[192,1280]{1,0:T(8,128)(2,1)}, bf16[192,1280]{1,0:T(8,128)(2,1)S(1)}, u32[]{:S(2)}, u32[]{:S(2)}) %collective-permute-start.31) | collective-permute-done | bytes 491552 | tf_op jit(solution)/shard_map/ppermute | solution.py:1113
  369.4 8.0 %share.15 = (bf16[384,1792]{1,0:T(8,128)(2,1)}, bf16[384,1792]{1,0:T(8,128)(2,1)S(1)}, f32[8,128]{1,0:T(8,128)S(1)}) custom-call(s32[1]{0:T(128)} %bitcast.11.refs_0_, s32[4]{0:T(128)S(1)} %pad_add_fusion.refs_1_, bf16[1536,1024]{1,0:T(8,128)(2,1)S(1)} %copy-done.13, bf16[1024,2240]{1,0:T(8,128)(2,1)S(1)} %bitcast.49, ...), custom_call_target="tpu_custom_call" | custom-call | flops 2818572 | bytes 7995 | tf_op jit(solution)/shard_map/share/pallas_call | solution.py:92
  377.4 3.3 place.2
  380.6 7.3 %collective-permute-done.27.refs_3_ = bf16[256,1536]{1,0:T(8,128)(2,1)S(1)} collective-permute-done((bf16[256,1536]{1,0:T(8,128)(2,1)}, bf16[256,1536]{1,0:T(8,128)(2,1)S(1)}, u32[]{:S(2)}, u32[]{:S(2)}) %collective-permute-start.27) | collective-permute-done | bytes 786464 | tf_op jit(solution)/shard_map/ppermute | solution.py:52
  388.0 15.7 %collective-permute-done.28.refs_4_ = bf16[256,1536]{1,0:T(8,128)(2,1)S(1)} collective-permute-done((bf16[256,1536]{1,0:T(8,128)(2,1)}, bf16[256,1536]{1,0:T(8,128)(2,1)S(1)}, u32[]{:S(2)}, u32[]{:S(2)}) %collective-permute-start.28) | collective-permute-done | bytes 786464 | tf_op jit(solution)/shard_map/ppermute | solution.py:52
  405.7 3.5 layer.1
  410.4 7.1 %share.16 = (bf16[384,896]{1,0:T(8,128)(2,1)S(1)}, bf16[384,896]{1,0:T(8,128)(2,1)S(1)}, f32[8,128]{1,0:T(8,128)S(1)}) custom-call(s32[1]{0:T(128)} %bitcast.11.refs_0_, s32[4]{0:T(128)S(1)} %pad_add_fusion.refs_1_, bf16[1536,1024]{1,0:T(8,128)(2,1)S(1)} %copy-done.25, bf16[1536,1024]{1,0:T(8,128)(2,1)S(1)} %copy-done.31, ...), custom_call_target="tpu_custom_call" | custom-call | flops 1409286 | bytes 4784 | tf_op jit(solution)/shard_map/share/pallas_call | solution.py:92
  420.1 9.5 %collective-permute-done.39.refs_4_ = bf16[768,512]{1,0:T(8,128)(2,1)S(1)} collective-permute-done((bf16[768,512]{1,0:T(8,128)(2,1)}, bf16[768,512]{1,0:T(8,128)(2,1)S(1)}, u32[]{:S(2)}, u32[]{:S(2)}) %collective-permute-start.39) | collective-permute-done | bytes 786464 | tf_op jit(solution)/shard_map/ppermute | solution.py:1103
  432.4 13.7 %collective-permute-done.38.refs_1_ = bf16[384,896]{1,0:T(8,128)(2,1)S(1)} collective-permute-done((bf16[384,896]{1,0:T(8,128)(2,1)S(1)}, bf16[384,896]{1,0:T(8,128)(2,1)S(1)}, u32[]{:S(2)}, u32[]{:S(2)}) %collective-permute-start.38) | collective-permute-done | bytes 688160 | tf_op jit(solution)/shard_map/ppermute | solution.py:1108
  447.6 3.0 collective-permute-done.44.refs_1_
  450.6 11.1 %collective-permute-done.43.refs_1_.refs_4_ = bf16[384,512]{1,0:T(8,128)(2,1)S(1)} collective-permute-done((bf16[384,512]{1,0:T(8,128)(2,1)S(1)}, bf16[384,512]{1,0:T(8,128)(2,1)S(1)}, u32[]{:S(2)}, u32[]{:S(2)}) %collective-permute-start.43) | collective-permute-done | bytes 393248 | tf_op jit(solution)/shard_map/ppermute | solution.py:1108
  464.1 3.8 finish.4
  470.4 3.7 finish.5
  474.1 3.5 finish.6
  480.8 4.0 finish.7
  488.9 4.7 collective-permute-done.50
  (389 shorter events, 141.7 us)
Async XLA Ops:
  7.2 272.4 %reduce-scatter.3.cloned.1.call-start = ((), (), s32[]{:S(2)}) async-start(), calls=%async_computation.2 | async-start | bytes 3932160 | tf_op jit(solution)/shard_map/reduce_scatter | solution.py:1128
  23.4 11.1 %collective-permute-start.1 = (bf16[2,512,128]{2,1,0:T(8,128)(2,1)S(1)}, bf16[2,512,128]{2,1,0:T(8,128)(2,1)}, u32[]{:S(2)}, u32[]{:S(2)}) collective-permute-start(bf16[2,512,128]{2,1,0:T(8,128)(2,1)S(1)} %bitcast.77), channel_id=1, source_target_pairs={{0,4},{4,8},{8,12},{1,5},{5,9},{9,13},{2,6},{6,10},{10,14},{3,7},{... | collective-permute-start | bytes 786440 | tf_op jit(solution)/shard_map/ppermute | solution.py:66
  29.0 9.8 %collective-permute-start = (bf16[2,512,128]{2,1,0:T(8,128)(2,1)S(1)}, bf16[2,512,128]{2,1,0:T(8,128)(2,1)}, u32[]{:S(2)}, u32[]{:S(2)}) collective-permute-start(bf16[2,512,128]{2,1,0:T(8,128)(2,1)S(1)} %bitcast.78), channel_id=1, source_target_pairs={{0,8},{4,12},{1,9},{5,13},{2,10},{6,14},{3,11},{7,15},{16,24},{20,... | collective-permute-start | bytes 786440 | tf_op jit(solution)/shard_map/ppermute | solution.py:66
  33.5 5.5 %collective-permute-start.4 = (bf16[2,512,128]{2,1,0:T(8,128)(2,1)S(1)}, bf16[2,512,128]{2,1,0:T(8,128)(2,1)}, u32[]{:S(2)}, u32[]{:S(2)}) collective-permute-start(bf16[2,512,128]{2,1,0:T(8,128)(2,1)S(1)} %bitcast.79), channel_id=1, source_target_pairs={{0,1},{1,0},{2,3},{3,2},{4,5},{5,4},{6,7},{7,6},{8,9},{9,8},{10,11... | collective-permute-start | bytes 786440 | tf_op jit(solution)/shard_map/ppermute | solution.py:48
  34.5 4.5 collective-permute-start.3
  50.3 3.3 collective-permute-start.6
  57.1 37.5 %collective-permute-start.7 = (bf16[256,1536]{1,0:T(8,128)(2,1)}, bf16[256,1536]{1,0:T(8,128)(2,1)}, u32[]{:S(2)}, u32[]{:S(2)}) collective-permute-start(bf16[256,1536]{1,0:T(8,128)(2,1)} %get-tuple-element.142.refs_3_), channel_id=1, source_target_pairs={{0,2},{1,3},{2,0},{3,1},{4,6},{5,7},{6,4},{7,5},{8,10},{9,11},{10,... | collective-permute-start | bytes 2359304 | tf_op jit(solution)/shard_map/ppermute | solution.py:52
  58.6 36.0 %collective-permute-start.8 = (bf16[256,1536]{1,0:T(8,128)(2,1)}, bf16[256,1536]{1,0:T(8,128)(2,1)}, u32[]{:S(2)}, u32[]{:S(2)}) collective-permute-start(bf16[256,1536]{1,0:T(8,128)(2,1)} %get-tuple-element.143.refs_4_), channel_id=1, source_target_pairs={{0,2},{1,3},{2,0},{3,1},{4,6},{5,7},{6,4},{7,5},{8,10},{9,11},{10,... | collective-permute-start | bytes 2359304 | tf_op jit(solution)/shard_map/ppermute | solution.py:52
  98.4 3.4 collective-permute-start.10
  135.3 333.1 %reduce-scatter.5.cloned.1.call-start = ((), (), s32[]{:S(2)}) async-start(), calls=%async_computation.3 | async-start | bytes 4423680 | tf_op jit(solution)/shard_map/reduce_scatter | solution.py:1148
  144.1 54.5 %collective-permute-start.15 = (bf16[768,1280]{1,0:T(8,128)(2,1)}, bf16[768,1280]{1,0:T(8,128)(2,1)}, u32[]{:S(2)}, u32[]{:S(2)}) collective-permute-start(bf16[768,1280]{1,0:T(8,128)(2,1)} %get-tuple-element.167), channel_id=1, source_target_pairs={{0,16},{16,0},{1,17},{17,1},{2,18},{18,2},{3,19},{19,3},{4,20},{20... | collective-permute-start | bytes 5898248 | tf_op jit(solution)/shard_map/ppermute | solution.py:1103
  161.2 3.4 collective-permute-start.12
  178.9 29.9 %collective-permute-start.13 = (bf16[256,1536]{1,0:T(8,128)(2,1)}, bf16[256,1536]{1,0:T(8,128)(2,1)S(1)}, u32[]{:S(2)}, u32[]{:S(2)}) collective-permute-start(bf16[256,1536]{1,0:T(8,128)(2,1)} %get-tuple-element.165.refs_4_), channel_id=1, source_target_pairs={{0,2},{1,3},{2,0},{3,1},{4,6},{5,7},{6,4},{7,5},{8,10},{9,11},{10,... | collective-permute-start | bytes 2359304 | tf_op jit(solution)/shard_map/ppermute | solution.py:52
  180.4 35.3 %collective-permute-start.14 = (bf16[256,1536]{1,0:T(8,128)(2,1)}, bf16[256,1536]{1,0:T(8,128)(2,1)}, u32[]{:S(2)}, u32[]{:S(2)}) collective-permute-start(bf16[256,1536]{1,0:T(8,128)(2,1)} %get-tuple-element.166.refs_5_), channel_id=1, source_target_pairs={{0,2},{1,3},{2,0},{3,1},{4,6},{5,7},{6,4},{7,5},{8,10},{9,11},{10,... | collective-permute-start | bytes 2359304 | tf_op jit(solution)/shard_map/ppermute | solution.py:52
  198.0 90.2 %collective-permute-start.24 = (bf16[768,2304]{1,0:T(8,128)(2,1)}, bf16[768,2304]{1,0:T(8,128)(2,1)}, u32[]{:S(2)}, u32[]{:S(2)}) collective-permute-start(bf16[768,2304]{1,0:T(8,128)(2,1)} %get-tuple-element.199), channel_id=1, source_target_pairs={{0,16},{16,0},{1,17},{17,1},{2,18},{18,2},{3,19},{19,3},{4,20},{20... | collective-permute-start | bytes 10616840 | tf_op jit(solution)/shard_map/ppermute | solution.py:1103
  219.8 11.3 %collective-permute-start.16 = (bf16[256,1536]{1,0:T(8,128)(2,1)S(1)}, bf16[256,1536]{1,0:T(8,128)(2,1)S(1)}, u32[]{:S(2)}, u32[]{:S(2)}) collective-permute-start(bf16[256,1536]{1,0:T(8,128)(2,1)S(1)} %get-tuple-element.173.refs_1_.refs_0_), channel_id=1, source_target_pairs={{0,1},{1,0},{2,3},{3,2},{4,5},{5,4},{6,7},{7,6},{8,9},{9,8},{10,11... | collective-permute-start | bytes 2359304 | tf_op jit(solution)/shard_map/ppermute | solution.py:48
  219.9 11.2 %collective-permute-start.17 = (bf16[256,1536]{1,0:T(8,128)(2,1)S(1)}, bf16[256,1536]{1,0:T(8,128)(2,1)S(1)}, u32[]{:S(2)}, u32[]{:S(2)}) collective-permute-start(bf16[256,1536]{1,0:T(8,128)(2,1)S(1)} %get-tuple-element.174.refs_2_.refs_1_), channel_id=1, source_target_pairs={{0,1},{1,0},{2,3},{3,2},{4,5},{5,4},{6,7},{7,6},{8,9},{9,8},{10,11... | collective-permute-start | bytes 2359304 | tf_op jit(solution)/shard_map/ppermute | solution.py:48
  220.4 32.7 %collective-permute-start.19 = (bf16[384,1280]{1,0:T(8,128)(2,1)S(1)}, bf16[384,1280]{1,0:T(8,128)(2,1)S(1)}, u32[]{:S(2)}, u32[]{:S(2)}) collective-permute-start(bf16[384,1280]{1,0:T(8,128)(2,1)S(1)} %get-tuple-element.182), channel_id=1, source_target_pairs={{0,4},{4,0},{8,12},{12,8},{1,5},{5,1},{9,13},{13,9},{2,6},{6,2},{1... | collective-permute-start | bytes 2949128 | tf_op jit(solution)/shard_map/ppermute | solution.py:1108
  241.9 12.9 %collective-permute-start.18 = (bf16[2,1536,128]{2,1,0:T(8,128)(2,1)S(1)}, bf16[2,1536,128]{2,1,0:T(8,128)(2,1)S(1)}, u32[]{:S(2)}, u32[]{:S(2)}) collective-permute-start(bf16[2,1536,128]{2,1,0:T(8,128)(2,1)S(1)} %get-tuple-element.180), channel_id=1, source_target_pairs={{0,1},{1,0},{2,3},{3,2},{4,5},{5,4},{6,7},{7,6},{8,9},{9,8},{10,11... | collective-permute-start | bytes 2359304 | tf_op jit(solution)/shard_map/ppermute | solution.py:48
  255.0 9.8 %collective-permute-start.22 = (bf16[2,512,128]{2,1,0:T(8,128)(2,1)S(1)}, bf16[2,512,128]{2,1,0:T(8,128)(2,1)S(1)}, u32[]{:S(2)}, u32[]{:S(2)}) collective-permute-start(bf16[2,512,128]{2,1,0:T(8,128)(2,1)S(1)} %get-tuple-element.194), channel_id=1, source_target_pairs={{4,0},{8,4},{12,8},{5,1},{9,5},{13,9},{6,2},{10,6},{14,10},{7,3},{... | collective-permute-start | bytes 786440 | tf_op jit(solution)/shard_map/ppermute | solution.py:66
  264.9 10.1 %collective-permute-start.23 = (bf16[2,512,128]{2,1,0:T(8,128)(2,1)S(1)}, bf16[2,512,128]{2,1,0:T(8,128)(2,1)S(1)}, u32[]{:S(2)}, u32[]{:S(2)}) collective-permute-start(bf16[2,512,128]{2,1,0:T(8,128)(2,1)S(1)} %get-tuple-element.196), channel_id=1, source_target_pairs={{4,0},{8,4},{12,8},{5,1},{9,5},{13,9},{6,2},{10,6},{14,10},{7,3},{... | collective-permute-start | bytes 786440 | tf_op jit(solution)/shard_map/ppermute | solution.py:66
  279.1 2.6 collective-permute-start.25
  279.1 3.7 collective-permute-start.26
  301.5 67.4 %collective-permute-start.34 = (bf16[768,1792]{1,0:T(8,128)(2,1)}, bf16[768,1792]{1,0:T(8,128)(2,1)}, u32[]{:S(2)}, u32[]{:S(2)}) collective-permute-start(bf16[768,1792]{1,0:T(8,128)(2,1)} %copy-done.88), channel_id=1, source_target_pairs={{0,16},{16,0},{1,17},{17,1},{2,18},{18,2},{3,19},{19,3},{4,20},{20... | collective-permute-start | bytes 8257544 | tf_op jit(solution)/shard_map/ppermute | solution.py:1103
  301.6 3.1 collective-permute-start.20
  301.8 14.6 %collective-permute-start.21 = (bf16[256,1536]{1,0:T(8,128)(2,1)}, bf16[256,1536]{1,0:T(8,128)(2,1)S(1)}, u32[]{:S(2)}, u32[]{:S(2)}) collective-permute-start(bf16[256,1536]{1,0:T(8,128)(2,1)} %copy-done.89), channel_id=1, source_target_pairs={{0,1},{1,0},{2,3},{3,2},{4,5},{5,4},{6,7},{7,6},{8,9},{9,8},{10,11... | collective-permute-start | bytes 2359304 | tf_op jit(solution)/shard_map/ppermute | solution.py:48
  302.6 58.3 %collective-permute-start.29 = (bf16[256,1536]{1,0:T(8,128)(2,1)S(1)}, bf16[256,1536]{1,0:T(8,128)(2,1)S(1)}, u32[]{:S(2)}, u32[]{:S(2)}) collective-permute-start(bf16[256,1536]{1,0:T(8,128)(2,1)S(1)} %copy-done.81), channel_id=1, source_target_pairs={{0,2},{1,3},{2,0},{3,1},{4,6},{5,7},{6,4},{7,5},{8,10},{9,11},{10,... | collective-permute-start | bytes 2359304 | tf_op jit(solution)/shard_map/ppermute | solution.py:52
  304.2 56.7 %collective-permute-start.30 = (bf16[256,1536]{1,0:T(8,128)(2,1)}, bf16[256,1536]{1,0:T(8,128)(2,1)S(1)}, u32[]{:S(2)}, u32[]{:S(2)}) collective-permute-start(bf16[256,1536]{1,0:T(8,128)(2,1)} %copy-done.82), channel_id=1, source_target_pairs={{0,2},{1,3},{2,0},{3,1},{4,6},{5,7},{6,4},{7,5},{8,10},{9,11},{10,... | collective-permute-start | bytes 2359304 | tf_op jit(solution)/shard_map/ppermute | solution.py:52
  304.7 56.3 %collective-permute-start.31 = (bf16[192,1280]{1,0:T(8,128)(2,1)}, bf16[192,1280]{1,0:T(8,128)(2,1)S(1)}, u32[]{:S(2)}, u32[]{:S(2)}) collective-permute-start(bf16[192,1280]{1,0:T(8,128)(2,1)} %copy-done.91), channel_id=1, source_target_pairs={{0,8},{4,12},{8,0},{12,4},{1,9},{5,13},{9,1},{13,5},{2,10},{6,14},... | collective-permute-start | bytes 1474568 | tf_op jit(solution)/shard_map/ppermute | solution.py:1113
  365.3 12.1 %collective-permute-start.32 = (f32[256,1536]{1,0:T(8,128)S(1)}, f32[256,1536]{1,0:T(8,128)S(1)}, u32[]{:S(2)}, u32[]{:S(2)}) collective-permute-start(f32[256,1536]{1,0:T(8,128)S(1)} %get-tuple-element.215.refs_1_), channel_id=1, source_target_pairs={{0,1},{1,0},{2,3},{3,2},{4,5},{5,4},{6,7},{7,6},{8,9},{9,8},{10,11... | collective-permute-start | bytes 4718600 | tf_op jit(solution)/shard_map/ppermute | solution.py:48
  365.3 12.0 %collective-permute-start.33 = (f32[256,1536]{1,0:T(8,128)S(1)}, f32[256,1536]{1,0:T(8,128)S(1)}, u32[]{:S(2)}, u32[]{:S(2)}) collective-permute-start(f32[256,1536]{1,0:T(8,128)S(1)} %get-tuple-element.216.refs_2_), channel_id=1, source_target_pairs={{0,1},{1,0},{2,3},{3,2},{4,5},{5,4},{6,7},{7,6},{8,9},{9,8},{10,11... | collective-permute-start | bytes 4718600 | tf_op jit(solution)/shard_map/ppermute | solution.py:48
  365.8 44.5 %collective-permute-start.37 = (bf16[768,896]{1,0:T(8,128)(2,1)}, bf16[768,896]{1,0:T(8,128)(2,1)}, u32[]{:S(2)}, u32[]{:S(2)}) collective-permute-start(bf16[768,896]{1,0:T(8,128)(2,1)} %get-tuple-element.223), channel_id=1, source_target_pairs={{0,16},{16,0},{1,17},{17,1},{2,18},{18,2},{3,19},{19,3},{4,20},{20... | collective-permute-start | bytes 4128776 | tf_op jit(solution)/shard_map/ppermute | solution.py:1103
  367.3 20.6 %collective-permute-start.27 = (bf16[256,1536]{1,0:T(8,128)(2,1)}, bf16[256,1536]{1,0:T(8,128)(2,1)S(1)}, u32[]{:S(2)}, u32[]{:S(2)}) collective-permute-start(bf16[256,1536]{1,0:T(8,128)(2,1)} %get-tuple-element.208.refs_1_), channel_id=1, source_target_pairs={{0,2},{1,3},{2,0},{3,1},{4,6},{5,7},{6,4},{7,5},{8,10},{9,11},{10,... | collective-permute-start | bytes 2359304 | tf_op jit(solution)/shard_map/ppermute | solution.py:52
  369.0 34.7 %collective-permute-start.28 = (bf16[256,1536]{1,0:T(8,128)(2,1)}, bf16[256,1536]{1,0:T(8,128)(2,1)S(1)}, u32[]{:S(2)}, u32[]{:S(2)}) collective-permute-start(bf16[256,1536]{1,0:T(8,128)(2,1)} %get-tuple-element.209.refs_2_), channel_id=1, source_target_pairs={{0,2},{1,3},{2,0},{3,1},{4,6},{5,7},{6,4},{7,5},{8,10},{9,11},{10,... | collective-permute-start | bytes 2359304 | tf_op jit(solution)/shard_map/ppermute | solution.py:52
  377.3 42.5 %collective-permute-start.40 = (bf16[384,1792]{1,0:T(8,128)(2,1)}, bf16[384,1792]{1,0:T(8,128)(2,1)S(1)}, u32[]{:S(2)}, u32[]{:S(2)}) collective-permute-start(bf16[384,1792]{1,0:T(8,128)(2,1)} %get-tuple-element.232), channel_id=1, source_target_pairs={{0,4},{4,0},{8,12},{12,8},{1,5},{5,1},{9,13},{13,9},{2,6},{6,2},{1... | collective-permute-start | bytes 4128776 | tf_op jit(solution)/shard_map/ppermute | solution.py:1108
  409.3 8.4 %collective-permute-start.35 = (bf16[256,1536]{1,0:T(8,128)(2,1)S(1)}, bf16[256,1536]{1,0:T(8,128)(2,1)S(1)}, u32[]{:S(2)}, u32[]{:S(2)}) collective-permute-start(bf16[256,1536]{1,0:T(8,128)(2,1)S(1)} %get-tuple-element.221.refs_1_), channel_id=1, source_target_pairs={{0,1},{1,0},{2,3},{3,2},{4,5},{5,4},{6,7},{7,6},{8,9},{9,8},{10,11... | collective-permute-start | bytes 2359304 | tf_op jit(solution)/shard_map/ppermute | solution.py:48
  409.3 8.3 %collective-permute-start.36 = (bf16[256,1536]{1,0:T(8,128)(2,1)S(1)}, bf16[256,1536]{1,0:T(8,128)(2,1)S(1)}, u32[]{:S(2)}, u32[]{:S(2)}) collective-permute-start(bf16[256,1536]{1,0:T(8,128)(2,1)S(1)} %get-tuple-element.222.refs_2_), channel_id=1, source_target_pairs={{0,1},{1,0},{2,3},{3,2},{4,5},{5,4},{6,7},{7,6},{8,9},{9,8},{10,11... | collective-permute-start | bytes 2359304 | tf_op jit(solution)/shard_map/ppermute | solution.py:48
  409.8 19.7 %collective-permute-start.39 = (bf16[768,512]{1,0:T(8,128)(2,1)}, bf16[768,512]{1,0:T(8,128)(2,1)S(1)}, u32[]{:S(2)}, u32[]{:S(2)}) collective-permute-start(bf16[768,512]{1,0:T(8,128)(2,1)} %get-tuple-element.230), channel_id=1, source_target_pairs={{0,16},{16,0},{1,17},{17,1},{2,18},{18,2},{3,19},{19,3},{4,20},{20... | collective-permute-start | bytes 2359304 | tf_op jit(solution)/shard_map/ppermute | solution.py:1103
  417.5 28.5 %collective-permute-start.38 = (bf16[384,896]{1,0:T(8,128)(2,1)S(1)}, bf16[384,896]{1,0:T(8,128)(2,1)S(1)}, u32[]{:S(2)}, u32[]{:S(2)}) collective-permute-start(bf16[384,896]{1,0:T(8,128)(2,1)S(1)} %get-tuple-element.229), channel_id=1, source_target_pairs={{0,4},{4,0},{8,12},{12,8},{1,5},{5,1},{9,13},{13,9},{2,6},{6,2},{1... | collective-permute-start | bytes 2064392 | tf_op jit(solution)/shard_map/ppermute | solution.py:1108
  420.0 41.7 %collective-permute-start.45 = (bf16[192,1792]{1,0:T(8,128)(2,1)S(1)}, bf16[192,1792]{1,0:T(8,128)(2,1)S(1)}, u32[]{:S(2)}, u32[]{:S(2)}) collective-permute-start(bf16[192,1792]{1,0:T(8,128)(2,1)S(1)} %get-tuple-element.243), channel_id=1, source_target_pairs={{0,8},{4,12},{8,0},{12,4},{1,9},{5,13},{9,1},{13,5},{2,10},{6,14},... | collective-permute-start | bytes 2064392 | tf_op jit(solution)/shard_map/ppermute | solution.py:1113
  431.7 30.1 %collective-permute-start.43 = (bf16[384,512]{1,0:T(8,128)(2,1)S(1)}, bf16[384,512]{1,0:T(8,128)(2,1)S(1)}, u32[]{:S(2)}, u32[]{:S(2)}) collective-permute-start(bf16[384,512]{1,0:T(8,128)(2,1)S(1)} %get-tuple-element.239), channel_id=1, source_target_pairs={{0,4},{4,0},{8,12},{12,8},{1,5},{5,1},{9,13},{13,9},{2,6},{6,2},{1... | collective-permute-start | bytes 1179656 | tf_op jit(solution)/shard_map/ppermute | solution.py:1108
  431.7 32.3 %collective-permute-start.42 = (bf16[192,1024]{1,0:T(8,128)(2,1)S(1)}, bf16[192,1024]{1,0:T(8,128)(2,1)S(1)}, u32[]{:S(2)}, u32[]{:S(2)}) collective-permute-start(bf16[192,1024]{1,0:T(8,128)(2,1)S(1)} %copy-done.76), channel_id=1, source_target_pairs={{0,16},{16,0},{1,17},{17,1},{2,18},{18,2},{3,19},{19,3},{4,20},{20... | collective-permute-start | bytes 1179656 | tf_op jit(solution)/shard_map/ppermute | solution.py:1135
  446.9 27.2 %collective-permute-start.41 = (bf16[192,896]{1,0:T(8,128)(2,1)}, bf16[192,896]{1,0:T(8,128)(2,1)}, u32[]{:S(2)}, u32[]{:S(2)}) collective-permute-start(bf16[192,896]{1,0:T(8,128)(2,1)} %get-tuple-element.236), channel_id=1, source_target_pairs={{0,8},{4,12},{8,0},{12,4},{1,9},{5,13},{9,1},{13,5},{2,10},{6,14},... | collective-permute-start | bytes 1032200 | tf_op jit(solution)/shard_map/ppermute | solution.py:1113
  446.9 3.7 collective-permute-start.44
  462.5 18.2 %collective-permute-start.48 = (bf16[192,512]{1,0:T(8,128)(2,1)}, bf16[192,512]{1,0:T(8,128)(2,1)S(1)}, u32[]{:S(2)}, u32[]{:S(2)}) collective-permute-start(bf16[192,512]{1,0:T(8,128)(2,1)} %get-tuple-element.252), channel_id=1, source_target_pairs={{0,8},{4,12},{8,0},{12,4},{1,9},{5,13},{9,1},{13,5},{2,10},{6,14},... | collective-permute-start | bytes 589832 | tf_op jit(solution)/shard_map/ppermute | solution.py:1113
  462.5 15.0 %collective-permute-start.46 = (f32[8,512]{1,0:T(8,128)S(1)}, f32[8,512]{1,0:T(8,128)}, u32[]{:S(2)}, u32[]{:S(2)}) collective-permute-start(f32[8,512]{1,0:T(8,128)S(1)} %get-tuple-element.248.refs_0_), channel_id=1, source_target_pairs={{0,4},{4,0},{8,12},{12,8},{1,5},{5,1},{9,13},{13,9},{2,6},{6,2},{1... | collective-permute-start | bytes 49160 | tf_op jit(solution)/shard_map/ppermute | solution.py:1238
  478.3 6.7 %collective-permute-start.47 = (f32[8,512]{1,0:T(8,128)S(1)}, f32[8,512]{1,0:T(8,128)S(1)}, u32[]{:S(2)}, u32[]{:S(2)}) collective-permute-start(f32[8,512]{1,0:T(8,128)S(1)} %get-tuple-element.250), channel_id=1, source_target_pairs={{0,8},{4,12},{8,0},{12,4},{1,9},{5,13},{9,1},{13,5},{2,10},{6,14},... | collective-permute-start | bytes 49160 | tf_op jit(solution)/shard_map/ppermute | solution.py:1247
  486.4 7.2 %collective-permute-start.50 = (f32[2,200,128]{2,1,0:T(8,128)S(1)}, f32[2,200,128]{2,1,0:T(8,128)S(1)}, u32[]{:S(2)}, u32[]{:S(2)}) collective-permute-start(f32[2,200,128]{2,1,0:T(8,128)S(1)} %maximum_select_fusion.1), channel_id=1, source_target_pairs={{0,2},{1,3},{2,0},{3,1},{4,6},{5,7},{6,4},{7,5},{8,10},{9,11},{10,... | collective-permute-start | bytes 614408 | tf_op jit(solution)/shard_map/ppermute | solution.py:52
  (116 other events, 1217.9 us)
Sparse Core Ops, SparseCore 0:
  135.5 71.6 reduce-scatter.2
  301.6 81.4 reduce-scatter.4

commit v14 on v13

--- a/solution.py
+++ b/solution.py
@@ -1215,11 +1215,11 @@
     down_b.across()
     mine = narrow(order, [(grad_qkv, weight)], 0, sent, 1)
     come = chip_swaps(mine)
+    down_a.settled()
     gate.own()
     last_parts = [(0, 0, 0, grad_qkv.shape[1] // HD, 0), (1, 1, 0, heads, 0)]
     last = Rows([h_one_t, branch_t], [grad_qkv, mixed], last_parts, HD)
     ffn_mine = narrow(order, [(hidden, down_t)], 0, ffn_sent)
-    down_a.settled()
     token = norm_back(order, core_one, mine, come, flat_tokens, gain_one, grad_middle, True)
     token += core_swaps(token)
     ffn_come = chip_swaps(ffn_mine)

time: 507 us -> 515 us (1.016)
  waiting for transfers between devices: 145 us -> 155 us
    ppermute x5, waiting for transfers between devices: 9.49 us -> 25.8 us  [__init__(): self.come = lax.ppermute(sent, 'dp', flipped('dp', 0))]
    ppermute x4, waiting for transfers between devices: 35.4 us -> 26.9 us  [relay(): self.last = lax.ppermute(sent, 'seq', flipped('seq', 1))]
    ppermute x4, waiting for transfers between devices: 32.7 us -> 38 us  [own(): self.come = lax.ppermute(send, 'seq', flipped('seq', 0))]
    unnamed x227 -> x221, local copies, waits for them, and re-layouts: 74.9 us -> 72.5 us
  transfers between devices with their start and end apart: 53 -> 53, of which waited for: 24 -> 25; matrix products, arithmetic and copies ran while one was open for 3% -> 3% of each run, Pallas kernels for 29% -> 29%
where the time goes in v14:
time: 515 us; the launch traced here: 514 us
  Pallas kernels  201 us (39%)
  waiting for transfers between devices  155 us (30%)
  local copies, waits for them, and re-layouts  82.7 us (16%)
  starting transfers between devices  50.1 us (10%)
  between operations  15.5 us (3%)
  other arithmetic  9.38 us (2%)
    pallas_call x44, Pallas kernels, __call__(): pl.pallas_call(run, grid_spec=pltpu.PrefetchScalarGridSpec(num_scalar_pre...  191 us
    unnamed x221, local copies, waits for them, and re-layouts  72.5 us
    ppermute x4, waiting for transfers between devices, own(): self.come = lax.ppermute(send, 'seq', flipped('seq', 0))  38 us
    ppermute x9, waiting for transfers between devices, chip_swap(): return lax.ppermute(value, 'tensor', flipped('tensor', 1))  31.4 us
    ppermute x4, waiting for transfers between devices, relay(): self.last = lax.ppermute(sent, 'seq', flipped('seq', 1))  26.9 us
    ppermute x5, waiting for transfers between devices, __init__(): self.come = lax.ppermute(sent, 'dp', flipped('dp', 0))  25.8 us
    ppermute x4, waiting for transfers between devices, shifted(): return lax.ppermute(value, 'seq', route)  18.5 us
    ppermute x4, starting transfers between devices, shifted(): return lax.ppermute(value, 'seq', route)  13 us
  transfers between devices with their start and end apart: 53, of which 25 were waited for; matrix products, arithmetic and copies ran while one was open for 3% of the time, Pallas kernels for 29%

profile of v14, /device:TPU:0, one launch (start us, length us, event | category | flops | bytes accessed | tf_op | source)
XLA Modules:
  0.0 513.6 jit_solution(2138085045549836786)
XLA Ops:
  17.2 3.6 first.1
  23.4 5.6 %collective-permute-start.1 = (bf16[2,512,128]{2,1,0:T(8,128)(2,1)S(1)}, bf16[2,512,128]{2,1,0:T(8,128)(2,1)}, u32[]{:S(2)}, u32[]{:S(2)}) collective-permute-start(bf16[2,512,128]{2,1,0:T(8,128)(2,1)S(1)} %bitcast.77), channel_id=1, source_target_pairs={{0,4},{4,8},{8,12},{1,5},{5,9},{9,13},{2,6},{6,10},{10,14},{3,7},{... | collective-permute-start | bytes 786440 | tf_op jit(solution)/shard_map/ppermute | solution.py:66
  29.1 4.5 collective-permute-start
  34.5 4.3 collective-permute-done.refs_0_.refs_9_
  41.9 6.1 %attend.1 = (bf16[2,512,384]{2,1,0:T(8,128)(2,1)S(1)}, f32[2,2,768]{2,1,0:T(2,128)S(1)}) custom-call(s32[2,2]{1,0:T(2,128)S(1)} %shift-right-logical_maximum_fusion.low_ref.refs_0_, s32[1]{0:T(128)} %bitcast.core_ref.refs_0_.refs_1_, bf16[2,512,384]{2,1,0:T(8,128)(2,1)S(1)} %bitcast.74, s32[2,1,512]{2,1,0:T(1,128)S(1)} %sub.44.start_ref.refs_3_, ...), custom_call_target="tpu_custom_call" | custom-call | flops 8000000 | bytes 4194 | tf_op jit(solution)/shard_map/attend/pallas_call | solution.py:253
  53.6 3.5 narrow.9
  60.4 4.5 constant_dynamic-slice_fusion.2
  74.6 5.2 %copy-done.9 = bf16[1536,2240]{0,1:T(8,128)(2,1)S(1)} copy-done((bf16[1536,2240]{0,1:T(8,128)(2,1)S(1)}, bf16[1536,2240]{0,1:T(8,128)(2,1)}, u32[]{:S(2)}) %copy-start.9) | copy-done | bytes 6881304
  79.8 9.3 %grad_hidden.1 = (bf16[1024,2240]{1,0:T(8,128)(2,1)S(1)}, f32[8,128]{1,0:T(8,128)S(1)}) custom-call(bf16[1024,1536]{1,0:T(8,128)(2,1)S(1)} %get-tuple-element.146.refs_0_.refs_3_, bf16[2240,1536]{1,0:T(8,128)(2,1)S(1)} %bitcast.61, f32[8,128]{1,0:T(8,128)S(1)} %get-tuple-element.147.refs_2_, bf16[192,2240]{1,0:T(8,128)(2,1)S(1)} %copy-done.40, ...), custom_call_target="tpu_custom_call" | custom-call | flops 7046430 | bytes 15728 | tf_op jit(solution)/shard_map/grad_hidden/pallas_call | solution.py:92
  94.6 3.8 middle.1
  104.2 20.3 %gated.1 = (bf16[1024,2240]{1,0:T(8,128)(2,1)S(1)}, bf16[1024,2240]{1,0:T(8,128)(2,1)S(1)}, bf16[1024,2240]{1,0:T(8,128)(2,1)S(1)}, f32[8,128]{1,0:T(8,128)S(1)}) custom-call(bf16[1024,2240]{1,0:T(8,128)(2,1)S(1)} %copy-done.49, bf16[2240,1536]{1,0:T(8,128)(2,1)} %bitcast.58, bf16[2240,1536]{1,0:T(8,128)(2,1)} %bitcast.83, ...), custom_call_target="tpu_custom_call" | custom-call | flops 14092861 | bytes 31457 | tf_op jit(solution)/shard_map/gated/pallas_call | solution.py:92
  126.7 4.8 share.9
  139.9 4.2 share.10
  150.9 10.3 %narrow.10 = (bf16[256,1536]{1,0:T(8,128)(2,1)S(1)}, bf16[256,1536]{1,0:T(8,128)(2,1)S(1)}, f32[8,128]{1,0:T(8,128)S(1)}) custom-call(bf16[1024,2240]{1,0:T(8,128)(2,1)S(1)} %copy-done.5, bf16[2240,1536]{1,0:T(8,128)(2,1)S(1)} %bitcast.59, bf16[1024,2240]{1,0:T(8,128)(2,1)S(1)} %bitcast.47, bf16[2240,1536]{1,0:T(8,128)(2,1)} %bitcast.84, ...), custom_call_target="tpu_custom_call" | custom-call | flops 7046430 | bytes 19922 | tf_op jit(solution)/shard_map/narrow/pallas_call | solution.py:92
  164.7 3.2 copy-done.8
  167.9 11.1 %narrow.11 = (bf16[256,1536]{1,0:T(8,128)(2,1)}, bf16[256,1536]{1,0:T(8,128)(2,1)}, f32[8,128]{1,0:T(8,128)S(1)}) custom-call(bf16[1024,2240]{1,0:T(8,128)(2,1)S(1)} %bitcast.55, bf16[2240,1536]{1,0:T(8,128)(2,1)S(1)} %bitcast.60, bf16[1024,2240]{1,0:T(8,128)(2,1)S(1)} %bitcast.47, bf16[2240,1536]{1,0:T(8,128)(2,1)} %bitcast.85, ...), custom_call_target="tpu_custom_call" | custom-call | flops 7046430 | bytes 19922 | tf_op jit(solution)/shard_map/narrow/pallas_call | solution.py:92
  182.5 13.7 %share.11 = (bf16[768,2304]{1,0:T(8,128)(2,1)}, bf16[768,1792]{1,0:T(8,128)(2,1)S(1)}, bf16[768,512]{1,0:T(8,128)(2,1)S(1)}, f32[8,128]{1,0:T(8,128)S(1)}) custom-call(s32[1]{0:T(128)} %bitcast.10.refs_0_, s32[1]{0:T(128)} %constant.59.clone.1.refs_0_.refs_1_, bf16[1536,1024]{1,0:T(8,128)(2,1)S(1)} %get-tuple-element.169.refs_2_, ...), custom_call_target="tpu_custom_call" | custom-call | flops 7247757 | bytes 18087 | tf_op jit(solution)/shard_map/share/pallas_call | solution.py:92
  203.5 5.9 %share.12 = (bf16[384,1280]{1,0:T(8,128)(2,1)S(1)}, bf16[384,1280]{1,0:T(8,128)(2,1)S(1)}, f32[8,128]{1,0:T(8,128)S(1)}) custom-call(s32[1]{0:T(128)} %bitcast.11.refs_0_, s32[4]{0:T(128)S(1)} %pad_add_fusion.refs_1_, bf16[1536,1024]{1,0:T(8,128)(2,1)S(1)} %copy-done.18, bf16[1024,2240]{1,0:T(8,128)(2,1)S(1)} %copy-done.3, ...), custom_call_target="tpu_custom_call" | custom-call | flops 2013265 | bytes 6160 | tf_op jit(solution)/shard_map/share/pallas_call | solution.py:92
  209.5 6.2 %collective-permute-done.14.refs_7_ = bf16[256,1536]{1,0:T(8,128)(2,1)} collective-permute-done((bf16[256,1536]{1,0:T(8,128)(2,1)}, bf16[256,1536]{1,0:T(8,128)(2,1)}, u32[]{:S(2)}, u32[]{:S(2)}) %collective-permute-start.14) | collective-permute-done | bytes 786464 | tf_op jit(solution)/shard_map/ppermute | solution.py:52
  215.6 4.1 norm_back.2
  220.4 9.2 %collective-permute-start.19 = (bf16[384,1280]{1,0:T(8,128)(2,1)S(1)}, bf16[384,1280]{1,0:T(8,128)(2,1)S(1)}, u32[]{:S(2)}, u32[]{:S(2)}) collective-permute-start(bf16[384,1280]{1,0:T(8,128)(2,1)S(1)} %get-tuple-element.182), channel_id=1, source_target_pairs={{0,4},{4,0},{8,12},{12,8},{1,5},{5,1},{9,13},{13,9},{2,6},{6,2},{1... | collective-permute-start | bytes 2949128 | tf_op jit(solution)/shard_map/ppermute | solution.py:1108
  231.5 8.9 %attend_back.1 = (bf16[2,512,384]{2,1,0:T(8,128)(2,1)S(1)}, bf16[2,1536,128]{2,1,0:T(8,128)(2,1)S(1)}, bf16[2,1536,128]{2,1,0:T(8,128)(2,1)S(1)}, f32[8,128]{1,0:T(8,128)S(1)}) custom-call(s32[2,2]{1,0:T(2,128)S(1)} %shift-right-logical_maximum_fusion.low_ref.refs_0_, s32[1]{0:T(128)} %bitcast.core_ref.refs_0_.refs_1_, bf16[2,512,384]{2,1,0:T(8,128)(2,1)S(1)} %bitcast.75, ...), custom_call_target="tpu_custom_call" | custom-call | flops 20000000 | bytes 6291 | tf_op jit(solution)/shard_map/attend_back/pallas_call | solution.py:92
  243.6 7.9 %collective-permute-done.19.refs_1_ = bf16[384,1280]{1,0:T(8,128)(2,1)S(1)} collective-permute-done((bf16[384,1280]{1,0:T(8,128)(2,1)S(1)}, bf16[384,1280]{1,0:T(8,128)(2,1)S(1)}, u32[]{:S(2)}, u32[]{:S(2)}) %collective-permute-start.19) | collective-permute-done | bytes 983072 | tf_op jit(solution)/shard_map/ppermute | solution.py:1108
  254.3 5.3 %narrow.12 = (bf16[256,1536]{1,0:T(8,128)(2,1)S(1)}, bf16[256,1536]{1,0:T(8,128)(2,1)S(1)}, f32[8,128]{1,0:T(8,128)S(1)}) custom-call(bf16[1024,2240]{1,0:T(8,128)(2,1)S(1)} %bitcast.51, bf16[2240,1536]{1,0:T(8,128)(2,1)S(1)} %bitcast.64, f32[8,128]{1,0:T(8,128)S(1)} %get-tuple-element.186.refs_2_), custom_call_target="tpu_custom_call" | custom-call | flops 3523215 | bytes 10747 | tf_op jit(solution)/shard_map/narrow/pallas_call | solution.py:92
  264.3 10.9 %collective-permute-done.23.refs_5_ = bf16[2,512,128]{2,1,0:T(8,128)(2,1)S(1)} collective-permute-done((bf16[2,512,128]{2,1,0:T(8,128)(2,1)S(1)}, bf16[2,512,128]{2,1,0:T(8,128)(2,1)S(1)}, u32[]{:S(2)}, u32[]{:S(2)}) %collective-permute-start.23) | collective-permute-done | bytes 262176 | tf_op jit(solution)/shard_map/ppermute | solution.py:66
  275.9 3.4 narrow.13
  283.7 4.7 narrow.14
  289.3 15.5 %collective-permute-done.27.refs_6_.refs_2_ = bf16[192,1280]{1,0:T(8,128)(2,1)} collective-permute-done((bf16[192,1280]{1,0:T(8,128)(2,1)}, bf16[192,1280]{1,0:T(8,128)(2,1)}, u32[]{:S(2)}, u32[]{:S(2)}) %collective-permute-start.27) | collective-permute-done | bytes 491552 | tf_op jit(solution)/shard_map/ppermute | solution.py:1113
  307.1 8.3 %share.13 = (bf16[768,2304]{1,0:T(8,128)(2,1)S(1)}, f32[8,128]{1,0:T(8,128)S(1)}) custom-call(s32[1]{0:T(128)} %bitcast.11.refs_0_, s32[1]{0:T(128)} %constant.59.clone.1.refs_0_.refs_1_, bf16[1536,1024]{1,0:T(8,128)(2,1)S(1)} %copy-done.12, bf16[1024,2240]{1,0:T(8,128)(2,1)S(1)} %copy-done.6, bf16[768,2304]{1,0:T(8,128)(2,1)} %collective-permute-done.24.refs_4_, ...), custom_call_target="tpu_custom_call" | custom-call | flops 3623878 | bytes 9830 | tf_op jit(solution)/shard_map/share/pallas_call | solution.py:92
  324.9 5.3 %share.14 = (bf16[768,896]{1,0:T(8,128)(2,1)}, f32[8,128]{1,0:T(8,128)S(1)}) custom-call(s32[1]{0:T(128)} %bitcast.10.refs_0_, s32[1]{0:T(128)} %constant.59.clone.1.refs_0_.refs_1_, bf16[1536,1024]{1,0:T(8,128)(2,1)S(1)} %copy-done.24, bf16[1536,1024]{1,0:T(8,128)(2,1)S(1)} %copy-done.30, bf16[1024,512]{1,0:T(8,128)(2,1)S(1)} %get-tuple-element.198.refs_0_.refs_4_, ...), custom_call_target="tpu_custom_call" | custom-call | flops 1409286 | bytes 4784 | tf_op jit(solution)/shard_map/share/pallas_call | solution.py:92
  333.1 6.0 %narrow.15 = (bf16[256,1536]{1,0:T(8,128)(2,1)}, bf16[256,1536]{1,0:T(8,128)(2,1)}, f32[8,128]{1,0:T(8,128)S(1)}) custom-call(bf16[1024,2240]{1,0:T(8,128)(2,1)S(1)} %bitcast.53, bf16[2240,1536]{1,0:T(8,128)(2,1)S(1)} %bitcast.65, bf16[256,1536]{1,0:T(8,128)(2,1)S(1)} %collective-permute-done.20.refs_2_, ...), custom_call_target="tpu_custom_call" | custom-call | flops 3523215 | bytes 10747 | tf_op jit(solution)/shard_map/narrow/pallas_call | solution.py:92
  339.2 15.2 %collective-permute-done.31.refs_7_ = bf16[256,1536]{1,0:T(8,128)(2,1)S(1)} collective-permute-done((bf16[256,1536]{1,0:T(8,128)(2,1)}, bf16[256,1536]{1,0:T(8,128)(2,1)S(1)}, u32[]{:S(2)}, u32[]{:S(2)}) %collective-permute-start.31) | collective-permute-done | bytes 786464 | tf_op jit(solution)/shard_map/ppermute | solution.py:52
  362.5 17.8 %collective-permute-done.34.refs_4_ = bf16[768,1792]{1,0:T(8,128)(2,1)} collective-permute-done((bf16[768,1792]{1,0:T(8,128)(2,1)}, bf16[768,1792]{1,0:T(8,128)(2,1)}, u32[]{:S(2)}, u32[]{:S(2)}) %collective-permute-start.34) | collective-permute-done | bytes 2752544 | tf_op jit(solution)/shard_map/ppermute | solution.py:1103
  381.8 8.0 %share.15 = (bf16[384,1792]{1,0:T(8,128)(2,1)}, bf16[384,1792]{1,0:T(8,128)(2,1)S(1)}, f32[8,128]{1,0:T(8,128)S(1)}) custom-call(s32[1]{0:T(128)} %bitcast.11.refs_0_, s32[4]{0:T(128)S(1)} %pad_add_fusion.refs_1_, bf16[1536,1024]{1,0:T(8,128)(2,1)S(1)} %copy-done.13, bf16[1024,2240]{1,0:T(8,128)(2,1)S(1)} %bitcast.49, ...), custom_call_target="tpu_custom_call" | custom-call | flops 2818572 | bytes 7995 | tf_op jit(solution)/shard_map/share/pallas_call | solution.py:92
  389.8 3.3 place.2
  393.1 4.3 collective-permute-done.29.refs_4_
  397.3 3.5 layer.1
  401.8 8.0 %collective-permute-done.37.refs_6_ = bf16[768,896]{1,0:T(8,128)(2,1)S(1)} collective-permute-done((bf16[768,896]{1,0:T(8,128)(2,1)}, bf16[768,896]{1,0:T(8,128)(2,1)S(1)}, u32[]{:S(2)}, u32[]{:S(2)}) %collective-permute-start.37) | collective-permute-done | bytes 1376288 | tf_op jit(solution)/shard_map/ppermute | solution.py:1103
  409.7 5.8 %share.16 = (bf16[384,896]{1,0:T(8,128)(2,1)S(1)}, bf16[384,896]{1,0:T(8,128)(2,1)S(1)}, f32[8,128]{1,0:T(8,128)S(1)}) custom-call(s32[1]{0:T(128)} %bitcast.11.refs_0_, s32[4]{0:T(128)S(1)} %pad_add_fusion.refs_1_, bf16[1536,1024]{1,0:T(8,128)(2,1)S(1)} %copy-done.25, bf16[1536,1024]{1,0:T(8,128)(2,1)S(1)} %copy-done.31, ...), custom_call_target="tpu_custom_call" | custom-call | flops 1409286 | bytes 4784 | tf_op jit(solution)/shard_map/share/pallas_call | solution.py:92
  417.8 11.3 %collective-permute-done.40.refs_1_ = bf16[384,1792]{1,0:T(8,128)(2,1)S(1)} collective-permute-done((bf16[384,1792]{1,0:T(8,128)(2,1)}, bf16[384,1792]{1,0:T(8,128)(2,1)S(1)}, u32[]{:S(2)}, u32[]{:S(2)}) %collective-permute-start.40) | collective-permute-done | bytes 1376288 | tf_op jit(solution)/shard_map/ppermute | solution.py:1108
  434.3 12.0 %collective-permute-done.38.refs_1_ = bf16[384,896]{1,0:T(8,128)(2,1)S(1)} collective-permute-done((bf16[384,896]{1,0:T(8,128)(2,1)S(1)}, bf16[384,896]{1,0:T(8,128)(2,1)S(1)}, u32[]{:S(2)}, u32[]{:S(2)}) %collective-permute-start.38) | collective-permute-done | bytes 688160 | tf_op jit(solution)/shard_map/ppermute | solution.py:1108
  450.9 6.7 %collective-permute-done.43.refs_1_.refs_4_ = bf16[384,512]{1,0:T(8,128)(2,1)S(1)} collective-permute-done((bf16[384,512]{1,0:T(8,128)(2,1)S(1)}, bf16[384,512]{1,0:T(8,128)(2,1)S(1)}, u32[]{:S(2)}, u32[]{:S(2)}) %collective-permute-start.43) | collective-permute-done | bytes 393248 | tf_op jit(solution)/shard_map/ppermute | solution.py:1108
  457.6 11.4 %collective-permute-done.45.refs_3_.refs_2_ = bf16[192,1792]{1,0:T(8,128)(2,1)S(1)} collective-permute-done((bf16[192,1792]{1,0:T(8,128)(2,1)S(1)}, bf16[192,1792]{1,0:T(8,128)(2,1)S(1)}, u32[]{:S(2)}, u32[]{:S(2)}) %collective-permute-start.45) | collective-permute-done | bytes 688160 | tf_op jit(solution)/shard_map/ppermute | solution.py:1113
  472.8 5.1 %finish.4 = (f32[192,2240]{1,0:T(8,128)}, f32[8,128]{1,0:T(8,128)S(1)}) custom-call(bf16[384,1280]{1,0:T(8,128)(2,1)S(1)} %copy-done.51, bf16[384,1280]{1,0:T(8,128)(2,1)S(1)} %copy-done.53, bf16[192,1280]{1,0:T(8,128)(2,1)} %collective-permute-done.27.refs_6_.refs_2_, bf16[192,1024]{1,0:T(8,128)(2,1)S(1)} %copy-done.56, ...), custom_call_target="tpu_custom_call" | custom-call | bytes 6021 | tf_op jit(solution)/shard_map/finish/pallas_call | solution.py:92
  480.4 3.7 finish.5
  484.1 3.5 finish.6
  490.1 4.0 finish.7
  497.2 5.7 %collective-permute-done.50 = f32[2,200,128]{2,1,0:T(8,128)S(1)} collective-permute-done((f32[2,200,128]{2,1,0:T(8,128)S(1)}, f32[2,200,128]{2,1,0:T(8,128)S(1)}, u32[]{:S(2)}, u32[]{:S(2)}) %collective-permute-start.50) | collective-permute-done | bytes 204832 | tf_op jit(solution)/shard_map/ppermute | solution.py:52
  (383 shorter events, 149.2 us)
Async XLA Ops:
  7.2 275.3 %reduce-scatter.3.cloned.1.call-start = ((), (), s32[]{:S(2)}) async-start(), calls=%async_computation.2 | async-start | bytes 3932160 | tf_op jit(solution)/shard_map/reduce_scatter | solution.py:1128
  23.4 11.1 %collective-permute-start.1 = (bf16[2,512,128]{2,1,0:T(8,128)(2,1)S(1)}, bf16[2,512,128]{2,1,0:T(8,128)(2,1)}, u32[]{:S(2)}, u32[]{:S(2)}) collective-permute-start(bf16[2,512,128]{2,1,0:T(8,128)(2,1)S(1)} %bitcast.77), channel_id=1, source_target_pairs={{0,4},{4,8},{8,12},{1,5},{5,9},{9,13},{2,6},{6,10},{10,14},{3,7},{... | collective-permute-start | bytes 786440 | tf_op jit(solution)/shard_map/ppermute | solution.py:66
  29.1 9.8 %collective-permute-start = (bf16[2,512,128]{2,1,0:T(8,128)(2,1)S(1)}, bf16[2,512,128]{2,1,0:T(8,128)(2,1)}, u32[]{:S(2)}, u32[]{:S(2)}) collective-permute-start(bf16[2,512,128]{2,1,0:T(8,128)(2,1)S(1)} %bitcast.78), channel_id=1, source_target_pairs={{0,8},{4,12},{1,9},{5,13},{2,10},{6,14},{3,11},{7,15},{16,24},{20,... | collective-permute-start | bytes 786440 | tf_op jit(solution)/shard_map/ppermute | solution.py:66
  33.6 5.4 %collective-permute-start.4 = (bf16[2,512,128]{2,1,0:T(8,128)(2,1)S(1)}, bf16[2,512,128]{2,1,0:T(8,128)(2,1)}, u32[]{:S(2)}, u32[]{:S(2)}) collective-permute-start(bf16[2,512,128]{2,1,0:T(8,128)(2,1)S(1)} %bitcast.79), channel_id=1, source_target_pairs={{0,1},{1,0},{2,3},{3,2},{4,5},{5,4},{6,7},{7,6},{8,9},{9,8},{10,11... | collective-permute-start | bytes 786440 | tf_op jit(solution)/shard_map/ppermute | solution.py:48
  34.5 4.5 collective-permute-start.3
  50.3 3.3 collective-permute-start.6
  57.1 37.4 %collective-permute-start.7 = (bf16[256,1536]{1,0:T(8,128)(2,1)}, bf16[256,1536]{1,0:T(8,128)(2,1)}, u32[]{:S(2)}, u32[]{:S(2)}) collective-permute-start(bf16[256,1536]{1,0:T(8,128)(2,1)} %get-tuple-element.142.refs_3_), channel_id=1, source_target_pairs={{0,2},{1,3},{2,0},{3,1},{4,6},{5,7},{6,4},{7,5},{8,10},{9,11},{10,... | collective-permute-start | bytes 2359304 | tf_op jit(solution)/shard_map/ppermute | solution.py:52
  58.6 35.9 %collective-permute-start.8 = (bf16[256,1536]{1,0:T(8,128)(2,1)}, bf16[256,1536]{1,0:T(8,128)(2,1)}, u32[]{:S(2)}, u32[]{:S(2)}) collective-permute-start(bf16[256,1536]{1,0:T(8,128)(2,1)} %get-tuple-element.143.refs_4_), channel_id=1, source_target_pairs={{0,2},{1,3},{2,0},{3,1},{4,6},{5,7},{6,4},{7,5},{8,10},{9,11},{10,... | collective-permute-start | bytes 2359304 | tf_op jit(solution)/shard_map/ppermute | solution.py:52
  98.4 3.4 collective-permute-start.10
  135.4 343.1 %reduce-scatter.5.cloned.1.call-start = ((), (), s32[]{:S(2)}) async-start(), calls=%async_computation.3 | async-start | bytes 4423680 | tf_op jit(solution)/shard_map/reduce_scatter | solution.py:1148
  144.1 55.2 %collective-permute-start.15 = (bf16[768,1280]{1,0:T(8,128)(2,1)}, bf16[768,1280]{1,0:T(8,128)(2,1)}, u32[]{:S(2)}, u32[]{:S(2)}) collective-permute-start(bf16[768,1280]{1,0:T(8,128)(2,1)} %get-tuple-element.167), channel_id=1, source_target_pairs={{0,16},{16,0},{1,17},{17,1},{2,18},{18,2},{3,19},{19,3},{4,20},{20... | collective-permute-start | bytes 5898248 | tf_op jit(solution)/shard_map/ppermute | solution.py:1103
  161.3 3.4 collective-permute-start.12
  178.9 30.5 %collective-permute-start.13 = (bf16[256,1536]{1,0:T(8,128)(2,1)}, bf16[256,1536]{1,0:T(8,128)(2,1)S(1)}, u32[]{:S(2)}, u32[]{:S(2)}) collective-permute-start(bf16[256,1536]{1,0:T(8,128)(2,1)} %get-tuple-element.165.refs_4_), channel_id=1, source_target_pairs={{0,2},{1,3},{2,0},{3,1},{4,6},{5,7},{6,4},{7,5},{8,10},{9,11},{10,... | collective-permute-start | bytes 2359304 | tf_op jit(solution)/shard_map/ppermute | solution.py:52
  180.4 35.2 %collective-permute-start.14 = (bf16[256,1536]{1,0:T(8,128)(2,1)}, bf16[256,1536]{1,0:T(8,128)(2,1)}, u32[]{:S(2)}, u32[]{:S(2)}) collective-permute-start(bf16[256,1536]{1,0:T(8,128)(2,1)} %get-tuple-element.166.refs_5_), channel_id=1, source_target_pairs={{0,2},{1,3},{2,0},{3,1},{4,6},{5,7},{6,4},{7,5},{8,10},{9,11},{10,... | collective-permute-start | bytes 2359304 | tf_op jit(solution)/shard_map/ppermute | solution.py:52
  198.7 106.1 %collective-permute-start.24 = (bf16[768,2304]{1,0:T(8,128)(2,1)}, bf16[768,2304]{1,0:T(8,128)(2,1)}, u32[]{:S(2)}, u32[]{:S(2)}) collective-permute-start(bf16[768,2304]{1,0:T(8,128)(2,1)} %get-tuple-element.199), channel_id=1, source_target_pairs={{0,16},{16,0},{1,17},{17,1},{2,18},{18,2},{3,19},{19,3},{4,20},{20... | collective-permute-start | bytes 10616840 | tf_op jit(solution)/shard_map/ppermute | solution.py:1103
  219.8 9.8 %collective-permute-start.16 = (bf16[256,1536]{1,0:T(8,128)(2,1)S(1)}, bf16[256,1536]{1,0:T(8,128)(2,1)S(1)}, u32[]{:S(2)}, u32[]{:S(2)}) collective-permute-start(bf16[256,1536]{1,0:T(8,128)(2,1)S(1)} %get-tuple-element.173.refs_1_.refs_0_), channel_id=1, source_target_pairs={{0,1},{1,0},{2,3},{3,2},{4,5},{5,4},{6,7},{7,6},{8,9},{9,8},{10,11... | collective-permute-start | bytes 2359304 | tf_op jit(solution)/shard_map/ppermute | solution.py:48
  219.9 9.7 %collective-permute-start.17 = (bf16[256,1536]{1,0:T(8,128)(2,1)S(1)}, bf16[256,1536]{1,0:T(8,128)(2,1)S(1)}, u32[]{:S(2)}, u32[]{:S(2)}) collective-permute-start(bf16[256,1536]{1,0:T(8,128)(2,1)S(1)} %get-tuple-element.174.refs_2_.refs_1_), channel_id=1, source_target_pairs={{0,1},{1,0},{2,3},{3,2},{4,5},{5,4},{6,7},{7,6},{8,9},{9,8},{10,11... | collective-permute-start | bytes 2359304 | tf_op jit(solution)/shard_map/ppermute | solution.py:48
  220.4 31.2 %collective-permute-start.19 = (bf16[384,1280]{1,0:T(8,128)(2,1)S(1)}, bf16[384,1280]{1,0:T(8,128)(2,1)S(1)}, u32[]{:S(2)}, u32[]{:S(2)}) collective-permute-start(bf16[384,1280]{1,0:T(8,128)(2,1)S(1)} %get-tuple-element.182), channel_id=1, source_target_pairs={{0,4},{4,0},{8,12},{12,8},{1,5},{5,1},{9,13},{13,9},{2,6},{6,2},{1... | collective-permute-start | bytes 2949128 | tf_op jit(solution)/shard_map/ppermute | solution.py:1108
  240.4 12.3 %collective-permute-start.18 = (bf16[2,1536,128]{2,1,0:T(8,128)(2,1)S(1)}, bf16[2,1536,128]{2,1,0:T(8,128)(2,1)S(1)}, u32[]{:S(2)}, u32[]{:S(2)}) collective-permute-start(bf16[2,1536,128]{2,1,0:T(8,128)(2,1)S(1)} %get-tuple-element.180), channel_id=1, source_target_pairs={{0,1},{1,0},{2,3},{3,2},{4,5},{5,4},{6,7},{7,6},{8,9},{9,8},{10,11... | collective-permute-start | bytes 2359304 | tf_op jit(solution)/shard_map/ppermute | solution.py:48
  252.9 9.8 %collective-permute-start.22 = (bf16[2,512,128]{2,1,0:T(8,128)(2,1)S(1)}, bf16[2,512,128]{2,1,0:T(8,128)(2,1)S(1)}, u32[]{:S(2)}, u32[]{:S(2)}) collective-permute-start(bf16[2,512,128]{2,1,0:T(8,128)(2,1)S(1)} %get-tuple-element.194), channel_id=1, source_target_pairs={{4,0},{8,4},{12,8},{5,1},{9,5},{13,9},{6,2},{10,6},{14,10},{7,3},{... | collective-permute-start | bytes 786440 | tf_op jit(solution)/shard_map/ppermute | solution.py:66
  262.8 12.5 %collective-permute-start.23 = (bf16[2,512,128]{2,1,0:T(8,128)(2,1)S(1)}, bf16[2,512,128]{2,1,0:T(8,128)(2,1)S(1)}, u32[]{:S(2)}, u32[]{:S(2)}) collective-permute-start(bf16[2,512,128]{2,1,0:T(8,128)(2,1)S(1)} %get-tuple-element.196), channel_id=1, source_target_pairs={{4,0},{8,4},{12,8},{5,1},{9,5},{13,9},{6,2},{10,6},{14,10},{7,3},{... | collective-permute-start | bytes 786440 | tf_op jit(solution)/shard_map/ppermute | solution.py:66
  279.3 4.3 collective-permute-start.25
  279.3 4.3 collective-permute-start.26
  279.8 24.9 %collective-permute-start.27 = (bf16[192,1280]{1,0:T(8,128)(2,1)}, bf16[192,1280]{1,0:T(8,128)(2,1)}, u32[]{:S(2)}, u32[]{:S(2)}) collective-permute-start(bf16[192,1280]{1,0:T(8,128)(2,1)} %get-tuple-element.206), channel_id=1, source_target_pairs={{0,8},{4,12},{8,0},{12,4},{1,9},{5,13},{9,1},{13,5},{2,10},{6,14},... | collective-permute-start | bytes 1474568 | tf_op jit(solution)/shard_map/ppermute | solution.py:1113
  317.3 63.0 %collective-permute-start.34 = (bf16[768,1792]{1,0:T(8,128)(2,1)}, bf16[768,1792]{1,0:T(8,128)(2,1)}, u32[]{:S(2)}, u32[]{:S(2)}) collective-permute-start(bf16[768,1792]{1,0:T(8,128)(2,1)} %copy-done.84), channel_id=1, source_target_pairs={{0,16},{16,0},{1,17},{17,1},{2,18},{18,2},{3,19},{19,3},{4,20},{20... | collective-permute-start | bytes 8257544 | tf_op jit(solution)/shard_map/ppermute | solution.py:1103
  317.4 12.8 %collective-permute-start.20 = (bf16[256,1536]{1,0:T(8,128)(2,1)}, bf16[256,1536]{1,0:T(8,128)(2,1)S(1)}, u32[]{:S(2)}, u32[]{:S(2)}) collective-permute-start(bf16[256,1536]{1,0:T(8,128)(2,1)} %copy-done.88), channel_id=1, source_target_pairs={{0,1},{1,0},{2,3},{3,2},{4,5},{5,4},{6,7},{7,6},{8,9},{9,8},{10,11... | collective-permute-start | bytes 2359304 | tf_op jit(solution)/shard_map/ppermute | solution.py:48
  317.5 12.7 %collective-permute-start.21 = (bf16[256,1536]{1,0:T(8,128)(2,1)}, bf16[256,1536]{1,0:T(8,128)(2,1)S(1)}, u32[]{:S(2)}, u32[]{:S(2)}) collective-permute-start(bf16[256,1536]{1,0:T(8,128)(2,1)} %copy-done.87), channel_id=1, source_target_pairs={{0,1},{1,0},{2,3},{3,2},{4,5},{5,4},{6,7},{7,6},{8,9},{9,8},{10,11... | collective-permute-start | bytes 2359304 | tf_op jit(solution)/shard_map/ppermute | solution.py:48
  318.4 20.7 %collective-permute-start.30 = (bf16[256,1536]{1,0:T(8,128)(2,1)S(1)}, bf16[256,1536]{1,0:T(8,128)(2,1)S(1)}, u32[]{:S(2)}, u32[]{:S(2)}) collective-permute-start(bf16[256,1536]{1,0:T(8,128)(2,1)S(1)} %copy-done.79), channel_id=1, source_target_pairs={{0,2},{1,3},{2,0},{3,1},{4,6},{5,7},{6,4},{7,5},{8,10},{9,11},{10,... | collective-permute-start | bytes 2359304 | tf_op jit(solution)/shard_map/ppermute | solution.py:52
  319.9 34.4 %collective-permute-start.31 = (bf16[256,1536]{1,0:T(8,128)(2,1)}, bf16[256,1536]{1,0:T(8,128)(2,1)S(1)}, u32[]{:S(2)}, u32[]{:S(2)}) collective-permute-start(bf16[256,1536]{1,0:T(8,128)(2,1)} %copy-done.80), channel_id=1, source_target_pairs={{0,2},{1,3},{2,0},{3,1},{4,6},{5,7},{6,4},{7,5},{8,10},{9,11},{10,... | collective-permute-start | bytes 2359304 | tf_op jit(solution)/shard_map/ppermute | solution.py:52
  358.6 31.2 %collective-permute-start.32 = (f32[256,1536]{1,0:T(8,128)S(1)}, f32[256,1536]{1,0:T(8,128)S(1)}, u32[]{:S(2)}, u32[]{:S(2)}) collective-permute-start(f32[256,1536]{1,0:T(8,128)S(1)} %get-tuple-element.215.refs_1_), channel_id=1, source_target_pairs={{0,1},{1,0},{2,3},{3,2},{4,5},{5,4},{6,7},{7,6},{8,9},{9,8},{10,11... | collective-permute-start | bytes 4718600 | tf_op jit(solution)/shard_map/ppermute | solution.py:48
  358.7 31.1 %collective-permute-start.33 = (f32[256,1536]{1,0:T(8,128)S(1)}, f32[256,1536]{1,0:T(8,128)S(1)}, u32[]{:S(2)}, u32[]{:S(2)}) collective-permute-start(f32[256,1536]{1,0:T(8,128)S(1)} %get-tuple-element.216.refs_2_), channel_id=1, source_target_pairs={{0,1},{1,0},{2,3},{3,2},{4,5},{5,4},{6,7},{7,6},{8,9},{9,8},{10,11... | collective-permute-start | bytes 4718600 | tf_op jit(solution)/shard_map/ppermute | solution.py:48
  359.2 50.5 %collective-permute-start.37 = (bf16[768,896]{1,0:T(8,128)(2,1)}, bf16[768,896]{1,0:T(8,128)(2,1)S(1)}, u32[]{:S(2)}, u32[]{:S(2)}) collective-permute-start(bf16[768,896]{1,0:T(8,128)(2,1)} %get-tuple-element.223), channel_id=1, source_target_pairs={{0,16},{16,0},{1,17},{17,1},{2,18},{18,2},{3,19},{19,3},{4,20},{20... | collective-permute-start | bytes 4128776 | tf_op jit(solution)/shard_map/ppermute | solution.py:1103
  361.0 32.0 %collective-permute-start.28 = (bf16[256,1536]{1,0:T(8,128)(2,1)}, bf16[256,1536]{1,0:T(8,128)(2,1)S(1)}, u32[]{:S(2)}, u32[]{:S(2)}) collective-permute-start(bf16[256,1536]{1,0:T(8,128)(2,1)} %get-tuple-element.209.refs_1_), channel_id=1, source_target_pairs={{0,2},{1,3},{2,0},{3,1},{4,6},{5,7},{6,4},{7,5},{8,10},{9,11},{10,... | collective-permute-start | bytes 2359304 | tf_op jit(solution)/shard_map/ppermute | solution.py:52
  380.3 17.0 %collective-permute-start.29 = (bf16[256,1536]{1,0:T(8,128)(2,1)}, bf16[256,1536]{1,0:T(8,128)(2,1)S(1)}, u32[]{:S(2)}, u32[]{:S(2)}) collective-permute-start(bf16[256,1536]{1,0:T(8,128)(2,1)} %get-tuple-element.210.refs_2_), channel_id=1, source_target_pairs={{0,2},{1,3},{2,0},{3,1},{4,6},{5,7},{6,4},{7,5},{8,10},{9,11},{10,... | collective-permute-start | bytes 2359304 | tf_op jit(solution)/shard_map/ppermute | solution.py:52
  389.8 39.4 %collective-permute-start.40 = (bf16[384,1792]{1,0:T(8,128)(2,1)}, bf16[384,1792]{1,0:T(8,128)(2,1)S(1)}, u32[]{:S(2)}, u32[]{:S(2)}) collective-permute-start(bf16[384,1792]{1,0:T(8,128)(2,1)} %get-tuple-element.232), channel_id=1, source_target_pairs={{0,4},{4,0},{8,12},{12,8},{1,5},{5,1},{9,13},{13,9},{2,6},{6,2},{1... | collective-permute-start | bytes 4128776 | tf_op jit(solution)/shard_map/ppermute | solution.py:1108
  400.9 14.7 %collective-permute-start.35 = (bf16[256,1536]{1,0:T(8,128)(2,1)S(1)}, bf16[256,1536]{1,0:T(8,128)(2,1)S(1)}, u32[]{:S(2)}, u32[]{:S(2)}) collective-permute-start(bf16[256,1536]{1,0:T(8,128)(2,1)S(1)} %get-tuple-element.221.refs_1_), channel_id=1, source_target_pairs={{0,1},{1,0},{2,3},{3,2},{4,5},{5,4},{6,7},{7,6},{8,9},{9,8},{10,11... | collective-permute-start | bytes 2359304 | tf_op jit(solution)/shard_map/ppermute | solution.py:48
  401.0 14.7 %collective-permute-start.36 = (bf16[256,1536]{1,0:T(8,128)(2,1)S(1)}, bf16[256,1536]{1,0:T(8,128)(2,1)S(1)}, u32[]{:S(2)}, u32[]{:S(2)}) collective-permute-start(bf16[256,1536]{1,0:T(8,128)(2,1)S(1)} %get-tuple-element.222.refs_2_), channel_id=1, source_target_pairs={{0,1},{1,0},{2,3},{3,2},{4,5},{5,4},{6,7},{7,6},{8,9},{9,8},{10,11... | collective-permute-start | bytes 2359304 | tf_op jit(solution)/shard_map/ppermute | solution.py:48
  401.5 27.9 %collective-permute-start.39 = (bf16[768,512]{1,0:T(8,128)(2,1)S(1)}, bf16[768,512]{1,0:T(8,128)(2,1)S(1)}, u32[]{:S(2)}, u32[]{:S(2)}) collective-permute-start(bf16[768,512]{1,0:T(8,128)(2,1)S(1)} %copy-done.86), channel_id=1, source_target_pairs={{0,16},{16,0},{1,17},{17,1},{2,18},{18,2},{3,19},{19,3},{4,20},{20... | collective-permute-start | bytes 2359304 | tf_op jit(solution)/shard_map/ppermute | solution.py:1103
  415.5 30.8 %collective-permute-start.38 = (bf16[384,896]{1,0:T(8,128)(2,1)S(1)}, bf16[384,896]{1,0:T(8,128)(2,1)S(1)}, u32[]{:S(2)}, u32[]{:S(2)}) collective-permute-start(bf16[384,896]{1,0:T(8,128)(2,1)S(1)} %get-tuple-element.229), channel_id=1, source_target_pairs={{0,4},{4,0},{8,12},{12,8},{1,5},{5,1},{9,13},{13,9},{2,6},{6,2},{1... | collective-permute-start | bytes 2064392 | tf_op jit(solution)/shard_map/ppermute | solution.py:1108
  429.3 39.7 %collective-permute-start.45 = (bf16[192,1792]{1,0:T(8,128)(2,1)S(1)}, bf16[192,1792]{1,0:T(8,128)(2,1)S(1)}, u32[]{:S(2)}, u32[]{:S(2)}) collective-permute-start(bf16[192,1792]{1,0:T(8,128)(2,1)S(1)} %get-tuple-element.243), channel_id=1, source_target_pairs={{0,8},{4,12},{8,0},{12,4},{1,9},{5,13},{9,1},{13,5},{2,10},{6,14},... | collective-permute-start | bytes 2064392 | tf_op jit(solution)/shard_map/ppermute | solution.py:1113
  431.5 26.1 %collective-permute-start.43 = (bf16[384,512]{1,0:T(8,128)(2,1)S(1)}, bf16[384,512]{1,0:T(8,128)(2,1)S(1)}, u32[]{:S(2)}, u32[]{:S(2)}) collective-permute-start(bf16[384,512]{1,0:T(8,128)(2,1)S(1)} %get-tuple-element.239), channel_id=1, source_target_pairs={{0,4},{4,0},{8,12},{12,8},{1,5},{5,1},{9,13},{13,9},{2,6},{6,2},{1... | collective-permute-start | bytes 1179656 | tf_op jit(solution)/shard_map/ppermute | solution.py:1108
  433.6 39.1 %collective-permute-start.42 = (bf16[192,1024]{1,0:T(8,128)(2,1)S(1)}, bf16[192,1024]{1,0:T(8,128)(2,1)S(1)}, u32[]{:S(2)}, u32[]{:S(2)}) collective-permute-start(bf16[192,1024]{1,0:T(8,128)(2,1)S(1)} %copy-done.74), channel_id=1, source_target_pairs={{0,16},{16,0},{1,17},{17,1},{2,18},{18,2},{3,19},{19,3},{4,20},{20... | collective-permute-start | bytes 1179656 | tf_op jit(solution)/shard_map/ppermute | solution.py:1135
  447.1 37.0 %collective-permute-start.41 = (bf16[192,896]{1,0:T(8,128)(2,1)}, bf16[192,896]{1,0:T(8,128)(2,1)}, u32[]{:S(2)}, u32[]{:S(2)}) collective-permute-start(bf16[192,896]{1,0:T(8,128)(2,1)} %get-tuple-element.236), channel_id=1, source_target_pairs={{0,8},{4,12},{8,0},{12,4},{1,9},{5,13},{9,1},{13,5},{2,10},{6,14},... | collective-permute-start | bytes 1032200 | tf_op jit(solution)/shard_map/ppermute | solution.py:1113
  447.1 3.7 collective-permute-start.44
  470.5 19.6 %collective-permute-start.48 = (bf16[192,512]{1,0:T(8,128)(2,1)}, bf16[192,512]{1,0:T(8,128)(2,1)S(1)}, u32[]{:S(2)}, u32[]{:S(2)}) collective-permute-start(bf16[192,512]{1,0:T(8,128)(2,1)} %get-tuple-element.252), channel_id=1, source_target_pairs={{0,8},{4,12},{8,0},{12,4},{1,9},{5,13},{9,1},{13,5},{2,10},{6,14},... | collective-permute-start | bytes 589832 | tf_op jit(solution)/shard_map/ppermute | solution.py:1113
  470.5 17.1 %collective-permute-start.46 = (f32[8,512]{1,0:T(8,128)S(1)}, f32[8,512]{1,0:T(8,128)}, u32[]{:S(2)}, u32[]{:S(2)}) collective-permute-start(f32[8,512]{1,0:T(8,128)S(1)} %get-tuple-element.248.refs_0_), channel_id=1, source_target_pairs={{0,4},{4,0},{8,12},{12,8},{1,5},{5,1},{9,13},{13,9},{2,6},{6,2},{1... | collective-permute-start | bytes 49160 | tf_op jit(solution)/shard_map/ppermute | solution.py:1238
  488.3 6.0 %collective-permute-start.47 = (f32[8,512]{1,0:T(8,128)S(1)}, f32[8,512]{1,0:T(8,128)S(1)}, u32[]{:S(2)}, u32[]{:S(2)}) collective-permute-start(f32[8,512]{1,0:T(8,128)S(1)} %get-tuple-element.250), channel_id=1, source_target_pairs={{0,8},{4,12},{8,0},{12,4},{1,9},{5,13},{9,1},{13,5},{2,10},{6,14},... | collective-permute-start | bytes 49160 | tf_op jit(solution)/shard_map/ppermute | solution.py:1247
  495.7 7.2 %collective-permute-start.50 = (f32[2,200,128]{2,1,0:T(8,128)S(1)}, f32[2,200,128]{2,1,0:T(8,128)S(1)}, u32[]{:S(2)}, u32[]{:S(2)}) collective-permute-start(f32[2,200,128]{2,1,0:T(8,128)S(1)} %maximum_select_fusion.1), channel_id=1, source_target_pairs={{0,2},{1,3},{2,0},{3,1},{4,6},{5,7},{6,4},{7,5},{8,10},{9,11},{10,... | collective-permute-start | bytes 614408 | tf_op jit(solution)/shard_map/ppermute | solution.py:52
  (113 other events, 1270.7 us)
Sparse Core Ops, SparseCore 0:
  135.5 72.2 reduce-scatter.2
  317.4 64.6 reduce-scatter.4

commit v15 on v12

--- a/solution.py
+++ b/solution.py
@@ -1080,7 +1080,7 @@
     units = gate_t.shape[0]
     tiles = -(-units // TILE)
     cut = (tiles + 1) // 2
-    long = max(tiles - 2, 1)
+    long = -(-2 * tiles // 3)
     one, two = seq_index ^ 1, seq_index ^ 2
     three = seq_index ^ 3
     quad = jnp.stack([one, three, seq_index, two])

time: 515 us -> 501 us (0.973)
  waiting for transfers between devices: 149 us -> 138 us
    ppermute x4, waiting for transfers between devices: 27.5 us -> 11 us  [relay(): self.last = lax.ppermute(sent, 'seq', flipped('seq', 1))]
    ppermute x9, waiting for transfers between devices: 30.2 us -> 38.7 us  [chip_swap(): return lax.ppermute(value, 'tensor', flipped('tensor', 1))]
    ppermute x5, waiting for transfers between devices: 28.9 us -> 20.7 us  [__init__(): self.come = lax.ppermute(sent, 'dp', flipped('dp', 0))]
    ppermute x4, starting transfers between devices: 17.4 us -> 10.5 us  [own(): self.come = lax.ppermute(send, 'seq', flipped('seq', 0))]
    unnamed x225 -> x213, local copies, waits for them, and re-layouts: 74.1 us -> 74.7 us
  transfers between devices with their start and end apart: 53 -> 53, of which waited for: 26 -> 27; matrix products, arithmetic and copies ran while one was open for 3% -> 3% of each run, Pallas kernels for 28% -> 29%
where the time goes in v15:
time: 501 us; the launch traced here: 499 us
  Pallas kernels  198 us (40%)
  waiting for transfers between devices  138 us (28%)
  local copies, waits for them, and re-layouts  84.9 us (17%)
  starting transfers between devices  53.1 us (11%)
  between operations  15.4 us (3%)
  other arithmetic  9.38 us (2%)
    pallas_call x44, Pallas kernels, __call__(): pl.pallas_call(run, grid_spec=pltpu.PrefetchScalarGridSpec(num_scalar_pre...  189 us
    unnamed x213, local copies, waits for them, and re-layouts  74.7 us
    ppermute x9, waiting for transfers between devices, chip_swap(): return lax.ppermute(value, 'tensor', flipped('tensor', 1))  38.7 us
    ppermute x4, waiting for transfers between devices, own(): self.come = lax.ppermute(send, 'seq', flipped('seq', 0))  30.9 us
    ppermute x5, waiting for transfers between devices, __init__(): self.come = lax.ppermute(sent, 'dp', flipped('dp', 0))  20.7 us
    ppermute x4, waiting for transfers between devices, shifted(): return lax.ppermute(value, 'seq', route)  19.8 us
    ppermute x21, waiting for transfers between devices, core_swap(): return lax.ppermute(value, 'tensor', flipped('tensor', 0))  13.8 us
    ppermute x4, starting transfers between devices, shifted(): return lax.ppermute(value, 'seq', route)  13 us
  transfers between devices with their start and end apart: 53, of which 27 were waited for; matrix products, arithmetic and copies ran while one was open for 3% of the time, Pallas kernels for 29%

profile of v15, /device:TPU:0, one launch (start us, length us, event | category | flops | bytes accessed | tf_op | source)
XLA Modules:
  0.0 498.9 jit_solution(13338678907253117031)
XLA Ops:
  17.2 3.6 first.1
  23.4 5.6 %collective-permute-start.1 = (bf16[2,512,128]{2,1,0:T(8,128)(2,1)S(1)}, bf16[2,512,128]{2,1,0:T(8,128)(2,1)}, u32[]{:S(2)}, u32[]{:S(2)}) collective-permute-start(bf16[2,512,128]{2,1,0:T(8,128)(2,1)S(1)} %bitcast.77), channel_id=1, source_target_pairs={{0,4},{4,8},{8,12},{1,5},{5,9},{9,13},{2,6},{6,10},{10,14},{3,7},{... | collective-permute-start | bytes 786440 | tf_op jit(solution)/shard_map/ppermute | solution.py:66
  29.1 4.5 collective-permute-start
  34.6 4.3 collective-permute-done.refs_0_.refs_9_
  41.9 6.1 %attend.1 = (bf16[2,512,384]{2,1,0:T(8,128)(2,1)S(1)}, f32[2,2,768]{2,1,0:T(2,128)S(1)}) custom-call(s32[2,2]{1,0:T(2,128)S(1)} %shift-right-logical_maximum_fusion.low_ref.refs_0_, s32[1]{0:T(128)} %bitcast.core_ref.refs_0_.refs_1_, bf16[2,512,384]{2,1,0:T(8,128)(2,1)S(1)} %bitcast.74, s32[2,1,512]{2,1,0:T(1,128)S(1)} %sub.44.start_ref.refs_3_, ...), custom_call_target="tpu_custom_call" | custom-call | flops 8000000 | bytes 4194 | tf_op jit(solution)/shard_map/attend/pallas_call | solution.py:253
  53.6 3.4 narrow.9
  60.4 4.5 constant_dynamic-slice_fusion.2
  74.6 5.2 %copy-done.9 = bf16[1536,2240]{0,1:T(8,128)(2,1)S(1)} copy-done((bf16[1536,2240]{0,1:T(8,128)(2,1)S(1)}, bf16[1536,2240]{0,1:T(8,128)(2,1)}, u32[]{:S(2)}) %copy-start.9) | copy-done | bytes 6881304
  79.8 9.3 %grad_hidden.1 = (bf16[1024,2240]{1,0:T(8,128)(2,1)S(1)}, f32[8,128]{1,0:T(8,128)S(1)}) custom-call(bf16[1024,1536]{1,0:T(8,128)(2,1)S(1)} %get-tuple-element.146.refs_0_.refs_3_, bf16[2240,1536]{1,0:T(8,128)(2,1)S(1)} %bitcast.61, f32[8,128]{1,0:T(8,128)S(1)} %get-tuple-element.147.refs_2_, bf16[192,2240]{1,0:T(8,128)(2,1)S(1)} %copy-done.40, ...), custom_call_target="tpu_custom_call" | custom-call | flops 7046430 | bytes 15728 | tf_op jit(solution)/shard_map/grad_hidden/pallas_call | solution.py:92
  94.5 3.8 middle.1
  104.1 20.3 %gated.1 = (bf16[1024,2240]{1,0:T(8,128)(2,1)S(1)}, bf16[1024,2240]{1,0:T(8,128)(2,1)S(1)}, bf16[1024,2240]{1,0:T(8,128)(2,1)S(1)}, f32[8,128]{1,0:T(8,128)S(1)}) custom-call(bf16[1024,2240]{1,0:T(8,128)(2,1)S(1)} %copy-done.49, bf16[2240,1536]{1,0:T(8,128)(2,1)} %bitcast.58, bf16[2240,1536]{1,0:T(8,128)(2,1)} %bitcast.83, ...), custom_call_target="tpu_custom_call" | custom-call | flops 14092861 | bytes 31457 | tf_op jit(solution)/shard_map/gated/pallas_call | solution.py:92
  126.6 4.8 share.9
  139.8 4.2 share.10
  150.8 10.4 %narrow.10 = (bf16[256,1536]{1,0:T(8,128)(2,1)S(1)}, bf16[256,1536]{1,0:T(8,128)(2,1)S(1)}, f32[8,128]{1,0:T(8,128)S(1)}) custom-call(bf16[1024,2240]{1,0:T(8,128)(2,1)S(1)} %copy-done.5, bf16[2240,1536]{1,0:T(8,128)(2,1)S(1)} %bitcast.59, bf16[1024,2240]{1,0:T(8,128)(2,1)S(1)} %bitcast.47, bf16[2240,1536]{1,0:T(8,128)(2,1)} %bitcast.84, ...), custom_call_target="tpu_custom_call" | custom-call | flops 7046430 | bytes 19922 | tf_op jit(solution)/shard_map/narrow/pallas_call | solution.py:92
  164.7 3.2 copy-done.8
  167.8 11.0 %narrow.11 = (bf16[256,1536]{1,0:T(8,128)(2,1)}, bf16[256,1536]{1,0:T(8,128)(2,1)}, f32[8,128]{1,0:T(8,128)S(1)}) custom-call(bf16[1024,2240]{1,0:T(8,128)(2,1)S(1)} %bitcast.55, bf16[2240,1536]{1,0:T(8,128)(2,1)S(1)} %bitcast.60, bf16[1024,2240]{1,0:T(8,128)(2,1)S(1)} %bitcast.47, bf16[2240,1536]{1,0:T(8,128)(2,1)} %bitcast.85, ...), custom_call_target="tpu_custom_call" | custom-call | flops 7046430 | bytes 19922 | tf_op jit(solution)/shard_map/narrow/pallas_call | solution.py:92
  182.4 13.9 %share.11 = (bf16[768,2304]{1,0:T(8,128)(2,1)}, bf16[768,1536]{1,0:T(8,128)(2,1)S(1)}, bf16[768,768]{1,0:T(8,128)(2,1)}, f32[8,128]{1,0:T(8,128)S(1)}) custom-call(s32[1]{0:T(128)} %bitcast.10.refs_0_, s32[1]{0:T(128)} %constant.59.clone.1.refs_0_.refs_1_, bf16[1536,1024]{1,0:T(8,128)(2,1)S(1)} %get-tuple-element.169.refs_2_, ...), custom_call_target="tpu_custom_call" | custom-call | flops 7247757 | bytes 18087 | tf_op jit(solution)/shard_map/share/pallas_call | solution.py:92
  202.6 5.9 %share.12 = (bf16[384,1280]{1,0:T(8,128)(2,1)S(1)}, bf16[384,1280]{1,0:T(8,128)(2,1)S(1)}, f32[8,128]{1,0:T(8,128)S(1)}) custom-call(s32[1]{0:T(128)} %bitcast.11.refs_0_, s32[4]{0:T(128)S(1)} %pad_add_fusion.refs_1_, bf16[1536,1024]{1,0:T(8,128)(2,1)S(1)} %copy-done.18, bf16[1024,2240]{1,0:T(8,128)(2,1)S(1)} %copy-done.3, ...), custom_call_target="tpu_custom_call" | custom-call | flops 2013265 | bytes 6160 | tf_op jit(solution)/shard_map/share/pallas_call | solution.py:92
  208.6 7.0 %collective-permute-done.14.refs_7_ = bf16[256,1536]{1,0:T(8,128)(2,1)} collective-permute-done((bf16[256,1536]{1,0:T(8,128)(2,1)}, bf16[256,1536]{1,0:T(8,128)(2,1)}, u32[]{:S(2)}, u32[]{:S(2)}) %collective-permute-start.14) | collective-permute-done | bytes 786464 | tf_op jit(solution)/shard_map/ppermute | solution.py:52
  215.6 4.1 norm_back.2
  220.4 8.6 %collective-permute-start.19 = (bf16[384,1280]{1,0:T(8,128)(2,1)S(1)}, bf16[384,1280]{1,0:T(8,128)(2,1)S(1)}, u32[]{:S(2)}, u32[]{:S(2)}) collective-permute-start(bf16[384,1280]{1,0:T(8,128)(2,1)S(1)} %get-tuple-element.182), channel_id=1, source_target_pairs={{0,4},{4,0},{8,12},{12,8},{1,5},{5,1},{9,13},{13,9},{2,6},{6,2},{1... | collective-permute-start | bytes 2949128 | tf_op jit(solution)/shard_map/ppermute | solution.py:1108
  230.9 8.9 %attend_back.1 = (bf16[2,512,384]{2,1,0:T(8,128)(2,1)S(1)}, bf16[2,1536,128]{2,1,0:T(8,128)(2,1)S(1)}, bf16[2,1536,128]{2,1,0:T(8,128)(2,1)S(1)}, f32[8,128]{1,0:T(8,128)S(1)}) custom-call(s32[2,2]{1,0:T(2,128)S(1)} %shift-right-logical_maximum_fusion.low_ref.refs_0_, s32[1]{0:T(128)} %bitcast.core_ref.refs_0_.refs_1_, bf16[2,512,384]{2,1,0:T(8,128)(2,1)S(1)} %bitcast.75, ...), custom_call_target="tpu_custom_call" | custom-call | flops 20000000 | bytes 6291 | tf_op jit(solution)/shard_map/attend_back/pallas_call | solution.py:92
  243.0 8.0 %collective-permute-done.19.refs_1_ = bf16[384,1280]{1,0:T(8,128)(2,1)S(1)} collective-permute-done((bf16[384,1280]{1,0:T(8,128)(2,1)S(1)}, bf16[384,1280]{1,0:T(8,128)(2,1)S(1)}, u32[]{:S(2)}, u32[]{:S(2)}) %collective-permute-start.19) | collective-permute-done | bytes 983072 | tf_op jit(solution)/shard_map/ppermute | solution.py:1108
  254.3 5.3 %narrow.12 = (bf16[256,1536]{1,0:T(8,128)(2,1)S(1)}, bf16[256,1536]{1,0:T(8,128)(2,1)S(1)}, f32[8,128]{1,0:T(8,128)S(1)}) custom-call(bf16[1024,2240]{1,0:T(8,128)(2,1)S(1)} %bitcast.51, bf16[2240,1536]{1,0:T(8,128)(2,1)S(1)} %bitcast.64, f32[8,128]{1,0:T(8,128)S(1)} %get-tuple-element.186.refs_2_), custom_call_target="tpu_custom_call" | custom-call | flops 3523215 | bytes 10747 | tf_op jit(solution)/shard_map/narrow/pallas_call | solution.py:92
  264.3 12.2 %collective-permute-done.23.refs_5_ = bf16[2,512,128]{2,1,0:T(8,128)(2,1)S(1)} collective-permute-done((bf16[2,512,128]{2,1,0:T(8,128)(2,1)S(1)}, bf16[2,512,128]{2,1,0:T(8,128)(2,1)S(1)}, u32[]{:S(2)}, u32[]{:S(2)}) %collective-permute-start.23) | collective-permute-done | bytes 262176 | tf_op jit(solution)/shard_map/ppermute | solution.py:66
  277.2 3.4 narrow.13
  284.4 4.6 narrow.14
  293.1 8.3 %share.13 = (bf16[768,2304]{1,0:T(8,128)(2,1)S(1)}, f32[8,128]{1,0:T(8,128)S(1)}) custom-call(s32[1]{0:T(128)} %bitcast.11.refs_0_, s32[1]{0:T(128)} %constant.59.clone.1.refs_0_.refs_1_, bf16[1536,1024]{1,0:T(8,128)(2,1)S(1)} %copy-done.12, bf16[1024,2240]{1,0:T(8,128)(2,1)S(1)} %copy-done.6, bf16[768,2304]{1,0:T(8,128)(2,1)} %collective-permute-done.24.refs_4_, ...), custom_call_target="tpu_custom_call" | custom-call | flops 3623878 | bytes 9830 | tf_op jit(solution)/shard_map/share/pallas_call | solution.py:92
  310.8 5.3 %share.14 = (bf16[768,896]{1,0:T(8,128)(2,1)}, f32[8,128]{1,0:T(8,128)S(1)}) custom-call(s32[1]{0:T(128)} %bitcast.10.refs_0_, s32[1]{0:T(128)} %constant.59.clone.1.refs_0_.refs_1_, bf16[1536,1024]{1,0:T(8,128)(2,1)S(1)} %copy-done.24, bf16[1536,1024]{1,0:T(8,128)(2,1)S(1)} %copy-done.30, bf16[1024,512]{1,0:T(8,128)(2,1)S(1)} %get-tuple-element.198.refs_0_.refs_4_, ...), custom_call_target="tpu_custom_call" | custom-call | flops 1409286 | bytes 4784 | tf_op jit(solution)/shard_map/share/pallas_call | solution.py:92
  316.1 3.0 copy-done.10
  319.2 6.0 %narrow.15 = (bf16[256,1536]{1,0:T(8,128)(2,1)}, bf16[256,1536]{1,0:T(8,128)(2,1)}, f32[8,128]{1,0:T(8,128)S(1)}) custom-call(bf16[1024,2240]{1,0:T(8,128)(2,1)S(1)} %bitcast.53, bf16[2240,1536]{1,0:T(8,128)(2,1)S(1)} %bitcast.65, bf16[256,1536]{1,0:T(8,128)(2,1)S(1)} %collective-permute-done.20.refs_2_, ...), custom_call_target="tpu_custom_call" | custom-call | flops 3523215 | bytes 10747 | tf_op jit(solution)/shard_map/narrow/pallas_call | solution.py:92
  325.2 15.6 %collective-permute-done.30.refs_7_ = bf16[256,1536]{1,0:T(8,128)(2,1)S(1)} collective-permute-done((bf16[256,1536]{1,0:T(8,128)(2,1)}, bf16[256,1536]{1,0:T(8,128)(2,1)S(1)}, u32[]{:S(2)}, u32[]{:S(2)}) %collective-permute-start.30) | collective-permute-done | bytes 786464 | tf_op jit(solution)/shard_map/ppermute | solution.py:52
  348.5 9.3 %collective-permute-done.33.refs_4_ = bf16[768,1536]{1,0:T(8,128)(2,1)} collective-permute-done((bf16[768,1536]{1,0:T(8,128)(2,1)}, bf16[768,1536]{1,0:T(8,128)(2,1)}, u32[]{:S(2)}, u32[]{:S(2)}) %collective-permute-start.33) | collective-permute-done | bytes 2359328 | tf_op jit(solution)/shard_map/ppermute | solution.py:1103
  359.3 7.0 %share.15 = (bf16[384,1536]{1,0:T(8,128)(2,1)}, bf16[384,1536]{1,0:T(8,128)(2,1)S(1)}, f32[8,128]{1,0:T(8,128)S(1)}) custom-call(s32[1]{0:T(128)} %bitcast.11.refs_0_, s32[4]{0:T(128)S(1)} %pad_add_fusion.refs_1_, bf16[1536,1024]{1,0:T(8,128)(2,1)S(1)} %copy-done.13, bf16[1024,2240]{1,0:T(8,128)(2,1)S(1)} %bitcast.49, ...), custom_call_target="tpu_custom_call" | custom-call | flops 2415919 | bytes 7077 | tf_op jit(solution)/shard_map/share/pallas_call | solution.py:92
  368.8 3.2 place.2
  372.0 11.2 %collective-permute-done.28.refs_4_ = bf16[256,1536]{1,0:T(8,128)(2,1)S(1)} collective-permute-done((bf16[256,1536]{1,0:T(8,128)(2,1)}, bf16[256,1536]{1,0:T(8,128)(2,1)S(1)}, u32[]{:S(2)}, u32[]{:S(2)}) %collective-permute-start.28) | collective-permute-done | bytes 786464 | tf_op jit(solution)/shard_map/ppermute | solution.py:52
  385.3 3.5 layer.1
  392.0 5.8 %share.16 = (bf16[384,896]{1,0:T(8,128)(2,1)S(1)}, bf16[384,896]{1,0:T(8,128)(2,1)S(1)}, f32[8,128]{1,0:T(8,128)S(1)}) custom-call(s32[1]{0:T(128)} %bitcast.11.refs_0_, s32[4]{0:T(128)S(1)} %pad_add_fusion.refs_1_, bf16[1536,1024]{1,0:T(8,128)(2,1)S(1)} %copy-done.25, bf16[1536,1024]{1,0:T(8,128)(2,1)S(1)} %copy-done.31, ...), custom_call_target="tpu_custom_call" | custom-call | flops 1409286 | bytes 4784 | tf_op jit(solution)/shard_map/share/pallas_call | solution.py:92
  400.2 11.4 %collective-permute-done.38.refs_4_ = bf16[768,768]{1,0:T(8,128)(2,1)S(1)} collective-permute-done((bf16[768,768]{1,0:T(8,128)(2,1)}, bf16[768,768]{1,0:T(8,128)(2,1)S(1)}, u32[]{:S(2)}, u32[]{:S(2)}) %collective-permute-start.38) | collective-permute-done | bytes 1179680 | tf_op jit(solution)/shard_map/ppermute | solution.py:1103
  420.5 16.2 %collective-permute-done.37.refs_1_ = bf16[384,896]{1,0:T(8,128)(2,1)S(1)} collective-permute-done((bf16[384,896]{1,0:T(8,128)(2,1)S(1)}, bf16[384,896]{1,0:T(8,128)(2,1)S(1)}, u32[]{:S(2)}, u32[]{:S(2)}) %collective-permute-start.37) | collective-permute-done | bytes 688160 | tf_op jit(solution)/shard_map/ppermute | solution.py:1108
  438.6 3.0 collective-permute-done.44.refs_1_
  441.6 6.7 %collective-permute-done.43.refs_1_.refs_4_ = bf16[384,768]{1,0:T(8,128)(2,1)S(1)} collective-permute-done((bf16[384,768]{1,0:T(8,128)(2,1)S(1)}, bf16[384,768]{1,0:T(8,128)(2,1)S(1)}, u32[]{:S(2)}, u32[]{:S(2)}) %collective-permute-start.43) | collective-permute-done | bytes 589856 | tf_op jit(solution)/shard_map/ppermute | solution.py:1108
  452.7 3.8 finish.4
  457.6 3.7 finish.5
  461.4 6.3 %collective-permute-done.41.refs_2_ = bf16[192,896]{1,0:T(8,128)(2,1)} collective-permute-done((bf16[192,896]{1,0:T(8,128)(2,1)}, bf16[192,896]{1,0:T(8,128)(2,1)}, u32[]{:S(2)}, u32[]{:S(2)}) %collective-permute-start.41) | collective-permute-done | bytes 344096 | tf_op jit(solution)/shard_map/ppermute | solution.py:1113
  467.6 3.5 finish.6
  474.2 5.2 %finish.7 = (f32[192,2240]{1,0:T(8,128)}, f32[192,128]{1,0:T(8,128)S(1)}, f32[8,128]{1,0:T(8,128)}) custom-call(bf16[384,1536]{1,0:T(8,128)(2,1)S(1)} %copy-done.45, bf16[384,1536]{1,0:T(8,128)(2,1)S(1)} %copy-done.47, bf16[192,1536]{1,0:T(8,128)(2,1)S(1)} %copy-done.71, bf16[384,768]{1,0:T(8,128)(2,1)S(1)} %get-tuple-element.238.refs_0_.refs_3_, ...), custom_call_target="tpu_custom_call" | custom-call | bytes 6021 | tf_op jit(solution)/shard_map/finish/pallas_call | solution.py:92
  483.4 4.8 collective-permute-done.50
  (375 shorter events, 154.6 us)
Async XLA Ops:
  7.2 273.9 %reduce-scatter.3.cloned.1.call-start = ((), (), s32[]{:S(2)}) async-start(), calls=%async_computation.2 | async-start | bytes 3932160 | tf_op jit(solution)/shard_map/reduce_scatter | solution.py:1128
  23.4 11.1 %collective-permute-start.1 = (bf16[2,512,128]{2,1,0:T(8,128)(2,1)S(1)}, bf16[2,512,128]{2,1,0:T(8,128)(2,1)}, u32[]{:S(2)}, u32[]{:S(2)}) collective-permute-start(bf16[2,512,128]{2,1,0:T(8,128)(2,1)S(1)} %bitcast.77), channel_id=1, source_target_pairs={{0,4},{4,8},{8,12},{1,5},{5,9},{9,13},{2,6},{6,10},{10,14},{3,7},{... | collective-permute-start | bytes 786440 | tf_op jit(solution)/shard_map/ppermute | solution.py:66
  29.1 9.8 %collective-permute-start = (bf16[2,512,128]{2,1,0:T(8,128)(2,1)S(1)}, bf16[2,512,128]{2,1,0:T(8,128)(2,1)}, u32[]{:S(2)}, u32[]{:S(2)}) collective-permute-start(bf16[2,512,128]{2,1,0:T(8,128)(2,1)S(1)} %bitcast.78), channel_id=1, source_target_pairs={{0,8},{4,12},{1,9},{5,13},{2,10},{6,14},{3,11},{7,15},{16,24},{20,... | collective-permute-start | bytes 786440 | tf_op jit(solution)/shard_map/ppermute | solution.py:66
  33.6 5.4 %collective-permute-start.4 = (bf16[2,512,128]{2,1,0:T(8,128)(2,1)S(1)}, bf16[2,512,128]{2,1,0:T(8,128)(2,1)}, u32[]{:S(2)}, u32[]{:S(2)}) collective-permute-start(bf16[2,512,128]{2,1,0:T(8,128)(2,1)S(1)} %bitcast.79), channel_id=1, source_target_pairs={{0,1},{1,0},{2,3},{3,2},{4,5},{5,4},{6,7},{7,6},{8,9},{9,8},{10,11... | collective-permute-start | bytes 786440 | tf_op jit(solution)/shard_map/ppermute | solution.py:48
  34.6 4.5 collective-permute-start.3
  50.3 3.3 collective-permute-start.6
  57.0 37.4 %collective-permute-start.7 = (bf16[256,1536]{1,0:T(8,128)(2,1)}, bf16[256,1536]{1,0:T(8,128)(2,1)}, u32[]{:S(2)}, u32[]{:S(2)}) collective-permute-start(bf16[256,1536]{1,0:T(8,128)(2,1)} %get-tuple-element.142.refs_3_), channel_id=1, source_target_pairs={{0,2},{1,3},{2,0},{3,1},{4,6},{5,7},{6,4},{7,5},{8,10},{9,11},{10,... | collective-permute-start | bytes 2359304 | tf_op jit(solution)/shard_map/ppermute | solution.py:52
  58.5 35.9 %collective-permute-start.8 = (bf16[256,1536]{1,0:T(8,128)(2,1)}, bf16[256,1536]{1,0:T(8,128)(2,1)}, u32[]{:S(2)}, u32[]{:S(2)}) collective-permute-start(bf16[256,1536]{1,0:T(8,128)(2,1)} %get-tuple-element.143.refs_4_), channel_id=1, source_target_pairs={{0,2},{1,3},{2,0},{3,1},{4,6},{5,7},{6,4},{7,5},{8,10},{9,11},{10,... | collective-permute-start | bytes 2359304 | tf_op jit(solution)/shard_map/ppermute | solution.py:52
  98.4 3.4 collective-permute-start.10
  135.2 321.2 %reduce-scatter.5.cloned.1.call-start = ((), (), s32[]{:S(2)}) async-start(), calls=%async_computation.3 | async-start | bytes 4423680 | tf_op jit(solution)/shard_map/reduce_scatter | solution.py:1148
  144.0 54.4 %collective-permute-start.15 = (bf16[768,1280]{1,0:T(8,128)(2,1)}, bf16[768,1280]{1,0:T(8,128)(2,1)}, u32[]{:S(2)}, u32[]{:S(2)}) collective-permute-start(bf16[768,1280]{1,0:T(8,128)(2,1)} %get-tuple-element.167), channel_id=1, source_target_pairs={{0,16},{16,0},{1,17},{17,1},{2,18},{18,2},{3,19},{19,3},{4,20},{20... | collective-permute-start | bytes 5898248 | tf_op jit(solution)/shard_map/ppermute | solution.py:1103
  161.2 3.4 collective-permute-start.12
  178.9 29.7 %collective-permute-start.13 = (bf16[256,1536]{1,0:T(8,128)(2,1)}, bf16[256,1536]{1,0:T(8,128)(2,1)S(1)}, u32[]{:S(2)}, u32[]{:S(2)}) collective-permute-start(bf16[256,1536]{1,0:T(8,128)(2,1)} %get-tuple-element.165.refs_4_), channel_id=1, source_target_pairs={{0,2},{1,3},{2,0},{3,1},{4,6},{5,7},{6,4},{7,5},{8,10},{9,11},{10,... | collective-permute-start | bytes 2359304 | tf_op jit(solution)/shard_map/ppermute | solution.py:52
  180.3 35.3 %collective-permute-start.14 = (bf16[256,1536]{1,0:T(8,128)(2,1)}, bf16[256,1536]{1,0:T(8,128)(2,1)}, u32[]{:S(2)}, u32[]{:S(2)}) collective-permute-start(bf16[256,1536]{1,0:T(8,128)(2,1)} %get-tuple-element.166.refs_5_), channel_id=1, source_target_pairs={{0,2},{1,3},{2,0},{3,1},{4,6},{5,7},{6,4},{7,5},{8,10},{9,11},{10,... | collective-permute-start | bytes 2359304 | tf_op jit(solution)/shard_map/ppermute | solution.py:52
  197.8 92.1 %collective-permute-start.24 = (bf16[768,2304]{1,0:T(8,128)(2,1)}, bf16[768,2304]{1,0:T(8,128)(2,1)}, u32[]{:S(2)}, u32[]{:S(2)}) collective-permute-start(bf16[768,2304]{1,0:T(8,128)(2,1)} %get-tuple-element.199), channel_id=1, source_target_pairs={{0,16},{16,0},{1,17},{17,1},{2,18},{18,2},{3,19},{19,3},{4,20},{20... | collective-permute-start | bytes 10616840 | tf_op jit(solution)/shard_map/ppermute | solution.py:1103
  219.8 9.2 %collective-permute-start.16 = (bf16[256,1536]{1,0:T(8,128)(2,1)S(1)}, bf16[256,1536]{1,0:T(8,128)(2,1)S(1)}, u32[]{:S(2)}, u32[]{:S(2)}) collective-permute-start(bf16[256,1536]{1,0:T(8,128)(2,1)S(1)} %get-tuple-element.173.refs_1_.refs_0_), channel_id=1, source_target_pairs={{0,1},{1,0},{2,3},{3,2},{4,5},{5,4},{6,7},{7,6},{8,9},{9,8},{10,11... | collective-permute-start | bytes 2359304 | tf_op jit(solution)/shard_map/ppermute | solution.py:48
  219.9 9.1 %collective-permute-start.17 = (bf16[256,1536]{1,0:T(8,128)(2,1)S(1)}, bf16[256,1536]{1,0:T(8,128)(2,1)S(1)}, u32[]{:S(2)}, u32[]{:S(2)}) collective-permute-start(bf16[256,1536]{1,0:T(8,128)(2,1)S(1)} %get-tuple-element.174.refs_2_.refs_1_), channel_id=1, source_target_pairs={{0,1},{1,0},{2,3},{3,2},{4,5},{5,4},{6,7},{7,6},{8,9},{9,8},{10,11... | collective-permute-start | bytes 2359304 | tf_op jit(solution)/shard_map/ppermute | solution.py:48
  220.4 30.6 %collective-permute-start.19 = (bf16[384,1280]{1,0:T(8,128)(2,1)S(1)}, bf16[384,1280]{1,0:T(8,128)(2,1)S(1)}, u32[]{:S(2)}, u32[]{:S(2)}) collective-permute-start(bf16[384,1280]{1,0:T(8,128)(2,1)S(1)} %get-tuple-element.182), channel_id=1, source_target_pairs={{0,4},{4,0},{8,12},{12,8},{1,5},{5,1},{9,13},{13,9},{2,6},{6,2},{1... | collective-permute-start | bytes 2949128 | tf_op jit(solution)/shard_map/ppermute | solution.py:1108
  239.8 12.9 %collective-permute-start.18 = (bf16[2,1536,128]{2,1,0:T(8,128)(2,1)S(1)}, bf16[2,1536,128]{2,1,0:T(8,128)(2,1)S(1)}, u32[]{:S(2)}, u32[]{:S(2)}) collective-permute-start(bf16[2,1536,128]{2,1,0:T(8,128)(2,1)S(1)} %get-tuple-element.180), channel_id=1, source_target_pairs={{0,1},{1,0},{2,3},{3,2},{4,5},{5,4},{6,7},{7,6},{8,9},{9,8},{10,11... | collective-permute-start | bytes 2359304 | tf_op jit(solution)/shard_map/ppermute | solution.py:48
  252.9 9.8 %collective-permute-start.22 = (bf16[2,512,128]{2,1,0:T(8,128)(2,1)S(1)}, bf16[2,512,128]{2,1,0:T(8,128)(2,1)S(1)}, u32[]{:S(2)}, u32[]{:S(2)}) collective-permute-start(bf16[2,512,128]{2,1,0:T(8,128)(2,1)S(1)} %get-tuple-element.194), channel_id=1, source_target_pairs={{4,0},{8,4},{12,8},{5,1},{9,5},{13,9},{6,2},{10,6},{14,10},{7,3},{... | collective-permute-start | bytes 786440 | tf_op jit(solution)/shard_map/ppermute | solution.py:66
  262.8 13.8 %collective-permute-start.23 = (bf16[2,512,128]{2,1,0:T(8,128)(2,1)S(1)}, bf16[2,512,128]{2,1,0:T(8,128)(2,1)S(1)}, u32[]{:S(2)}, u32[]{:S(2)}) collective-permute-start(bf16[2,512,128]{2,1,0:T(8,128)(2,1)S(1)} %get-tuple-element.196), channel_id=1, source_target_pairs={{4,0},{8,4},{12,8},{5,1},{9,5},{13,9},{6,2},{10,6},{14,10},{7,3},{... | collective-permute-start | bytes 786440 | tf_op jit(solution)/shard_map/ppermute | solution.py:66
  280.6 2.6 collective-permute-start.25
  280.6 3.7 collective-permute-start.26
  303.3 54.5 %collective-permute-start.33 = (bf16[768,1536]{1,0:T(8,128)(2,1)}, bf16[768,1536]{1,0:T(8,128)(2,1)}, u32[]{:S(2)}, u32[]{:S(2)}) collective-permute-start(bf16[768,1536]{1,0:T(8,128)(2,1)} %copy-done.82), channel_id=1, source_target_pairs={{0,16},{16,0},{1,17},{17,1},{2,18},{18,2},{3,19},{19,3},{4,20},{20... | collective-permute-start | bytes 7077896 | tf_op jit(solution)/shard_map/ppermute | solution.py:1103
  303.3 12.8 %collective-permute-start.20 = (bf16[256,1536]{1,0:T(8,128)(2,1)}, bf16[256,1536]{1,0:T(8,128)(2,1)S(1)}, u32[]{:S(2)}, u32[]{:S(2)}) collective-permute-start(bf16[256,1536]{1,0:T(8,128)(2,1)} %copy-done.84), channel_id=1, source_target_pairs={{0,1},{1,0},{2,3},{3,2},{4,5},{5,4},{6,7},{7,6},{8,9},{9,8},{10,11... | collective-permute-start | bytes 2359304 | tf_op jit(solution)/shard_map/ppermute | solution.py:48
  303.5 12.6 %collective-permute-start.21 = (bf16[256,1536]{1,0:T(8,128)(2,1)}, bf16[256,1536]{1,0:T(8,128)(2,1)S(1)}, u32[]{:S(2)}, u32[]{:S(2)}) collective-permute-start(bf16[256,1536]{1,0:T(8,128)(2,1)} %copy-done.83), channel_id=1, source_target_pairs={{0,1},{1,0},{2,3},{3,2},{4,5},{5,4},{6,7},{7,6},{8,9},{9,8},{10,11... | collective-permute-start | bytes 2359304 | tf_op jit(solution)/shard_map/ppermute | solution.py:48
  304.4 20.8 %collective-permute-start.29 = (bf16[256,1536]{1,0:T(8,128)(2,1)S(1)}, bf16[256,1536]{1,0:T(8,128)(2,1)S(1)}, u32[]{:S(2)}, u32[]{:S(2)}) collective-permute-start(bf16[256,1536]{1,0:T(8,128)(2,1)S(1)} %copy-done.77), channel_id=1, source_target_pairs={{0,2},{1,3},{2,0},{3,1},{4,6},{5,7},{6,4},{7,5},{8,10},{9,11},{10,... | collective-permute-start | bytes 2359304 | tf_op jit(solution)/shard_map/ppermute | solution.py:52
  305.9 34.9 %collective-permute-start.30 = (bf16[256,1536]{1,0:T(8,128)(2,1)}, bf16[256,1536]{1,0:T(8,128)(2,1)S(1)}, u32[]{:S(2)}, u32[]{:S(2)}) collective-permute-start(bf16[256,1536]{1,0:T(8,128)(2,1)} %copy-done.78), channel_id=1, source_target_pairs={{0,2},{1,3},{2,0},{3,1},{4,6},{5,7},{6,4},{7,5},{8,10},{9,11},{10,... | collective-permute-start | bytes 2359304 | tf_op jit(solution)/shard_map/ppermute | solution.py:52
  345.0 21.3 %collective-permute-start.31 = (f32[256,1536]{1,0:T(8,128)S(1)}, f32[256,1536]{1,0:T(8,128)S(1)}, u32[]{:S(2)}, u32[]{:S(2)}) collective-permute-start(f32[256,1536]{1,0:T(8,128)S(1)} %get-tuple-element.214.refs_1_), channel_id=1, source_target_pairs={{0,1},{1,0},{2,3},{3,2},{4,5},{5,4},{6,7},{7,6},{8,9},{9,8},{10,11... | collective-permute-start | bytes 4718600 | tf_op jit(solution)/shard_map/ppermute | solution.py:48
  345.1 23.0 %collective-permute-start.32 = (f32[256,1536]{1,0:T(8,128)S(1)}, f32[256,1536]{1,0:T(8,128)S(1)}, u32[]{:S(2)}, u32[]{:S(2)}) collective-permute-start(f32[256,1536]{1,0:T(8,128)S(1)} %get-tuple-element.215.refs_2_), channel_id=1, source_target_pairs={{0,1},{1,0},{2,3},{3,2},{4,5},{5,4},{6,7},{7,6},{8,9},{9,8},{10,11... | collective-permute-start | bytes 4718600 | tf_op jit(solution)/shard_map/ppermute | solution.py:48
  345.6 43.8 %collective-permute-start.36 = (bf16[768,896]{1,0:T(8,128)(2,1)}, bf16[768,896]{1,0:T(8,128)(2,1)S(1)}, u32[]{:S(2)}, u32[]{:S(2)}) collective-permute-start(bf16[768,896]{1,0:T(8,128)(2,1)} %get-tuple-element.222), channel_id=1, source_target_pairs={{0,16},{16,0},{1,17},{17,1},{2,18},{18,2},{3,19},{19,3},{4,20},{20... | collective-permute-start | bytes 4128776 | tf_op jit(solution)/shard_map/ppermute | solution.py:1103
  346.9 25.1 %collective-permute-start.27 = (bf16[256,1536]{1,0:T(8,128)(2,1)}, bf16[256,1536]{1,0:T(8,128)(2,1)S(1)}, u32[]{:S(2)}, u32[]{:S(2)}) collective-permute-start(bf16[256,1536]{1,0:T(8,128)(2,1)} %get-tuple-element.208.refs_1_), channel_id=1, source_target_pairs={{0,2},{1,3},{2,0},{3,1},{4,6},{5,7},{6,4},{7,5},{8,10},{9,11},{10,... | collective-permute-start | bytes 2359304 | tf_op jit(solution)/shard_map/ppermute | solution.py:52
  357.7 25.5 %collective-permute-start.28 = (bf16[256,1536]{1,0:T(8,128)(2,1)}, bf16[256,1536]{1,0:T(8,128)(2,1)S(1)}, u32[]{:S(2)}, u32[]{:S(2)}) collective-permute-start(bf16[256,1536]{1,0:T(8,128)(2,1)} %get-tuple-element.209.refs_2_), channel_id=1, source_target_pairs={{0,2},{1,3},{2,0},{3,1},{4,6},{5,7},{6,4},{7,5},{8,10},{9,11},{10,... | collective-permute-start | bytes 2359304 | tf_op jit(solution)/shard_map/ppermute | solution.py:52
  366.3 33.8 %collective-permute-start.39 = (bf16[384,1536]{1,0:T(8,128)(2,1)}, bf16[384,1536]{1,0:T(8,128)(2,1)S(1)}, u32[]{:S(2)}, u32[]{:S(2)}) collective-permute-start(bf16[384,1536]{1,0:T(8,128)(2,1)} %get-tuple-element.231), channel_id=1, source_target_pairs={{0,4},{4,0},{8,12},{12,8},{1,5},{5,1},{9,13},{13,9},{2,6},{6,2},{1... | collective-permute-start | bytes 3538952 | tf_op jit(solution)/shard_map/ppermute | solution.py:1108
  368.0 43.6 %collective-permute-start.38 = (bf16[768,768]{1,0:T(8,128)(2,1)}, bf16[768,768]{1,0:T(8,128)(2,1)S(1)}, u32[]{:S(2)}, u32[]{:S(2)}) collective-permute-start(bf16[768,768]{1,0:T(8,128)(2,1)} %get-tuple-element.229), channel_id=1, source_target_pairs={{0,16},{16,0},{1,17},{17,1},{2,18},{18,2},{3,19},{19,3},{4,20},{20... | collective-permute-start | bytes 3538952 | tf_op jit(solution)/shard_map/ppermute | solution.py:1103
  388.8 9.0 %collective-permute-start.34 = (bf16[256,1536]{1,0:T(8,128)(2,1)S(1)}, bf16[256,1536]{1,0:T(8,128)(2,1)S(1)}, u32[]{:S(2)}, u32[]{:S(2)}) collective-permute-start(bf16[256,1536]{1,0:T(8,128)(2,1)S(1)} %get-tuple-element.220.refs_1_), channel_id=1, source_target_pairs={{0,1},{1,0},{2,3},{3,2},{4,5},{5,4},{6,7},{7,6},{8,9},{9,8},{10,11... | collective-permute-start | bytes 2359304 | tf_op jit(solution)/shard_map/ppermute | solution.py:48
  388.9 9.0 %collective-permute-start.35 = (bf16[256,1536]{1,0:T(8,128)(2,1)S(1)}, bf16[256,1536]{1,0:T(8,128)(2,1)S(1)}, u32[]{:S(2)}, u32[]{:S(2)}) collective-permute-start(bf16[256,1536]{1,0:T(8,128)(2,1)S(1)} %get-tuple-element.221.refs_2_), channel_id=1, source_target_pairs={{0,1},{1,0},{2,3},{3,2},{4,5},{5,4},{6,7},{7,6},{8,9},{9,8},{10,11... | collective-permute-start | bytes 2359304 | tf_op jit(solution)/shard_map/ppermute | solution.py:48
  389.4 25.0 %collective-permute-start.40 = (bf16[192,1280]{1,0:T(8,128)(2,1)}, bf16[192,1280]{1,0:T(8,128)(2,1)S(1)}, u32[]{:S(2)}, u32[]{:S(2)}) collective-permute-start(bf16[192,1280]{1,0:T(8,128)(2,1)} %copy-done.85), channel_id=1, source_target_pairs={{0,8},{4,12},{8,0},{12,4},{1,9},{5,13},{9,1},{13,5},{2,10},{6,14},... | collective-permute-start | bytes 1474568 | tf_op jit(solution)/shard_map/ppermute | solution.py:1113
  397.8 38.9 %collective-permute-start.37 = (bf16[384,896]{1,0:T(8,128)(2,1)S(1)}, bf16[384,896]{1,0:T(8,128)(2,1)S(1)}, u32[]{:S(2)}, u32[]{:S(2)}) collective-permute-start(bf16[384,896]{1,0:T(8,128)(2,1)S(1)} %get-tuple-element.228), channel_id=1, source_target_pairs={{0,4},{4,0},{8,12},{12,8},{1,5},{5,1},{9,13},{13,9},{2,6},{6,2},{1... | collective-permute-start | bytes 2064392 | tf_op jit(solution)/shard_map/ppermute | solution.py:1108
  417.2 31.1 %collective-permute-start.43 = (bf16[384,768]{1,0:T(8,128)(2,1)S(1)}, bf16[384,768]{1,0:T(8,128)(2,1)S(1)}, u32[]{:S(2)}, u32[]{:S(2)}) collective-permute-start(bf16[384,768]{1,0:T(8,128)(2,1)S(1)} %get-tuple-element.239), channel_id=1, source_target_pairs={{0,4},{4,0},{8,12},{12,8},{1,5},{5,1},{9,13},{13,9},{2,6},{6,2},{1... | collective-permute-start | bytes 1769480 | tf_op jit(solution)/shard_map/ppermute | solution.py:1108
  417.3 31.0 %collective-permute-start.45 = (bf16[192,1536]{1,0:T(8,128)(2,1)S(1)}, bf16[192,1536]{1,0:T(8,128)(2,1)S(1)}, u32[]{:S(2)}, u32[]{:S(2)}) collective-permute-start(bf16[192,1536]{1,0:T(8,128)(2,1)S(1)} %get-tuple-element.243), channel_id=1, source_target_pairs={{0,8},{4,12},{8,0},{12,4},{1,9},{5,13},{9,1},{13,5},{2,10},{6,14},... | collective-permute-start | bytes 1769480 | tf_op jit(solution)/shard_map/ppermute | solution.py:1113
  419.4 33.3 %collective-permute-start.42 = (bf16[192,1024]{1,0:T(8,128)(2,1)S(1)}, bf16[192,1024]{1,0:T(8,128)(2,1)S(1)}, u32[]{:S(2)}, u32[]{:S(2)}) collective-permute-start(bf16[192,1024]{1,0:T(8,128)(2,1)S(1)} %copy-done.74), channel_id=1, source_target_pairs={{0,16},{16,0},{1,17},{17,1},{2,18},{18,2},{3,19},{19,3},{4,20},{20... | collective-permute-start | bytes 1179656 | tf_op jit(solution)/shard_map/ppermute | solution.py:1135
  437.5 30.1 %collective-permute-start.41 = (bf16[192,896]{1,0:T(8,128)(2,1)}, bf16[192,896]{1,0:T(8,128)(2,1)}, u32[]{:S(2)}, u32[]{:S(2)}) collective-permute-start(bf16[192,896]{1,0:T(8,128)(2,1)} %get-tuple-element.236), channel_id=1, source_target_pairs={{0,8},{4,12},{8,0},{12,4},{1,9},{5,13},{9,1},{13,5},{2,10},{6,14},... | collective-permute-start | bytes 1032200 | tf_op jit(solution)/shard_map/ppermute | solution.py:1113
  437.9 3.7 collective-permute-start.44
  449.9 24.3 %collective-permute-start.48 = (bf16[192,768]{1,0:T(8,128)(2,1)}, bf16[192,768]{1,0:T(8,128)(2,1)}, u32[]{:S(2)}, u32[]{:S(2)}) collective-permute-start(bf16[192,768]{1,0:T(8,128)(2,1)} %get-tuple-element.252), channel_id=1, source_target_pairs={{0,8},{4,12},{8,0},{12,4},{1,9},{5,13},{9,1},{13,5},{2,10},{6,14},... | collective-permute-start | bytes 884744 | tf_op jit(solution)/shard_map/ppermute | solution.py:1113
  450.2 20.9 %collective-permute-start.46 = (f32[8,512]{1,0:T(8,128)S(1)}, f32[8,512]{1,0:T(8,128)S(1)}, u32[]{:S(2)}, u32[]{:S(2)}) collective-permute-start(f32[8,512]{1,0:T(8,128)S(1)} %get-tuple-element.248.refs_0_), channel_id=1, source_target_pairs={{0,4},{4,0},{8,12},{12,8},{1,5},{5,1},{9,13},{13,9},{2,6},{6,2},{1... | collective-permute-start | bytes 49160 | tf_op jit(solution)/shard_map/ppermute | solution.py:1238
  471.1 8.5 %collective-permute-start.47 = (f32[8,512]{1,0:T(8,128)S(1)}, f32[8,512]{1,0:T(8,128)S(1)}, u32[]{:S(2)}, u32[]{:S(2)}) collective-permute-start(f32[8,512]{1,0:T(8,128)S(1)} %get-tuple-element.250), channel_id=1, source_target_pairs={{0,8},{4,12},{8,0},{12,4},{1,9},{5,13},{9,1},{13,5},{2,10},{6,14},... | collective-permute-start | bytes 49160 | tf_op jit(solution)/shard_map/ppermute | solution.py:1247
  481.0 7.2 %collective-permute-start.50 = (f32[2,200,128]{2,1,0:T(8,128)S(1)}, f32[2,200,128]{2,1,0:T(8,128)S(1)}, u32[]{:S(2)}, u32[]{:S(2)}) collective-permute-start(f32[2,200,128]{2,1,0:T(8,128)S(1)} %maximum_select_fusion.1), channel_id=1, source_target_pairs={{0,2},{1,3},{2,0},{3,1},{4,6},{5,7},{6,4},{7,5},{8,10},{9,11},{10,... | collective-permute-start | bytes 614408 | tf_op jit(solution)/shard_map/ppermute | solution.py:52
  (109 other events, 1123.1 us)
Sparse Core Ops, SparseCore 0:
  135.4 73.4 reduce-scatter.2
  303.4 66.2 reduce-scatter.4

commit v16 on v11

--- a/solution.py
+++ b/solution.py
@@ -595,7 +595,7 @@
     hidden = gate_weight.shape[0]
     column = pl.BlockSpec((total, TILE), lambda i: (0, i))
     weight = pl.BlockSpec((TILE, width), lambda i: (i, 0))
-    shape = jax.ShapeDtypeStruct((total, hidden), jnp.bfloat16)
+    shape = pltpu.HBM((total, hidden), jnp.bfloat16)
     return order(
         gated_kernel,
         [grad_hidden, gate_weight, up_weight, *pieces],

time: 496 us -> 495 us (level)
    unnamed x215 -> x233, local copies, waits for them, and re-layouts: 73.6 us -> 73.4 us
  transfers between devices with their start and end apart: 53 -> 53, of which waited for: 28 -> 28; matrix products, arithmetic and copies ran while one was open for 3% -> 3% of each run, Pallas kernels for 30% -> 29%
where the time goes in v16:
time: 495 us; the launch traced here: 493 us
  Pallas kernels  196 us (40%)
  waiting for transfers between devices  135 us (27%)
  local copies, waits for them, and re-layouts  83.6 us (17%)
  starting transfers between devices  53.4 us (11%)
  between operations  15.4 us (3%)
  other arithmetic  9.39 us (2%)
    pallas_call x44, Pallas kernels, __call__(): pl.pallas_call(run, grid_spec=pltpu.PrefetchScalarGridSpec(num_scalar_pre...  186 us
    unnamed x233, local copies, waits for them, and re-layouts  73.4 us
    ppermute x9, waiting for transfers between devices, chip_swap(): return lax.ppermute(value, 'tensor', flipped('tensor', 1))  41.7 us
    ppermute x4, waiting for transfers between devices, relay(): self.last = lax.ppermute(sent, 'seq', flipped('seq', 1))  20.3 us
    ppermute x5, waiting for transfers between devices, __init__(): self.come = lax.ppermute(sent, 'dp', flipped('dp', 0))  19 us
    ppermute x4, waiting for transfers between devices, own(): self.come = lax.ppermute(send, 'seq', flipped('seq', 0))  17 us
    ppermute x4, waiting for transfers between devices, shifted(): return lax.ppermute(value, 'seq', route)  14.9 us
    ppermute x21, waiting for transfers between devices, core_swap(): return lax.ppermute(value, 'tensor', flipped('tensor', 0))  13.8 us
  transfers between devices with their start and end apart: 53, of which 28 were waited for; matrix products, arithmetic and copies ran while one was open for 3% of the time, Pallas kernels for 29%

profile of v16, /device:TPU:0, one launch (start us, length us, event | category | flops | bytes accessed | tf_op | source)
XLA Modules:
  0.0 492.8 jit_solution(5608701861164878729)
XLA Ops:
  17.2 3.6 first.1
  23.4 5.6 %collective-permute-start.1 = (bf16[2,512,128]{2,1,0:T(8,128)(2,1)S(1)}, bf16[2,512,128]{2,1,0:T(8,128)(2,1)}, u32[]{:S(2)}, u32[]{:S(2)}) collective-permute-start(bf16[2,512,128]{2,1,0:T(8,128)(2,1)S(1)} %bitcast.84), channel_id=1, source_target_pairs={{0,4},{4,8},{8,12},{1,5},{5,9},{9,13},{2,6},{6,10},{10,14},{3,7},{... | collective-permute-start | bytes 786440 | tf_op jit(solution)/shard_map/ppermute | solution.py:66
  29.1 4.5 collective-permute-start
  34.5 4.3 collective-permute-done.refs_0_.refs_9_
  41.9 6.1 %attend.1 = (bf16[2,512,384]{2,1,0:T(8,128)(2,1)S(1)}, f32[2,2,768]{2,1,0:T(2,128)S(1)}) custom-call(s32[2,2]{1,0:T(2,128)S(1)} %shift-right-logical_maximum_fusion.low_ref.refs_0_, s32[1]{0:T(128)} %bitcast.core_ref.refs_0_.refs_1_, bf16[2,512,384]{2,1,0:T(8,128)(2,1)S(1)} %bitcast.81, s32[2,1,512]{2,1,0:T(1,128)S(1)} %sub.44.start_ref.refs_3_, ...), custom_call_target="tpu_custom_call" | custom-call | flops 8000000 | bytes 4194 | tf_op jit(solution)/shard_map/attend/pallas_call | solution.py:253
  53.6 3.5 narrow.9
  60.4 4.5 constant_dynamic-slice_fusion.2
  76.2 4.1 copy-done.7
  80.4 9.3 %grad_hidden.1 = (bf16[1024,2240]{1,0:T(8,128)(2,1)S(1)}, f32[8,128]{1,0:T(8,128)S(1)}) custom-call(bf16[1024,1536]{1,0:T(8,128)(2,1)S(1)} %get-tuple-element.146.refs_0_.refs_3_, bf16[2240,1536]{1,0:T(8,128)(2,1)S(1)} %bitcast.68, f32[8,128]{1,0:T(8,128)S(1)} %get-tuple-element.147.refs_2_, bf16[192,2240]{1,0:T(8,128)(2,1)S(1)} %copy-done.39, ...), custom_call_target="tpu_custom_call" | custom-call | flops 7046430 | bytes 15728 | tf_op jit(solution)/shard_map/grad_hidden/pallas_call | solution.py:92
  97.0 3.9 middle.1
  106.0 19.2 %gated.1 = (bf16[1024,2240]{1,0:T(8,128)(2,1)}, bf16[1024,2240]{1,0:T(8,128)(2,1)}, bf16[1024,2240]{1,0:T(8,128)(2,1)}, f32[8,128]{1,0:T(8,128)S(1)}) custom-call(bf16[1024,2240]{1,0:T(8,128)(2,1)S(1)} %copy-done.48, bf16[2240,1536]{1,0:T(8,128)(2,1)S(1)} %bitcast.65, bf16[2240,1536]{1,0:T(8,128)(2,1)S(1)} %bitcast.62, ...), custom_call_target="tpu_custom_call" | custom-call | flops 14092861 | bytes 31457 | tf_op jit(solution)/shard_map/gated/pallas_call | solution.py:92
  127.6 4.8 share.9
  138.6 4.3 share.10
  149.7 10.3 %narrow.10 = (bf16[256,1536]{1,0:T(8,128)(2,1)S(1)}, bf16[256,1536]{1,0:T(8,128)(2,1)S(1)}, f32[8,128]{1,0:T(8,128)S(1)}) custom-call(bf16[1024,2240]{1,0:T(8,128)(2,1)S(1)} %copy-done.3, bf16[2240,1536]{1,0:T(8,128)(2,1)S(1)} %bitcast.66, bf16[1024,2240]{1,0:T(8,128)(2,1)S(1)} %bitcast.47, bf16[2240,1536]{1,0:T(8,128)(2,1)} %bitcast.58, ...), custom_call_target="tpu_custom_call" | custom-call | flops 7046430 | bytes 19922 | tf_op jit(solution)/shard_map/narrow/pallas_call | solution.py:92
  166.7 11.0 %narrow.11 = (bf16[256,1536]{1,0:T(8,128)(2,1)S(1)}, bf16[256,1536]{1,0:T(8,128)(2,1)}, f32[8,128]{1,0:T(8,128)S(1)}) custom-call(bf16[1024,2240]{1,0:T(8,128)(2,1)S(1)} %bitcast.55, bf16[2240,1536]{1,0:T(8,128)(2,1)S(1)} %bitcast.67, bf16[1024,2240]{1,0:T(8,128)(2,1)S(1)} %bitcast.47, bf16[2240,1536]{1,0:T(8,128)(2,1)} %bitcast.59, ...), custom_call_target="tpu_custom_call" | custom-call | flops 7046430 | bytes 19922 | tf_op jit(solution)/shard_map/narrow/pallas_call | solution.py:92
  181.3 13.8 %share.11 = (bf16[768,2304]{1,0:T(8,128)(2,1)}, bf16[768,1536]{1,0:T(8,128)(2,1)S(1)}, bf16[768,768]{1,0:T(8,128)(2,1)}, f32[8,128]{1,0:T(8,128)S(1)}) custom-call(s32[1]{0:T(128)} %bitcast.10.refs_0_, s32[1]{0:T(128)} %constant.59.clone.1.refs_0_.refs_1_, bf16[1536,1024]{1,0:T(8,128)(2,1)S(1)} %get-tuple-element.169.refs_2_, ...), custom_call_target="tpu_custom_call" | custom-call | flops 7247757 | bytes 18087 | tf_op jit(solution)/shard_map/share/pallas_call | solution.py:92
  201.5 4.2 share.12
  205.7 8.6 %collective-permute-done.14.refs_7_ = bf16[256,1536]{1,0:T(8,128)(2,1)} collective-permute-done((bf16[256,1536]{1,0:T(8,128)(2,1)}, bf16[256,1536]{1,0:T(8,128)(2,1)}, u32[]{:S(2)}, u32[]{:S(2)}) %collective-permute-start.14) | collective-permute-done | bytes 786464 | tf_op jit(solution)/shard_map/ppermute | solution.py:52
  214.3 4.1 norm_back.2
  219.0 11.7 %collective-permute-start.19 = (bf16[384,1280]{1,0:T(8,128)(2,1)S(1)}, bf16[384,1280]{1,0:T(8,128)(2,1)S(1)}, u32[]{:S(2)}, u32[]{:S(2)}) collective-permute-start(bf16[384,1280]{1,0:T(8,128)(2,1)S(1)} %get-tuple-element.182), channel_id=1, source_target_pairs={{0,4},{4,0},{8,12},{12,8},{1,5},{5,1},{9,13},{13,9},{2,6},{6,2},{1... | collective-permute-start | bytes 2949128 | tf_op jit(solution)/shard_map/ppermute | solution.py:1108
  232.6 8.9 %attend_back.1 = (bf16[2,512,384]{2,1,0:T(8,128)(2,1)S(1)}, bf16[2,1536,128]{2,1,0:T(8,128)(2,1)S(1)}, bf16[2,1536,128]{2,1,0:T(8,128)(2,1)S(1)}, f32[8,128]{1,0:T(8,128)S(1)}) custom-call(s32[2,2]{1,0:T(2,128)S(1)} %shift-right-logical_maximum_fusion.low_ref.refs_0_, s32[1]{0:T(128)} %bitcast.core_ref.refs_0_.refs_1_, bf16[2,512,384]{2,1,0:T(8,128)(2,1)S(1)} %bitcast.82, ...), custom_call_target="tpu_custom_call" | custom-call | flops 20000000 | bytes 6291 | tf_op jit(solution)/shard_map/attend_back/pallas_call | solution.py:92
  244.8 7.9 %collective-permute-done.19.refs_1_ = bf16[384,1280]{1,0:T(8,128)(2,1)S(1)} collective-permute-done((bf16[384,1280]{1,0:T(8,128)(2,1)S(1)}, bf16[384,1280]{1,0:T(8,128)(2,1)S(1)}, u32[]{:S(2)}, u32[]{:S(2)}) %collective-permute-start.19) | collective-permute-done | bytes 983072 | tf_op jit(solution)/shard_map/ppermute | solution.py:1108
  256.3 5.3 %narrow.12 = (bf16[256,1536]{1,0:T(8,128)(2,1)S(1)}, bf16[256,1536]{1,0:T(8,128)(2,1)S(1)}, f32[8,128]{1,0:T(8,128)S(1)}) custom-call(bf16[1024,2240]{1,0:T(8,128)(2,1)S(1)} %bitcast.51, bf16[2240,1536]{1,0:T(8,128)(2,1)S(1)} %bitcast.71, f32[8,128]{1,0:T(8,128)S(1)} %get-tuple-element.186.refs_2_), custom_call_target="tpu_custom_call" | custom-call | flops 3523215 | bytes 10747 | tf_op jit(solution)/shard_map/narrow/pallas_call | solution.py:92
  265.8 7.7 %collective-permute-done.23.refs_5_ = bf16[2,512,128]{2,1,0:T(8,128)(2,1)S(1)} collective-permute-done((bf16[2,512,128]{2,1,0:T(8,128)(2,1)S(1)}, bf16[2,512,128]{2,1,0:T(8,128)(2,1)S(1)}, u32[]{:S(2)}, u32[]{:S(2)}) %collective-permute-start.23) | collective-permute-done | bytes 262176 | tf_op jit(solution)/shard_map/ppermute | solution.py:66
  274.2 3.4 narrow.13
  281.3 4.5 narrow.14
  290.0 8.3 %share.13 = (bf16[768,2304]{1,0:T(8,128)(2,1)S(1)}, f32[8,128]{1,0:T(8,128)S(1)}) custom-call(s32[1]{0:T(128)} %bitcast.11.refs_0_, s32[1]{0:T(128)} %constant.59.clone.1.refs_0_.refs_1_, bf16[1536,1024]{1,0:T(8,128)(2,1)S(1)} %copy-done.10, bf16[1024,2240]{1,0:T(8,128)(2,1)S(1)} %copy-done.4, bf16[768,2304]{1,0:T(8,128)(2,1)} %collective-permute-done.24.refs_4_, ...), custom_call_target="tpu_custom_call" | custom-call | flops 3623878 | bytes 9830 | tf_op jit(solution)/shard_map/share/pallas_call | solution.py:92
  307.3 5.3 %share.14 = (bf16[768,896]{1,0:T(8,128)(2,1)}, f32[8,128]{1,0:T(8,128)S(1)}) custom-call(s32[1]{0:T(128)} %bitcast.10.refs_0_, s32[1]{0:T(128)} %constant.59.clone.1.refs_0_.refs_1_, bf16[1536,1024]{1,0:T(8,128)(2,1)S(1)} %copy-done.23, bf16[1536,1024]{1,0:T(8,128)(2,1)S(1)} %copy-done.29, bf16[1024,512]{1,0:T(8,128)(2,1)S(1)} %get-tuple-element.198.refs_0_.refs_4_, ...), custom_call_target="tpu_custom_call" | custom-call | flops 1409286 | bytes 4784 | tf_op jit(solution)/shard_map/share/pallas_call | solution.py:92
  315.7 6.1 %narrow.15 = (bf16[256,1536]{1,0:T(8,128)(2,1)}, bf16[256,1536]{1,0:T(8,128)(2,1)}, f32[8,128]{1,0:T(8,128)S(1)}) custom-call(bf16[1024,2240]{1,0:T(8,128)(2,1)S(1)} %bitcast.53, bf16[2240,1536]{1,0:T(8,128)(2,1)S(1)} %bitcast.72, bf16[256,1536]{1,0:T(8,128)(2,1)S(1)} %collective-permute-done.20.refs_2_, ...), custom_call_target="tpu_custom_call" | custom-call | flops 3523215 | bytes 10747 | tf_op jit(solution)/shard_map/narrow/pallas_call | solution.py:92
  321.7 16.0 %collective-permute-done.30.refs_7_ = bf16[256,1536]{1,0:T(8,128)(2,1)S(1)} collective-permute-done((bf16[256,1536]{1,0:T(8,128)(2,1)}, bf16[256,1536]{1,0:T(8,128)(2,1)S(1)}, u32[]{:S(2)}, u32[]{:S(2)}) %collective-permute-start.30) | collective-permute-done | bytes 786464 | tf_op jit(solution)/shard_map/ppermute | solution.py:52
  345.3 9.3 %collective-permute-done.33.refs_4_ = bf16[768,1536]{1,0:T(8,128)(2,1)} collective-permute-done((bf16[768,1536]{1,0:T(8,128)(2,1)}, bf16[768,1536]{1,0:T(8,128)(2,1)}, u32[]{:S(2)}, u32[]{:S(2)}) %collective-permute-start.33) | collective-permute-done | bytes 2359328 | tf_op jit(solution)/shard_map/ppermute | solution.py:1103
  356.2 7.0 %share.15 = (bf16[384,1536]{1,0:T(8,128)(2,1)}, bf16[384,1536]{1,0:T(8,128)(2,1)S(1)}, f32[8,128]{1,0:T(8,128)S(1)}) custom-call(s32[1]{0:T(128)} %bitcast.11.refs_0_, s32[4]{0:T(128)S(1)} %pad_add_fusion.refs_1_, bf16[1536,1024]{1,0:T(8,128)(2,1)S(1)} %copy-done.11, bf16[1024,2240]{1,0:T(8,128)(2,1)S(1)} %bitcast.49, ...), custom_call_target="tpu_custom_call" | custom-call | flops 2415919 | bytes 7077 | tf_op jit(solution)/shard_map/share/pallas_call | solution.py:92
  364.5 3.3 place.2
  367.8 12.3 %collective-permute-done.28.refs_4_ = bf16[256,1536]{1,0:T(8,128)(2,1)S(1)} collective-permute-done((bf16[256,1536]{1,0:T(8,128)(2,1)}, bf16[256,1536]{1,0:T(8,128)(2,1)S(1)}, u32[]{:S(2)}, u32[]{:S(2)}) %collective-permute-start.28) | collective-permute-done | bytes 786464 | tf_op jit(solution)/shard_map/ppermute | solution.py:52
  382.2 3.5 layer.1
  388.5 5.8 %share.16 = (bf16[384,896]{1,0:T(8,128)(2,1)S(1)}, bf16[384,896]{1,0:T(8,128)(2,1)S(1)}, f32[8,128]{1,0:T(8,128)S(1)}) custom-call(s32[1]{0:T(128)} %bitcast.11.refs_0_, s32[4]{0:T(128)S(1)} %pad_add_fusion.refs_1_, bf16[1536,1024]{1,0:T(8,128)(2,1)S(1)} %copy-done.24, bf16[1536,1024]{1,0:T(8,128)(2,1)S(1)} %copy-done.30, ...), custom_call_target="tpu_custom_call" | custom-call | flops 1409286 | bytes 4784 | tf_op jit(solution)/shard_map/share/pallas_call | solution.py:92
  398.9 9.7 %collective-permute-done.38.refs_4_ = bf16[768,768]{1,0:T(8,128)(2,1)S(1)} collective-permute-done((bf16[768,768]{1,0:T(8,128)(2,1)}, bf16[768,768]{1,0:T(8,128)(2,1)S(1)}, u32[]{:S(2)}, u32[]{:S(2)}) %collective-permute-start.38) | collective-permute-done | bytes 1179680 | tf_op jit(solution)/shard_map/ppermute | solution.py:1103
  408.5 3.4 collective-permute-done.40.refs_6_.refs_2_
  415.7 8.6 %collective-permute-done.41.refs_3_.refs_4_ = bf16[192,1024]{1,0:T(8,128)(2,1)S(1)} collective-permute-done((bf16[192,1024]{1,0:T(8,128)(2,1)S(1)}, bf16[192,1024]{1,0:T(8,128)(2,1)S(1)}, u32[]{:S(2)}, u32[]{:S(2)}) %collective-permute-start.41) | collective-permute-done | bytes 393248 | tf_op jit(solution)/shard_map/ppermute | solution.py:1135
  424.3 3.2 collective-permute-done.37.refs_1_
  427.5 8.9 %collective-permute-done.42.refs_4_.refs_2_ = bf16[192,1536]{1,0:T(8,128)(2,1)S(1)} collective-permute-done((bf16[192,1536]{1,0:T(8,128)(2,1)S(1)}, bf16[192,1536]{1,0:T(8,128)(2,1)S(1)}, u32[]{:S(2)}, u32[]{:S(2)}) %collective-permute-start.42) | collective-permute-done | bytes 589856 | tf_op jit(solution)/shard_map/ppermute | solution.py:1113
  438.1 3.8 finish.4
  441.9 5.8 %collective-permute-done.44.refs_1_.refs_4_ = bf16[384,768]{1,0:T(8,128)(2,1)S(1)} collective-permute-done((bf16[384,768]{1,0:T(8,128)(2,1)S(1)}, bf16[384,768]{1,0:T(8,128)(2,1)S(1)}, u32[]{:S(2)}, u32[]{:S(2)}) %collective-permute-start.44) | collective-permute-done | bytes 589856 | tf_op jit(solution)/shard_map/ppermute | solution.py:1108
  451.7 3.7 finish.5
  455.5 7.5 %collective-permute-done.43.refs_2_ = bf16[192,896]{1,0:T(8,128)(2,1)} collective-permute-done((bf16[192,896]{1,0:T(8,128)(2,1)}, bf16[192,896]{1,0:T(8,128)(2,1)}, u32[]{:S(2)}, u32[]{:S(2)}) %collective-permute-start.43) | collective-permute-done | bytes 344096 | tf_op jit(solution)/shard_map/ppermute | solution.py:1113
  462.9 3.5 finish.6
  468.2 5.2 %finish.7 = (f32[192,2240]{1,0:T(8,128)}, f32[192,128]{1,0:T(8,128)S(1)}, f32[8,128]{1,0:T(8,128)}) custom-call(bf16[384,1536]{1,0:T(8,128)(2,1)S(1)} %copy-done.44, bf16[384,1536]{1,0:T(8,128)(2,1)S(1)} %copy-done.46, bf16[192,1536]{1,0:T(8,128)(2,1)S(1)} %copy-done.74, bf16[384,768]{1,0:T(8,128)(2,1)S(1)} %get-tuple-element.239.refs_0_.refs_3_, ...), custom_call_target="tpu_custom_call" | custom-call | bytes 6021 | tf_op jit(solution)/shard_map/finish/pallas_call | solution.py:92
  477.3 4.8 collective-permute-done.50
  (397 shorter events, 153.3 us)
Async XLA Ops:
  7.2 270.9 %reduce-scatter.3.cloned.1.call-start = ((), (), s32[]{:S(2)}) async-start(), calls=%async_computation.2 | async-start | bytes 3932160 | tf_op jit(solution)/shard_map/reduce_scatter | solution.py:1128
  23.4 11.1 %collective-permute-start.1 = (bf16[2,512,128]{2,1,0:T(8,128)(2,1)S(1)}, bf16[2,512,128]{2,1,0:T(8,128)(2,1)}, u32[]{:S(2)}, u32[]{:S(2)}) collective-permute-start(bf16[2,512,128]{2,1,0:T(8,128)(2,1)S(1)} %bitcast.84), channel_id=1, source_target_pairs={{0,4},{4,8},{8,12},{1,5},{5,9},{9,13},{2,6},{6,10},{10,14},{3,7},{... | collective-permute-start | bytes 786440 | tf_op jit(solution)/shard_map/ppermute | solution.py:66
  29.1 9.8 %collective-permute-start = (bf16[2,512,128]{2,1,0:T(8,128)(2,1)S(1)}, bf16[2,512,128]{2,1,0:T(8,128)(2,1)}, u32[]{:S(2)}, u32[]{:S(2)}) collective-permute-start(bf16[2,512,128]{2,1,0:T(8,128)(2,1)S(1)} %bitcast.85), channel_id=1, source_target_pairs={{0,8},{4,12},{1,9},{5,13},{2,10},{6,14},{3,11},{7,15},{16,24},{20,... | collective-permute-start | bytes 786440 | tf_op jit(solution)/shard_map/ppermute | solution.py:66
  33.6 5.4 %collective-permute-start.4 = (bf16[2,512,128]{2,1,0:T(8,128)(2,1)S(1)}, bf16[2,512,128]{2,1,0:T(8,128)(2,1)}, u32[]{:S(2)}, u32[]{:S(2)}) collective-permute-start(bf16[2,512,128]{2,1,0:T(8,128)(2,1)S(1)} %bitcast.86), channel_id=1, source_target_pairs={{0,1},{1,0},{2,3},{3,2},{4,5},{5,4},{6,7},{7,6},{8,9},{9,8},{10,11... | collective-permute-start | bytes 786440 | tf_op jit(solution)/shard_map/ppermute | solution.py:48
  34.5 4.5 collective-permute-start.3
  50.3 3.3 collective-permute-start.6
  57.1 39.9 %collective-permute-start.7 = (bf16[256,1536]{1,0:T(8,128)(2,1)}, bf16[256,1536]{1,0:T(8,128)(2,1)}, u32[]{:S(2)}, u32[]{:S(2)}) collective-permute-start(bf16[256,1536]{1,0:T(8,128)(2,1)} %get-tuple-element.142.refs_3_), channel_id=1, source_target_pairs={{0,2},{1,3},{2,0},{3,1},{4,6},{5,7},{6,4},{7,5},{8,10},{9,11},{10,... | collective-permute-start | bytes 2359304 | tf_op jit(solution)/shard_map/ppermute | solution.py:52
  58.6 38.4 %collective-permute-start.8 = (bf16[256,1536]{1,0:T(8,128)(2,1)}, bf16[256,1536]{1,0:T(8,128)(2,1)}, u32[]{:S(2)}, u32[]{:S(2)}) collective-permute-start(bf16[256,1536]{1,0:T(8,128)(2,1)} %get-tuple-element.143.refs_4_), channel_id=1, source_target_pairs={{0,2},{1,3},{2,0},{3,1},{4,6},{5,7},{6,4},{7,5},{8,10},{9,11},{10,... | collective-permute-start | bytes 2359304 | tf_op jit(solution)/shard_map/ppermute | solution.py:52
  102.6 3.4 collective-permute-start.10
  134.1 316.5 %reduce-scatter.5.cloned.1.call-start = ((), (), s32[]{:S(2)}) async-start(), calls=%async_computation.3 | async-start | bytes 4423680 | tf_op jit(solution)/shard_map/reduce_scatter | solution.py:1148
  142.8 54.4 %collective-permute-start.15 = (bf16[768,1280]{1,0:T(8,128)(2,1)}, bf16[768,1280]{1,0:T(8,128)(2,1)S(1)}, u32[]{:S(2)}, u32[]{:S(2)}) collective-permute-start(bf16[768,1280]{1,0:T(8,128)(2,1)} %get-tuple-element.167), channel_id=1, source_target_pairs={{0,16},{16,0},{1,17},{17,1},{2,18},{18,2},{3,19},{19,3},{4,20},{20... | collective-permute-start | bytes 5898248 | tf_op jit(solution)/shard_map/ppermute | solution.py:1103
  160.1 3.4 collective-permute-start.12
  177.7 28.0 %collective-permute-start.13 = (bf16[256,1536]{1,0:T(8,128)(2,1)S(1)}, bf16[256,1536]{1,0:T(8,128)(2,1)}, u32[]{:S(2)}, u32[]{:S(2)}) collective-permute-start(bf16[256,1536]{1,0:T(8,128)(2,1)S(1)} %get-tuple-element.165.refs_4_), channel_id=1, source_target_pairs={{0,2},{1,3},{2,0},{3,1},{4,6},{5,7},{6,4},{7,5},{8,10},{9,11},{10,... | collective-permute-start | bytes 2359304 | tf_op jit(solution)/shard_map/ppermute | solution.py:52
  179.3 35.0 %collective-permute-start.14 = (bf16[256,1536]{1,0:T(8,128)(2,1)}, bf16[256,1536]{1,0:T(8,128)(2,1)}, u32[]{:S(2)}, u32[]{:S(2)}) collective-permute-start(bf16[256,1536]{1,0:T(8,128)(2,1)} %get-tuple-element.166.refs_5_), channel_id=1, source_target_pairs={{0,2},{1,3},{2,0},{3,1},{4,6},{5,7},{6,4},{7,5},{8,10},{9,11},{10,... | collective-permute-start | bytes 2359304 | tf_op jit(solution)/shard_map/ppermute | solution.py:52
  196.6 91.1 %collective-permute-start.24 = (bf16[768,2304]{1,0:T(8,128)(2,1)}, bf16[768,2304]{1,0:T(8,128)(2,1)}, u32[]{:S(2)}, u32[]{:S(2)}) collective-permute-start(bf16[768,2304]{1,0:T(8,128)(2,1)} %get-tuple-element.199), channel_id=1, source_target_pairs={{0,16},{16,0},{1,17},{17,1},{2,18},{18,2},{3,19},{19,3},{4,20},{20... | collective-permute-start | bytes 10616840 | tf_op jit(solution)/shard_map/ppermute | solution.py:1103
  218.4 12.3 %collective-permute-start.16 = (bf16[256,1536]{1,0:T(8,128)(2,1)S(1)}, bf16[256,1536]{1,0:T(8,128)(2,1)S(1)}, u32[]{:S(2)}, u32[]{:S(2)}) collective-permute-start(bf16[256,1536]{1,0:T(8,128)(2,1)S(1)} %get-tuple-element.173.refs_1_.refs_0_), channel_id=1, source_target_pairs={{0,1},{1,0},{2,3},{3,2},{4,5},{5,4},{6,7},{7,6},{8,9},{9,8},{10,11... | collective-permute-start | bytes 2359304 | tf_op jit(solution)/shard_map/ppermute | solution.py:48
  218.5 12.2 %collective-permute-start.17 = (bf16[256,1536]{1,0:T(8,128)(2,1)S(1)}, bf16[256,1536]{1,0:T(8,128)(2,1)S(1)}, u32[]{:S(2)}, u32[]{:S(2)}) collective-permute-start(bf16[256,1536]{1,0:T(8,128)(2,1)S(1)} %get-tuple-element.174.refs_2_.refs_1_), channel_id=1, source_target_pairs={{0,1},{1,0},{2,3},{3,2},{4,5},{5,4},{6,7},{7,6},{8,9},{9,8},{10,11... | collective-permute-start | bytes 2359304 | tf_op jit(solution)/shard_map/ppermute | solution.py:48
  219.0 33.7 %collective-permute-start.19 = (bf16[384,1280]{1,0:T(8,128)(2,1)S(1)}, bf16[384,1280]{1,0:T(8,128)(2,1)S(1)}, u32[]{:S(2)}, u32[]{:S(2)}) collective-permute-start(bf16[384,1280]{1,0:T(8,128)(2,1)S(1)} %get-tuple-element.182), channel_id=1, source_target_pairs={{0,4},{4,0},{8,12},{12,8},{1,5},{5,1},{9,13},{13,9},{2,6},{6,2},{1... | collective-permute-start | bytes 2949128 | tf_op jit(solution)/shard_map/ppermute | solution.py:1108
  241.5 12.9 %collective-permute-start.18 = (bf16[2,1536,128]{2,1,0:T(8,128)(2,1)S(1)}, bf16[2,1536,128]{2,1,0:T(8,128)(2,1)S(1)}, u32[]{:S(2)}, u32[]{:S(2)}) collective-permute-start(bf16[2,1536,128]{2,1,0:T(8,128)(2,1)S(1)} %get-tuple-element.180), channel_id=1, source_target_pairs={{0,1},{1,0},{2,3},{3,2},{4,5},{5,4},{6,7},{7,6},{8,9},{9,8},{10,11... | collective-permute-start | bytes 2359304 | tf_op jit(solution)/shard_map/ppermute | solution.py:48
  254.7 9.8 %collective-permute-start.22 = (bf16[2,512,128]{2,1,0:T(8,128)(2,1)S(1)}, bf16[2,512,128]{2,1,0:T(8,128)(2,1)S(1)}, u32[]{:S(2)}, u32[]{:S(2)}) collective-permute-start(bf16[2,512,128]{2,1,0:T(8,128)(2,1)S(1)} %get-tuple-element.194), channel_id=1, source_target_pairs={{4,0},{8,4},{12,8},{5,1},{9,5},{13,9},{6,2},{10,6},{14,10},{7,3},{... | collective-permute-start | bytes 786440 | tf_op jit(solution)/shard_map/ppermute | solution.py:66
  264.5 9.0 %collective-permute-start.23 = (bf16[2,512,128]{2,1,0:T(8,128)(2,1)S(1)}, bf16[2,512,128]{2,1,0:T(8,128)(2,1)S(1)}, u32[]{:S(2)}, u32[]{:S(2)}) collective-permute-start(bf16[2,512,128]{2,1,0:T(8,128)(2,1)S(1)} %get-tuple-element.196), channel_id=1, source_target_pairs={{4,0},{8,4},{12,8},{5,1},{9,5},{13,9},{6,2},{10,6},{14,10},{7,3},{... | collective-permute-start | bytes 786440 | tf_op jit(solution)/shard_map/ppermute | solution.py:66
  277.6 2.6 collective-permute-start.25
  277.6 3.7 collective-permute-start.26
  300.2 54.5 %collective-permute-start.33 = (bf16[768,1536]{1,0:T(8,128)(2,1)}, bf16[768,1536]{1,0:T(8,128)(2,1)}, u32[]{:S(2)}, u32[]{:S(2)}) collective-permute-start(bf16[768,1536]{1,0:T(8,128)(2,1)} %copy-done.87), channel_id=1, source_target_pairs={{0,16},{16,0},{1,17},{17,1},{2,18},{18,2},{3,19},{19,3},{4,20},{20... | collective-permute-start | bytes 7077896 | tf_op jit(solution)/shard_map/ppermute | solution.py:1103
  300.3 12.3 %collective-permute-start.20 = (bf16[256,1536]{1,0:T(8,128)(2,1)}, bf16[256,1536]{1,0:T(8,128)(2,1)S(1)}, u32[]{:S(2)}, u32[]{:S(2)}) collective-permute-start(bf16[256,1536]{1,0:T(8,128)(2,1)} %copy-done.89), channel_id=1, source_target_pairs={{0,1},{1,0},{2,3},{3,2},{4,5},{5,4},{6,7},{7,6},{8,9},{9,8},{10,11... | collective-permute-start | bytes 2359304 | tf_op jit(solution)/shard_map/ppermute | solution.py:48
  300.5 12.1 %collective-permute-start.21 = (bf16[256,1536]{1,0:T(8,128)(2,1)}, bf16[256,1536]{1,0:T(8,128)(2,1)S(1)}, u32[]{:S(2)}, u32[]{:S(2)}) collective-permute-start(bf16[256,1536]{1,0:T(8,128)(2,1)} %copy-done.88), channel_id=1, source_target_pairs={{0,1},{1,0},{2,3},{3,2},{4,5},{5,4},{6,7},{7,6},{8,9},{9,8},{10,11... | collective-permute-start | bytes 2359304 | tf_op jit(solution)/shard_map/ppermute | solution.py:48
  301.3 20.5 %collective-permute-start.29 = (bf16[256,1536]{1,0:T(8,128)(2,1)S(1)}, bf16[256,1536]{1,0:T(8,128)(2,1)S(1)}, u32[]{:S(2)}, u32[]{:S(2)}) collective-permute-start(bf16[256,1536]{1,0:T(8,128)(2,1)S(1)} %copy-done.82), channel_id=1, source_target_pairs={{0,2},{1,3},{2,0},{3,1},{4,6},{5,7},{6,4},{7,5},{8,10},{9,11},{10,... | collective-permute-start | bytes 2359304 | tf_op jit(solution)/shard_map/ppermute | solution.py:52
  302.8 35.0 %collective-permute-start.30 = (bf16[256,1536]{1,0:T(8,128)(2,1)}, bf16[256,1536]{1,0:T(8,128)(2,1)S(1)}, u32[]{:S(2)}, u32[]{:S(2)}) collective-permute-start(bf16[256,1536]{1,0:T(8,128)(2,1)} %copy-done.83), channel_id=1, source_target_pairs={{0,2},{1,3},{2,0},{3,1},{4,6},{5,7},{6,4},{7,5},{8,10},{9,11},{10,... | collective-permute-start | bytes 2359304 | tf_op jit(solution)/shard_map/ppermute | solution.py:52
  341.9 21.2 %collective-permute-start.31 = (f32[256,1536]{1,0:T(8,128)S(1)}, f32[256,1536]{1,0:T(8,128)S(1)}, u32[]{:S(2)}, u32[]{:S(2)}) collective-permute-start(f32[256,1536]{1,0:T(8,128)S(1)} %get-tuple-element.214.refs_1_), channel_id=1, source_target_pairs={{0,1},{1,0},{2,3},{3,2},{4,5},{5,4},{6,7},{7,6},{8,9},{9,8},{10,11... | collective-permute-start | bytes 4718600 | tf_op jit(solution)/shard_map/ppermute | solution.py:48
  342.0 22.4 %collective-permute-start.32 = (f32[256,1536]{1,0:T(8,128)S(1)}, f32[256,1536]{1,0:T(8,128)S(1)}, u32[]{:S(2)}, u32[]{:S(2)}) collective-permute-start(f32[256,1536]{1,0:T(8,128)S(1)} %get-tuple-element.215.refs_2_), channel_id=1, source_target_pairs={{0,1},{1,0},{2,3},{3,2},{4,5},{5,4},{6,7},{7,6},{8,9},{9,8},{10,11... | collective-permute-start | bytes 4718600 | tf_op jit(solution)/shard_map/ppermute | solution.py:48
  342.5 43.8 %collective-permute-start.36 = (bf16[768,896]{1,0:T(8,128)(2,1)}, bf16[768,896]{1,0:T(8,128)(2,1)S(1)}, u32[]{:S(2)}, u32[]{:S(2)}) collective-permute-start(bf16[768,896]{1,0:T(8,128)(2,1)} %get-tuple-element.222), channel_id=1, source_target_pairs={{0,16},{16,0},{1,17},{17,1},{2,18},{18,2},{3,19},{19,3},{4,20},{20... | collective-permute-start | bytes 4128776 | tf_op jit(solution)/shard_map/ppermute | solution.py:1103
  343.8 24.0 %collective-permute-start.27 = (bf16[256,1536]{1,0:T(8,128)(2,1)}, bf16[256,1536]{1,0:T(8,128)(2,1)S(1)}, u32[]{:S(2)}, u32[]{:S(2)}) collective-permute-start(bf16[256,1536]{1,0:T(8,128)(2,1)} %get-tuple-element.208.refs_1_), channel_id=1, source_target_pairs={{0,2},{1,3},{2,0},{3,1},{4,6},{5,7},{6,4},{7,5},{8,10},{9,11},{10,... | collective-permute-start | bytes 2359304 | tf_op jit(solution)/shard_map/ppermute | solution.py:52
  354.6 25.5 %collective-permute-start.28 = (bf16[256,1536]{1,0:T(8,128)(2,1)}, bf16[256,1536]{1,0:T(8,128)(2,1)S(1)}, u32[]{:S(2)}, u32[]{:S(2)}) collective-permute-start(bf16[256,1536]{1,0:T(8,128)(2,1)} %get-tuple-element.209.refs_2_), channel_id=1, source_target_pairs={{0,2},{1,3},{2,0},{3,1},{4,6},{5,7},{6,4},{7,5},{8,10},{9,11},{10,... | collective-permute-start | bytes 2359304 | tf_op jit(solution)/shard_map/ppermute | solution.py:52
  363.1 33.5 %collective-permute-start.39 = (bf16[384,1536]{1,0:T(8,128)(2,1)}, bf16[384,1536]{1,0:T(8,128)(2,1)S(1)}, u32[]{:S(2)}, u32[]{:S(2)}) collective-permute-start(bf16[384,1536]{1,0:T(8,128)(2,1)} %get-tuple-element.231), channel_id=1, source_target_pairs={{0,4},{4,0},{8,12},{12,8},{1,5},{5,1},{9,13},{13,9},{2,6},{6,2},{1... | collective-permute-start | bytes 3538952 | tf_op jit(solution)/shard_map/ppermute | solution.py:1108
  364.5 44.0 %collective-permute-start.38 = (bf16[768,768]{1,0:T(8,128)(2,1)}, bf16[768,768]{1,0:T(8,128)(2,1)S(1)}, u32[]{:S(2)}, u32[]{:S(2)}) collective-permute-start(bf16[768,768]{1,0:T(8,128)(2,1)} %get-tuple-element.229), channel_id=1, source_target_pairs={{0,16},{16,0},{1,17},{17,1},{2,18},{18,2},{3,19},{19,3},{4,20},{20... | collective-permute-start | bytes 3538952 | tf_op jit(solution)/shard_map/ppermute | solution.py:1103
  385.8 8.6 %collective-permute-start.34 = (bf16[256,1536]{1,0:T(8,128)(2,1)S(1)}, bf16[256,1536]{1,0:T(8,128)(2,1)S(1)}, u32[]{:S(2)}, u32[]{:S(2)}) collective-permute-start(bf16[256,1536]{1,0:T(8,128)(2,1)S(1)} %get-tuple-element.220.refs_1_), channel_id=1, source_target_pairs={{0,1},{1,0},{2,3},{3,2},{4,5},{5,4},{6,7},{7,6},{8,9},{9,8},{10,11... | collective-permute-start | bytes 2359304 | tf_op jit(solution)/shard_map/ppermute | solution.py:48
  385.9 8.6 %collective-permute-start.35 = (bf16[256,1536]{1,0:T(8,128)(2,1)S(1)}, bf16[256,1536]{1,0:T(8,128)(2,1)S(1)}, u32[]{:S(2)}, u32[]{:S(2)}) collective-permute-start(bf16[256,1536]{1,0:T(8,128)(2,1)S(1)} %get-tuple-element.221.refs_2_), channel_id=1, source_target_pairs={{0,1},{1,0},{2,3},{3,2},{4,5},{5,4},{6,7},{7,6},{8,9},{9,8},{10,11... | collective-permute-start | bytes 2359304 | tf_op jit(solution)/shard_map/ppermute | solution.py:48
  386.4 25.6 %collective-permute-start.40 = (bf16[192,1280]{1,0:T(8,128)(2,1)S(1)}, bf16[192,1280]{1,0:T(8,128)(2,1)S(1)}, u32[]{:S(2)}, u32[]{:S(2)}) collective-permute-start(bf16[192,1280]{1,0:T(8,128)(2,1)S(1)} %copy-done.91), channel_id=1, source_target_pairs={{0,8},{4,12},{8,0},{12,4},{1,9},{5,13},{9,1},{13,5},{2,10},{6,14},... | collective-permute-start | bytes 1474568 | tf_op jit(solution)/shard_map/ppermute | solution.py:1113
  394.4 33.1 %collective-permute-start.37 = (bf16[384,896]{1,0:T(8,128)(2,1)S(1)}, bf16[384,896]{1,0:T(8,128)(2,1)S(1)}, u32[]{:S(2)}, u32[]{:S(2)}) collective-permute-start(bf16[384,896]{1,0:T(8,128)(2,1)S(1)} %get-tuple-element.228), channel_id=1, source_target_pairs={{0,4},{4,0},{8,12},{12,8},{1,5},{5,1},{9,13},{13,9},{2,6},{6,2},{1... | collective-permute-start | bytes 2064392 | tf_op jit(solution)/shard_map/ppermute | solution.py:1108
  396.8 39.6 %collective-permute-start.42 = (bf16[192,1536]{1,0:T(8,128)(2,1)S(1)}, bf16[192,1536]{1,0:T(8,128)(2,1)S(1)}, u32[]{:S(2)}, u32[]{:S(2)}) collective-permute-start(bf16[192,1536]{1,0:T(8,128)(2,1)S(1)} %get-tuple-element.236), channel_id=1, source_target_pairs={{0,8},{4,12},{8,0},{12,4},{1,9},{5,13},{9,1},{13,5},{2,10},{6,14},... | collective-permute-start | bytes 1769480 | tf_op jit(solution)/shard_map/ppermute | solution.py:1113
  414.7 33.0 %collective-permute-start.44 = (bf16[384,768]{1,0:T(8,128)(2,1)S(1)}, bf16[384,768]{1,0:T(8,128)(2,1)S(1)}, u32[]{:S(2)}, u32[]{:S(2)}) collective-permute-start(bf16[384,768]{1,0:T(8,128)(2,1)S(1)} %get-tuple-element.240), channel_id=1, source_target_pairs={{0,4},{4,0},{8,12},{12,8},{1,5},{5,1},{9,13},{13,9},{2,6},{6,2},{1... | collective-permute-start | bytes 1769480 | tf_op jit(solution)/shard_map/ppermute | solution.py:1108
  414.8 9.5 %collective-permute-start.41 = (bf16[192,1024]{1,0:T(8,128)(2,1)S(1)}, bf16[192,1024]{1,0:T(8,128)(2,1)S(1)}, u32[]{:S(2)}, u32[]{:S(2)}) collective-permute-start(bf16[192,1024]{1,0:T(8,128)(2,1)S(1)} %copy-done.77), channel_id=1, source_target_pairs={{0,16},{16,0},{1,17},{17,1},{2,18},{18,2},{3,19},{19,3},{4,20},{20... | collective-permute-start | bytes 1179656 | tf_op jit(solution)/shard_map/ppermute | solution.py:1135
  437.3 25.6 %collective-permute-start.43 = (bf16[192,896]{1,0:T(8,128)(2,1)}, bf16[192,896]{1,0:T(8,128)(2,1)}, u32[]{:S(2)}, u32[]{:S(2)}) collective-permute-start(bf16[192,896]{1,0:T(8,128)(2,1)} %get-tuple-element.237), channel_id=1, source_target_pairs={{0,8},{4,12},{8,0},{12,4},{1,9},{5,13},{9,1},{13,5},{2,10},{6,14},... | collective-permute-start | bytes 1032200 | tf_op jit(solution)/shard_map/ppermute | solution.py:1113
  437.3 4.5 collective-permute-start.45
  448.5 19.7 %collective-permute-start.48 = (bf16[192,768]{1,0:T(8,128)(2,1)}, bf16[192,768]{1,0:T(8,128)(2,1)}, u32[]{:S(2)}, u32[]{:S(2)}) collective-permute-start(bf16[192,768]{1,0:T(8,128)(2,1)} %get-tuple-element.252), channel_id=1, source_target_pairs={{0,8},{4,12},{8,0},{12,4},{1,9},{5,13},{9,1},{13,5},{2,10},{6,14},... | collective-permute-start | bytes 884744 | tf_op jit(solution)/shard_map/ppermute | solution.py:1113
  448.5 17.9 %collective-permute-start.46 = (f32[8,512]{1,0:T(8,128)S(1)}, f32[8,512]{1,0:T(8,128)S(1)}, u32[]{:S(2)}, u32[]{:S(2)}) collective-permute-start(f32[8,512]{1,0:T(8,128)S(1)} %get-tuple-element.248.refs_0_), channel_id=1, source_target_pairs={{0,4},{4,0},{8,12},{12,8},{1,5},{5,1},{9,13},{13,9},{2,6},{6,2},{1... | collective-permute-start | bytes 49160 | tf_op jit(solution)/shard_map/ppermute | solution.py:1241
  466.4 7.1 %collective-permute-start.47 = (f32[8,512]{1,0:T(8,128)S(1)}, f32[8,512]{1,0:T(8,128)S(1)}, u32[]{:S(2)}, u32[]{:S(2)}) collective-permute-start(f32[8,512]{1,0:T(8,128)S(1)} %get-tuple-element.250), channel_id=1, source_target_pairs={{0,8},{4,12},{8,0},{12,4},{1,9},{5,13},{9,1},{13,5},{2,10},{6,14},... | collective-permute-start | bytes 49160 | tf_op jit(solution)/shard_map/ppermute | solution.py:1248
  474.9 7.2 %collective-permute-start.50 = (f32[2,200,128]{2,1,0:T(8,128)S(1)}, f32[2,200,128]{2,1,0:T(8,128)S(1)}, u32[]{:S(2)}, u32[]{:S(2)}) collective-permute-start(f32[2,200,128]{2,1,0:T(8,128)S(1)} %maximum_select_fusion.1), channel_id=1, source_target_pairs={{0,2},{1,3},{2,0},{3,1},{4,6},{5,7},{6,4},{7,5},{8,10},{9,11},{10,... | collective-permute-start | bytes 614408 | tf_op jit(solution)/shard_map/ppermute | solution.py:52
  (119 other events, 1286.3 us)
Sparse Core Ops, SparseCore 0:
  134.2 69.6 reduce-scatter.2
  300.3 65.2 reduce-scatter.4
